TPU v7x, 32 devices: a whole 2x2x4 slice. The times are simulated.
32 devices in a mesh: groups: 2 (over y), cls: 4 (over z), img: 4 (over x, core).
Axes of the slice: x: 2, y: 2, z: 4, core: 2. Of those that a mesh axis runs over, the one named last changes fastest.
Arguments:
- particles: bfloat16 [512, 2, 4608], P(('groups', 'img', 'cls')), parts along dimension 0, may hold values from -30 to 30
- classes: bfloat16 [256, 2, 4608], P(('groups', 'cls')), parts along dimension 0, may hold values from -4 to 4
- ctf: float32 [128, 4608], P('groups'), parts along dimension 0, may hold values from 0.1 to 1
- noise_weight: float32 [9216], P('groups'), parts along dimension 0, may hold values from 0.01 to 0.1
- group_ids: int32 [512], P(('groups', 'img', 'cls')), parts along dimension 0, may hold values from 0 to 63
- shifts: int32 [48, 2], P('groups'), parts along dimension 0, may hold values from -6 to 6
Outputs:
- log_resp: float32 [512, 128], P(('groups', 'img'), 'cls'), parts along dimension 0
- averages: float32 [256, 2, 4608], P(('groups', 'cls'), None, 'img'), parts along dimension 0
There are 2 independent parts, one for each index of `groups`. A program takes and returns all parts, laid end to end along the dimension named above; each array names one. Nothing has to cross between parts.
All inputs are finite; a program needn't handle non-finite values.
Results may differ from a plain program's by a relative error of at most 0.012.
The roundings to bfloat16 on the way count: a program that leaves them out, or rounds other values in their place, can miss the bound.
Values may be sent and summed in bfloat16 or wider, within the bound.
No kernel may reach another device: no remote copies, remote signals or barrier semaphores. Data moves between devices by JAX's collectives and lax.ppermute only.
A program may use at most 128 MiB of HBM per device.

v0:
```python
import jax
import jax.numpy as jnp
from jax import lax
from jax.sharding import PartitionSpec as P

BOX = 128


prior_precision = 0.02


def phase_tables(shifts, freq):
    index = jnp.arange(freq)
    along_y = (index // BOX).astype(jnp.float32)
    along_x = (index % BOX - BOX // 2).astype(jnp.float32)
    angle = (
        2.0
        * jnp.pi
        / BOX
        * (
            shifts[:, 0:1].astype(jnp.float32) * along_x[None, :]
            + shifts[:, 1:2].astype(jnp.float32) * along_y[None, :]
        )
    )
    return (jnp.cos(angle), jnp.sin(angle))


def local(particles, classes, ctf, noise_weight, group_ids, shifts):
    part_rows = particles.shape[0]
    freq = particles.shape[2]
    cls_rows = classes.shape[0]
    poses = shifts.shape[0]
    groups = ctf.shape[0]
    total_rows = part_rows * lax.axis_size("cls")
    cos_t, sin_t = phase_tables(shifts, freq)
    real_part = classes[:, 0, :].astype(jnp.float32)
    imag_part = classes[:, 1, :].astype(jnp.float32)
    temp_re = real_part[None] * cos_t[:, None, :] - imag_part[None] * sin_t[:, None, :]
    temp_im = real_part[None] * sin_t[:, None, :] + imag_part[None] * cos_t[:, None, :]
    templates = (
        jnp.stack([temp_re, temp_im], axis=2)
        .astype(jnp.bfloat16)
        .reshape(poses * cls_rows, 2 * freq)
    )
    marks_local = (group_ids[:, None] == jnp.arange(groups)[None, :]).astype(jnp.float32)
    selected = jnp.dot(marks_local, ctf, precision=lax.Precision.HIGHEST)
    weighted = (
        particles.astype(jnp.float32) * (selected * noise_weight[None, :])[:, None, :]
    ).astype(jnp.bfloat16)
    weighted = weighted.reshape(part_rows, 2 * freq)
    marks_low = marks_local.astype(jnp.bfloat16)
    ctf_weight = ctf * ctf * noise_weight[None, :]
    power = jnp.dot(
        ctf_weight,
        (real_part * real_part + imag_part * imag_part).T,
        precision=lax.Precision.HIGHEST,
    )
    gathered, marks_all = (
        lax.all_gather(weighted, "cls", axis=0, tiled=True),
        lax.all_gather(marks_low, "cls", axis=0, tiled=True),
    )
    cross = lax.dot_general(
        gathered, templates, (((1,), (1,)), ((), ())), preferred_element_type=jnp.float32
    )
    penalty = jnp.dot(marks_all.astype(jnp.float32), power, precision=lax.Precision.HIGHEST)
    scores = cross.reshape(gathered.shape[0], poses, cls_rows) - 0.5 * penalty[:, None, :]
    local_peak = jnp.max(scores, axis=(1, 2))
    peak = lax.pmax(local_peak, "cls")
    total = lax.psum(jnp.sum(jnp.exp(scores - peak[:, None, None]), axis=(1, 2)), "cls")
    log_norm = peak + jnp.log(total)
    pose_peak = jnp.max(scores, axis=1)
    log_resp = (
        pose_peak
        + jnp.log(jnp.sum(jnp.exp(scores - pose_peak[:, None, :]), axis=1))
        - log_norm[:, None]
    )
    rho = jnp.exp(scores - log_norm[:, None, None])
    rho_low = rho.astype(jnp.bfloat16).reshape(total_rows, poses * cls_rows)
    pose_total = jnp.sum(rho, axis=1)
    sums = lax.dot_general(
        rho_low, gathered, (((0,), (0,)), ((), ())), preferred_element_type=jnp.float32
    )
    mass_table = jnp.dot(
        pose_total.T, marks_all.astype(jnp.float32), precision=lax.Precision.HIGHEST
    )
    sums = sums.reshape(poses, cls_rows, 2, freq)
    cos_b = cos_t[:, None, :]
    sin_b = sin_t[:, None, :]
    numer_re = jnp.sum(sums[:, :, 0, :] * cos_b + sums[:, :, 1, :] * sin_b, axis=0)
    numer_im = jnp.sum(sums[:, :, 1, :] * cos_b - sums[:, :, 0, :] * sin_b, axis=0)
    numer = jnp.stack([numer_re, numer_im], axis=1)
    denom = jnp.dot(mass_table, ctf_weight, precision=lax.Precision.HIGHEST)
    numer_part, denom_part = (
        lax.psum_scatter(numer, "img", scatter_dimension=2, tiled=True),
        lax.psum_scatter(denom, "img", scatter_dimension=1, tiled=True),
    )
    averages = numer_part / (denom_part[:, None, :] + prior_precision)
    return (log_resp, averages)


def solution(mesh):
    placed = (
        P(("groups", "img", "cls"), None, None),
        P(("groups", "cls"), None, None),
        P("groups", None),
        P("groups"),
        P(("groups", "img", "cls")),
        P("groups", None),
    )
    return jax.shard_map(
        local,
        mesh=mesh,
        in_specs=placed,
        out_specs=(P(("groups", "img"), "cls"), P(("groups", "cls"), None, "img")),
        check_vma=False,
    )
```

profile of v0, /device:TPU:0, one launch (start us, length us, event | category | flops | bytes accessed | tf_op | source)
XLA Modules:
  0.0 220.5 jit_solution(17909339871494409727)
XLA Ops:
  7.2 0.0 all-gather.2.cloned.1.call-start
  7.2 1.8 convolution_multiply_fusion
  9.0 1.3 multiply_convert_fusion
  10.3 0.7 copy.26
  11.0 0.0 all-gather.2.cloned.1.call-update
  11.0 0.0 reduce-scatter.5.cloned.1.call-start
  11.1 2.4 %fusion.34 = (bf16[32,1,4608]{2,1,0:T(2,128)(2,1)S(1)}, bf16[32,1,4608]{2,1,0:T(2,128)(2,1)S(1)}) fusion(bf16[32,2,4608]{2,1,0:T(2,128)(2,1)} %param.7), kind=kLoop, calls=%fused_computation.61 | loop fusion | bytes 1179648 | tf_op jit(solution)/shard_map/slice | solution.py:36
  13.5 0.8 convert_bitcast_fusion.1
  14.3 0.1 fusion.18
  14.3 1.6 fusion.15
  16.0 0.0 copy-start.2
  16.0 30.8 %subtract_convert_fusion = (bf16[24,32,1,4608]{3,2,1,0:T(2,128)(2,1)S(1)}, bf16[24,32,1,4608]{3,2,1,0:T(2,128)(2,1)}) fusion(f32[24,4608]{1,0:T(8,128)S(1)} %get-tuple-element.17, f32[32,4608]{1,0:T(8,128)S(1)} %get-tuple-element.22, f32[24,4608]{1,0:T(8,128)S(1)} %get-tuple-element.16, f32[32,4608]{1,0:T(8,128)S(1)} %get-tuple-element.23), kind=kLoop, calls=%fused_computation.6 | loop fusion | flops 28311552 | bytes 16220160 | tf_op jit(solution)/shard_map/convert.2
  46.8 0.0 copy-done.2
  46.8 34.8 %pad_maximum_fusion = bf16[24,32,2,4608]{3,2,1,0:T(2,128)(2,1)} fusion(bf16[24,32,1,4608]{3,2,1,0:T(2,128)(2,1)} %get-tuple-element.13, bf16[24,32,1,4608]{3,2,1,0:T(2,128)(2,1)S(1)} %get-tuple-element.12), kind=kLoop, calls=%fused_computation.2 | loop fusion | flops 28311552 | bytes 28311552 | tf_op jit(solution)/shard_map/stack | solution.py:41
  81.6 0.0 copy-start.4
  81.6 0.0 copy-start
  81.6 0.0 copy-start.3
  81.6 22.7 %convert_element_type.73 = bf16[24,32,9216]{2,1,0:T(8,128)(2,1)} reshape(bf16[24,32,2,4608]{3,2,1,0:T(2,128)(2,1)} %pad_maximum_fusion) | data formatting | bytes 28311552 | tf_op jit(solution)/shard_map/convert_element_type | solution.py:42
  104.3 0.0 copy-done.4
  104.3 0.1 convert_convert_fusion
  104.4 14.8 %all_gather.7 = bf16[64,64]{1,0:T(8,128)(2,1)S(1)} all-gather(bf16[16,64]{1,0:T(8,128)(2,1)S(1)} %convert_convert_fusion), channel_id=1, replica_groups=mesh['groups'=2,'cls'=4,'img'=4] {'cls'}, dimensions={0}, use_global_device_ids=true | all-gather | bytes 10240 | tf_op jit(solution)/shard_map/all_gather | solution.py:60
  119.2 0.0 copy-done
  119.2 0.0 copy-done.3
  119.2 1.2 fusion.8
  120.4 0.1 convolution_multiply_fusion.1
  120.5 0.0 all-gather.2.cloned.1.call-done
  120.6 0.0 copy-start.1
  120.6 7.5 %fusion.35 = (f32[64]{0:T(128)S(1)}, f32[64,24,32]{0,2,1:T(8,128)S(1)}) fusion(f32[64,32]{0,1:T(8,128)S(1)} %convolution_multiply_fusion.1, bf16[24,32,9216]{2,1,0:T(8,128)(2,1)} %convert_element_type.73, bf16[64,9216]{1,0:T(8,128)(2,1)} %all-gather.2.cloned.1.call-done), kind=kOutput, calls=%fused_computation.62 | convolution fusion | flops 906067904 | bytes 15540480 | tf_op jit(solution)/shard_map/dot_general | solution.py:62
  128.1 11.7 %pmax.7 = f32[64]{0:T(128)S(1)} all-reduce(f32[64]{0:T(128)S(1)} %get-tuple-element.20), channel_id=1, replica_groups=mesh['groups'=2,'cls'=4,'img'=4] {'cls'}, use_global_device_ids=true, to_apply=%region_3.4 | all-reduce | flops 64 | bytes 512 | tf_op jit(solution)/shard_map/pmax | solution.py:68
  139.8 0.1 exponential_reduce_fusion
  139.9 8.5 %psum.7 = f32[64]{0:T(128)S(1)} all-reduce(f32[64]{0:T(128)S(1)} %get-tuple-element.10), channel_id=1, replica_groups=mesh['groups'=2,'cls'=4,'img'=4] {'cls'}, use_global_device_ids=true, to_apply=%region_5.6 | all-reduce | flops 64 | bytes 512 | tf_op jit(solution)/shard_map/psum | solution.py:69
  148.5 0.1 fusion.16
  148.6 0.0 copy-done.1
  148.6 11.4 %fusion = f32[24,32,2,4608]{3,1,2,0:T(8,128)} fusion(bf16[8,2,8,4608]{3,2,1,0:T(8,128)(2,1)S(1)} %bitcast.71, f32[64,24,32]{0,2,1:T(8,128)S(1)} %get-tuple-element.21, f32[64]{0:T(128)S(1)} %log_add_fusion), kind=kOutput, calls=%fused_computation.9 | convolution fusion | flops 906067968 | bytes 29688064 | tf_op jit(solution)/shard_map/dot_general | solution.py:80
  160.1 0.1 fusion.36
  160.2 1.6 fusion.7
  161.8 0.0 reduce-scatter.5.cloned.1.call-update
  161.8 0.0 reduce-scatter.3.cloned.1.call-start
  161.8 10.9 %add_reduce_fusion = (f32[32,4608]{1,0:T(8,128)S(1)}, f32[32,4608]{1,0:T(8,128)S(1)}) fusion(f32[24,32,2,4608]{3,1,2,0:T(8,128)} %fusion, f32[24,4608]{1,0:T(8,128)} %copy-done.2, f32[24,4608]{1,0:T(8,128)S(1)} %get-tuple-element.16), kind=kLoop, calls=%fused_computation.4 | loop fusion | flops 28016640 | bytes 30375936 | tf_op jit(solution)/shard_map/reduce_sum | solution.py:89
  172.8 1.1 pad_maximum_fusion.1
  173.9 0.0 reduce-scatter.3.cloned.1.call-update
  173.9 0.6 add_subtract_fusion
  174.5 9.2 %reduce-scatter.5.cloned.1.call-done = f32[32,1152]{1,0:T(8,128)} async-done(((f32[32,4608]{1,0:T(8,128)}), f32[32,1152]{1,0:T(8,128)}) %reduce-scatter.5.cloned.1.call-update) | async-done | bytes 147472 | tf_op jit(solution)/shard_map/reduce_scatter | solution.py:95
  183.7 0.9 broadcast_add_fusion
  184.6 27.4 %reduce-scatter.3.cloned.1.call-done = f32[32,2,1152]{2,0,1:T(8,128)} async-done(((f32[32,2,4608]{2,0,1:T(8,128)}), f32[32,2,1152]{2,0,1:T(8,128)}) %reduce-scatter.3.cloned.1.call-update) | async-done | bytes 294928 | tf_op jit(solution)/shard_map/reduce_scatter | solution.py:94
  212.0 1.0 broadcast_divide_fusion
  213.0 0.9 copy.20
  (2 shorter events, 0.0 us)
Async XLA Ops:
  7.2 113.4 %all-gather.2.cloned.1.call-start = ((), (), s32[]{:S(2)}) async-start(), calls=%async_computation.2 | async-start | bytes 1474560 | tf_op jit(solution)/shard_map/all_gather | solution.py:59
  11.0 172.6 %reduce-scatter.5.cloned.1.call-start = ((), (), s32[]{:S(2)}) async-start(), calls=%async_computation.4 | async-start | bytes 737280 | tf_op jit(solution)/shard_map/reduce_scatter | solution.py:95
  16.0 30.8 %copy-start.2 = (f32[24,4608]{1,0:T(8,128)}, f32[24,4608]{1,0:T(8,128)S(1)}, u32[]{:S(2)}) copy-start(f32[24,4608]{1,0:T(8,128)S(1)} %get-tuple-element.17) | copy-start | bytes 1327108
  81.6 22.7 %copy-start.4 = (s32[16]{0:T(128)S(1)}, s32[16]{0:T(128)}, u32[]{:S(2)}) copy-start(s32[16]{0:T(128)} %param.10) | copy-start | bytes 196
  81.6 37.6 %copy-start = (f32[64,4608]{1,0:T(8,128)S(1)}, f32[64,4608]{1,0:T(8,128)}, u32[]{:S(2)}) copy-start(f32[64,4608]{1,0:T(8,128)} %param.8) | copy-start | bytes 3538948
  81.6 37.6 %copy-start.3 = (f32[4608]{0:T(1024)S(1)}, f32[4608]{0:T(1024)}, u32[]{:S(2)}) copy-start(f32[4608]{0:T(1024)} %param.9) | copy-start | bytes 55300
  120.6 28.1 %copy-start.1 = (bf16[64,9216]{1,0:T(8,128)(2,1)S(1)}, bf16[64,9216]{1,0:T(8,128)(2,1)}, u32[]{:S(2)}) copy-start(bf16[64,9216]{1,0:T(8,128)(2,1)} %all-gather.2.cloned.1.call-done) | copy-start | bytes 3538948
  161.8 50.2 %reduce-scatter.3.cloned.1.call-start = ((), (), s32[]{:S(2)}) async-start(), calls=%async_computation.3 | async-start | bytes 1474560 | tf_op jit(solution)/shard_map/reduce_scatter | solution.py:94
Sparse Core Ops, SparseCore 0:
  11.2 33.1 all-gather.1
  161.9 21.7 reduce-scatter.4
  186.3 25.7 reduce-scatter.2
where the time goes:
time: 221 us; the launch traced here: 220 us
  other arithmetic  84.3 us (38%)
  waiting for transfers between devices  36.7 us (17%)
  blocking collectives  35.1 us (16%)
  local copies, waits for them, and re-layouts  26.8 us (12%)
  matrix products  23.7 us (11%)
  between operations  13.9 us (6%)
    another operation x1, other arithmetic, local(): jnp.stack([temp_re, temp_im], axis=2).astype(jnp.bfloat16)  34.8 us
    another operation x1, other arithmetic  30.8 us
    reduce_scatter x1, waiting for transfers between devices, local(): lax.psum_scatter(numer, 'img', scatter_dimension=2, tiled=True)  27.4 us
    convert_element_type x1, local copies, waits for them, and re-layouts, local(): templates = jnp.stack([temp_re, temp_im], axis=2).astype(jnp.bfloat16).re...  22.7 us
    all_gather x1, blocking collectives, local(): lax.all_gather(marks_low, 'cls', axis=0, tiled=True)  14.8 us
    pmax x1, blocking collectives, local(): peak = lax.pmax(local_peak, 'cls')  11.7 us
    dot_general x1, matrix products, local(): lax.dot_general(rho_low, gathered, (((0,), (0,)), ((), ())), preferred_el...  11.4 us
    reduce_sum x1, other arithmetic, local(): jnp.sum(sums[:, :, 0, :] * cos_b + sums[:, :, 1, :] * sin_b, axis=0)  10.9 us
  transfers between devices with their start and end apart: 3, of which 2 were waited for; matrix products, arithmetic and copies ran while one was open for 49% of the time, Pallas kernels for 0%

commit v1 on v0

v1 whole, which is shorter than its diff:
```python
import functools

import jax
import jax.numpy as jnp
from jax import lax
from jax.experimental import pallas as pl
from jax.experimental.pallas import tpu as pltpu
from jax.sharding import PartitionSpec as P

BOX = 128
CHUNKS = 2
VMEM_LIMIT = 48 * 1024 * 1024

prior_precision = 0.02

NT = (((1,), (1,)), ((), ()))
NN = (((1,), (0,)), ((), ()))
HIGHEST = lax.Precision.HIGHEST
f32 = jnp.float32
bf16 = jnp.bfloat16


def phase_tables(shifts, freq):
    index = jnp.arange(freq)
    along_y = (index // BOX).astype(f32)
    along_x = (index % BOX - BOX // 2).astype(f32)
    angle = (
        2.0
        * jnp.pi
        / BOX
        * (
            shifts[:, 0:1].astype(f32) * along_x[None, :]
            + shifts[:, 1:2].astype(f32) * along_y[None, :]
        )
    )
    return (jnp.cos(angle), jnp.sin(angle))


def tile_of(extent):
    return max(t for t in range(128, 513, 128) if extent % t == 0)


def params(grid_rank):
    return pltpu.CompilerParams(
        dimension_semantics=("arbitrary",) * grid_rank, vmem_limit_bytes=VMEM_LIMIT
    )


def weigh_kernel(ids_ref, p_ref, ctf_ref, nw_ref, *refs):
    out_refs, scale_ref = refs[:-1], refs[-1]
    rows = p_ref.shape[0] // 2
    freq = p_ref.shape[1]
    for n in range(rows):
        row = ctf_ref[pl.ds(ids_ref[n], 1), :] * nw_ref[...]
        scale_ref[2 * n : 2 * n + 2, :] = jnp.broadcast_to(row, (2, freq))
    chunk = freq // len(out_refs)
    for c, out_ref in enumerate(out_refs):
        cut = slice(c * chunk, (c + 1) * chunk)
        out_ref[...] = (p_ref[:, cut].astype(f32) * scale_ref[:, cut]).astype(bf16)


def weigh(particles, ctf, noise_row, group_ids):
    rows, _, freq = particles.shape
    flat = particles.reshape(2 * rows, freq)
    vmem = pl.BlockSpec(memory_space=pltpu.VMEM)
    return pl.pallas_call(
        weigh_kernel,
        in_specs=[pl.BlockSpec(memory_space=pltpu.SMEM), vmem, vmem, vmem],
        out_specs=[vmem] * CHUNKS,
        out_shape=[jax.ShapeDtypeStruct((2 * rows, freq // CHUNKS), bf16)] * CHUNKS,
        scratch_shapes=[pltpu.VMEM((2 * rows, freq), f32)],
        compiler_params=pltpu.CompilerParams(vmem_limit_bytes=VMEM_LIMIT),
        cost_estimate=pl.CostEstimate(
            flops=4 * rows * freq, bytes_accessed=ctf.size * 4 + 8 * rows * freq, transcendentals=0
        ),
        name="weigh",
    )(group_ids, flat, ctf, noise_row)


def even_lanes(shape, axis):
    return lax.rem(lax.broadcasted_iota(jnp.int32, shape, axis), 2) == 0


def group_marks(lane_ids, groups):
    lanes = lane_ids.shape[1]
    return (lax.broadcasted_iota(jnp.int32, (groups, lanes), 0) == lane_ids).astype(f32)


def score_kernel(
    sources, first, last, poses, cls_ref, cos_ref, sin_ref, ctf_ref, nw_ref, ids_ref, *refs
):
    refs = list(refs)
    w_refs = [refs.pop(0) for _ in range(sources)]
    if not first:
        acc_in, pow_in, _ = [refs.pop(0) for _ in range(3)]
    acc_ref, pow_ref, all_ref = [refs.pop(0) for _ in range(3)]
    stat_ref = refs.pop(0) if last else None
    temp_ref = refs.pop(0)
    step = pl.program_id(0)
    rows, tile = cls_ref.shape[1], cls_ref.shape[2]

    @pl.when(step == 0)
    def _():
        acc_ref[...] = jnp.zeros_like(acc_ref) if first else acc_in[...]
        pow_ref[...] = jnp.zeros_like(pow_ref) if first else pow_in[...]

    re = cls_ref[0].astype(f32)
    im = cls_ref[1].astype(f32)
    for r in range(poses):
        cos_r = cos_ref[r : r + 1, :]
        sin_r = sin_ref[r : r + 1, :]
        temp_ref[r * rows : (r + 1) * rows, :tile] = (re * cos_r - im * sin_r).astype(bf16)
        temp_ref[r * rows : (r + 1) * rows, tile:] = (re * sin_r + im * cos_r).astype(bf16)
    weighted = jnp.concatenate([ref[...] for ref in w_refs], axis=0)
    all_ref[...] = weighted
    wide = weighted.astype(f32)
    even = even_lanes(wide.shape, 0)
    parts = jnp.concatenate(
        [jnp.where(even, wide, 0.0).astype(bf16), jnp.where(even, 0.0, wide).astype(bf16)], axis=1
    )
    acc_ref[...] += lax.dot_general(temp_ref[...], parts, NT, preferred_element_type=f32)
    ctf = ctf_ref[...]
    pow_ref[...] += lax.dot_general(
        re * re + im * im,
        ctf * ctf * nw_ref[...],
        NT,
        precision=HIGHEST,
        preferred_element_type=f32,
    )

    if last:

        @pl.when(step == pl.num_programs(0) - 1)
        def _():
            acc = acc_ref[...]
            lanes = acc.shape[1]
            acc = acc + jnp.where(
                even_lanes(acc.shape, 1),
                pltpu.roll(acc, lanes - 1, 1),
                pltpu.roll(acc, 1, 1),
            )
            penalty = lax.dot_general(
                pow_ref[...],
                group_marks(ids_ref[...], ctf.shape[0]),
                NN,
                precision=HIGHEST,
                preferred_element_type=f32,
            )
            scores = acc.reshape(poses, rows, lanes) - 0.5 * penalty[None]
            peak = jnp.max(jnp.max(scores, axis=0), axis=0, keepdims=True)
            total = jnp.sum(jnp.sum(jnp.exp(scores - peak[None]), axis=0), axis=0, keepdims=True)
            acc_ref[...] = scores.reshape(poses * rows, lanes)
            stat_ref[0:1, :] = peak
            stat_ref[1:2, :] = total
            stat_ref[2:8, :] = jnp.zeros((6, lanes), f32)


def score(chunk, parts, classes, cos_t, sin_t, ctf, noise_row, lane_ids, carried):
    rows, freq = classes.shape[1], classes.shape[2]
    poses, groups = cos_t.shape[0], ctf.shape[0]
    lanes = lane_ids.shape[1]
    span = freq // CHUNKS
    tile = tile_of(span)
    steps = span // tile
    first, last = chunk == 0, chunk == CHUNKS - 1
    base = chunk * steps

    def at(j):
        return (0, base + j)

    def whole(shape):
        return pl.BlockSpec(shape, lambda j: (0, 0))

    in_specs = [
        pl.BlockSpec((2, rows, tile), lambda j: (0, 0, base + j)),
        pl.BlockSpec((poses, tile), at),
        pl.BlockSpec((poses, tile), at),
        pl.BlockSpec((groups, tile), at),
        pl.BlockSpec((1, tile), at),
        whole((1, lanes)),
    ] + [pl.BlockSpec((p.shape[0], tile), lambda j: (0, j)) for p in parts]
    operands = [classes, cos_t, sin_t, ctf, noise_row, lane_ids, *parts]
    aliases = {}
    if not first:
        in_specs += [
            whole((poses * rows, lanes)),
            whole((rows, groups)),
            pl.BlockSpec(memory_space=pl.ANY),
        ]
        operands += list(carried)
        aliases = {len(operands) - 1: 2}
    out_specs = [
        whole((poses * rows, lanes)),
        whole((rows, groups)),
        pl.BlockSpec((lanes, tile), at),
    ]
    out_shape = [
        jax.ShapeDtypeStruct((poses * rows, lanes), f32),
        jax.ShapeDtypeStruct((rows, groups), f32),
        jax.ShapeDtypeStruct((lanes, freq), bf16),
    ]
    if last:
        out_specs.append(whole((8, lanes)))
        out_shape.append(jax.ShapeDtypeStruct((8, lanes), f32))
    return pl.pallas_call(
        functools.partial(score_kernel, len(parts), first, last, poses),
        grid=(steps,),
        in_specs=in_specs,
        out_specs=out_specs,
        out_shape=out_shape,
        scratch_shapes=[pltpu.VMEM((poses * rows, 2 * tile), bf16)],
        input_output_aliases=aliases,
        compiler_params=params(1),
        cost_estimate=pl.CostEstimate(
            flops=4 * 128 * poses * rows * span, bytes_accessed=4 * 300 * span, transcendentals=0
        ),
        name=f"score{chunk}",
    )(*operands)


def xor_blocks(values, block, distance):
    lanes = values.shape[1]
    lane = lax.broadcasted_iota(jnp.int32, values.shape, 1)
    width = block
    while distance:
        if distance % 2:
            low = lax.rem(lane // width, 2) == 0
            values = jnp.where(
                low, pltpu.roll(values, lanes - width, 1), pltpu.roll(values, width, 1)
            )
        distance //= 2
        width *= 2
    return values


def rotate_sum(rho, weighted, cos_ref, sin_ref, poses, rows, write):
    tile = weighted.shape[1]
    sums_re = jnp.dot(rho[0], weighted, preferred_element_type=f32)
    sums_im = jnp.dot(rho[1], weighted, preferred_element_type=f32)
    numer_re = jnp.zeros((rows, tile), f32)
    numer_im = jnp.zeros((rows, tile), f32)
    for r in range(poses):
        cos_r = cos_ref[r : r + 1, :]
        sin_r = sin_ref[r : r + 1, :]
        s_re = sums_re[r * rows : (r + 1) * rows]
        s_im = sums_im[r * rows : (r + 1) * rows]
        numer_re = numer_re + s_re * cos_r + s_im * sin_r
        numer_im = numer_im + s_im * cos_r - s_re * sin_r
    write(numer_re, numer_im)


def write_slices(out_refs, steps):
    def write(numer_re, numer_im):
        for s, ref in enumerate(out_refs):

            @pl.when(pl.program_id(0) // steps == s)
            def _():
                ref[0] = numer_re.astype(ref.dtype)
                ref[1] = numer_im.astype(ref.dtype)

    return write


def resp_kernel(
    poses, block, paired, steps, where_ref, s_ref, ids_ref, dest_ref, cos_ref, sin_ref, w_ref, *refs
):
    refs = list(refs)
    stat_refs, refs = refs[: len(paired)], refs[len(paired) :]
    resp_ref, rho_ref, mass_ref = refs[:3]
    out_refs = refs[3:]
    rows = mass_ref.shape[0]
    groups = mass_ref.shape[1]
    lanes = s_ref.shape[1]

    @pl.when(pl.program_id(0) == 0)
    def _():
        peaks, totals = [], []
        for ref, distance in zip(stat_refs, paired):
            for at in range(0, ref.shape[0], 8):
                stats = xor_blocks(ref[at : at + 8, :], block, distance)
                peaks.append(stats[0:1])
                totals.append(stats[1:2])
        peak = functools.reduce(jnp.maximum, peaks)
        total = sum(t * jnp.exp(p - peak) for t, p in zip(totals, peaks))
        log_norm = peak + jnp.log(total)
        scores = s_ref[...].reshape(poses, rows, lanes)
        pose_peak = jnp.max(scores, axis=0)
        log_resp = (
            pose_peak + jnp.log(jnp.sum(jnp.exp(scores - pose_peak[None]), axis=0)) - log_norm
        )
        particle_rows = lax.broadcasted_iota(jnp.int32, (resp_ref.shape[0], lanes), 0)
        resp_ref[...] = lax.dot_general(
            (particle_rows == dest_ref[...]).astype(f32),
            log_resp,
            NT,
            precision=HIGHEST,
            preferred_element_type=f32,
        )
        rho = jnp.exp(scores - log_norm[None])
        even = even_lanes((rows, lanes), 1)
        mass_ref[...] = lax.dot_general(
            jnp.where(even, jnp.sum(rho, axis=0), 0.0),
            group_marks(ids_ref[...], groups),
            NT,
            precision=HIGHEST,
            preferred_element_type=f32,
        )
        flat = rho.reshape(poses * rows, lanes)
        even = even_lanes(flat.shape, 1)
        rho_ref[0] = jnp.where(even, flat, 0.0).astype(bf16)
        rho_ref[1] = jnp.where(even, 0.0, flat).astype(bf16)

    rotate_sum(
        rho_ref, w_ref[...], cos_ref, sin_ref, poses, rows, write_slices(out_refs, steps)
    )


def rest_kernel(poses, rows, steps, where_ref, rho_ref, cos_ref, sin_ref, w_ref, *out_refs):
    rotate_sum(
        rho_ref, w_ref[...], cos_ref, sin_ref, poses, rows, write_slices(out_refs, steps)
    )


def slice_specs(tile, steps, poses, lanes):
    def at(j, where):
        return (0, where[j // steps] * steps + lax.rem(j, steps))

    return [
        pl.BlockSpec((poses, tile), at),
        pl.BlockSpec((poses, tile), at),
        pl.BlockSpec((lanes, tile), at),
    ]


def numer_specs(count, tile, steps, rows):
    def spec(s):
        return pl.BlockSpec(
            (2, rows, tile), lambda j, where: (0, 0, jnp.clip(j - s * steps, 0, steps - 1))
        )

    return [spec(s) for s in range(count)]


def pinned(shape):
    return pl.BlockSpec(shape, lambda j, where: (0,) * len(shape))


def responsibilities(
    where, scores, lane_ids, dest, cos_t, sin_t, weighted, stats, paired, block, rows, groups, span, n_rows
):
    poses, lanes = cos_t.shape[0], scores.shape[1]
    tile = tile_of(span)
    steps = span // tile
    count = where.shape[0]
    return pl.pallas_call(
        functools.partial(resp_kernel, poses, block, paired, steps),
        grid_spec=pltpu.PrefetchScalarGridSpec(
            num_scalar_prefetch=1,
            grid=(count * steps,),
            in_specs=[pinned(scores.shape), pinned(lane_ids.shape), pinned(dest.shape)]
            + slice_specs(tile, steps, poses, lanes)
            + [pinned(s.shape) for s in stats],
            out_specs=[
                pinned((n_rows, rows)),
                pinned((2, poses * rows, lanes)),
                pinned((rows, groups)),
            ]
            + numer_specs(count, tile, steps, rows),
        ),
        out_shape=[
            jax.ShapeDtypeStruct((n_rows, rows), f32),
            jax.ShapeDtypeStruct((2, poses * rows, lanes), bf16),
            jax.ShapeDtypeStruct((rows, groups), f32),
        ]
        + [jax.ShapeDtypeStruct((2, rows, span), bf16)] * count,
        compiler_params=params(1),
        cost_estimate=pl.CostEstimate(
            flops=4 * 128 * poses * rows * span * count,
            bytes_accessed=4 * 300 * span * count,
            transcendentals=0,
        ),
        name="responsibilities",
    )(where, scores, lane_ids, dest, cos_t, sin_t, weighted, *stats)


def remaining(where, rho, cos_t, sin_t, weighted, rows, span, dtypes):
    poses, lanes = cos_t.shape[0], weighted.shape[0]
    tile = tile_of(span)
    steps = span // tile
    count = where.shape[0]
    return pl.pallas_call(
        functools.partial(rest_kernel, poses, rows, steps),
        grid_spec=pltpu.PrefetchScalarGridSpec(
            num_scalar_prefetch=1,
            grid=(count * steps,),
            in_specs=[pinned(rho.shape)] + slice_specs(tile, steps, poses, lanes),
            out_specs=numer_specs(count, tile, steps, rows),
        ),
        out_shape=[jax.ShapeDtypeStruct((2, rows, span), d) for d in dtypes],
        compiler_params=params(1),
        cost_estimate=pl.CostEstimate(
            flops=4 * 128 * poses * rows * span * count,
            bytes_accessed=4 * 300 * span * count,
            transcendentals=0,
        ),
        name="remaining",
    )(where, rho, cos_t, sin_t, weighted)


def finish_kernel(count, where_ref, ctf_ref, nw_ref, *refs):
    mass_refs, refs = refs[:count], refs[count:]
    numer_refs, out_ref = refs[:count], refs[count]
    ctf = ctf_ref[...]
    mass = functools.reduce(jnp.add, [ref[...] for ref in mass_refs])
    denom = (
        lax.dot_general(
            mass, ctf * ctf * nw_ref[...], NN, precision=HIGHEST, preferred_element_type=f32
        )
        + prior_precision
    )
    for part in range(2):
        numer = functools.reduce(jnp.add, [ref[part].astype(f32) for ref in numer_refs])
        out_ref[:, part, :] = numer / denom


def finish(where, ctf, noise_row, masses, numers):
    groups = ctf.shape[0]
    _, rows, span = numers[0].shape
    tile = span
    count = len(masses)
    steps = span // tile

    def at(j, where):
        return (0, where[0] * steps + j)

    return pl.pallas_call(
        functools.partial(finish_kernel, count),
        grid_spec=pltpu.PrefetchScalarGridSpec(
            num_scalar_prefetch=1,
            grid=(steps,),
            in_specs=[pl.BlockSpec((groups, tile), at), pl.BlockSpec((1, tile), at)]
            + [pinned((rows, groups))] * count
            + [pl.BlockSpec((2, rows, tile), lambda j, where: (0, 0, j))] * count,
            out_specs=pl.BlockSpec((rows, 2, tile), lambda j, where: (0, 0, j)),
        ),
        out_shape=jax.ShapeDtypeStruct((rows, 2, span), f32),
        compiler_params=params(1),
        name="finish",
    )(where, ctf, noise_row, *masses, *numers)


def swap(values, axis, distance):
    size = lax.axis_size(axis)
    return lax.ppermute(values, axis, [(i, i ^ distance) for i in range(size)])


def local(particles, classes, ctf, noise_weight, group_ids, shifts):
    part_rows, _, freq = particles.shape
    cls_rows = classes.shape[0]
    groups = ctf.shape[0]
    n_cls = lax.axis_size("cls")
    n_img = lax.axis_size("img")
    me_cls = lax.axis_index("cls")
    me_img = lax.axis_index("img")
    span = freq // n_img
    pairwise = n_cls <= 4
    noise_row = noise_weight[None, :]

    own = weigh(particles, ctf, noise_row, group_ids)
    if pairwise:
        ids = [group_ids] + [swap(group_ids, "cls", k) for k in range(1, n_cls)]
        lane_ids = jnp.repeat(jnp.concatenate(ids), 2)[None, :]
        owners = me_cls ^ jnp.arange(n_cls)
        gathered = [[w] + [swap(w, "cls", k) for k in range(1, n_cls)] for w in own]
    else:
        lane_ids = jnp.repeat(lax.all_gather(group_ids, "cls", axis=0, tiled=True), 2)[None, :]
        owners = jnp.arange(n_cls)
        gathered = [[lax.all_gather(w, "cls", axis=0, tiled=True)] for w in own]
    dest = owners[:, None] * part_rows + jnp.arange(part_rows)[None, :]
    dest = jnp.stack([dest, jnp.full_like(dest, -1)], axis=-1).reshape(1, -1).astype(jnp.int32)

    cos_t, sin_t = phase_tables(shifts, freq)
    split = jnp.transpose(classes, (1, 0, 2))
    carried = None
    for c in range(CHUNKS):
        carried = score(
            c, gathered[c], split, cos_t, sin_t, ctf, noise_row, lane_ids, carried
        )
    scores, _, weighted, stat = carried
    if pairwise:
        stats = [stat] + [swap(stat, "cls", k) for k in range(1, n_cls)]
        paired = tuple(range(n_cls))
    else:
        stats = [lax.all_gather(stat, "cls", axis=0, tiled=True)]
        paired = (0,)

    far = list(range(n_img - 1, 0, -1))
    early = max(1, n_img // 2)
    early, late = far[:early], far[early:]

    def slices(distances):
        return jnp.stack([me_img ^ d for d in distances]).astype(jnp.int32)

    log_resp, rho, mass, *first = responsibilities(
        slices(early),
        scores,
        lane_ids,
        dest,
        cos_t,
        sin_t,
        weighted,
        stats,
        paired,
        2 * part_rows,
        cls_rows,
        groups,
        span,
        part_rows * n_cls,
    )
    masses = [mass] + [swap(mass, "img", d) for d in far]
    numers = [swap(part, "img", d) for part, d in zip(first, early)]
    *second, mine = remaining(
        slices(late + [0]),
        rho,
        cos_t,
        sin_t,
        weighted,
        cls_rows,
        span,
        [bf16] * len(late) + [f32],
    )
    numers += [swap(part, "img", d) for part, d in zip(second, late)]
    averages = finish(slices([0]), ctf, noise_row, masses, [mine] + numers)
    return (log_resp, averages)


def solution(mesh):
    placed = (
        P(("groups", "img", "cls"), None, None),
        P(("groups", "cls"), None, None),
        P("groups", None),
        P("groups"),
        P(("groups", "img", "cls")),
        P("groups", None),
    )
    return jax.shard_map(
        local,
        mesh=mesh,
        in_specs=placed,
        out_specs=(P(("groups", "img"), "cls"), P(("groups", "cls"), None, "img")),
        check_vma=False,
    )
```

time: 221 us -> 77.5 us (0.35)
  other arithmetic: 84.3 us -> 2.62 us
  blocking collectives: 35.1 us -> 0 us
  starting transfers between devices: 0.12 us -> 25.4 us
  matrix products: 23.7 us -> 0 us
  Pallas kernels: 0 us -> 23.1 us
  waiting for transfers between devices: 36.7 us -> 14 us
  local copies, waits for them, and re-layouts: 26.8 us -> 10.9 us
  between operations: 13.9 us -> 0.83 us
    another operation x3 -> x2, other arithmetic: 66.7 us -> 0.15 us  [slices(): return jnp.stack([me_img ^ d for d in distances]).astype(jnp.int32)]
    reduce_scatter x2 -> x0, waiting for transfers between devices: 36.6 us -> none  [the longest x1 27.4 us: local(): lax.psum_scatter(numer, 'img', scatter_dimension=2, tiled=True)]
    ppermute x0 -> x18, starting transfers between devices: none -> 25.4 us  [swap(): return lax.ppermute(values, axis, [(i, i ^ distance) for i in range(size)])]
    dot_general x7 -> x0, matrix products: 23.7 us -> none  [the longest x1 11.4 us: local(): lax.dot_general(rho_low, gathered, (((0,), (0,)), ((), ())), preferred_el...]
    pallas_call x0 -> x6, Pallas kernels: none -> 23.1 us  [the longest x2 11.3 us: score(): pl.pallas_call(functools.partial(score_kernel, len(parts), first, last, p...]
    convert_element_type x1 -> x0, local copies, waits for them, and re-layouts: 22.7 us -> none  [local(): templates = jnp.stack([temp_re, temp_im], axis=2).astype(jnp.bfloat16).re...]
    all_gather x1 -> x0, blocking collectives: 14.8 us -> none  [local(): lax.all_gather(marks_low, 'cls', axis=0, tiled=True)]
    ppermute x0 -> x18, waiting for transfers between devices: none -> 14 us  [swap(): return lax.ppermute(values, axis, [(i, i ^ distance) for i in range(size)])]
  transfers between devices with their start and end apart: 3 -> 18, of which waited for: 2 -> 5; matrix products, arithmetic and copies ran while one was open for 49% -> 6% of each run, Pallas kernels for 0% -> 7%
where the time goes in v1:
time: 77.5 us; the launch traced here: 76.9 us
  starting transfers between devices  25.4 us (33%)
  Pallas kernels  23.1 us (30%)
  waiting for transfers between devices  14 us (18%)
  local copies, waits for them, and re-layouts  10.9 us (14%)
  other arithmetic  2.62 us (3%)
  between operations  0.83 us (1%)
    ppermute x18, starting transfers between devices, swap(): return lax.ppermute(values, axis, [(i, i ^ distance) for i in range(size)])  25.4 us
    ppermute x18, waiting for transfers between devices, swap(): return lax.ppermute(values, axis, [(i, i ^ distance) for i in range(size)])  14 us
    pallas_call x2, Pallas kernels, score(): pl.pallas_call(functools.partial(score_kernel, len(parts), first, last, p...  11.3 us
    unnamed x22, local copies, waits for them, and re-layouts  8.69 us
    pallas_call x1, Pallas kernels, responsibilities(): pl.pallas_call(functools.partial(resp_kernel, poses, block, paired, steps...  5.16 us
    pallas_call x1, Pallas kernels, remaining(): pl.pallas_call(functools.partial(rest_kernel, poses, rows, steps), grid_s...  4.66 us
    sin x1, other arithmetic, phase_tables(): return (jnp.cos(angle), jnp.sin(angle))  1.65 us
  transfers between devices with their start and end apart: 18, of which 5 were waited for; matrix products, arithmetic and copies ran while one was open for 6% of the time, Pallas kernels for 7%

profile of v1, /device:TPU:0, one launch (start us, length us, event | category | flops | bytes accessed | tf_op | source)
XLA Modules:
  0.0 76.9 jit_solution(18313657701510915501)
XLA Ops:
  0.6 0.7 broadcast_in_dim.4.nw_ref
  1.4 1.1 %reshape.71.p_ref = bf16[32,4608]{1,0:T(8,128)(2,1)S(1)} reshape(bf16[16,2,4608]{2,1,0:T(2,128)(2,1)} %param.6) | data formatting | bytes 589824 | tf_op jit(solution)/shard_map/reshape | solution.py:64
  2.5 0.0 copy-start
  2.5 1.3 %copy-done = f32[64,4608]{1,0:T(8,128)S(1)} copy-done((f32[64,4608]{1,0:T(8,128)S(1)}, f32[64,4608]{1,0:T(8,128)}, u32[]{:S(2)}) %copy-start) | copy-done | bytes 1179672
  3.7 1.0 %weigh.1 = (bf16[32,2304]{1,0:T(8,128)(2,1)S(1)}, bf16[32,2304]{1,0:T(8,128)(2,1)S(1)}) custom-call(s32[16]{0:T(128)} %ids_ref.1, bf16[32,4608]{1,0:T(8,128)(2,1)S(1)} %reshape.71.p_ref, f32[64,4608]{1,0:T(8,128)S(1)} %copy-done, f32[1,4608]{1,0:T(1,128)S(1)} %broadcast_in_dim.4.nw_ref), custom_call_target="tpu_custom_call" | custom-call | flops 294912 | bytes 1769472 | tf_op jit(solution)/shard_map/weigh/pallas_call | solution.py:66
  4.7 0.0 copy-start.1
  4.8 3.1 %collective-permute-start.6 = (bf16[32,2304]{1,0:T(8,128)(2,1)S(1)}, bf16[32,2304]{1,0:T(8,128)(2,1)S(1)}, u32[]{:S(2)}, u32[]{:S(2)}) collective-permute-start(bf16[32,2304]{1,0:T(8,128)(2,1)S(1)} %get-tuple-element.18.refs_0_), channel_id=1, source_target_pairs={{0,4},{4,0},{8,12},{12,8},{1,5},{5,1},{9,13},{13,9},{2,6},{6,2},{1... | collective-permute-start | bytes 442376 | tf_op jit(solution)/shard_map/ppermute | solution.py:454
  7.8 2.6 %collective-permute-start.7 = (bf16[32,2304]{1,0:T(8,128)(2,1)S(1)}, bf16[32,2304]{1,0:T(8,128)(2,1)}, u32[]{:S(2)}, u32[]{:S(2)}) collective-permute-start(bf16[32,2304]{1,0:T(8,128)(2,1)S(1)} %get-tuple-element.18.refs_0_), channel_id=1, source_target_pairs={{0,8},{4,12},{8,0},{12,4},{1,9},{5,13},{9,1},{13,5},{2,10},{6,14},... | collective-permute-start | bytes 442376 | tf_op jit(solution)/shard_map/ppermute | solution.py:454
  10.4 0.9 %collective-permute-start = (s32[16]{0:T(128)}, s32[16]{0:T(128)S(1)}, u32[]{:S(2)}, u32[]{:S(2)}) collective-permute-start(s32[16]{0:T(128)} %ids_ref.1), channel_id=1, source_target_pairs={{0,4},{4,0},{8,12},{12,8},{1,5},{5,1},{9,13},{13,9},{2,6},{6,2},{1... | collective-permute-start | bytes 200 | tf_op jit(solution)/shard_map/ppermute | solution.py:454
  11.3 3.5 %collective-permute-start.1 = (s32[16]{0:T(128)}, s32[16]{0:T(128)S(1)}, u32[]{:S(2)}, u32[]{:S(2)}) collective-permute-start(s32[16]{0:T(128)} %ids_ref.1), channel_id=1, source_target_pairs={{0,8},{4,12},{8,0},{12,4},{1,9},{5,13},{9,1},{13,5},{2,10},{6,14},... | collective-permute-start | bytes 200 | tf_op jit(solution)/shard_map/ppermute | solution.py:454
  14.9 1.6 %fusion = (f32[24,4608]{1,0:T(8,128)S(1)}, f32[24,4608]{1,0:T(8,128)S(1)}) fusion(f32[4608]{0:T(1024)S(1)} %get-tuple-element.41, f32[24]{0:T(128)S(1)} %get-tuple-element.39, f32[4608]{0:T(1024)S(1)} %get-tuple-element.40, f32[24]{0:T(128)S(1)} %get-tuple-element.38), kind=kLoop, calls=%fused_computation.2 | loop fusion | flops 442368 | bytes 921792 | tf_op jit(solution)/shard_map/sin | solution.py:36
  16.5 0.1 iota_add_fusion
  16.6 0.1 pad_add_fusion.where_ref
  16.7 1.1 %copy.14 = bf16[32,2,4608]{2,0,1:T(8,128)(2,1)S(1)} copy(bf16[32,2,4608]{2,1,0:T(2,128)(2,1)} %param.7) | data formatting | bytes 1179648 | tf_op args[1]
  17.8 2.0 %collective-permute-start.2 = (s32[16]{0:T(128)}, s32[16]{0:T(128)S(1)}, u32[]{:S(2)}, u32[]{:S(2)}) collective-permute-start(s32[16]{0:T(128)} %ids_ref.1), channel_id=1, source_target_pairs={{0,12},{4,8},{8,4},{12,0},{1,13},{5,9},{9,5},{13,1},{2,14},{6,10},... | collective-permute-start | bytes 200 | tf_op jit(solution)/shard_map/ppermute | solution.py:454
  19.8 3.7 %collective-permute-done.1 = s32[16]{0:T(128)S(1)} collective-permute-done((s32[16]{0:T(128)}, s32[16]{0:T(128)S(1)}, u32[]{:S(2)}, u32[]{:S(2)}) %collective-permute-start.1) | collective-permute-done | bytes 96 | tf_op jit(solution)/shard_map/ppermute | solution.py:454
  23.6 3.0 %collective-permute-start.4 = (bf16[32,2304]{1,0:T(8,128)(2,1)S(1)}, bf16[32,2304]{1,0:T(8,128)(2,1)S(1)}, u32[]{:S(2)}, u32[]{:S(2)}) collective-permute-start(bf16[32,2304]{1,0:T(8,128)(2,1)S(1)} %get-tuple-element.17.refs_0_), channel_id=1, source_target_pairs={{0,8},{4,12},{8,0},{12,4},{1,9},{5,13},{9,1},{13,5},{2,10},{6,14},... | collective-permute-start | bytes 442376 | tf_op jit(solution)/shard_map/ppermute | solution.py:454
  26.6 0.7 copy-done.7
  27.3 1.4 %collective-permute-start.5 = (bf16[32,2304]{1,0:T(8,128)(2,1)S(1)}, bf16[32,2304]{1,0:T(8,128)(2,1)S(1)}, u32[]{:S(2)}, u32[]{:S(2)}) collective-permute-start(bf16[32,2304]{1,0:T(8,128)(2,1)S(1)} %get-tuple-element.17.refs_0_), channel_id=1, source_target_pairs={{0,12},{4,8},{8,4},{12,0},{1,13},{5,9},{9,5},{13,1},{2,14},{6,10},... | collective-permute-start | bytes 442376 | tf_op jit(solution)/shard_map/ppermute | solution.py:454
  28.6 0.7 pad_add_fusion.1
  29.4 0.1 broadcast_in_dim.5
  29.5 0.1 broadcast_in_dim_reshape.3.ids_ref
  29.6 0.0 copy-start.8
  29.6 0.9 %copy-done.8 = bf16[32,2304]{1,0:T(8,128)(2,1)S(1)} copy-done((bf16[32,2304]{1,0:T(8,128)(2,1)S(1)}, bf16[32,2304]{1,0:T(8,128)(2,1)}, u32[]{:S(2)}) %copy-start.8) | copy-done | bytes 147480
  30.5 5.4 %score0.1 = (f32[768,128]{1,0:T(8,128)S(1)}, f32[32,64]{1,0:T(8,128)S(1)}, bf16[128,4608]{1,0:T(8,128)(2,1)S(1)}) custom-call(bf16[2,32,4608]{2,1,0:T(8,128)(2,1)S(1)} %bitcast.11, f32[24,4608]{1,0:T(8,128)S(1)} %get-tuple-element.37.cos_ref, f32[24,4608]{1,0:T(8,128)S(1)} %get-tuple-element.36.sin_ref, f32[64,4608]{1,0:T(8,128)S(1)} %copy-done.1, ...), custom_call_target="tpu_custom_call" | custom-call | flops 905969664 | bytes 2764800 | tf_op jit(solution)/shard_map/score0/pallas_call | solution.py:205
  36.0 0.9 %collective-permute-done.4.refs_2_ = bf16[32,2304]{1,0:T(8,128)(2,1)S(1)} collective-permute-done((bf16[32,2304]{1,0:T(8,128)(2,1)S(1)}, bf16[32,2304]{1,0:T(8,128)(2,1)S(1)}, u32[]{:S(2)}, u32[]{:S(2)}) %collective-permute-start.4) | collective-permute-done | bytes 147488 | tf_op jit(solution)/shard_map/ppermute | solution.py:454
  36.9 5.9 %score1.1 = (f32[768,128]{1,0:T(8,128)S(1)}, f32[32,64]{1,0:T(8,128)}, bf16[128,4608]{1,0:T(8,128)(2,1)S(1)}, f32[8,128]{1,0:T(8,128)S(1)}) custom-call(bf16[2,32,4608]{2,1,0:T(8,128)(2,1)S(1)} %bitcast.12, f32[24,4608]{1,0:T(8,128)S(1)} %get-tuple-element.37.cos_ref, f32[24,4608]{1,0:T(8,128)S(1)} %get-tuple-element.36.sin_ref, ...), custom_call_target="tpu_custom_call", output_to_operand_aliasing={{2}: (12, {})} | custom-call | flops 905969664 | bytes 2764800 | tf_op jit(solution)/shard_map/score1/pallas_call | solution.py:205
  42.7 1.0 %copy-done.2 = bf16[128,4608]{1,0:T(8,128)(2,1)} copy-done((bf16[128,4608]{1,0:T(8,128)(2,1)}, bf16[128,4608]{1,0:T(8,128)(2,1)S(1)}, u32[]{:S(2)}) %copy-start.2) | copy-done | bytes 1179672
  43.7 0.7 copy-done.5
  44.5 3.1 %collective-permute-start.10 = (f32[8,128]{1,0:T(8,128)S(1)}, f32[8,128]{1,0:T(8,128)S(1)}, u32[]{:S(2)}, u32[]{:S(2)}) collective-permute-start(f32[8,128]{1,0:T(8,128)S(1)} %get-tuple-element.24.refs_0_), channel_id=1, source_target_pairs={{0,8},{4,12},{8,0},{12,4},{1,9},{5,13},{9,1},{13,5},{2,10},{6,14},... | collective-permute-start | bytes 12296 | tf_op jit(solution)/shard_map/ppermute | solution.py:454
  47.5 1.5 %collective-permute-start.11 = (f32[8,128]{1,0:T(8,128)S(1)}, f32[8,128]{1,0:T(8,128)S(1)}, u32[]{:S(2)}, u32[]{:S(2)}) collective-permute-start(f32[8,128]{1,0:T(8,128)S(1)} %get-tuple-element.24.refs_0_), channel_id=1, source_target_pairs={{0,12},{4,8},{8,4},{12,0},{1,13},{5,9},{9,5},{13,1},{2,14},{6,10},... | collective-permute-start | bytes 12296 | tf_op jit(solution)/shard_map/ppermute | solution.py:454
  49.0 0.1 pad_add_fusion.2.where_ref
  49.1 0.1 reshape.72.dest_ref
  49.2 3.7 %collective-permute-done.11.refs_3_ = f32[8,128]{1,0:T(8,128)S(1)} collective-permute-done((f32[8,128]{1,0:T(8,128)S(1)}, f32[8,128]{1,0:T(8,128)S(1)}, u32[]{:S(2)}, u32[]{:S(2)}) %collective-permute-start.11) | collective-permute-done | bytes 4128 | tf_op jit(solution)/shard_map/ppermute | solution.py:454
  53.0 1.3 %copy-done.3 = bf16[128,4608]{1,0:T(8,128)(2,1)S(1)} copy-done((bf16[128,4608]{1,0:T(8,128)(2,1)S(1)}, bf16[128,4608]{1,0:T(8,128)(2,1)}, u32[]{:S(2)}) %copy-start.3) | copy-done | bytes 1179672
  54.2 1.0 %copy-done.6 = f32[768,128]{1,0:T(8,128)S(1)} copy-done((f32[768,128]{1,0:T(8,128)S(1)}, f32[768,128]{1,0:T(8,128)}, u32[]{:S(2)}) %copy-start.6) | copy-done | bytes 393240
  55.2 5.2 %responsibilities.1 = (f32[64,32]{1,0:T(8,128)S(1)}, bf16[2,768,128]{2,1,0:T(8,128)(2,1)S(1)}, f32[32,64]{1,0:T(8,128)S(1)}, bf16[2,32,1152]{2,1,0:T(8,128)(2,1)S(1)}, bf16[2,32,1152]{2,1,0:T(8,128)(2,1)S(1)}) custom-call(s32[2]{0:T(128)S(1)} %pad_add_fusion.where_ref, f32[768,128]{1,0:T(8,128)S(1)} %copy-done.6, ...), custom_call_target="tpu_custom_call" | custom-call | flops 905969664 | bytes 2764800 | tf_op jit(solution)/shard_map/responsibilities/pallas_call | solution.py:355
  60.4 4.7 %remaining.1 = (bf16[2,32,1152]{2,1,0:T(8,128)(2,1)S(1)}, f32[2,32,1152]{2,1,0:T(8,128)S(1)}) custom-call(s32[2]{0:T(128)S(1)} %pad_add_fusion.2.where_ref, bf16[2,768,128]{2,1,0:T(8,128)(2,1)S(1)} %get-tuple-element.27.rho_ref, f32[24,4608]{1,0:T(8,128)S(1)} %get-tuple-element.37.cos_ref, f32[24,4608]{1,0:T(8,128)S(1)} %get-tuple-element.36.sin_ref, ...), custom_call_target="tpu_custom_call" | custom-call | flops 905969664 | bytes 2764800 | tf_op jit(solution)/shard_map/remaining/pallas_call | solution.py:391
  65.1 0.1 collective-permute-start.17
  65.1 1.6 %collective-permute-start.15 = (bf16[2,32,1152]{2,1,0:T(8,128)(2,1)S(1)}, bf16[2,32,1152]{2,1,0:T(8,128)(2,1)S(1)}, u32[]{:S(2)}, u32[]{:S(2)}) collective-permute-start(bf16[2,32,1152]{2,1,0:T(8,128)(2,1)S(1)} %get-tuple-element.29), channel_id=1, source_target_pairs={{0,3},{1,2},{2,1},{3,0},{4,7},{5,6},{6,5},{7,4},{8,11},{9,10},{10,... | collective-permute-start | bytes 442376 | tf_op jit(solution)/shard_map/ppermute | solution.py:454
  66.8 0.5 collective-permute-start.16
  67.3 0.9 %collective-permute-start.12 = (f32[32,64]{1,0:T(8,128)S(1)}, f32[32,64]{1,0:T(8,128)S(1)}, u32[]{:S(2)}, u32[]{:S(2)}) collective-permute-start(f32[32,64]{1,0:T(8,128)S(1)} %get-tuple-element.26.refs_0_), channel_id=1, source_target_pairs={{0,3},{1,2},{2,1},{3,0},{4,7},{5,6},{6,5},{7,4},{8,11},{9,10},{10,... | collective-permute-start | bytes 24584 | tf_op jit(solution)/shard_map/ppermute | solution.py:454
  68.2 0.6 collective-permute-start.13
  68.8 5.5 %collective-permute-done.12.refs_1_ = f32[32,64]{1,0:T(8,128)S(1)} collective-permute-done((f32[32,64]{1,0:T(8,128)S(1)}, f32[32,64]{1,0:T(8,128)S(1)}, u32[]{:S(2)}, u32[]{:S(2)}) %collective-permute-start.12) | collective-permute-done | bytes 8224 | tf_op jit(solution)/shard_map/ppermute | solution.py:454
  74.3 0.7 collective-permute-start.14
  75.0 0.7 copy.12
  75.7 0.2 collective-permute-done.14.refs_3_
  75.8 1.0 %finish.1 = f32[32,2,1152]{2,1,0:T(2,128)} custom-call(s32[1]{0:T(128)} %bitcast.5.where_ref, f32[64,4608]{1,0:T(8,128)S(1)} %copy-done.1, f32[1,4608]{1,0:T(1,128)S(1)} %broadcast_in_dim.4.nw_ref, f32[32,64]{1,0:T(8,128)S(1)} %get-tuple-element.26.refs_0_, f32[32,64]{1,0:T(8,128)S(1)} %collective-permute-done.12.refs_1_, ...), custom_call_target="tpu_custom_call" | custom-call | tf_op jit(solution)/shard_map/finish/pallas_call | solution.py:436
  (30 shorter events, 0.1 us)
Async XLA Ops:
  0.6 14.2 %copy-start.9 = (s32[24,2]{0,1:T(2,128)S(1)}, s32[24,2]{0,1:T(2,128)}, u32[]{:S(2)}) copy-start(s32[24,2]{0,1:T(2,128)} %param.11) | copy-start | bytes 580
  2.5 1.3 %copy-start = (f32[64,4608]{1,0:T(8,128)S(1)}, f32[64,4608]{1,0:T(8,128)}, u32[]{:S(2)}) copy-start(f32[64,4608]{1,0:T(8,128)} %ctf_ref.7) | copy-start | bytes 3538948
  4.7 24.9 %copy-start.1 = (f32[64,4608]{1,0:T(8,128)S(1)}, f32[64,4608]{1,0:T(8,128)}, u32[]{:S(2)}) copy-start(f32[64,4608]{1,0:T(8,128)} %ctf_ref.7) | copy-start | bytes 3538948
  4.8 21.9 %collective-permute-start.6 = (bf16[32,2304]{1,0:T(8,128)(2,1)S(1)}, bf16[32,2304]{1,0:T(8,128)(2,1)S(1)}, u32[]{:S(2)}, u32[]{:S(2)}) collective-permute-start(bf16[32,2304]{1,0:T(8,128)(2,1)S(1)} %get-tuple-element.18.refs_0_), channel_id=1, source_target_pairs={{0,4},{4,0},{8,12},{12,8},{1,5},{5,1},{9,13},{13,9},{2,6},{6,2},{1... | collective-permute-start | bytes 442376 | tf_op jit(solution)/shard_map/ppermute | solution.py:454
  7.8 21.8 %collective-permute-start.7 = (bf16[32,2304]{1,0:T(8,128)(2,1)S(1)}, bf16[32,2304]{1,0:T(8,128)(2,1)}, u32[]{:S(2)}, u32[]{:S(2)}) collective-permute-start(bf16[32,2304]{1,0:T(8,128)(2,1)S(1)} %get-tuple-element.18.refs_0_), channel_id=1, source_target_pairs={{0,8},{4,12},{8,0},{12,4},{1,9},{5,13},{9,1},{13,5},{2,10},{6,14},... | collective-permute-start | bytes 442376 | tf_op jit(solution)/shard_map/ppermute | solution.py:454
  10.4 19.2 %collective-permute-start.8 = (bf16[32,2304]{1,0:T(8,128)(2,1)S(1)}, bf16[32,2304]{1,0:T(8,128)(2,1)}, u32[]{:S(2)}, u32[]{:S(2)}) collective-permute-start(bf16[32,2304]{1,0:T(8,128)(2,1)S(1)} %get-tuple-element.18.refs_0_), channel_id=1, source_target_pairs={{0,12},{4,8},{8,4},{12,0},{1,13},{5,9},{9,5},{13,1},{2,14},{6,10},... | collective-permute-start | bytes 442376 | tf_op jit(solution)/shard_map/ppermute | solution.py:454
  10.4 7.4 %collective-permute-start = (s32[16]{0:T(128)}, s32[16]{0:T(128)S(1)}, u32[]{:S(2)}, u32[]{:S(2)}) collective-permute-start(s32[16]{0:T(128)} %ids_ref.1), channel_id=1, source_target_pairs={{0,4},{4,0},{8,12},{12,8},{1,5},{5,1},{9,13},{13,9},{2,6},{6,2},{1... | collective-permute-start | bytes 200 | tf_op jit(solution)/shard_map/ppermute | solution.py:454
  11.3 12.3 %collective-permute-start.1 = (s32[16]{0:T(128)}, s32[16]{0:T(128)S(1)}, u32[]{:S(2)}, u32[]{:S(2)}) collective-permute-start(s32[16]{0:T(128)} %ids_ref.1), channel_id=1, source_target_pairs={{0,8},{4,12},{8,0},{12,4},{1,9},{5,13},{9,1},{13,5},{2,10},{6,14},... | collective-permute-start | bytes 200 | tf_op jit(solution)/shard_map/ppermute | solution.py:454
  17.8 5.8 %collective-permute-start.2 = (s32[16]{0:T(128)}, s32[16]{0:T(128)S(1)}, u32[]{:S(2)}, u32[]{:S(2)}) collective-permute-start(s32[16]{0:T(128)} %ids_ref.1), channel_id=1, source_target_pairs={{0,12},{4,8},{8,4},{12,0},{1,13},{5,9},{9,5},{13,1},{2,14},{6,10},... | collective-permute-start | bytes 200 | tf_op jit(solution)/shard_map/ppermute | solution.py:454
  23.6 12.4 %collective-permute-start.3 = (bf16[32,2304]{1,0:T(8,128)(2,1)S(1)}, bf16[32,2304]{1,0:T(8,128)(2,1)S(1)}, u32[]{:S(2)}, u32[]{:S(2)}) collective-permute-start(bf16[32,2304]{1,0:T(8,128)(2,1)S(1)} %get-tuple-element.17.refs_0_), channel_id=1, source_target_pairs={{0,4},{4,0},{8,12},{12,8},{1,5},{5,1},{9,13},{13,9},{2,6},{6,2},{1... | collective-permute-start | bytes 442376 | tf_op jit(solution)/shard_map/ppermute | solution.py:454
  23.6 13.3 %collective-permute-start.4 = (bf16[32,2304]{1,0:T(8,128)(2,1)S(1)}, bf16[32,2304]{1,0:T(8,128)(2,1)S(1)}, u32[]{:S(2)}, u32[]{:S(2)}) collective-permute-start(bf16[32,2304]{1,0:T(8,128)(2,1)S(1)} %get-tuple-element.17.refs_0_), channel_id=1, source_target_pairs={{0,8},{4,12},{8,0},{12,4},{1,9},{5,13},{9,1},{13,5},{2,10},{6,14},... | collective-permute-start | bytes 442376 | tf_op jit(solution)/shard_map/ppermute | solution.py:454
  26.6 0.7 copy-start.7
  27.3 9.6 %collective-permute-start.5 = (bf16[32,2304]{1,0:T(8,128)(2,1)S(1)}, bf16[32,2304]{1,0:T(8,128)(2,1)S(1)}, u32[]{:S(2)}, u32[]{:S(2)}) collective-permute-start(bf16[32,2304]{1,0:T(8,128)(2,1)S(1)} %get-tuple-element.17.refs_0_), channel_id=1, source_target_pairs={{0,12},{4,8},{8,4},{12,0},{1,13},{5,9},{9,5},{13,1},{2,14},{6,10},... | collective-permute-start | bytes 442376 | tf_op jit(solution)/shard_map/ppermute | solution.py:454
  29.6 0.9 %copy-start.8 = (bf16[32,2304]{1,0:T(8,128)(2,1)S(1)}, bf16[32,2304]{1,0:T(8,128)(2,1)}, u32[]{:S(2)}) copy-start(bf16[32,2304]{1,0:T(8,128)(2,1)} %copy-done.7) | copy-start | bytes 442372
  42.7 1.0 %copy-start.2 = (bf16[128,4608]{1,0:T(8,128)(2,1)}, bf16[128,4608]{1,0:T(8,128)(2,1)S(1)}, u32[]{:S(2)}) copy-start(bf16[128,4608]{1,0:T(8,128)(2,1)S(1)} %get-tuple-element.23.w_ref) | copy-start | bytes 3538948
  43.7 0.7 copy-start.5
  44.5 4.7 %collective-permute-start.10 = (f32[8,128]{1,0:T(8,128)S(1)}, f32[8,128]{1,0:T(8,128)S(1)}, u32[]{:S(2)}, u32[]{:S(2)}) collective-permute-start(f32[8,128]{1,0:T(8,128)S(1)} %get-tuple-element.24.refs_0_), channel_id=1, source_target_pairs={{0,8},{4,12},{8,0},{12,4},{1,9},{5,13},{9,1},{13,5},{2,10},{6,14},... | collective-permute-start | bytes 12296 | tf_op jit(solution)/shard_map/ppermute | solution.py:454
  47.5 5.4 %collective-permute-start.11 = (f32[8,128]{1,0:T(8,128)S(1)}, f32[8,128]{1,0:T(8,128)S(1)}, u32[]{:S(2)}, u32[]{:S(2)}) collective-permute-start(f32[8,128]{1,0:T(8,128)S(1)} %get-tuple-element.24.refs_0_), channel_id=1, source_target_pairs={{0,12},{4,8},{8,4},{12,0},{1,13},{5,9},{9,5},{13,1},{2,14},{6,10},... | collective-permute-start | bytes 12296 | tf_op jit(solution)/shard_map/ppermute | solution.py:454
  49.0 4.0 %collective-permute-start.9 = (f32[8,128]{1,0:T(8,128)S(1)}, f32[8,128]{1,0:T(8,128)S(1)}, u32[]{:S(2)}, u32[]{:S(2)}) collective-permute-start(f32[8,128]{1,0:T(8,128)S(1)} %get-tuple-element.24.refs_0_), channel_id=1, source_target_pairs={{0,4},{4,0},{8,12},{12,8},{1,5},{5,1},{9,13},{13,9},{2,6},{6,2},{1... | collective-permute-start | bytes 12296 | tf_op jit(solution)/shard_map/ppermute | solution.py:454
  53.0 1.3 %copy-start.3 = (bf16[128,4608]{1,0:T(8,128)(2,1)S(1)}, bf16[128,4608]{1,0:T(8,128)(2,1)}, u32[]{:S(2)}) copy-start(bf16[128,4608]{1,0:T(8,128)(2,1)} %copy-done.2) | copy-start | bytes 3538948
  54.2 1.0 %copy-start.6 = (f32[768,128]{1,0:T(8,128)S(1)}, f32[768,128]{1,0:T(8,128)}, u32[]{:S(2)}) copy-start(f32[768,128]{1,0:T(8,128)} %copy-done.5) | copy-start | bytes 1179652
  55.2 5.2 %copy-start.4 = (bf16[128,4608]{1,0:T(8,128)(2,1)S(1)}, bf16[128,4608]{1,0:T(8,128)(2,1)}, u32[]{:S(2)}) copy-start(bf16[128,4608]{1,0:T(8,128)(2,1)} %copy-done.2) | copy-start | bytes 3538948
  65.1 10.8 %collective-permute-start.17 = (bf16[2,32,1152]{2,1,0:T(8,128)(2,1)S(1)}, bf16[2,32,1152]{2,1,0:T(8,128)(2,1)S(1)}, u32[]{:S(2)}, u32[]{:S(2)}) collective-permute-start(bf16[2,32,1152]{2,1,0:T(8,128)(2,1)S(1)} %get-tuple-element.31), channel_id=1, source_target_pairs={{0,1},{1,0},{2,3},{3,2},{4,5},{5,4},{6,7},{7,6},{8,9},{9,8},{10,11... | collective-permute-start | bytes 442376 | tf_op jit(solution)/shard_map/ppermute | solution.py:454
  65.1 10.7 %collective-permute-start.15 = (bf16[2,32,1152]{2,1,0:T(8,128)(2,1)S(1)}, bf16[2,32,1152]{2,1,0:T(8,128)(2,1)S(1)}, u32[]{:S(2)}, u32[]{:S(2)}) collective-permute-start(bf16[2,32,1152]{2,1,0:T(8,128)(2,1)S(1)} %get-tuple-element.29), channel_id=1, source_target_pairs={{0,3},{1,2},{2,1},{3,0},{4,7},{5,6},{6,5},{7,4},{8,11},{9,10},{10,... | collective-permute-start | bytes 442376 | tf_op jit(solution)/shard_map/ppermute | solution.py:454
  66.8 9.1 %collective-permute-start.16 = (bf16[2,32,1152]{2,1,0:T(8,128)(2,1)S(1)}, bf16[2,32,1152]{2,1,0:T(8,128)(2,1)S(1)}, u32[]{:S(2)}, u32[]{:S(2)}) collective-permute-start(bf16[2,32,1152]{2,1,0:T(8,128)(2,1)S(1)} %get-tuple-element.30), channel_id=1, source_target_pairs={{0,2},{1,3},{2,0},{3,1},{4,6},{5,7},{6,4},{7,5},{8,10},{9,11},{10,... | collective-permute-start | bytes 442376 | tf_op jit(solution)/shard_map/ppermute | solution.py:454
  67.3 7.0 %collective-permute-start.12 = (f32[32,64]{1,0:T(8,128)S(1)}, f32[32,64]{1,0:T(8,128)S(1)}, u32[]{:S(2)}, u32[]{:S(2)}) collective-permute-start(f32[32,64]{1,0:T(8,128)S(1)} %get-tuple-element.26.refs_0_), channel_id=1, source_target_pairs={{0,3},{1,2},{2,1},{3,0},{4,7},{5,6},{6,5},{7,4},{8,11},{9,10},{10,... | collective-permute-start | bytes 24584 | tf_op jit(solution)/shard_map/ppermute | solution.py:454
  68.2 7.5 %collective-permute-start.13 = (f32[32,64]{1,0:T(8,128)S(1)}, f32[32,64]{1,0:T(8,128)S(1)}, u32[]{:S(2)}, u32[]{:S(2)}) collective-permute-start(f32[32,64]{1,0:T(8,128)S(1)} %get-tuple-element.26.refs_0_), channel_id=1, source_target_pairs={{0,2},{1,3},{2,0},{3,1},{4,6},{5,7},{6,4},{7,5},{8,10},{9,11},{10,... | collective-permute-start | bytes 24584 | tf_op jit(solution)/shard_map/ppermute | solution.py:454
  74.3 1.5 %collective-permute-start.14 = (f32[32,64]{1,0:T(8,128)S(1)}, f32[32,64]{1,0:T(8,128)S(1)}, u32[]{:S(2)}, u32[]{:S(2)}) collective-permute-start(f32[32,64]{1,0:T(8,128)S(1)} %get-tuple-element.26.refs_0_), channel_id=1, source_target_pairs={{0,1},{1,0},{2,3},{3,2},{4,5},{5,4},{6,7},{7,6},{8,9},{9,8},{10,11... | collective-permute-start | bytes 24584 | tf_op jit(solution)/shard_map/ppermute | solution.py:454

commit v2 on v0

v2 whole, which is shorter than its diff:
```python
import functools

import jax
import jax.numpy as jnp
from jax import lax
from jax.experimental import pallas as pl
from jax.experimental.pallas import tpu as pltpu
from jax.sharding import PartitionSpec as P

BOX = 128
CHUNKS = 2
LANES = 128
VMEM_LIMIT = 24 * 1024 * 1024

prior_precision = 0.02

NT = (((1,), (1,)), ((), ()))
NN = (((1,), (0,)), ((), ()))
HIGHEST = lax.Precision.HIGHEST
f32 = jnp.float32
bf16 = jnp.bfloat16

SMEM = pl.BlockSpec(memory_space=pltpu.SMEM)
VMEM = pl.BlockSpec(memory_space=pltpu.VMEM)
ANY = pl.BlockSpec(memory_space=pl.ANY)


def phase_tables(shifts, freq):
    index = jnp.arange(freq)
    along_y = (index // BOX).astype(f32)
    along_x = (index % BOX - BOX // 2).astype(f32)
    angle = (
        2.0
        * jnp.pi
        / BOX
        * (
            shifts[:, 0:1].astype(f32) * along_x[None, :]
            + shifts[:, 1:2].astype(f32) * along_y[None, :]
        )
    )
    return (jnp.cos(angle), jnp.sin(angle))


def call(kernel, name, in_specs, out_shape, operands, scratch=(), flops=0, moved=0, out_specs=None):
    return pl.pallas_call(
        kernel,
        in_specs=in_specs,
        out_specs=[VMEM] * len(out_shape) if out_specs is None else out_specs,
        out_shape=out_shape,
        scratch_shapes=list(scratch),
        compiler_params=pltpu.CompilerParams(vmem_limit_bytes=VMEM_LIMIT),
        cost_estimate=pl.CostEstimate(flops=flops, bytes_accessed=moved, transcendentals=0),
        name=name,
    )(*operands)


def even_index(shape, axis):
    return lax.rem(lax.broadcasted_iota(jnp.int32, shape, axis), 2) == 0


def weigh_kernel(ids_ref, p_ref, ctf_ref, nw_ref, *refs):
    out_refs, (rows_ref, scale_ref, sem) = refs[:-3], refs[-3:]
    count, _, freq = p_ref.shape
    copies = [
        pltpu.make_async_copy(
            ctf_ref.at[pl.ds(ids_ref[n], 1), :], rows_ref.at[pl.ds(n, 1), :], sem.at[n]
        )
        for n in range(count)
    ]
    for copy in copies:
        copy.start()
    row = lax.broadcasted_iota(jnp.int32, (2 * count, LANES), 0) // 2
    ids = jnp.zeros((2 * count, LANES), f32)
    for n in range(count):
        ids = jnp.where(row == n, ids_ref[n].astype(f32), ids)
    values = p_ref[...].astype(f32).reshape(2 * count, freq)
    for copy in copies:
        copy.wait()
    scale = rows_ref[...] * nw_ref[...]
    for n in range(count):
        scale_ref[2 * n : 2 * n + 2, :] = jnp.broadcast_to(scale[n : n + 1], (2, freq))
    weighted = (values * scale_ref[...]).astype(bf16)
    chunk = freq // len(out_refs)
    for c, out_ref in enumerate(out_refs):
        out_ref[:, :chunk] = weighted[:, c * chunk : (c + 1) * chunk]
    out_refs[0][:, chunk:] = ids.astype(bf16)


def weigh(particles, ctf, noise_weight, group_ids):
    rows, _, freq = particles.shape
    chunk = freq // CHUNKS
    return call(
        weigh_kernel,
        "weigh",
        [SMEM, VMEM, ANY, VMEM],
        [
            jax.ShapeDtypeStruct((2 * rows, chunk + (LANES if c == 0 else 0)), bf16)
            for c in range(CHUNKS)
        ],
        (group_ids, particles, pltpu.with_memory_space_constraint(ctf, pltpu.HBM), noise_weight),
        [
            pltpu.VMEM((rows, freq), f32),
            pltpu.VMEM((2 * rows, freq), f32),
            pltpu.SemaphoreType.DMA((rows,)),
        ],
        flops=4 * rows * freq,
        moved=16 * rows * freq,
    )


def template_kernel(cls_ref, cos_ref, sin_ref, ctf_ref, nw_ref, temp_ref, pow_ref):
    _, rows, freq = cls_ref.shape
    poses = cos_ref.shape[0]

    @pl.loop(0, freq // LANES)
    def _(t):
        at = pl.ds(pl.multiple_of(t * LANES, LANES), LANES)
        later = pl.ds(pl.multiple_of(freq + t * LANES, LANES), LANES)
        re = cls_ref[0, :, at].astype(f32)
        im = cls_ref[1, :, at].astype(f32)
        for r in range(poses):
            cos_r = cos_ref[r : r + 1, at]
            sin_r = sin_ref[r : r + 1, at]
            temp_ref[r * rows : (r + 1) * rows, at] = (re * cos_r - im * sin_r).astype(bf16)
            temp_ref[r * rows : (r + 1) * rows, later] = (re * sin_r + im * cos_r).astype(bf16)

    cut = freq // 4
    power = jnp.zeros(pow_ref.shape, f32)
    for q in range(4):
        at = slice(q * cut, (q + 1) * cut)
        re = cls_ref[0, :, at].astype(f32)
        im = cls_ref[1, :, at].astype(f32)
        ctf = ctf_ref[:, at]
        power += lax.dot_general(
            re * re + im * im,
            ctf * ctf * nw_ref[:, at],
            NT,
            precision=HIGHEST,
            preferred_element_type=f32,
        )
    pow_ref[...] = power


def build_templates(split, cos_t, sin_t, ctf, noise_weight):
    _, rows, freq = split.shape
    poses, groups = cos_t.shape[0], ctf.shape[0]
    return call(
        template_kernel,
        "templates",
        [VMEM] * 5,
        [
            pltpu.VMEM((poses * rows, 2 * freq), bf16),
            jax.ShapeDtypeStruct((rows, groups), f32),
        ],
        (split, cos_t, sin_t, ctf, noise_weight),
        flops=40 * poses * rows * freq,
        moved=4 * poses * rows * freq,
    )


def add_products(acc_ref, temp_ref, parts, chunk, span):
    freq = temp_ref.shape[1] // 2
    tile = max(t for t in range(LANES, 1153, LANES) if span % t == 0)
    lanes = acc_ref.shape[1]
    even = even_index((lanes, tile), 0)
    for t in range(span // tile):
        at = slice(t * tile, (t + 1) * tile)
        where = chunk * span + t * tile
        wide = jnp.concatenate([p[:, at] for p in parts], axis=0).astype(f32)
        acc_ref[...] += lax.dot_general(
            temp_ref[:, where : where + tile],
            jnp.where(even, wide, 0.0).astype(bf16),
            NT,
            preferred_element_type=f32,
        ) + lax.dot_general(
            temp_ref[:, freq + where : freq + where + tile],
            jnp.where(even, 0.0, wide).astype(bf16),
            NT,
            preferred_element_type=f32,
        )


def score_kernel(chunk, span, temp_ref, *refs):
    *parts, acc_ref = refs if chunk == 0 else refs[1:]
    acc_ref[...] = jnp.zeros_like(acc_ref) if chunk == 0 else refs[0][...]
    add_products(acc_ref, temp_ref, parts, chunk, span)


def last_score_kernel(sources, span, temp_ref, pow_ref, *refs):
    refs = list(refs)
    s_ref, all_ref, marks_ref, stat_ref = refs[-4:]
    chunks = [refs[c * sources : (c + 1) * sources] for c in range(CHUNKS)]
    rows, groups = pow_ref.shape
    lanes = s_ref.shape[1]
    poses = s_ref.shape[0] // rows
    s_ref[...] = refs[-5][...] if CHUNKS > 1 else jnp.zeros_like(s_ref)
    add_products(s_ref, temp_ref, chunks[-1], CHUNKS - 1, span)
    for c, parts in enumerate(chunks):
        at = 0
        for p in parts:
            all_ref[at : at + p.shape[0], c * span : (c + 1) * span] = p[:, :span]
            at += p.shape[0]
    ids = jnp.concatenate([p[:, span:] for p in chunks[0]], axis=0).astype(f32)
    group = lax.broadcasted_iota(jnp.int32, (lanes, groups), 1).astype(f32)
    marks = (ids[:, :groups] == group).astype(f32)
    marks_ref[...] = marks
    penalty = lax.dot_general(
        pow_ref[...], marks, NT, precision=HIGHEST, preferred_element_type=f32
    )
    acc = s_ref[...]
    acc = acc + jnp.where(
        even_index(acc.shape, 1), pltpu.roll(acc, lanes - 1, 1), pltpu.roll(acc, 1, 1)
    )
    scores = acc.reshape(poses, rows, lanes) - 0.5 * penalty[None]
    peak = jnp.max(jnp.max(scores, axis=0), axis=0, keepdims=True)
    total = jnp.sum(jnp.sum(jnp.exp(scores - peak[None]), axis=0), axis=0, keepdims=True)
    s_ref[...] = scores.reshape(poses * rows, lanes)
    stat_ref[0:1, :] = peak
    stat_ref[1:2, :] = total
    stat_ref[2:8, :] = jnp.zeros((6, lanes), f32)


def score(temps, power, gathered, freq):
    span = freq // CHUNKS
    lanes = sum(p.shape[0] for p in gathered[0])
    acc_shape = jax.ShapeDtypeStruct((temps.shape[0], lanes), f32)
    flops = 2 * temps.shape[0] * 256 * 2 * span
    acc = []
    for c in range(CHUNKS - 1):
        operands = [temps, *acc, *gathered[c]]
        acc = call(
            functools.partial(score_kernel, c, span),
            f"score{c}",
            [VMEM] * len(operands),
            [acc_shape],
            operands,
            flops=flops,
        )
    operands = [temps, power, *[p for parts in gathered for p in parts], *acc]
    return call(
        functools.partial(last_score_kernel, len(gathered[0]), span),
        f"score{CHUNKS - 1}",
        [VMEM] * len(operands),
        [
            acc_shape,
            jax.ShapeDtypeStruct((lanes, freq), bf16),
            jax.ShapeDtypeStruct((lanes, power.shape[1]), f32),
            jax.ShapeDtypeStruct((8, lanes), f32),
        ],
        operands,
        flops=flops,
    )


def xor_blocks(values, block, distance):
    lanes = values.shape[1]
    lane = lax.broadcasted_iota(jnp.int32, values.shape, 1)
    width = block
    while distance:
        if distance % 2:
            low = lax.rem(lane // width, 2) == 0
            values = jnp.where(
                low, pltpu.roll(values, lanes - width, 1), pltpu.roll(values, width, 1)
            )
        distance //= 2
        width *= 2
    return values


def rotate_slice(rho_ref, w_ref, cos_ref, sin_ref, base, span, poses, buffers, write):
    rows = rho_ref.shape[1] // poses
    tiles = [(a, min(256, span - a)) for a in range(0, span, 256)]

    def products(i):
        start, width = tiles[i]
        at = pl.ds(pl.multiple_of(base + start, LANES), width)
        weighted = w_ref[:, at]
        buffer = buffers[i % 2]
        buffer[0, :, :width] = jnp.dot(rho_ref[0], weighted, preferred_element_type=f32)
        buffer[1, :, :width] = jnp.dot(rho_ref[1], weighted, preferred_element_type=f32)

    def rotate(i):
        start, width = tiles[i]
        buffer = buffers[i % 2]
        for a in range(0, width, LANES):
            at = pl.ds(pl.multiple_of(base + start + a, LANES), LANES)
            numer_re = jnp.zeros((rows, LANES), f32)
            numer_im = jnp.zeros((rows, LANES), f32)
            for r in range(poses):
                cos_r = cos_ref[r : r + 1, at]
                sin_r = sin_ref[r : r + 1, at]
                s_re = buffer[0, r * rows : (r + 1) * rows, a : a + LANES]
                s_im = buffer[1, r * rows : (r + 1) * rows, a : a + LANES]
                numer_re = numer_re + s_re * cos_r + s_im * sin_r
                numer_im = numer_im + s_im * cos_r - s_re * sin_r
            write(start + a, numer_re, numer_im)

    products(0)
    for i in range(1, len(tiles)):
        products(i)
        rotate(i - 1)
    rotate(len(tiles) - 1)


def write_to(ref, span):
    def write(at, numer_re, numer_im):
        ref[:, at : at + LANES] = numer_re.astype(ref.dtype)
        ref[:, span + at : span + at + LANES] = numer_im.astype(ref.dtype)

    return write


def resp_kernel(
    poses, block, paired, far, span, me_ref, s_ref, marks_ref, cos_ref, sin_ref, w_ref, *refs
):
    stat_refs, refs = refs[: len(paired)], refs[len(paired) :]
    resp_ref, rho_ref, mass_ref = refs[:3]
    out_refs, buffers = refs[3:-2], refs[-2:]
    rows, groups = mass_ref.shape
    lanes = s_ref.shape[1]
    peaks, totals = [], []
    for ref, distance in zip(stat_refs, paired):
        for at in range(0, ref.shape[0], 8):
            stats = xor_blocks(ref[at : at + 8, :], block, distance)
            peaks.append(stats[0:1])
            totals.append(stats[1:2])
    peak = functools.reduce(jnp.maximum, peaks)
    total = sum(t * jnp.exp(p - peak) for t, p in zip(totals, peaks))
    log_norm = peak + jnp.log(total)
    scores = s_ref[...].reshape(poses, rows, lanes)
    rho = jnp.exp(scores - log_norm[None])
    even = even_index((rows, lanes), 1)
    mass = lax.dot_general(
        jnp.where(even, jnp.sum(rho, axis=0), 0.0),
        marks_ref[...],
        NN,
        precision=HIGHEST,
        preferred_element_type=f32,
    )
    mass_ref[...] = mass
    high = mass.astype(bf16)
    low = (mass - high.astype(f32)).astype(bf16)
    for ref in out_refs:
        ref[:, 2 * span : 2 * span + groups] = high
        ref[:, 2 * span + groups :] = low
    flat = rho.reshape(poses * rows, lanes)
    even = even_index(flat.shape, 1)
    rho_ref[0] = jnp.where(even, flat, 0.0).astype(bf16)
    rho_ref[1] = jnp.where(even, 0.0, flat).astype(bf16)
    for ref, distance in zip(out_refs, far):
        base = (me_ref[0] ^ distance) * span
        rotate_slice(
            rho_ref, w_ref, cos_ref, sin_ref, base, span, poses, buffers, write_to(ref, span)
        )
    pose_peak = jnp.max(scores, axis=0)
    log_resp = pose_peak + jnp.log(jnp.sum(jnp.exp(scores - pose_peak[None]), axis=0)) - log_norm
    shape = (resp_ref.shape[1], lanes)
    lane = lax.broadcasted_iota(jnp.int32, shape, 1)
    row = ((lane // block) ^ me_ref[1]) * (block // 2) + lax.rem(lane, block) // 2
    take = (lax.broadcasted_iota(jnp.int32, shape, 0) == row) & (lax.rem(lane, 2) == 0)
    resp_ref[...] = lax.dot_general(
        log_resp, take.astype(f32), NT, precision=HIGHEST, preferred_element_type=f32
    )


def responsibilities(me, scores, marks, cos_t, sin_t, weighted, stats, paired, far, block, span):
    poses, lanes = cos_t.shape[0], scores.shape[1]
    rows, groups = scores.shape[0] // poses, marks.shape[1]
    return call(
        functools.partial(resp_kernel, poses, block, paired, far, span),
        "responsibilities",
        [SMEM] + [VMEM] * (5 + len(stats)),
        [
            jax.ShapeDtypeStruct((rows, lanes // 2), f32),
            jax.ShapeDtypeStruct((2, poses * rows, lanes), bf16),
            jax.ShapeDtypeStruct((rows, groups), f32),
        ]
        + [jax.ShapeDtypeStruct((rows, 2 * span + 2 * groups), bf16)] * len(far),
        (me, scores, marks, cos_t, sin_t, weighted, *stats),
        [pltpu.VMEM((2, poses * rows, 256), f32)] * 2,
        flops=4 * 256 * poses * rows * span * len(far),
    )


def own_kernel(poses, span, me_ref, rho_ref, cos_ref, sin_ref, w_ref, out_ref, *buffers):
    base = me_ref[0] * span
    rotate_slice(
        rho_ref, w_ref, cos_ref, sin_ref, base, span, poses, buffers, write_to(out_ref, span)
    )


def own_slice(me, rho, cos_t, sin_t, weighted, span):
    poses = cos_t.shape[0]
    rows = rho.shape[1] // poses
    return call(
        functools.partial(own_kernel, poses, span),
        "own_slice",
        [SMEM] + [VMEM] * 4,
        [jax.ShapeDtypeStruct((rows, 2 * span), f32)],
        (me, rho, cos_t, sin_t, weighted),
        [pltpu.VMEM((2, poses * rows, 256), f32)] * 2,
        flops=4 * 256 * poses * rows * span,
    )[0]


def finish_kernel(span, me_ref, ctf_ref, nw_ref, mass_ref, own_ref, *refs):
    received, out_ref = refs[:-1], refs[-1]
    groups = mass_ref.shape[1]
    at = pl.ds(pl.multiple_of(me_ref[0] * span, LANES), span)
    ctf = ctf_ref[:, at]
    mass = mass_ref[...]
    for ref in received:
        mass += ref[:, 2 * span : 2 * span + groups].astype(f32)
        mass += ref[:, 2 * span + groups :].astype(f32)
    denom = (
        lax.dot_general(
            mass,
            ctf * ctf * nw_ref[:, at],
            NN,
            precision=HIGHEST,
            preferred_element_type=f32,
        )
        + prior_precision
    )
    for part in range(2):
        cut = slice(part * span, (part + 1) * span)
        numer = own_ref[:, cut]
        for ref in received:
            numer += ref[:, cut].astype(f32)
        out_ref[:, part, :] = numer / denom


def finish(me, ctf, noise_weight, mass, own, received, span):
    rows = own.shape[0]
    return call(
        functools.partial(finish_kernel, span),
        "finish",
        [SMEM] + [VMEM] * (4 + len(received)),
        [jax.ShapeDtypeStruct((rows, 2, span), f32)],
        (me, ctf, noise_weight, mass, own, *received),
    )[0]


def swap(values, axis, distance):
    size = lax.axis_size(axis)
    return lax.ppermute(values, axis, [(i, i ^ distance) for i in range(size)])


def gather_pairs(shard):
    size = lax.axis_size("cls")
    slots = [shard]
    hop = 1
    while hop < size:
        if len(slots) == 1:
            slots.append(swap(shard, "cls", hop))
        else:
            direct = swap(shard, "cls", hop)
            slots += [direct] + [swap(direct, "cls", k) for k in range(1, hop)]
        hop *= 2
    return slots


def local(particles, classes, ctf, noise_weight, group_ids, shifts):
    part_rows, _, freq = particles.shape
    n_cls = lax.axis_size("cls")
    n_img = lax.axis_size("img")
    span = freq // n_img
    noise_weight = noise_weight[None, :]
    pairwise = n_cls <= 4
    me_cls = lax.axis_index("cls") if pairwise else 0
    me = jnp.stack([lax.axis_index("img"), me_cls]).astype(jnp.int32)

    shards = weigh(particles, ctf, noise_weight, group_ids)
    if pairwise:
        gathered = [gather_pairs(w) for w in shards]
    else:
        gathered = [[lax.all_gather(w, "cls", axis=0, tiled=True)] for w in shards]

    cos_t, sin_t = phase_tables(shifts, freq)
    split = jnp.transpose(classes, (1, 0, 2))
    temps, power = build_templates(split, cos_t, sin_t, ctf, noise_weight)
    scores, weighted, marks, stat = score(temps, power, gathered, freq)
    if pairwise:
        stats = [stat] + [swap(stat, "cls", k) for k in range(1, n_cls)]
        paired = tuple(range(n_cls))
    else:
        stats = [lax.all_gather(stat, "cls", axis=0, tiled=True)]
        paired = (0,)

    far = tuple(range(n_img - 1, 0, -1))
    log_resp, rho, mass, *parts = responsibilities(
        me, scores, marks, cos_t, sin_t, weighted, stats, paired, far, 2 * part_rows, span
    )
    received = [swap(part, "img", d) for part, d in zip(parts, far)]
    mine = own_slice(me, rho, cos_t, sin_t, weighted, span)
    averages = finish(me, ctf, noise_weight, mass, mine, received, span)
    return (log_resp.T, averages)


def solution(mesh):
    placed = (
        P(("groups", "img", "cls"), None, None),
        P(("groups", "cls"), None, None),
        P("groups", None),
        P("groups"),
        P(("groups", "img", "cls")),
        P("groups", None),
    )
    return jax.shard_map(
        local,
        mesh=mesh,
        in_specs=placed,
        out_specs=(P(("groups", "img"), "cls"), P(("groups", "cls"), None, "img")),
        check_vma=False,
    )
```

time: 221 us -> 60 us (0.27)
  other arithmetic: 84.3 us -> 1.73 us
  blocking collectives: 35.1 us -> 0 us
  local copies, waits for them, and re-layouts: 26.8 us -> 2.43 us
  matrix products: 23.7 us -> 0 us
  Pallas kernels: 0 us -> 22.3 us
  waiting for transfers between devices: 36.7 us -> 16.4 us
  starting transfers between devices: 0.12 us -> 15.7 us
  between operations: 13.9 us -> 0.76 us
    another operation x3 -> x1, other arithmetic: 66.7 us -> 0.07 us  [local(): me = jnp.stack([lax.axis_index('img'), me_cls]).astype(jnp.int32)]
    reduce_scatter x2 -> x0, waiting for transfers between devices: 36.6 us -> none  [the longest x1 27.4 us: local(): lax.psum_scatter(numer, 'img', scatter_dimension=2, tiled=True)]
    dot_general x7 -> x0, matrix products: 23.7 us -> none  [the longest x1 11.4 us: local(): lax.dot_general(rho_low, gathered, (((0,), (0,)), ((), ())), preferred_el...]
    convert_element_type x1 -> x0, local copies, waits for them, and re-layouts: 22.7 us -> none  [local(): templates = jnp.stack([temp_re, temp_im], axis=2).astype(jnp.bfloat16).re...]
    pallas_call x0 -> x7, Pallas kernels: none -> 22.3 us  [call(): pl.pallas_call(kernel, in_specs=in_specs, out_specs=[VMEM] * len(out_shap...]
    ppermute x0 -> x12, waiting for transfers between devices: none -> 16.4 us  [swap(): return lax.ppermute(values, axis, [(i, i ^ distance) for i in range(size)])]
    ppermute x0 -> x12, starting transfers between devices: none -> 15.7 us  [swap(): return lax.ppermute(values, axis, [(i, i ^ distance) for i in range(size)])]
    all_gather x1 -> x0, blocking collectives: 14.8 us -> none  [local(): lax.all_gather(marks_low, 'cls', axis=0, tiled=True)]
  transfers between devices with their start and end apart: 3 -> 12, of which waited for: 2 -> 6; matrix products, arithmetic and copies ran while one was open for 49% -> 3% of each run, Pallas kernels for 0% -> 17%
where the time goes in v2:
time: 60 us; the launch traced here: 59.3 us
  Pallas kernels  22.3 us (37%)
  waiting for transfers between devices  16.4 us (27%)
  starting transfers between devices  15.7 us (26%)
  local copies, waits for them, and re-layouts  2.43 us (4%)
  other arithmetic  1.73 us (3%)
  between operations  0.76 us (1%)
    pallas_call x7, Pallas kernels, call(): pl.pallas_call(kernel, in_specs=in_specs, out_specs=[VMEM] * len(out_shap...  22.3 us
    ppermute x12, waiting for transfers between devices, swap(): return lax.ppermute(values, axis, [(i, i ^ distance) for i in range(size)])  16.4 us
    ppermute x12, starting transfers between devices, swap(): return lax.ppermute(values, axis, [(i, i ^ distance) for i in range(size)])  15.7 us
    unnamed x11, local copies, waits for them, and re-layouts  1.69 us
    sin x1, other arithmetic, phase_tables(): return (jnp.cos(angle), jnp.sin(angle))  1.65 us
  transfers between devices with their start and end apart: 12, of which 6 were waited for; matrix products, arithmetic and copies ran while one was open for 3% of the time, Pallas kernels for 17%

profile of v2, /device:TPU:0, one launch (start us, length us, event | category | flops | bytes accessed | tf_op | source)
XLA Modules:
  0.0 59.3 jit_solution(9817730182578358645)
XLA Ops:
  0.6 0.0 copy-start.4
  0.6 0.7 %broadcast_in_dim.2.nw_ref = f32[1,4608]{1,0:T(1,128)S(1)} reshape(f32[4608]{0:T(1024)} %param.9) | data formatting | bytes 36864 | tf_op jit(solution)/shard_map/broadcast_in_dim | solution.py:468
  1.4 0.0 copy-start.1
  1.4 1.0 %copy-done.1 = bf16[16,2,4608]{2,1,0:T(2,128)(2,1)S(1)} copy-done((bf16[16,2,4608]{2,1,0:T(2,128)(2,1)S(1)}, bf16[16,2,4608]{2,1,0:T(2,128)(2,1)}, u32[]{:S(2)}) %copy-start.1) | copy-done | bytes 294936
  2.4 0.0 copy-start.2
  2.4 0.7 %copy-done.2 = s32[16]{0:T(128)S(1)} copy-done((s32[16]{0:T(128)S(1)}, s32[16]{0:T(128)}, u32[]{:S(2)}) %copy-start.2) | copy-done | bytes 88
  3.0 0.0 copy-start.3
  3.0 2.0 %weigh.1 = (bf16[32,2432]{1,0:T(8,128)(2,1)S(1)}, bf16[32,2304]{1,0:T(8,128)(2,1)S(1)}) custom-call(s32[16]{0:T(128)S(1)} %copy-done.2, bf16[16,2,4608]{2,1,0:T(2,128)(2,1)S(1)} %copy-done.1, f32[64,4608]{1,0:T(8,128)} %ctf_ref.5, f32[1,4608]{1,0:T(1,128)S(1)} %broadcast_in_dim.2.nw_ref), custom_call_target="tpu_custom_call" | custom-call | flops 294912 | bytes 1179648 | tf_op jit(solution)/shard_map/weigh/pallas_call | solution.py:45
  5.0 0.0 copy-start
  5.0 4.1 %collective-permute-start.1 = (bf16[32,2432]{1,0:T(8,128)(2,1)S(1)}, bf16[32,2432]{1,0:T(8,128)(2,1)S(1)}, u32[]{:S(2)}, u32[]{:S(2)}) collective-permute-start(bf16[32,2432]{1,0:T(8,128)(2,1)S(1)} %get-tuple-element.18.refs_0_), channel_id=1, source_target_pairs={{0,8},{4,12},{8,0},{12,4},{1,9},{5,13},{9,1},{13,5},{2,10},{6,14},... | collective-permute-start | bytes 466952 | tf_op jit(solution)/shard_map/ppermute | solution.py:446
  9.1 1.6 %collective-permute-start = (bf16[32,2432]{1,0:T(8,128)(2,1)S(1)}, bf16[32,2432]{1,0:T(8,128)(2,1)S(1)}, u32[]{:S(2)}, u32[]{:S(2)}) collective-permute-start(bf16[32,2432]{1,0:T(8,128)(2,1)S(1)} %get-tuple-element.18.refs_0_), channel_id=1, source_target_pairs={{0,4},{4,0},{8,12},{12,8},{1,5},{5,1},{9,13},{13,9},{2,6},{6,2},{1... | collective-permute-start | bytes 466952 | tf_op jit(solution)/shard_map/ppermute | solution.py:446
  10.7 0.3 collective-permute-start.4
  11.0 0.2 collective-permute-start.3
  11.2 0.0 copy-done.4
  11.3 7.0 %collective-permute-done.1.refs_2_ = bf16[32,2432]{1,0:T(8,128)(2,1)S(1)} collective-permute-done((bf16[32,2432]{1,0:T(8,128)(2,1)S(1)}, bf16[32,2432]{1,0:T(8,128)(2,1)S(1)}, u32[]{:S(2)}, u32[]{:S(2)}) %collective-permute-start.1) | collective-permute-done | bytes 155680 | tf_op jit(solution)/shard_map/ppermute | solution.py:446
  18.2 0.0 collective-permute-start.2
  18.3 1.6 %fusion = (f32[24,4608]{1,0:T(8,128)S(1)}, f32[24,4608]{1,0:T(8,128)S(1)}) fusion(f32[4608]{0:T(1024)S(1)} %get-tuple-element.35, f32[24]{0:T(128)S(1)} %get-tuple-element.33, f32[4608]{0:T(1024)S(1)} %get-tuple-element.34, f32[24]{0:T(128)S(1)} %get-tuple-element.32), kind=kLoop, calls=%fused_computation.2 | loop fusion | flops 442368 | bytes 921792 | tf_op jit(solution)/shard_map/sin | solution.py:41
  19.9 0.0 copy-done.3
  19.9 0.1 copy.10
  20.0 0.0 copy-done
  20.0 6.5 %templates.1 = (bf16[768,9216]{1,0:T(8,128)(2,1)S(1)}, f32[32,64]{1,0:T(8,128)S(1)}) custom-call(bf16[2,32,4608]{2,1,0:T(8,128)(2,1)S(1)} %bitcast.10, f32[24,4608]{1,0:T(8,128)S(1)} %get-tuple-element.31.cos_ref, f32[24,4608]{1,0:T(8,128)S(1)} %get-tuple-element.30.sin_ref, f32[64,4608]{1,0:T(8,128)S(1)} %copy-done, f32[1,4608]{1,0:T(1,128)S(1)} %broadcast_in_dim.2.nw_ref), custom_call_target="tpu_custom_call" | custom-call | flops 141557760 | bytes 14155776 | tf_op jit(solution)/shard_map/templates/pallas_call | solution.py:45
  26.5 0.0 collective-permute-done.4.refs_6_
  26.5 2.1 %collective-permute-start.5 = (bf16[32,2304]{1,0:T(8,128)(2,1)}, bf16[32,2304]{1,0:T(8,128)(2,1)S(1)}, u32[]{:S(2)}, u32[]{:S(2)}) collective-permute-start(bf16[32,2304]{1,0:T(8,128)(2,1)} %collective-permute-done.4.refs_6_), channel_id=1, source_target_pairs={{0,4},{4,0},{8,12},{12,8},{1,5},{5,1},{9,13},{13,9},{2,6},{6,2},{1... | collective-permute-start | bytes 442376 | tf_op jit(solution)/shard_map/ppermute | solution.py:446
  28.6 0.0 collective-permute-done.refs_1_
  28.6 0.0 collective-permute-done.2.refs_3_
  28.6 2.1 %score0.1.refs_8_ = f32[768,128]{1,0:T(8,128)S(1)} custom-call(bf16[768,9216]{1,0:T(8,128)(2,1)S(1)} %get-tuple-element.16.temp_ref, bf16[32,2432]{1,0:T(8,128)(2,1)S(1)} %get-tuple-element.18.refs_0_, bf16[32,2432]{1,0:T(8,128)(2,1)S(1)} %collective-permute-done.refs_1_, bf16[32,2432]{1,0:T(8,128)(2,1)S(1)} %collective-permute-done.1.refs_2_, ...), custom_call_target="tpu_custom_call" | custom-call | flops 1811939328 | tf_op jit(solution)/shard_map/score0/pallas_call | solution.py:45
  30.7 0.0 collective-permute-done.3.refs_5_
  30.7 1.3 %collective-permute-done.5.refs_7_ = bf16[32,2304]{1,0:T(8,128)(2,1)S(1)} collective-permute-done((bf16[32,2304]{1,0:T(8,128)(2,1)}, bf16[32,2304]{1,0:T(8,128)(2,1)S(1)}, u32[]{:S(2)}, u32[]{:S(2)}) %collective-permute-start.5) | collective-permute-done | bytes 147488 | tf_op jit(solution)/shard_map/ppermute | solution.py:446
  31.9 3.4 %score1.1 = (f32[768,128]{1,0:T(8,128)S(1)}, bf16[128,4608]{1,0:T(8,128)(2,1)S(1)}, f32[128,64]{1,0:T(8,128)S(1)}, f32[8,128]{1,0:T(8,128)S(1)}) custom-call(bf16[768,9216]{1,0:T(8,128)(2,1)S(1)} %get-tuple-element.16.temp_ref, f32[32,64]{1,0:T(8,128)S(1)} %get-tuple-element.17.pow_ref, bf16[32,2432]{1,0:T(8,128)(2,1)S(1)} %get-tuple-element.18.refs_0_, ...), custom_call_target="tpu_custom_call" | custom-call | flops 1811939328 | tf_op jit(solution)/shard_map/score1/pallas_call | solution.py:45
  35.3 2.0 %collective-permute-start.6 = (f32[8,128]{1,0:T(8,128)S(1)}, f32[8,128]{1,0:T(8,128)S(1)}, u32[]{:S(2)}, u32[]{:S(2)}) collective-permute-start(f32[8,128]{1,0:T(8,128)S(1)} %get-tuple-element.23.refs_0_), channel_id=1, source_target_pairs={{0,4},{4,0},{8,12},{12,8},{1,5},{5,1},{9,13},{13,9},{2,6},{6,2},{1... | collective-permute-start | bytes 12296 | tf_op jit(solution)/shard_map/ppermute | solution.py:446
  37.4 2.1 %collective-permute-start.7 = (f32[8,128]{1,0:T(8,128)S(1)}, f32[8,128]{1,0:T(8,128)S(1)}, u32[]{:S(2)}, u32[]{:S(2)}) collective-permute-start(f32[8,128]{1,0:T(8,128)S(1)} %get-tuple-element.23.refs_0_), channel_id=1, source_target_pairs={{0,8},{4,12},{8,0},{12,4},{1,9},{5,13},{9,1},{13,5},{2,10},{6,14},... | collective-permute-start | bytes 12296 | tf_op jit(solution)/shard_map/ppermute | solution.py:446
  39.4 1.2 %collective-permute-start.8 = (f32[8,128]{1,0:T(8,128)S(1)}, f32[8,128]{1,0:T(8,128)S(1)}, u32[]{:S(2)}, u32[]{:S(2)}) collective-permute-start(f32[8,128]{1,0:T(8,128)S(1)} %get-tuple-element.23.refs_0_), channel_id=1, source_target_pairs={{0,12},{4,8},{8,4},{12,0},{1,13},{5,9},{9,5},{13,1},{2,14},{6,10},... | collective-permute-start | bytes 12296 | tf_op jit(solution)/shard_map/ppermute | solution.py:446
  40.6 0.1 pad_add_fusion.me_ref
  40.7 0.0 collective-permute-done.6.refs_1_
  40.7 1.2 %collective-permute-done.7.refs_2_ = f32[8,128]{1,0:T(8,128)S(1)} collective-permute-done((f32[8,128]{1,0:T(8,128)S(1)}, f32[8,128]{1,0:T(8,128)S(1)}, u32[]{:S(2)}, u32[]{:S(2)}) %collective-permute-start.7) | collective-permute-done | bytes 4128 | tf_op jit(solution)/shard_map/ppermute | solution.py:446
  41.9 3.0 %collective-permute-done.8.refs_3_ = f32[8,128]{1,0:T(8,128)S(1)} collective-permute-done((f32[8,128]{1,0:T(8,128)S(1)}, f32[8,128]{1,0:T(8,128)S(1)}, u32[]{:S(2)}, u32[]{:S(2)}) %collective-permute-start.8) | collective-permute-done | bytes 4128 | tf_op jit(solution)/shard_map/ppermute | solution.py:446
  44.8 5.1 %responsibilities.1 = (f32[32,64]{1,0:T(8,128)}, bf16[2,768,128]{2,1,0:T(8,128)(2,1)S(1)}, f32[32,64]{1,0:T(8,128)S(1)}, bf16[32,2432]{1,0:T(8,128)(2,1)S(1)}, b...) custom-call(s32[2]{0:T(128)S(1)} %pad_add_fusion.me_ref, f32[768,128]{1,0:T(8,128)S(1)} %get-tuple-element.20.s_ref, ...), custom_call_target="tpu_custom_call" | custom-call | flops 2717908992 | tf_op jit(solution)/shard_map/responsibilities/pallas_call | solution.py:45
  49.9 1.5 %collective-permute-start.10 = (bf16[32,2432]{1,0:T(8,128)(2,1)S(1)}, bf16[32,2432]{1,0:T(8,128)(2,1)S(1)}, u32[]{:S(2)}, u32[]{:S(2)}) collective-permute-start(bf16[32,2432]{1,0:T(8,128)(2,1)S(1)} %get-tuple-element.28), channel_id=1, source_target_pairs={{0,2},{1,3},{2,0},{3,1},{4,6},{5,7},{6,4},{7,5},{8,10},{9,11},{10,... | collective-permute-start | bytes 466952 | tf_op jit(solution)/shard_map/ppermute | solution.py:446
  51.4 0.0 collective-permute-start.11
  51.4 0.7 %collective-permute-start.9 = (bf16[32,2432]{1,0:T(8,128)(2,1)S(1)}, bf16[32,2432]{1,0:T(8,128)(2,1)S(1)}, u32[]{:S(2)}, u32[]{:S(2)}) collective-permute-start(bf16[32,2432]{1,0:T(8,128)(2,1)S(1)} %get-tuple-element.27), channel_id=1, source_target_pairs={{0,3},{1,2},{2,1},{3,0},{4,7},{5,6},{6,5},{7,4},{8,11},{9,10},{10,... | collective-permute-start | bytes 466952 | tf_op jit(solution)/shard_map/ppermute | solution.py:446
  52.1 1.6 %own_slice.1.own_ref = f32[32,2304]{1,0:T(8,128)S(1)} custom-call(s32[2]{0:T(128)S(1)} %pad_add_fusion.me_ref, bf16[2,768,128]{2,1,0:T(8,128)(2,1)S(1)} %get-tuple-element.26.rho_ref, f32[24,4608]{1,0:T(8,128)S(1)} %get-tuple-element.31.cos_ref, f32[24,4608]{1,0:T(8,128)S(1)} %get-tuple-element.30.sin_ref, bf16[128,4608]{1,0:T(8,128)(2,1)S(1)} %get-tuple-element.22.w_ref), custom_call_target="tpu_custom_call" | custom-call | flops 905969664 | tf_op jit(solution)/shard_map/own_slice/pallas_call | solution.py:45
  53.7 2.3 %collective-permute-done.10.refs_1_ = bf16[32,2432]{1,0:T(8,128)(2,1)S(1)} collective-permute-done((bf16[32,2432]{1,0:T(8,128)(2,1)S(1)}, bf16[32,2432]{1,0:T(8,128)(2,1)S(1)}, u32[]{:S(2)}, u32[]{:S(2)}) %collective-permute-start.10) | collective-permute-done | bytes 155680 | tf_op jit(solution)/shard_map/ppermute | solution.py:446
  55.9 0.0 collective-permute-done.11.refs_2_
  56.0 1.7 %collective-permute-done.9.refs_0_ = bf16[32,2432]{1,0:T(8,128)(2,1)S(1)} collective-permute-done((bf16[32,2432]{1,0:T(8,128)(2,1)S(1)}, bf16[32,2432]{1,0:T(8,128)(2,1)S(1)}, u32[]{:S(2)}, u32[]{:S(2)}) %collective-permute-start.9) | collective-permute-done | bytes 155680 | tf_op jit(solution)/shard_map/ppermute | solution.py:446
  57.7 1.6 %finish.1 = f32[32,2,1152]{2,1,0:T(2,128)} custom-call(s32[2]{0:T(128)S(1)} %pad_add_fusion.me_ref, f32[64,4608]{1,0:T(8,128)S(1)} %copy-done, f32[1,4608]{1,0:T(1,128)S(1)} %broadcast_in_dim.2.nw_ref, f32[32,64]{1,0:T(8,128)S(1)} %get-tuple-element.25.mass_ref, f32[32,2304]{1,0:T(8,128)S(1)} %own_slice.1.own_ref, ...), custom_call_target="tpu_custom_call" | custom-call | tf_op jit(solution)/shard_map/finish/pallas_call | solution.py:45
  (2 shorter events, 0.0 us)
Async XLA Ops:
  0.6 10.6 %copy-start.4 = (s32[24,2]{0,1:T(2,128)S(1)}, s32[24,2]{0,1:T(2,128)}, u32[]{:S(2)}) copy-start(s32[24,2]{0,1:T(2,128)} %param.11) | copy-start | bytes 580
  1.4 1.0 %copy-start.1 = (bf16[16,2,4608]{2,1,0:T(2,128)(2,1)S(1)}, bf16[16,2,4608]{2,1,0:T(2,128)(2,1)}, u32[]{:S(2)}) copy-start(bf16[16,2,4608]{2,1,0:T(2,128)(2,1)} %p_ref.1) | copy-start | bytes 884740
  2.4 0.7 %copy-start.2 = (s32[16]{0:T(128)S(1)}, s32[16]{0:T(128)}, u32[]{:S(2)}) copy-start(s32[16]{0:T(128)} %ids_ref.1) | copy-start | bytes 196
  3.0 16.9 %copy-start.3 = (bf16[32,2,4608]{2,1,0:T(2,128)(2,1)S(1)}, bf16[32,2,4608]{2,1,0:T(2,128)(2,1)}, u32[]{:S(2)}) copy-start(bf16[32,2,4608]{2,1,0:T(2,128)(2,1)} %param.7) | copy-start | bytes 1769476
  5.0 15.0 %copy-start = (f32[64,4608]{1,0:T(8,128)S(1)}, f32[64,4608]{1,0:T(8,128)}, u32[]{:S(2)}) copy-start(f32[64,4608]{1,0:T(8,128)} %ctf_ref.5) | copy-start | bytes 3538948
  5.0 13.2 %collective-permute-start.1 = (bf16[32,2432]{1,0:T(8,128)(2,1)S(1)}, bf16[32,2432]{1,0:T(8,128)(2,1)S(1)}, u32[]{:S(2)}, u32[]{:S(2)}) collective-permute-start(bf16[32,2432]{1,0:T(8,128)(2,1)S(1)} %get-tuple-element.18.refs_0_), channel_id=1, source_target_pairs={{0,8},{4,12},{8,0},{12,4},{1,9},{5,13},{9,1},{13,5},{2,10},{6,14},... | collective-permute-start | bytes 466952 | tf_op jit(solution)/shard_map/ppermute | solution.py:446
  9.1 19.5 %collective-permute-start = (bf16[32,2432]{1,0:T(8,128)(2,1)S(1)}, bf16[32,2432]{1,0:T(8,128)(2,1)S(1)}, u32[]{:S(2)}, u32[]{:S(2)}) collective-permute-start(bf16[32,2432]{1,0:T(8,128)(2,1)S(1)} %get-tuple-element.18.refs_0_), channel_id=1, source_target_pairs={{0,4},{4,0},{8,12},{12,8},{1,5},{5,1},{9,13},{13,9},{2,6},{6,2},{1... | collective-permute-start | bytes 466952 | tf_op jit(solution)/shard_map/ppermute | solution.py:446
  10.7 15.8 %collective-permute-start.4 = (bf16[32,2304]{1,0:T(8,128)(2,1)S(1)}, bf16[32,2304]{1,0:T(8,128)(2,1)}, u32[]{:S(2)}, u32[]{:S(2)}) collective-permute-start(bf16[32,2304]{1,0:T(8,128)(2,1)S(1)} %get-tuple-element.19.refs_4_), channel_id=1, source_target_pairs={{0,8},{4,12},{8,0},{12,4},{1,9},{5,13},{9,1},{13,5},{2,10},{6,14},... | collective-permute-start | bytes 442376 | tf_op jit(solution)/shard_map/ppermute | solution.py:446
  11.0 19.6 %collective-permute-start.3 = (bf16[32,2304]{1,0:T(8,128)(2,1)S(1)}, bf16[32,2304]{1,0:T(8,128)(2,1)}, u32[]{:S(2)}, u32[]{:S(2)}) collective-permute-start(bf16[32,2304]{1,0:T(8,128)(2,1)S(1)} %get-tuple-element.19.refs_4_), channel_id=1, source_target_pairs={{0,4},{4,0},{8,12},{12,8},{1,5},{5,1},{9,13},{13,9},{2,6},{6,2},{1... | collective-permute-start | bytes 442376 | tf_op jit(solution)/shard_map/ppermute | solution.py:446
  18.2 10.4 %collective-permute-start.2 = (bf16[32,2432]{1,0:T(8,128)(2,1)S(1)}, bf16[32,2432]{1,0:T(8,128)(2,1)S(1)}, u32[]{:S(2)}, u32[]{:S(2)}) collective-permute-start(bf16[32,2432]{1,0:T(8,128)(2,1)S(1)} %collective-permute-done.1.refs_2_), channel_id=1, source_target_pairs={{0,4},{4,0},{8,12},{12,8},{1,5},{5,1},{9,13},{13,9},{2,6},{6,2},{1... | collective-permute-start | bytes 466952 | tf_op jit(solution)/shard_map/ppermute | solution.py:446
  26.5 5.4 %collective-permute-start.5 = (bf16[32,2304]{1,0:T(8,128)(2,1)}, bf16[32,2304]{1,0:T(8,128)(2,1)S(1)}, u32[]{:S(2)}, u32[]{:S(2)}) collective-permute-start(bf16[32,2304]{1,0:T(8,128)(2,1)} %collective-permute-done.4.refs_6_), channel_id=1, source_target_pairs={{0,4},{4,0},{8,12},{12,8},{1,5},{5,1},{9,13},{13,9},{2,6},{6,2},{1... | collective-permute-start | bytes 442376 | tf_op jit(solution)/shard_map/ppermute | solution.py:446
  35.3 5.3 %collective-permute-start.6 = (f32[8,128]{1,0:T(8,128)S(1)}, f32[8,128]{1,0:T(8,128)S(1)}, u32[]{:S(2)}, u32[]{:S(2)}) collective-permute-start(f32[8,128]{1,0:T(8,128)S(1)} %get-tuple-element.23.refs_0_), channel_id=1, source_target_pairs={{0,4},{4,0},{8,12},{12,8},{1,5},{5,1},{9,13},{13,9},{2,6},{6,2},{1... | collective-permute-start | bytes 12296 | tf_op jit(solution)/shard_map/ppermute | solution.py:446
  37.4 4.5 %collective-permute-start.7 = (f32[8,128]{1,0:T(8,128)S(1)}, f32[8,128]{1,0:T(8,128)S(1)}, u32[]{:S(2)}, u32[]{:S(2)}) collective-permute-start(f32[8,128]{1,0:T(8,128)S(1)} %get-tuple-element.23.refs_0_), channel_id=1, source_target_pairs={{0,8},{4,12},{8,0},{12,4},{1,9},{5,13},{9,1},{13,5},{2,10},{6,14},... | collective-permute-start | bytes 12296 | tf_op jit(solution)/shard_map/ppermute | solution.py:446
  39.4 5.4 %collective-permute-start.8 = (f32[8,128]{1,0:T(8,128)S(1)}, f32[8,128]{1,0:T(8,128)S(1)}, u32[]{:S(2)}, u32[]{:S(2)}) collective-permute-start(f32[8,128]{1,0:T(8,128)S(1)} %get-tuple-element.23.refs_0_), channel_id=1, source_target_pairs={{0,12},{4,8},{8,4},{12,0},{1,13},{5,9},{9,5},{13,1},{2,14},{6,10},... | collective-permute-start | bytes 12296 | tf_op jit(solution)/shard_map/ppermute | solution.py:446
  49.9 6.0 %collective-permute-start.10 = (bf16[32,2432]{1,0:T(8,128)(2,1)S(1)}, bf16[32,2432]{1,0:T(8,128)(2,1)S(1)}, u32[]{:S(2)}, u32[]{:S(2)}) collective-permute-start(bf16[32,2432]{1,0:T(8,128)(2,1)S(1)} %get-tuple-element.28), channel_id=1, source_target_pairs={{0,2},{1,3},{2,0},{3,1},{4,6},{5,7},{6,4},{7,5},{8,10},{9,11},{10,... | collective-permute-start | bytes 466952 | tf_op jit(solution)/shard_map/ppermute | solution.py:446
  51.4 4.6 %collective-permute-start.11 = (bf16[32,2432]{1,0:T(8,128)(2,1)S(1)}, bf16[32,2432]{1,0:T(8,128)(2,1)S(1)}, u32[]{:S(2)}, u32[]{:S(2)}) collective-permute-start(bf16[32,2432]{1,0:T(8,128)(2,1)S(1)} %get-tuple-element.29), channel_id=1, source_target_pairs={{0,1},{1,0},{2,3},{3,2},{4,5},{5,4},{6,7},{7,6},{8,9},{9,8},{10,11... | collective-permute-start | bytes 466952 | tf_op jit(solution)/shard_map/ppermute | solution.py:446
  51.4 6.3 %collective-permute-start.9 = (bf16[32,2432]{1,0:T(8,128)(2,1)S(1)}, bf16[32,2432]{1,0:T(8,128)(2,1)S(1)}, u32[]{:S(2)}, u32[]{:S(2)}) collective-permute-start(bf16[32,2432]{1,0:T(8,128)(2,1)S(1)} %get-tuple-element.27), channel_id=1, source_target_pairs={{0,3},{1,2},{2,1},{3,0},{4,7},{5,6},{6,5},{7,4},{8,11},{9,10},{10,... | collective-permute-start | bytes 466952 | tf_op jit(solution)/shard_map/ppermute | solution.py:446

commit v3 on v2

--- a/solution.py
+++ b/solution.py
@@ -26,19 +26,12 @@
 
 
 def phase_tables(shifts, freq):
-    index = jnp.arange(freq)
-    along_y = (index // BOX).astype(f32)
-    along_x = (index % BOX - BOX // 2).astype(f32)
-    angle = (
-        2.0
-        * jnp.pi
-        / BOX
-        * (
-            shifts[:, 0:1].astype(f32) * along_x[None, :]
-            + shifts[:, 1:2].astype(f32) * along_y[None, :]
-        )
-    )
-    return (jnp.cos(angle), jnp.sin(angle))
+    along_x = (jnp.arange(BOX) - BOX // 2).astype(f32)
+    along_y = jnp.arange(freq // BOX).astype(f32)
+    step = 2.0 * jnp.pi / BOX
+    angle_x = step * (shifts[:, 0:1].astype(f32) * along_x[None, :])
+    angle_y = step * (shifts[:, 1:2].astype(f32) * along_y[None, :])
+    return (jnp.cos(angle_x), jnp.sin(angle_x), jnp.cos(angle_y), jnp.sin(angle_y))
 
 
 def call(kernel, name, in_specs, out_shape, operands, scratch=(), flops=0, moved=0, out_specs=None):
@@ -58,27 +51,29 @@
     return lax.rem(lax.broadcasted_iota(jnp.int32, shape, axis), 2) == 0
 
 
-def weigh_kernel(ids_ref, p_ref, ctf_ref, nw_ref, *refs):
-    out_refs, (rows_ref, scale_ref, sem) = refs[:-3], refs[-3:]
+def weigh_kernel(ids_hbm, p_hbm, ctf_hbm, nw_hbm, *refs):
+    out_refs, (ids_ref, p_ref, ctf_ref, nw_ref, scale_ref, sem) = refs[:-6], refs[-6:]
     count, _, freq = p_ref.shape
     copies = [
-        pltpu.make_async_copy(
-            ctf_ref.at[pl.ds(ids_ref[n], 1), :], rows_ref.at[pl.ds(n, 1), :], sem.at[n]
+        pltpu.make_async_copy(source, target, sem.at[i])
+        for i, (source, target) in enumerate(
+            [(ids_hbm, ids_ref), (ctf_hbm, ctf_ref), (nw_hbm, nw_ref), (p_hbm, p_ref)]
         )
-        for n in range(count)
     ]
     for copy in copies:
         copy.start()
+    copies[0].wait()
     row = lax.broadcasted_iota(jnp.int32, (2 * count, LANES), 0) // 2
     ids = jnp.zeros((2 * count, LANES), f32)
     for n in range(count):
         ids = jnp.where(row == n, ids_ref[n].astype(f32), ids)
+    for copy in copies[1:]:
+        copy.wait()
+    noise = nw_ref[...].reshape(1, freq)
+    for n in range(count):
+        scale = ctf_ref[pl.ds(ids_ref[n], 1), :] * noise
+        scale_ref[2 * n : 2 * n + 2, :] = jnp.broadcast_to(scale, (2, freq))
     values = p_ref[...].astype(f32).reshape(2 * count, freq)
-    for copy in copies:
-        copy.wait()
-    scale = rows_ref[...] * nw_ref[...]
-    for n in range(count):
-        scale_ref[2 * n : 2 * n + 2, :] = jnp.broadcast_to(scale[n : n + 1], (2, freq))
     weighted = (values * scale_ref[...]).astype(bf16)
     chunk = freq // len(out_refs)
     for c, out_ref in enumerate(out_refs):
@@ -89,28 +84,40 @@
 def weigh(particles, ctf, noise_weight, group_ids):
     rows, _, freq = particles.shape
     chunk = freq // CHUNKS
+    operands = (group_ids, particles, ctf, noise_weight)
     return call(
         weigh_kernel,
         "weigh",
-        [SMEM, VMEM, ANY, VMEM],
+        [ANY] * 4,
         [
             jax.ShapeDtypeStruct((2 * rows, chunk + (LANES if c == 0 else 0)), bf16)
             for c in range(CHUNKS)
         ],
-        (group_ids, particles, pltpu.with_memory_space_constraint(ctf, pltpu.HBM), noise_weight),
+        [pltpu.with_memory_space_constraint(x, pltpu.HBM) for x in operands],
         [
-            pltpu.VMEM((rows, freq), f32),
+            pltpu.SMEM((rows,), jnp.int32),
+            pltpu.VMEM(particles.shape, bf16),
+            pltpu.VMEM(ctf.shape, f32),
+            pltpu.VMEM((freq,), f32),
             pltpu.VMEM((2 * rows, freq), f32),
-            pltpu.SemaphoreType.DMA((rows,)),
+            pltpu.SemaphoreType.DMA((4,)),
         ],
         flops=4 * rows * freq,
         moved=16 * rows * freq,
     )
 
 
-def template_kernel(cls_ref, cos_ref, sin_ref, ctf_ref, nw_ref, temp_ref, pow_ref):
+def template_kernel(
+    cls_ref, xc_ref, xs_ref, yc_ref, ys_ref, ctf_ref, nw_ref, temp_ref, cos_ref, sin_ref, pow_ref
+):
     _, rows, freq = cls_ref.shape
     poses = cos_ref.shape[0]
+    x_cos, x_sin = xc_ref[...], xs_ref[...]
+    for t in range(freq // BOX):
+        y_cos = jnp.broadcast_to(yc_ref[:, t : t + 1], x_cos.shape)
+        y_sin = jnp.broadcast_to(ys_ref[:, t : t + 1], x_cos.shape)
+        cos_ref[:, t * BOX : (t + 1) * BOX] = x_cos * y_cos - x_sin * y_sin
+        sin_ref[:, t * BOX : (t + 1) * BOX] = x_sin * y_cos + x_cos * y_sin
 
     @pl.loop(0, freq // LANES)
     def _(t):
@@ -141,18 +148,20 @@
     pow_ref[...] = power
 
 
-def build_templates(split, cos_t, sin_t, ctf, noise_weight):
+def build_templates(split, tables, ctf, noise_weight):
     _, rows, freq = split.shape
-    poses, groups = cos_t.shape[0], ctf.shape[0]
+    poses, groups = tables[0].shape[0], ctf.shape[0]
     return call(
         template_kernel,
         "templates",
-        [VMEM] * 5,
+        [VMEM] * 7,
         [
             pltpu.VMEM((poses * rows, 2 * freq), bf16),
+            pltpu.VMEM((poses, freq), f32),
+            pltpu.VMEM((poses, freq), f32),
             jax.ShapeDtypeStruct((rows, groups), f32),
         ],
-        (split, cos_t, sin_t, ctf, noise_weight),
+        (split, *tables, ctf, noise_weight),
         flops=40 * poses * rows * freq,
         moved=4 * poses * rows * freq,
     )
@@ -382,32 +391,38 @@
     )
 
 
-def own_kernel(poses, span, me_ref, rho_ref, cos_ref, sin_ref, w_ref, out_ref, *buffers):
+def own_kernel(
+    poses, span, me_ref, rho_ref, cos_ref, sin_ref, w_ref, ctf_ref, nw_ref, out_ref, cw_ref, *buffers
+):
     base = me_ref[0] * span
+    at = pl.ds(pl.multiple_of(base, LANES), span)
+    ctf = ctf_ref[:, at]
+    cw_ref[...] = ctf * ctf * nw_ref[:, at]
     rotate_slice(
         rho_ref, w_ref, cos_ref, sin_ref, base, span, poses, buffers, write_to(out_ref, span)
     )
 
 
-def own_slice(me, rho, cos_t, sin_t, weighted, span):
+def own_slice(me, rho, cos_t, sin_t, weighted, ctf, noise_weight, span):
     poses = cos_t.shape[0]
     rows = rho.shape[1] // poses
     return call(
         functools.partial(own_kernel, poses, span),
         "own_slice",
-        [SMEM] + [VMEM] * 4,
-        [jax.ShapeDtypeStruct((rows, 2 * span), f32)],
-        (me, rho, cos_t, sin_t, weighted),
+        [SMEM] + [VMEM] * 6,
+        [
+            jax.ShapeDtypeStruct((rows, 2 * span), f32),
+            jax.ShapeDtypeStruct((ctf.shape[0], span), f32),
+        ],
+        (me, rho, cos_t, sin_t, weighted, ctf, noise_weight),
         [pltpu.VMEM((2, poses * rows, 256), f32)] * 2,
         flops=4 * 256 * poses * rows * span,
-    )[0]
-
-
-def finish_kernel(span, me_ref, ctf_ref, nw_ref, mass_ref, own_ref, *refs):
+    )
+
+
+def finish_kernel(span, cw_ref, mass_ref, own_ref, *refs):
     received, out_ref = refs[:-1], refs[-1]
     groups = mass_ref.shape[1]
-    at = pl.ds(pl.multiple_of(me_ref[0] * span, LANES), span)
-    ctf = ctf_ref[:, at]
     mass = mass_ref[...]
     for ref in received:
         mass += ref[:, 2 * span : 2 * span + groups].astype(f32)
@@ -415,7 +430,7 @@
     denom = (
         lax.dot_general(
             mass,
-            ctf * ctf * nw_ref[:, at],
+            cw_ref[...],
             NN,
             precision=HIGHEST,
             preferred_element_type=f32,
@@ -430,14 +445,14 @@
         out_ref[:, part, :] = numer / denom
 
 
-def finish(me, ctf, noise_weight, mass, own, received, span):
+def finish(weight, mass, own, received, span):
     rows = own.shape[0]
     return call(
         functools.partial(finish_kernel, span),
         "finish",
-        [SMEM] + [VMEM] * (4 + len(received)),
+        [VMEM] * (3 + len(received)),
         [jax.ShapeDtypeStruct((rows, 2, span), f32)],
-        (me, ctf, noise_weight, mass, own, *received),
+        (weight, mass, own, *received),
     )[0]
 
 
@@ -446,17 +461,15 @@
     return lax.ppermute(values, axis, [(i, i ^ distance) for i in range(size)])
 
 
-def gather_pairs(shard):
-    size = lax.axis_size("cls")
+def direct_shards(shard):
+    distances = [1 << b for b in range(lax.axis_size("cls").bit_length() - 1)]
+    return [swap(shard, "cls", d) for d in distances]
+
+
+def gather_pairs(shard, direct):
     slots = [shard]
-    hop = 1
-    while hop < size:
-        if len(slots) == 1:
-            slots.append(swap(shard, "cls", hop))
-        else:
-            direct = swap(shard, "cls", hop)
-            slots += [direct] + [swap(direct, "cls", k) for k in range(1, hop)]
-        hop *= 2
+    for i, arrived in enumerate(direct):
+        slots += [arrived] + [swap(arrived, "cls", k) for k in range(1, 1 << i)]
     return slots
 
 
@@ -465,20 +478,25 @@
     n_cls = lax.axis_size("cls")
     n_img = lax.axis_size("img")
     span = freq // n_img
-    noise_weight = noise_weight[None, :]
     pairwise = n_cls <= 4
     me_cls = lax.axis_index("cls") if pairwise else 0
     me = jnp.stack([lax.axis_index("img"), me_cls]).astype(jnp.int32)
 
     shards = weigh(particles, ctf, noise_weight, group_ids)
+    noise_weight = noise_weight[None, :]
     if pairwise:
-        gathered = [gather_pairs(w) for w in shards]
+        direct = [direct_shards(w) for w in shards]
     else:
         gathered = [[lax.all_gather(w, "cls", axis=0, tiled=True)] for w in shards]
 
-    cos_t, sin_t = phase_tables(shifts, freq)
     split = jnp.transpose(classes, (1, 0, 2))
-    temps, power = build_templates(split, cos_t, sin_t, ctf, noise_weight)
+    temps, cos_t, sin_t, power = build_templates(
+        split, phase_tables(shifts, freq), ctf, noise_weight
+    )
+    if pairwise:
+        for shard in direct:
+            shard[-1], power = lax.optimization_barrier((shard[-1], power))
+        gathered = [gather_pairs(w, d) for w, d in zip(shards, direct)]
     scores, weighted, marks, stat = score(temps, power, gathered, freq)
     if pairwise:
         stats = [stat] + [swap(stat, "cls", k) for k in range(1, n_cls)]
@@ -492,8 +510,8 @@
         me, scores, marks, cos_t, sin_t, weighted, stats, paired, far, 2 * part_rows, span
     )
     received = [swap(part, "img", d) for part, d in zip(parts, far)]
-    mine = own_slice(me, rho, cos_t, sin_t, weighted, span)
-    averages = finish(me, ctf, noise_weight, mass, mine, received, span)
+    mine, weight = own_slice(me, rho, cos_t, sin_t, weighted, ctf, noise_weight, span)
+    averages = finish(weight, mass, mine, received, span)
     return (log_resp.T, averages)
 
 

time: 60 us -> 64.2 us (1.070)
  local copies, waits for them, and re-layouts: 2.43 us -> 11.2 us
  Pallas kernels: 22.3 us -> 20.9 us
  other arithmetic: 1.73 us -> 0.34 us
  waiting for transfers between devices: 16.4 us -> 15.4 us
    unnamed x11, local copies, waits for them, and re-layouts: 1.69 us -> 11.2 us
    pallas_call x7, Pallas kernels: 22.3 us -> 20.9 us  [call(): pl.pallas_call(kernel, in_specs=in_specs, out_specs=[VMEM] * len(out_shap...]
    sin x1 -> x2, other arithmetic: 1.65 us -> 0.25 us  [the longest x1 0.12 us: phase_tables(): jnp.sin(angle_y)]
    ppermute x12, waiting for transfers between devices: 16.4 us -> 15.4 us  [swap(): return lax.ppermute(values, axis, [(i, i ^ distance) for i in range(size)])]
    broadcast_in_dim x1, local copies, waits for them, and re-layouts: 0.75 us -> 0.01 us  [local(): noise_weight = noise_weight[None, :]]
  transfers between devices with their start and end apart: 12 -> 12, of which waited for: 6 -> 5; matrix products, arithmetic and copies ran while one was open for 3% -> 2% of each run, Pallas kernels for 17% -> 16%
where the time goes in v3:
time: 64.2 us; the launch traced here: 63.8 us
  Pallas kernels  20.9 us (33%)
  waiting for transfers between devices  15.4 us (24%)
  starting transfers between devices  15.1 us (24%)
  local copies, waits for them, and re-layouts  11.2 us (17%)
  between operations  0.78 us (1%)
    pallas_call x7, Pallas kernels, call(): pl.pallas_call(kernel, in_specs=in_specs, out_specs=[VMEM] * len(out_shap...  20.9 us
    ppermute x12, waiting for transfers between devices, swap(): return lax.ppermute(values, axis, [(i, i ^ distance) for i in range(size)])  15.4 us
    ppermute x12, starting transfers between devices, swap(): return lax.ppermute(values, axis, [(i, i ^ distance) for i in range(size)])  15.1 us
    unnamed x11, local copies, waits for them, and re-layouts  11.2 us
  transfers between devices with their start and end apart: 12, of which 5 were waited for; matrix products, arithmetic and copies ran while one was open for 2% of the time, Pallas kernels for 16%

profile of v3, /device:TPU:0, one launch (start us, length us, event | category | flops | bytes accessed | tf_op | source)
XLA Modules:
  0.0 63.8 jit_solution(16395461518337728611)
XLA Ops:
  0.6 0.0 copy-start.3
  0.6 0.0 copy-start.2
  0.7 0.0 copy-start.4
  0.7 1.9 %weigh.1 = (bf16[32,2432]{1,0:T(8,128)(2,1)S(1)}, bf16[32,2304]{1,0:T(8,128)(2,1)S(1)}) custom-call(s32[16]{0:T(128)} %ids_hbm.1, bf16[16,2,4608]{2,1,0:T(2,128)(2,1)} %p_hbm.1, f32[64,4608]{1,0:T(8,128)} %ctf_ref.3, f32[4608]{0:T(1024)} %nw_hbm.1), custom_call_target="tpu_custom_call" | custom-call | flops 294912 | bytes 1179648 | tf_op jit(solution)/shard_map/weigh/pallas_call | solution.py:38
  2.6 4.1 %collective-permute-start.1 = (bf16[32,2432]{1,0:T(8,128)(2,1)S(1)}, bf16[32,2432]{1,0:T(8,128)(2,1)S(1)}, u32[]{:S(2)}, u32[]{:S(2)}) collective-permute-start(bf16[32,2432]{1,0:T(8,128)(2,1)S(1)} %get-tuple-element.26.refs_0_), channel_id=1, source_target_pairs={{0,8},{4,12},{8,0},{12,4},{1,9},{5,13},{9,1},{13,5},{2,10},{6,14},... | collective-permute-start | bytes 466952 | tf_op jit(solution)/shard_map/ppermute | solution.py:461
  6.7 1.6 %collective-permute-start.2 = (bf16[32,2432]{1,0:T(8,128)(2,1)S(1)}, bf16[32,2432]{1,0:T(8,128)(2,1)S(1)}, u32[]{:S(2)}, u32[]{:S(2)}) collective-permute-start(bf16[32,2432]{1,0:T(8,128)(2,1)S(1)} %get-tuple-element.26.refs_0_), channel_id=1, source_target_pairs={{0,4},{4,0},{8,12},{12,8},{1,5},{5,1},{9,13},{13,9},{2,6},{6,2},{1... | collective-permute-start | bytes 466952 | tf_op jit(solution)/shard_map/ppermute | solution.py:461
  8.3 0.0 copy-done.3
  8.3 0.0 copy-done.4
  8.3 1.1 %copy.10 = bf16[32,2,4608]{2,0,1:T(8,128)(2,1)S(1)} copy(bf16[32,2,4608]{2,1,0:T(2,128)(2,1)} %param.7) | data formatting | bytes 1179648 | tf_op args[1]
  9.5 0.1 fusion
  9.6 0.1 fusion.2
  9.7 0.0 copy-done.2
  9.7 6.7 %templates.1 = (bf16[768,9216]{1,0:T(8,128)(2,1)S(1)}, f32[24,4608]{1,0:T(8,128)S(1)}, f32[24,4608]{1,0:T(8,128)S(1)}, f32[32,64]{1,0:T(8,128)S(1)}) custom-call(bf16[2,32,4608]{2,1,0:T(8,128)(2,1)S(1)} %bitcast.10, f32[24,128]{1,0:T(8,128)S(1)} %get-tuple-element.51.xc_ref, f32[24,128]{1,0:T(8,128)S(1)} %get-tuple-element.50.xs_ref, ...), custom_call_target="tpu_custom_call" | custom-call | flops 141557760 | bytes 14155776 | tf_op jit(solution)/shard_map/templates/pallas_call | solution.py:38
  16.4 0.0 copy-start
  16.4 5.0 %copy-done = bf16[768,9216]{1,0:T(8,128)(2,1)} copy-done((bf16[768,9216]{1,0:T(8,128)(2,1)}, bf16[768,9216]{1,0:T(8,128)(2,1)S(1)}, u32[]{:S(2)}) %copy-start) | copy-done | bytes 14155800
  21.4 0.0 collective-permute-done.1.refs_2_
  21.4 0.5 collective-permute-start.3
  21.9 0.1 collective-permute-start
  22.0 1.8 %collective-permute-start.4 = (bf16[32,2304]{1,0:T(8,128)(2,1)S(1)}, bf16[32,2304]{1,0:T(8,128)(2,1)S(1)}, u32[]{:S(2)}, u32[]{:S(2)}) collective-permute-start(bf16[32,2304]{1,0:T(8,128)(2,1)S(1)} %get-tuple-element.25.refs_4_), channel_id=1, source_target_pairs={{0,4},{4,0},{8,12},{12,8},{1,5},{5,1},{9,13},{13,9},{2,6},{6,2},{1... | collective-permute-start | bytes 442376 | tf_op jit(solution)/shard_map/ppermute | solution.py:461
  23.8 7.0 %collective-permute-done.refs_6_ = bf16[32,2304]{1,0:T(8,128)(2,1)S(1)} collective-permute-done((bf16[32,2304]{1,0:T(8,128)(2,1)S(1)}, bf16[32,2304]{1,0:T(8,128)(2,1)S(1)}, u32[]{:S(2)}, u32[]{:S(2)}) %collective-permute-start) | collective-permute-done | bytes 147488 | tf_op jit(solution)/shard_map/ppermute | solution.py:461
  30.9 0.4 collective-permute-start.5
  31.3 0.0 collective-permute-done.2.refs_1_
  31.3 0.0 collective-permute-done.3.refs_3_
  31.3 0.0 copy-start.1
  31.3 5.0 %copy-done.1 = bf16[768,9216]{1,0:T(8,128)(2,1)S(1)} copy-done((bf16[768,9216]{1,0:T(8,128)(2,1)S(1)}, bf16[768,9216]{1,0:T(8,128)(2,1)}, u32[]{:S(2)}) %copy-start.1) | copy-done | bytes 14155800
  36.3 2.0 %score0.1.refs_8_ = f32[768,128]{1,0:T(8,128)S(1)} custom-call(bf16[768,9216]{1,0:T(8,128)(2,1)S(1)} %copy-done.1, bf16[32,2432]{1,0:T(8,128)(2,1)S(1)} %get-tuple-element.26.refs_0_, bf16[32,2432]{1,0:T(8,128)(2,1)S(1)} %collective-permute-done.2.refs_1_, bf16[32,2432]{1,0:T(8,128)(2,1)S(1)} %collective-permute-done.1.refs_2_, ...), custom_call_target="tpu_custom_call" | custom-call | flops 1811939328 | tf_op jit(solution)/shard_map/score0/pallas_call | solution.py:38
  38.4 0.0 collective-permute-done.4.refs_5_
  38.4 0.0 collective-permute-done.5.refs_7_
  38.4 2.3 %score1.1 = (f32[768,128]{1,0:T(8,128)S(1)}, bf16[128,4608]{1,0:T(8,128)(2,1)S(1)}, f32[128,64]{1,0:T(8,128)S(1)}, f32[8,128]{1,0:T(8,128)S(1)}) custom-call(bf16[768,9216]{1,0:T(8,128)(2,1)S(1)} %copy-done.1, f32[32,64]{1,0:T(8,128)S(1)} %get-tuple-element.29.pow_ref, bf16[32,2432]{1,0:T(8,128)(2,1)S(1)} %get-tuple-element.26.refs_0_, ...), custom_call_target="tpu_custom_call" | custom-call | flops 1811939328 | tf_op jit(solution)/shard_map/score1/pallas_call | solution.py:38
  40.7 1.6 %collective-permute-start.6 = (f32[8,128]{1,0:T(8,128)S(1)}, f32[8,128]{1,0:T(8,128)S(1)}, u32[]{:S(2)}, u32[]{:S(2)}) collective-permute-start(f32[8,128]{1,0:T(8,128)S(1)} %get-tuple-element.37.refs_0_), channel_id=1, source_target_pairs={{0,4},{4,0},{8,12},{12,8},{1,5},{5,1},{9,13},{13,9},{2,6},{6,2},{1... | collective-permute-start | bytes 12296 | tf_op jit(solution)/shard_map/ppermute | solution.py:461
  42.4 1.9 %collective-permute-start.7 = (f32[8,128]{1,0:T(8,128)S(1)}, f32[8,128]{1,0:T(8,128)S(1)}, u32[]{:S(2)}, u32[]{:S(2)}) collective-permute-start(f32[8,128]{1,0:T(8,128)S(1)} %get-tuple-element.37.refs_0_), channel_id=1, source_target_pairs={{0,8},{4,12},{8,0},{12,4},{1,9},{5,13},{9,1},{13,5},{2,10},{6,14},... | collective-permute-start | bytes 12296 | tf_op jit(solution)/shard_map/ppermute | solution.py:461
  44.3 0.9 %collective-permute-start.8 = (f32[8,128]{1,0:T(8,128)S(1)}, f32[8,128]{1,0:T(8,128)S(1)}, u32[]{:S(2)}, u32[]{:S(2)}) collective-permute-start(f32[8,128]{1,0:T(8,128)S(1)} %get-tuple-element.37.refs_0_), channel_id=1, source_target_pairs={{0,12},{4,8},{8,4},{12,0},{1,13},{5,9},{9,5},{13,1},{2,14},{6,10},... | collective-permute-start | bytes 12296 | tf_op jit(solution)/shard_map/ppermute | solution.py:461
  45.2 0.1 pad_add_fusion.me_ref
  45.3 0.0 collective-permute-done.6.refs_1_
  45.3 1.6 %collective-permute-done.7.refs_2_ = f32[8,128]{1,0:T(8,128)S(1)} collective-permute-done((f32[8,128]{1,0:T(8,128)S(1)}, f32[8,128]{1,0:T(8,128)S(1)}, u32[]{:S(2)}, u32[]{:S(2)}) %collective-permute-start.7) | collective-permute-done | bytes 4128 | tf_op jit(solution)/shard_map/ppermute | solution.py:461
  46.9 2.8 %collective-permute-done.8.refs_3_ = f32[8,128]{1,0:T(8,128)S(1)} collective-permute-done((f32[8,128]{1,0:T(8,128)S(1)}, f32[8,128]{1,0:T(8,128)S(1)}, u32[]{:S(2)}, u32[]{:S(2)}) %collective-permute-start.8) | collective-permute-done | bytes 4128 | tf_op jit(solution)/shard_map/ppermute | solution.py:461
  49.7 5.2 %responsibilities.1 = (f32[32,64]{1,0:T(8,128)}, bf16[2,768,128]{2,1,0:T(8,128)(2,1)S(1)}, f32[32,64]{1,0:T(8,128)S(1)}, bf16[32,2432]{1,0:T(8,128)(2,1)S(1)}, b...) custom-call(s32[2]{0:T(128)S(1)} %pad_add_fusion.me_ref, f32[768,128]{1,0:T(8,128)S(1)} %get-tuple-element.32.s_ref, ...), custom_call_target="tpu_custom_call" | custom-call | flops 2717908992 | tf_op jit(solution)/shard_map/responsibilities/pallas_call | solution.py:38
  54.9 1.5 %collective-permute-start.10 = (bf16[32,2432]{1,0:T(8,128)(2,1)S(1)}, bf16[32,2432]{1,0:T(8,128)(2,1)S(1)}, u32[]{:S(2)}, u32[]{:S(2)}) collective-permute-start(bf16[32,2432]{1,0:T(8,128)(2,1)S(1)} %get-tuple-element.44), channel_id=1, source_target_pairs={{0,2},{1,3},{2,0},{3,1},{4,6},{5,7},{6,4},{7,5},{8,10},{9,11},{10,... | collective-permute-start | bytes 466952 | tf_op jit(solution)/shard_map/ppermute | solution.py:461
  56.3 0.0 collective-permute-start.11
  56.3 0.7 %collective-permute-start.9 = (bf16[32,2432]{1,0:T(8,128)(2,1)S(1)}, bf16[32,2432]{1,0:T(8,128)(2,1)S(1)}, u32[]{:S(2)}, u32[]{:S(2)}) collective-permute-start(bf16[32,2432]{1,0:T(8,128)(2,1)S(1)} %get-tuple-element.43), channel_id=1, source_target_pairs={{0,3},{1,2},{2,1},{3,0},{4,7},{5,6},{6,5},{7,4},{8,11},{9,10},{10,... | collective-permute-start | bytes 466952 | tf_op jit(solution)/shard_map/ppermute | solution.py:461
  57.0 1.6 %own_slice.1 = (f32[32,2304]{1,0:T(8,128)S(1)}, f32[64,1152]{1,0:T(8,128)S(1)}) custom-call(s32[2]{0:T(128)S(1)} %pad_add_fusion.me_ref, bf16[2,768,128]{2,1,0:T(8,128)(2,1)S(1)} %get-tuple-element.39.rho_ref, f32[24,4608]{1,0:T(8,128)S(1)} %get-tuple-element.34.cos_ref, f32[24,4608]{1,0:T(8,128)S(1)} %get-tuple-element.35.sin_ref, ...), custom_call_target="tpu_custom_call" | custom-call | flops 905969664 | tf_op jit(solution)/shard_map/own_slice/pallas_call | solution.py:38
  58.7 2.2 %collective-permute-done.10.refs_1_ = bf16[32,2432]{1,0:T(8,128)(2,1)S(1)} collective-permute-done((bf16[32,2432]{1,0:T(8,128)(2,1)S(1)}, bf16[32,2432]{1,0:T(8,128)(2,1)S(1)}, u32[]{:S(2)}, u32[]{:S(2)}) %collective-permute-start.10) | collective-permute-done | bytes 155680 | tf_op jit(solution)/shard_map/ppermute | solution.py:461
  60.9 0.0 collective-permute-done.11.refs_2_
  60.9 1.7 %collective-permute-done.9.refs_0_ = bf16[32,2432]{1,0:T(8,128)(2,1)S(1)} collective-permute-done((bf16[32,2432]{1,0:T(8,128)(2,1)S(1)}, bf16[32,2432]{1,0:T(8,128)(2,1)S(1)}, u32[]{:S(2)}, u32[]{:S(2)}) %collective-permute-start.9) | collective-permute-done | bytes 155680 | tf_op jit(solution)/shard_map/ppermute | solution.py:461
  62.6 1.1 %finish.1 = f32[32,2,1152]{2,1,0:T(2,128)} custom-call(f32[64,1152]{1,0:T(8,128)S(1)} %get-tuple-element.40.cw_ref, f32[32,64]{1,0:T(8,128)S(1)} %get-tuple-element.41.mass_ref, f32[32,2304]{1,0:T(8,128)S(1)} %get-tuple-element.42.own_ref, bf16[32,2432]{1,0:T(8,128)(2,1)S(1)} %collective-permute-done.9.refs_0_, ...), custom_call_target="tpu_custom_call" | custom-call | tf_op jit(solution)/shard_map/finish/pallas_call | solution.py:38
  (4 shorter events, 0.0 us)
Async XLA Ops:
  0.6 7.7 %copy-start.3 = (f32[4608]{0:T(1024)S(1)}, f32[4608]{0:T(1024)}, u32[]{:S(2)}) copy-start(f32[4608]{0:T(1024)} %nw_hbm.1) | copy-start | bytes 55300
  0.6 9.1 %copy-start.2 = (f32[64,4608]{1,0:T(8,128)S(1)}, f32[64,4608]{1,0:T(8,128)}, u32[]{:S(2)}) copy-start(f32[64,4608]{1,0:T(8,128)} %ctf_ref.3) | copy-start | bytes 3538948
  0.7 7.7 %copy-start.4 = (s32[24,2]{0,1:T(2,128)S(1)}, s32[24,2]{0,1:T(2,128)}, u32[]{:S(2)}) copy-start(s32[24,2]{0,1:T(2,128)} %param.11) | copy-start | bytes 580
  2.6 18.8 %collective-permute-start.1 = (bf16[32,2432]{1,0:T(8,128)(2,1)S(1)}, bf16[32,2432]{1,0:T(8,128)(2,1)S(1)}, u32[]{:S(2)}, u32[]{:S(2)}) collective-permute-start(bf16[32,2432]{1,0:T(8,128)(2,1)S(1)} %get-tuple-element.26.refs_0_), channel_id=1, source_target_pairs={{0,8},{4,12},{8,0},{12,4},{1,9},{5,13},{9,1},{13,5},{2,10},{6,14},... | collective-permute-start | bytes 466952 | tf_op jit(solution)/shard_map/ppermute | solution.py:461
  6.7 24.6 %collective-permute-start.2 = (bf16[32,2432]{1,0:T(8,128)(2,1)S(1)}, bf16[32,2432]{1,0:T(8,128)(2,1)S(1)}, u32[]{:S(2)}, u32[]{:S(2)}) collective-permute-start(bf16[32,2432]{1,0:T(8,128)(2,1)S(1)} %get-tuple-element.26.refs_0_), channel_id=1, source_target_pairs={{0,4},{4,0},{8,12},{12,8},{1,5},{5,1},{9,13},{13,9},{2,6},{6,2},{1... | collective-permute-start | bytes 466952 | tf_op jit(solution)/shard_map/ppermute | solution.py:461
  16.4 5.0 %copy-start = (bf16[768,9216]{1,0:T(8,128)(2,1)}, bf16[768,9216]{1,0:T(8,128)(2,1)S(1)}, u32[]{:S(2)}) copy-start(bf16[768,9216]{1,0:T(8,128)(2,1)S(1)} %get-tuple-element.24.temp_ref) | copy-start | bytes 42467332
  21.4 9.8 %collective-permute-start.3 = (bf16[32,2432]{1,0:T(8,128)(2,1)S(1)}, bf16[32,2432]{1,0:T(8,128)(2,1)S(1)}, u32[]{:S(2)}, u32[]{:S(2)}) collective-permute-start(bf16[32,2432]{1,0:T(8,128)(2,1)S(1)} %collective-permute-done.1.refs_2_), channel_id=1, source_target_pairs={{0,4},{4,0},{8,12},{12,8},{1,5},{5,1},{9,13},{13,9},{2,6},{6,2},{1... | collective-permute-start | bytes 466952 | tf_op jit(solution)/shard_map/ppermute | solution.py:461
  21.9 9.0 %collective-permute-start = (bf16[32,2304]{1,0:T(8,128)(2,1)S(1)}, bf16[32,2304]{1,0:T(8,128)(2,1)S(1)}, u32[]{:S(2)}, u32[]{:S(2)}) collective-permute-start(bf16[32,2304]{1,0:T(8,128)(2,1)S(1)} %get-tuple-element.25.refs_4_), channel_id=1, source_target_pairs={{0,8},{4,12},{8,0},{12,4},{1,9},{5,13},{9,1},{13,5},{2,10},{6,14},... | collective-permute-start | bytes 442376 | tf_op jit(solution)/shard_map/ppermute | solution.py:461
  22.0 16.4 %collective-permute-start.4 = (bf16[32,2304]{1,0:T(8,128)(2,1)S(1)}, bf16[32,2304]{1,0:T(8,128)(2,1)S(1)}, u32[]{:S(2)}, u32[]{:S(2)}) collective-permute-start(bf16[32,2304]{1,0:T(8,128)(2,1)S(1)} %get-tuple-element.25.refs_4_), channel_id=1, source_target_pairs={{0,4},{4,0},{8,12},{12,8},{1,5},{5,1},{9,13},{13,9},{2,6},{6,2},{1... | collective-permute-start | bytes 442376 | tf_op jit(solution)/shard_map/ppermute | solution.py:461
  30.9 7.5 %collective-permute-start.5 = (bf16[32,2304]{1,0:T(8,128)(2,1)S(1)}, bf16[32,2304]{1,0:T(8,128)(2,1)S(1)}, u32[]{:S(2)}, u32[]{:S(2)}) collective-permute-start(bf16[32,2304]{1,0:T(8,128)(2,1)S(1)} %collective-permute-done.refs_6_), channel_id=1, source_target_pairs={{0,4},{4,0},{8,12},{12,8},{1,5},{5,1},{9,13},{13,9},{2,6},{6,2},{1... | collective-permute-start | bytes 442376 | tf_op jit(solution)/shard_map/ppermute | solution.py:461
  31.3 5.0 %copy-start.1 = (bf16[768,9216]{1,0:T(8,128)(2,1)S(1)}, bf16[768,9216]{1,0:T(8,128)(2,1)}, u32[]{:S(2)}) copy-start(bf16[768,9216]{1,0:T(8,128)(2,1)} %copy-done) | copy-start | bytes 42467332
  40.7 4.5 %collective-permute-start.6 = (f32[8,128]{1,0:T(8,128)S(1)}, f32[8,128]{1,0:T(8,128)S(1)}, u32[]{:S(2)}, u32[]{:S(2)}) collective-permute-start(f32[8,128]{1,0:T(8,128)S(1)} %get-tuple-element.37.refs_0_), channel_id=1, source_target_pairs={{0,4},{4,0},{8,12},{12,8},{1,5},{5,1},{9,13},{13,9},{2,6},{6,2},{1... | collective-permute-start | bytes 12296 | tf_op jit(solution)/shard_map/ppermute | solution.py:461
  42.4 4.5 %collective-permute-start.7 = (f32[8,128]{1,0:T(8,128)S(1)}, f32[8,128]{1,0:T(8,128)S(1)}, u32[]{:S(2)}, u32[]{:S(2)}) collective-permute-start(f32[8,128]{1,0:T(8,128)S(1)} %get-tuple-element.37.refs_0_), channel_id=1, source_target_pairs={{0,8},{4,12},{8,0},{12,4},{1,9},{5,13},{9,1},{13,5},{2,10},{6,14},... | collective-permute-start | bytes 12296 | tf_op jit(solution)/shard_map/ppermute | solution.py:461
  44.3 5.4 %collective-permute-start.8 = (f32[8,128]{1,0:T(8,128)S(1)}, f32[8,128]{1,0:T(8,128)S(1)}, u32[]{:S(2)}, u32[]{:S(2)}) collective-permute-start(f32[8,128]{1,0:T(8,128)S(1)} %get-tuple-element.37.refs_0_), channel_id=1, source_target_pairs={{0,12},{4,8},{8,4},{12,0},{1,13},{5,9},{9,5},{13,1},{2,14},{6,10},... | collective-permute-start | bytes 12296 | tf_op jit(solution)/shard_map/ppermute | solution.py:461
  54.9 6.0 %collective-permute-start.10 = (bf16[32,2432]{1,0:T(8,128)(2,1)S(1)}, bf16[32,2432]{1,0:T(8,128)(2,1)S(1)}, u32[]{:S(2)}, u32[]{:S(2)}) collective-permute-start(bf16[32,2432]{1,0:T(8,128)(2,1)S(1)} %get-tuple-element.44), channel_id=1, source_target_pairs={{0,2},{1,3},{2,0},{3,1},{4,6},{5,7},{6,4},{7,5},{8,10},{9,11},{10,... | collective-permute-start | bytes 466952 | tf_op jit(solution)/shard_map/ppermute | solution.py:461
  56.3 4.6 %collective-permute-start.11 = (bf16[32,2432]{1,0:T(8,128)(2,1)S(1)}, bf16[32,2432]{1,0:T(8,128)(2,1)S(1)}, u32[]{:S(2)}, u32[]{:S(2)}) collective-permute-start(bf16[32,2432]{1,0:T(8,128)(2,1)S(1)} %get-tuple-element.45), channel_id=1, source_target_pairs={{0,1},{1,0},{2,3},{3,2},{4,5},{5,4},{6,7},{7,6},{8,9},{9,8},{10,11... | collective-permute-start | bytes 466952 | tf_op jit(solution)/shard_map/ppermute | solution.py:461
  56.3 6.3 %collective-permute-start.9 = (bf16[32,2432]{1,0:T(8,128)(2,1)S(1)}, bf16[32,2432]{1,0:T(8,128)(2,1)S(1)}, u32[]{:S(2)}, u32[]{:S(2)}) collective-permute-start(bf16[32,2432]{1,0:T(8,128)(2,1)S(1)} %get-tuple-element.43), channel_id=1, source_target_pairs={{0,3},{1,2},{2,1},{3,0},{4,7},{5,6},{6,5},{7,4},{8,11},{9,10},{10,... | collective-permute-start | bytes 466952 | tf_op jit(solution)/shard_map/ppermute | solution.py:461

commit v4 on v3

--- a/solution.py
+++ b/solution.py
@@ -231,6 +231,7 @@
 
 def score(temps, power, gathered, freq):
     span = freq // CHUNKS
+    temps = pltpu.with_memory_space_constraint(temps, pltpu.VMEM)
     lanes = sum(p.shape[0] for p in gathered[0])
     acc_shape = jax.ShapeDtypeStruct((temps.shape[0], lanes), f32)
     flops = 2 * temps.shape[0] * 256 * 2 * span
@@ -494,8 +495,7 @@
         split, phase_tables(shifts, freq), ctf, noise_weight
     )
     if pairwise:
-        for shard in direct:
-            shard[-1], power = lax.optimization_barrier((shard[-1], power))
+        direct, power = lax.optimization_barrier((direct, power))
         gathered = [gather_pairs(w, d) for w, d in zip(shards, direct)]
     scores, weighted, marks, stat = score(temps, power, gathered, freq)
     if pairwise:

time: 64.2 us -> 62.1 us (0.967)
  waiting for transfers between devices: 15.4 us -> 13.6 us
    ppermute x12, waiting for transfers between devices: 15.4 us -> 13.6 us  [swap(): return lax.ppermute(values, axis, [(i, i ^ distance) for i in range(size)])]
  transfers between devices with their start and end apart: 12 -> 12, of which waited for: 5 -> 5; matrix products, arithmetic and copies ran while one was open for 2% -> 2% of each run, Pallas kernels for 16% -> 17%
where the time goes in v4:
time: 62.1 us; the launch traced here: 61.7 us
  Pallas kernels  20.9 us (34%)
  starting transfers between devices  14.8 us (24%)
  waiting for transfers between devices  13.6 us (22%)
  local copies, waits for them, and re-layouts  11.2 us (18%)
  between operations  0.78 us (1%)
    pallas_call x7, Pallas kernels, call(): pl.pallas_call(kernel, in_specs=in_specs, out_specs=[VMEM] * len(out_shap...  20.9 us
    ppermute x12, starting transfers between devices, swap(): return lax.ppermute(values, axis, [(i, i ^ distance) for i in range(size)])  14.8 us
    ppermute x12, waiting for transfers between devices, swap(): return lax.ppermute(values, axis, [(i, i ^ distance) for i in range(size)])  13.6 us
    unnamed x11, local copies, waits for them, and re-layouts  11.2 us
  transfers between devices with their start and end apart: 12, of which 5 were waited for; matrix products, arithmetic and copies ran while one was open for 2% of the time, Pallas kernels for 17%

profile of v4, /device:TPU:0, one launch (start us, length us, event | category | flops | bytes accessed | tf_op | source)
XLA Modules:
  0.0 61.7 jit_solution(12050325143541367920)
XLA Ops:
  0.6 0.0 copy-start.3
  0.6 0.0 copy-start.2
  0.7 0.0 copy-start.4
  0.7 1.9 %weigh.1 = (bf16[32,2432]{1,0:T(8,128)(2,1)S(1)}, bf16[32,2304]{1,0:T(8,128)(2,1)S(1)}) custom-call(s32[16]{0:T(128)} %ids_hbm.1, bf16[16,2,4608]{2,1,0:T(2,128)(2,1)} %p_hbm.1, f32[64,4608]{1,0:T(8,128)} %ctf_ref.3, f32[4608]{0:T(1024)} %nw_hbm.1), custom_call_target="tpu_custom_call" | custom-call | flops 294912 | bytes 1179648 | tf_op jit(solution)/shard_map/weigh/pallas_call | solution.py:38
  2.6 3.1 %collective-permute-start = (bf16[32,2432]{1,0:T(8,128)(2,1)S(1)}, bf16[32,2432]{1,0:T(8,128)(2,1)S(1)}, u32[]{:S(2)}, u32[]{:S(2)}) collective-permute-start(bf16[32,2432]{1,0:T(8,128)(2,1)S(1)} %get-tuple-element.26.refs_0_), channel_id=1, source_target_pairs={{0,4},{4,0},{8,12},{12,8},{1,5},{5,1},{9,13},{13,9},{2,6},{6,2},{1... | collective-permute-start | bytes 466952 | tf_op jit(solution)/shard_map/ppermute | solution.py:462
  5.7 2.6 %collective-permute-start.1 = (bf16[32,2432]{1,0:T(8,128)(2,1)S(1)}, bf16[32,2432]{1,0:T(8,128)(2,1)S(1)}, u32[]{:S(2)}, u32[]{:S(2)}) collective-permute-start(bf16[32,2432]{1,0:T(8,128)(2,1)S(1)} %get-tuple-element.26.refs_0_), channel_id=1, source_target_pairs={{0,8},{4,12},{8,0},{12,4},{1,9},{5,13},{9,1},{13,5},{2,10},{6,14},... | collective-permute-start | bytes 466952 | tf_op jit(solution)/shard_map/ppermute | solution.py:462
  8.3 0.4 collective-permute-start.2
  8.7 0.0 collective-permute-start.3
  8.7 0.0 copy-done.3
  8.8 0.0 copy-done.4
  8.8 1.1 %copy.10 = bf16[32,2,4608]{2,0,1:T(8,128)(2,1)S(1)} copy(bf16[32,2,4608]{2,1,0:T(2,128)(2,1)} %param.7) | data formatting | bytes 1179648 | tf_op args[1]
  9.9 0.1 fusion
  10.1 0.1 fusion.2
  10.2 0.0 copy-done.2
  10.2 6.7 %templates.1 = (bf16[768,9216]{1,0:T(8,128)(2,1)S(1)}, f32[24,4608]{1,0:T(8,128)S(1)}, f32[24,4608]{1,0:T(8,128)S(1)}, f32[32,64]{1,0:T(8,128)S(1)}) custom-call(bf16[2,32,4608]{2,1,0:T(8,128)(2,1)S(1)} %bitcast.10, f32[24,128]{1,0:T(8,128)S(1)} %get-tuple-element.53.xc_ref, f32[24,128]{1,0:T(8,128)S(1)} %get-tuple-element.52.xs_ref, ...), custom_call_target="tpu_custom_call" | custom-call | flops 141557760 | bytes 14155776 | tf_op jit(solution)/shard_map/templates/pallas_call | solution.py:38
  16.9 0.0 copy-start
  16.9 5.0 %copy-done = bf16[768,9216]{1,0:T(8,128)(2,1)} copy-done((bf16[768,9216]{1,0:T(8,128)(2,1)}, bf16[768,9216]{1,0:T(8,128)(2,1)S(1)}, u32[]{:S(2)}) %copy-start) | copy-done | bytes 14155800
  21.9 0.0 collective-permute-done.2.refs_5_
  21.9 0.0 collective-permute-done.3.refs_6_
  21.9 0.0 collective-permute-done.refs_1_
  21.9 0.0 collective-permute-done.1.refs_2_
  21.9 2.0 %collective-permute-start.4 = (bf16[32,2432]{1,0:T(8,128)(2,1)S(1)}, bf16[32,2432]{1,0:T(8,128)(2,1)S(1)}, u32[]{:S(2)}, u32[]{:S(2)}) collective-permute-start(bf16[32,2432]{1,0:T(8,128)(2,1)S(1)} %collective-permute-done.1.refs_2_), channel_id=1, source_target_pairs={{0,4},{4,0},{8,12},{12,8},{1,5},{5,1},{9,13},{13,9},{2,6},{6,2},{1... | collective-permute-start | bytes 466952 | tf_op jit(solution)/shard_map/ppermute | solution.py:462
  23.9 0.1 collective-permute-start.5
  24.0 4.5 %collective-permute-done.4.refs_3_ = bf16[32,2432]{1,0:T(8,128)(2,1)S(1)} collective-permute-done((bf16[32,2432]{1,0:T(8,128)(2,1)S(1)}, bf16[32,2432]{1,0:T(8,128)(2,1)S(1)}, u32[]{:S(2)}, u32[]{:S(2)}) %collective-permute-start.4) | collective-permute-done | bytes 155680 | tf_op jit(solution)/shard_map/ppermute | solution.py:462
  28.5 0.0 copy-start.1
  28.5 5.0 %copy-done.1 = bf16[768,9216]{1,0:T(8,128)(2,1)S(1)} copy-done((bf16[768,9216]{1,0:T(8,128)(2,1)S(1)}, bf16[768,9216]{1,0:T(8,128)(2,1)}, u32[]{:S(2)}) %copy-start.1) | copy-done | bytes 14155800
  33.5 2.0 %score0.1.refs_8_ = f32[768,128]{1,0:T(8,128)S(1)} custom-call(bf16[768,9216]{1,0:T(8,128)(2,1)S(1)} %copy-done.1, bf16[32,2432]{1,0:T(8,128)(2,1)S(1)} %get-tuple-element.26.refs_0_, bf16[32,2432]{1,0:T(8,128)(2,1)S(1)} %collective-permute-done.refs_1_, bf16[32,2432]{1,0:T(8,128)(2,1)S(1)} %collective-permute-done.1.refs_2_, ...), custom_call_target="tpu_custom_call" | custom-call | flops 1811939328 | tf_op jit(solution)/shard_map/score0/pallas_call | solution.py:38
  35.6 0.0 collective-permute-done.5.refs_7_
  35.6 2.3 %score1.1 = (f32[768,128]{1,0:T(8,128)S(1)}, bf16[128,4608]{1,0:T(8,128)(2,1)S(1)}, f32[128,64]{1,0:T(8,128)S(1)}, f32[8,128]{1,0:T(8,128)S(1)}) custom-call(bf16[768,9216]{1,0:T(8,128)(2,1)S(1)} %copy-done.1, f32[32,64]{1,0:T(8,128)S(1)} %get-tuple-element.29.pow_ref, bf16[32,2432]{1,0:T(8,128)(2,1)S(1)} %get-tuple-element.26.refs_0_, ...), custom_call_target="tpu_custom_call" | custom-call | flops 1811939328 | tf_op jit(solution)/shard_map/score1/pallas_call | solution.py:38
  37.9 1.7 %collective-permute-start.6 = (f32[8,128]{1,0:T(8,128)S(1)}, f32[8,128]{1,0:T(8,128)S(1)}, u32[]{:S(2)}, u32[]{:S(2)}) collective-permute-start(f32[8,128]{1,0:T(8,128)S(1)} %get-tuple-element.39.refs_0_), channel_id=1, source_target_pairs={{0,4},{4,0},{8,12},{12,8},{1,5},{5,1},{9,13},{13,9},{2,6},{6,2},{1... | collective-permute-start | bytes 12296 | tf_op jit(solution)/shard_map/ppermute | solution.py:462
  39.6 2.6 %collective-permute-start.7 = (f32[8,128]{1,0:T(8,128)S(1)}, f32[8,128]{1,0:T(8,128)S(1)}, u32[]{:S(2)}, u32[]{:S(2)}) collective-permute-start(f32[8,128]{1,0:T(8,128)S(1)} %get-tuple-element.39.refs_0_), channel_id=1, source_target_pairs={{0,8},{4,12},{8,0},{12,4},{1,9},{5,13},{9,1},{13,5},{2,10},{6,14},... | collective-permute-start | bytes 12296 | tf_op jit(solution)/shard_map/ppermute | solution.py:462
  42.2 0.2 collective-permute-start.8
  42.4 0.1 pad_add_fusion.me_ref
  42.4 0.0 collective-permute-done.6.refs_1_
  42.4 1.7 %collective-permute-done.7.refs_2_ = f32[8,128]{1,0:T(8,128)S(1)} collective-permute-done((f32[8,128]{1,0:T(8,128)S(1)}, f32[8,128]{1,0:T(8,128)S(1)}, u32[]{:S(2)}, u32[]{:S(2)}) %collective-permute-start.7) | collective-permute-done | bytes 4128 | tf_op jit(solution)/shard_map/ppermute | solution.py:462
  44.1 3.5 %collective-permute-done.8.refs_3_ = f32[8,128]{1,0:T(8,128)S(1)} collective-permute-done((f32[8,128]{1,0:T(8,128)S(1)}, f32[8,128]{1,0:T(8,128)S(1)}, u32[]{:S(2)}, u32[]{:S(2)}) %collective-permute-start.8) | collective-permute-done | bytes 4128 | tf_op jit(solution)/shard_map/ppermute | solution.py:462
  47.6 5.2 %responsibilities.1 = (f32[32,64]{1,0:T(8,128)}, bf16[2,768,128]{2,1,0:T(8,128)(2,1)S(1)}, f32[32,64]{1,0:T(8,128)S(1)}, bf16[32,2432]{1,0:T(8,128)(2,1)S(1)}, b...) custom-call(s32[2]{0:T(128)S(1)} %pad_add_fusion.me_ref, f32[768,128]{1,0:T(8,128)S(1)} %get-tuple-element.34.s_ref, ...), custom_call_target="tpu_custom_call" | custom-call | flops 2717908992 | tf_op jit(solution)/shard_map/responsibilities/pallas_call | solution.py:38
  52.8 1.5 %collective-permute-start.10 = (bf16[32,2432]{1,0:T(8,128)(2,1)S(1)}, bf16[32,2432]{1,0:T(8,128)(2,1)S(1)}, u32[]{:S(2)}, u32[]{:S(2)}) collective-permute-start(bf16[32,2432]{1,0:T(8,128)(2,1)S(1)} %get-tuple-element.46), channel_id=1, source_target_pairs={{0,2},{1,3},{2,0},{3,1},{4,6},{5,7},{6,4},{7,5},{8,10},{9,11},{10,... | collective-permute-start | bytes 466952 | tf_op jit(solution)/shard_map/ppermute | solution.py:462
  54.3 0.0 collective-permute-start.11
  54.3 0.7 %collective-permute-start.9 = (bf16[32,2432]{1,0:T(8,128)(2,1)S(1)}, bf16[32,2432]{1,0:T(8,128)(2,1)S(1)}, u32[]{:S(2)}, u32[]{:S(2)}) collective-permute-start(bf16[32,2432]{1,0:T(8,128)(2,1)S(1)} %get-tuple-element.45), channel_id=1, source_target_pairs={{0,3},{1,2},{2,1},{3,0},{4,7},{5,6},{6,5},{7,4},{8,11},{9,10},{10,... | collective-permute-start | bytes 466952 | tf_op jit(solution)/shard_map/ppermute | solution.py:462
  54.9 1.6 %own_slice.1 = (f32[32,2304]{1,0:T(8,128)S(1)}, f32[64,1152]{1,0:T(8,128)S(1)}) custom-call(s32[2]{0:T(128)S(1)} %pad_add_fusion.me_ref, bf16[2,768,128]{2,1,0:T(8,128)(2,1)S(1)} %get-tuple-element.41.rho_ref, f32[24,4608]{1,0:T(8,128)S(1)} %get-tuple-element.36.cos_ref, f32[24,4608]{1,0:T(8,128)S(1)} %get-tuple-element.37.sin_ref, ...), custom_call_target="tpu_custom_call" | custom-call | flops 905969664 | tf_op jit(solution)/shard_map/own_slice/pallas_call | solution.py:38
  56.6 2.2 %collective-permute-done.10.refs_1_ = bf16[32,2432]{1,0:T(8,128)(2,1)S(1)} collective-permute-done((bf16[32,2432]{1,0:T(8,128)(2,1)S(1)}, bf16[32,2432]{1,0:T(8,128)(2,1)S(1)}, u32[]{:S(2)}, u32[]{:S(2)}) %collective-permute-start.10) | collective-permute-done | bytes 155680 | tf_op jit(solution)/shard_map/ppermute | solution.py:462
  58.8 0.0 collective-permute-done.11.refs_2_
  58.8 1.8 %collective-permute-done.9.refs_0_ = bf16[32,2432]{1,0:T(8,128)(2,1)S(1)} collective-permute-done((bf16[32,2432]{1,0:T(8,128)(2,1)S(1)}, bf16[32,2432]{1,0:T(8,128)(2,1)S(1)}, u32[]{:S(2)}, u32[]{:S(2)}) %collective-permute-start.9) | collective-permute-done | bytes 155680 | tf_op jit(solution)/shard_map/ppermute | solution.py:462
  60.6 1.1 %finish.1 = f32[32,2,1152]{2,1,0:T(2,128)} custom-call(f32[64,1152]{1,0:T(8,128)S(1)} %get-tuple-element.42.cw_ref, f32[32,64]{1,0:T(8,128)S(1)} %get-tuple-element.43.mass_ref, f32[32,2304]{1,0:T(8,128)S(1)} %get-tuple-element.44.own_ref, bf16[32,2432]{1,0:T(8,128)(2,1)S(1)} %collective-permute-done.9.refs_0_, ...), custom_call_target="tpu_custom_call" | custom-call | tf_op jit(solution)/shard_map/finish/pallas_call | solution.py:38
  (4 shorter events, 0.0 us)
Async XLA Ops:
  0.6 8.1 %copy-start.3 = (f32[4608]{0:T(1024)S(1)}, f32[4608]{0:T(1024)}, u32[]{:S(2)}) copy-start(f32[4608]{0:T(1024)} %nw_hbm.1) | copy-start | bytes 55300
  0.6 9.6 %copy-start.2 = (f32[64,4608]{1,0:T(8,128)S(1)}, f32[64,4608]{1,0:T(8,128)}, u32[]{:S(2)}) copy-start(f32[64,4608]{1,0:T(8,128)} %ctf_ref.3) | copy-start | bytes 3538948
  0.7 8.1 %copy-start.4 = (s32[24,2]{0,1:T(2,128)S(1)}, s32[24,2]{0,1:T(2,128)}, u32[]{:S(2)}) copy-start(s32[24,2]{0,1:T(2,128)} %param.11) | copy-start | bytes 580
  2.6 19.3 %collective-permute-start = (bf16[32,2432]{1,0:T(8,128)(2,1)S(1)}, bf16[32,2432]{1,0:T(8,128)(2,1)S(1)}, u32[]{:S(2)}, u32[]{:S(2)}) collective-permute-start(bf16[32,2432]{1,0:T(8,128)(2,1)S(1)} %get-tuple-element.26.refs_0_), channel_id=1, source_target_pairs={{0,4},{4,0},{8,12},{12,8},{1,5},{5,1},{9,13},{13,9},{2,6},{6,2},{1... | collective-permute-start | bytes 466952 | tf_op jit(solution)/shard_map/ppermute | solution.py:462
  5.7 16.2 %collective-permute-start.1 = (bf16[32,2432]{1,0:T(8,128)(2,1)S(1)}, bf16[32,2432]{1,0:T(8,128)(2,1)S(1)}, u32[]{:S(2)}, u32[]{:S(2)}) collective-permute-start(bf16[32,2432]{1,0:T(8,128)(2,1)S(1)} %get-tuple-element.26.refs_0_), channel_id=1, source_target_pairs={{0,8},{4,12},{8,0},{12,4},{1,9},{5,13},{9,1},{13,5},{2,10},{6,14},... | collective-permute-start | bytes 466952 | tf_op jit(solution)/shard_map/ppermute | solution.py:462
  8.3 13.6 %collective-permute-start.2 = (bf16[32,2304]{1,0:T(8,128)(2,1)S(1)}, bf16[32,2304]{1,0:T(8,128)(2,1)S(1)}, u32[]{:S(2)}, u32[]{:S(2)}) collective-permute-start(bf16[32,2304]{1,0:T(8,128)(2,1)S(1)} %get-tuple-element.27.refs_4_), channel_id=1, source_target_pairs={{0,4},{4,0},{8,12},{12,8},{1,5},{5,1},{9,13},{13,9},{2,6},{6,2},{1... | collective-permute-start | bytes 442376 | tf_op jit(solution)/shard_map/ppermute | solution.py:462
  8.7 13.2 %collective-permute-start.3 = (bf16[32,2304]{1,0:T(8,128)(2,1)S(1)}, bf16[32,2304]{1,0:T(8,128)(2,1)S(1)}, u32[]{:S(2)}, u32[]{:S(2)}) collective-permute-start(bf16[32,2304]{1,0:T(8,128)(2,1)S(1)} %get-tuple-element.27.refs_4_), channel_id=1, source_target_pairs={{0,8},{4,12},{8,0},{12,4},{1,9},{5,13},{9,1},{13,5},{2,10},{6,14},... | collective-permute-start | bytes 442376 | tf_op jit(solution)/shard_map/ppermute | solution.py:462
  16.9 5.0 %copy-start = (bf16[768,9216]{1,0:T(8,128)(2,1)}, bf16[768,9216]{1,0:T(8,128)(2,1)S(1)}, u32[]{:S(2)}) copy-start(bf16[768,9216]{1,0:T(8,128)(2,1)S(1)} %get-tuple-element.25.temp_ref) | copy-start | bytes 42467332
  21.9 6.6 %collective-permute-start.4 = (bf16[32,2432]{1,0:T(8,128)(2,1)S(1)}, bf16[32,2432]{1,0:T(8,128)(2,1)S(1)}, u32[]{:S(2)}, u32[]{:S(2)}) collective-permute-start(bf16[32,2432]{1,0:T(8,128)(2,1)S(1)} %collective-permute-done.1.refs_2_), channel_id=1, source_target_pairs={{0,4},{4,0},{8,12},{12,8},{1,5},{5,1},{9,13},{13,9},{2,6},{6,2},{1... | collective-permute-start | bytes 466952 | tf_op jit(solution)/shard_map/ppermute | solution.py:462
  23.9 11.7 %collective-permute-start.5 = (bf16[32,2304]{1,0:T(8,128)(2,1)S(1)}, bf16[32,2304]{1,0:T(8,128)(2,1)S(1)}, u32[]{:S(2)}, u32[]{:S(2)}) collective-permute-start(bf16[32,2304]{1,0:T(8,128)(2,1)S(1)} %collective-permute-done.3.refs_6_), channel_id=1, source_target_pairs={{0,4},{4,0},{8,12},{12,8},{1,5},{5,1},{9,13},{13,9},{2,6},{6,2},{1... | collective-permute-start | bytes 442376 | tf_op jit(solution)/shard_map/ppermute | solution.py:462
  28.5 5.0 %copy-start.1 = (bf16[768,9216]{1,0:T(8,128)(2,1)S(1)}, bf16[768,9216]{1,0:T(8,128)(2,1)}, u32[]{:S(2)}) copy-start(bf16[768,9216]{1,0:T(8,128)(2,1)} %copy-done) | copy-start | bytes 42467332
  37.9 4.5 %collective-permute-start.6 = (f32[8,128]{1,0:T(8,128)S(1)}, f32[8,128]{1,0:T(8,128)S(1)}, u32[]{:S(2)}, u32[]{:S(2)}) collective-permute-start(f32[8,128]{1,0:T(8,128)S(1)} %get-tuple-element.39.refs_0_), channel_id=1, source_target_pairs={{0,4},{4,0},{8,12},{12,8},{1,5},{5,1},{9,13},{13,9},{2,6},{6,2},{1... | collective-permute-start | bytes 12296 | tf_op jit(solution)/shard_map/ppermute | solution.py:462
  39.6 4.5 %collective-permute-start.7 = (f32[8,128]{1,0:T(8,128)S(1)}, f32[8,128]{1,0:T(8,128)S(1)}, u32[]{:S(2)}, u32[]{:S(2)}) collective-permute-start(f32[8,128]{1,0:T(8,128)S(1)} %get-tuple-element.39.refs_0_), channel_id=1, source_target_pairs={{0,8},{4,12},{8,0},{12,4},{1,9},{5,13},{9,1},{13,5},{2,10},{6,14},... | collective-permute-start | bytes 12296 | tf_op jit(solution)/shard_map/ppermute | solution.py:462
  42.2 5.4 %collective-permute-start.8 = (f32[8,128]{1,0:T(8,128)S(1)}, f32[8,128]{1,0:T(8,128)S(1)}, u32[]{:S(2)}, u32[]{:S(2)}) collective-permute-start(f32[8,128]{1,0:T(8,128)S(1)} %get-tuple-element.39.refs_0_), channel_id=1, source_target_pairs={{0,12},{4,8},{8,4},{12,0},{1,13},{5,9},{9,5},{13,1},{2,14},{6,10},... | collective-permute-start | bytes 12296 | tf_op jit(solution)/shard_map/ppermute | solution.py:462
  52.8 6.0 %collective-permute-start.10 = (bf16[32,2432]{1,0:T(8,128)(2,1)S(1)}, bf16[32,2432]{1,0:T(8,128)(2,1)S(1)}, u32[]{:S(2)}, u32[]{:S(2)}) collective-permute-start(bf16[32,2432]{1,0:T(8,128)(2,1)S(1)} %get-tuple-element.46), channel_id=1, source_target_pairs={{0,2},{1,3},{2,0},{3,1},{4,6},{5,7},{6,4},{7,5},{8,10},{9,11},{10,... | collective-permute-start | bytes 466952 | tf_op jit(solution)/shard_map/ppermute | solution.py:462
  54.3 4.5 %collective-permute-start.11 = (bf16[32,2432]{1,0:T(8,128)(2,1)S(1)}, bf16[32,2432]{1,0:T(8,128)(2,1)S(1)}, u32[]{:S(2)}, u32[]{:S(2)}) collective-permute-start(bf16[32,2432]{1,0:T(8,128)(2,1)S(1)} %get-tuple-element.47), channel_id=1, source_target_pairs={{0,1},{1,0},{2,3},{3,2},{4,5},{5,4},{6,7},{7,6},{8,9},{9,8},{10,11... | collective-permute-start | bytes 466952 | tf_op jit(solution)/shard_map/ppermute | solution.py:462
  54.3 6.3 %collective-permute-start.9 = (bf16[32,2432]{1,0:T(8,128)(2,1)S(1)}, bf16[32,2432]{1,0:T(8,128)(2,1)S(1)}, u32[]{:S(2)}, u32[]{:S(2)}) collective-permute-start(bf16[32,2432]{1,0:T(8,128)(2,1)S(1)} %get-tuple-element.45), channel_id=1, source_target_pairs={{0,3},{1,2},{2,1},{3,0},{4,7},{5,6},{6,5},{7,4},{8,11},{9,10},{10,... | collective-permute-start | bytes 466952 | tf_op jit(solution)/shard_map/ppermute | solution.py:462

commit v5 on v4

--- a/solution.py
+++ b/solution.py
@@ -107,30 +107,16 @@
     )
 
 
-def template_kernel(
-    cls_ref, xc_ref, xs_ref, yc_ref, ys_ref, ctf_ref, nw_ref, temp_ref, cos_ref, sin_ref, pow_ref
+def prepare_kernel(
+    cls_ref, xc_ref, xs_ref, yc_ref, ys_ref, ctf_ref, nw_ref, cos_ref, sin_ref, pow_ref
 ):
-    _, rows, freq = cls_ref.shape
-    poses = cos_ref.shape[0]
+    freq = cls_ref.shape[2]
     x_cos, x_sin = xc_ref[...], xs_ref[...]
     for t in range(freq // BOX):
         y_cos = jnp.broadcast_to(yc_ref[:, t : t + 1], x_cos.shape)
         y_sin = jnp.broadcast_to(ys_ref[:, t : t + 1], x_cos.shape)
         cos_ref[:, t * BOX : (t + 1) * BOX] = x_cos * y_cos - x_sin * y_sin
         sin_ref[:, t * BOX : (t + 1) * BOX] = x_sin * y_cos + x_cos * y_sin
-
-    @pl.loop(0, freq // LANES)
-    def _(t):
-        at = pl.ds(pl.multiple_of(t * LANES, LANES), LANES)
-        later = pl.ds(pl.multiple_of(freq + t * LANES, LANES), LANES)
-        re = cls_ref[0, :, at].astype(f32)
-        im = cls_ref[1, :, at].astype(f32)
-        for r in range(poses):
-            cos_r = cos_ref[r : r + 1, at]
-            sin_r = sin_ref[r : r + 1, at]
-            temp_ref[r * rows : (r + 1) * rows, at] = (re * cos_r - im * sin_r).astype(bf16)
-            temp_ref[r * rows : (r + 1) * rows, later] = (re * sin_r + im * cos_r).astype(bf16)
-
     cut = freq // 4
     power = jnp.zeros(pow_ref.shape, f32)
     for q in range(4):
@@ -148,23 +134,52 @@
     pow_ref[...] = power
 
 
-def build_templates(split, tables, ctf, noise_weight):
+def prepare(split, tables, ctf, noise_weight):
     _, rows, freq = split.shape
     poses, groups = tables[0].shape[0], ctf.shape[0]
     return call(
-        template_kernel,
-        "templates",
+        prepare_kernel,
+        "prepare",
         [VMEM] * 7,
         [
-            pltpu.VMEM((poses * rows, 2 * freq), bf16),
-            pltpu.VMEM((poses, freq), f32),
-            pltpu.VMEM((poses, freq), f32),
+            jax.ShapeDtypeStruct((poses, freq), f32),
+            jax.ShapeDtypeStruct((poses, freq), f32),
             jax.ShapeDtypeStruct((rows, groups), f32),
         ],
         (split, *tables, ctf, noise_weight),
+        flops=24 * rows * groups * freq,
+    )
+
+
+def template_kernel(cls_ref, cos_ref, sin_ref, temp_ref):
+    _, rows, freq = cls_ref.shape
+    poses = cos_ref.shape[0]
+
+    @pl.loop(0, freq // LANES)
+    def _(t):
+        at = pl.ds(pl.multiple_of(t * LANES, LANES), LANES)
+        later = pl.ds(pl.multiple_of(freq + t * LANES, LANES), LANES)
+        re = cls_ref[0, :, at].astype(f32)
+        im = cls_ref[1, :, at].astype(f32)
+        for r in range(poses):
+            cos_r = cos_ref[r : r + 1, at]
+            sin_r = sin_ref[r : r + 1, at]
+            temp_ref[r * rows : (r + 1) * rows, at] = (re * cos_r - im * sin_r).astype(bf16)
+            temp_ref[r * rows : (r + 1) * rows, later] = (re * sin_r + im * cos_r).astype(bf16)
+
+
+def build_templates(split, cos_t, sin_t):
+    _, rows, freq = split.shape
+    poses = cos_t.shape[0]
+    return call(
+        template_kernel,
+        "templates",
+        [VMEM] * 3,
+        [pltpu.VMEM((poses * rows, 2 * freq), bf16)],
+        (split, cos_t, sin_t),
         flops=40 * poses * rows * freq,
         moved=4 * poses * rows * freq,
-    )
+    )[0]
 
 
 def add_products(acc_ref, temp_ref, parts, chunk, span):
@@ -231,7 +246,6 @@
 
 def score(temps, power, gathered, freq):
     span = freq // CHUNKS
-    temps = pltpu.with_memory_space_constraint(temps, pltpu.VMEM)
     lanes = sum(p.shape[0] for p in gathered[0])
     acc_shape = jax.ShapeDtypeStruct((temps.shape[0], lanes), f32)
     flops = 2 * temps.shape[0] * 256 * 2 * span
@@ -320,11 +334,9 @@
     return write
 
 
-def resp_kernel(
-    poses, block, paired, far, span, me_ref, s_ref, marks_ref, cos_ref, sin_ref, w_ref, *refs
-):
+def rho_kernel(poses, block, paired, far, span, me_ref, s_ref, marks_ref, cos_ref, sin_ref, w_ref, *refs):
     stat_refs, refs = refs[: len(paired)], refs[len(paired) :]
-    resp_ref, rho_ref, mass_ref = refs[:3]
+    norm_ref, rho_ref, mass_ref = refs[:3]
     out_refs, buffers = refs[3:-2], refs[-2:]
     rows, groups = mass_ref.shape
     lanes = s_ref.shape[1]
@@ -337,8 +349,8 @@
     peak = functools.reduce(jnp.maximum, peaks)
     total = sum(t * jnp.exp(p - peak) for t, p in zip(totals, peaks))
     log_norm = peak + jnp.log(total)
-    scores = s_ref[...].reshape(poses, rows, lanes)
-    rho = jnp.exp(scores - log_norm[None])
+    norm_ref[...] = log_norm
+    rho = jnp.exp(s_ref[...].reshape(poses, rows, lanes) - log_norm[None])
     even = even_index((rows, lanes), 1)
     mass = lax.dot_general(
         jnp.where(even, jnp.sum(rho, axis=0), 0.0),
@@ -362,26 +374,17 @@
         rotate_slice(
             rho_ref, w_ref, cos_ref, sin_ref, base, span, poses, buffers, write_to(ref, span)
         )
-    pose_peak = jnp.max(scores, axis=0)
-    log_resp = pose_peak + jnp.log(jnp.sum(jnp.exp(scores - pose_peak[None]), axis=0)) - log_norm
-    shape = (resp_ref.shape[1], lanes)
-    lane = lax.broadcasted_iota(jnp.int32, shape, 1)
-    row = ((lane // block) ^ me_ref[1]) * (block // 2) + lax.rem(lane, block) // 2
-    take = (lax.broadcasted_iota(jnp.int32, shape, 0) == row) & (lax.rem(lane, 2) == 0)
-    resp_ref[...] = lax.dot_general(
-        log_resp, take.astype(f32), NT, precision=HIGHEST, preferred_element_type=f32
-    )
-
-
-def responsibilities(me, scores, marks, cos_t, sin_t, weighted, stats, paired, far, block, span):
+
+
+def outgoing_slices(me, scores, marks, cos_t, sin_t, weighted, stats, paired, far, block, span):
     poses, lanes = cos_t.shape[0], scores.shape[1]
     rows, groups = scores.shape[0] // poses, marks.shape[1]
     return call(
-        functools.partial(resp_kernel, poses, block, paired, far, span),
-        "responsibilities",
+        functools.partial(rho_kernel, poses, block, paired, far, span),
+        "outgoing",
         [SMEM] + [VMEM] * (5 + len(stats)),
         [
-            jax.ShapeDtypeStruct((rows, lanes // 2), f32),
+            jax.ShapeDtypeStruct((1, lanes), f32),
             jax.ShapeDtypeStruct((2, poses * rows, lanes), bf16),
             jax.ShapeDtypeStruct((rows, groups), f32),
         ]
@@ -393,7 +396,22 @@
 
 
 def own_kernel(
-    poses, span, me_ref, rho_ref, cos_ref, sin_ref, w_ref, ctf_ref, nw_ref, out_ref, cw_ref, *buffers
+    poses,
+    block,
+    span,
+    me_ref,
+    s_ref,
+    norm_ref,
+    rho_ref,
+    cos_ref,
+    sin_ref,
+    w_ref,
+    ctf_ref,
+    nw_ref,
+    out_ref,
+    cw_ref,
+    resp_ref,
+    *buffers,
 ):
     base = me_ref[0] * span
     at = pl.ds(pl.multiple_of(base, LANES), span)
@@ -402,20 +420,34 @@
     rotate_slice(
         rho_ref, w_ref, cos_ref, sin_ref, base, span, poses, buffers, write_to(out_ref, span)
     )
-
-
-def own_slice(me, rho, cos_t, sin_t, weighted, ctf, noise_weight, span):
-    poses = cos_t.shape[0]
-    rows = rho.shape[1] // poses
-    return call(
-        functools.partial(own_kernel, poses, span),
+    rows = resp_ref.shape[0]
+    lanes = s_ref.shape[1]
+    scores = s_ref[...].reshape(poses, rows, lanes)
+    pose_peak = jnp.max(scores, axis=0)
+    total = jnp.sum(jnp.exp(scores - pose_peak[None]), axis=0)
+    log_resp = pose_peak + jnp.log(total) - norm_ref[...]
+    shape = (resp_ref.shape[1], lanes)
+    lane = lax.broadcasted_iota(jnp.int32, shape, 1)
+    row = ((lane // block) ^ me_ref[1]) * (block // 2) + lax.rem(lane, block) // 2
+    take = (lax.broadcasted_iota(jnp.int32, shape, 0) == row) & (lax.rem(lane, 2) == 0)
+    resp_ref[...] = lax.dot_general(
+        log_resp, take.astype(f32), NT, precision=HIGHEST, preferred_element_type=f32
+    )
+
+
+def own_slice(me, scores, norm, rho, cos_t, sin_t, weighted, ctf, noise_weight, block, span):
+    poses, lanes = cos_t.shape[0], scores.shape[1]
+    rows = scores.shape[0] // poses
+    return call(
+        functools.partial(own_kernel, poses, block, span),
         "own_slice",
-        [SMEM] + [VMEM] * 6,
+        [SMEM] + [VMEM] * 8,
         [
             jax.ShapeDtypeStruct((rows, 2 * span), f32),
             jax.ShapeDtypeStruct((ctf.shape[0], span), f32),
+            jax.ShapeDtypeStruct((rows, lanes // 2), f32),
         ],
-        (me, rho, cos_t, sin_t, weighted, ctf, noise_weight),
+        (me, scores, norm, rho, cos_t, sin_t, weighted, ctf, noise_weight),
         [pltpu.VMEM((2, poses * rows, 256), f32)] * 2,
         flops=4 * 256 * poses * rows * span,
     )
@@ -491,12 +523,11 @@
         gathered = [[lax.all_gather(w, "cls", axis=0, tiled=True)] for w in shards]
 
     split = jnp.transpose(classes, (1, 0, 2))
-    temps, cos_t, sin_t, power = build_templates(
-        split, phase_tables(shifts, freq), ctf, noise_weight
-    )
+    cos_t, sin_t, power = prepare(split, phase_tables(shifts, freq), ctf, noise_weight)
     if pairwise:
-        direct, power = lax.optimization_barrier((direct, power))
+        direct, split, cos_t = lax.optimization_barrier((direct, split, cos_t))
         gathered = [gather_pairs(w, d) for w, d in zip(shards, direct)]
+    temps = build_templates(split, cos_t, sin_t)
     scores, weighted, marks, stat = score(temps, power, gathered, freq)
     if pairwise:
         stats = [stat] + [swap(stat, "cls", k) for k in range(1, n_cls)]
@@ -506,11 +537,14 @@
         paired = (0,)
 
     far = tuple(range(n_img - 1, 0, -1))
-    log_resp, rho, mass, *parts = responsibilities(
-        me, scores, marks, cos_t, sin_t, weighted, stats, paired, far, 2 * part_rows, span
+    block = 2 * part_rows
+    norm, rho, mass, *parts = outgoing_slices(
+        me, scores, marks, cos_t, sin_t, weighted, stats, paired, far, block, span
     )
     received = [swap(part, "img", d) for part, d in zip(parts, far)]
-    mine, weight = own_slice(me, rho, cos_t, sin_t, weighted, ctf, noise_weight, span)
+    mine, weight, log_resp = own_slice(
+        me, scores, norm, rho, cos_t, sin_t, weighted, ctf, noise_weight, block, span
+    )
     averages = finish(weight, mass, mine, received, span)
     return (log_resp.T, averages)
 

time: 62.1 us -> 56.8 us (0.915)
  local copies, waits for them, and re-layouts: 11.2 us -> 2.47 us
  waiting for transfers between devices: 13.6 us -> 16.8 us
    unnamed x11 -> x15, local copies, waits for them, and re-layouts: 11.2 us -> 2.45 us
    ppermute x12, waiting for transfers between devices: 13.6 us -> 16.8 us  [swap(): return lax.ppermute(values, axis, [(i, i ^ distance) for i in range(size)])]
    pallas_call x7 -> x8, Pallas kernels: 20.9 us -> 21.3 us  [call(): pl.pallas_call(kernel, in_specs=in_specs, out_specs=[VMEM] * len(out_shap...]
  transfers between devices with their start and end apart: 12 -> 12, of which waited for: 5 -> 6; matrix products, arithmetic and copies ran while one was open for 2% -> 3% of each run, Pallas kernels for 17% -> 20%
where the time goes in v5:
time: 56.8 us; the launch traced here: 56.5 us
  Pallas kernels  21.3 us (38%)
  waiting for transfers between devices  16.8 us (30%)
  starting transfers between devices  14.8 us (26%)
  local copies, waits for them, and re-layouts  2.47 us (4%)
  between operations  0.81 us (1%)
    pallas_call x8, Pallas kernels, call(): pl.pallas_call(kernel, in_specs=in_specs, out_specs=[VMEM] * len(out_shap...  21.3 us
    ppermute x12, waiting for transfers between devices, swap(): return lax.ppermute(values, axis, [(i, i ^ distance) for i in range(size)])  16.8 us
    ppermute x12, starting transfers between devices, swap(): return lax.ppermute(values, axis, [(i, i ^ distance) for i in range(size)])  14.8 us
    unnamed x15, local copies, waits for them, and re-layouts  2.45 us
  transfers between devices with their start and end apart: 12, of which 6 were waited for; matrix products, arithmetic and copies ran while one was open for 3% of the time, Pallas kernels for 20%

profile of v5, /device:TPU:0, one launch (start us, length us, event | category | flops | bytes accessed | tf_op | source)
XLA Modules:
  0.0 56.5 jit_solution(5600212961830787968)
XLA Ops:
  0.6 0.0 copy-start.5
  0.6 0.0 copy-start
  0.7 0.0 copy-start.6
  0.7 1.9 %weigh.1 = (bf16[32,2432]{1,0:T(8,128)(2,1)S(1)}, bf16[32,2304]{1,0:T(8,128)(2,1)S(1)}) custom-call(s32[16]{0:T(128)} %ids_hbm.1, bf16[16,2,4608]{2,1,0:T(2,128)(2,1)} %p_hbm.1, f32[64,4608]{1,0:T(8,128)} %ctf_ref.3, f32[4608]{0:T(1024)} %nw_hbm.1), custom_call_target="tpu_custom_call" | custom-call | flops 294912 | bytes 1179648 | tf_op jit(solution)/shard_map/weigh/pallas_call | solution.py:38
  2.6 3.1 %collective-permute-start = (bf16[32,2432]{1,0:T(8,128)(2,1)S(1)}, bf16[32,2432]{1,0:T(8,128)(2,1)S(1)}, u32[]{:S(2)}, u32[]{:S(2)}) collective-permute-start(bf16[32,2432]{1,0:T(8,128)(2,1)S(1)} %get-tuple-element.26.refs_0_), channel_id=1, source_target_pairs={{0,4},{4,0},{8,12},{12,8},{1,5},{5,1},{9,13},{13,9},{2,6},{6,2},{1... | collective-permute-start | bytes 466952 | tf_op jit(solution)/shard_map/ppermute | solution.py:494
  5.7 2.6 %collective-permute-start.1 = (bf16[32,2432]{1,0:T(8,128)(2,1)S(1)}, bf16[32,2432]{1,0:T(8,128)(2,1)S(1)}, u32[]{:S(2)}, u32[]{:S(2)}) collective-permute-start(bf16[32,2432]{1,0:T(8,128)(2,1)S(1)} %get-tuple-element.26.refs_0_), channel_id=1, source_target_pairs={{0,8},{4,12},{8,0},{12,4},{1,9},{5,13},{9,1},{13,5},{2,10},{6,14},... | collective-permute-start | bytes 466952 | tf_op jit(solution)/shard_map/ppermute | solution.py:494
  8.3 0.4 collective-permute-start.2
  8.7 0.0 collective-permute-start.3
  8.7 0.0 copy-done.5
  8.8 0.0 copy-done.6
  8.8 1.1 %copy.10 = bf16[32,2,4608]{2,0,1:T(8,128)(2,1)S(1)} copy(bf16[32,2,4608]{2,1,0:T(2,128)(2,1)} %param.7) | data formatting | bytes 1179648 | tf_op args[1]
  9.9 0.1 fusion
  10.1 0.1 fusion.2
  10.2 0.0 copy-done
  10.2 1.2 %prepare.1 = (f32[24,4608]{1,0:T(8,128)S(1)}, f32[24,4608]{1,0:T(8,128)S(1)}, f32[32,64]{1,0:T(8,128)S(1)}) custom-call(bf16[2,32,4608]{2,1,0:T(8,128)(2,1)S(1)} %bitcast.10, f32[24,128]{1,0:T(8,128)S(1)} %get-tuple-element.55.xc_ref, f32[24,128]{1,0:T(8,128)S(1)} %get-tuple-element.54.xs_ref, f32[24,36]{1,0:T(8,128)S(1)} %get-tuple-element.51.yc_ref, ...), custom_call_target="tpu_custom_call" | custom-call | flops 226492416 | tf_op jit(solution)/shard_map/prepare/pallas_call | solution.py:38
  11.4 7.4 %collective-permute-done.2.refs_5_ = bf16[32,2304]{1,0:T(8,128)(2,1)S(1)} collective-permute-done((bf16[32,2304]{1,0:T(8,128)(2,1)S(1)}, bf16[32,2304]{1,0:T(8,128)(2,1)S(1)}, u32[]{:S(2)}, u32[]{:S(2)}) %collective-permute-start.2) | collective-permute-done | bytes 147488 | tf_op jit(solution)/shard_map/ppermute | solution.py:494
  18.8 0.7 %copy-done.1 = bf16[32,2304]{1,0:T(8,128)(2,1)} copy-done((bf16[32,2304]{1,0:T(8,128)(2,1)}, bf16[32,2304]{1,0:T(8,128)(2,1)S(1)}, u32[]{:S(2)}) %copy-start.1) | copy-done | bytes 147480
  19.5 2.3 %collective-permute-done.3.refs_6_ = bf16[32,2304]{1,0:T(8,128)(2,1)S(1)} collective-permute-done((bf16[32,2304]{1,0:T(8,128)(2,1)S(1)}, bf16[32,2304]{1,0:T(8,128)(2,1)S(1)}, u32[]{:S(2)}, u32[]{:S(2)}) %collective-permute-start.3) | collective-permute-done | bytes 147488 | tf_op jit(solution)/shard_map/ppermute | solution.py:494
  21.8 0.0 collective-permute-done.refs_1_
  21.8 0.0 collective-permute-done.1.refs_2_
  21.8 0.6 %copy-done.3 = bf16[32,2304]{1,0:T(8,128)(2,1)} copy-done((bf16[32,2304]{1,0:T(8,128)(2,1)}, bf16[32,2304]{1,0:T(8,128)(2,1)S(1)}, u32[]{:S(2)}) %copy-start.3) | copy-done | bytes 147480
  22.4 0.5 collective-permute-start.4
  22.9 1.5 %collective-permute-start.5 = (bf16[32,2304]{1,0:T(8,128)(2,1)}, bf16[32,2304]{1,0:T(8,128)(2,1)S(1)}, u32[]{:S(2)}, u32[]{:S(2)}) collective-permute-start(bf16[32,2304]{1,0:T(8,128)(2,1)} %copy-done.3), channel_id=1, source_target_pairs={{0,4},{4,0},{8,12},{12,8},{1,5},{5,1},{9,13},{13,9},{2,6},{6,2},{1... | collective-permute-start | bytes 442376 | tf_op jit(solution)/shard_map/ppermute | solution.py:494
  24.5 5.2 %templates.1.temp_ref = bf16[768,9216]{1,0:T(8,128)(2,1)S(1)} custom-call(bf16[2,32,4608]{2,1,0:T(8,128)(2,1)S(1)} %bitcast.11, f32[24,4608]{1,0:T(8,128)S(1)} %get-tuple-element.30.cos_ref, f32[24,4608]{1,0:T(8,128)S(1)} %get-tuple-element.31.sin_ref), custom_call_target="tpu_custom_call" | custom-call | flops 141557760 | bytes 14155776 | tf_op jit(solution)/shard_map/templates/pallas_call | solution.py:38
  29.6 0.0 copy-start.2
  29.6 0.0 copy-start.4
  29.6 0.0 collective-permute-done.4.refs_3_
  29.7 2.1 %score0.1.refs_8_ = f32[768,128]{1,0:T(8,128)S(1)} custom-call(bf16[768,9216]{1,0:T(8,128)(2,1)S(1)} %templates.1.temp_ref, bf16[32,2432]{1,0:T(8,128)(2,1)S(1)} %get-tuple-element.26.refs_0_, bf16[32,2432]{1,0:T(8,128)(2,1)S(1)} %collective-permute-done.refs_1_, bf16[32,2432]{1,0:T(8,128)(2,1)S(1)} %collective-permute-done.1.refs_2_, ...), custom_call_target="tpu_custom_call" | custom-call | flops 1811939328 | tf_op jit(solution)/shard_map/score0/pallas_call | solution.py:38
  31.7 0.0 collective-permute-done.5.refs_7_
  31.7 0.0 copy-done.2
  31.7 0.0 copy-done.4
  31.8 2.4 %score1.1 = (f32[768,128]{1,0:T(8,128)S(1)}, bf16[128,4608]{1,0:T(8,128)(2,1)S(1)}, f32[128,64]{1,0:T(8,128)S(1)}, f32[8,128]{1,0:T(8,128)S(1)}) custom-call(bf16[768,9216]{1,0:T(8,128)(2,1)S(1)} %templates.1.temp_ref, f32[32,64]{1,0:T(8,128)S(1)} %get-tuple-element.32.pow_ref, bf16[32,2432]{1,0:T(8,128)(2,1)S(1)} %get-tuple-element.26.refs_0_, ...), custom_call_target="tpu_custom_call" | custom-call | flops 1811939328 | tf_op jit(solution)/shard_map/score1/pallas_call | solution.py:38
  34.2 0.6 collective-permute-start.6
  34.7 2.6 %collective-permute-start.7 = (f32[8,128]{1,0:T(8,128)S(1)}, f32[8,128]{1,0:T(8,128)S(1)}, u32[]{:S(2)}, u32[]{:S(2)}) collective-permute-start(f32[8,128]{1,0:T(8,128)S(1)} %get-tuple-element.40.refs_0_), channel_id=1, source_target_pairs={{0,8},{4,12},{8,0},{12,4},{1,9},{5,13},{9,1},{13,5},{2,10},{6,14},... | collective-permute-start | bytes 12296 | tf_op jit(solution)/shard_map/ppermute | solution.py:494
  37.3 1.3 %collective-permute-start.8 = (f32[8,128]{1,0:T(8,128)S(1)}, f32[8,128]{1,0:T(8,128)S(1)}, u32[]{:S(2)}, u32[]{:S(2)}) collective-permute-start(f32[8,128]{1,0:T(8,128)S(1)} %get-tuple-element.40.refs_0_), channel_id=1, source_target_pairs={{0,12},{4,8},{8,4},{12,0},{1,13},{5,9},{9,5},{13,1},{2,14},{6,10},... | collective-permute-start | bytes 12296 | tf_op jit(solution)/shard_map/ppermute | solution.py:494
  38.6 0.1 pad_add_fusion.me_ref
  38.7 0.0 collective-permute-done.6.refs_1_
  38.7 0.5 collective-permute-done.7.refs_2_
  39.2 3.5 %collective-permute-done.8.refs_3_ = f32[8,128]{1,0:T(8,128)S(1)} collective-permute-done((f32[8,128]{1,0:T(8,128)S(1)}, f32[8,128]{1,0:T(8,128)S(1)}, u32[]{:S(2)}, u32[]{:S(2)}) %collective-permute-start.8) | collective-permute-done | bytes 4128 | tf_op jit(solution)/shard_map/ppermute | solution.py:494
  42.7 4.8 %outgoing.1 = (f32[1,128]{1,0:T(1,128)S(1)}, bf16[2,768,128]{2,1,0:T(8,128)(2,1)S(1)}, f32[32,64]{1,0:T(8,128)S(1)}, bf16[32,2432]{1,0:T(8,128)(2,1)S(1)}, bf16[...) custom-call(s32[2]{0:T(128)S(1)} %pad_add_fusion.me_ref, f32[768,128]{1,0:T(8,128)S(1)} %get-tuple-element.37.s_ref, ...), custom_call_target="tpu_custom_call" | custom-call | flops 2717908992 | tf_op jit(solution)/shard_map/outgoing/pallas_call | solution.py:38
  47.5 1.6 %collective-permute-start.10 = (bf16[32,2432]{1,0:T(8,128)(2,1)S(1)}, bf16[32,2432]{1,0:T(8,128)(2,1)S(1)}, u32[]{:S(2)}, u32[]{:S(2)}) collective-permute-start(bf16[32,2432]{1,0:T(8,128)(2,1)S(1)} %get-tuple-element.48), channel_id=1, source_target_pairs={{0,2},{1,3},{2,0},{3,1},{4,6},{5,7},{6,4},{7,5},{8,10},{9,11},{10,... | collective-permute-start | bytes 466952 | tf_op jit(solution)/shard_map/ppermute | solution.py:494
  49.1 0.0 collective-permute-start.11
  49.1 0.6 %collective-permute-start.9 = (bf16[32,2432]{1,0:T(8,128)(2,1)S(1)}, bf16[32,2432]{1,0:T(8,128)(2,1)S(1)}, u32[]{:S(2)}, u32[]{:S(2)}) collective-permute-start(bf16[32,2432]{1,0:T(8,128)(2,1)S(1)} %get-tuple-element.47), channel_id=1, source_target_pairs={{0,3},{1,2},{2,1},{3,0},{4,7},{5,6},{6,5},{7,4},{8,11},{9,10},{10,... | collective-permute-start | bytes 466952 | tf_op jit(solution)/shard_map/ppermute | solution.py:494
  49.7 2.6 %own_slice.1 = (f32[32,2304]{1,0:T(8,128)S(1)}, f32[64,1152]{1,0:T(8,128)S(1)}, f32[32,64]{1,0:T(8,128)}) custom-call(s32[2]{0:T(128)S(1)} %pad_add_fusion.me_ref, f32[768,128]{1,0:T(8,128)S(1)} %get-tuple-element.37.s_ref, f32[1,128]{1,0:T(1,128)S(1)} %get-tuple-element.41.norm_ref, bf16[2,768,128]{2,1,0:T(8,128)(2,1)S(1)} %get-tuple-element.42.rho_ref, ...), custom_call_target="tpu_custom_call" | custom-call | flops 905969664 | tf_op jit(solution)/shard_map/own_slice/pallas_call | solution.py:38
  52.3 1.2 %collective-permute-done.10.refs_1_ = bf16[32,2432]{1,0:T(8,128)(2,1)S(1)} collective-permute-done((bf16[32,2432]{1,0:T(8,128)(2,1)S(1)}, bf16[32,2432]{1,0:T(8,128)(2,1)S(1)}, u32[]{:S(2)}, u32[]{:S(2)}) %collective-permute-start.10) | collective-permute-done | bytes 155680 | tf_op jit(solution)/shard_map/ppermute | solution.py:494
  53.5 0.0 collective-permute-done.11.refs_2_
  53.5 1.8 %collective-permute-done.9.refs_0_ = bf16[32,2432]{1,0:T(8,128)(2,1)S(1)} collective-permute-done((bf16[32,2432]{1,0:T(8,128)(2,1)S(1)}, bf16[32,2432]{1,0:T(8,128)(2,1)S(1)}, u32[]{:S(2)}, u32[]{:S(2)}) %collective-permute-start.9) | collective-permute-done | bytes 155680 | tf_op jit(solution)/shard_map/ppermute | solution.py:494
  55.4 1.1 %finish.1 = f32[32,2,1152]{2,1,0:T(2,128)} custom-call(f32[64,1152]{1,0:T(8,128)S(1)} %get-tuple-element.44.cw_ref, f32[32,64]{1,0:T(8,128)S(1)} %get-tuple-element.45.mass_ref, f32[32,2304]{1,0:T(8,128)S(1)} %get-tuple-element.46.own_ref, bf16[32,2432]{1,0:T(8,128)(2,1)S(1)} %collective-permute-done.9.refs_0_, ...), custom_call_target="tpu_custom_call" | custom-call | tf_op jit(solution)/shard_map/finish/pallas_call | solution.py:38
  (6 shorter events, 0.0 us)
Async XLA Ops:
  0.6 8.1 %copy-start.5 = (f32[4608]{0:T(1024)S(1)}, f32[4608]{0:T(1024)}, u32[]{:S(2)}) copy-start(f32[4608]{0:T(1024)} %nw_hbm.1) | copy-start | bytes 55300
  0.6 9.6 %copy-start = (f32[64,4608]{1,0:T(8,128)S(1)}, f32[64,4608]{1,0:T(8,128)}, u32[]{:S(2)}) copy-start(f32[64,4608]{1,0:T(8,128)} %ctf_ref.3) | copy-start | bytes 3538948
  0.7 8.1 %copy-start.6 = (s32[24,2]{0,1:T(2,128)S(1)}, s32[24,2]{0,1:T(2,128)}, u32[]{:S(2)}) copy-start(s32[24,2]{0,1:T(2,128)} %param.11) | copy-start | bytes 580
  2.6 19.2 %collective-permute-start = (bf16[32,2432]{1,0:T(8,128)(2,1)S(1)}, bf16[32,2432]{1,0:T(8,128)(2,1)S(1)}, u32[]{:S(2)}, u32[]{:S(2)}) collective-permute-start(bf16[32,2432]{1,0:T(8,128)(2,1)S(1)} %get-tuple-element.26.refs_0_), channel_id=1, source_target_pairs={{0,4},{4,0},{8,12},{12,8},{1,5},{5,1},{9,13},{13,9},{2,6},{6,2},{1... | collective-permute-start | bytes 466952 | tf_op jit(solution)/shard_map/ppermute | solution.py:494
  5.7 16.1 %collective-permute-start.1 = (bf16[32,2432]{1,0:T(8,128)(2,1)S(1)}, bf16[32,2432]{1,0:T(8,128)(2,1)S(1)}, u32[]{:S(2)}, u32[]{:S(2)}) collective-permute-start(bf16[32,2432]{1,0:T(8,128)(2,1)S(1)} %get-tuple-element.26.refs_0_), channel_id=1, source_target_pairs={{0,8},{4,12},{8,0},{12,4},{1,9},{5,13},{9,1},{13,5},{2,10},{6,14},... | collective-permute-start | bytes 466952 | tf_op jit(solution)/shard_map/ppermute | solution.py:494
  8.3 10.5 %collective-permute-start.2 = (bf16[32,2304]{1,0:T(8,128)(2,1)S(1)}, bf16[32,2304]{1,0:T(8,128)(2,1)S(1)}, u32[]{:S(2)}, u32[]{:S(2)}) collective-permute-start(bf16[32,2304]{1,0:T(8,128)(2,1)S(1)} %get-tuple-element.27.refs_4_), channel_id=1, source_target_pairs={{0,4},{4,0},{8,12},{12,8},{1,5},{5,1},{9,13},{13,9},{2,6},{6,2},{1... | collective-permute-start | bytes 442376 | tf_op jit(solution)/shard_map/ppermute | solution.py:494
  8.7 13.0 %collective-permute-start.3 = (bf16[32,2304]{1,0:T(8,128)(2,1)S(1)}, bf16[32,2304]{1,0:T(8,128)(2,1)S(1)}, u32[]{:S(2)}, u32[]{:S(2)}) collective-permute-start(bf16[32,2304]{1,0:T(8,128)(2,1)S(1)} %get-tuple-element.27.refs_4_), channel_id=1, source_target_pairs={{0,8},{4,12},{8,0},{12,4},{1,9},{5,13},{9,1},{13,5},{2,10},{6,14},... | collective-permute-start | bytes 442376 | tf_op jit(solution)/shard_map/ppermute | solution.py:494
  18.8 0.7 %copy-start.1 = (bf16[32,2304]{1,0:T(8,128)(2,1)}, bf16[32,2304]{1,0:T(8,128)(2,1)S(1)}, u32[]{:S(2)}) copy-start(bf16[32,2304]{1,0:T(8,128)(2,1)S(1)} %collective-permute-done.2.refs_5_) | copy-start | bytes 442372
  21.8 0.7 %copy-start.3 = (bf16[32,2304]{1,0:T(8,128)(2,1)}, bf16[32,2304]{1,0:T(8,128)(2,1)S(1)}, u32[]{:S(2)}) copy-start(bf16[32,2304]{1,0:T(8,128)(2,1)S(1)} %collective-permute-done.3.refs_6_) | copy-start | bytes 442372
  22.4 7.2 %collective-permute-start.4 = (bf16[32,2432]{1,0:T(8,128)(2,1)S(1)}, bf16[32,2432]{1,0:T(8,128)(2,1)S(1)}, u32[]{:S(2)}, u32[]{:S(2)}) collective-permute-start(bf16[32,2432]{1,0:T(8,128)(2,1)S(1)} %collective-permute-done.1.refs_2_), channel_id=1, source_target_pairs={{0,4},{4,0},{8,12},{12,8},{1,5},{5,1},{9,13},{13,9},{2,6},{6,2},{1... | collective-permute-start | bytes 466952 | tf_op jit(solution)/shard_map/ppermute | solution.py:494
  22.9 8.8 %collective-permute-start.5 = (bf16[32,2304]{1,0:T(8,128)(2,1)}, bf16[32,2304]{1,0:T(8,128)(2,1)S(1)}, u32[]{:S(2)}, u32[]{:S(2)}) collective-permute-start(bf16[32,2304]{1,0:T(8,128)(2,1)} %copy-done.3), channel_id=1, source_target_pairs={{0,4},{4,0},{8,12},{12,8},{1,5},{5,1},{9,13},{13,9},{2,6},{6,2},{1... | collective-permute-start | bytes 442376 | tf_op jit(solution)/shard_map/ppermute | solution.py:494
  29.6 2.1 %copy-start.2 = (bf16[32,2304]{1,0:T(8,128)(2,1)S(1)}, bf16[32,2304]{1,0:T(8,128)(2,1)}, u32[]{:S(2)}) copy-start(bf16[32,2304]{1,0:T(8,128)(2,1)} %copy-done.1) | copy-start | bytes 442372
  29.6 2.1 %copy-start.4 = (bf16[32,2304]{1,0:T(8,128)(2,1)S(1)}, bf16[32,2304]{1,0:T(8,128)(2,1)}, u32[]{:S(2)}) copy-start(bf16[32,2304]{1,0:T(8,128)(2,1)} %copy-done.3) | copy-start | bytes 442372
  34.2 4.5 %collective-permute-start.6 = (f32[8,128]{1,0:T(8,128)S(1)}, f32[8,128]{1,0:T(8,128)S(1)}, u32[]{:S(2)}, u32[]{:S(2)}) collective-permute-start(f32[8,128]{1,0:T(8,128)S(1)} %get-tuple-element.40.refs_0_), channel_id=1, source_target_pairs={{0,4},{4,0},{8,12},{12,8},{1,5},{5,1},{9,13},{13,9},{2,6},{6,2},{1... | collective-permute-start | bytes 12296 | tf_op jit(solution)/shard_map/ppermute | solution.py:494
  34.7 4.5 %collective-permute-start.7 = (f32[8,128]{1,0:T(8,128)S(1)}, f32[8,128]{1,0:T(8,128)S(1)}, u32[]{:S(2)}, u32[]{:S(2)}) collective-permute-start(f32[8,128]{1,0:T(8,128)S(1)} %get-tuple-element.40.refs_0_), channel_id=1, source_target_pairs={{0,8},{4,12},{8,0},{12,4},{1,9},{5,13},{9,1},{13,5},{2,10},{6,14},... | collective-permute-start | bytes 12296 | tf_op jit(solution)/shard_map/ppermute | solution.py:494
  37.3 5.4 %collective-permute-start.8 = (f32[8,128]{1,0:T(8,128)S(1)}, f32[8,128]{1,0:T(8,128)S(1)}, u32[]{:S(2)}, u32[]{:S(2)}) collective-permute-start(f32[8,128]{1,0:T(8,128)S(1)} %get-tuple-element.40.refs_0_), channel_id=1, source_target_pairs={{0,12},{4,8},{8,4},{12,0},{1,13},{5,9},{9,5},{13,1},{2,14},{6,10},... | collective-permute-start | bytes 12296 | tf_op jit(solution)/shard_map/ppermute | solution.py:494
  47.5 6.0 %collective-permute-start.10 = (bf16[32,2432]{1,0:T(8,128)(2,1)S(1)}, bf16[32,2432]{1,0:T(8,128)(2,1)S(1)}, u32[]{:S(2)}, u32[]{:S(2)}) collective-permute-start(bf16[32,2432]{1,0:T(8,128)(2,1)S(1)} %get-tuple-element.48), channel_id=1, source_target_pairs={{0,2},{1,3},{2,0},{3,1},{4,6},{5,7},{6,4},{7,5},{8,10},{9,11},{10,... | collective-permute-start | bytes 466952 | tf_op jit(solution)/shard_map/ppermute | solution.py:494
  49.1 4.5 %collective-permute-start.11 = (bf16[32,2432]{1,0:T(8,128)(2,1)S(1)}, bf16[32,2432]{1,0:T(8,128)(2,1)S(1)}, u32[]{:S(2)}, u32[]{:S(2)}) collective-permute-start(bf16[32,2432]{1,0:T(8,128)(2,1)S(1)} %get-tuple-element.49), channel_id=1, source_target_pairs={{0,1},{1,0},{2,3},{3,2},{4,5},{5,4},{6,7},{7,6},{8,9},{9,8},{10,11... | collective-permute-start | bytes 466952 | tf_op jit(solution)/shard_map/ppermute | solution.py:494
  49.1 6.3 %collective-permute-start.9 = (bf16[32,2432]{1,0:T(8,128)(2,1)S(1)}, bf16[32,2432]{1,0:T(8,128)(2,1)S(1)}, u32[]{:S(2)}, u32[]{:S(2)}) collective-permute-start(bf16[32,2432]{1,0:T(8,128)(2,1)S(1)} %get-tuple-element.47), channel_id=1, source_target_pairs={{0,3},{1,2},{2,1},{3,0},{4,7},{5,6},{6,5},{7,4},{8,11},{9,10},{10,... | collective-permute-start | bytes 466952 | tf_op jit(solution)/shard_map/ppermute | solution.py:494

commit v6 on v5

--- a/solution.py
+++ b/solution.py
@@ -152,13 +152,11 @@
 
 
 def template_kernel(cls_ref, cos_ref, sin_ref, temp_ref):
-    _, rows, freq = cls_ref.shape
+    _, rows, tile = cls_ref.shape
     poses = cos_ref.shape[0]
-
-    @pl.loop(0, freq // LANES)
-    def _(t):
-        at = pl.ds(pl.multiple_of(t * LANES, LANES), LANES)
-        later = pl.ds(pl.multiple_of(freq + t * LANES, LANES), LANES)
+    for a in range(0, tile, LANES):
+        at = slice(a, a + LANES)
+        later = slice(tile + a, tile + a + LANES)
         re = cls_ref[0, :, at].astype(f32)
         im = cls_ref[1, :, at].astype(f32)
         for r in range(poses):
@@ -171,54 +169,66 @@
 def build_templates(split, cos_t, sin_t):
     _, rows, freq = split.shape
     poses = cos_t.shape[0]
-    return call(
+    tile = max(t for t in range(LANES, 385, LANES) if freq // CHUNKS % t == 0)
+    return pl.pallas_call(
         template_kernel,
-        "templates",
-        [VMEM] * 3,
-        [pltpu.VMEM((poses * rows, 2 * freq), bf16)],
-        (split, cos_t, sin_t),
-        flops=40 * poses * rows * freq,
-        moved=4 * poses * rows * freq,
-    )[0]
-
-
-def add_products(acc_ref, temp_ref, parts, chunk, span):
-    freq = temp_ref.shape[1] // 2
-    tile = max(t for t in range(LANES, 1153, LANES) if span % t == 0)
-    lanes = acc_ref.shape[1]
-    even = even_index((lanes, tile), 0)
-    for t in range(span // tile):
+        grid=(freq // tile,),
+        in_specs=[
+            pl.BlockSpec((2, rows, tile), lambda j: (0, 0, j)),
+            pl.BlockSpec((poses, tile), lambda j: (0, j)),
+            pl.BlockSpec((poses, tile), lambda j: (0, j)),
+        ],
+        out_specs=pl.BlockSpec((None, poses * rows, 2 * tile), lambda j: (j, 0, 0)),
+        out_shape=pltpu.HBM((freq // tile, poses * rows, 2 * tile), bf16),
+        compiler_params=pltpu.CompilerParams(vmem_limit_bytes=VMEM_LIMIT),
+        cost_estimate=pl.CostEstimate(
+            flops=40 * poses * rows * freq, bytes_accessed=4 * poses * rows * freq, transcendentals=0
+        ),
+        name="templates",
+    )(split, cos_t, sin_t)
+
+
+def template_copies(temp_hbm, temp_ref, sem, chunk):
+    count = temp_ref.shape[0]
+    copies = [
+        pltpu.make_async_copy(temp_hbm.at[chunk * count + t], temp_ref.at[t], sem.at[t])
+        for t in range(count)
+    ]
+    for copy in copies:
+        copy.start()
+    return copies
+
+
+def add_products(acc_ref, temp_ref, copies, parts):
+    tile = temp_ref.shape[2] // 2
+    even = even_index((acc_ref.shape[0], tile), 0)
+    for t, copy in enumerate(copies):
         at = slice(t * tile, (t + 1) * tile)
-        where = chunk * span + t * tile
         wide = jnp.concatenate([p[:, at] for p in parts], axis=0).astype(f32)
-        acc_ref[...] += lax.dot_general(
-            temp_ref[:, where : where + tile],
-            jnp.where(even, wide, 0.0).astype(bf16),
-            NT,
-            preferred_element_type=f32,
-        ) + lax.dot_general(
-            temp_ref[:, freq + where : freq + where + tile],
-            jnp.where(even, 0.0, wide).astype(bf16),
-            NT,
-            preferred_element_type=f32,
+        split = jnp.concatenate(
+            [jnp.where(even, wide, 0.0).astype(bf16), jnp.where(even, 0.0, wide).astype(bf16)],
+            axis=1,
         )
-
-
-def score_kernel(chunk, span, temp_ref, *refs):
-    *parts, acc_ref = refs if chunk == 0 else refs[1:]
+        copy.wait()
+        acc_ref[...] += lax.dot_general(split, temp_ref[t], NT, preferred_element_type=f32)
+
+
+def score_kernel(chunk, temp_hbm, *refs):
+    refs, (acc_ref, temp_ref, sem) = refs[:-3], refs[-3:]
+    copies = template_copies(temp_hbm, temp_ref, sem, chunk)
+    parts = refs if chunk == 0 else refs[1:]
     acc_ref[...] = jnp.zeros_like(acc_ref) if chunk == 0 else refs[0][...]
-    add_products(acc_ref, temp_ref, parts, chunk, span)
-
-
-def last_score_kernel(sources, span, temp_ref, pow_ref, *refs):
+    add_products(acc_ref, temp_ref, copies, parts)
+
+
+def last_score_kernel(sources, span, temp_hbm, pow_ref, *refs):
     refs = list(refs)
-    s_ref, all_ref, marks_ref, stat_ref = refs[-4:]
+    s_ref, all_ref, marks_ref, stat_ref, temp_ref, acc_ref, sem = refs[-7:]
+    copies = template_copies(temp_hbm, temp_ref, sem, CHUNKS - 1)
     chunks = [refs[c * sources : (c + 1) * sources] for c in range(CHUNKS)]
     rows, groups = pow_ref.shape
     lanes = s_ref.shape[1]
     poses = s_ref.shape[0] // rows
-    s_ref[...] = refs[-5][...] if CHUNKS > 1 else jnp.zeros_like(s_ref)
-    add_products(s_ref, temp_ref, chunks[-1], CHUNKS - 1, span)
     for c, parts in enumerate(chunks):
         at = 0
         for p in parts:
@@ -231,7 +241,9 @@
     penalty = lax.dot_general(
         pow_ref[...], marks, NT, precision=HIGHEST, preferred_element_type=f32
     )
-    acc = s_ref[...]
+    acc_ref[...] = refs[CHUNKS * sources][...] if CHUNKS > 1 else jnp.zeros_like(acc_ref)
+    add_products(acc_ref, temp_ref, copies, chunks[-1])
+    acc = acc_ref[...].T
     acc = acc + jnp.where(
         even_index(acc.shape, 1), pltpu.roll(acc, lanes - 1, 1), pltpu.roll(acc, 1, 1)
     )
@@ -245,33 +257,39 @@
 
 
 def score(temps, power, gathered, freq):
+    temps = pltpu.with_memory_space_constraint(temps, pltpu.HBM)
+    tiles, columns, width = temps.shape
     span = freq // CHUNKS
     lanes = sum(p.shape[0] for p in gathered[0])
-    acc_shape = jax.ShapeDtypeStruct((temps.shape[0], lanes), f32)
-    flops = 2 * temps.shape[0] * 256 * 2 * span
+    acc_shape = (lanes, columns)
+    scratch = [pltpu.VMEM((tiles // CHUNKS, columns, width), bf16)]
+    sems = [pltpu.SemaphoreType.DMA((tiles // CHUNKS,))]
+    flops = 2 * columns * 256 * 2 * span
     acc = []
     for c in range(CHUNKS - 1):
         operands = [temps, *acc, *gathered[c]]
         acc = call(
-            functools.partial(score_kernel, c, span),
+            functools.partial(score_kernel, c),
             f"score{c}",
-            [VMEM] * len(operands),
-            [acc_shape],
+            [ANY] + [VMEM] * (len(operands) - 1),
+            [jax.ShapeDtypeStruct(acc_shape, f32)],
             operands,
+            scratch + sems,
             flops=flops,
         )
     operands = [temps, power, *[p for parts in gathered for p in parts], *acc]
     return call(
         functools.partial(last_score_kernel, len(gathered[0]), span),
         f"score{CHUNKS - 1}",
-        [VMEM] * len(operands),
+        [ANY] + [VMEM] * (len(operands) - 1),
         [
-            acc_shape,
+            jax.ShapeDtypeStruct((columns, lanes), f32),
             jax.ShapeDtypeStruct((lanes, freq), bf16),
             jax.ShapeDtypeStruct((lanes, power.shape[1]), f32),
             jax.ShapeDtypeStruct((8, lanes), f32),
         ],
         operands,
+        scratch + [pltpu.VMEM(acc_shape, f32)] + sems,
         flops=flops,
     )
 
@@ -524,10 +542,10 @@
 
     split = jnp.transpose(classes, (1, 0, 2))
     cos_t, sin_t, power = prepare(split, phase_tables(shifts, freq), ctf, noise_weight)
+    temps = build_templates(split, cos_t, sin_t)
     if pairwise:
-        direct, split, cos_t = lax.optimization_barrier((direct, split, cos_t))
+        direct, power, temps = lax.optimization_barrier((direct, power, temps))
         gathered = [gather_pairs(w, d) for w, d in zip(shards, direct)]
-    temps = build_templates(split, cos_t, sin_t)
     scores, weighted, marks, stat = score(temps, power, gathered, freq)
     if pairwise:
         stats = [stat] + [swap(stat, "cls", k) for k in range(1, n_cls)]

time: 56.8 us -> 60.4 us (1.063)
  Pallas kernels: 21.3 us -> 30.1 us
  waiting for transfers between devices: 16.8 us -> 12.9 us
  local copies, waits for them, and re-layouts: 2.47 us -> 1.15 us
    pallas_call x0 -> x1, Pallas kernels: none -> 8.86 us  [build_templates(): pl.pallas_call(template_kernel, grid=(freq // tile,), in_specs=[pl.BlockS...]
    ppermute x12, waiting for transfers between devices: 16.8 us -> 12.9 us  [swap(): return lax.ppermute(values, axis, [(i, i ^ distance) for i in range(size)])]
    unnamed x15 -> x7, local copies, waits for them, and re-layouts: 2.45 us -> 1.14 us
    pallas_call x8 -> x7, Pallas kernels: 21.3 us -> 21.2 us  [call(): pl.pallas_call(kernel, in_specs=in_specs, out_specs=[VMEM] * len(out_shap...]
  transfers between devices with their start and end apart: 12 -> 12, of which waited for: 6 -> 6; matrix products, arithmetic and copies ran while one was open for 3% -> 2% of each run, Pallas kernels for 20% -> 29%
where the time goes in v6:
time: 60.4 us; the launch traced here: 60.1 us
  Pallas kernels  30.1 us (50%)
  starting transfers between devices  14.8 us (25%)
  waiting for transfers between devices  12.9 us (21%)
  local copies, waits for them, and re-layouts  1.15 us (2%)
  between operations  0.77 us (1%)
    pallas_call x7, Pallas kernels, call(): pl.pallas_call(kernel, in_specs=in_specs, out_specs=[VMEM] * len(out_shap...  21.2 us
    ppermute x12, starting transfers between devices, swap(): return lax.ppermute(values, axis, [(i, i ^ distance) for i in range(size)])  14.8 us
    ppermute x12, waiting for transfers between devices, swap(): return lax.ppermute(values, axis, [(i, i ^ distance) for i in range(size)])  12.9 us
    pallas_call x1, Pallas kernels, build_templates(): pl.pallas_call(template_kernel, grid=(freq // tile,), in_specs=[pl.BlockS...  8.86 us
  transfers between devices with their start and end apart: 12, of which 6 were waited for; matrix products, arithmetic and copies ran while one was open for 2% of the time, Pallas kernels for 29%

profile of v6, /device:TPU:0, one launch (start us, length us, event | category | flops | bytes accessed | tf_op | source)
XLA Modules:
  0.0 60.1 jit_solution(13542754136528360055)
XLA Ops:
  0.6 0.0 copy-start.1
  0.6 0.0 copy-start
  0.7 0.0 copy-start.2
  0.7 1.9 %weigh.1 = (bf16[32,2432]{1,0:T(8,128)(2,1)S(1)}, bf16[32,2304]{1,0:T(8,128)(2,1)S(1)}) custom-call(s32[16]{0:T(128)} %ids_hbm.1, bf16[16,2,4608]{2,1,0:T(2,128)(2,1)} %p_hbm.1, f32[64,4608]{1,0:T(8,128)} %ctf_ref.3, f32[4608]{0:T(1024)} %nw_hbm.1), custom_call_target="tpu_custom_call" | custom-call | flops 294912 | bytes 1179648 | tf_op jit(solution)/shard_map/weigh/pallas_call | solution.py:38
  2.6 3.1 %collective-permute-start = (bf16[32,2432]{1,0:T(8,128)(2,1)S(1)}, bf16[32,2432]{1,0:T(8,128)(2,1)S(1)}, u32[]{:S(2)}, u32[]{:S(2)}) collective-permute-start(bf16[32,2432]{1,0:T(8,128)(2,1)S(1)} %get-tuple-element.26.refs_0_), channel_id=1, source_target_pairs={{0,4},{4,0},{8,12},{12,8},{1,5},{5,1},{9,13},{13,9},{2,6},{6,2},{1... | collective-permute-start | bytes 466952 | tf_op jit(solution)/shard_map/ppermute | solution.py:512
  5.7 2.6 %collective-permute-start.1 = (bf16[32,2432]{1,0:T(8,128)(2,1)S(1)}, bf16[32,2432]{1,0:T(8,128)(2,1)S(1)}, u32[]{:S(2)}, u32[]{:S(2)}) collective-permute-start(bf16[32,2432]{1,0:T(8,128)(2,1)S(1)} %get-tuple-element.26.refs_0_), channel_id=1, source_target_pairs={{0,8},{4,12},{8,0},{12,4},{1,9},{5,13},{9,1},{13,5},{2,10},{6,14},... | collective-permute-start | bytes 466952 | tf_op jit(solution)/shard_map/ppermute | solution.py:512
  8.3 0.4 collective-permute-start.2
  8.7 0.0 collective-permute-start.3
  8.7 0.0 copy-done.1
  8.8 0.0 copy-done.2
  8.8 1.1 %copy.10 = bf16[32,2,4608]{2,0,1:T(8,128)(2,1)S(1)} copy(bf16[32,2,4608]{2,1,0:T(2,128)(2,1)} %param.7) | data formatting | bytes 1179648 | tf_op args[1]
  9.9 0.1 fusion
  10.1 0.1 fusion.2
  10.2 0.0 copy-done
  10.2 1.2 %prepare.1 = (f32[24,4608]{1,0:T(8,128)S(1)}, f32[24,4608]{1,0:T(8,128)S(1)}, f32[32,64]{1,0:T(8,128)S(1)}) custom-call(bf16[2,32,4608]{2,1,0:T(8,128)(2,1)S(1)} %bitcast.10, f32[24,128]{1,0:T(8,128)S(1)} %get-tuple-element.55.xc_ref, f32[24,128]{1,0:T(8,128)S(1)} %get-tuple-element.54.xs_ref, f32[24,36]{1,0:T(8,128)S(1)} %get-tuple-element.51.yc_ref, ...), custom_call_target="tpu_custom_call" | custom-call | flops 226492416 | tf_op jit(solution)/shard_map/prepare/pallas_call | solution.py:38
  11.4 8.9 %templates.1.temp_hbm = bf16[12,768,768]{2,1,0:T(8,128)(2,1)} custom-call(bf16[2,32,4608]{2,1,0:T(8,128)(2,1)S(1)} %bitcast.11, f32[24,4608]{1,0:T(8,128)S(1)} %get-tuple-element.29.cos_ref, f32[24,4608]{1,0:T(8,128)S(1)} %get-tuple-element.30.sin_ref), custom_call_target="tpu_custom_call" | custom-call | flops 141557760 | bytes 14155776 | tf_op jit(solution)/shard_map/templates/pallas_call | solution.py:173
  20.3 0.0 collective-permute-done.2.refs_5_
  20.3 1.5 %collective-permute-done.3.refs_6_ = bf16[32,2304]{1,0:T(8,128)(2,1)S(1)} collective-permute-done((bf16[32,2304]{1,0:T(8,128)(2,1)S(1)}, bf16[32,2304]{1,0:T(8,128)(2,1)S(1)}, u32[]{:S(2)}, u32[]{:S(2)}) %collective-permute-start.3) | collective-permute-done | bytes 147488 | tf_op jit(solution)/shard_map/ppermute | solution.py:512
  21.8 0.0 collective-permute-done.refs_1_
  21.8 0.0 collective-permute-done.1.refs_2_
  21.8 0.5 collective-permute-start.4
  22.3 1.5 %collective-permute-start.5 = (bf16[32,2304]{1,0:T(8,128)(2,1)S(1)}, bf16[32,2304]{1,0:T(8,128)(2,1)S(1)}, u32[]{:S(2)}, u32[]{:S(2)}) collective-permute-start(bf16[32,2304]{1,0:T(8,128)(2,1)S(1)} %collective-permute-done.3.refs_6_), channel_id=1, source_target_pairs={{0,4},{4,0},{8,12},{12,8},{1,5},{5,1},{9,13},{13,9},{2,6},{6,2},{1... | collective-permute-start | bytes 442376 | tf_op jit(solution)/shard_map/ppermute | solution.py:512
  23.8 3.2 %collective-permute-done.4.refs_3_ = bf16[32,2432]{1,0:T(8,128)(2,1)S(1)} collective-permute-done((bf16[32,2432]{1,0:T(8,128)(2,1)S(1)}, bf16[32,2432]{1,0:T(8,128)(2,1)S(1)}, u32[]{:S(2)}, u32[]{:S(2)}) %collective-permute-start.4) | collective-permute-done | bytes 155680 | tf_op jit(solution)/shard_map/ppermute | solution.py:512
  27.0 4.7 %score0.1.refs_8_ = f32[128,768]{1,0:T(8,128)S(1)} custom-call(bf16[12,768,768]{2,1,0:T(8,128)(2,1)} %templates.1.temp_hbm, bf16[32,2432]{1,0:T(8,128)(2,1)S(1)} %get-tuple-element.26.refs_0_, bf16[32,2432]{1,0:T(8,128)(2,1)S(1)} %collective-permute-done.refs_1_, bf16[32,2432]{1,0:T(8,128)(2,1)S(1)} %collective-permute-done.1.refs_2_, ...), custom_call_target="tpu_custom_call" | custom-call | flops 1811939328 | tf_op jit(solution)/shard_map/score0/pallas_call | solution.py:38
  31.7 0.0 collective-permute-done.5.refs_7_
  31.7 4.9 %score1.1 = (f32[768,128]{1,0:T(8,128)S(1)}, bf16[128,4608]{1,0:T(8,128)(2,1)S(1)}, f32[128,64]{1,0:T(8,128)S(1)}, f32[8,128]{1,0:T(8,128)S(1)}) custom-call(bf16[12,768,768]{2,1,0:T(8,128)(2,1)} %templates.1.temp_hbm, f32[32,64]{1,0:T(8,128)S(1)} %get-tuple-element.32.pow_ref, bf16[32,2432]{1,0:T(8,128)(2,1)S(1)} %get-tuple-element.26.refs_0_, ...), custom_call_target="tpu_custom_call" | custom-call | flops 1811939328 | tf_op jit(solution)/shard_map/score1/pallas_call | solution.py:38
  36.7 1.7 %collective-permute-start.6 = (f32[8,128]{1,0:T(8,128)S(1)}, f32[8,128]{1,0:T(8,128)S(1)}, u32[]{:S(2)}, u32[]{:S(2)}) collective-permute-start(f32[8,128]{1,0:T(8,128)S(1)} %get-tuple-element.40.refs_0_), channel_id=1, source_target_pairs={{0,4},{4,0},{8,12},{12,8},{1,5},{5,1},{9,13},{13,9},{2,6},{6,2},{1... | collective-permute-start | bytes 12296 | tf_op jit(solution)/shard_map/ppermute | solution.py:512
  38.4 2.6 %collective-permute-start.7 = (f32[8,128]{1,0:T(8,128)S(1)}, f32[8,128]{1,0:T(8,128)S(1)}, u32[]{:S(2)}, u32[]{:S(2)}) collective-permute-start(f32[8,128]{1,0:T(8,128)S(1)} %get-tuple-element.40.refs_0_), channel_id=1, source_target_pairs={{0,8},{4,12},{8,0},{12,4},{1,9},{5,13},{9,1},{13,5},{2,10},{6,14},... | collective-permute-start | bytes 12296 | tf_op jit(solution)/shard_map/ppermute | solution.py:512
  41.0 0.2 collective-permute-start.8
  41.1 0.1 pad_add_fusion.me_ref
  41.2 0.0 collective-permute-done.6.refs_1_
  41.2 1.7 %collective-permute-done.7.refs_2_ = f32[8,128]{1,0:T(8,128)S(1)} collective-permute-done((f32[8,128]{1,0:T(8,128)S(1)}, f32[8,128]{1,0:T(8,128)S(1)}, u32[]{:S(2)}, u32[]{:S(2)}) %collective-permute-start.7) | collective-permute-done | bytes 4128 | tf_op jit(solution)/shard_map/ppermute | solution.py:512
  42.9 3.5 %collective-permute-done.8.refs_3_ = f32[8,128]{1,0:T(8,128)S(1)} collective-permute-done((f32[8,128]{1,0:T(8,128)S(1)}, f32[8,128]{1,0:T(8,128)S(1)}, u32[]{:S(2)}, u32[]{:S(2)}) %collective-permute-start.8) | collective-permute-done | bytes 4128 | tf_op jit(solution)/shard_map/ppermute | solution.py:512
  46.4 4.8 %outgoing.1 = (f32[1,128]{1,0:T(1,128)S(1)}, bf16[2,768,128]{2,1,0:T(8,128)(2,1)S(1)}, f32[32,64]{1,0:T(8,128)S(1)}, bf16[32,2432]{1,0:T(8,128)(2,1)S(1)}, bf16[...) custom-call(s32[2]{0:T(128)S(1)} %pad_add_fusion.me_ref, f32[768,128]{1,0:T(8,128)S(1)} %get-tuple-element.37.s_ref, ...), custom_call_target="tpu_custom_call" | custom-call | flops 2717908992 | tf_op jit(solution)/shard_map/outgoing/pallas_call | solution.py:38
  51.1 1.6 %collective-permute-start.10 = (bf16[32,2432]{1,0:T(8,128)(2,1)S(1)}, bf16[32,2432]{1,0:T(8,128)(2,1)S(1)}, u32[]{:S(2)}, u32[]{:S(2)}) collective-permute-start(bf16[32,2432]{1,0:T(8,128)(2,1)S(1)} %get-tuple-element.48), channel_id=1, source_target_pairs={{0,2},{1,3},{2,0},{3,1},{4,6},{5,7},{6,4},{7,5},{8,10},{9,11},{10,... | collective-permute-start | bytes 466952 | tf_op jit(solution)/shard_map/ppermute | solution.py:512
  52.7 0.0 collective-permute-start.11
  52.7 0.7 %collective-permute-start.9 = (bf16[32,2432]{1,0:T(8,128)(2,1)S(1)}, bf16[32,2432]{1,0:T(8,128)(2,1)S(1)}, u32[]{:S(2)}, u32[]{:S(2)}) collective-permute-start(bf16[32,2432]{1,0:T(8,128)(2,1)S(1)} %get-tuple-element.47), channel_id=1, source_target_pairs={{0,3},{1,2},{2,1},{3,0},{4,7},{5,6},{6,5},{7,4},{8,11},{9,10},{10,... | collective-permute-start | bytes 466952 | tf_op jit(solution)/shard_map/ppermute | solution.py:512
  53.3 2.6 %own_slice.1 = (f32[32,2304]{1,0:T(8,128)S(1)}, f32[64,1152]{1,0:T(8,128)S(1)}, f32[32,64]{1,0:T(8,128)}) custom-call(s32[2]{0:T(128)S(1)} %pad_add_fusion.me_ref, f32[768,128]{1,0:T(8,128)S(1)} %get-tuple-element.37.s_ref, f32[1,128]{1,0:T(1,128)S(1)} %get-tuple-element.41.norm_ref, bf16[2,768,128]{2,1,0:T(8,128)(2,1)S(1)} %get-tuple-element.42.rho_ref, ...), custom_call_target="tpu_custom_call" | custom-call | flops 905969664 | tf_op jit(solution)/shard_map/own_slice/pallas_call | solution.py:38
  56.0 1.2 %collective-permute-done.10.refs_1_ = bf16[32,2432]{1,0:T(8,128)(2,1)S(1)} collective-permute-done((bf16[32,2432]{1,0:T(8,128)(2,1)S(1)}, bf16[32,2432]{1,0:T(8,128)(2,1)S(1)}, u32[]{:S(2)}, u32[]{:S(2)}) %collective-permute-start.10) | collective-permute-done | bytes 155680 | tf_op jit(solution)/shard_map/ppermute | solution.py:512
  57.2 0.0 collective-permute-done.11.refs_2_
  57.2 1.8 %collective-permute-done.9.refs_0_ = bf16[32,2432]{1,0:T(8,128)(2,1)S(1)} collective-permute-done((bf16[32,2432]{1,0:T(8,128)(2,1)S(1)}, bf16[32,2432]{1,0:T(8,128)(2,1)S(1)}, u32[]{:S(2)}, u32[]{:S(2)}) %collective-permute-start.9) | collective-permute-done | bytes 155680 | tf_op jit(solution)/shard_map/ppermute | solution.py:512
  59.0 1.1 %finish.1 = f32[32,2,1152]{2,1,0:T(2,128)} custom-call(f32[64,1152]{1,0:T(8,128)S(1)} %get-tuple-element.44.cw_ref, f32[32,64]{1,0:T(8,128)S(1)} %get-tuple-element.45.mass_ref, f32[32,2304]{1,0:T(8,128)S(1)} %get-tuple-element.46.own_ref, bf16[32,2432]{1,0:T(8,128)(2,1)S(1)} %collective-permute-done.9.refs_0_, ...), custom_call_target="tpu_custom_call" | custom-call | tf_op jit(solution)/shard_map/finish/pallas_call | solution.py:38
  (4 shorter events, 0.0 us)
Async XLA Ops:
  0.6 8.1 %copy-start.1 = (f32[4608]{0:T(1024)S(1)}, f32[4608]{0:T(1024)}, u32[]{:S(2)}) copy-start(f32[4608]{0:T(1024)} %nw_hbm.1) | copy-start | bytes 55300
  0.6 9.6 %copy-start = (f32[64,4608]{1,0:T(8,128)S(1)}, f32[64,4608]{1,0:T(8,128)}, u32[]{:S(2)}) copy-start(f32[64,4608]{1,0:T(8,128)} %ctf_ref.3) | copy-start | bytes 3538948
  0.7 8.1 %copy-start.2 = (s32[24,2]{0,1:T(2,128)S(1)}, s32[24,2]{0,1:T(2,128)}, u32[]{:S(2)}) copy-start(s32[24,2]{0,1:T(2,128)} %param.11) | copy-start | bytes 580
  2.6 19.2 %collective-permute-start = (bf16[32,2432]{1,0:T(8,128)(2,1)S(1)}, bf16[32,2432]{1,0:T(8,128)(2,1)S(1)}, u32[]{:S(2)}, u32[]{:S(2)}) collective-permute-start(bf16[32,2432]{1,0:T(8,128)(2,1)S(1)} %get-tuple-element.26.refs_0_), channel_id=1, source_target_pairs={{0,4},{4,0},{8,12},{12,8},{1,5},{5,1},{9,13},{13,9},{2,6},{6,2},{1... | collective-permute-start | bytes 466952 | tf_op jit(solution)/shard_map/ppermute | solution.py:512
  5.7 16.1 %collective-permute-start.1 = (bf16[32,2432]{1,0:T(8,128)(2,1)S(1)}, bf16[32,2432]{1,0:T(8,128)(2,1)S(1)}, u32[]{:S(2)}, u32[]{:S(2)}) collective-permute-start(bf16[32,2432]{1,0:T(8,128)(2,1)S(1)} %get-tuple-element.26.refs_0_), channel_id=1, source_target_pairs={{0,8},{4,12},{8,0},{12,4},{1,9},{5,13},{9,1},{13,5},{2,10},{6,14},... | collective-permute-start | bytes 466952 | tf_op jit(solution)/shard_map/ppermute | solution.py:512
  8.3 12.0 %collective-permute-start.2 = (bf16[32,2304]{1,0:T(8,128)(2,1)S(1)}, bf16[32,2304]{1,0:T(8,128)(2,1)S(1)}, u32[]{:S(2)}, u32[]{:S(2)}) collective-permute-start(bf16[32,2304]{1,0:T(8,128)(2,1)S(1)} %get-tuple-element.27.refs_4_), channel_id=1, source_target_pairs={{0,4},{4,0},{8,12},{12,8},{1,5},{5,1},{9,13},{13,9},{2,6},{6,2},{1... | collective-permute-start | bytes 442376 | tf_op jit(solution)/shard_map/ppermute | solution.py:512
  8.7 13.0 %collective-permute-start.3 = (bf16[32,2304]{1,0:T(8,128)(2,1)S(1)}, bf16[32,2304]{1,0:T(8,128)(2,1)S(1)}, u32[]{:S(2)}, u32[]{:S(2)}) collective-permute-start(bf16[32,2304]{1,0:T(8,128)(2,1)S(1)} %get-tuple-element.27.refs_4_), channel_id=1, source_target_pairs={{0,8},{4,12},{8,0},{12,4},{1,9},{5,13},{9,1},{13,5},{2,10},{6,14},... | collective-permute-start | bytes 442376 | tf_op jit(solution)/shard_map/ppermute | solution.py:512
  21.8 5.2 %collective-permute-start.4 = (bf16[32,2432]{1,0:T(8,128)(2,1)S(1)}, bf16[32,2432]{1,0:T(8,128)(2,1)S(1)}, u32[]{:S(2)}, u32[]{:S(2)}) collective-permute-start(bf16[32,2432]{1,0:T(8,128)(2,1)S(1)} %collective-permute-done.1.refs_2_), channel_id=1, source_target_pairs={{0,4},{4,0},{8,12},{12,8},{1,5},{5,1},{9,13},{13,9},{2,6},{6,2},{1... | collective-permute-start | bytes 466952 | tf_op jit(solution)/shard_map/ppermute | solution.py:512
  22.3 9.4 %collective-permute-start.5 = (bf16[32,2304]{1,0:T(8,128)(2,1)S(1)}, bf16[32,2304]{1,0:T(8,128)(2,1)S(1)}, u32[]{:S(2)}, u32[]{:S(2)}) collective-permute-start(bf16[32,2304]{1,0:T(8,128)(2,1)S(1)} %collective-permute-done.3.refs_6_), channel_id=1, source_target_pairs={{0,4},{4,0},{8,12},{12,8},{1,5},{5,1},{9,13},{13,9},{2,6},{6,2},{1... | collective-permute-start | bytes 442376 | tf_op jit(solution)/shard_map/ppermute | solution.py:512
  36.7 4.5 %collective-permute-start.6 = (f32[8,128]{1,0:T(8,128)S(1)}, f32[8,128]{1,0:T(8,128)S(1)}, u32[]{:S(2)}, u32[]{:S(2)}) collective-permute-start(f32[8,128]{1,0:T(8,128)S(1)} %get-tuple-element.40.refs_0_), channel_id=1, source_target_pairs={{0,4},{4,0},{8,12},{12,8},{1,5},{5,1},{9,13},{13,9},{2,6},{6,2},{1... | collective-permute-start | bytes 12296 | tf_op jit(solution)/shard_map/ppermute | solution.py:512
  38.4 4.5 %collective-permute-start.7 = (f32[8,128]{1,0:T(8,128)S(1)}, f32[8,128]{1,0:T(8,128)S(1)}, u32[]{:S(2)}, u32[]{:S(2)}) collective-permute-start(f32[8,128]{1,0:T(8,128)S(1)} %get-tuple-element.40.refs_0_), channel_id=1, source_target_pairs={{0,8},{4,12},{8,0},{12,4},{1,9},{5,13},{9,1},{13,5},{2,10},{6,14},... | collective-permute-start | bytes 12296 | tf_op jit(solution)/shard_map/ppermute | solution.py:512
  41.0 5.4 %collective-permute-start.8 = (f32[8,128]{1,0:T(8,128)S(1)}, f32[8,128]{1,0:T(8,128)S(1)}, u32[]{:S(2)}, u32[]{:S(2)}) collective-permute-start(f32[8,128]{1,0:T(8,128)S(1)} %get-tuple-element.40.refs_0_), channel_id=1, source_target_pairs={{0,12},{4,8},{8,4},{12,0},{1,13},{5,9},{9,5},{13,1},{2,14},{6,10},... | collective-permute-start | bytes 12296 | tf_op jit(solution)/shard_map/ppermute | solution.py:512
  51.1 6.1 %collective-permute-start.10 = (bf16[32,2432]{1,0:T(8,128)(2,1)S(1)}, bf16[32,2432]{1,0:T(8,128)(2,1)S(1)}, u32[]{:S(2)}, u32[]{:S(2)}) collective-permute-start(bf16[32,2432]{1,0:T(8,128)(2,1)S(1)} %get-tuple-element.48), channel_id=1, source_target_pairs={{0,2},{1,3},{2,0},{3,1},{4,6},{5,7},{6,4},{7,5},{8,10},{9,11},{10,... | collective-permute-start | bytes 466952 | tf_op jit(solution)/shard_map/ppermute | solution.py:512
  52.7 4.5 %collective-permute-start.11 = (bf16[32,2432]{1,0:T(8,128)(2,1)S(1)}, bf16[32,2432]{1,0:T(8,128)(2,1)S(1)}, u32[]{:S(2)}, u32[]{:S(2)}) collective-permute-start(bf16[32,2432]{1,0:T(8,128)(2,1)S(1)} %get-tuple-element.49), channel_id=1, source_target_pairs={{0,1},{1,0},{2,3},{3,2},{4,5},{5,4},{6,7},{7,6},{8,9},{9,8},{10,11... | collective-permute-start | bytes 466952 | tf_op jit(solution)/shard_map/ppermute | solution.py:512
  52.7 6.3 %collective-permute-start.9 = (bf16[32,2432]{1,0:T(8,128)(2,1)S(1)}, bf16[32,2432]{1,0:T(8,128)(2,1)S(1)}, u32[]{:S(2)}, u32[]{:S(2)}) collective-permute-start(bf16[32,2432]{1,0:T(8,128)(2,1)S(1)} %get-tuple-element.47), channel_id=1, source_target_pairs={{0,3},{1,2},{2,1},{3,0},{4,7},{5,6},{6,5},{7,4},{8,11},{9,10},{10,... | collective-permute-start | bytes 466952 | tf_op jit(solution)/shard_map/ppermute | solution.py:512

commit v7 on v6

--- a/solution.py
+++ b/solution.py
@@ -75,10 +75,12 @@
         scale_ref[2 * n : 2 * n + 2, :] = jnp.broadcast_to(scale, (2, freq))
     values = p_ref[...].astype(f32).reshape(2 * count, freq)
     weighted = (values * scale_ref[...]).astype(bf16)
-    chunk = freq // len(out_refs)
-    for c, out_ref in enumerate(out_refs):
+    chunk = freq // (len(out_refs) - 1)
+    for c, out_ref in enumerate(out_refs[1:]):
         out_ref[:, :chunk] = weighted[:, c * chunk : (c + 1) * chunk]
-    out_refs[0][:, chunk:] = ids.astype(bf16)
+    out_refs[0][:, :freq] = weighted
+    for out_ref in out_refs[:2]:
+        out_ref[:, out_ref.shape[1] - LANES :] = ids.astype(bf16)
 
 
 def weigh(particles, ctf, noise_weight, group_ids):
@@ -89,7 +91,8 @@
         weigh_kernel,
         "weigh",
         [ANY] * 4,
-        [
+        [jax.ShapeDtypeStruct((2 * rows, freq + LANES), bf16)]
+        + [
             jax.ShapeDtypeStruct((2 * rows, chunk + (LANES if c == 0 else 0)), bf16)
             for c in range(CHUNKS)
         ],
@@ -201,49 +204,62 @@
 
 def add_products(acc_ref, temp_ref, copies, parts):
     tile = temp_ref.shape[2] // 2
-    even = even_index((acc_ref.shape[0], tile), 0)
+    even = even_index((acc_ref.shape[1], tile), 0)
     for t, copy in enumerate(copies):
-        at = slice(t * tile, (t + 1) * tile)
-        wide = jnp.concatenate([p[:, at] for p in parts], axis=0).astype(f32)
+        wide = jnp.concatenate(
+            [ref[:, start + t * tile : start + (t + 1) * tile] for ref, start in parts], axis=0
+        ).astype(f32)
         split = jnp.concatenate(
             [jnp.where(even, wide, 0.0).astype(bf16), jnp.where(even, 0.0, wide).astype(bf16)],
             axis=1,
         )
         copy.wait()
-        acc_ref[...] += lax.dot_general(split, temp_ref[t], NT, preferred_element_type=f32)
-
-
-def score_kernel(chunk, temp_hbm, *refs):
+        acc_ref[...] += lax.dot_general(temp_ref[t], split, NT, preferred_element_type=f32)
+
+
+def chunk_parts(refs, chunked, chunk, span):
+    whole = [(ref, chunk * span) for ref in refs[: len(refs) - chunked]]
+    return whole + [(ref, 0) for ref in refs[len(refs) - chunked :]]
+
+
+def score_kernel(chunk, span, chunked, temp_hbm, *refs):
     refs, (acc_ref, temp_ref, sem) = refs[:-3], refs[-3:]
     copies = template_copies(temp_hbm, temp_ref, sem, chunk)
     parts = refs if chunk == 0 else refs[1:]
     acc_ref[...] = jnp.zeros_like(acc_ref) if chunk == 0 else refs[0][...]
-    add_products(acc_ref, temp_ref, copies, parts)
-
-
-def last_score_kernel(sources, span, temp_hbm, pow_ref, *refs):
+    add_products(acc_ref, temp_ref, copies, chunk_parts(parts, chunked, chunk, span))
+
+
+def last_score_kernel(wholes, chunked, span, temp_hbm, pow_ref, *refs):
     refs = list(refs)
-    s_ref, all_ref, marks_ref, stat_ref, temp_ref, acc_ref, sem = refs[-7:]
+    s_ref, all_ref, marks_ref, stat_ref, temp_ref, sem = refs[-6:]
     copies = template_copies(temp_hbm, temp_ref, sem, CHUNKS - 1)
-    chunks = [refs[c * sources : (c + 1) * sources] for c in range(CHUNKS)]
+    whole = refs[:wholes]
+    chunks = [refs[wholes + c * chunked : wholes + (c + 1) * chunked] for c in range(CHUNKS)]
     rows, groups = pow_ref.shape
     lanes = s_ref.shape[1]
     poses = s_ref.shape[0] // rows
-    for c, parts in enumerate(chunks):
-        at = 0
-        for p in parts:
-            all_ref[at : at + p.shape[0], c * span : (c + 1) * span] = p[:, :span]
-            at += p.shape[0]
-    ids = jnp.concatenate([p[:, span:] for p in chunks[0]], axis=0).astype(f32)
+    freq = span * CHUNKS
+    at = 0
+    for ref in whole:
+        all_ref[at : at + ref.shape[0], :] = ref[:, :freq]
+        at += ref.shape[0]
+    for k in range(chunked):
+        height = chunks[0][k].shape[0]
+        for c in range(CHUNKS):
+            all_ref[at : at + height, c * span : (c + 1) * span] = chunks[c][k][:, :span]
+        at += height
+    ids = jnp.concatenate([ref[:, freq:] for ref in whole] + [ref[:, span:] for ref in chunks[0]], axis=0)
     group = lax.broadcasted_iota(jnp.int32, (lanes, groups), 1).astype(f32)
-    marks = (ids[:, :groups] == group).astype(f32)
+    marks = (ids.astype(f32)[:, :groups] == group).astype(f32)
     marks_ref[...] = marks
     penalty = lax.dot_general(
         pow_ref[...], marks, NT, precision=HIGHEST, preferred_element_type=f32
     )
-    acc_ref[...] = refs[CHUNKS * sources][...] if CHUNKS > 1 else jnp.zeros_like(acc_ref)
-    add_products(acc_ref, temp_ref, copies, chunks[-1])
-    acc = acc_ref[...].T
+    s_ref[...] = refs[wholes + CHUNKS * chunked][...] if CHUNKS > 1 else jnp.zeros_like(s_ref)
+    parts = chunk_parts(whole + chunks[-1], chunked, CHUNKS - 1, span)
+    add_products(s_ref, temp_ref, copies, parts)
+    acc = s_ref[...]
     acc = acc + jnp.where(
         even_index(acc.shape, 1), pltpu.roll(acc, lanes - 1, 1), pltpu.roll(acc, 1, 1)
     )
@@ -256,40 +272,43 @@
     stat_ref[2:8, :] = jnp.zeros((6, lanes), f32)
 
 
-def score(temps, power, gathered, freq):
+def score(temps, power, whole, chunks, freq):
     temps = pltpu.with_memory_space_constraint(temps, pltpu.HBM)
     tiles, columns, width = temps.shape
     span = freq // CHUNKS
-    lanes = sum(p.shape[0] for p in gathered[0])
-    acc_shape = (lanes, columns)
-    scratch = [pltpu.VMEM((tiles // CHUNKS, columns, width), bf16)]
-    sems = [pltpu.SemaphoreType.DMA((tiles // CHUNKS,))]
+    chunked = len(chunks[0])
+    lanes = sum(p.shape[0] for p in whole + chunks[0])
+    acc_shape = jax.ShapeDtypeStruct((columns, lanes), f32)
+    scratch = [
+        pltpu.VMEM((tiles // CHUNKS, columns, width), bf16),
+        pltpu.SemaphoreType.DMA((tiles // CHUNKS,)),
+    ]
     flops = 2 * columns * 256 * 2 * span
     acc = []
     for c in range(CHUNKS - 1):
-        operands = [temps, *acc, *gathered[c]]
+        operands = [temps, *acc, *whole, *chunks[c]]
         acc = call(
-            functools.partial(score_kernel, c),
+            functools.partial(score_kernel, c, span, chunked),
             f"score{c}",
             [ANY] + [VMEM] * (len(operands) - 1),
-            [jax.ShapeDtypeStruct(acc_shape, f32)],
+            [acc_shape],
             operands,
-            scratch + sems,
+            scratch,
             flops=flops,
         )
-    operands = [temps, power, *[p for parts in gathered for p in parts], *acc]
+    operands = [temps, power, *whole, *[p for parts in chunks for p in parts], *acc]
     return call(
-        functools.partial(last_score_kernel, len(gathered[0]), span),
+        functools.partial(last_score_kernel, len(whole), chunked, span),
         f"score{CHUNKS - 1}",
         [ANY] + [VMEM] * (len(operands) - 1),
         [
-            jax.ShapeDtypeStruct((columns, lanes), f32),
+            acc_shape,
             jax.ShapeDtypeStruct((lanes, freq), bf16),
             jax.ShapeDtypeStruct((lanes, power.shape[1]), f32),
             jax.ShapeDtypeStruct((8, lanes), f32),
         ],
         operands,
-        scratch + [pltpu.VMEM(acc_shape, f32)] + sems,
+        scratch,
         flops=flops,
     )
 
@@ -512,41 +531,30 @@
     return lax.ppermute(values, axis, [(i, i ^ distance) for i in range(size)])
 
 
-def direct_shards(shard):
-    distances = [1 << b for b in range(lax.axis_size("cls").bit_length() - 1)]
-    return [swap(shard, "cls", d) for d in distances]
-
-
-def gather_pairs(shard, direct):
-    slots = [shard]
-    for i, arrived in enumerate(direct):
-        slots += [arrived] + [swap(arrived, "cls", k) for k in range(1, 1 << i)]
-    return slots
-
-
 def local(particles, classes, ctf, noise_weight, group_ids, shifts):
     part_rows, _, freq = particles.shape
     n_cls = lax.axis_size("cls")
     n_img = lax.axis_size("img")
     span = freq // n_img
-    pairwise = n_cls <= 4
+    pairwise = n_cls == 4
     me_cls = lax.axis_index("cls") if pairwise else 0
     me = jnp.stack([lax.axis_index("img"), me_cls]).astype(jnp.int32)
 
-    shards = weigh(particles, ctf, noise_weight, group_ids)
+    own, *shards = weigh(particles, ctf, noise_weight, group_ids)
     noise_weight = noise_weight[None, :]
     if pairwise:
-        direct = [direct_shards(w) for w in shards]
+        far = [swap(w, "cls", 2) for w in shards]
+        near = swap(own, "cls", 1)
     else:
-        gathered = [[lax.all_gather(w, "cls", axis=0, tiled=True)] for w in shards]
+        whole, chunks = [lax.all_gather(own, "cls", axis=0, tiled=True)], [[]] * CHUNKS
 
     split = jnp.transpose(classes, (1, 0, 2))
     cos_t, sin_t, power = prepare(split, phase_tables(shifts, freq), ctf, noise_weight)
     temps = build_templates(split, cos_t, sin_t)
     if pairwise:
-        direct, power, temps = lax.optimization_barrier((direct, power, temps))
-        gathered = [gather_pairs(w, d) for w, d in zip(shards, direct)]
-    scores, weighted, marks, stat = score(temps, power, gathered, freq)
+        far, power, temps = lax.optimization_barrier((far, power, temps))
+        whole, chunks = [own, near], [[w, swap(w, "cls", 1)] for w in far]
+    scores, weighted, marks, stat = score(temps, power, whole, chunks, freq)
     if pairwise:
         stats = [stat] + [swap(stat, "cls", k) for k in range(1, n_cls)]
         paired = tuple(range(n_cls))
@@ -554,12 +562,12 @@
         stats = [lax.all_gather(stat, "cls", axis=0, tiled=True)]
         paired = (0,)
 
-    far = tuple(range(n_img - 1, 0, -1))
+    others = tuple(range(n_img - 1, 0, -1))
     block = 2 * part_rows
     norm, rho, mass, *parts = outgoing_slices(
-        me, scores, marks, cos_t, sin_t, weighted, stats, paired, far, block, span
-    )
-    received = [swap(part, "img", d) for part, d in zip(parts, far)]
+        me, scores, marks, cos_t, sin_t, weighted, stats, paired, others, block, span
+    )
+    received = [swap(part, "img", d) for part, d in zip(parts, others)]
     mine, weight, log_resp = own_slice(
         me, scores, norm, rho, cos_t, sin_t, weighted, ctf, noise_weight, block, span
     )

time: 60.4 us -> 63.7 us (1.055)
  waiting for transfers between devices: 12.9 us -> 15.4 us
  Pallas kernels: 30.1 us -> 31.1 us
    ppermute x12 -> x11, waiting for transfers between devices: 12.9 us -> 15.4 us  [swap(): return lax.ppermute(values, axis, [(i, i ^ distance) for i in range(size)])]
    pallas_call x7, Pallas kernels: 21.2 us -> 22.5 us  [call(): pl.pallas_call(kernel, in_specs=in_specs, out_specs=[VMEM] * len(out_shap...]
    ppermute x12 -> x11, starting transfers between devices: 14.8 us -> 14.7 us  [swap(): return lax.ppermute(values, axis, [(i, i ^ distance) for i in range(size)])]
  transfers between devices with their start and end apart: 12 -> 11, of which waited for: 6 -> 6; matrix products, arithmetic and copies ran while one was open for 2% -> 2% of each run, Pallas kernels for 29% -> 28%
where the time goes in v7:
time: 63.7 us; the launch traced here: 63.5 us
  Pallas kernels  31.1 us (49%)
  waiting for transfers between devices  15.4 us (24%)
  starting transfers between devices  14.7 us (23%)
  local copies, waits for them, and re-layouts  1.15 us (2%)
  between operations  0.76 us (1%)
    pallas_call x7, Pallas kernels, call(): pl.pallas_call(kernel, in_specs=in_specs, out_specs=[VMEM] * len(out_shap...  22.5 us
    ppermute x11, waiting for transfers between devices, swap(): return lax.ppermute(values, axis, [(i, i ^ distance) for i in range(size)])  15.4 us
    ppermute x11, starting transfers between devices, swap(): return lax.ppermute(values, axis, [(i, i ^ distance) for i in range(size)])  14.7 us
    pallas_call x1, Pallas kernels, build_templates(): pl.pallas_call(template_kernel, grid=(freq // tile,), in_specs=[pl.BlockS...  8.68 us
  transfers between devices with their start and end apart: 11, of which 6 were waited for; matrix products, arithmetic and copies ran while one was open for 2% of the time, Pallas kernels for 28%

profile of v7, /device:TPU:0, one launch (start us, length us, event | category | flops | bytes accessed | tf_op | source)
XLA Modules:
  0.0 63.5 jit_solution(4969292127161412493)
XLA Ops:
  0.6 0.0 copy-start.1
  0.6 0.0 copy-start
  0.7 0.0 copy-start.2
  0.7 1.9 %weigh.1 = (bf16[32,4736]{1,0:T(8,128)(2,1)S(1)}, bf16[32,2432]{1,0:T(8,128)(2,1)S(1)}, bf16[32,2304]{1,0:T(8,128)(2,1)S(1)}) custom-call(s32[16]{0:T(128)} %ids_hbm.1, bf16[16,2,4608]{2,1,0:T(2,128)(2,1)} %p_hbm.1, f32[64,4608]{1,0:T(8,128)} %ctf_ref.3, f32[4608]{0:T(1024)} %nw_hbm.1), custom_call_target="tpu_custom_call" | custom-call | flops 294912 | bytes 1179648 | tf_op jit(solution)/shard_map/weigh/pallas_call | solution.py:38
  2.6 4.1 %collective-permute-start = (bf16[32,2432]{1,0:T(8,128)(2,1)S(1)}, bf16[32,2432]{1,0:T(8,128)(2,1)S(1)}, u32[]{:S(2)}, u32[]{:S(2)}) collective-permute-start(bf16[32,2432]{1,0:T(8,128)(2,1)S(1)} %get-tuple-element.25), channel_id=1, source_target_pairs={{0,8},{4,12},{8,0},{12,4},{1,9},{5,13},{9,1},{13,5},{2,10},{6,14},... | collective-permute-start | bytes 466952 | tf_op jit(solution)/shard_map/ppermute | solution.py:531
  6.7 0.1 collective-permute-start.1
  6.8 1.8 %collective-permute-start.2 = (bf16[32,4736]{1,0:T(8,128)(2,1)S(1)}, bf16[32,4736]{1,0:T(8,128)(2,1)S(1)}, u32[]{:S(2)}, u32[]{:S(2)}) collective-permute-start(bf16[32,4736]{1,0:T(8,128)(2,1)S(1)} %get-tuple-element.32.refs_0_), channel_id=1, source_target_pairs={{0,4},{4,0},{8,12},{12,8},{1,5},{5,1},{9,13},{13,9},{2,6},{6,2},{1... | collective-permute-start | bytes 909320 | tf_op jit(solution)/shard_map/ppermute | solution.py:531
  8.6 0.0 copy-done.2
  8.7 0.1 fusion
  8.8 0.1 fusion.2
  8.9 0.0 copy-done.1
  8.9 1.1 %copy.10 = bf16[32,2,4608]{2,0,1:T(8,128)(2,1)S(1)} copy(bf16[32,2,4608]{2,1,0:T(2,128)(2,1)} %param.7) | data formatting | bytes 1179648 | tf_op args[1]
  10.1 0.0 copy-done
  10.1 1.2 %prepare.1 = (f32[24,4608]{1,0:T(8,128)S(1)}, f32[24,4608]{1,0:T(8,128)S(1)}, f32[32,64]{1,0:T(8,128)S(1)}) custom-call(bf16[2,32,4608]{2,1,0:T(8,128)(2,1)S(1)} %bitcast.10, f32[24,128]{1,0:T(8,128)S(1)} %get-tuple-element.53.xc_ref, f32[24,128]{1,0:T(8,128)S(1)} %get-tuple-element.52.xs_ref, f32[24,36]{1,0:T(8,128)S(1)} %get-tuple-element.49.yc_ref, ...), custom_call_target="tpu_custom_call" | custom-call | flops 226492416 | tf_op jit(solution)/shard_map/prepare/pallas_call | solution.py:38
  11.3 8.7 %templates.1.temp_hbm = bf16[12,768,768]{2,1,0:T(8,128)(2,1)} custom-call(bf16[2,32,4608]{2,1,0:T(8,128)(2,1)S(1)} %bitcast.11, f32[24,4608]{1,0:T(8,128)S(1)} %get-tuple-element.28.cos_ref, f32[24,4608]{1,0:T(8,128)S(1)} %get-tuple-element.29.sin_ref), custom_call_target="tpu_custom_call" | custom-call | flops 141557760 | bytes 14155776 | tf_op jit(solution)/shard_map/templates/pallas_call | solution.py:176
  20.0 0.5 collective-permute-done.1.refs_4_
  20.5 0.0 collective-permute-done.refs_2_
  20.5 0.7 %collective-permute-start.3 = (bf16[32,2432]{1,0:T(8,128)(2,1)S(1)}, bf16[32,2432]{1,0:T(8,128)(2,1)S(1)}, u32[]{:S(2)}, u32[]{:S(2)}) collective-permute-start(bf16[32,2432]{1,0:T(8,128)(2,1)S(1)} %collective-permute-done.refs_2_), channel_id=1, source_target_pairs={{0,4},{4,0},{8,12},{12,8},{1,5},{5,1},{9,13},{13,9},{2,6},{6,2},{1... | collective-permute-start | bytes 466952 | tf_op jit(solution)/shard_map/ppermute | solution.py:531
  21.2 1.4 %collective-permute-start.4 = (bf16[32,2304]{1,0:T(8,128)(2,1)S(1)}, bf16[32,2304]{1,0:T(8,128)(2,1)S(1)}, u32[]{:S(2)}, u32[]{:S(2)}) collective-permute-start(bf16[32,2304]{1,0:T(8,128)(2,1)S(1)} %collective-permute-done.1.refs_4_), channel_id=1, source_target_pairs={{0,4},{4,0},{8,12},{12,8},{1,5},{5,1},{9,13},{13,9},{2,6},{6,2},{1... | collective-permute-start | bytes 442376 | tf_op jit(solution)/shard_map/ppermute | solution.py:531
  22.5 0.0 collective-permute-done.2.refs_1_
  22.5 4.7 %collective-permute-done.3.refs_3_ = bf16[32,2432]{1,0:T(8,128)(2,1)S(1)} collective-permute-done((bf16[32,2432]{1,0:T(8,128)(2,1)S(1)}, bf16[32,2432]{1,0:T(8,128)(2,1)S(1)}, u32[]{:S(2)}, u32[]{:S(2)}) %collective-permute-start.3) | collective-permute-done | bytes 155680 | tf_op jit(solution)/shard_map/ppermute | solution.py:531
  27.2 5.4 %score0.1.refs_6_ = f32[768,128]{1,0:T(8,128)S(1)} custom-call(bf16[12,768,768]{2,1,0:T(8,128)(2,1)} %templates.1.temp_hbm, bf16[32,4736]{1,0:T(8,128)(2,1)S(1)} %get-tuple-element.32.refs_0_, bf16[32,4736]{1,0:T(8,128)(2,1)S(1)} %collective-permute-done.2.refs_1_, bf16[32,2432]{1,0:T(8,128)(2,1)S(1)} %collective-permute-done.refs_2_, ...), custom_call_target="tpu_custom_call" | custom-call | flops 1811939328 | tf_op jit(solution)/shard_map/score0/pallas_call | solution.py:38
  32.6 0.0 collective-permute-done.4.refs_5_
  32.7 5.4 %score1.1 = (f32[768,128]{1,0:T(8,128)S(1)}, bf16[128,4608]{1,0:T(8,128)(2,1)S(1)}, f32[128,64]{1,0:T(8,128)S(1)}, f32[8,128]{1,0:T(8,128)S(1)}) custom-call(bf16[12,768,768]{2,1,0:T(8,128)(2,1)} %templates.1.temp_hbm, f32[32,64]{1,0:T(8,128)S(1)} %get-tuple-element.31.pow_ref, bf16[32,4736]{1,0:T(8,128)(2,1)S(1)} %get-tuple-element.32.refs_0_, ...), custom_call_target="tpu_custom_call" | custom-call | flops 1811939328 | tf_op jit(solution)/shard_map/score1/pallas_call | solution.py:38
  38.1 0.9 %collective-permute-start.5 = (f32[8,128]{1,0:T(8,128)S(1)}, f32[8,128]{1,0:T(8,128)S(1)}, u32[]{:S(2)}, u32[]{:S(2)}) collective-permute-start(f32[8,128]{1,0:T(8,128)S(1)} %get-tuple-element.38.refs_0_), channel_id=1, source_target_pairs={{0,4},{4,0},{8,12},{12,8},{1,5},{5,1},{9,13},{13,9},{2,6},{6,2},{1... | collective-permute-start | bytes 12296 | tf_op jit(solution)/shard_map/ppermute | solution.py:531
  39.0 3.5 %collective-permute-start.6 = (f32[8,128]{1,0:T(8,128)S(1)}, f32[8,128]{1,0:T(8,128)S(1)}, u32[]{:S(2)}, u32[]{:S(2)}) collective-permute-start(f32[8,128]{1,0:T(8,128)S(1)} %get-tuple-element.38.refs_0_), channel_id=1, source_target_pairs={{0,8},{4,12},{8,0},{12,4},{1,9},{5,13},{9,1},{13,5},{2,10},{6,14},... | collective-permute-start | bytes 12296 | tf_op jit(solution)/shard_map/ppermute | solution.py:531
  42.4 0.1 collective-permute-start.7
  42.6 0.1 pad_add_fusion.me_ref
  42.6 0.0 collective-permute-done.5.refs_1_
  42.6 1.4 %collective-permute-done.6.refs_2_ = f32[8,128]{1,0:T(8,128)S(1)} collective-permute-done((f32[8,128]{1,0:T(8,128)S(1)}, f32[8,128]{1,0:T(8,128)S(1)}, u32[]{:S(2)}, u32[]{:S(2)}) %collective-permute-start.6) | collective-permute-done | bytes 4128 | tf_op jit(solution)/shard_map/ppermute | solution.py:531
  44.0 3.8 %collective-permute-done.7.refs_3_ = f32[8,128]{1,0:T(8,128)S(1)} collective-permute-done((f32[8,128]{1,0:T(8,128)S(1)}, f32[8,128]{1,0:T(8,128)S(1)}, u32[]{:S(2)}, u32[]{:S(2)}) %collective-permute-start.7) | collective-permute-done | bytes 4128 | tf_op jit(solution)/shard_map/ppermute | solution.py:531
  47.8 4.8 %outgoing.1 = (f32[1,128]{1,0:T(1,128)S(1)}, bf16[2,768,128]{2,1,0:T(8,128)(2,1)S(1)}, f32[32,64]{1,0:T(8,128)S(1)}, bf16[32,2432]{1,0:T(8,128)(2,1)S(1)}, bf16[...) custom-call(s32[2]{0:T(128)S(1)} %pad_add_fusion.me_ref, f32[768,128]{1,0:T(8,128)S(1)} %get-tuple-element.35.s_ref, ...), custom_call_target="tpu_custom_call" | custom-call | flops 2717908992 | tf_op jit(solution)/shard_map/outgoing/pallas_call | solution.py:38
  52.6 0.1 collective-permute-start.10
  52.7 1.6 %collective-permute-start.8 = (bf16[32,2432]{1,0:T(8,128)(2,1)S(1)}, bf16[32,2432]{1,0:T(8,128)(2,1)S(1)}, u32[]{:S(2)}, u32[]{:S(2)}) collective-permute-start(bf16[32,2432]{1,0:T(8,128)(2,1)S(1)} %get-tuple-element.45), channel_id=1, source_target_pairs={{0,3},{1,2},{2,1},{3,0},{4,7},{5,6},{6,5},{7,4},{8,11},{9,10},{10,... | collective-permute-start | bytes 466952 | tf_op jit(solution)/shard_map/ppermute | solution.py:531
  54.3 0.5 collective-permute-start.9
  54.8 2.6 %own_slice.1 = (f32[32,2304]{1,0:T(8,128)S(1)}, f32[64,1152]{1,0:T(8,128)S(1)}, f32[32,64]{1,0:T(8,128)}) custom-call(s32[2]{0:T(128)S(1)} %pad_add_fusion.me_ref, f32[768,128]{1,0:T(8,128)S(1)} %get-tuple-element.35.s_ref, f32[1,128]{1,0:T(1,128)S(1)} %get-tuple-element.39.norm_ref, bf16[2,768,128]{2,1,0:T(8,128)(2,1)S(1)} %get-tuple-element.40.rho_ref, ...), custom_call_target="tpu_custom_call" | custom-call | flops 905969664 | tf_op jit(solution)/shard_map/own_slice/pallas_call | solution.py:38
  57.4 0.0 collective-permute-done.10.refs_2_
  57.5 1.2 %collective-permute-done.8.refs_0_ = bf16[32,2432]{1,0:T(8,128)(2,1)S(1)} collective-permute-done((bf16[32,2432]{1,0:T(8,128)(2,1)S(1)}, bf16[32,2432]{1,0:T(8,128)(2,1)S(1)}, u32[]{:S(2)}, u32[]{:S(2)}) %collective-permute-start.8) | collective-permute-done | bytes 155680 | tf_op jit(solution)/shard_map/ppermute | solution.py:531
  58.6 3.8 %collective-permute-done.9.refs_1_ = bf16[32,2432]{1,0:T(8,128)(2,1)S(1)} collective-permute-done((bf16[32,2432]{1,0:T(8,128)(2,1)S(1)}, bf16[32,2432]{1,0:T(8,128)(2,1)S(1)}, u32[]{:S(2)}, u32[]{:S(2)}) %collective-permute-start.9) | collective-permute-done | bytes 155680 | tf_op jit(solution)/shard_map/ppermute | solution.py:531
  62.4 1.1 %finish.1 = f32[32,2,1152]{2,1,0:T(2,128)} custom-call(f32[64,1152]{1,0:T(8,128)S(1)} %get-tuple-element.42.cw_ref, f32[32,64]{1,0:T(8,128)S(1)} %get-tuple-element.43.mass_ref, f32[32,2304]{1,0:T(8,128)S(1)} %get-tuple-element.44.own_ref, bf16[32,2432]{1,0:T(8,128)(2,1)S(1)} %collective-permute-done.8.refs_0_, ...), custom_call_target="tpu_custom_call" | custom-call | tf_op jit(solution)/shard_map/finish/pallas_call | solution.py:38
  (4 shorter events, 0.0 us)
Async XLA Ops:
  0.6 8.3 %copy-start.1 = (f32[4608]{0:T(1024)S(1)}, f32[4608]{0:T(1024)}, u32[]{:S(2)}) copy-start(f32[4608]{0:T(1024)} %nw_hbm.1) | copy-start | bytes 55300
  0.6 9.4 %copy-start = (f32[64,4608]{1,0:T(8,128)S(1)}, f32[64,4608]{1,0:T(8,128)}, u32[]{:S(2)}) copy-start(f32[64,4608]{1,0:T(8,128)} %ctf_ref.3) | copy-start | bytes 3538948
  0.7 8.0 %copy-start.2 = (s32[24,2]{0,1:T(2,128)S(1)}, s32[24,2]{0,1:T(2,128)}, u32[]{:S(2)}) copy-start(s32[24,2]{0,1:T(2,128)} %param.11) | copy-start | bytes 580
  2.6 17.9 %collective-permute-start = (bf16[32,2432]{1,0:T(8,128)(2,1)S(1)}, bf16[32,2432]{1,0:T(8,128)(2,1)S(1)}, u32[]{:S(2)}, u32[]{:S(2)}) collective-permute-start(bf16[32,2432]{1,0:T(8,128)(2,1)S(1)} %get-tuple-element.25), channel_id=1, source_target_pairs={{0,8},{4,12},{8,0},{12,4},{1,9},{5,13},{9,1},{13,5},{2,10},{6,14},... | collective-permute-start | bytes 466952 | tf_op jit(solution)/shard_map/ppermute | solution.py:531
  6.7 13.8 %collective-permute-start.1 = (bf16[32,2304]{1,0:T(8,128)(2,1)S(1)}, bf16[32,2304]{1,0:T(8,128)(2,1)S(1)}, u32[]{:S(2)}, u32[]{:S(2)}) collective-permute-start(bf16[32,2304]{1,0:T(8,128)(2,1)S(1)} %get-tuple-element.26), channel_id=1, source_target_pairs={{0,8},{4,12},{8,0},{12,4},{1,9},{5,13},{9,1},{13,5},{2,10},{6,14},... | collective-permute-start | bytes 442376 | tf_op jit(solution)/shard_map/ppermute | solution.py:531
  6.8 15.7 %collective-permute-start.2 = (bf16[32,4736]{1,0:T(8,128)(2,1)S(1)}, bf16[32,4736]{1,0:T(8,128)(2,1)S(1)}, u32[]{:S(2)}, u32[]{:S(2)}) collective-permute-start(bf16[32,4736]{1,0:T(8,128)(2,1)S(1)} %get-tuple-element.32.refs_0_), channel_id=1, source_target_pairs={{0,4},{4,0},{8,12},{12,8},{1,5},{5,1},{9,13},{13,9},{2,6},{6,2},{1... | collective-permute-start | bytes 909320 | tf_op jit(solution)/shard_map/ppermute | solution.py:531
  20.5 6.7 %collective-permute-start.3 = (bf16[32,2432]{1,0:T(8,128)(2,1)S(1)}, bf16[32,2432]{1,0:T(8,128)(2,1)S(1)}, u32[]{:S(2)}, u32[]{:S(2)}) collective-permute-start(bf16[32,2432]{1,0:T(8,128)(2,1)S(1)} %collective-permute-done.refs_2_), channel_id=1, source_target_pairs={{0,4},{4,0},{8,12},{12,8},{1,5},{5,1},{9,13},{13,9},{2,6},{6,2},{1... | collective-permute-start | bytes 466952 | tf_op jit(solution)/shard_map/ppermute | solution.py:531
  21.2 11.5 %collective-permute-start.4 = (bf16[32,2304]{1,0:T(8,128)(2,1)S(1)}, bf16[32,2304]{1,0:T(8,128)(2,1)S(1)}, u32[]{:S(2)}, u32[]{:S(2)}) collective-permute-start(bf16[32,2304]{1,0:T(8,128)(2,1)S(1)} %collective-permute-done.1.refs_4_), channel_id=1, source_target_pairs={{0,4},{4,0},{8,12},{12,8},{1,5},{5,1},{9,13},{13,9},{2,6},{6,2},{1... | collective-permute-start | bytes 442376 | tf_op jit(solution)/shard_map/ppermute | solution.py:531
  38.1 4.5 %collective-permute-start.5 = (f32[8,128]{1,0:T(8,128)S(1)}, f32[8,128]{1,0:T(8,128)S(1)}, u32[]{:S(2)}, u32[]{:S(2)}) collective-permute-start(f32[8,128]{1,0:T(8,128)S(1)} %get-tuple-element.38.refs_0_), channel_id=1, source_target_pairs={{0,4},{4,0},{8,12},{12,8},{1,5},{5,1},{9,13},{13,9},{2,6},{6,2},{1... | collective-permute-start | bytes 12296 | tf_op jit(solution)/shard_map/ppermute | solution.py:531
  39.0 5.0 %collective-permute-start.6 = (f32[8,128]{1,0:T(8,128)S(1)}, f32[8,128]{1,0:T(8,128)S(1)}, u32[]{:S(2)}, u32[]{:S(2)}) collective-permute-start(f32[8,128]{1,0:T(8,128)S(1)} %get-tuple-element.38.refs_0_), channel_id=1, source_target_pairs={{0,8},{4,12},{8,0},{12,4},{1,9},{5,13},{9,1},{13,5},{2,10},{6,14},... | collective-permute-start | bytes 12296 | tf_op jit(solution)/shard_map/ppermute | solution.py:531
  42.4 5.4 %collective-permute-start.7 = (f32[8,128]{1,0:T(8,128)S(1)}, f32[8,128]{1,0:T(8,128)S(1)}, u32[]{:S(2)}, u32[]{:S(2)}) collective-permute-start(f32[8,128]{1,0:T(8,128)S(1)} %get-tuple-element.38.refs_0_), channel_id=1, source_target_pairs={{0,12},{4,8},{8,4},{12,0},{1,13},{5,9},{9,5},{13,1},{2,14},{6,10},... | collective-permute-start | bytes 12296 | tf_op jit(solution)/shard_map/ppermute | solution.py:531
  52.6 4.9 %collective-permute-start.10 = (bf16[32,2432]{1,0:T(8,128)(2,1)S(1)}, bf16[32,2432]{1,0:T(8,128)(2,1)S(1)}, u32[]{:S(2)}, u32[]{:S(2)}) collective-permute-start(bf16[32,2432]{1,0:T(8,128)(2,1)S(1)} %get-tuple-element.47), channel_id=1, source_target_pairs={{0,1},{1,0},{2,3},{3,2},{4,5},{5,4},{6,7},{7,6},{8,9},{9,8},{10,11... | collective-permute-start | bytes 466952 | tf_op jit(solution)/shard_map/ppermute | solution.py:531
  52.7 6.0 %collective-permute-start.8 = (bf16[32,2432]{1,0:T(8,128)(2,1)S(1)}, bf16[32,2432]{1,0:T(8,128)(2,1)S(1)}, u32[]{:S(2)}, u32[]{:S(2)}) collective-permute-start(bf16[32,2432]{1,0:T(8,128)(2,1)S(1)} %get-tuple-element.45), channel_id=1, source_target_pairs={{0,3},{1,2},{2,1},{3,0},{4,7},{5,6},{6,5},{7,4},{8,11},{9,10},{10,... | collective-permute-start | bytes 466952 | tf_op jit(solution)/shard_map/ppermute | solution.py:531
  54.3 8.1 %collective-permute-start.9 = (bf16[32,2432]{1,0:T(8,128)(2,1)S(1)}, bf16[32,2432]{1,0:T(8,128)(2,1)S(1)}, u32[]{:S(2)}, u32[]{:S(2)}) collective-permute-start(bf16[32,2432]{1,0:T(8,128)(2,1)S(1)} %get-tuple-element.46), channel_id=1, source_target_pairs={{0,2},{1,3},{2,0},{3,1},{4,6},{5,7},{6,4},{7,5},{8,10},{9,11},{10,... | collective-permute-start | bytes 466952 | tf_op jit(solution)/shard_map/ppermute | solution.py:531

commit v8 on v7

--- a/solution.py
+++ b/solution.py
@@ -154,58 +154,92 @@
     )
 
 
-def template_kernel(cls_ref, cos_ref, sin_ref, temp_ref):
-    _, rows, tile = cls_ref.shape
-    poses = cos_ref.shape[0]
+def write_templates(cls_ref, cos_ref, sin_ref, temp_ref, start, tile):
+    rows = cls_ref.shape[1]
     for a in range(0, tile, LANES):
-        at = slice(a, a + LANES)
-        later = slice(tile + a, tile + a + LANES)
+        at = pl.ds(pl.multiple_of(start + a, LANES), LANES)
         re = cls_ref[0, :, at].astype(f32)
         im = cls_ref[1, :, at].astype(f32)
-        for r in range(poses):
+        for r in range(cos_ref.shape[0]):
             cos_r = cos_ref[r : r + 1, at]
             sin_r = sin_ref[r : r + 1, at]
-            temp_ref[r * rows : (r + 1) * rows, at] = (re * cos_r - im * sin_r).astype(bf16)
-            temp_ref[r * rows : (r + 1) * rows, later] = (re * sin_r + im * cos_r).astype(bf16)
-
-
-def build_templates(split, cos_t, sin_t):
+            here = slice(r * rows, (r + 1) * rows)
+            temp_ref[here, a : a + LANES] = (re * cos_r - im * sin_r).astype(bf16)
+            temp_ref[here, tile + a : tile + a + LANES] = (re * sin_r + im * cos_r).astype(bf16)
+
+
+def template_tile(freq):
+    return max(t for t in range(LANES, 385, LANES) if freq // CHUNKS % t == 0)
+
+
+def early_kernel(cls_ref, cos_ref, sin_ref, temp_ref):
+    write_templates(cls_ref, cos_ref, sin_ref, temp_ref, 0, cls_ref.shape[2])
+
+
+def early_templates(split, cos_t, sin_t):
     _, rows, freq = split.shape
     poses = cos_t.shape[0]
-    tile = max(t for t in range(LANES, 385, LANES) if freq // CHUNKS % t == 0)
+    tile = template_tile(freq)
+    count = freq // tile // 2
+    skip = freq // tile - count
     return pl.pallas_call(
-        template_kernel,
-        grid=(freq // tile,),
+        early_kernel,
+        grid=(count,),
         in_specs=[
-            pl.BlockSpec((2, rows, tile), lambda j: (0, 0, j)),
-            pl.BlockSpec((poses, tile), lambda j: (0, j)),
-            pl.BlockSpec((poses, tile), lambda j: (0, j)),
+            pl.BlockSpec((2, rows, tile), lambda j: (0, 0, skip + j)),
+            pl.BlockSpec((poses, tile), lambda j: (0, skip + j)),
+            pl.BlockSpec((poses, tile), lambda j: (0, skip + j)),
         ],
         out_specs=pl.BlockSpec((None, poses * rows, 2 * tile), lambda j: (j, 0, 0)),
-        out_shape=pltpu.HBM((freq // tile, poses * rows, 2 * tile), bf16),
+        out_shape=pltpu.HBM((count, poses * rows, 2 * tile), bf16),
         compiler_params=pltpu.CompilerParams(vmem_limit_bytes=VMEM_LIMIT),
         cost_estimate=pl.CostEstimate(
-            flops=40 * poses * rows * freq, bytes_accessed=4 * poses * rows * freq, transcendentals=0
+            flops=20 * poses * rows * freq, bytes_accessed=2 * poses * rows * freq, transcendentals=0
         ),
-        name="templates",
+        name="early_templates",
     )(split, cos_t, sin_t)
 
 
-def template_copies(temp_hbm, temp_ref, sem, chunk):
-    count = temp_ref.shape[0]
+def template_kernel(early_hbm, cls_ref, cos_ref, sin_ref, temp_ref, sem):
+    count = early_hbm.shape[0]
+    built = temp_ref.shape[0] - count
+    tile = temp_ref.shape[2] // 2
     copies = [
-        pltpu.make_async_copy(temp_hbm.at[chunk * count + t], temp_ref.at[t], sem.at[t])
+        pltpu.make_async_copy(early_hbm.at[t], temp_ref.at[built + t], sem.at[t])
         for t in range(count)
     ]
     for copy in copies:
         copy.start()
-    return copies
-
-
-def add_products(acc_ref, temp_ref, copies, parts):
+
+    @pl.loop(0, built)
+    def _(t):
+        write_templates(cls_ref, cos_ref, sin_ref, temp_ref.at[t], t * tile, tile)
+
+    for copy in copies:
+        copy.wait()
+
+
+def all_templates(early, split, cos_t, sin_t):
+    _, rows, freq = split.shape
+    poses = cos_t.shape[0]
+    count, columns, width = early.shape
+    return call(
+        template_kernel,
+        "templates",
+        [ANY] + [VMEM] * 3,
+        [pltpu.VMEM((freq // (width // 2), columns, width), bf16)],
+        (pltpu.with_memory_space_constraint(early, pltpu.HBM), split, cos_t, sin_t),
+        [pltpu.SemaphoreType.DMA((count,))],
+        flops=20 * poses * rows * freq,
+        moved=2 * poses * rows * freq,
+    )[0]
+
+
+def add_products(acc_ref, temp_ref, chunk, parts):
+    count = temp_ref.shape[0] // CHUNKS
     tile = temp_ref.shape[2] // 2
-    even = even_index((acc_ref.shape[1], tile), 0)
-    for t, copy in enumerate(copies):
+    even = even_index((acc_ref.shape[0], tile), 0)
+    for t in range(count):
         wide = jnp.concatenate(
             [ref[:, start + t * tile : start + (t + 1) * tile] for ref, start in parts], axis=0
         ).astype(f32)
@@ -213,8 +247,9 @@
             [jnp.where(even, wide, 0.0).astype(bf16), jnp.where(even, 0.0, wide).astype(bf16)],
             axis=1,
         )
-        copy.wait()
-        acc_ref[...] += lax.dot_general(temp_ref[t], split, NT, preferred_element_type=f32)
+        acc_ref[...] += lax.dot_general(
+            split, temp_ref[chunk * count + t], NT, preferred_element_type=f32
+        )
 
 
 def chunk_parts(refs, chunked, chunk, span):
@@ -222,18 +257,16 @@
     return whole + [(ref, 0) for ref in refs[len(refs) - chunked :]]
 
 
-def score_kernel(chunk, span, chunked, temp_hbm, *refs):
-    refs, (acc_ref, temp_ref, sem) = refs[:-3], refs[-3:]
-    copies = template_copies(temp_hbm, temp_ref, sem, chunk)
+def score_kernel(chunk, span, chunked, temp_ref, *refs):
+    refs, acc_ref = refs[:-1], refs[-1]
     parts = refs if chunk == 0 else refs[1:]
     acc_ref[...] = jnp.zeros_like(acc_ref) if chunk == 0 else refs[0][...]
-    add_products(acc_ref, temp_ref, copies, chunk_parts(parts, chunked, chunk, span))
-
-
-def last_score_kernel(wholes, chunked, span, temp_hbm, pow_ref, *refs):
+    add_products(acc_ref, temp_ref, chunk, chunk_parts(parts, chunked, chunk, span))
+
+
+def last_score_kernel(wholes, chunked, span, temp_ref, pow_ref, *refs):
     refs = list(refs)
-    s_ref, all_ref, marks_ref, stat_ref, temp_ref, sem = refs[-6:]
-    copies = template_copies(temp_hbm, temp_ref, sem, CHUNKS - 1)
+    s_ref, all_ref, marks_ref, stat_ref, acc_ref = refs[-5:]
     whole = refs[:wholes]
     chunks = [refs[wholes + c * chunked : wholes + (c + 1) * chunked] for c in range(CHUNKS)]
     rows, groups = pow_ref.shape
@@ -256,10 +289,10 @@
     penalty = lax.dot_general(
         pow_ref[...], marks, NT, precision=HIGHEST, preferred_element_type=f32
     )
-    s_ref[...] = refs[wholes + CHUNKS * chunked][...] if CHUNKS > 1 else jnp.zeros_like(s_ref)
+    acc_ref[...] = refs[wholes + CHUNKS * chunked][...] if CHUNKS > 1 else jnp.zeros_like(acc_ref)
     parts = chunk_parts(whole + chunks[-1], chunked, CHUNKS - 1, span)
-    add_products(s_ref, temp_ref, copies, parts)
-    acc = s_ref[...]
+    add_products(acc_ref, temp_ref, CHUNKS - 1, parts)
+    acc = acc_ref[...].T
     acc = acc + jnp.where(
         even_index(acc.shape, 1), pltpu.roll(acc, lanes - 1, 1), pltpu.roll(acc, 1, 1)
     )
@@ -273,16 +306,10 @@
 
 
 def score(temps, power, whole, chunks, freq):
-    temps = pltpu.with_memory_space_constraint(temps, pltpu.HBM)
-    tiles, columns, width = temps.shape
+    columns = temps.shape[1]
     span = freq // CHUNKS
     chunked = len(chunks[0])
     lanes = sum(p.shape[0] for p in whole + chunks[0])
-    acc_shape = jax.ShapeDtypeStruct((columns, lanes), f32)
-    scratch = [
-        pltpu.VMEM((tiles // CHUNKS, columns, width), bf16),
-        pltpu.SemaphoreType.DMA((tiles // CHUNKS,)),
-    ]
     flops = 2 * columns * 256 * 2 * span
     acc = []
     for c in range(CHUNKS - 1):
@@ -290,25 +317,24 @@
         acc = call(
             functools.partial(score_kernel, c, span, chunked),
             f"score{c}",
-            [ANY] + [VMEM] * (len(operands) - 1),
-            [acc_shape],
+            [VMEM] * len(operands),
+            [jax.ShapeDtypeStruct((lanes, columns), f32)],
             operands,
-            scratch,
             flops=flops,
         )
     operands = [temps, power, *whole, *[p for parts in chunks for p in parts], *acc]
     return call(
         functools.partial(last_score_kernel, len(whole), chunked, span),
         f"score{CHUNKS - 1}",
-        [ANY] + [VMEM] * (len(operands) - 1),
+        [VMEM] * len(operands),
         [
-            acc_shape,
+            jax.ShapeDtypeStruct((columns, lanes), f32),
             jax.ShapeDtypeStruct((lanes, freq), bf16),
             jax.ShapeDtypeStruct((lanes, power.shape[1]), f32),
             jax.ShapeDtypeStruct((8, lanes), f32),
         ],
         operands,
-        scratch,
+        [pltpu.VMEM((lanes, columns), f32)],
         flops=flops,
     )
 
@@ -550,10 +576,11 @@
 
     split = jnp.transpose(classes, (1, 0, 2))
     cos_t, sin_t, power = prepare(split, phase_tables(shifts, freq), ctf, noise_weight)
-    temps = build_templates(split, cos_t, sin_t)
+    early = early_templates(split, cos_t, sin_t)
     if pairwise:
-        far, power, temps = lax.optimization_barrier((far, power, temps))
+        far, split, early = lax.optimization_barrier((far, split, early))
         whole, chunks = [own, near], [[w, swap(w, "cls", 1)] for w in far]
+    temps = all_templates(early, split, cos_t, sin_t)
     scores, weighted, marks, stat = score(temps, power, whole, chunks, freq)
     if pairwise:
         stats = [stat] + [swap(stat, "cls", k) for k in range(1, n_cls)]

time: 63.7 us -> 58.2 us (0.914)
  Pallas kernels: 31.1 us -> 24.5 us
  local copies, waits for them, and re-layouts: 1.15 us -> 3.14 us
  waiting for transfers between devices: 15.4 us -> 13.7 us
  other arithmetic: 0.34 us -> 1.09 us
    pallas_call x1, Pallas kernels: 8.68 us -> 4.57 us  [early_templates(): pl.pallas_call(early_kernel, grid=(count,), in_specs=[pl.BlockSpec((2, ro...]
    pallas_call x7 -> x8, Pallas kernels: 22.5 us -> 19.9 us  [call(): pl.pallas_call(kernel, in_specs=in_specs, out_specs=[VMEM] * len(out_shap...]
    ppermute x11, waiting for transfers between devices: 15.4 us -> 13.7 us  [swap(): return lax.ppermute(values, axis, [(i, i ^ distance) for i in range(size)])]
    unnamed x7 -> x5, local copies, waits for them, and re-layouts: 1.14 us -> 2.4 us
    mul x1, other arithmetic: 0.01 us -> 0.76 us  [phase_tables(): angle_y = step * (shifts[:, 1:2].astype(f32) * along_y[None, :])]
    broadcast_in_dim x1, local copies, waits for them, and re-layouts: 0.01 us -> 0.74 us  [local(): noise_weight = noise_weight[None, :]]
  transfers between devices with their start and end apart: 11 -> 11, of which waited for: 6 -> 6; matrix products, arithmetic and copies ran while one was open for 2% -> 5% of each run, Pallas kernels for 28% -> 24%
where the time goes in v8:
time: 58.2 us; the launch traced here: 57.9 us
  Pallas kernels  24.5 us (42%)
  starting transfers between devices  14.7 us (25%)
  waiting for transfers between devices  13.7 us (24%)
  local copies, waits for them, and re-layouts  3.14 us (5%)
  other arithmetic  1.09 us (2%)
  between operations  0.74 us (1%)
    pallas_call x8, Pallas kernels, call(): pl.pallas_call(kernel, in_specs=in_specs, out_specs=[VMEM] * len(out_shap...  19.9 us
    ppermute x11, starting transfers between devices, swap(): return lax.ppermute(values, axis, [(i, i ^ distance) for i in range(size)])  14.7 us
    ppermute x11, waiting for transfers between devices, swap(): return lax.ppermute(values, axis, [(i, i ^ distance) for i in range(size)])  13.7 us
    pallas_call x1, Pallas kernels, early_templates(): pl.pallas_call(early_kernel, grid=(count,), in_specs=[pl.BlockSpec((2, ro...  4.57 us
    unnamed x5, local copies, waits for them, and re-layouts  2.4 us
  transfers between devices with their start and end apart: 11, of which 6 were waited for; matrix products, arithmetic and copies ran while one was open for 5% of the time, Pallas kernels for 24%

profile of v8, /device:TPU:0, one launch (start us, length us, event | category | flops | bytes accessed | tf_op | source)
XLA Modules:
  0.0 57.9 jit_solution(13342432870392657862)
XLA Ops:
  0.6 1.8 %weigh.1 = (bf16[32,4736]{1,0:T(8,128)(2,1)S(1)}, bf16[32,2432]{1,0:T(8,128)(2,1)S(1)}, bf16[32,2304]{1,0:T(8,128)(2,1)S(1)}) custom-call(s32[16]{0:T(128)} %ids_hbm.1, bf16[16,2,4608]{2,1,0:T(2,128)(2,1)} %p_hbm.1, f32[64,4608]{1,0:T(8,128)} %ctf_ref.3, f32[4608]{0:T(1024)} %nw_hbm.1), custom_call_target="tpu_custom_call" | custom-call | flops 294912 | bytes 1179648 | tf_op jit(solution)/shard_map/weigh/pallas_call | solution.py:38
  2.5 4.1 %collective-permute-start = (bf16[32,2432]{1,0:T(8,128)(2,1)S(1)}, bf16[32,2432]{1,0:T(8,128)(2,1)S(1)}, u32[]{:S(2)}, u32[]{:S(2)}) collective-permute-start(bf16[32,2432]{1,0:T(8,128)(2,1)S(1)} %get-tuple-element.25), channel_id=1, source_target_pairs={{0,8},{4,12},{8,0},{12,4},{1,9},{5,13},{9,1},{13,5},{2,10},{6,14},... | collective-permute-start | bytes 466952 | tf_op jit(solution)/shard_map/ppermute | solution.py:557
  6.6 0.1 collective-permute-start.1
  6.7 1.8 %collective-permute-start.2 = (bf16[32,4736]{1,0:T(8,128)(2,1)S(1)}, bf16[32,4736]{1,0:T(8,128)(2,1)S(1)}, u32[]{:S(2)}, u32[]{:S(2)}) collective-permute-start(bf16[32,4736]{1,0:T(8,128)(2,1)S(1)} %get-tuple-element.32.refs_0_), channel_id=1, source_target_pairs={{0,4},{4,0},{8,12},{12,8},{1,5},{5,1},{9,13},{13,9},{2,6},{6,2},{1... | collective-permute-start | bytes 909320 | tf_op jit(solution)/shard_map/ppermute | solution.py:557
  8.5 0.7 %broadcast_in_dim.2.nw_ref = f32[1,4608]{1,0:T(1,128)S(1)} reshape(f32[4608]{0:T(1024)} %nw_hbm.1) | data formatting | bytes 36864 | tf_op jit(solution)/shard_map/broadcast_in_dim | solution.py:570
  9.3 1.1 %copy.10 = bf16[32,2,4608]{2,0,1:T(8,128)(2,1)S(1)} copy(bf16[32,2,4608]{2,1,0:T(2,128)(2,1)} %param.7) | data formatting | bytes 1179648 | tf_op args[1]
  10.4 0.8 %convert_bitcast_fusion = (f32[24]{0:T(128)S(1)}, f32[24]{0:T(128)S(1)}) fusion(s32[24,2]{0,1:T(2,128)} %param.11), kind=kLoop, calls=%fused_computation.9 | loop fusion | flops 48 | bytes 384 | tf_op jit(solution)/shard_map/mul | solution.py:33
  11.1 0.1 fusion
  11.3 0.1 fusion.2
  11.4 0.0 copy-start
  11.4 1.3 %copy-done = f32[64,4608]{1,0:T(8,128)S(1)} copy-done((f32[64,4608]{1,0:T(8,128)S(1)}, f32[64,4608]{1,0:T(8,128)}, u32[]{:S(2)}) %copy-start) | copy-done | bytes 1179672
  12.7 1.2 %prepare.1 = (f32[24,4608]{1,0:T(8,128)S(1)}, f32[24,4608]{1,0:T(8,128)S(1)}, f32[32,64]{1,0:T(8,128)S(1)}) custom-call(bf16[2,32,4608]{2,1,0:T(8,128)(2,1)S(1)} %bitcast.10, f32[24,128]{1,0:T(8,128)S(1)} %get-tuple-element.53.xc_ref, f32[24,128]{1,0:T(8,128)S(1)} %get-tuple-element.52.xs_ref, f32[24,36]{1,0:T(8,128)S(1)} %get-tuple-element.49.yc_ref, ...), custom_call_target="tpu_custom_call" | custom-call | flops 226492416 | tf_op jit(solution)/shard_map/prepare/pallas_call | solution.py:38
  13.9 4.6 %early_templates.1.early_hbm = bf16[6,768,768]{2,1,0:T(8,128)(2,1)} custom-call(bf16[2,32,4608]{2,1,0:T(8,128)(2,1)S(1)} %bitcast.11, f32[24,4608]{1,0:T(8,128)S(1)} %get-tuple-element.27.cos_ref, f32[24,4608]{1,0:T(8,128)S(1)} %get-tuple-element.28.sin_ref), custom_call_target="tpu_custom_call" | custom-call | flops 70778880 | bytes 7077888 | tf_op jit(solution)/shard_map/early_templates/pallas_call | solution.py:185
  18.4 1.9 %collective-permute-done.1.refs_4_ = bf16[32,2304]{1,0:T(8,128)(2,1)S(1)} collective-permute-done((bf16[32,2304]{1,0:T(8,128)(2,1)S(1)}, bf16[32,2304]{1,0:T(8,128)(2,1)S(1)}, u32[]{:S(2)}, u32[]{:S(2)}) %collective-permute-start.1) | collective-permute-done | bytes 147488 | tf_op jit(solution)/shard_map/ppermute | solution.py:557
  20.4 0.0 collective-permute-done.refs_2_
  20.4 0.7 %collective-permute-start.3 = (bf16[32,2432]{1,0:T(8,128)(2,1)S(1)}, bf16[32,2432]{1,0:T(8,128)(2,1)S(1)}, u32[]{:S(2)}, u32[]{:S(2)}) collective-permute-start(bf16[32,2432]{1,0:T(8,128)(2,1)S(1)} %collective-permute-done.refs_2_), channel_id=1, source_target_pairs={{0,4},{4,0},{8,12},{12,8},{1,5},{5,1},{9,13},{13,9},{2,6},{6,2},{1... | collective-permute-start | bytes 466952 | tf_op jit(solution)/shard_map/ppermute | solution.py:557
  21.0 1.4 %collective-permute-start.4 = (bf16[32,2304]{1,0:T(8,128)(2,1)S(1)}, bf16[32,2304]{1,0:T(8,128)(2,1)S(1)}, u32[]{:S(2)}, u32[]{:S(2)}) collective-permute-start(bf16[32,2304]{1,0:T(8,128)(2,1)S(1)} %collective-permute-done.1.refs_4_), channel_id=1, source_target_pairs={{0,4},{4,0},{8,12},{12,8},{1,5},{5,1},{9,13},{13,9},{2,6},{6,2},{1... | collective-permute-start | bytes 442376 | tf_op jit(solution)/shard_map/ppermute | solution.py:557
  22.4 3.1 %templates.1.temp_ref = bf16[12,768,768]{2,1,0:T(8,128)(2,1)S(1)} custom-call(bf16[6,768,768]{2,1,0:T(8,128)(2,1)} %early_templates.1.early_hbm, bf16[2,32,4608]{2,1,0:T(8,128)(2,1)S(1)} %bitcast.12, f32[24,4608]{1,0:T(8,128)S(1)} %get-tuple-element.27.cos_ref, f32[24,4608]{1,0:T(8,128)S(1)} %get-tuple-element.28.sin_ref), custom_call_target="tpu_custom_call" | custom-call | flops 70778880 | bytes 7077888 | tf_op jit(solution)/shard_map/templates/pallas_call | solution.py:38
  25.5 0.0 collective-permute-done.2.refs_1_
  25.5 1.6 %collective-permute-done.3.refs_3_ = bf16[32,2432]{1,0:T(8,128)(2,1)S(1)} collective-permute-done((bf16[32,2432]{1,0:T(8,128)(2,1)S(1)}, bf16[32,2432]{1,0:T(8,128)(2,1)S(1)}, u32[]{:S(2)}, u32[]{:S(2)}) %collective-permute-start.3) | collective-permute-done | bytes 155680 | tf_op jit(solution)/shard_map/ppermute | solution.py:557
  27.1 2.4 %score0.1.refs_6_ = f32[128,768]{1,0:T(8,128)S(1)} custom-call(bf16[12,768,768]{2,1,0:T(8,128)(2,1)S(1)} %templates.1.temp_ref, bf16[32,4736]{1,0:T(8,128)(2,1)S(1)} %get-tuple-element.32.refs_0_, bf16[32,4736]{1,0:T(8,128)(2,1)S(1)} %collective-permute-done.2.refs_1_, bf16[32,2432]{1,0:T(8,128)(2,1)S(1)} %collective-permute-done.refs_2_, ...), custom_call_target="tpu_custom_call" | custom-call | flops 1811939328 | tf_op jit(solution)/shard_map/score0/pallas_call | solution.py:38
  29.5 0.0 collective-permute-done.4.refs_5_
  29.5 2.9 %score1.1 = (f32[768,128]{1,0:T(8,128)S(1)}, bf16[128,4608]{1,0:T(8,128)(2,1)S(1)}, f32[128,64]{1,0:T(8,128)S(1)}, f32[8,128]{1,0:T(8,128)S(1)}) custom-call(bf16[12,768,768]{2,1,0:T(8,128)(2,1)S(1)} %templates.1.temp_ref, f32[32,64]{1,0:T(8,128)S(1)} %get-tuple-element.31.pow_ref, bf16[32,4736]{1,0:T(8,128)(2,1)S(1)} %get-tuple-element.32.refs_0_, ...), custom_call_target="tpu_custom_call" | custom-call | flops 1811939328 | tf_op jit(solution)/shard_map/score1/pallas_call | solution.py:38
  32.4 0.0 copy-start.1
  32.5 0.9 %collective-permute-start.5 = (f32[8,128]{1,0:T(8,128)S(1)}, f32[8,128]{1,0:T(8,128)S(1)}, u32[]{:S(2)}, u32[]{:S(2)}) collective-permute-start(f32[8,128]{1,0:T(8,128)S(1)} %get-tuple-element.38.refs_0_), channel_id=1, source_target_pairs={{0,4},{4,0},{8,12},{12,8},{1,5},{5,1},{9,13},{13,9},{2,6},{6,2},{1... | collective-permute-start | bytes 12296 | tf_op jit(solution)/shard_map/ppermute | solution.py:557
  33.3 3.5 %collective-permute-start.6 = (f32[8,128]{1,0:T(8,128)S(1)}, f32[8,128]{1,0:T(8,128)S(1)}, u32[]{:S(2)}, u32[]{:S(2)}) collective-permute-start(f32[8,128]{1,0:T(8,128)S(1)} %get-tuple-element.38.refs_0_), channel_id=1, source_target_pairs={{0,8},{4,12},{8,0},{12,4},{1,9},{5,13},{9,1},{13,5},{2,10},{6,14},... | collective-permute-start | bytes 12296 | tf_op jit(solution)/shard_map/ppermute | solution.py:557
  36.8 0.1 collective-permute-start.7
  36.9 0.1 pad_add_fusion.me_ref
  37.0 0.0 collective-permute-done.5.refs_1_
  37.0 1.4 %collective-permute-done.6.refs_2_ = f32[8,128]{1,0:T(8,128)S(1)} collective-permute-done((f32[8,128]{1,0:T(8,128)S(1)}, f32[8,128]{1,0:T(8,128)S(1)}, u32[]{:S(2)}, u32[]{:S(2)}) %collective-permute-start.6) | collective-permute-done | bytes 4128 | tf_op jit(solution)/shard_map/ppermute | solution.py:557
  38.4 3.8 %collective-permute-done.7.refs_3_ = f32[8,128]{1,0:T(8,128)S(1)} collective-permute-done((f32[8,128]{1,0:T(8,128)S(1)}, f32[8,128]{1,0:T(8,128)S(1)}, u32[]{:S(2)}, u32[]{:S(2)}) %collective-permute-start.7) | collective-permute-done | bytes 4128 | tf_op jit(solution)/shard_map/ppermute | solution.py:557
  42.2 4.8 %outgoing.1 = (f32[1,128]{1,0:T(1,128)S(1)}, bf16[2,768,128]{2,1,0:T(8,128)(2,1)S(1)}, f32[32,64]{1,0:T(8,128)S(1)}, bf16[32,2432]{1,0:T(8,128)(2,1)S(1)}, bf16[...) custom-call(s32[2]{0:T(128)S(1)} %pad_add_fusion.me_ref, f32[768,128]{1,0:T(8,128)S(1)} %get-tuple-element.35.s_ref, ...), custom_call_target="tpu_custom_call" | custom-call | flops 2717908992 | tf_op jit(solution)/shard_map/outgoing/pallas_call | solution.py:38
  47.0 0.1 collective-permute-start.10
  47.0 1.6 %collective-permute-start.8 = (bf16[32,2432]{1,0:T(8,128)(2,1)S(1)}, bf16[32,2432]{1,0:T(8,128)(2,1)S(1)}, u32[]{:S(2)}, u32[]{:S(2)}) collective-permute-start(bf16[32,2432]{1,0:T(8,128)(2,1)S(1)} %get-tuple-element.45), channel_id=1, source_target_pairs={{0,3},{1,2},{2,1},{3,0},{4,7},{5,6},{6,5},{7,4},{8,11},{9,10},{10,... | collective-permute-start | bytes 466952 | tf_op jit(solution)/shard_map/ppermute | solution.py:557
  48.6 0.5 collective-permute-start.9
  49.2 0.0 copy-done.1
  49.2 2.6 %own_slice.1 = (f32[32,2304]{1,0:T(8,128)S(1)}, f32[64,1152]{1,0:T(8,128)S(1)}, f32[32,64]{1,0:T(8,128)}) custom-call(s32[2]{0:T(128)S(1)} %pad_add_fusion.me_ref, f32[768,128]{1,0:T(8,128)S(1)} %get-tuple-element.35.s_ref, f32[1,128]{1,0:T(1,128)S(1)} %get-tuple-element.39.norm_ref, bf16[2,768,128]{2,1,0:T(8,128)(2,1)S(1)} %get-tuple-element.40.rho_ref, ...), custom_call_target="tpu_custom_call" | custom-call | flops 905969664 | tf_op jit(solution)/shard_map/own_slice/pallas_call | solution.py:38
  51.8 0.0 collective-permute-done.10.refs_2_
  51.8 1.2 %collective-permute-done.8.refs_0_ = bf16[32,2432]{1,0:T(8,128)(2,1)S(1)} collective-permute-done((bf16[32,2432]{1,0:T(8,128)(2,1)S(1)}, bf16[32,2432]{1,0:T(8,128)(2,1)S(1)}, u32[]{:S(2)}, u32[]{:S(2)}) %collective-permute-start.8) | collective-permute-done | bytes 155680 | tf_op jit(solution)/shard_map/ppermute | solution.py:557
  53.0 3.8 %collective-permute-done.9.refs_1_ = bf16[32,2432]{1,0:T(8,128)(2,1)S(1)} collective-permute-done((bf16[32,2432]{1,0:T(8,128)(2,1)S(1)}, bf16[32,2432]{1,0:T(8,128)(2,1)S(1)}, u32[]{:S(2)}, u32[]{:S(2)}) %collective-permute-start.9) | collective-permute-done | bytes 155680 | tf_op jit(solution)/shard_map/ppermute | solution.py:557
  56.8 1.1 %finish.1 = f32[32,2,1152]{2,1,0:T(2,128)} custom-call(f32[64,1152]{1,0:T(8,128)S(1)} %get-tuple-element.42.cw_ref, f32[32,64]{1,0:T(8,128)S(1)} %get-tuple-element.43.mass_ref, f32[32,2304]{1,0:T(8,128)S(1)} %get-tuple-element.44.own_ref, bf16[32,2432]{1,0:T(8,128)(2,1)S(1)} %collective-permute-done.8.refs_0_, ...), custom_call_target="tpu_custom_call" | custom-call | tf_op jit(solution)/shard_map/finish/pallas_call | solution.py:38
  (2 shorter events, 0.0 us)
Async XLA Ops:
  2.5 17.9 %collective-permute-start = (bf16[32,2432]{1,0:T(8,128)(2,1)S(1)}, bf16[32,2432]{1,0:T(8,128)(2,1)S(1)}, u32[]{:S(2)}, u32[]{:S(2)}) collective-permute-start(bf16[32,2432]{1,0:T(8,128)(2,1)S(1)} %get-tuple-element.25), channel_id=1, source_target_pairs={{0,8},{4,12},{8,0},{12,4},{1,9},{5,13},{9,1},{13,5},{2,10},{6,14},... | collective-permute-start | bytes 466952 | tf_op jit(solution)/shard_map/ppermute | solution.py:557
  6.6 13.8 %collective-permute-start.1 = (bf16[32,2304]{1,0:T(8,128)(2,1)S(1)}, bf16[32,2304]{1,0:T(8,128)(2,1)S(1)}, u32[]{:S(2)}, u32[]{:S(2)}) collective-permute-start(bf16[32,2304]{1,0:T(8,128)(2,1)S(1)} %get-tuple-element.26), channel_id=1, source_target_pairs={{0,8},{4,12},{8,0},{12,4},{1,9},{5,13},{9,1},{13,5},{2,10},{6,14},... | collective-permute-start | bytes 442376 | tf_op jit(solution)/shard_map/ppermute | solution.py:557
  6.7 18.8 %collective-permute-start.2 = (bf16[32,4736]{1,0:T(8,128)(2,1)S(1)}, bf16[32,4736]{1,0:T(8,128)(2,1)S(1)}, u32[]{:S(2)}, u32[]{:S(2)}) collective-permute-start(bf16[32,4736]{1,0:T(8,128)(2,1)S(1)} %get-tuple-element.32.refs_0_), channel_id=1, source_target_pairs={{0,4},{4,0},{8,12},{12,8},{1,5},{5,1},{9,13},{13,9},{2,6},{6,2},{1... | collective-permute-start | bytes 909320 | tf_op jit(solution)/shard_map/ppermute | solution.py:557
  11.4 1.3 %copy-start = (f32[64,4608]{1,0:T(8,128)S(1)}, f32[64,4608]{1,0:T(8,128)}, u32[]{:S(2)}) copy-start(f32[64,4608]{1,0:T(8,128)} %ctf_ref.3) | copy-start | bytes 3538948
  20.4 6.7 %collective-permute-start.3 = (bf16[32,2432]{1,0:T(8,128)(2,1)S(1)}, bf16[32,2432]{1,0:T(8,128)(2,1)S(1)}, u32[]{:S(2)}, u32[]{:S(2)}) collective-permute-start(bf16[32,2432]{1,0:T(8,128)(2,1)S(1)} %collective-permute-done.refs_2_), channel_id=1, source_target_pairs={{0,4},{4,0},{8,12},{12,8},{1,5},{5,1},{9,13},{13,9},{2,6},{6,2},{1... | collective-permute-start | bytes 466952 | tf_op jit(solution)/shard_map/ppermute | solution.py:557
  21.0 8.5 %collective-permute-start.4 = (bf16[32,2304]{1,0:T(8,128)(2,1)S(1)}, bf16[32,2304]{1,0:T(8,128)(2,1)S(1)}, u32[]{:S(2)}, u32[]{:S(2)}) collective-permute-start(bf16[32,2304]{1,0:T(8,128)(2,1)S(1)} %collective-permute-done.1.refs_4_), channel_id=1, source_target_pairs={{0,4},{4,0},{8,12},{12,8},{1,5},{5,1},{9,13},{13,9},{2,6},{6,2},{1... | collective-permute-start | bytes 442376 | tf_op jit(solution)/shard_map/ppermute | solution.py:557
  32.4 16.7 %copy-start.1 = (f32[64,4608]{1,0:T(8,128)S(1)}, f32[64,4608]{1,0:T(8,128)}, u32[]{:S(2)}) copy-start(f32[64,4608]{1,0:T(8,128)} %ctf_ref.3) | copy-start | bytes 3538948
  32.5 4.5 %collective-permute-start.5 = (f32[8,128]{1,0:T(8,128)S(1)}, f32[8,128]{1,0:T(8,128)S(1)}, u32[]{:S(2)}, u32[]{:S(2)}) collective-permute-start(f32[8,128]{1,0:T(8,128)S(1)} %get-tuple-element.38.refs_0_), channel_id=1, source_target_pairs={{0,4},{4,0},{8,12},{12,8},{1,5},{5,1},{9,13},{13,9},{2,6},{6,2},{1... | collective-permute-start | bytes 12296 | tf_op jit(solution)/shard_map/ppermute | solution.py:557
  33.3 5.0 %collective-permute-start.6 = (f32[8,128]{1,0:T(8,128)S(1)}, f32[8,128]{1,0:T(8,128)S(1)}, u32[]{:S(2)}, u32[]{:S(2)}) collective-permute-start(f32[8,128]{1,0:T(8,128)S(1)} %get-tuple-element.38.refs_0_), channel_id=1, source_target_pairs={{0,8},{4,12},{8,0},{12,4},{1,9},{5,13},{9,1},{13,5},{2,10},{6,14},... | collective-permute-start | bytes 12296 | tf_op jit(solution)/shard_map/ppermute | solution.py:557
  36.8 5.4 %collective-permute-start.7 = (f32[8,128]{1,0:T(8,128)S(1)}, f32[8,128]{1,0:T(8,128)S(1)}, u32[]{:S(2)}, u32[]{:S(2)}) collective-permute-start(f32[8,128]{1,0:T(8,128)S(1)} %get-tuple-element.38.refs_0_), channel_id=1, source_target_pairs={{0,12},{4,8},{8,4},{12,0},{1,13},{5,9},{9,5},{13,1},{2,14},{6,10},... | collective-permute-start | bytes 12296 | tf_op jit(solution)/shard_map/ppermute | solution.py:557
  47.0 4.9 %collective-permute-start.10 = (bf16[32,2432]{1,0:T(8,128)(2,1)S(1)}, bf16[32,2432]{1,0:T(8,128)(2,1)S(1)}, u32[]{:S(2)}, u32[]{:S(2)}) collective-permute-start(bf16[32,2432]{1,0:T(8,128)(2,1)S(1)} %get-tuple-element.47), channel_id=1, source_target_pairs={{0,1},{1,0},{2,3},{3,2},{4,5},{5,4},{6,7},{7,6},{8,9},{9,8},{10,11... | collective-permute-start | bytes 466952 | tf_op jit(solution)/shard_map/ppermute | solution.py:557
  47.0 6.0 %collective-permute-start.8 = (bf16[32,2432]{1,0:T(8,128)(2,1)S(1)}, bf16[32,2432]{1,0:T(8,128)(2,1)S(1)}, u32[]{:S(2)}, u32[]{:S(2)}) collective-permute-start(bf16[32,2432]{1,0:T(8,128)(2,1)S(1)} %get-tuple-element.45), channel_id=1, source_target_pairs={{0,3},{1,2},{2,1},{3,0},{4,7},{5,6},{6,5},{7,4},{8,11},{9,10},{10,... | collective-permute-start | bytes 466952 | tf_op jit(solution)/shard_map/ppermute | solution.py:557
  48.6 8.1 %collective-permute-start.9 = (bf16[32,2432]{1,0:T(8,128)(2,1)S(1)}, bf16[32,2432]{1,0:T(8,128)(2,1)S(1)}, u32[]{:S(2)}, u32[]{:S(2)}) collective-permute-start(bf16[32,2432]{1,0:T(8,128)(2,1)S(1)} %get-tuple-element.46), channel_id=1, source_target_pairs={{0,2},{1,3},{2,0},{3,1},{4,6},{5,7},{6,4},{7,5},{8,10},{9,11},{10,... | collective-permute-start | bytes 466952 | tf_op jit(solution)/shard_map/ppermute | solution.py:557

commit v9 on v8

--- a/solution.py
+++ b/solution.py
@@ -238,7 +238,7 @@
 def add_products(acc_ref, temp_ref, chunk, parts):
     count = temp_ref.shape[0] // CHUNKS
     tile = temp_ref.shape[2] // 2
-    even = even_index((acc_ref.shape[0], tile), 0)
+    even = even_index((acc_ref.shape[1], tile), 0)
     for t in range(count):
         wide = jnp.concatenate(
             [ref[:, start + t * tile : start + (t + 1) * tile] for ref, start in parts], axis=0
@@ -248,7 +248,7 @@
             axis=1,
         )
         acc_ref[...] += lax.dot_general(
-            split, temp_ref[chunk * count + t], NT, preferred_element_type=f32
+            temp_ref[chunk * count + t], split, NT, preferred_element_type=f32
         )
 
 
@@ -266,7 +266,7 @@
 
 def last_score_kernel(wholes, chunked, span, temp_ref, pow_ref, *refs):
     refs = list(refs)
-    s_ref, all_ref, marks_ref, stat_ref, acc_ref = refs[-5:]
+    s_ref, all_ref, marks_ref, stat_ref = refs[-4:]
     whole = refs[:wholes]
     chunks = [refs[wholes + c * chunked : wholes + (c + 1) * chunked] for c in range(CHUNKS)]
     rows, groups = pow_ref.shape
@@ -289,10 +289,10 @@
     penalty = lax.dot_general(
         pow_ref[...], marks, NT, precision=HIGHEST, preferred_element_type=f32
     )
-    acc_ref[...] = refs[wholes + CHUNKS * chunked][...] if CHUNKS > 1 else jnp.zeros_like(acc_ref)
+    s_ref[...] = refs[wholes + CHUNKS * chunked][...] if CHUNKS > 1 else jnp.zeros_like(s_ref)
     parts = chunk_parts(whole + chunks[-1], chunked, CHUNKS - 1, span)
-    add_products(acc_ref, temp_ref, CHUNKS - 1, parts)
-    acc = acc_ref[...].T
+    add_products(s_ref, temp_ref, CHUNKS - 1, parts)
+    acc = s_ref[...]
     acc = acc + jnp.where(
         even_index(acc.shape, 1), pltpu.roll(acc, lanes - 1, 1), pltpu.roll(acc, 1, 1)
     )
@@ -318,7 +318,7 @@
             functools.partial(score_kernel, c, span, chunked),
             f"score{c}",
             [VMEM] * len(operands),
-            [jax.ShapeDtypeStruct((lanes, columns), f32)],
+            [jax.ShapeDtypeStruct((columns, lanes), f32)],
             operands,
             flops=flops,
         )
@@ -334,7 +334,6 @@
             jax.ShapeDtypeStruct((8, lanes), f32),
         ],
         operands,
-        [pltpu.VMEM((lanes, columns), f32)],
         flops=flops,
     )
 
@@ -594,10 +593,12 @@
     norm, rho, mass, *parts = outgoing_slices(
         me, scores, marks, cos_t, sin_t, weighted, stats, paired, others, block, span
     )
-    received = [swap(part, "img", d) for part, d in zip(parts, others)]
+    received = [swap(part, "img", d) for part, d in zip(parts[:-1], others[:-1])]
     mine, weight, log_resp = own_slice(
         me, scores, norm, rho, cos_t, sin_t, weighted, ctf, noise_weight, block, span
     )
+    last, mine = lax.optimization_barrier((parts[-1], mine))
+    received.append(swap(last, "img", others[-1]))
     averages = finish(weight, mass, mine, received, span)
     return (log_resp.T, averages)
 

time: 58.2 us -> 59.9 us (1.029)
  waiting for transfers between devices: 13.7 us -> 16.4 us
  Pallas kernels: 24.5 us -> 23.6 us
    ppermute x11, waiting for transfers between devices: 13.7 us -> 16.4 us  [swap(): return lax.ppermute(values, axis, [(i, i ^ distance) for i in range(size)])]
    pallas_call x8, Pallas kernels: 19.9 us -> 19 us  [call(): pl.pallas_call(kernel, in_specs=in_specs, out_specs=[VMEM] * len(out_shap...]
  transfers between devices with their start and end apart: 11 -> 11, of which waited for: 6 -> 6; matrix products, arithmetic and copies ran while one was open for 5% -> 5% of each run, Pallas kernels for 24% -> 18%
where the time goes in v9:
time: 59.9 us; the launch traced here: 59.6 us
  Pallas kernels  23.6 us (39%)
  waiting for transfers between devices  16.4 us (27%)
  starting transfers between devices  14.7 us (25%)
  local copies, waits for them, and re-layouts  3.14 us (5%)
  other arithmetic  1.09 us (2%)
  between operations  0.74 us (1%)
    pallas_call x8, Pallas kernels, call(): pl.pallas_call(kernel, in_specs=in_specs, out_specs=[VMEM] * len(out_shap...  19 us
    ppermute x11, waiting for transfers between devices, swap(): return lax.ppermute(values, axis, [(i, i ^ distance) for i in range(size)])  16.4 us
    ppermute x11, starting transfers between devices, swap(): return lax.ppermute(values, axis, [(i, i ^ distance) for i in range(size)])  14.7 us
    pallas_call x1, Pallas kernels, early_templates(): pl.pallas_call(early_kernel, grid=(count,), in_specs=[pl.BlockSpec((2, ro...  4.57 us
    unnamed x5, local copies, waits for them, and re-layouts  2.4 us
  transfers between devices with their start and end apart: 11, of which 6 were waited for; matrix products, arithmetic and copies ran while one was open for 5% of the time, Pallas kernels for 18%

profile of v9, /device:TPU:0, one launch (start us, length us, event | category | flops | bytes accessed | tf_op | source)
XLA Modules:
  0.0 59.6 jit_solution(2341025238274603688)
XLA Ops:
  0.6 1.8 %weigh.1 = (bf16[32,4736]{1,0:T(8,128)(2,1)S(1)}, bf16[32,2432]{1,0:T(8,128)(2,1)S(1)}, bf16[32,2304]{1,0:T(8,128)(2,1)S(1)}) custom-call(s32[16]{0:T(128)} %ids_hbm.1, bf16[16,2,4608]{2,1,0:T(2,128)(2,1)} %p_hbm.1, f32[64,4608]{1,0:T(8,128)} %ctf_ref.3, f32[4608]{0:T(1024)} %nw_hbm.1), custom_call_target="tpu_custom_call" | custom-call | flops 294912 | bytes 1179648 | tf_op jit(solution)/shard_map/weigh/pallas_call | solution.py:38
  2.5 4.1 %collective-permute-start = (bf16[32,2432]{1,0:T(8,128)(2,1)S(1)}, bf16[32,2432]{1,0:T(8,128)(2,1)S(1)}, u32[]{:S(2)}, u32[]{:S(2)}) collective-permute-start(bf16[32,2432]{1,0:T(8,128)(2,1)S(1)} %get-tuple-element.27), channel_id=1, source_target_pairs={{0,8},{4,12},{8,0},{12,4},{1,9},{5,13},{9,1},{13,5},{2,10},{6,14},... | collective-permute-start | bytes 466952 | tf_op jit(solution)/shard_map/ppermute | solution.py:556
  6.6 0.1 collective-permute-start.1
  6.7 1.8 %collective-permute-start.2 = (bf16[32,4736]{1,0:T(8,128)(2,1)S(1)}, bf16[32,4736]{1,0:T(8,128)(2,1)S(1)}, u32[]{:S(2)}, u32[]{:S(2)}) collective-permute-start(bf16[32,4736]{1,0:T(8,128)(2,1)S(1)} %get-tuple-element.34.refs_0_), channel_id=1, source_target_pairs={{0,4},{4,0},{8,12},{12,8},{1,5},{5,1},{9,13},{13,9},{2,6},{6,2},{1... | collective-permute-start | bytes 909320 | tf_op jit(solution)/shard_map/ppermute | solution.py:556
  8.5 0.7 %broadcast_in_dim.2.nw_ref = f32[1,4608]{1,0:T(1,128)S(1)} reshape(f32[4608]{0:T(1024)} %nw_hbm.1) | data formatting | bytes 36864 | tf_op jit(solution)/shard_map/broadcast_in_dim | solution.py:569
  9.3 1.1 %copy.10 = bf16[32,2,4608]{2,0,1:T(8,128)(2,1)S(1)} copy(bf16[32,2,4608]{2,1,0:T(2,128)(2,1)} %param.7) | data formatting | bytes 1179648 | tf_op args[1]
  10.4 0.8 %convert_bitcast_fusion = (f32[24]{0:T(128)S(1)}, f32[24]{0:T(128)S(1)}) fusion(s32[24,2]{0,1:T(2,128)} %param.11), kind=kLoop, calls=%fused_computation.9 | loop fusion | flops 48 | bytes 384 | tf_op jit(solution)/shard_map/mul | solution.py:33
  11.1 0.1 fusion
  11.3 0.1 fusion.2
  11.4 0.0 copy-start
  11.4 1.3 %copy-done = f32[64,4608]{1,0:T(8,128)S(1)} copy-done((f32[64,4608]{1,0:T(8,128)S(1)}, f32[64,4608]{1,0:T(8,128)}, u32[]{:S(2)}) %copy-start) | copy-done | bytes 1179672
  12.7 1.2 %prepare.1 = (f32[24,4608]{1,0:T(8,128)S(1)}, f32[24,4608]{1,0:T(8,128)S(1)}, f32[32,64]{1,0:T(8,128)S(1)}) custom-call(bf16[2,32,4608]{2,1,0:T(8,128)(2,1)S(1)} %bitcast.10, f32[24,128]{1,0:T(8,128)S(1)} %get-tuple-element.57.xc_ref, f32[24,128]{1,0:T(8,128)S(1)} %get-tuple-element.56.xs_ref, f32[24,36]{1,0:T(8,128)S(1)} %get-tuple-element.53.yc_ref, ...), custom_call_target="tpu_custom_call" | custom-call | flops 226492416 | tf_op jit(solution)/shard_map/prepare/pallas_call | solution.py:38
  13.9 4.6 %early_templates.1.early_hbm = bf16[6,768,768]{2,1,0:T(8,128)(2,1)} custom-call(bf16[2,32,4608]{2,1,0:T(8,128)(2,1)S(1)} %bitcast.11, f32[24,4608]{1,0:T(8,128)S(1)} %get-tuple-element.29.cos_ref, f32[24,4608]{1,0:T(8,128)S(1)} %get-tuple-element.30.sin_ref), custom_call_target="tpu_custom_call" | custom-call | flops 70778880 | bytes 7077888 | tf_op jit(solution)/shard_map/early_templates/pallas_call | solution.py:185
  18.4 1.9 %collective-permute-done.1.refs_4_ = bf16[32,2304]{1,0:T(8,128)(2,1)S(1)} collective-permute-done((bf16[32,2304]{1,0:T(8,128)(2,1)S(1)}, bf16[32,2304]{1,0:T(8,128)(2,1)S(1)}, u32[]{:S(2)}, u32[]{:S(2)}) %collective-permute-start.1) | collective-permute-done | bytes 147488 | tf_op jit(solution)/shard_map/ppermute | solution.py:556
  20.4 0.0 collective-permute-done.refs_2_
  20.4 0.7 %collective-permute-start.3 = (bf16[32,2432]{1,0:T(8,128)(2,1)S(1)}, bf16[32,2432]{1,0:T(8,128)(2,1)S(1)}, u32[]{:S(2)}, u32[]{:S(2)}) collective-permute-start(bf16[32,2432]{1,0:T(8,128)(2,1)S(1)} %collective-permute-done.refs_2_), channel_id=1, source_target_pairs={{0,4},{4,0},{8,12},{12,8},{1,5},{5,1},{9,13},{13,9},{2,6},{6,2},{1... | collective-permute-start | bytes 466952 | tf_op jit(solution)/shard_map/ppermute | solution.py:556
  21.0 1.4 %collective-permute-start.4 = (bf16[32,2304]{1,0:T(8,128)(2,1)S(1)}, bf16[32,2304]{1,0:T(8,128)(2,1)S(1)}, u32[]{:S(2)}, u32[]{:S(2)}) collective-permute-start(bf16[32,2304]{1,0:T(8,128)(2,1)S(1)} %collective-permute-done.1.refs_4_), channel_id=1, source_target_pairs={{0,4},{4,0},{8,12},{12,8},{1,5},{5,1},{9,13},{13,9},{2,6},{6,2},{1... | collective-permute-start | bytes 442376 | tf_op jit(solution)/shard_map/ppermute | solution.py:556
  22.4 3.1 %templates.1.temp_ref = bf16[12,768,768]{2,1,0:T(8,128)(2,1)S(1)} custom-call(bf16[6,768,768]{2,1,0:T(8,128)(2,1)} %early_templates.1.early_hbm, bf16[2,32,4608]{2,1,0:T(8,128)(2,1)S(1)} %bitcast.12, f32[24,4608]{1,0:T(8,128)S(1)} %get-tuple-element.29.cos_ref, f32[24,4608]{1,0:T(8,128)S(1)} %get-tuple-element.30.sin_ref), custom_call_target="tpu_custom_call" | custom-call | flops 70778880 | bytes 7077888 | tf_op jit(solution)/shard_map/templates/pallas_call | solution.py:38
  25.5 0.0 collective-permute-done.2.refs_1_
  25.5 1.6 %collective-permute-done.3.refs_3_ = bf16[32,2432]{1,0:T(8,128)(2,1)S(1)} collective-permute-done((bf16[32,2432]{1,0:T(8,128)(2,1)S(1)}, bf16[32,2432]{1,0:T(8,128)(2,1)S(1)}, u32[]{:S(2)}, u32[]{:S(2)}) %collective-permute-start.3) | collective-permute-done | bytes 155680 | tf_op jit(solution)/shard_map/ppermute | solution.py:556
  27.1 2.0 %score0.1.refs_6_ = f32[768,128]{1,0:T(8,128)S(1)} custom-call(bf16[12,768,768]{2,1,0:T(8,128)(2,1)S(1)} %templates.1.temp_ref, bf16[32,4736]{1,0:T(8,128)(2,1)S(1)} %get-tuple-element.34.refs_0_, bf16[32,4736]{1,0:T(8,128)(2,1)S(1)} %collective-permute-done.2.refs_1_, bf16[32,2432]{1,0:T(8,128)(2,1)S(1)} %collective-permute-done.refs_2_, ...), custom_call_target="tpu_custom_call" | custom-call | flops 1811939328 | tf_op jit(solution)/shard_map/score0/pallas_call | solution.py:38
  29.1 0.0 collective-permute-done.4.refs_5_
  29.1 2.4 %score1.1 = (f32[768,128]{1,0:T(8,128)S(1)}, bf16[128,4608]{1,0:T(8,128)(2,1)S(1)}, f32[128,64]{1,0:T(8,128)S(1)}, f32[8,128]{1,0:T(8,128)S(1)}) custom-call(bf16[12,768,768]{2,1,0:T(8,128)(2,1)S(1)} %templates.1.temp_ref, f32[32,64]{1,0:T(8,128)S(1)} %get-tuple-element.33.pow_ref, bf16[32,4736]{1,0:T(8,128)(2,1)S(1)} %get-tuple-element.34.refs_0_, ...), custom_call_target="tpu_custom_call" | custom-call | flops 1811939328 | tf_op jit(solution)/shard_map/score1/pallas_call | solution.py:38
  31.5 0.0 copy-start.1
  31.5 1.1 %collective-permute-start.5 = (f32[8,128]{1,0:T(8,128)S(1)}, f32[8,128]{1,0:T(8,128)S(1)}, u32[]{:S(2)}, u32[]{:S(2)}) collective-permute-start(f32[8,128]{1,0:T(8,128)S(1)} %get-tuple-element.40.refs_0_), channel_id=1, source_target_pairs={{0,4},{4,0},{8,12},{12,8},{1,5},{5,1},{9,13},{13,9},{2,6},{6,2},{1... | collective-permute-start | bytes 12296 | tf_op jit(solution)/shard_map/ppermute | solution.py:556
  32.6 3.4 %collective-permute-start.6 = (f32[8,128]{1,0:T(8,128)S(1)}, f32[8,128]{1,0:T(8,128)S(1)}, u32[]{:S(2)}, u32[]{:S(2)}) collective-permute-start(f32[8,128]{1,0:T(8,128)S(1)} %get-tuple-element.40.refs_0_), channel_id=1, source_target_pairs={{0,8},{4,12},{8,0},{12,4},{1,9},{5,13},{9,1},{13,5},{2,10},{6,14},... | collective-permute-start | bytes 12296 | tf_op jit(solution)/shard_map/ppermute | solution.py:556
  36.0 0.0 collective-permute-start.7
  36.0 0.1 pad_add_fusion.me_ref
  36.1 0.0 collective-permute-done.5.refs_1_
  36.1 1.5 %collective-permute-done.6.refs_2_ = f32[8,128]{1,0:T(8,128)S(1)} collective-permute-done((f32[8,128]{1,0:T(8,128)S(1)}, f32[8,128]{1,0:T(8,128)S(1)}, u32[]{:S(2)}, u32[]{:S(2)}) %collective-permute-start.6) | collective-permute-done | bytes 4128 | tf_op jit(solution)/shard_map/ppermute | solution.py:556
  37.6 3.8 %collective-permute-done.7.refs_3_ = f32[8,128]{1,0:T(8,128)S(1)} collective-permute-done((f32[8,128]{1,0:T(8,128)S(1)}, f32[8,128]{1,0:T(8,128)S(1)}, u32[]{:S(2)}, u32[]{:S(2)}) %collective-permute-start.7) | collective-permute-done | bytes 4128 | tf_op jit(solution)/shard_map/ppermute | solution.py:556
  41.4 4.8 %outgoing.1 = (f32[1,128]{1,0:T(1,128)S(1)}, bf16[2,768,128]{2,1,0:T(8,128)(2,1)S(1)}, f32[32,64]{1,0:T(8,128)S(1)}, bf16[32,2432]{1,0:T(8,128)(2,1)S(1)}, bf16[...) custom-call(s32[2]{0:T(128)S(1)} %pad_add_fusion.me_ref, f32[768,128]{1,0:T(8,128)S(1)} %get-tuple-element.37.s_ref, ...), custom_call_target="tpu_custom_call" | custom-call | flops 2717908992 | tf_op jit(solution)/shard_map/outgoing/pallas_call | solution.py:38
  46.2 0.0 copy-done.1
  46.2 2.6 %own_slice.1 = (f32[32,2304]{1,0:T(8,128)S(1)}, f32[64,1152]{1,0:T(8,128)S(1)}, f32[32,64]{1,0:T(8,128)}) custom-call(s32[2]{0:T(128)S(1)} %pad_add_fusion.me_ref, f32[768,128]{1,0:T(8,128)S(1)} %get-tuple-element.37.s_ref, f32[1,128]{1,0:T(1,128)S(1)} %get-tuple-element.41.norm_ref, bf16[2,768,128]{2,1,0:T(8,128)(2,1)S(1)} %get-tuple-element.42.rho_ref, ...), custom_call_target="tpu_custom_call" | custom-call | flops 905969664 | tf_op jit(solution)/shard_map/own_slice/pallas_call | solution.py:38
  48.8 0.0 collective-permute-start.10
  48.8 1.6 %collective-permute-start.8 = (bf16[32,2432]{1,0:T(8,128)(2,1)S(1)}, bf16[32,2432]{1,0:T(8,128)(2,1)S(1)}, u32[]{:S(2)}, u32[]{:S(2)}) collective-permute-start(bf16[32,2432]{1,0:T(8,128)(2,1)S(1)} %get-tuple-element.49), channel_id=1, source_target_pairs={{0,3},{1,2},{2,1},{3,0},{4,7},{5,6},{6,5},{7,4},{8,11},{9,10},{10,... | collective-permute-start | bytes 466952 | tf_op jit(solution)/shard_map/ppermute | solution.py:556
  50.4 0.5 collective-permute-start.9
  51.0 0.0 collective-permute-done.10.refs_2_
  51.0 3.8 %collective-permute-done.8.refs_0_ = bf16[32,2432]{1,0:T(8,128)(2,1)S(1)} collective-permute-done((bf16[32,2432]{1,0:T(8,128)(2,1)S(1)}, bf16[32,2432]{1,0:T(8,128)(2,1)S(1)}, u32[]{:S(2)}, u32[]{:S(2)}) %collective-permute-start.8) | collective-permute-done | bytes 155680 | tf_op jit(solution)/shard_map/ppermute | solution.py:556
  54.8 3.7 %collective-permute-done.9.refs_1_ = bf16[32,2432]{1,0:T(8,128)(2,1)S(1)} collective-permute-done((bf16[32,2432]{1,0:T(8,128)(2,1)S(1)}, bf16[32,2432]{1,0:T(8,128)(2,1)S(1)}, u32[]{:S(2)}, u32[]{:S(2)}) %collective-permute-start.9) | collective-permute-done | bytes 155680 | tf_op jit(solution)/shard_map/ppermute | solution.py:556
  58.5 1.1 %finish.1 = f32[32,2,1152]{2,1,0:T(2,128)} custom-call(f32[64,1152]{1,0:T(8,128)S(1)} %get-tuple-element.44.cw_ref, f32[32,64]{1,0:T(8,128)S(1)} %get-tuple-element.45.mass_ref, f32[32,2304]{1,0:T(8,128)S(1)} %get-tuple-element.48.own_ref, bf16[32,2432]{1,0:T(8,128)(2,1)S(1)} %collective-permute-done.8.refs_0_, ...), custom_call_target="tpu_custom_call" | custom-call | tf_op jit(solution)/shard_map/finish/pallas_call | solution.py:38
  (2 shorter events, 0.0 us)
Async XLA Ops:
  2.5 17.9 %collective-permute-start = (bf16[32,2432]{1,0:T(8,128)(2,1)S(1)}, bf16[32,2432]{1,0:T(8,128)(2,1)S(1)}, u32[]{:S(2)}, u32[]{:S(2)}) collective-permute-start(bf16[32,2432]{1,0:T(8,128)(2,1)S(1)} %get-tuple-element.27), channel_id=1, source_target_pairs={{0,8},{4,12},{8,0},{12,4},{1,9},{5,13},{9,1},{13,5},{2,10},{6,14},... | collective-permute-start | bytes 466952 | tf_op jit(solution)/shard_map/ppermute | solution.py:556
  6.6 13.8 %collective-permute-start.1 = (bf16[32,2304]{1,0:T(8,128)(2,1)S(1)}, bf16[32,2304]{1,0:T(8,128)(2,1)S(1)}, u32[]{:S(2)}, u32[]{:S(2)}) collective-permute-start(bf16[32,2304]{1,0:T(8,128)(2,1)S(1)} %get-tuple-element.28), channel_id=1, source_target_pairs={{0,8},{4,12},{8,0},{12,4},{1,9},{5,13},{9,1},{13,5},{2,10},{6,14},... | collective-permute-start | bytes 442376 | tf_op jit(solution)/shard_map/ppermute | solution.py:556
  6.7 18.8 %collective-permute-start.2 = (bf16[32,4736]{1,0:T(8,128)(2,1)S(1)}, bf16[32,4736]{1,0:T(8,128)(2,1)S(1)}, u32[]{:S(2)}, u32[]{:S(2)}) collective-permute-start(bf16[32,4736]{1,0:T(8,128)(2,1)S(1)} %get-tuple-element.34.refs_0_), channel_id=1, source_target_pairs={{0,4},{4,0},{8,12},{12,8},{1,5},{5,1},{9,13},{13,9},{2,6},{6,2},{1... | collective-permute-start | bytes 909320 | tf_op jit(solution)/shard_map/ppermute | solution.py:556
  11.4 1.3 %copy-start = (f32[64,4608]{1,0:T(8,128)S(1)}, f32[64,4608]{1,0:T(8,128)}, u32[]{:S(2)}) copy-start(f32[64,4608]{1,0:T(8,128)} %ctf_ref.3) | copy-start | bytes 3538948
  20.4 6.7 %collective-permute-start.3 = (bf16[32,2432]{1,0:T(8,128)(2,1)S(1)}, bf16[32,2432]{1,0:T(8,128)(2,1)S(1)}, u32[]{:S(2)}, u32[]{:S(2)}) collective-permute-start(bf16[32,2432]{1,0:T(8,128)(2,1)S(1)} %collective-permute-done.refs_2_), channel_id=1, source_target_pairs={{0,4},{4,0},{8,12},{12,8},{1,5},{5,1},{9,13},{13,9},{2,6},{6,2},{1... | collective-permute-start | bytes 466952 | tf_op jit(solution)/shard_map/ppermute | solution.py:556
  21.0 8.1 %collective-permute-start.4 = (bf16[32,2304]{1,0:T(8,128)(2,1)S(1)}, bf16[32,2304]{1,0:T(8,128)(2,1)S(1)}, u32[]{:S(2)}, u32[]{:S(2)}) collective-permute-start(bf16[32,2304]{1,0:T(8,128)(2,1)S(1)} %collective-permute-done.1.refs_4_), channel_id=1, source_target_pairs={{0,4},{4,0},{8,12},{12,8},{1,5},{5,1},{9,13},{13,9},{2,6},{6,2},{1... | collective-permute-start | bytes 442376 | tf_op jit(solution)/shard_map/ppermute | solution.py:556
  31.5 14.7 %copy-start.1 = (f32[64,4608]{1,0:T(8,128)S(1)}, f32[64,4608]{1,0:T(8,128)}, u32[]{:S(2)}) copy-start(f32[64,4608]{1,0:T(8,128)} %ctf_ref.3) | copy-start | bytes 3538948
  31.5 4.6 %collective-permute-start.5 = (f32[8,128]{1,0:T(8,128)S(1)}, f32[8,128]{1,0:T(8,128)S(1)}, u32[]{:S(2)}, u32[]{:S(2)}) collective-permute-start(f32[8,128]{1,0:T(8,128)S(1)} %get-tuple-element.40.refs_0_), channel_id=1, source_target_pairs={{0,4},{4,0},{8,12},{12,8},{1,5},{5,1},{9,13},{13,9},{2,6},{6,2},{1... | collective-permute-start | bytes 12296 | tf_op jit(solution)/shard_map/ppermute | solution.py:556
  32.6 5.0 %collective-permute-start.6 = (f32[8,128]{1,0:T(8,128)S(1)}, f32[8,128]{1,0:T(8,128)S(1)}, u32[]{:S(2)}, u32[]{:S(2)}) collective-permute-start(f32[8,128]{1,0:T(8,128)S(1)} %get-tuple-element.40.refs_0_), channel_id=1, source_target_pairs={{0,8},{4,12},{8,0},{12,4},{1,9},{5,13},{9,1},{13,5},{2,10},{6,14},... | collective-permute-start | bytes 12296 | tf_op jit(solution)/shard_map/ppermute | solution.py:556
  36.0 5.4 %collective-permute-start.7 = (f32[8,128]{1,0:T(8,128)S(1)}, f32[8,128]{1,0:T(8,128)S(1)}, u32[]{:S(2)}, u32[]{:S(2)}) collective-permute-start(f32[8,128]{1,0:T(8,128)S(1)} %get-tuple-element.40.refs_0_), channel_id=1, source_target_pairs={{0,12},{4,8},{8,4},{12,0},{1,13},{5,9},{9,5},{13,1},{2,14},{6,10},... | collective-permute-start | bytes 12296 | tf_op jit(solution)/shard_map/ppermute | solution.py:556
  48.8 2.1 %collective-permute-start.10 = (bf16[32,2432]{1,0:T(8,128)(2,1)S(1)}, bf16[32,2432]{1,0:T(8,128)(2,1)S(1)}, u32[]{:S(2)}, u32[]{:S(2)}) collective-permute-start(bf16[32,2432]{1,0:T(8,128)(2,1)S(1)} %get-tuple-element.51), channel_id=1, source_target_pairs={{0,1},{1,0},{2,3},{3,2},{4,5},{5,4},{6,7},{7,6},{8,9},{9,8},{10,11... | collective-permute-start | bytes 466952 | tf_op jit(solution)/shard_map/ppermute | solution.py:556
  48.8 6.0 %collective-permute-start.8 = (bf16[32,2432]{1,0:T(8,128)(2,1)S(1)}, bf16[32,2432]{1,0:T(8,128)(2,1)S(1)}, u32[]{:S(2)}, u32[]{:S(2)}) collective-permute-start(bf16[32,2432]{1,0:T(8,128)(2,1)S(1)} %get-tuple-element.49), channel_id=1, source_target_pairs={{0,3},{1,2},{2,1},{3,0},{4,7},{5,6},{6,5},{7,4},{8,11},{9,10},{10,... | collective-permute-start | bytes 466952 | tf_op jit(solution)/shard_map/ppermute | solution.py:556
  50.4 8.1 %collective-permute-start.9 = (bf16[32,2432]{1,0:T(8,128)(2,1)S(1)}, bf16[32,2432]{1,0:T(8,128)(2,1)S(1)}, u32[]{:S(2)}, u32[]{:S(2)}) collective-permute-start(bf16[32,2432]{1,0:T(8,128)(2,1)S(1)} %get-tuple-element.50), channel_id=1, source_target_pairs={{0,2},{1,3},{2,0},{3,1},{4,6},{5,7},{6,4},{7,5},{8,10},{9,11},{10,... | collective-permute-start | bytes 466952 | tf_op jit(solution)/shard_map/ppermute | solution.py:556

commit v10 on v9

v10 whole, which is shorter than its diff:
```python
import functools

import jax
import jax.numpy as jnp
from jax import lax
from jax.experimental import pallas as pl
from jax.experimental.pallas import tpu as pltpu
from jax.sharding import PartitionSpec as P

BOX = 128
LANES = 128
VMEM_LIMIT = 24 * 1024 * 1024

prior_precision = 0.02

NT = (((1,), (1,)), ((), ()))
NN = (((1,), (0,)), ((), ()))
HIGHEST = lax.Precision.HIGHEST
f32 = jnp.float32
bf16 = jnp.bfloat16

SMEM = pl.BlockSpec(memory_space=pltpu.SMEM)
VMEM = pl.BlockSpec(memory_space=pltpu.VMEM)
ANY = pl.BlockSpec(memory_space=pl.ANY)


def phase_tables(shifts, freq):
    along_x = (jnp.arange(BOX) - BOX // 2).astype(f32)
    along_y = jnp.arange(freq // BOX).astype(f32)
    step = 2.0 * jnp.pi / BOX
    angle_x = step * (shifts[:, 0:1].astype(f32) * along_x[None, :])
    angle_y = step * (shifts[:, 1:2].astype(f32) * along_y[None, :])
    return (jnp.cos(angle_x), jnp.sin(angle_x), jnp.cos(angle_y), jnp.sin(angle_y))


def call(kernel, name, in_specs, out_shape, operands, scratch=(), flops=0, moved=0, limit=VMEM_LIMIT):
    return pl.pallas_call(
        kernel,
        in_specs=in_specs,
        out_specs=[VMEM] * len(out_shape),
        out_shape=out_shape,
        scratch_shapes=list(scratch),
        compiler_params=pltpu.CompilerParams(vmem_limit_bytes=limit),
        cost_estimate=pl.CostEstimate(flops=flops, bytes_accessed=moved, transcendentals=0),
        name=name,
    )(*operands)


def real_index(shape, axis, half):
    return lax.rem(lax.broadcasted_iota(jnp.int32, shape, axis) // half, 2) == 0


def weigh_kernel(
    ids_hbm, p_hbm, ctf_hbm, nw_hbm, out_ref, ids_ref, p_ref, ctf_ref, nw_ref, scale_ref, sem
):
    count, _, freq = p_ref.shape
    copies = [
        pltpu.make_async_copy(source, target, sem.at[i])
        for i, (source, target) in enumerate(
            [(ids_hbm, ids_ref), (ctf_hbm, ctf_ref), (nw_hbm, nw_ref), (p_hbm, p_ref)]
        )
    ]
    for copy in copies:
        copy.start()
    copies[0].wait()
    row = lax.rem(lax.broadcasted_iota(jnp.int32, (2 * count, LANES), 0), count)
    ids = jnp.zeros((2 * count, LANES), f32)
    for n in range(count):
        ids = jnp.where(row == n, ids_ref[n].astype(f32), ids)
    for copy in copies[1:]:
        copy.wait()
    noise = nw_ref[...].reshape(1, freq)
    for n in range(count):
        scale_ref[n : n + 1, :] = ctf_ref[pl.ds(ids_ref[n], 1), :] * noise
    scale = scale_ref[...]
    values = p_ref[...].astype(f32)
    out_ref[:count, :freq] = (values[:, 0, :] * scale).astype(bf16)
    out_ref[count:, :freq] = (values[:, 1, :] * scale).astype(bf16)
    out_ref[:, freq:] = ids.astype(bf16)


def weigh(particles, ctf, noise_weight, group_ids):
    rows, _, freq = particles.shape
    operands = (group_ids, particles, ctf, noise_weight)
    return call(
        weigh_kernel,
        "weigh",
        [ANY] * 4,
        [jax.ShapeDtypeStruct((2 * rows, freq + LANES), bf16)],
        [pltpu.with_memory_space_constraint(x, pltpu.HBM) for x in operands],
        [
            pltpu.SMEM((rows,), jnp.int32),
            pltpu.VMEM(particles.shape, bf16),
            pltpu.VMEM(ctf.shape, f32),
            pltpu.VMEM((freq,), f32),
            pltpu.VMEM((rows, freq), f32),
            pltpu.SemaphoreType.DMA((4,)),
        ],
        flops=4 * rows * freq,
        moved=16 * rows * freq,
    )[0]


def prepare_kernel(
    cls_ref, xc_ref, xs_ref, yc_ref, ys_ref, ctf_ref, nw_ref, cos_ref, sin_ref, pow_ref
):
    freq = cls_ref.shape[2]
    x_cos, x_sin = xc_ref[...], xs_ref[...]
    for t in range(freq // BOX):
        y_cos = jnp.broadcast_to(yc_ref[:, t : t + 1], x_cos.shape)
        y_sin = jnp.broadcast_to(ys_ref[:, t : t + 1], x_cos.shape)
        cos_ref[:, t * BOX : (t + 1) * BOX] = x_cos * y_cos - x_sin * y_sin
        sin_ref[:, t * BOX : (t + 1) * BOX] = x_sin * y_cos + x_cos * y_sin
    cut = freq // 4
    power = jnp.zeros(pow_ref.shape, f32)
    for q in range(4):
        at = slice(q * cut, (q + 1) * cut)
        re = cls_ref[0, :, at].astype(f32)
        im = cls_ref[1, :, at].astype(f32)
        ctf = ctf_ref[:, at]
        power += lax.dot_general(
            re * re + im * im,
            ctf * ctf * nw_ref[:, at],
            NT,
            precision=HIGHEST,
            preferred_element_type=f32,
        )
    pow_ref[...] = power


def prepare(split, tables, ctf, noise_weight):
    _, rows, freq = split.shape
    poses, groups = tables[0].shape[0], ctf.shape[0]
    return call(
        prepare_kernel,
        "prepare",
        [VMEM] * 7,
        [
            jax.ShapeDtypeStruct((poses, freq), f32),
            jax.ShapeDtypeStruct((poses, freq), f32),
            jax.ShapeDtypeStruct((rows, groups), f32),
        ],
        (split, *tables, ctf, noise_weight),
        flops=24 * rows * groups * freq,
    )


def write_templates(cls_ref, cos_ref, sin_ref, temp_ref, start, tile):
    rows = cls_ref.shape[1]
    for a in range(0, tile, LANES):
        at = pl.ds(pl.multiple_of(start + a, LANES), LANES)
        re = cls_ref[0, :, at].astype(f32)
        im = cls_ref[1, :, at].astype(f32)
        for r in range(cos_ref.shape[0]):
            cos_r = cos_ref[r : r + 1, at]
            sin_r = sin_ref[r : r + 1, at]
            here = slice(r * rows, (r + 1) * rows)
            temp_ref[here, a : a + LANES] = (re * cos_r - im * sin_r).astype(bf16)
            temp_ref[here, tile + a : tile + a + LANES] = (re * sin_r + im * cos_r).astype(bf16)


def template_tile(freq):
    return max(t for t in range(LANES, 385, LANES) if freq % t == 0)


def early_kernel(cls_ref, cos_ref, sin_ref, temp_ref):
    write_templates(cls_ref, cos_ref, sin_ref, temp_ref, 0, cls_ref.shape[2])


def early_templates(split, cos_t, sin_t):
    _, rows, freq = split.shape
    poses = cos_t.shape[0]
    tile = template_tile(freq)
    count = freq // tile // 2
    skip = freq // tile - count
    return pl.pallas_call(
        early_kernel,
        grid=(count,),
        in_specs=[
            pl.BlockSpec((2, rows, tile), lambda j: (0, 0, skip + j)),
            pl.BlockSpec((poses, tile), lambda j: (0, skip + j)),
            pl.BlockSpec((poses, tile), lambda j: (0, skip + j)),
        ],
        out_specs=pl.BlockSpec((None, poses * rows, 2 * tile), lambda j: (j, 0, 0)),
        out_shape=pltpu.HBM((count, poses * rows, 2 * tile), bf16),
        compiler_params=pltpu.CompilerParams(vmem_limit_bytes=VMEM_LIMIT),
        cost_estimate=pl.CostEstimate(
            flops=20 * poses * rows * freq, bytes_accessed=2 * poses * rows * freq, transcendentals=0
        ),
        name="early_templates",
    )(split, cos_t, sin_t)


def template_kernel(early_hbm, cls_ref, cos_ref, sin_ref, temp_ref, sem):
    count = early_hbm.shape[0]
    built = temp_ref.shape[0] - count
    tile = temp_ref.shape[2] // 2
    copies = [
        pltpu.make_async_copy(early_hbm.at[t], temp_ref.at[built + t], sem.at[t])
        for t in range(count)
    ]
    for copy in copies:
        copy.start()

    @pl.loop(0, built)
    def _(t):
        write_templates(cls_ref, cos_ref, sin_ref, temp_ref.at[t], t * tile, tile)

    for copy in copies:
        copy.wait()


def all_templates(early, split, cos_t, sin_t):
    _, rows, freq = split.shape
    poses = cos_t.shape[0]
    count, columns, width = early.shape
    return call(
        template_kernel,
        "templates",
        [ANY] + [VMEM] * 3,
        [pltpu.VMEM((freq // (width // 2), columns, width), bf16)],
        (pltpu.with_memory_space_constraint(early, pltpu.HBM), split, cos_t, sin_t),
        [pltpu.SemaphoreType.DMA((count,))],
        flops=20 * poses * rows * freq,
        moved=2 * poses * rows * freq,
    )[0]


def score_kernel(half, temp_ref, pow_ref, *refs):
    shards, (s_ref, marks_ref, stat_ref) = refs[:-3], refs[-3:]
    rows, groups = pow_ref.shape
    lanes = s_ref.shape[1]
    poses = s_ref.shape[0] // rows
    count = temp_ref.shape[0]
    tile = temp_ref.shape[2] // 2
    ids = jnp.concatenate([ref[:, count * tile :] for ref in shards], axis=0).astype(f32)
    group = lax.broadcasted_iota(jnp.int32, (lanes, groups), 1).astype(f32)
    marks = (ids[:, :groups] == group).astype(f32)
    marks_ref[...] = marks
    penalty = lax.dot_general(
        pow_ref[...], marks, NT, precision=HIGHEST, preferred_element_type=f32
    )
    s_ref[...] = jnp.zeros_like(s_ref)
    real = real_index((lanes, tile), 0, half)
    for t in range(count):
        at = slice(t * tile, (t + 1) * tile)
        wide = jnp.concatenate([ref[:, at] for ref in shards], axis=0).astype(f32)
        split = jnp.concatenate(
            [jnp.where(real, wide, 0.0).astype(bf16), jnp.where(real, 0.0, wide).astype(bf16)],
            axis=1,
        )
        s_ref[...] += lax.dot_general(temp_ref[t], split, NT, preferred_element_type=f32)
    acc = s_ref[...]
    acc = acc + jnp.where(
        real_index(acc.shape, 1, half), pltpu.roll(acc, lanes - half, 1), pltpu.roll(acc, half, 1)
    )
    scores = acc.reshape(poses, rows, lanes) - 0.5 * penalty[None]
    peak = jnp.max(jnp.max(scores, axis=0), axis=0, keepdims=True)
    total = jnp.sum(jnp.sum(jnp.exp(scores - peak[None]), axis=0), axis=0, keepdims=True)
    s_ref[...] = scores.reshape(poses * rows, lanes)
    stat_ref[0:1, :] = peak
    stat_ref[1:2, :] = total
    stat_ref[2:8, :] = jnp.zeros((6, lanes), f32)


def score(temps, power, shards, half):
    count, columns, width = temps.shape
    lanes = sum(p.shape[0] for p in shards)
    operands = [temps, power, *shards]
    return call(
        functools.partial(score_kernel, half),
        "score",
        [VMEM] * len(operands),
        [
            jax.ShapeDtypeStruct((columns, lanes), f32),
            jax.ShapeDtypeStruct((lanes, power.shape[1]), f32),
            jax.ShapeDtypeStruct((8, lanes), f32),
        ],
        operands,
        flops=2 * columns * 256 * count * width,
    )


def slices_kernel(targets, me_ref, *refs):
    shards, out_refs = refs[: -len(targets)], refs[-len(targets) :]
    span = out_refs[0].shape[1]
    at = 0
    for ref in shards:
        for out_ref, distance in zip(out_refs, targets):
            base = pl.multiple_of((me_ref[0] ^ distance) * span, LANES)
            out_ref[at : at + ref.shape[0], :] = ref[:, pl.ds(base, span)]
        at += ref.shape[0]


def cut_slices(me, shards, targets, span):
    height = sum(ref.shape[0] for ref in shards)
    return call(
        functools.partial(slices_kernel, targets),
        "cut_slices",
        [SMEM] + [VMEM] * len(shards),
        [jax.ShapeDtypeStruct((height, span), bf16)] * len(targets),
        (me, *shards),
        moved=4 * height * span * len(targets),
        limit=VMEM_LIMIT if height <= 128 else 2 * VMEM_LIMIT,
    )


def bundle_kernel(*refs):
    sources, out_ref = refs[:-1], refs[-1]
    rows = sources[0].shape[0] // 2
    for i, ref in enumerate(sources):
        out_ref[i * rows : (i + 1) * rows, :] = ref[rows:, :]


def bundle(slices):
    rows, span = slices[0].shape
    return call(
        bundle_kernel,
        "bundle",
        [VMEM] * len(slices),
        [jax.ShapeDtypeStruct((len(slices) * rows // 2, span), bf16)],
        slices,
        moved=2 * len(slices) * rows * span,
    )[0]


def xor_blocks(values, block, distance):
    lanes = values.shape[1]
    lane = lax.broadcasted_iota(jnp.int32, values.shape, 1)
    width = block
    while distance:
        if distance % 2:
            low = lax.rem(lane // width, 2) == 0
            values = jnp.where(
                low, pltpu.roll(values, lanes - width, 1), pltpu.roll(values, width, 1)
            )
        distance //= 2
        width *= 2
    return values


def rho_kernel(poses, half, paired, s_ref, marks_ref, *refs):
    stat_refs, (norm_ref, out_ref) = refs[: len(paired)], refs[len(paired) :]
    lanes = s_ref.shape[1]
    rows = s_ref.shape[0] // poses
    groups = marks_ref.shape[1]
    block = 2 * half
    peaks, totals = [], []
    for ref, distance in zip(stat_refs, paired):
        for at in range(0, ref.shape[0], 8):
            stats = xor_blocks(ref[at : at + 8, :], block, distance)
            peaks.append(stats[0:1])
            totals.append(stats[1:2])
    peak = functools.reduce(jnp.maximum, peaks)
    total = sum(t * jnp.exp(p - peak) for t, p in zip(totals, peaks))
    log_norm = peak + jnp.log(total)
    norm_ref[...] = log_norm
    rho = jnp.exp(s_ref[...].reshape(poses, rows, lanes) - log_norm[None])
    mass = lax.dot_general(
        jnp.where(real_index((rows, lanes), 1, half), jnp.sum(rho, axis=0), 0.0),
        marks_ref[...],
        NN,
        precision=HIGHEST,
        preferred_element_type=f32,
    )
    high = mass.astype(bf16)
    low = (mass - high.astype(f32)).astype(bf16)
    rho_low = rho.reshape(poses * rows, lanes).astype(bf16)
    cut = poses // 2 * rows
    lane = lax.broadcasted_iota(jnp.int32, (lanes, lanes), 0)
    column = lax.broadcasted_iota(jnp.int32, (lanes, lanes), 1)
    particle = lane // block * half + lax.rem(lane, block)
    real = lax.rem(lane, block) < half
    first = (real & (column == particle)).astype(f32).astype(bf16)
    second = (real & (column == particle + lanes // 2)).astype(f32).astype(bf16)
    packed = jnp.dot(rho_low[:cut], first, preferred_element_type=f32)
    packed += jnp.dot(rho_low[cut:], second, preferred_element_type=f32)
    out_ref[:cut, :] = packed.astype(bf16)
    if lanes > 2 * groups:
        out_ref[cut:, :] = jnp.zeros((rows, lanes), bf16)
    out_ref[cut:, :groups] = high
    out_ref[cut:, groups : 2 * groups] = low


def responsibilities(scores, marks, stats, paired, poses, half):
    columns, lanes = scores.shape
    return call(
        functools.partial(rho_kernel, poses, half, paired),
        "responsibilities",
        [VMEM] * (2 + len(stats)),
        [
            jax.ShapeDtypeStruct((1, lanes), f32),
            jax.ShapeDtypeStruct((columns // 2 + columns // poses, lanes), bf16),
        ],
        (scores, marks, *stats),
        flops=40 * columns * lanes,
    )


def gather_kernel(poses, half, sources, bundled, me_ref, s_ref, norm_ref, ctf_ref, nw_ref, *refs):
    w_refs, (resp_ref, cw_ref, rows_ref) = refs[:-3], refs[-3:]
    last, w_refs = w_refs[: 2 * bundled], w_refs[2 * bundled :]
    span = rows_ref.shape[2]
    block = 2 * half
    here = pl.ds(pl.multiple_of(me_ref[0] * span, LANES), span)
    at = 0

    def put(real, imag):
        rows_ref[0, at : at + half, :] = real
        rows_ref[1, at : at + half, :] = imag
        return at + half

    for i in range(sources):
        for ref in w_refs[i::sources]:
            for start in range(0, ref.shape[0], block):
                at = put(ref[start : start + half, :], ref[start + half : start + block, :])
        if bundled and i == 0:
            at = put(last[0][:half, here], last[0][half:, here])
        elif bundled:
            start = (i - 1) * block
            at = put(last[1][start : start + half, :], last[1][start + half : start + block, :])
    ctf = ctf_ref[:, here]
    cw_ref[...] = ctf * ctf * nw_ref[:, here]
    rows = resp_ref.shape[0]
    lanes = s_ref.shape[1]
    scores = s_ref[...].reshape(poses, rows, lanes)
    pose_peak = jnp.max(scores, axis=0)
    total = jnp.sum(jnp.exp(scores - pose_peak[None]), axis=0)
    log_resp = pose_peak + jnp.log(total) - norm_ref[...]
    shape = (resp_ref.shape[1], lanes)
    lane = lax.broadcasted_iota(jnp.int32, shape, 1)
    row = ((lane // block) ^ me_ref[1]) * half + lax.rem(lane, block)
    take = (lax.broadcasted_iota(jnp.int32, shape, 0) == row) & (lax.rem(lane, block) < half)
    resp_ref[...] = lax.dot_general(
        log_resp, take.astype(f32), NT, precision=HIGHEST, preferred_element_type=f32
    )


def gather_rows(me, scores, norm, ctf, noise_weight, slices, last, sources, poses, half, span):
    columns, lanes = scores.shape
    particles = sources * lanes // 2
    return call(
        functools.partial(gather_kernel, poses, half, sources, len(last) // 2),
        "gather_rows",
        [SMEM] + [VMEM] * (4 + len(last) + len(slices)),
        [
            jax.ShapeDtypeStruct((columns // poses, lanes // 2), f32),
            jax.ShapeDtypeStruct((ctf.shape[0], span), f32),
            jax.ShapeDtypeStruct((2, particles, span), bf16),
        ],
        (me, scores, norm, ctf, noise_weight, *last, *slices),
        flops=40 * columns * lanes,
        moved=8 * particles * span,
        limit=VMEM_LIMIT if particles <= 512 else 2 * VMEM_LIMIT,
    )


def finish_kernel(poses, groups, sources, me_ref, cw_ref, cos_ref, sin_ref, rows_ref, *refs):
    payloads, (out_ref, rho_ref, denom_ref, *buffers) = refs[:sources], refs[sources:]
    rows, _, span = out_ref.shape
    cut = poses // 2 * rows
    count = payloads[0].shape[1] // 2
    mass = jnp.zeros((rows, groups), f32)
    for i, ref in enumerate(payloads):
        rho_ref[:cut, i * count : (i + 1) * count] = ref[:cut, :count]
        rho_ref[cut:, i * count : (i + 1) * count] = ref[:cut, count:]
        mass += ref[cut:, :groups].astype(f32) + ref[cut:, groups : 2 * groups].astype(f32)
    denom_ref[...] = (
        lax.dot_general(mass, cw_ref[...], NN, precision=HIGHEST, preferred_element_type=f32)
        + prior_precision
    )
    tiles = [(a, min(256, span - a)) for a in range(0, span, 256)]

    def products(i):
        start, width = tiles[i]
        for part in range(2):
            buffers[i % 2][part, :, :width] = jnp.dot(
                rho_ref[...],
                rows_ref[part, :, start : start + width],
                preferred_element_type=f32,
            )

    def rotate(i):
        start, width = tiles[i]
        buffer = buffers[i % 2]
        for a in range(0, width, LANES):
            at = pl.ds(pl.multiple_of(me_ref[0] * span + start + a, LANES), LANES)
            numer_re = jnp.zeros((rows, LANES), f32)
            numer_im = jnp.zeros((rows, LANES), f32)
            for r in range(poses):
                cos_r = cos_ref[r : r + 1, at]
                sin_r = sin_ref[r : r + 1, at]
                s_re = buffer[0, r * rows : (r + 1) * rows, a : a + LANES]
                s_im = buffer[1, r * rows : (r + 1) * rows, a : a + LANES]
                numer_re = numer_re + s_re * cos_r + s_im * sin_r
                numer_im = numer_im + s_im * cos_r - s_re * sin_r
            here = slice(start + a, start + a + LANES)
            denom = denom_ref[:, here]
            out_ref[:, 0, here] = numer_re / denom
            out_ref[:, 1, here] = numer_im / denom

    products(0)
    for i in range(1, len(tiles)):
        products(i)
        rotate(i - 1)
    rotate(len(tiles) - 1)


def finish(me, weight, cos_t, sin_t, rows, payloads, cls_rows):
    poses = cos_t.shape[0]
    _, particles, span = rows.shape
    return call(
        functools.partial(finish_kernel, poses, weight.shape[0], len(payloads)),
        "finish",
        [SMEM] + [VMEM] * (4 + len(payloads)),
        [jax.ShapeDtypeStruct((cls_rows, 2, span), f32)],
        (me, weight, cos_t, sin_t, rows, *payloads),
        [
            pltpu.VMEM((poses * cls_rows, particles), bf16),
            pltpu.VMEM((cls_rows, span), f32),
            pltpu.VMEM((2, poses * cls_rows, 256), f32),
            pltpu.VMEM((2, poses * cls_rows, 256), f32),
        ],
        flops=4 * poses * cls_rows * particles * span,
        limit=VMEM_LIMIT if particles <= 512 else 2 * VMEM_LIMIT,
    )[0]


def swap(values, axis, distance):
    size = lax.axis_size(axis)
    return lax.ppermute(values, axis, [(i, i ^ distance) for i in range(size)])


def local(particles, classes, ctf, noise_weight, group_ids, shifts):
    half, _, freq = particles.shape
    cls_rows = classes.shape[0]
    poses = shifts.shape[0]
    n_cls = lax.axis_size("cls")
    n_img = lax.axis_size("img")
    span = freq // n_img
    pairwise = n_cls == 4
    me_cls = lax.axis_index("cls") if pairwise else 0
    me = jnp.stack([lax.axis_index("img"), me_cls]).astype(jnp.int32)
    others = tuple(range(n_img - 1, 0, -1))
    targets = (0,) + others

    def share(*shards):
        mine, *outgoing = cut_slices(me, shards, targets, span)
        return [mine] + [swap(w, "img", d) for w, d in zip(outgoing, others)]

    own = weigh(particles, ctf, noise_weight, group_ids)
    noise_weight = noise_weight[None, :]
    if pairwise:
        far, near = swap(own, "cls", 2), swap(own, "cls", 1)
        slices = share(own)
    else:
        shards = [lax.all_gather(own, "cls", axis=0, tiled=True)]
        slices = share(*shards)

    split = jnp.transpose(classes, (1, 0, 2))
    cos_t, sin_t, power = prepare(split, phase_tables(shifts, freq), ctf, noise_weight)
    early = early_templates(split, cos_t, sin_t)
    if pairwise:
        far, split, early, slices = lax.optimization_barrier((far, split, early, slices))
        third = swap(far, "cls", 1)
        slices += share(near, far)
        shards = [own, near, far, third]
    temps = all_templates(early, split, cos_t, sin_t)
    scores, marks, stat = score(temps, power, shards, half)
    if pairwise:
        stat, slices = lax.optimization_barrier((stat, slices))
        stats = [stat] + [swap(stat, "cls", k) for k in range(1, n_cls)]
        paired = tuple(range(n_cls))
        last = [third, swap(bundle(slices[-len(others) :]), "cls", 1)]
    else:
        stats = [lax.all_gather(stat, "cls", axis=0, tiled=True)]
        paired = (0,)
        last = []
    norm, payload = responsibilities(scores, marks, stats, paired, poses, half)
    payloads = [payload] + [swap(payload, "img", d) for d in others]
    log_resp, weight, rows = gather_rows(
        me, scores, norm, ctf, noise_weight, slices, last, n_img, poses, half, span
    )
    averages = finish(me, weight, cos_t, sin_t, rows, payloads, cls_rows)
    return (log_resp.T, averages)


def solution(mesh):
    placed = (
        P(("groups", "img", "cls"), None, None),
        P(("groups", "cls"), None, None),
        P("groups", None),
        P("groups"),
        P(("groups", "img", "cls")),
        P("groups", None),
    )
    return jax.shard_map(
        local,
        mesh=mesh,
        in_specs=placed,
        out_specs=(P(("groups", "img"), "cls"), P(("groups", "cls"), None, "img")),
        check_vma=False,
    )
```

time: 59.9 us -> 54.5 us (0.910)
  waiting for transfers between devices: 16.4 us -> 11.9 us
  Pallas kernels: 23.6 us -> 21 us
  starting transfers between devices: 14.7 us -> 16.4 us
    ppermute x11 -> x16, waiting for transfers between devices: 16.4 us -> 11.9 us  [swap(): return lax.ppermute(values, axis, [(i, i ^ distance) for i in range(size)])]
    pallas_call x8 -> x10, Pallas kernels: 19 us -> 16.4 us  [call(): pl.pallas_call(kernel, in_specs=in_specs, out_specs=[VMEM] * len(out_shap...]
    ppermute x11 -> x16, starting transfers between devices: 14.7 us -> 16.4 us  [swap(): return lax.ppermute(values, axis, [(i, i ^ distance) for i in range(size)])]
  transfers between devices with their start and end apart: 11 -> 16, of which waited for: 6 -> 5; matrix products, arithmetic and copies ran while one was open for 5% -> 5% of each run, Pallas kernels for 18% -> 30%
where the time goes in v10:
time: 54.5 us; the launch traced here: 54.2 us
  Pallas kernels  21 us (39%)
  starting transfers between devices  16.4 us (30%)
  waiting for transfers between devices  11.9 us (22%)
  local copies, waits for them, and re-layouts  3.14 us (6%)
  other arithmetic  1.09 us (2%)
  between operations  0.76 us (1%)
    pallas_call x10, Pallas kernels, call(): pl.pallas_call(kernel, in_specs=in_specs, out_specs=[VMEM] * len(out_shap...  16.4 us
    ppermute x16, starting transfers between devices, swap(): return lax.ppermute(values, axis, [(i, i ^ distance) for i in range(size)])  16.4 us
    ppermute x16, waiting for transfers between devices, swap(): return lax.ppermute(values, axis, [(i, i ^ distance) for i in range(size)])  11.9 us
    pallas_call x1, Pallas kernels, early_templates(): pl.pallas_call(early_kernel, grid=(count,), in_specs=[pl.BlockSpec((2, ro...  4.54 us
    unnamed x5, local copies, waits for them, and re-layouts  2.4 us
  transfers between devices with their start and end apart: 16, of which 5 were waited for; matrix products, arithmetic and copies ran while one was open for 5% of the time, Pallas kernels for 30%

profile of v10, /device:TPU:0, one launch (start us, length us, event | category | flops | bytes accessed | tf_op | source)
XLA Modules:
  0.0 54.2 jit_solution(417562678445900883)
XLA Ops:
  0.6 1.7 %weigh.1.refs_0_ = bf16[32,4736]{1,0:T(8,128)(2,1)S(1)} custom-call(s32[16]{0:T(128)} %ids_hbm.1, bf16[16,2,4608]{2,1,0:T(2,128)(2,1)} %p_hbm.1, f32[64,4608]{1,0:T(8,128)} %ctf_ref.3, f32[4608]{0:T(1024)} %nw_hbm.1), custom_call_target="tpu_custom_call" | custom-call | flops 294912 | bytes 1179648 | tf_op jit(solution)/shard_map/weigh/pallas_call | solution.py:37
  2.3 4.1 %collective-permute-start = (bf16[32,4736]{1,0:T(8,128)(2,1)S(1)}, bf16[32,4736]{1,0:T(8,128)(2,1)S(1)}, u32[]{:S(2)}, u32[]{:S(2)}) collective-permute-start(bf16[32,4736]{1,0:T(8,128)(2,1)S(1)} %weigh.1.refs_0_), channel_id=1, source_target_pairs={{0,8},{4,12},{8,0},{12,4},{1,9},{5,13},{9,1},{13,5},{2,10},{6,14},... | collective-permute-start | bytes 909320 | tf_op jit(solution)/shard_map/ppermute | solution.py:531
  6.4 1.6 %collective-permute-start.4 = (bf16[32,4736]{1,0:T(8,128)(2,1)S(1)}, bf16[32,4736]{1,0:T(8,128)(2,1)S(1)}, u32[]{:S(2)}, u32[]{:S(2)}) collective-permute-start(bf16[32,4736]{1,0:T(8,128)(2,1)S(1)} %weigh.1.refs_0_), channel_id=1, source_target_pairs={{0,4},{4,0},{8,12},{12,8},{1,5},{5,1},{9,13},{13,9},{2,6},{6,2},{1... | collective-permute-start | bytes 909320 | tf_op jit(solution)/shard_map/ppermute | solution.py:531
  8.0 0.1 pad_add_fusion.me_ref
  8.1 0.6 %cut_slices.2 = (bf16[32,1152]{1,0:T(8,128)(2,1)S(1)}, bf16[32,1152]{1,0:T(8,128)(2,1)S(1)}, bf16[32,1152]{1,0:T(8,128)(2,1)S(1)}, bf16[32,1152]{1,0:T(8,128)(2,1)S(1)}) custom-call(s32[2]{0:T(128)S(1)} %pad_add_fusion.me_ref, bf16[32,4736]{1,0:T(8,128)(2,1)S(1)} %weigh.1.refs_0_), custom_call_target="tpu_custom_call" | custom-call | bytes 589824 | tf_op jit(solution)/shard_map/cut_slices/pallas_call | solution.py:37
  8.7 0.4 collective-permute-start.1
  9.1 1.2 %collective-permute-start.2 = (bf16[32,1152]{1,0:T(8,128)(2,1)S(1)}, bf16[32,1152]{1,0:T(8,128)(2,1)S(1)}, u32[]{:S(2)}, u32[]{:S(2)}) collective-permute-start(bf16[32,1152]{1,0:T(8,128)(2,1)S(1)} %get-tuple-element.41), channel_id=1, source_target_pairs={{0,2},{1,3},{2,0},{3,1},{4,6},{5,7},{6,4},{7,5},{8,10},{9,11},{10,... | collective-permute-start | bytes 221192 | tf_op jit(solution)/shard_map/ppermute | solution.py:531
  10.3 0.3 collective-permute-start.3
  10.6 0.8 %convert_bitcast_fusion = (f32[24]{0:T(128)S(1)}, f32[24]{0:T(128)S(1)}) fusion(s32[24,2]{0,1:T(2,128)} %param.11), kind=kLoop, calls=%fused_computation.9 | loop fusion | flops 48 | bytes 384 | tf_op jit(solution)/shard_map/mul | solution.py:32
  11.4 0.1 fusion
  11.5 0.1 fusion.2
  11.6 0.7 %broadcast_in_dim.2.nw_ref = f32[1,4608]{1,0:T(1,128)S(1)} reshape(f32[4608]{0:T(1024)} %nw_hbm.1) | data formatting | bytes 36864 | tf_op jit(solution)/shard_map/broadcast_in_dim | solution.py:552
  12.4 1.1 %copy.10 = bf16[32,2,4608]{2,0,1:T(8,128)(2,1)S(1)} copy(bf16[32,2,4608]{2,1,0:T(2,128)(2,1)} %param.7) | data formatting | bytes 1179648 | tf_op args[1]
  13.5 0.0 copy-start
  13.5 1.3 %copy-done = f32[64,4608]{1,0:T(8,128)S(1)} copy-done((f32[64,4608]{1,0:T(8,128)S(1)}, f32[64,4608]{1,0:T(8,128)}, u32[]{:S(2)}) %copy-start) | copy-done | bytes 1179672
  14.8 1.2 %prepare.1 = (f32[24,4608]{1,0:T(8,128)S(1)}, f32[24,4608]{1,0:T(8,128)S(1)}, f32[32,64]{1,0:T(8,128)S(1)}) custom-call(bf16[2,32,4608]{2,1,0:T(8,128)(2,1)S(1)} %bitcast.10, f32[24,128]{1,0:T(8,128)S(1)} %get-tuple-element.77.xc_ref, f32[24,128]{1,0:T(8,128)S(1)} %get-tuple-element.76.xs_ref, f32[24,36]{1,0:T(8,128)S(1)} %get-tuple-element.73.yc_ref, ...), custom_call_target="tpu_custom_call" | custom-call | flops 226492416 | tf_op jit(solution)/shard_map/prepare/pallas_call | solution.py:37
  16.0 4.5 %early_templates.1.early_hbm = bf16[6,768,768]{2,1,0:T(8,128)(2,1)} custom-call(bf16[2,32,4608]{2,1,0:T(8,128)(2,1)S(1)} %bitcast.11, f32[24,4608]{1,0:T(8,128)S(1)} %get-tuple-element.37.cos_ref, f32[24,4608]{1,0:T(8,128)S(1)} %get-tuple-element.38.sin_ref), custom_call_target="tpu_custom_call" | custom-call | flops 70778880 | bytes 7077888 | tf_op jit(solution)/shard_map/early_templates/pallas_call | solution.py:176
  20.5 0.0 collective-permute-done.1.refs_3_
  20.5 0.0 collective-permute-done.2.refs_4_
  20.5 0.0 collective-permute-done.3.refs_5_
  20.5 0.0 collective-permute-done.refs_2_.refs_1_
  20.5 0.5 collective-permute-start.5
  21.1 0.0 collective-permute-done.4.refs_1_.refs_0_
  21.1 0.6 %cut_slices.3 = (bf16[64,1152]{1,0:T(8,128)(2,1)S(1)}, bf16[64,1152]{1,0:T(8,128)(2,1)S(1)}, bf16[64,1152]{1,0:T(8,128)(2,1)S(1)}, bf16[64,1152]{1,0:T(8,128)(2,1)S(1)}) custom-call(s32[2]{0:T(128)S(1)} %pad_add_fusion.me_ref, bf16[32,4736]{1,0:T(8,128)(2,1)S(1)} %collective-permute-done.4.refs_1_.refs_0_, ...), custom_call_target="tpu_custom_call" | custom-call | bytes 1179648 | tf_op jit(solution)/shard_map/cut_slices/pallas_call | solution.py:37
  21.7 0.9 %collective-permute-start.6 = (bf16[64,1152]{1,0:T(8,128)(2,1)S(1)}, bf16[64,1152]{1,0:T(8,128)(2,1)S(1)}, u32[]{:S(2)}, u32[]{:S(2)}) collective-permute-start(bf16[64,1152]{1,0:T(8,128)(2,1)S(1)} %get-tuple-element.55), channel_id=1, source_target_pairs={{0,3},{1,2},{2,1},{3,0},{4,7},{5,6},{6,5},{7,4},{8,11},{9,10},{10,... | collective-permute-start | bytes 442376 | tf_op jit(solution)/shard_map/ppermute | solution.py:531
  22.5 0.8 %collective-permute-start.7 = (bf16[64,1152]{1,0:T(8,128)(2,1)S(1)}, bf16[64,1152]{1,0:T(8,128)(2,1)S(1)}, u32[]{:S(2)}, u32[]{:S(2)}) collective-permute-start(bf16[64,1152]{1,0:T(8,128)(2,1)S(1)} %get-tuple-element.56), channel_id=1, source_target_pairs={{0,2},{1,3},{2,0},{3,1},{4,6},{5,7},{6,4},{7,5},{8,10},{9,11},{10,... | collective-permute-start | bytes 442376 | tf_op jit(solution)/shard_map/ppermute | solution.py:531
  23.3 0.3 collective-permute-start.8
  23.6 3.1 %templates.1.temp_ref = bf16[12,768,768]{2,1,0:T(8,128)(2,1)S(1)} custom-call(bf16[6,768,768]{2,1,0:T(8,128)(2,1)} %early_templates.1.early_hbm, bf16[2,32,4608]{2,1,0:T(8,128)(2,1)S(1)} %bitcast.12, f32[24,4608]{1,0:T(8,128)S(1)} %get-tuple-element.37.cos_ref, f32[24,4608]{1,0:T(8,128)S(1)} %get-tuple-element.38.sin_ref), custom_call_target="tpu_custom_call" | custom-call | flops 70778880 | bytes 7077888 | tf_op jit(solution)/shard_map/templates/pallas_call | solution.py:37
  26.7 3.2 %collective-permute-done.5.refs_3_.refs_0_ = bf16[32,4736]{1,0:T(8,128)(2,1)S(1)} collective-permute-done((bf16[32,4736]{1,0:T(8,128)(2,1)S(1)}, bf16[32,4736]{1,0:T(8,128)(2,1)S(1)}, u32[]{:S(2)}, u32[]{:S(2)}) %collective-permute-start.5) | collective-permute-done | bytes 303136 | tf_op jit(solution)/shard_map/ppermute | solution.py:531
  29.9 4.1 %score.1 = (f32[768,128]{1,0:T(8,128)S(1)}, f32[128,64]{1,0:T(8,128)S(1)}, f32[8,128]{1,0:T(8,128)S(1)}) custom-call(bf16[12,768,768]{2,1,0:T(8,128)(2,1)S(1)} %templates.1.temp_ref, f32[32,64]{1,0:T(8,128)S(1)} %get-tuple-element.45.pow_ref, bf16[32,4736]{1,0:T(8,128)(2,1)S(1)} %weigh.1.refs_0_, ...), custom_call_target="tpu_custom_call" | custom-call | flops 3623878656 | tf_op jit(solution)/shard_map/score/pallas_call | solution.py:37
  34.0 0.0 collective-permute-done.6.refs_0_.refs_7_
  34.0 0.0 collective-permute-done.7.refs_1_.refs_8_
  34.0 0.0 collective-permute-done.8.refs_2_.refs_9_
  34.0 0.5 collective-permute-start.12
  34.5 3.0 %collective-permute-start.10 = (f32[8,128]{1,0:T(8,128)S(1)}, f32[8,128]{1,0:T(8,128)S(1)}, u32[]{:S(2)}, u32[]{:S(2)}) collective-permute-start(f32[8,128]{1,0:T(8,128)S(1)} %get-tuple-element.58.refs_0_), channel_id=1, source_target_pairs={{0,8},{4,12},{8,0},{12,4},{1,9},{5,13},{9,1},{13,5},{2,10},{6,14},... | collective-permute-start | bytes 12296 | tf_op jit(solution)/shard_map/ppermute | solution.py:531
  37.5 1.0 %collective-permute-start.11 = (f32[8,128]{1,0:T(8,128)S(1)}, f32[8,128]{1,0:T(8,128)S(1)}, u32[]{:S(2)}, u32[]{:S(2)}) collective-permute-start(f32[8,128]{1,0:T(8,128)S(1)} %get-tuple-element.58.refs_0_), channel_id=1, source_target_pairs={{0,12},{4,8},{8,4},{12,0},{1,13},{5,9},{9,5},{13,1},{2,14},{6,10},... | collective-permute-start | bytes 12296 | tf_op jit(solution)/shard_map/ppermute | solution.py:531
  38.5 0.0 collective-permute-start.9
  38.5 0.7 %collective-permute-done.10.refs_2_ = f32[8,128]{1,0:T(8,128)S(1)} collective-permute-done((f32[8,128]{1,0:T(8,128)S(1)}, f32[8,128]{1,0:T(8,128)S(1)}, u32[]{:S(2)}, u32[]{:S(2)}) %collective-permute-start.10) | collective-permute-done | bytes 4128 | tf_op jit(solution)/shard_map/ppermute | solution.py:531
  39.2 3.7 %collective-permute-done.11.refs_3_ = f32[8,128]{1,0:T(8,128)S(1)} collective-permute-done((f32[8,128]{1,0:T(8,128)S(1)}, f32[8,128]{1,0:T(8,128)S(1)}, u32[]{:S(2)}, u32[]{:S(2)}) %collective-permute-start.11) | collective-permute-done | bytes 4128 | tf_op jit(solution)/shard_map/ppermute | solution.py:531
  42.9 0.5 responsibilities.1
  43.4 0.0 collective-permute-start.13
  43.4 1.6 %collective-permute-start.14 = (bf16[416,128]{1,0:T(8,128)(2,1)S(1)}, bf16[416,128]{1,0:T(8,128)(2,1)S(1)}, u32[]{:S(2)}, u32[]{:S(2)}) collective-permute-start(bf16[416,128]{1,0:T(8,128)(2,1)S(1)} %get-tuple-element.71.refs_0_), channel_id=1, source_target_pairs={{0,2},{1,3},{2,0},{3,1},{4,6},{5,7},{6,4},{7,5},{8,10},{9,11},{10,... | collective-permute-start | bytes 319496 | tf_op jit(solution)/shard_map/ppermute | solution.py:531
  45.0 0.3 collective-permute-start.15
  45.3 0.0 collective-permute-done.12.refs_1_
  45.3 1.5 %gather_rows.1 = (f32[32,64]{1,0:T(8,128)}, f32[64,1152]{1,0:T(8,128)S(1)}, bf16[2,256,1152]{2,1,0:T(8,128)(2,1)S(1)}) custom-call(s32[2]{0:T(128)S(1)} %pad_add_fusion.me_ref, f32[768,128]{1,0:T(8,128)S(1)} %get-tuple-element.47.s_ref, f32[1,128]{1,0:T(1,128)S(1)} %get-tuple-element.59.norm_ref, f32[64,4608]{1,0:T(8,128)S(1)} %copy-done.1, ...), custom_call_target="tpu_custom_call" | custom-call | flops 3932160 | bytes 2359296 | tf_op jit(solution)/shard_map/gather_rows/pallas_call | solution.py:37
  46.8 1.8 %collective-permute-done.13.refs_1_ = bf16[416,128]{1,0:T(8,128)(2,1)S(1)} collective-permute-done((bf16[416,128]{1,0:T(8,128)(2,1)S(1)}, bf16[416,128]{1,0:T(8,128)(2,1)S(1)}, u32[]{:S(2)}, u32[]{:S(2)}) %collective-permute-start.13) | collective-permute-done | bytes 106528 | tf_op jit(solution)/shard_map/ppermute | solution.py:531
  48.6 2.3 %collective-permute-done.14.refs_2_ = bf16[416,128]{1,0:T(8,128)(2,1)S(1)} collective-permute-done((bf16[416,128]{1,0:T(8,128)(2,1)S(1)}, bf16[416,128]{1,0:T(8,128)(2,1)S(1)}, u32[]{:S(2)}, u32[]{:S(2)}) %collective-permute-start.14) | collective-permute-done | bytes 106528 | tf_op jit(solution)/shard_map/ppermute | solution.py:531
  51.0 3.2 %finish.1 = f32[32,2,1152]{2,1,0:T(2,128)} custom-call(s32[2]{0:T(128)S(1)} %pad_add_fusion.me_ref, f32[64,1152]{1,0:T(8,128)S(1)} %get-tuple-element.69.cw_ref, f32[24,4608]{1,0:T(8,128)S(1)} %get-tuple-element.37.cos_ref, f32[24,4608]{1,0:T(8,128)S(1)} %get-tuple-element.38.sin_ref, bf16[2,256,1152]{2,1,0:T(8,128)(2,1)S(1)} %get-tuple-element.70.rows_ref, ...), custom_call_target="tpu_custom_call" | custom-call | flops 905969664 | tf_op jit(solution)/shard_map/finish/pallas_call | solution.py:37
  (7 shorter events, 0.0 us)
Async XLA Ops:
  2.3 18.2 %collective-permute-start = (bf16[32,4736]{1,0:T(8,128)(2,1)S(1)}, bf16[32,4736]{1,0:T(8,128)(2,1)S(1)}, u32[]{:S(2)}, u32[]{:S(2)}) collective-permute-start(bf16[32,4736]{1,0:T(8,128)(2,1)S(1)} %weigh.1.refs_0_), channel_id=1, source_target_pairs={{0,8},{4,12},{8,0},{12,4},{1,9},{5,13},{9,1},{13,5},{2,10},{6,14},... | collective-permute-start | bytes 909320 | tf_op jit(solution)/shard_map/ppermute | solution.py:531
  6.4 14.6 %collective-permute-start.4 = (bf16[32,4736]{1,0:T(8,128)(2,1)S(1)}, bf16[32,4736]{1,0:T(8,128)(2,1)S(1)}, u32[]{:S(2)}, u32[]{:S(2)}) collective-permute-start(bf16[32,4736]{1,0:T(8,128)(2,1)S(1)} %weigh.1.refs_0_), channel_id=1, source_target_pairs={{0,4},{4,0},{8,12},{12,8},{1,5},{5,1},{9,13},{13,9},{2,6},{6,2},{1... | collective-permute-start | bytes 909320 | tf_op jit(solution)/shard_map/ppermute | solution.py:531
  8.7 11.8 %collective-permute-start.1 = (bf16[32,1152]{1,0:T(8,128)(2,1)S(1)}, bf16[32,1152]{1,0:T(8,128)(2,1)S(1)}, u32[]{:S(2)}, u32[]{:S(2)}) collective-permute-start(bf16[32,1152]{1,0:T(8,128)(2,1)S(1)} %get-tuple-element.40), channel_id=1, source_target_pairs={{0,3},{1,2},{2,1},{3,0},{4,7},{5,6},{6,5},{7,4},{8,11},{9,10},{10,... | collective-permute-start | bytes 221192 | tf_op jit(solution)/shard_map/ppermute | solution.py:531
  9.1 11.4 %collective-permute-start.2 = (bf16[32,1152]{1,0:T(8,128)(2,1)S(1)}, bf16[32,1152]{1,0:T(8,128)(2,1)S(1)}, u32[]{:S(2)}, u32[]{:S(2)}) collective-permute-start(bf16[32,1152]{1,0:T(8,128)(2,1)S(1)} %get-tuple-element.41), channel_id=1, source_target_pairs={{0,2},{1,3},{2,0},{3,1},{4,6},{5,7},{6,4},{7,5},{8,10},{9,11},{10,... | collective-permute-start | bytes 221192 | tf_op jit(solution)/shard_map/ppermute | solution.py:531
  10.3 10.2 %collective-permute-start.3 = (bf16[32,1152]{1,0:T(8,128)(2,1)S(1)}, bf16[32,1152]{1,0:T(8,128)(2,1)S(1)}, u32[]{:S(2)}, u32[]{:S(2)}) collective-permute-start(bf16[32,1152]{1,0:T(8,128)(2,1)S(1)} %get-tuple-element.42), channel_id=1, source_target_pairs={{0,1},{1,0},{2,3},{3,2},{4,5},{5,4},{6,7},{7,6},{8,9},{9,8},{10,11... | collective-permute-start | bytes 221192 | tf_op jit(solution)/shard_map/ppermute | solution.py:531
  13.5 1.3 %copy-start = (f32[64,4608]{1,0:T(8,128)S(1)}, f32[64,4608]{1,0:T(8,128)}, u32[]{:S(2)}) copy-start(f32[64,4608]{1,0:T(8,128)} %ctf_ref.3) | copy-start | bytes 3538948
  20.5 9.4 %collective-permute-start.5 = (bf16[32,4736]{1,0:T(8,128)(2,1)S(1)}, bf16[32,4736]{1,0:T(8,128)(2,1)S(1)}, u32[]{:S(2)}, u32[]{:S(2)}) collective-permute-start(bf16[32,4736]{1,0:T(8,128)(2,1)S(1)} %collective-permute-done.refs_2_.refs_1_), channel_id=1, source_target_pairs={{0,4},{4,0},{8,12},{12,8},{1,5},{5,1},{9,13},{13,9},{2,6},{6,2},{1... | collective-permute-start | bytes 909320 | tf_op jit(solution)/shard_map/ppermute | solution.py:531
  21.7 12.3 %collective-permute-start.6 = (bf16[64,1152]{1,0:T(8,128)(2,1)S(1)}, bf16[64,1152]{1,0:T(8,128)(2,1)S(1)}, u32[]{:S(2)}, u32[]{:S(2)}) collective-permute-start(bf16[64,1152]{1,0:T(8,128)(2,1)S(1)} %get-tuple-element.55), channel_id=1, source_target_pairs={{0,3},{1,2},{2,1},{3,0},{4,7},{5,6},{6,5},{7,4},{8,11},{9,10},{10,... | collective-permute-start | bytes 442376 | tf_op jit(solution)/shard_map/ppermute | solution.py:531
  22.5 11.4 %collective-permute-start.7 = (bf16[64,1152]{1,0:T(8,128)(2,1)S(1)}, bf16[64,1152]{1,0:T(8,128)(2,1)S(1)}, u32[]{:S(2)}, u32[]{:S(2)}) collective-permute-start(bf16[64,1152]{1,0:T(8,128)(2,1)S(1)} %get-tuple-element.56), channel_id=1, source_target_pairs={{0,2},{1,3},{2,0},{3,1},{4,6},{5,7},{6,4},{7,5},{8,10},{9,11},{10,... | collective-permute-start | bytes 442376 | tf_op jit(solution)/shard_map/ppermute | solution.py:531
  23.3 10.7 %collective-permute-start.8 = (bf16[64,1152]{1,0:T(8,128)(2,1)S(1)}, bf16[64,1152]{1,0:T(8,128)(2,1)S(1)}, u32[]{:S(2)}, u32[]{:S(2)}) collective-permute-start(bf16[64,1152]{1,0:T(8,128)(2,1)S(1)} %get-tuple-element.57), channel_id=1, source_target_pairs={{0,1},{1,0},{2,3},{3,2},{4,5},{5,4},{6,7},{7,6},{8,9},{9,8},{10,11... | collective-permute-start | bytes 442376 | tf_op jit(solution)/shard_map/ppermute | solution.py:531
  29.9 15.4 %copy-start.1 = (f32[64,4608]{1,0:T(8,128)S(1)}, f32[64,4608]{1,0:T(8,128)}, u32[]{:S(2)}) copy-start(f32[64,4608]{1,0:T(8,128)} %ctf_ref.3) | copy-start | bytes 3538948
  34.0 11.3 %collective-permute-start.12 = (bf16[96,1152]{1,0:T(8,128)(2,1)S(1)}, bf16[96,1152]{1,0:T(8,128)(2,1)S(1)}, u32[]{:S(2)}, u32[]{:S(2)}) collective-permute-start(bf16[96,1152]{1,0:T(8,128)(2,1)S(1)} %bundle.1), channel_id=1, source_target_pairs={{0,4},{4,0},{8,12},{12,8},{1,5},{5,1},{9,13},{13,9},{2,6},{6,2},{1... | collective-permute-start | bytes 663560 | tf_op jit(solution)/shard_map/ppermute | solution.py:531
  34.5 4.7 %collective-permute-start.10 = (f32[8,128]{1,0:T(8,128)S(1)}, f32[8,128]{1,0:T(8,128)S(1)}, u32[]{:S(2)}, u32[]{:S(2)}) collective-permute-start(f32[8,128]{1,0:T(8,128)S(1)} %get-tuple-element.58.refs_0_), channel_id=1, source_target_pairs={{0,8},{4,12},{8,0},{12,4},{1,9},{5,13},{9,1},{13,5},{2,10},{6,14},... | collective-permute-start | bytes 12296 | tf_op jit(solution)/shard_map/ppermute | solution.py:531
  37.5 5.4 %collective-permute-start.11 = (f32[8,128]{1,0:T(8,128)S(1)}, f32[8,128]{1,0:T(8,128)S(1)}, u32[]{:S(2)}, u32[]{:S(2)}) collective-permute-start(f32[8,128]{1,0:T(8,128)S(1)} %get-tuple-element.58.refs_0_), channel_id=1, source_target_pairs={{0,12},{4,8},{8,4},{12,0},{1,13},{5,9},{9,5},{13,1},{2,14},{6,10},... | collective-permute-start | bytes 12296 | tf_op jit(solution)/shard_map/ppermute | solution.py:531
  38.5 4.4 %collective-permute-start.9 = (f32[8,128]{1,0:T(8,128)S(1)}, f32[8,128]{1,0:T(8,128)S(1)}, u32[]{:S(2)}, u32[]{:S(2)}) collective-permute-start(f32[8,128]{1,0:T(8,128)S(1)} %get-tuple-element.58.refs_0_), channel_id=1, source_target_pairs={{0,4},{4,0},{8,12},{12,8},{1,5},{5,1},{9,13},{13,9},{2,6},{6,2},{1... | collective-permute-start | bytes 12296 | tf_op jit(solution)/shard_map/ppermute | solution.py:531
  43.4 5.2 %collective-permute-start.13 = (bf16[416,128]{1,0:T(8,128)(2,1)S(1)}, bf16[416,128]{1,0:T(8,128)(2,1)S(1)}, u32[]{:S(2)}, u32[]{:S(2)}) collective-permute-start(bf16[416,128]{1,0:T(8,128)(2,1)S(1)} %get-tuple-element.71.refs_0_), channel_id=1, source_target_pairs={{0,3},{1,2},{2,1},{3,0},{4,7},{5,6},{6,5},{7,4},{8,11},{9,10},{10,... | collective-permute-start | bytes 319496 | tf_op jit(solution)/shard_map/ppermute | solution.py:531
  43.4 7.5 %collective-permute-start.14 = (bf16[416,128]{1,0:T(8,128)(2,1)S(1)}, bf16[416,128]{1,0:T(8,128)(2,1)S(1)}, u32[]{:S(2)}, u32[]{:S(2)}) collective-permute-start(bf16[416,128]{1,0:T(8,128)(2,1)S(1)} %get-tuple-element.71.refs_0_), channel_id=1, source_target_pairs={{0,2},{1,3},{2,0},{3,1},{4,6},{5,7},{6,4},{7,5},{8,10},{9,11},{10,... | collective-permute-start | bytes 319496 | tf_op jit(solution)/shard_map/ppermute | solution.py:531
  45.0 6.0 %collective-permute-start.15 = (bf16[416,128]{1,0:T(8,128)(2,1)S(1)}, bf16[416,128]{1,0:T(8,128)(2,1)S(1)}, u32[]{:S(2)}, u32[]{:S(2)}) collective-permute-start(bf16[416,128]{1,0:T(8,128)(2,1)S(1)} %get-tuple-element.71.refs_0_), channel_id=1, source_target_pairs={{0,1},{1,0},{2,3},{3,2},{4,5},{5,4},{6,7},{7,6},{8,9},{9,8},{10,11... | collective-permute-start | bytes 319496 | tf_op jit(solution)/shard_map/ppermute | solution.py:531

commit v11 on v10

--- a/solution.py
+++ b/solution.py
@@ -8,6 +8,7 @@
 from jax.sharding import PartitionSpec as P
 
 BOX = 128
+CHUNKS = 2
 LANES = 128
 VMEM_LIMIT = 24 * 1024 * 1024
 
@@ -22,15 +23,6 @@
 SMEM = pl.BlockSpec(memory_space=pltpu.SMEM)
 VMEM = pl.BlockSpec(memory_space=pltpu.VMEM)
 ANY = pl.BlockSpec(memory_space=pl.ANY)
-
-
-def phase_tables(shifts, freq):
-    along_x = (jnp.arange(BOX) - BOX // 2).astype(f32)
-    along_y = jnp.arange(freq // BOX).astype(f32)
-    step = 2.0 * jnp.pi / BOX
-    angle_x = step * (shifts[:, 0:1].astype(f32) * along_x[None, :])
-    angle_y = step * (shifts[:, 1:2].astype(f32) * along_y[None, :])
-    return (jnp.cos(angle_x), jnp.sin(angle_x), jnp.cos(angle_y), jnp.sin(angle_y))
 
 
 def call(kernel, name, in_specs, out_shape, operands, scratch=(), flops=0, moved=0, limit=VMEM_LIMIT):
@@ -50,9 +42,8 @@
     return lax.rem(lax.broadcasted_iota(jnp.int32, shape, axis) // half, 2) == 0
 
 
-def weigh_kernel(
-    ids_hbm, p_hbm, ctf_hbm, nw_hbm, out_ref, ids_ref, p_ref, ctf_ref, nw_ref, scale_ref, sem
-):
+def weigh_kernel(ids_hbm, p_hbm, ctf_hbm, nw_hbm, *refs):
+    out_refs, (ids_ref, p_ref, ctf_ref, nw_ref, scale_ref, sem) = refs[:-6], refs[-6:]
     count, _, freq = p_ref.shape
     copies = [
         pltpu.make_async_copy(source, target, sem.at[i])
@@ -74,9 +65,15 @@
         scale_ref[n : n + 1, :] = ctf_ref[pl.ds(ids_ref[n], 1), :] * noise
     scale = scale_ref[...]
     values = p_ref[...].astype(f32)
-    out_ref[:count, :freq] = (values[:, 0, :] * scale).astype(bf16)
-    out_ref[count:, :freq] = (values[:, 1, :] * scale).astype(bf16)
-    out_ref[:, freq:] = ids.astype(bf16)
+    chunk = freq // CHUNKS
+    for part in range(2):
+        weighted = (values[:, part, :] * scale).astype(bf16)
+        here = slice(part * count, (part + 1) * count)
+        out_refs[0][here, :freq] = weighted
+        for c, out_ref in enumerate(out_refs[1:]):
+            out_ref[here, :chunk] = weighted[:, c * chunk : (c + 1) * chunk]
+    for out_ref in out_refs[:2]:
+        out_ref[:, out_ref.shape[1] - LANES :] = ids.astype(bf16)
 
 
 def weigh(particles, ctf, noise_weight, group_ids):
@@ -86,7 +83,10 @@
         weigh_kernel,
         "weigh",
         [ANY] * 4,
-        [jax.ShapeDtypeStruct((2 * rows, freq + LANES), bf16)],
+        [
+            jax.ShapeDtypeStruct((2 * rows, width), bf16)
+            for width in [freq + LANES, freq // CHUNKS + LANES] + [freq // CHUNKS] * (CHUNKS - 1)
+        ],
         [pltpu.with_memory_space_constraint(x, pltpu.HBM) for x in operands],
         [
             pltpu.SMEM((rows,), jnp.int32),
@@ -98,49 +98,80 @@
         ],
         flops=4 * rows * freq,
         moved=16 * rows * freq,
-    )[0]
+    )
 
 
 def prepare_kernel(
-    cls_ref, xc_ref, xs_ref, yc_ref, ys_ref, ctf_ref, nw_ref, cos_ref, sin_ref, pow_ref
+    shifts_ref, cls_hbm, ctf_hbm, nw_hbm, cos_ref, sin_ref, pow_ref, split_ref, cw_ref, *scratch
 ):
-    freq = cls_ref.shape[2]
-    x_cos, x_sin = xc_ref[...], xs_ref[...]
+    cls_ref, ctf_ref, nw_ref, angle_ref, sem = scratch
+    rows, _, freq = cls_ref.shape
+    poses = cos_ref.shape[0]
+    copies = [
+        pltpu.make_async_copy(source, target, sem.at[i])
+        for i, (source, target) in enumerate(
+            [(cls_hbm, cls_ref), (ctf_hbm, ctf_ref), (nw_hbm, nw_ref)]
+        )
+    ]
+    for copy in copies:
+        copy.start()
+    lane = lax.broadcasted_iota(jnp.int32, (1, BOX), 1).astype(f32)
+    step = 2.0 * jnp.pi / BOX
+    for r in range(poses):
+        angle_ref[0, r : r + 1, :] = step * (shifts_ref[0, r].astype(f32) * (lane - BOX // 2))
+        angle_ref[1, r : r + 1, :] = step * (shifts_ref[1, r].astype(f32) * lane)
+    x_cos, x_sin = jnp.cos(angle_ref[0]), jnp.sin(angle_ref[0])
+    y_cos, y_sin = jnp.cos(angle_ref[1]), jnp.sin(angle_ref[1])
     for t in range(freq // BOX):
-        y_cos = jnp.broadcast_to(yc_ref[:, t : t + 1], x_cos.shape)
-        y_sin = jnp.broadcast_to(ys_ref[:, t : t + 1], x_cos.shape)
-        cos_ref[:, t * BOX : (t + 1) * BOX] = x_cos * y_cos - x_sin * y_sin
-        sin_ref[:, t * BOX : (t + 1) * BOX] = x_sin * y_cos + x_cos * y_sin
+        c = jnp.broadcast_to(y_cos[:, t : t + 1], x_cos.shape)
+        s = jnp.broadcast_to(y_sin[:, t : t + 1], x_cos.shape)
+        cos_ref[:, t * BOX : (t + 1) * BOX] = x_cos * c - x_sin * s
+        sin_ref[:, t * BOX : (t + 1) * BOX] = x_sin * c + x_cos * s
+    for copy in copies:
+        copy.wait()
+    noise = nw_ref[...].reshape(1, freq)
     cut = freq // 4
     power = jnp.zeros(pow_ref.shape, f32)
     for q in range(4):
         at = slice(q * cut, (q + 1) * cut)
-        re = cls_ref[0, :, at].astype(f32)
-        im = cls_ref[1, :, at].astype(f32)
+        values = cls_ref[:, :, at].astype(f32)
+        re, im = values[:, 0, :], values[:, 1, :]
+        split_ref[0, :, at] = re.astype(bf16)
+        split_ref[1, :, at] = im.astype(bf16)
         ctf = ctf_ref[:, at]
+        weight = ctf * ctf * noise[:, at]
+        cw_ref[:, at] = weight
         power += lax.dot_general(
-            re * re + im * im,
-            ctf * ctf * nw_ref[:, at],
-            NT,
-            precision=HIGHEST,
-            preferred_element_type=f32,
+            re * re + im * im, weight, NT, precision=HIGHEST, preferred_element_type=f32
         )
     pow_ref[...] = power
 
 
-def prepare(split, tables, ctf, noise_weight):
-    _, rows, freq = split.shape
-    poses, groups = tables[0].shape[0], ctf.shape[0]
+def prepare(shifts, classes, ctf, noise_weight):
+    rows, _, freq = classes.shape
+    poses, groups = shifts.shape[0], ctf.shape[0]
     return call(
         prepare_kernel,
         "prepare",
-        [VMEM] * 7,
+        [SMEM, ANY, ANY, ANY],
         [
             jax.ShapeDtypeStruct((poses, freq), f32),
             jax.ShapeDtypeStruct((poses, freq), f32),
             jax.ShapeDtypeStruct((rows, groups), f32),
-        ],
-        (split, *tables, ctf, noise_weight),
+            jax.ShapeDtypeStruct((2, rows, freq), bf16),
+            jax.ShapeDtypeStruct((groups, freq), f32),
+        ],
+        (
+            shifts.T,
+            *[pltpu.with_memory_space_constraint(x, pltpu.HBM) for x in (classes, ctf, noise_weight)],
+        ),
+        [
+            pltpu.VMEM(classes.shape, bf16),
+            pltpu.VMEM(ctf.shape, f32),
+            pltpu.VMEM((freq,), f32),
+            pltpu.VMEM((2, poses, BOX), f32),
+            pltpu.SemaphoreType.DMA((3,)),
+        ],
         flops=24 * rows * groups * freq,
     )
 
@@ -160,7 +191,7 @@
 
 
 def template_tile(freq):
-    return max(t for t in range(LANES, 385, LANES) if freq % t == 0)
+    return max(t for t in range(LANES, 385, LANES) if freq // CHUNKS % t == 0)
 
 
 def early_kernel(cls_ref, cos_ref, sin_ref, temp_ref):
@@ -226,30 +257,52 @@
     )[0]
 
 
-def score_kernel(half, temp_ref, pow_ref, *refs):
-    shards, (s_ref, marks_ref, stat_ref) = refs[:-3], refs[-3:]
+def add_products(acc_ref, temp_ref, chunk, shards, half):
+    count = temp_ref.shape[0] // CHUNKS
+    tile = temp_ref.shape[2] // 2
+    real = real_index((acc_ref.shape[1], tile), 0, half)
+    for t in range(count):
+        cuts = []
+        for refs in shards:
+            ref, at = (refs[0], chunk * count * tile) if len(refs) == 1 else (refs[chunk], 0)
+            cuts.append(ref[:, at + t * tile : at + (t + 1) * tile])
+        wide = jnp.concatenate(cuts, axis=0).astype(f32)
+        split = jnp.concatenate(
+            [jnp.where(real, wide, 0.0).astype(bf16), jnp.where(real, 0.0, wide).astype(bf16)],
+            axis=1,
+        )
+        acc_ref[...] += lax.dot_general(
+            temp_ref[chunk * count + t], split, NT, preferred_element_type=f32
+        )
+
+
+def regroup(refs, counts):
+    refs = list(refs)
+    return [[refs.pop(0) for _ in range(count)] for count in counts]
+
+
+def score_kernel(chunk, counts, half, temp_ref, *refs):
+    *refs, acc_ref = refs
+    acc_ref[...] = jnp.zeros_like(acc_ref) if chunk == 0 else refs.pop(0)[...]
+    add_products(acc_ref, temp_ref, chunk, regroup(refs, counts), half)
+
+
+def last_score_kernel(counts, half, temp_ref, pow_ref, acc_ref, *refs):
+    refs, (s_ref, marks_ref, stat_ref) = refs[:-3], refs[-3:]
+    shards = regroup(refs, counts)
     rows, groups = pow_ref.shape
     lanes = s_ref.shape[1]
     poses = s_ref.shape[0] // rows
-    count = temp_ref.shape[0]
-    tile = temp_ref.shape[2] // 2
-    ids = jnp.concatenate([ref[:, count * tile :] for ref in shards], axis=0).astype(f32)
+    tails = [refs[0][:, refs[0].shape[1] - LANES :] for refs in shards]
+    ids = jnp.concatenate(tails, axis=0).astype(f32)
     group = lax.broadcasted_iota(jnp.int32, (lanes, groups), 1).astype(f32)
     marks = (ids[:, :groups] == group).astype(f32)
     marks_ref[...] = marks
     penalty = lax.dot_general(
         pow_ref[...], marks, NT, precision=HIGHEST, preferred_element_type=f32
     )
-    s_ref[...] = jnp.zeros_like(s_ref)
-    real = real_index((lanes, tile), 0, half)
-    for t in range(count):
-        at = slice(t * tile, (t + 1) * tile)
-        wide = jnp.concatenate([ref[:, at] for ref in shards], axis=0).astype(f32)
-        split = jnp.concatenate(
-            [jnp.where(real, wide, 0.0).astype(bf16), jnp.where(real, 0.0, wide).astype(bf16)],
-            axis=1,
-        )
-        s_ref[...] += lax.dot_general(temp_ref[t], split, NT, preferred_element_type=f32)
+    s_ref[...] = acc_ref[...]
+    add_products(s_ref, temp_ref, CHUNKS - 1, shards, half)
     acc = s_ref[...]
     acc = acc + jnp.where(
         real_index(acc.shape, 1, half), pltpu.roll(acc, lanes - half, 1), pltpu.roll(acc, half, 1)
@@ -265,41 +318,67 @@
 
 def score(temps, power, shards, half):
     count, columns, width = temps.shape
-    lanes = sum(p.shape[0] for p in shards)
-    operands = [temps, power, *shards]
-    return call(
-        functools.partial(score_kernel, half),
-        "score",
+    lanes = sum(refs[0].shape[0] for refs in shards)
+    flops = 2 * columns * 256 * count * width // CHUNKS
+    acc_shape = jax.ShapeDtypeStruct((columns, lanes), f32)
+    acc = []
+    for c in range(CHUNKS - 1):
+        counts = [1 if len(refs) == 1 else CHUNKS for refs in shards]
+        operands = [temps, *acc]
+        for refs in shards:
+            operands += refs if len(refs) == 1 else [refs[c]] * CHUNKS
+        acc = call(
+            functools.partial(score_kernel, c, counts, half),
+            f"score{c}",
+            [VMEM] * len(operands),
+            [acc_shape],
+            operands,
+            flops=flops,
+        )
+    operands = [temps, power, *acc, *[ref for refs in shards for ref in refs]]
+    return call(
+        functools.partial(last_score_kernel, [len(refs) for refs in shards], half),
+        f"score{CHUNKS - 1}",
         [VMEM] * len(operands),
         [
-            jax.ShapeDtypeStruct((columns, lanes), f32),
+            acc_shape,
             jax.ShapeDtypeStruct((lanes, power.shape[1]), f32),
             jax.ShapeDtypeStruct((8, lanes), f32),
         ],
         operands,
-        flops=2 * columns * 256 * count * width,
-    )
-
-
-def slices_kernel(targets, me_ref, *refs):
-    shards, out_refs = refs[: -len(targets)], refs[-len(targets) :]
+        flops=flops,
+    )
+
+
+def slices_kernel(counts, targets, me_ref, *refs):
+    whole_ref, refs = refs[-1], refs[:-1]
+    shards, out_refs = regroup(refs[: -len(targets)], counts), refs[-len(targets) :]
     span = out_refs[0].shape[1]
     at = 0
-    for ref in shards:
+    for refs in shards:
+        source = refs[0]
+        height = source.shape[0]
+        if len(refs) > 1:
+            width = refs[-1].shape[1]
+            for c, ref in enumerate(refs):
+                whole_ref[:, c * width : (c + 1) * width] = ref[:, :width]
+            source = whole_ref
         for out_ref, distance in zip(out_refs, targets):
             base = pl.multiple_of((me_ref[0] ^ distance) * span, LANES)
-            out_ref[at : at + ref.shape[0], :] = ref[:, pl.ds(base, span)]
-        at += ref.shape[0]
-
-
-def cut_slices(me, shards, targets, span):
-    height = sum(ref.shape[0] for ref in shards)
-    return call(
-        functools.partial(slices_kernel, targets),
+            out_ref[at : at + height, :] = source[:, pl.ds(base, span)]
+        at += height
+
+
+def cut_slices(me, shards, targets, span, freq):
+    height = sum(refs[0].shape[0] for refs in shards)
+    operands = [me, *[ref for refs in shards for ref in refs]]
+    return call(
+        functools.partial(slices_kernel, [len(refs) for refs in shards], targets),
         "cut_slices",
-        [SMEM] + [VMEM] * len(shards),
+        [SMEM] + [VMEM] * (len(operands) - 1),
         [jax.ShapeDtypeStruct((height, span), bf16)] * len(targets),
-        (me, *shards),
+        operands,
+        [pltpu.VMEM((shards[-1][0].shape[0], freq), bf16)],
         moved=4 * height * span * len(targets),
         limit=VMEM_LIMIT if height <= 128 else 2 * VMEM_LIMIT,
     )
@@ -307,20 +386,20 @@
 
 def bundle_kernel(*refs):
     sources, out_ref = refs[:-1], refs[-1]
-    rows = sources[0].shape[0] // 2
+    rows = out_ref.shape[0] // len(sources)
     for i, ref in enumerate(sources):
-        out_ref[i * rows : (i + 1) * rows, :] = ref[rows:, :]
-
-
-def bundle(slices):
-    rows, span = slices[0].shape
+        out_ref[i * rows : (i + 1) * rows, :] = ref[ref.shape[0] - rows :, :]
+
+
+def bundle(slices, rows):
+    span = slices[0].shape[1]
     return call(
         bundle_kernel,
         "bundle",
         [VMEM] * len(slices),
-        [jax.ShapeDtypeStruct((len(slices) * rows // 2, span), bf16)],
+        [jax.ShapeDtypeStruct((len(slices) * rows, span), bf16)],
         slices,
-        moved=2 * len(slices) * rows * span,
+        moved=4 * len(slices) * rows * span,
     )[0]
 
 
@@ -397,30 +476,19 @@
     )
 
 
-def gather_kernel(poses, half, sources, bundled, me_ref, s_ref, norm_ref, ctf_ref, nw_ref, *refs):
+def gather_kernel(poses, half, sources, me_ref, s_ref, norm_ref, weight_ref, *refs):
     w_refs, (resp_ref, cw_ref, rows_ref) = refs[:-3], refs[-3:]
-    last, w_refs = w_refs[: 2 * bundled], w_refs[2 * bundled :]
     span = rows_ref.shape[2]
     block = 2 * half
     here = pl.ds(pl.multiple_of(me_ref[0] * span, LANES), span)
     at = 0
-
-    def put(real, imag):
-        rows_ref[0, at : at + half, :] = real
-        rows_ref[1, at : at + half, :] = imag
-        return at + half
-
     for i in range(sources):
         for ref in w_refs[i::sources]:
             for start in range(0, ref.shape[0], block):
-                at = put(ref[start : start + half, :], ref[start + half : start + block, :])
-        if bundled and i == 0:
-            at = put(last[0][:half, here], last[0][half:, here])
-        elif bundled:
-            start = (i - 1) * block
-            at = put(last[1][start : start + half, :], last[1][start + half : start + block, :])
-    ctf = ctf_ref[:, here]
-    cw_ref[...] = ctf * ctf * nw_ref[:, here]
+                rows_ref[0, at : at + half, :] = ref[start : start + half, :]
+                rows_ref[1, at : at + half, :] = ref[start + half : start + block, :]
+                at += half
+    cw_ref[...] = weight_ref[:, here]
     rows = resp_ref.shape[0]
     lanes = s_ref.shape[1]
     scores = s_ref[...].reshape(poses, rows, lanes)
@@ -436,27 +504,28 @@
     )
 
 
-def gather_rows(me, scores, norm, ctf, noise_weight, slices, last, sources, poses, half, span):
+def gather_rows(me, scores, norm, weight, slices, sources, poses, half, span):
     columns, lanes = scores.shape
-    particles = sources * lanes // 2
-    return call(
-        functools.partial(gather_kernel, poses, half, sources, len(last) // 2),
+    particles = sum(w.shape[0] for w in slices) // 2
+    return call(
+        functools.partial(gather_kernel, poses, half, sources),
         "gather_rows",
-        [SMEM] + [VMEM] * (4 + len(last) + len(slices)),
+        [SMEM] + [VMEM] * (3 + len(slices)),
         [
             jax.ShapeDtypeStruct((columns // poses, lanes // 2), f32),
-            jax.ShapeDtypeStruct((ctf.shape[0], span), f32),
+            jax.ShapeDtypeStruct((weight.shape[0], span), f32),
             jax.ShapeDtypeStruct((2, particles, span), bf16),
         ],
-        (me, scores, norm, ctf, noise_weight, *last, *slices),
+        (me, scores, norm, weight, *slices),
         flops=40 * columns * lanes,
         moved=8 * particles * span,
         limit=VMEM_LIMIT if particles <= 512 else 2 * VMEM_LIMIT,
     )
 
 
-def finish_kernel(poses, groups, sources, me_ref, cw_ref, cos_ref, sin_ref, rows_ref, *refs):
-    payloads, (out_ref, rho_ref, denom_ref, *buffers) = refs[:sources], refs[sources:]
+def finish_kernel(poses, groups, sources, half, me_ref, cw_ref, cos_ref, sin_ref, rows_ref, *refs):
+    payloads, refs = refs[:sources], refs[sources:]
+    last, (out_ref, rho_ref, denom_ref, *buffers) = refs[:-5], refs[-5:]
     rows, _, span = out_ref.shape
     cut = poses // 2 * rows
     count = payloads[0].shape[1] // 2
@@ -470,14 +539,27 @@
         + prior_precision
     )
     tiles = [(a, min(256, span - a)) for a in range(0, span, 256)]
+    known = rows_ref.shape[1] // sources
+
+    def rows_of(part, start, width):
+        here = slice(start, start + width)
+        if not last:
+            return rows_ref[part, :, here]
+        pieces = []
+        for i in range(sources):
+            pieces.append(rows_ref[part, i * known : (i + 1) * known, here])
+            if i == 0:
+                pieces.append(last[0][part * half : (part + 1) * half, here])
+            else:
+                at = (2 * (i - 1) + part) * half
+                pieces.append(last[1][at : at + half, here])
+        return jnp.concatenate(pieces, axis=0)
 
     def products(i):
         start, width = tiles[i]
         for part in range(2):
             buffers[i % 2][part, :, :width] = jnp.dot(
-                rho_ref[...],
-                rows_ref[part, :, start : start + width],
-                preferred_element_type=f32,
+                rho_ref[...], rows_of(part, start, width), preferred_element_type=f32
             )
 
     def rotate(i):
@@ -506,15 +588,16 @@
     rotate(len(tiles) - 1)
 
 
-def finish(me, weight, cos_t, sin_t, rows, payloads, cls_rows):
+def finish(me, weight, cos_t, sin_t, rows, payloads, last, cls_rows, half):
     poses = cos_t.shape[0]
-    _, particles, span = rows.shape
-    return call(
-        functools.partial(finish_kernel, poses, weight.shape[0], len(payloads)),
+    span = rows.shape[2]
+    particles = len(payloads) * payloads[0].shape[1] // 2
+    return call(
+        functools.partial(finish_kernel, poses, weight.shape[0], len(payloads), half),
         "finish",
-        [SMEM] + [VMEM] * (4 + len(payloads)),
+        [SMEM] + [VMEM] * (4 + len(payloads) + len(last)),
         [jax.ShapeDtypeStruct((cls_rows, 2, span), f32)],
-        (me, weight, cos_t, sin_t, rows, *payloads),
+        (me, weight, cos_t, sin_t, rows, *payloads, *last),
         [
             pltpu.VMEM((poses * cls_rows, particles), bf16),
             pltpu.VMEM((cls_rows, span), f32),
@@ -545,43 +628,42 @@
     targets = (0,) + others
 
     def share(*shards):
-        mine, *outgoing = cut_slices(me, shards, targets, span)
+        mine, *outgoing = cut_slices(me, shards, targets, span, freq)
         return [mine] + [swap(w, "img", d) for w, d in zip(outgoing, others)]
 
-    own = weigh(particles, ctf, noise_weight, group_ids)
-    noise_weight = noise_weight[None, :]
+    own, *own_chunks = weigh(particles, ctf, noise_weight, group_ids)
     if pairwise:
-        far, near = swap(own, "cls", 2), swap(own, "cls", 1)
-        slices = share(own)
+        far = [swap(w, "cls", 2) for w in own_chunks]
+        near = swap(own, "cls", 1)
     else:
-        shards = [lax.all_gather(own, "cls", axis=0, tiled=True)]
+        shards = [[lax.all_gather(own, "cls", axis=0, tiled=True)]]
         slices = share(*shards)
 
-    split = jnp.transpose(classes, (1, 0, 2))
-    cos_t, sin_t, power = prepare(split, phase_tables(shifts, freq), ctf, noise_weight)
+    cos_t, sin_t, power, split, weight = prepare(shifts, classes, ctf, noise_weight)
     early = early_templates(split, cos_t, sin_t)
     if pairwise:
-        far, split, early, slices = lax.optimization_barrier((far, split, early, slices))
-        third = swap(far, "cls", 1)
-        slices += share(near, far)
-        shards = [own, near, far, third]
+        far, near, split, early = lax.optimization_barrier((far, near, split, early))
+        third = [swap(w, "cls", 1) for w in far]
+        slices = share([own], [near], far)
+        shards = [[own], [near], far, third]
     temps = all_templates(early, split, cos_t, sin_t)
     scores, marks, stat = score(temps, power, shards, half)
     if pairwise:
         stat, slices = lax.optimization_barrier((stat, slices))
         stats = [stat] + [swap(stat, "cls", k) for k in range(1, n_cls)]
         paired = tuple(range(n_cls))
-        last = [third, swap(bundle(slices[-len(others) :]), "cls", 1)]
+        last = [*cut_slices(me, [third], (0,), span, freq)]
+        last.append(swap(bundle(slices[1:], 2 * half), "cls", 1))
     else:
         stats = [lax.all_gather(stat, "cls", axis=0, tiled=True)]
         paired = (0,)
         last = []
     norm, payload = responsibilities(scores, marks, stats, paired, poses, half)
     payloads = [payload] + [swap(payload, "img", d) for d in others]
-    log_resp, weight, rows = gather_rows(
-        me, scores, norm, ctf, noise_weight, slices, last, n_img, poses, half, span
-    )
-    averages = finish(me, weight, cos_t, sin_t, rows, payloads, cls_rows)
+    log_resp, weight_here, rows = gather_rows(
+        me, scores, norm, weight, slices, n_img, poses, half, span
+    )
+    averages = finish(me, weight_here, cos_t, sin_t, rows, payloads, last, cls_rows, half)
     return (log_resp.T, averages)
 
 

time: 54.5 us -> 55.7 us (1.022)
  Pallas kernels: 21 us -> 24.7 us
  local copies, waits for them, and re-layouts: 3.14 us -> 0.69 us
  other arithmetic: 1.09 us -> 0.07 us
    pallas_call x10 -> x11, Pallas kernels: 16.4 us -> 20.2 us  [call(): pl.pallas_call(kernel, in_specs=in_specs, out_specs=[VMEM] * len(out_shap...]
    unnamed x5 -> x6, local copies, waits for them, and re-layouts: 2.4 us -> 0.69 us
    mul x1 -> x0, other arithmetic: 0.76 us -> none  [phase_tables(): angle_y = step * (shifts[:, 1:2].astype(f32) * along_y[None, :])]
    broadcast_in_dim x1 -> x0, local copies, waits for them, and re-layouts: 0.74 us -> none  [local(): noise_weight = noise_weight[None, :]]
    ppermute x16 -> x15, waiting for transfers between devices: 11.9 us -> 12.4 us  [swap(): return lax.ppermute(values, axis, [(i, i ^ distance) for i in range(size)])]
    ppermute x16 -> x15, starting transfers between devices: 16.4 us -> 16.8 us  [swap(): return lax.ppermute(values, axis, [(i, i ^ distance) for i in range(size)])]
  transfers between devices with their start and end apart: 16 -> 15, of which waited for: 5 -> 6; matrix products, arithmetic and copies ran while one was open for 5% -> 0% of each run, Pallas kernels for 30% -> 36%
where the time goes in v11:
time: 55.7 us; the launch traced here: 55.4 us
  Pallas kernels  24.7 us (44%)
  starting transfers between devices  16.8 us (30%)
  waiting for transfers between devices  12.4 us (22%)
  between operations  0.76 us (1%)
  local copies, waits for them, and re-layouts  0.69 us (1%)
    pallas_call x11, Pallas kernels, call(): pl.pallas_call(kernel, in_specs=in_specs, out_specs=[VMEM] * len(out_shap...  20.2 us
    ppermute x15, starting transfers between devices, swap(): return lax.ppermute(values, axis, [(i, i ^ distance) for i in range(size)])  16.8 us
    ppermute x15, waiting for transfers between devices, swap(): return lax.ppermute(values, axis, [(i, i ^ distance) for i in range(size)])  12.4 us
    pallas_call x1, Pallas kernels, early_templates(): pl.pallas_call(early_kernel, grid=(count,), in_specs=[pl.BlockSpec((2, ro...  4.54 us
  transfers between devices with their start and end apart: 15, of which 6 were waited for; matrix products, arithmetic and copies ran while one was open for 0% of the time, Pallas kernels for 36%

profile of v11, /device:TPU:0, one launch (start us, length us, event | category | flops | bytes accessed | tf_op | source)
XLA Modules:
  0.0 55.4 jit_solution(6984508693791578869)
XLA Ops:
  0.6 1.7 %weigh.1 = (bf16[32,4736]{1,0:T(8,128)(2,1)S(1)}, bf16[32,2432]{1,0:T(8,128)(2,1)S(1)}, bf16[32,2304]{1,0:T(8,128)(2,1)S(1)}) custom-call(s32[16]{0:T(128)} %ids_hbm.1, bf16[16,2,4608]{2,1,0:T(2,128)(2,1)} %p_hbm.1, f32[64,4608]{1,0:T(8,128)} %ctf_hbm.3, f32[4608]{0:T(1024)} %nw_hbm.3), custom_call_target="tpu_custom_call" | custom-call | flops 294912 | bytes 1179648 | tf_op jit(solution)/shard_map/weigh/pallas_call | solution.py:29
  2.4 3.1 %collective-permute-start.2 = (bf16[32,4736]{1,0:T(8,128)(2,1)S(1)}, bf16[32,4736]{1,0:T(8,128)(2,1)S(1)}, u32[]{:S(2)}, u32[]{:S(2)}) collective-permute-start(bf16[32,4736]{1,0:T(8,128)(2,1)S(1)} %get-tuple-element.34.refs_0_), channel_id=1, source_target_pairs={{0,4},{4,0},{8,12},{12,8},{1,5},{5,1},{9,13},{13,9},{2,6},{6,2},{1... | collective-permute-start | bytes 909320 | tf_op jit(solution)/shard_map/ppermute | solution.py:614
  5.4 2.6 %collective-permute-start = (bf16[32,2432]{1,0:T(8,128)(2,1)S(1)}, bf16[32,2432]{1,0:T(8,128)(2,1)S(1)}, u32[]{:S(2)}, u32[]{:S(2)}) collective-permute-start(bf16[32,2432]{1,0:T(8,128)(2,1)S(1)} %get-tuple-element.32), channel_id=1, source_target_pairs={{0,8},{4,12},{8,0},{12,4},{1,9},{5,13},{9,1},{13,5},{2,10},{6,14},... | collective-permute-start | bytes 466952 | tf_op jit(solution)/shard_map/ppermute | solution.py:614
  8.0 0.3 collective-permute-start.1
  8.4 0.0 copy-start.2
  8.4 0.7 %copy-done.2 = s32[24,2]{0,1:T(2,128)S(1)} copy-done((s32[24,2]{0,1:T(2,128)S(1)}, s32[24,2]{0,1:T(2,128)}, u32[]{:S(2)}) %copy-start.2) | copy-done | bytes 216
  9.0 4.8 %prepare.1 = (f32[24,4608]{1,0:T(8,128)S(1)}, f32[24,4608]{1,0:T(8,128)S(1)}, f32[32,64]{1,0:T(8,128)S(1)}, bf16[2,32,4608]{2,1,0:T(8,128)(2,1)S(1)}, f32[64,4608]{1,0:T(8,128)S(1)}) custom-call(s32[2,24]{1,0:T(2,128)S(1)} %bitcast.4, bf16[32,2,4608]{2,1,0:T(2,128)(2,1)} %cls_hbm.1, f32[64,4608]{1,0:T(8,128)} %ctf_hbm.3, f32[4608]{0:T(1024)} %nw_hbm.3), custom_call_target="tpu_custom_call" | custom-call | flops 226492416 | tf_op jit(solution)/shard_map/prepare/pallas_call | solution.py:29
  13.8 0.0 copy-start
  13.8 4.5 %early_templates.1.early_hbm = bf16[6,768,768]{2,1,0:T(8,128)(2,1)} custom-call(bf16[2,32,4608]{2,1,0:T(8,128)(2,1)S(1)} %get-tuple-element.39.cls_ref, f32[24,4608]{1,0:T(8,128)S(1)} %get-tuple-element.36.cos_ref, f32[24,4608]{1,0:T(8,128)S(1)} %get-tuple-element.37.sin_ref), custom_call_target="tpu_custom_call" | custom-call | flops 70778880 | bytes 7077888 | tf_op jit(solution)/shard_map/early_templates/pallas_call | solution.py:207
  18.4 3.1 %collective-permute-done.1.refs_3_ = bf16[32,2304]{1,0:T(8,128)(2,1)S(1)} collective-permute-done((bf16[32,2304]{1,0:T(8,128)(2,1)S(1)}, bf16[32,2304]{1,0:T(8,128)(2,1)S(1)}, u32[]{:S(2)}, u32[]{:S(2)}) %collective-permute-start.1) | collective-permute-done | bytes 147488 | tf_op jit(solution)/shard_map/ppermute | solution.py:614
  21.5 0.0 collective-permute-done.refs_2_.refs_3_
  21.5 0.0 collective-permute-done.2.refs_1_
  21.5 0.0 copy-done
  21.5 0.5 collective-permute-start.3
  22.1 0.1 pad_add_fusion.me_ref
  22.1 1.6 %collective-permute-start.4 = (bf16[32,2304]{1,0:T(8,128)(2,1)S(1)}, bf16[32,2304]{1,0:T(8,128)(2,1)S(1)}, u32[]{:S(2)}, u32[]{:S(2)}) collective-permute-start(bf16[32,2304]{1,0:T(8,128)(2,1)S(1)} %collective-permute-done.1.refs_3_), channel_id=1, source_target_pairs={{0,4},{4,0},{8,12},{12,8},{1,5},{5,1},{9,13},{13,9},{2,6},{6,2},{1... | collective-permute-start | bytes 442376 | tf_op jit(solution)/shard_map/ppermute | solution.py:614
  23.7 0.6 %cut_slices.2 = (bf16[96,1152]{1,0:T(8,128)(2,1)S(1)}, bf16[96,1152]{1,0:T(8,128)(2,1)S(1)}, bf16[96,1152]{1,0:T(8,128)(2,1)S(1)}, bf16[96,1152]{1,0:T(8,128)(2,1)S(1)}) custom-call(s32[2]{0:T(128)S(1)} %pad_add_fusion.me_ref, bf16[32,4736]{1,0:T(8,128)(2,1)S(1)} %get-tuple-element.34.refs_0_, bf16[32,4736]{1,0:T(8,128)(2,1)S(1)} %collective-permute-done.2.refs_1_, ...), custom_call_target="tpu_custom_call" | custom-call | bytes 1769472 | tf_op jit(solution)/shard_map/cut_slices/pallas_call | solution.py:29
  24.3 0.1 collective-permute-start.5
  24.4 1.6 %collective-permute-start.6 = (bf16[96,1152]{1,0:T(8,128)(2,1)S(1)}, bf16[96,1152]{1,0:T(8,128)(2,1)S(1)}, u32[]{:S(2)}, u32[]{:S(2)}) collective-permute-start(bf16[96,1152]{1,0:T(8,128)(2,1)S(1)} %get-tuple-element.49), channel_id=1, source_target_pairs={{0,2},{1,3},{2,0},{3,1},{4,6},{5,7},{6,4},{7,5},{8,10},{9,11},{10,... | collective-permute-start | bytes 663560 | tf_op jit(solution)/shard_map/ppermute | solution.py:614
  26.0 0.3 collective-permute-start.7
  26.3 3.1 %templates.1.temp_ref = bf16[12,768,768]{2,1,0:T(8,128)(2,1)S(1)} custom-call(bf16[6,768,768]{2,1,0:T(8,128)(2,1)} %early_templates.1.early_hbm, bf16[2,32,4608]{2,1,0:T(8,128)(2,1)S(1)} %get-tuple-element.39.cls_ref, f32[24,4608]{1,0:T(8,128)S(1)} %get-tuple-element.36.cos_ref, f32[24,4608]{1,0:T(8,128)S(1)} %get-tuple-element.37.sin_ref), custom_call_target="tpu_custom_call" | custom-call | flops 70778880 | bytes 7077888 | tf_op jit(solution)/shard_map/templates/pallas_call | solution.py:29
  29.4 0.0 collective-permute-done.3.refs_4_.refs_5_.refs_0_
  29.4 2.0 %score0.1.acc_ref = f32[768,128]{1,0:T(8,128)S(1)} custom-call(bf16[12,768,768]{2,1,0:T(8,128)(2,1)S(1)} %templates.1.temp_ref, bf16[32,4736]{1,0:T(8,128)(2,1)S(1)} %get-tuple-element.34.refs_0_, bf16[32,4736]{1,0:T(8,128)(2,1)S(1)} %collective-permute-done.2.refs_1_, bf16[32,2432]{1,0:T(8,128)(2,1)S(1)} %collective-permute-done.refs_2_.refs_3_, ...), custom_call_target="tpu_custom_call" | custom-call | flops 1811939328 | tf_op jit(solution)/shard_map/score0/pallas_call | solution.py:29
  31.4 0.0 collective-permute-done.4.refs_5_.refs_1_
  31.4 0.0 copy-start.1
  31.4 2.2 %score1.1 = (f32[768,128]{1,0:T(8,128)S(1)}, f32[128,64]{1,0:T(8,128)S(1)}, f32[8,128]{1,0:T(8,128)S(1)}) custom-call(bf16[12,768,768]{2,1,0:T(8,128)(2,1)S(1)} %templates.1.temp_ref, f32[32,64]{1,0:T(8,128)S(1)} %get-tuple-element.40.pow_ref, f32[768,128]{1,0:T(8,128)S(1)} %score0.1.acc_ref, bf16[32,4736]{1,0:T(8,128)(2,1)S(1)} %get-tuple-element.34.refs_0_, ...), custom_call_target="tpu_custom_call" | custom-call | flops 1811939328 | tf_op jit(solution)/shard_map/score1/pallas_call | solution.py:29
  33.6 0.0 collective-permute-done.5.refs_1_.refs_0_
  33.7 3.2 %collective-permute-done.6.refs_2_.refs_1_ = bf16[96,1152]{1,0:T(8,128)(2,1)S(1)} collective-permute-done((bf16[96,1152]{1,0:T(8,128)(2,1)S(1)}, bf16[96,1152]{1,0:T(8,128)(2,1)S(1)}, u32[]{:S(2)}, u32[]{:S(2)}) %collective-permute-start.6) | collective-permute-done | bytes 221216 | tf_op jit(solution)/shard_map/ppermute | solution.py:614
  36.9 0.0 collective-permute-done.7.refs_3_.refs_2_
  36.9 0.5 collective-permute-start.14
  37.4 1.6 %collective-permute-start.8 = (f32[8,128]{1,0:T(8,128)S(1)}, f32[8,128]{1,0:T(8,128)S(1)}, u32[]{:S(2)}, u32[]{:S(2)}) collective-permute-start(f32[8,128]{1,0:T(8,128)S(1)} %get-tuple-element.51.refs_0_), channel_id=1, source_target_pairs={{0,4},{4,0},{8,12},{12,8},{1,5},{5,1},{9,13},{13,9},{2,6},{6,2},{1... | collective-permute-start | bytes 12296 | tf_op jit(solution)/shard_map/ppermute | solution.py:614
  39.0 1.2 %collective-permute-start.9 = (f32[8,128]{1,0:T(8,128)S(1)}, f32[8,128]{1,0:T(8,128)S(1)}, u32[]{:S(2)}, u32[]{:S(2)}) collective-permute-start(f32[8,128]{1,0:T(8,128)S(1)} %get-tuple-element.51.refs_0_), channel_id=1, source_target_pairs={{0,8},{4,12},{8,0},{12,4},{1,9},{5,13},{9,1},{13,5},{2,10},{6,14},... | collective-permute-start | bytes 12296 | tf_op jit(solution)/shard_map/ppermute | solution.py:614
  40.2 1.6 %collective-permute-start.10 = (f32[8,128]{1,0:T(8,128)S(1)}, f32[8,128]{1,0:T(8,128)S(1)}, u32[]{:S(2)}, u32[]{:S(2)}) collective-permute-start(f32[8,128]{1,0:T(8,128)S(1)} %get-tuple-element.51.refs_0_), channel_id=1, source_target_pairs={{0,12},{4,8},{8,4},{12,0},{1,13},{5,9},{9,5},{13,1},{2,14},{6,10},... | collective-permute-start | bytes 12296 | tf_op jit(solution)/shard_map/ppermute | solution.py:614
  41.8 2.7 %collective-permute-done.8.refs_1_ = f32[8,128]{1,0:T(8,128)S(1)} collective-permute-done((f32[8,128]{1,0:T(8,128)S(1)}, f32[8,128]{1,0:T(8,128)S(1)}, u32[]{:S(2)}, u32[]{:S(2)}) %collective-permute-start.8) | collective-permute-done | bytes 4128 | tf_op jit(solution)/shard_map/ppermute | solution.py:614
  44.5 0.0 collective-permute-done.9.refs_2_
  44.5 1.0 %collective-permute-done.10.refs_3_ = f32[8,128]{1,0:T(8,128)S(1)} collective-permute-done((f32[8,128]{1,0:T(8,128)S(1)}, f32[8,128]{1,0:T(8,128)S(1)}, u32[]{:S(2)}, u32[]{:S(2)}) %collective-permute-start.10) | collective-permute-done | bytes 4128 | tf_op jit(solution)/shard_map/ppermute | solution.py:614
  45.6 0.5 responsibilities.1
  46.1 0.0 collective-permute-start.11
  46.1 0.7 %collective-permute-start.12 = (bf16[416,128]{1,0:T(8,128)(2,1)S(1)}, bf16[416,128]{1,0:T(8,128)(2,1)S(1)}, u32[]{:S(2)}, u32[]{:S(2)}) collective-permute-start(bf16[416,128]{1,0:T(8,128)(2,1)S(1)} %get-tuple-element.61.refs_0_), channel_id=1, source_target_pairs={{0,2},{1,3},{2,0},{3,1},{4,6},{5,7},{6,4},{7,5},{8,10},{9,11},{10,... | collective-permute-start | bytes 319496 | tf_op jit(solution)/shard_map/ppermute | solution.py:614
  46.8 1.1 %collective-permute-start.13 = (bf16[416,128]{1,0:T(8,128)(2,1)S(1)}, bf16[416,128]{1,0:T(8,128)(2,1)S(1)}, u32[]{:S(2)}, u32[]{:S(2)}) collective-permute-start(bf16[416,128]{1,0:T(8,128)(2,1)S(1)} %get-tuple-element.61.refs_0_), channel_id=1, source_target_pairs={{0,1},{1,0},{2,3},{3,2},{4,5},{5,4},{6,7},{7,6},{8,9},{9,8},{10,11... | collective-permute-start | bytes 319496 | tf_op jit(solution)/shard_map/ppermute | solution.py:614
  47.9 0.6 %cut_slices.3.refs_4_ = bf16[32,1152]{1,0:T(8,128)(2,1)S(1)} custom-call(s32[2]{0:T(128)S(1)} %pad_add_fusion.me_ref, bf16[32,2432]{1,0:T(8,128)(2,1)S(1)} %collective-permute-done.3.refs_4_.refs_5_.refs_0_, bf16[32,2304]{1,0:T(8,128)(2,1)S(1)} %collective-permute-done.4.refs_5_.refs_1_), custom_call_target="tpu_custom_call" | custom-call | bytes 147456 | tf_op jit(solution)/shard_map/cut_slices/pallas_call | solution.py:29
  48.5 0.0 copy-done.1
  48.5 1.5 %gather_rows.1 = (f32[32,64]{1,0:T(8,128)}, f32[64,1152]{1,0:T(8,128)S(1)}, bf16[2,192,1152]{2,1,0:T(8,128)(2,1)S(1)}) custom-call(s32[2]{0:T(128)S(1)} %pad_add_fusion.me_ref, f32[768,128]{1,0:T(8,128)S(1)} %get-tuple-element.44.s_ref, f32[1,128]{1,0:T(1,128)S(1)} %get-tuple-element.52.norm_ref, f32[64,4608]{1,0:T(8,128)S(1)} %copy-done.1, ...), custom_call_target="tpu_custom_call" | custom-call | flops 3932160 | bytes 1769472 | tf_op jit(solution)/shard_map/gather_rows/pallas_call | solution.py:29
  50.0 1.3 %collective-permute-done.11.refs_1_ = bf16[416,128]{1,0:T(8,128)(2,1)S(1)} collective-permute-done((bf16[416,128]{1,0:T(8,128)(2,1)S(1)}, bf16[416,128]{1,0:T(8,128)(2,1)S(1)}, u32[]{:S(2)}, u32[]{:S(2)}) %collective-permute-start.11) | collective-permute-done | bytes 106528 | tf_op jit(solution)/shard_map/ppermute | solution.py:614
  51.3 0.9 %collective-permute-done.12.refs_2_ = bf16[416,128]{1,0:T(8,128)(2,1)S(1)} collective-permute-done((bf16[416,128]{1,0:T(8,128)(2,1)S(1)}, bf16[416,128]{1,0:T(8,128)(2,1)S(1)}, u32[]{:S(2)}, u32[]{:S(2)}) %collective-permute-start.12) | collective-permute-done | bytes 106528 | tf_op jit(solution)/shard_map/ppermute | solution.py:614
  52.2 0.0 collective-permute-done.13.refs_3_
  52.2 0.0 collective-permute-done.14.refs_5_
  52.2 3.2 %finish.1 = f32[32,2,1152]{2,1,0:T(2,128)} custom-call(s32[2]{0:T(128)S(1)} %pad_add_fusion.me_ref, f32[64,1152]{1,0:T(8,128)S(1)} %get-tuple-element.59.cw_ref, f32[24,4608]{1,0:T(8,128)S(1)} %get-tuple-element.36.cos_ref, f32[24,4608]{1,0:T(8,128)S(1)} %get-tuple-element.37.sin_ref, bf16[2,192,1152]{2,1,0:T(8,128)(2,1)S(1)} %get-tuple-element.60.rows_ref, ...), custom_call_target="tpu_custom_call" | custom-call | flops 905969664 | tf_op jit(solution)/shard_map/finish/pallas_call | solution.py:29
  (1 shorter events, 0.0 us)
Async XLA Ops:
  2.4 19.2 %collective-permute-start.2 = (bf16[32,4736]{1,0:T(8,128)(2,1)S(1)}, bf16[32,4736]{1,0:T(8,128)(2,1)S(1)}, u32[]{:S(2)}, u32[]{:S(2)}) collective-permute-start(bf16[32,4736]{1,0:T(8,128)(2,1)S(1)} %get-tuple-element.34.refs_0_), channel_id=1, source_target_pairs={{0,4},{4,0},{8,12},{12,8},{1,5},{5,1},{9,13},{13,9},{2,6},{6,2},{1... | collective-permute-start | bytes 909320 | tf_op jit(solution)/shard_map/ppermute | solution.py:614
  5.4 16.1 %collective-permute-start = (bf16[32,2432]{1,0:T(8,128)(2,1)S(1)}, bf16[32,2432]{1,0:T(8,128)(2,1)S(1)}, u32[]{:S(2)}, u32[]{:S(2)}) collective-permute-start(bf16[32,2432]{1,0:T(8,128)(2,1)S(1)} %get-tuple-element.32), channel_id=1, source_target_pairs={{0,8},{4,12},{8,0},{12,4},{1,9},{5,13},{9,1},{13,5},{2,10},{6,14},... | collective-permute-start | bytes 466952 | tf_op jit(solution)/shard_map/ppermute | solution.py:614
  8.0 13.5 %collective-permute-start.1 = (bf16[32,2304]{1,0:T(8,128)(2,1)S(1)}, bf16[32,2304]{1,0:T(8,128)(2,1)S(1)}, u32[]{:S(2)}, u32[]{:S(2)}) collective-permute-start(bf16[32,2304]{1,0:T(8,128)(2,1)S(1)} %get-tuple-element.33), channel_id=1, source_target_pairs={{0,8},{4,12},{8,0},{12,4},{1,9},{5,13},{9,1},{13,5},{2,10},{6,14},... | collective-permute-start | bytes 442376 | tf_op jit(solution)/shard_map/ppermute | solution.py:614
  8.4 0.7 %copy-start.2 = (s32[24,2]{0,1:T(2,128)S(1)}, s32[24,2]{0,1:T(2,128)}, u32[]{:S(2)}) copy-start(s32[24,2]{0,1:T(2,128)} %param.11) | copy-start | bytes 580
  13.8 7.7 %copy-start = (f32[64,4608]{1,0:T(8,128)}, f32[64,4608]{1,0:T(8,128)S(1)}, u32[]{:S(2)}) copy-start(f32[64,4608]{1,0:T(8,128)S(1)} %get-tuple-element.53.weight_ref) | copy-start | bytes 3538948
  21.5 7.8 %collective-permute-start.3 = (bf16[32,2432]{1,0:T(8,128)(2,1)S(1)}, bf16[32,2432]{1,0:T(8,128)(2,1)S(1)}, u32[]{:S(2)}, u32[]{:S(2)}) collective-permute-start(bf16[32,2432]{1,0:T(8,128)(2,1)S(1)} %collective-permute-done.refs_2_.refs_3_), channel_id=1, source_target_pairs={{0,4},{4,0},{8,12},{12,8},{1,5},{5,1},{9,13},{13,9},{2,6},{6,2},{1... | collective-permute-start | bytes 466952 | tf_op jit(solution)/shard_map/ppermute | solution.py:614
  22.1 9.2 %collective-permute-start.4 = (bf16[32,2304]{1,0:T(8,128)(2,1)S(1)}, bf16[32,2304]{1,0:T(8,128)(2,1)S(1)}, u32[]{:S(2)}, u32[]{:S(2)}) collective-permute-start(bf16[32,2304]{1,0:T(8,128)(2,1)S(1)} %collective-permute-done.1.refs_3_), channel_id=1, source_target_pairs={{0,4},{4,0},{8,12},{12,8},{1,5},{5,1},{9,13},{13,9},{2,6},{6,2},{1... | collective-permute-start | bytes 442376 | tf_op jit(solution)/shard_map/ppermute | solution.py:614
  24.3 9.3 %collective-permute-start.5 = (bf16[96,1152]{1,0:T(8,128)(2,1)S(1)}, bf16[96,1152]{1,0:T(8,128)(2,1)S(1)}, u32[]{:S(2)}, u32[]{:S(2)}) collective-permute-start(bf16[96,1152]{1,0:T(8,128)(2,1)S(1)} %get-tuple-element.48), channel_id=1, source_target_pairs={{0,3},{1,2},{2,1},{3,0},{4,7},{5,6},{6,5},{7,4},{8,11},{9,10},{10,... | collective-permute-start | bytes 663560 | tf_op jit(solution)/shard_map/ppermute | solution.py:614
  24.4 12.5 %collective-permute-start.6 = (bf16[96,1152]{1,0:T(8,128)(2,1)S(1)}, bf16[96,1152]{1,0:T(8,128)(2,1)S(1)}, u32[]{:S(2)}, u32[]{:S(2)}) collective-permute-start(bf16[96,1152]{1,0:T(8,128)(2,1)S(1)} %get-tuple-element.49), channel_id=1, source_target_pairs={{0,2},{1,3},{2,0},{3,1},{4,6},{5,7},{6,4},{7,5},{8,10},{9,11},{10,... | collective-permute-start | bytes 663560 | tf_op jit(solution)/shard_map/ppermute | solution.py:614
  26.0 10.9 %collective-permute-start.7 = (bf16[96,1152]{1,0:T(8,128)(2,1)S(1)}, bf16[96,1152]{1,0:T(8,128)(2,1)S(1)}, u32[]{:S(2)}, u32[]{:S(2)}) collective-permute-start(bf16[96,1152]{1,0:T(8,128)(2,1)S(1)} %get-tuple-element.50), channel_id=1, source_target_pairs={{0,1},{1,0},{2,3},{3,2},{4,5},{5,4},{6,7},{7,6},{8,9},{9,8},{10,11... | collective-permute-start | bytes 663560 | tf_op jit(solution)/shard_map/ppermute | solution.py:614
  31.4 17.1 %copy-start.1 = (f32[64,4608]{1,0:T(8,128)S(1)}, f32[64,4608]{1,0:T(8,128)}, u32[]{:S(2)}) copy-start(f32[64,4608]{1,0:T(8,128)} %copy-done) | copy-start | bytes 3538948
  36.9 15.3 %collective-permute-start.14 = (bf16[96,1152]{1,0:T(8,128)(2,1)S(1)}, bf16[96,1152]{1,0:T(8,128)(2,1)S(1)}, u32[]{:S(2)}, u32[]{:S(2)}) collective-permute-start(bf16[96,1152]{1,0:T(8,128)(2,1)S(1)} %bundle.1), channel_id=1, source_target_pairs={{0,4},{4,0},{8,12},{12,8},{1,5},{5,1},{9,13},{13,9},{2,6},{6,2},{1... | collective-permute-start | bytes 663560 | tf_op jit(solution)/shard_map/ppermute | solution.py:614
  37.4 7.1 %collective-permute-start.8 = (f32[8,128]{1,0:T(8,128)S(1)}, f32[8,128]{1,0:T(8,128)S(1)}, u32[]{:S(2)}, u32[]{:S(2)}) collective-permute-start(f32[8,128]{1,0:T(8,128)S(1)} %get-tuple-element.51.refs_0_), channel_id=1, source_target_pairs={{0,4},{4,0},{8,12},{12,8},{1,5},{5,1},{9,13},{13,9},{2,6},{6,2},{1... | collective-permute-start | bytes 12296 | tf_op jit(solution)/shard_map/ppermute | solution.py:614
  39.0 5.6 %collective-permute-start.9 = (f32[8,128]{1,0:T(8,128)S(1)}, f32[8,128]{1,0:T(8,128)S(1)}, u32[]{:S(2)}, u32[]{:S(2)}) collective-permute-start(f32[8,128]{1,0:T(8,128)S(1)} %get-tuple-element.51.refs_0_), channel_id=1, source_target_pairs={{0,8},{4,12},{8,0},{12,4},{1,9},{5,13},{9,1},{13,5},{2,10},{6,14},... | collective-permute-start | bytes 12296 | tf_op jit(solution)/shard_map/ppermute | solution.py:614
  40.2 5.4 %collective-permute-start.10 = (f32[8,128]{1,0:T(8,128)S(1)}, f32[8,128]{1,0:T(8,128)S(1)}, u32[]{:S(2)}, u32[]{:S(2)}) collective-permute-start(f32[8,128]{1,0:T(8,128)S(1)} %get-tuple-element.51.refs_0_), channel_id=1, source_target_pairs={{0,12},{4,8},{8,4},{12,0},{1,13},{5,9},{9,5},{13,1},{2,14},{6,10},... | collective-permute-start | bytes 12296 | tf_op jit(solution)/shard_map/ppermute | solution.py:614
  46.1 5.2 %collective-permute-start.11 = (bf16[416,128]{1,0:T(8,128)(2,1)S(1)}, bf16[416,128]{1,0:T(8,128)(2,1)S(1)}, u32[]{:S(2)}, u32[]{:S(2)}) collective-permute-start(bf16[416,128]{1,0:T(8,128)(2,1)S(1)} %get-tuple-element.61.refs_0_), channel_id=1, source_target_pairs={{0,3},{1,2},{2,1},{3,0},{4,7},{5,6},{6,5},{7,4},{8,11},{9,10},{10,... | collective-permute-start | bytes 319496 | tf_op jit(solution)/shard_map/ppermute | solution.py:614
  46.1 6.1 %collective-permute-start.12 = (bf16[416,128]{1,0:T(8,128)(2,1)S(1)}, bf16[416,128]{1,0:T(8,128)(2,1)S(1)}, u32[]{:S(2)}, u32[]{:S(2)}) collective-permute-start(bf16[416,128]{1,0:T(8,128)(2,1)S(1)} %get-tuple-element.61.refs_0_), channel_id=1, source_target_pairs={{0,2},{1,3},{2,0},{3,1},{4,6},{5,7},{6,4},{7,5},{8,10},{9,11},{10,... | collective-permute-start | bytes 319496 | tf_op jit(solution)/shard_map/ppermute | solution.py:614
  46.8 5.4 %collective-permute-start.13 = (bf16[416,128]{1,0:T(8,128)(2,1)S(1)}, bf16[416,128]{1,0:T(8,128)(2,1)S(1)}, u32[]{:S(2)}, u32[]{:S(2)}) collective-permute-start(bf16[416,128]{1,0:T(8,128)(2,1)S(1)} %get-tuple-element.61.refs_0_), channel_id=1, source_target_pairs={{0,1},{1,0},{2,3},{3,2},{4,5},{5,4},{6,7},{7,6},{8,9},{9,8},{10,11... | collective-permute-start | bytes 319496 | tf_op jit(solution)/shard_map/ppermute | solution.py:614

commit v12 on v11

--- a/solution.py
+++ b/solution.py
@@ -11,6 +11,7 @@
 CHUNKS = 2
 LANES = 128
 VMEM_LIMIT = 24 * 1024 * 1024
+GATHER_FLOPS = 20_000_000_000
 
 prior_precision = 0.02
 
@@ -354,8 +355,8 @@
     whole_ref, refs = refs[-1], refs[:-1]
     shards, out_refs = regroup(refs[: -len(targets)], counts), refs[-len(targets) :]
     span = out_refs[0].shape[1]
-    at = 0
-    for refs in shards:
+    filled = [0] * len(targets)
+    for k, refs in enumerate(shards):
         source = refs[0]
         height = source.shape[0]
         if len(refs) > 1:
@@ -363,24 +364,26 @@
             for c, ref in enumerate(refs):
                 whole_ref[:, c * width : (c + 1) * width] = ref[:, :width]
             source = whole_ref
-        for out_ref, distance in zip(out_refs, targets):
-            base = pl.multiple_of((me_ref[0] ^ distance) * span, LANES)
-            out_ref[at : at + height, :] = source[:, pl.ds(base, span)]
-        at += height
+        for i, (distance, skip) in enumerate(targets):
+            if k >= skip:
+                base = pl.multiple_of((me_ref[0] ^ distance) * span, LANES)
+                out_refs[i][filled[i] : filled[i] + height, :] = source[:, pl.ds(base, span)]
+                filled[i] += height
 
 
 def cut_slices(me, shards, targets, span, freq):
-    height = sum(refs[0].shape[0] for refs in shards)
+    heights = [refs[0].shape[0] for refs in shards]
     operands = [me, *[ref for refs in shards for ref in refs]]
+    out_heights = [sum(heights[skip:]) for _, skip in targets]
     return call(
         functools.partial(slices_kernel, [len(refs) for refs in shards], targets),
         "cut_slices",
         [SMEM] + [VMEM] * (len(operands) - 1),
-        [jax.ShapeDtypeStruct((height, span), bf16)] * len(targets),
+        [jax.ShapeDtypeStruct((height, span), bf16) for height in out_heights],
         operands,
-        [pltpu.VMEM((shards[-1][0].shape[0], freq), bf16)],
-        moved=4 * height * span * len(targets),
-        limit=VMEM_LIMIT if height <= 128 else 2 * VMEM_LIMIT,
+        [pltpu.VMEM((heights[-1], freq), bf16)],
+        moved=4 * span * sum(out_heights),
+        limit=VMEM_LIMIT if sum(heights) <= 128 else 2 * VMEM_LIMIT,
     )
 
 
@@ -476,14 +479,14 @@
     )
 
 
-def gather_kernel(poses, half, sources, me_ref, s_ref, norm_ref, weight_ref, *refs):
+def gather_kernel(poses, half, counts, me_ref, s_ref, norm_ref, weight_ref, *refs):
     w_refs, (resp_ref, cw_ref, rows_ref) = refs[:-3], refs[-3:]
     span = rows_ref.shape[2]
     block = 2 * half
     here = pl.ds(pl.multiple_of(me_ref[0] * span, LANES), span)
     at = 0
-    for i in range(sources):
-        for ref in w_refs[i::sources]:
+    for refs in regroup(w_refs, counts):
+        for ref in refs:
             for start in range(0, ref.shape[0], block):
                 rows_ref[0, at : at + half, :] = ref[start : start + half, :]
                 rows_ref[1, at : at + half, :] = ref[start + half : start + block, :]
@@ -504,11 +507,13 @@
     )
 
 
-def gather_rows(me, scores, norm, weight, slices, sources, poses, half, span):
+def gather_rows(me, scores, norm, weight, slices, poses, half, span):
     columns, lanes = scores.shape
+    counts = [len(refs) for refs in slices]
+    slices = [w for refs in slices for w in refs]
     particles = sum(w.shape[0] for w in slices) // 2
     return call(
-        functools.partial(gather_kernel, poses, half, sources),
+        functools.partial(gather_kernel, poses, half, counts),
         "gather_rows",
         [SMEM] + [VMEM] * (3 + len(slices)),
         [
@@ -517,7 +522,7 @@
             jax.ShapeDtypeStruct((2, particles, span), bf16),
         ],
         (me, scores, norm, weight, *slices),
-        flops=40 * columns * lanes,
+        flops=GATHER_FLOPS,
         moved=8 * particles * span,
         limit=VMEM_LIMIT if particles <= 512 else 2 * VMEM_LIMIT,
     )
@@ -625,35 +630,38 @@
     me_cls = lax.axis_index("cls") if pairwise else 0
     me = jnp.stack([lax.axis_index("img"), me_cls]).astype(jnp.int32)
     others = tuple(range(n_img - 1, 0, -1))
-    targets = (0,) + others
-
-    def share(*shards):
-        mine, *outgoing = cut_slices(me, shards, targets, span, freq)
-        return [mine] + [swap(w, "img", d) for w, d in zip(outgoing, others)]
 
     own, *own_chunks = weigh(particles, ctf, noise_weight, group_ids)
     if pairwise:
         far = [swap(w, "cls", 2) for w in own_chunks]
         near = swap(own, "cls", 1)
+        mine, *outgoing = cut_slices(me, [[own]], [(d, 0) for d in (0,) + others[:-1]], span, freq)
+        slices = [mine] + [swap(w, "img", d) for w, d in zip(outgoing, others)]
     else:
         shards = [[lax.all_gather(own, "cls", axis=0, tiled=True)]]
-        slices = share(*shards)
+        mine, *outgoing = cut_slices(me, shards, [(d, 0) for d in (0,) + others], span, freq)
+        slices = [[w] for w in [mine] + [swap(w, "img", d) for w, d in zip(outgoing, others)]]
 
     cos_t, sin_t, power, split, weight = prepare(shifts, classes, ctf, noise_weight)
     early = early_templates(split, cos_t, sin_t)
     if pairwise:
-        far, near, split, early = lax.optimization_barrier((far, near, split, early))
+        far, near, slices, split, early = lax.optimization_barrier(
+            (far, near, slices, split, early)
+        )
         third = [swap(w, "cls", 1) for w in far]
-        slices = share([own], [near], far)
+        targets = [(d, 1) for d in (0,) + others[:-1]] + [(others[-1], 0)]
+        mine, *outgoing = cut_slices(me, [[own], [near], far], targets, span, freq)
+        arrived = [mine] + [swap(w, "img", d) for w, d in zip(outgoing, others)]
         shards = [[own], [near], far, third]
     temps = all_templates(early, split, cos_t, sin_t)
     scores, marks, stat = score(temps, power, shards, half)
     if pairwise:
-        stat, slices = lax.optimization_barrier((stat, slices))
+        stat, arrived[-1] = lax.optimization_barrier((stat, arrived[-1]))
         stats = [stat] + [swap(stat, "cls", k) for k in range(1, n_cls)]
         paired = tuple(range(n_cls))
-        last = [*cut_slices(me, [third], (0,), span, freq)]
-        last.append(swap(bundle(slices[1:], 2 * half), "cls", 1))
+        last = [*cut_slices(me, [third], [(0, 0)], span, freq)]
+        last.append(swap(bundle(arrived[1:], 2 * half), "cls", 1))
+        slices = [[a, b] for a, b in zip(slices, arrived)] + [arrived[-1:]]
     else:
         stats = [lax.all_gather(stat, "cls", axis=0, tiled=True)]
         paired = (0,)
@@ -661,7 +669,7 @@
     norm, payload = responsibilities(scores, marks, stats, paired, poses, half)
     payloads = [payload] + [swap(payload, "img", d) for d in others]
     log_resp, weight_here, rows = gather_rows(
-        me, scores, norm, weight, slices, n_img, poses, half, span
+        me, scores, norm, weight, slices, poses, half, span
     )
     averages = finish(me, weight_here, cos_t, sin_t, rows, payloads, last, cls_rows, half)
     return (log_resp.T, averages)

time: 55.7 us -> 53.8 us (0.966)
  waiting for transfers between devices: 12.4 us -> 8.53 us
  starting transfers between devices: 16.8 us -> 18.3 us
  Pallas kernels: 24.7 us -> 25.3 us
    ppermute x15 -> x17, waiting for transfers between devices: 12.4 us -> 8.53 us  [swap(): return lax.ppermute(values, axis, [(i, i ^ distance) for i in range(size)])]
    ppermute x15 -> x17, starting transfers between devices: 16.8 us -> 18.3 us  [swap(): return lax.ppermute(values, axis, [(i, i ^ distance) for i in range(size)])]
    pallas_call x11 -> x12, Pallas kernels: 20.2 us -> 20.8 us  [call(): pl.pallas_call(kernel, in_specs=in_specs, out_specs=[VMEM] * len(out_shap...]
  transfers between devices with their start and end apart: 15 -> 17, of which waited for: 6 -> 4; matrix products, arithmetic and copies ran while one was open for 0% -> 0% of each run, Pallas kernels for 36% -> 38%
where the time goes in v12:
time: 53.8 us; the launch traced here: 53.6 us
  Pallas kernels  25.3 us (47%)
  starting transfers between devices  18.3 us (34%)
  waiting for transfers between devices  8.53 us (16%)
  between operations  0.79 us (1%)
  local copies, waits for them, and re-layouts  0.68 us (1%)
    pallas_call x12, Pallas kernels, call(): pl.pallas_call(kernel, in_specs=in_specs, out_specs=[VMEM] * len(out_shap...  20.8 us
    ppermute x17, starting transfers between devices, swap(): return lax.ppermute(values, axis, [(i, i ^ distance) for i in range(size)])  18.3 us
    ppermute x17, waiting for transfers between devices, swap(): return lax.ppermute(values, axis, [(i, i ^ distance) for i in range(size)])  8.53 us
    pallas_call x1, Pallas kernels, early_templates(): pl.pallas_call(early_kernel, grid=(count,), in_specs=[pl.BlockSpec((2, ro...  4.51 us
  transfers between devices with their start and end apart: 17, of which 4 were waited for; matrix products, arithmetic and copies ran while one was open for 0% of the time, Pallas kernels for 38%

profile of v12, /device:TPU:0, one launch (start us, length us, event | category | flops | bytes accessed | tf_op | source)
XLA Modules:
  0.0 53.6 jit_solution(13921014334060680286)
XLA Ops:
  0.6 1.7 %weigh.1 = (bf16[32,4736]{1,0:T(8,128)(2,1)S(1)}, bf16[32,2432]{1,0:T(8,128)(2,1)S(1)}, bf16[32,2304]{1,0:T(8,128)(2,1)S(1)}) custom-call(s32[16]{0:T(128)} %ids_hbm.1, bf16[16,2,4608]{2,1,0:T(2,128)(2,1)} %p_hbm.1, f32[64,4608]{1,0:T(8,128)} %ctf_hbm.3, f32[4608]{0:T(1024)} %nw_hbm.3), custom_call_target="tpu_custom_call" | custom-call | flops 294912 | bytes 1179648 | tf_op jit(solution)/shard_map/weigh/pallas_call | solution.py:30
  2.4 3.1 %collective-permute-start.2 = (bf16[32,4736]{1,0:T(8,128)(2,1)S(1)}, bf16[32,4736]{1,0:T(8,128)(2,1)S(1)}, u32[]{:S(2)}, u32[]{:S(2)}) collective-permute-start(bf16[32,4736]{1,0:T(8,128)(2,1)S(1)} %get-tuple-element.37.refs_0_), channel_id=1, source_target_pairs={{0,4},{4,0},{8,12},{12,8},{1,5},{5,1},{9,13},{13,9},{2,6},{6,2},{1... | collective-permute-start | bytes 909320 | tf_op jit(solution)/shard_map/ppermute | solution.py:619
  5.4 2.6 %collective-permute-start = (bf16[32,2432]{1,0:T(8,128)(2,1)S(1)}, bf16[32,2432]{1,0:T(8,128)(2,1)S(1)}, u32[]{:S(2)}, u32[]{:S(2)}) collective-permute-start(bf16[32,2432]{1,0:T(8,128)(2,1)S(1)} %get-tuple-element.35), channel_id=1, source_target_pairs={{0,8},{4,12},{8,0},{12,4},{1,9},{5,13},{9,1},{13,5},{2,10},{6,14},... | collective-permute-start | bytes 466952 | tf_op jit(solution)/shard_map/ppermute | solution.py:619
  8.0 0.3 collective-permute-start.1
  8.4 0.1 pad_add_fusion.me_ref
  8.4 0.6 %cut_slices.3 = (bf16[32,1152]{1,0:T(8,128)(2,1)S(1)}, bf16[32,1152]{1,0:T(8,128)(2,1)S(1)}, bf16[32,1152]{1,0:T(8,128)(2,1)S(1)}) custom-call(s32[2]{0:T(128)S(1)} %pad_add_fusion.me_ref, bf16[32,4736]{1,0:T(8,128)(2,1)S(1)} %get-tuple-element.37.refs_0_), custom_call_target="tpu_custom_call" | custom-call | bytes 442368 | tf_op jit(solution)/shard_map/cut_slices/pallas_call | solution.py:30
  9.0 0.2 collective-permute-start.3
  9.2 1.5 %collective-permute-start.4 = (bf16[32,1152]{1,0:T(8,128)(2,1)S(1)}, bf16[32,1152]{1,0:T(8,128)(2,1)S(1)}, u32[]{:S(2)}, u32[]{:S(2)}) collective-permute-start(bf16[32,1152]{1,0:T(8,128)(2,1)S(1)} %get-tuple-element.40), channel_id=1, source_target_pairs={{0,2},{1,3},{2,0},{3,1},{4,6},{5,7},{6,4},{7,5},{8,10},{9,11},{10,... | collective-permute-start | bytes 221192 | tf_op jit(solution)/shard_map/ppermute | solution.py:619
  10.7 0.7 %copy-done = s32[24,2]{0,1:T(2,128)S(1)} copy-done((s32[24,2]{0,1:T(2,128)S(1)}, s32[24,2]{0,1:T(2,128)}, u32[]{:S(2)}) %copy-start) | copy-done | bytes 216
  11.3 4.8 %prepare.1 = (f32[24,4608]{1,0:T(8,128)S(1)}, f32[24,4608]{1,0:T(8,128)S(1)}, f32[32,64]{1,0:T(8,128)S(1)}, bf16[2,32,4608]{2,1,0:T(8,128)(2,1)S(1)}, f32[64,4608]{1,0:T(8,128)S(1)}) custom-call(s32[2,24]{1,0:T(2,128)S(1)} %bitcast.4, bf16[32,2,4608]{2,1,0:T(2,128)(2,1)} %cls_hbm.1, f32[64,4608]{1,0:T(8,128)} %ctf_hbm.3, f32[4608]{0:T(1024)} %nw_hbm.3), custom_call_target="tpu_custom_call" | custom-call | flops 226492416 | tf_op jit(solution)/shard_map/prepare/pallas_call | solution.py:30
  16.1 4.5 %early_templates.1.early_hbm = bf16[6,768,768]{2,1,0:T(8,128)(2,1)} custom-call(bf16[2,32,4608]{2,1,0:T(8,128)(2,1)S(1)} %get-tuple-element.45.cls_ref, f32[24,4608]{1,0:T(8,128)S(1)} %get-tuple-element.42.cos_ref, f32[24,4608]{1,0:T(8,128)S(1)} %get-tuple-element.43.sin_ref), custom_call_target="tpu_custom_call" | custom-call | flops 70778880 | bytes 7077888 | tf_op jit(solution)/shard_map/early_templates/pallas_call | solution.py:208
  20.6 0.0 collective-permute-done.3.refs_2_
  20.6 0.0 collective-permute-done.4.refs_4_
  20.6 0.9 %collective-permute-done.1.refs_3_ = bf16[32,2304]{1,0:T(8,128)(2,1)S(1)} collective-permute-done((bf16[32,2304]{1,0:T(8,128)(2,1)S(1)}, bf16[32,2304]{1,0:T(8,128)(2,1)S(1)}, u32[]{:S(2)}, u32[]{:S(2)}) %collective-permute-start.1) | collective-permute-done | bytes 147488 | tf_op jit(solution)/shard_map/ppermute | solution.py:619
  21.5 0.0 collective-permute-done.refs_2_.refs_3_
  21.5 0.0 collective-permute-done.2.refs_1_
  21.5 0.5 collective-permute-start.5
  22.0 1.6 %collective-permute-start.6 = (bf16[32,2304]{1,0:T(8,128)(2,1)S(1)}, bf16[32,2304]{1,0:T(8,128)(2,1)S(1)}, u32[]{:S(2)}, u32[]{:S(2)}) collective-permute-start(bf16[32,2304]{1,0:T(8,128)(2,1)S(1)} %collective-permute-done.1.refs_3_), channel_id=1, source_target_pairs={{0,4},{4,0},{8,12},{12,8},{1,5},{5,1},{9,13},{13,9},{2,6},{6,2},{1... | collective-permute-start | bytes 442376 | tf_op jit(solution)/shard_map/ppermute | solution.py:619
  23.6 0.6 %cut_slices.4 = (bf16[64,1152]{1,0:T(8,128)(2,1)S(1)}, bf16[64,1152]{1,0:T(8,128)(2,1)S(1)}, bf16[64,1152]{1,0:T(8,128)(2,1)S(1)}, bf16[96,1152]{1,0:T(8,128)(2,1)S(1)}) custom-call(s32[2]{0:T(128)S(1)} %pad_add_fusion.me_ref, bf16[32,4736]{1,0:T(8,128)(2,1)S(1)} %get-tuple-element.37.refs_0_, bf16[32,4736]{1,0:T(8,128)(2,1)S(1)} %collective-permute-done.2.refs_1_, ...), custom_call_target="tpu_custom_call" | custom-call | bytes 1327104 | tf_op jit(solution)/shard_map/cut_slices/pallas_call | solution.py:30
  24.2 0.1 collective-permute-start.7
  24.3 1.6 %collective-permute-start.11 = (bf16[64,1152]{1,0:T(8,128)(2,1)S(1)}, bf16[64,1152]{1,0:T(8,128)(2,1)S(1)}, u32[]{:S(2)}, u32[]{:S(2)}) collective-permute-start(bf16[64,1152]{1,0:T(8,128)(2,1)S(1)} %get-tuple-element.60), channel_id=1, source_target_pairs={{0,3},{1,2},{2,1},{3,0},{4,7},{5,6},{6,5},{7,4},{8,11},{9,10},{10,... | collective-permute-start | bytes 442376 | tf_op jit(solution)/shard_map/ppermute | solution.py:619
  25.9 0.5 collective-permute-start.12
  26.4 3.1 %templates.1.temp_ref = bf16[12,768,768]{2,1,0:T(8,128)(2,1)S(1)} custom-call(bf16[6,768,768]{2,1,0:T(8,128)(2,1)} %early_templates.1.early_hbm, bf16[2,32,4608]{2,1,0:T(8,128)(2,1)S(1)} %get-tuple-element.45.cls_ref, f32[24,4608]{1,0:T(8,128)S(1)} %get-tuple-element.42.cos_ref, f32[24,4608]{1,0:T(8,128)S(1)} %get-tuple-element.43.sin_ref), custom_call_target="tpu_custom_call" | custom-call | flops 70778880 | bytes 7077888 | tf_op jit(solution)/shard_map/templates/pallas_call | solution.py:30
  29.5 0.0 collective-permute-done.5.refs_4_.refs_5_.refs_0_
  29.5 2.0 %score0.1.acc_ref = f32[768,128]{1,0:T(8,128)S(1)} custom-call(bf16[12,768,768]{2,1,0:T(8,128)(2,1)S(1)} %templates.1.temp_ref, bf16[32,4736]{1,0:T(8,128)(2,1)S(1)} %get-tuple-element.37.refs_0_, bf16[32,4736]{1,0:T(8,128)(2,1)S(1)} %collective-permute-done.2.refs_1_, bf16[32,2432]{1,0:T(8,128)(2,1)S(1)} %collective-permute-done.refs_2_.refs_3_, ...), custom_call_target="tpu_custom_call" | custom-call | flops 1811939328 | tf_op jit(solution)/shard_map/score0/pallas_call | solution.py:30
  31.5 0.0 collective-permute-done.6.refs_5_.refs_1_
  31.5 2.3 %score1.1 = (f32[768,128]{1,0:T(8,128)S(1)}, f32[128,64]{1,0:T(8,128)S(1)}, f32[8,128]{1,0:T(8,128)S(1)}) custom-call(bf16[12,768,768]{2,1,0:T(8,128)(2,1)S(1)} %templates.1.temp_ref, f32[32,64]{1,0:T(8,128)S(1)} %get-tuple-element.46.pow_ref, f32[768,128]{1,0:T(8,128)S(1)} %score0.1.acc_ref, bf16[32,4736]{1,0:T(8,128)(2,1)S(1)} %get-tuple-element.37.refs_0_, ...), custom_call_target="tpu_custom_call" | custom-call | flops 1811939328 | tf_op jit(solution)/shard_map/score1/pallas_call | solution.py:30
  33.8 0.0 collective-permute-done.7.refs_6_.refs_2_
  33.8 0.5 collective-permute-start.8
  34.3 2.6 %collective-permute-start.9 = (f32[8,128]{1,0:T(8,128)S(1)}, f32[8,128]{1,0:T(8,128)S(1)}, u32[]{:S(2)}, u32[]{:S(2)}) collective-permute-start(f32[8,128]{1,0:T(8,128)S(1)} %get-tuple-element.54.refs_0_), channel_id=1, source_target_pairs={{0,8},{4,12},{8,0},{12,4},{1,9},{5,13},{9,1},{13,5},{2,10},{6,14},... | collective-permute-start | bytes 12296 | tf_op jit(solution)/shard_map/ppermute | solution.py:619
  36.9 1.4 %collective-permute-start.10 = (f32[8,128]{1,0:T(8,128)S(1)}, f32[8,128]{1,0:T(8,128)S(1)}, u32[]{:S(2)}, u32[]{:S(2)}) collective-permute-start(f32[8,128]{1,0:T(8,128)S(1)} %get-tuple-element.54.refs_0_), channel_id=1, source_target_pairs={{0,12},{4,8},{8,4},{12,0},{1,13},{5,9},{9,5},{13,1},{2,14},{6,10},... | collective-permute-start | bytes 12296 | tf_op jit(solution)/shard_map/ppermute | solution.py:619
  38.2 0.6 %cut_slices.5.refs_4_ = bf16[32,1152]{1,0:T(8,128)(2,1)S(1)} custom-call(s32[2]{0:T(128)S(1)} %pad_add_fusion.me_ref, bf16[32,2432]{1,0:T(8,128)(2,1)S(1)} %collective-permute-done.5.refs_4_.refs_5_.refs_0_, bf16[32,2304]{1,0:T(8,128)(2,1)S(1)} %collective-permute-done.6.refs_5_.refs_1_), custom_call_target="tpu_custom_call" | custom-call | bytes 147456 | tf_op jit(solution)/shard_map/cut_slices/pallas_call | solution.py:30
  38.8 0.0 collective-permute-done.11.refs_3_.refs_0_
  38.8 0.0 collective-permute-done.12.refs_5_.refs_1_
  38.9 0.1 collective-permute-start.16
  38.9 0.0 collective-permute-done.8.refs_1_
  38.9 0.0 collective-permute-done.9.refs_2_
  39.0 3.4 %collective-permute-done.10.refs_3_ = f32[8,128]{1,0:T(8,128)S(1)} collective-permute-done((f32[8,128]{1,0:T(8,128)S(1)}, f32[8,128]{1,0:T(8,128)S(1)}, u32[]{:S(2)}, u32[]{:S(2)}) %collective-permute-start.10) | collective-permute-done | bytes 4128 | tf_op jit(solution)/shard_map/ppermute | solution.py:619
  42.3 0.5 responsibilities.1
  42.8 0.0 collective-permute-start.13
  42.8 1.6 %collective-permute-start.14 = (bf16[416,128]{1,0:T(8,128)(2,1)S(1)}, bf16[416,128]{1,0:T(8,128)(2,1)S(1)}, u32[]{:S(2)}, u32[]{:S(2)}) collective-permute-start(bf16[416,128]{1,0:T(8,128)(2,1)S(1)} %get-tuple-element.67.refs_0_), channel_id=1, source_target_pairs={{0,2},{1,3},{2,0},{3,1},{4,6},{5,7},{6,4},{7,5},{8,10},{9,11},{10,... | collective-permute-start | bytes 319496 | tf_op jit(solution)/shard_map/ppermute | solution.py:619
  44.4 0.3 collective-permute-start.15
  44.7 1.5 %gather_rows.1 = (f32[32,64]{1,0:T(8,128)}, f32[64,1152]{1,0:T(8,128)S(1)}, bf16[2,192,1152]{2,1,0:T(8,128)(2,1)S(1)}) custom-call(s32[2]{0:T(128)S(1)} %pad_add_fusion.me_ref, f32[768,128]{1,0:T(8,128)S(1)} %get-tuple-element.50.s_ref, f32[1,128]{1,0:T(1,128)S(1)} %get-tuple-element.55.norm_ref, f32[64,4608]{1,0:T(8,128)S(1)} %get-tuple-element.56.weight_ref, ...), custom_call_target="tpu_custom_call" | custom-call | flops 20000000000 | bytes 1769472 | tf_op jit(solution)/shard_map/gather_rows/pallas_call | solution.py:30
  46.2 1.9 %collective-permute-done.13.refs_1_ = bf16[416,128]{1,0:T(8,128)(2,1)S(1)} collective-permute-done((bf16[416,128]{1,0:T(8,128)(2,1)S(1)}, bf16[416,128]{1,0:T(8,128)(2,1)S(1)}, u32[]{:S(2)}, u32[]{:S(2)}) %collective-permute-start.13) | collective-permute-done | bytes 106528 | tf_op jit(solution)/shard_map/ppermute | solution.py:619
  48.1 2.3 %collective-permute-done.14.refs_2_ = bf16[416,128]{1,0:T(8,128)(2,1)S(1)} collective-permute-done((bf16[416,128]{1,0:T(8,128)(2,1)S(1)}, bf16[416,128]{1,0:T(8,128)(2,1)S(1)}, u32[]{:S(2)}, u32[]{:S(2)}) %collective-permute-start.14) | collective-permute-done | bytes 106528 | tf_op jit(solution)/shard_map/ppermute | solution.py:619
  50.4 0.0 collective-permute-done.15.refs_3_
  50.4 0.0 collective-permute-done.16.refs_5_
  50.4 3.2 %finish.1 = f32[32,2,1152]{2,1,0:T(2,128)} custom-call(s32[2]{0:T(128)S(1)} %pad_add_fusion.me_ref, f32[64,1152]{1,0:T(8,128)S(1)} %get-tuple-element.65.cw_ref, f32[24,4608]{1,0:T(8,128)S(1)} %get-tuple-element.42.cos_ref, f32[24,4608]{1,0:T(8,128)S(1)} %get-tuple-element.43.sin_ref, bf16[2,192,1152]{2,1,0:T(8,128)(2,1)S(1)} %get-tuple-element.66.rows_ref, ...), custom_call_target="tpu_custom_call" | custom-call | flops 905969664 | tf_op jit(solution)/shard_map/finish/pallas_call | solution.py:30
  (2 shorter events, 0.0 us)
Async XLA Ops:
  2.4 19.2 %collective-permute-start.2 = (bf16[32,4736]{1,0:T(8,128)(2,1)S(1)}, bf16[32,4736]{1,0:T(8,128)(2,1)S(1)}, u32[]{:S(2)}, u32[]{:S(2)}) collective-permute-start(bf16[32,4736]{1,0:T(8,128)(2,1)S(1)} %get-tuple-element.37.refs_0_), channel_id=1, source_target_pairs={{0,4},{4,0},{8,12},{12,8},{1,5},{5,1},{9,13},{13,9},{2,6},{6,2},{1... | collective-permute-start | bytes 909320 | tf_op jit(solution)/shard_map/ppermute | solution.py:619
  5.4 16.1 %collective-permute-start = (bf16[32,2432]{1,0:T(8,128)(2,1)S(1)}, bf16[32,2432]{1,0:T(8,128)(2,1)S(1)}, u32[]{:S(2)}, u32[]{:S(2)}) collective-permute-start(bf16[32,2432]{1,0:T(8,128)(2,1)S(1)} %get-tuple-element.35), channel_id=1, source_target_pairs={{0,8},{4,12},{8,0},{12,4},{1,9},{5,13},{9,1},{13,5},{2,10},{6,14},... | collective-permute-start | bytes 466952 | tf_op jit(solution)/shard_map/ppermute | solution.py:619
  8.0 13.5 %collective-permute-start.1 = (bf16[32,2304]{1,0:T(8,128)(2,1)S(1)}, bf16[32,2304]{1,0:T(8,128)(2,1)S(1)}, u32[]{:S(2)}, u32[]{:S(2)}) collective-permute-start(bf16[32,2304]{1,0:T(8,128)(2,1)S(1)} %get-tuple-element.36), channel_id=1, source_target_pairs={{0,8},{4,12},{8,0},{12,4},{1,9},{5,13},{9,1},{13,5},{2,10},{6,14},... | collective-permute-start | bytes 442376 | tf_op jit(solution)/shard_map/ppermute | solution.py:619
  9.0 11.6 %collective-permute-start.3 = (bf16[32,1152]{1,0:T(8,128)(2,1)S(1)}, bf16[32,1152]{1,0:T(8,128)(2,1)S(1)}, u32[]{:S(2)}, u32[]{:S(2)}) collective-permute-start(bf16[32,1152]{1,0:T(8,128)(2,1)S(1)} %get-tuple-element.39), channel_id=1, source_target_pairs={{0,3},{1,2},{2,1},{3,0},{4,7},{5,6},{6,5},{7,4},{8,11},{9,10},{10,... | collective-permute-start | bytes 221192 | tf_op jit(solution)/shard_map/ppermute | solution.py:619
  9.2 11.5 %collective-permute-start.4 = (bf16[32,1152]{1,0:T(8,128)(2,1)S(1)}, bf16[32,1152]{1,0:T(8,128)(2,1)S(1)}, u32[]{:S(2)}, u32[]{:S(2)}) collective-permute-start(bf16[32,1152]{1,0:T(8,128)(2,1)S(1)} %get-tuple-element.40), channel_id=1, source_target_pairs={{0,2},{1,3},{2,0},{3,1},{4,6},{5,7},{6,4},{7,5},{8,10},{9,11},{10,... | collective-permute-start | bytes 221192 | tf_op jit(solution)/shard_map/ppermute | solution.py:619
  10.6 0.7 %copy-start = (s32[24,2]{0,1:T(2,128)S(1)}, s32[24,2]{0,1:T(2,128)}, u32[]{:S(2)}) copy-start(s32[24,2]{0,1:T(2,128)} %param.11) | copy-start | bytes 580
  21.5 8.0 %collective-permute-start.5 = (bf16[32,2432]{1,0:T(8,128)(2,1)S(1)}, bf16[32,2432]{1,0:T(8,128)(2,1)S(1)}, u32[]{:S(2)}, u32[]{:S(2)}) collective-permute-start(bf16[32,2432]{1,0:T(8,128)(2,1)S(1)} %collective-permute-done.refs_2_.refs_3_), channel_id=1, source_target_pairs={{0,4},{4,0},{8,12},{12,8},{1,5},{5,1},{9,13},{13,9},{2,6},{6,2},{1... | collective-permute-start | bytes 466952 | tf_op jit(solution)/shard_map/ppermute | solution.py:619
  22.0 9.5 %collective-permute-start.6 = (bf16[32,2304]{1,0:T(8,128)(2,1)S(1)}, bf16[32,2304]{1,0:T(8,128)(2,1)S(1)}, u32[]{:S(2)}, u32[]{:S(2)}) collective-permute-start(bf16[32,2304]{1,0:T(8,128)(2,1)S(1)} %collective-permute-done.1.refs_3_), channel_id=1, source_target_pairs={{0,4},{4,0},{8,12},{12,8},{1,5},{5,1},{9,13},{13,9},{2,6},{6,2},{1... | collective-permute-start | bytes 442376 | tf_op jit(solution)/shard_map/ppermute | solution.py:619
  24.2 9.6 %collective-permute-start.7 = (bf16[96,1152]{1,0:T(8,128)(2,1)S(1)}, bf16[96,1152]{1,0:T(8,128)(2,1)S(1)}, u32[]{:S(2)}, u32[]{:S(2)}) collective-permute-start(bf16[96,1152]{1,0:T(8,128)(2,1)S(1)} %get-tuple-element.53), channel_id=1, source_target_pairs={{0,1},{1,0},{2,3},{3,2},{4,5},{5,4},{6,7},{7,6},{8,9},{9,8},{10,11... | collective-permute-start | bytes 663560 | tf_op jit(solution)/shard_map/ppermute | solution.py:619
  24.3 14.6 %collective-permute-start.11 = (bf16[64,1152]{1,0:T(8,128)(2,1)S(1)}, bf16[64,1152]{1,0:T(8,128)(2,1)S(1)}, u32[]{:S(2)}, u32[]{:S(2)}) collective-permute-start(bf16[64,1152]{1,0:T(8,128)(2,1)S(1)} %get-tuple-element.60), channel_id=1, source_target_pairs={{0,3},{1,2},{2,1},{3,0},{4,7},{5,6},{6,5},{7,4},{8,11},{9,10},{10,... | collective-permute-start | bytes 442376 | tf_op jit(solution)/shard_map/ppermute | solution.py:619
  25.9 13.0 %collective-permute-start.12 = (bf16[64,1152]{1,0:T(8,128)(2,1)S(1)}, bf16[64,1152]{1,0:T(8,128)(2,1)S(1)}, u32[]{:S(2)}, u32[]{:S(2)}) collective-permute-start(bf16[64,1152]{1,0:T(8,128)(2,1)S(1)} %get-tuple-element.62), channel_id=1, source_target_pairs={{0,2},{1,3},{2,0},{3,1},{4,6},{5,7},{6,4},{7,5},{8,10},{9,11},{10,... | collective-permute-start | bytes 442376 | tf_op jit(solution)/shard_map/ppermute | solution.py:619
  33.8 5.2 %collective-permute-start.8 = (f32[8,128]{1,0:T(8,128)S(1)}, f32[8,128]{1,0:T(8,128)S(1)}, u32[]{:S(2)}, u32[]{:S(2)}) collective-permute-start(f32[8,128]{1,0:T(8,128)S(1)} %get-tuple-element.54.refs_0_), channel_id=1, source_target_pairs={{0,4},{4,0},{8,12},{12,8},{1,5},{5,1},{9,13},{13,9},{2,6},{6,2},{1... | collective-permute-start | bytes 12296 | tf_op jit(solution)/shard_map/ppermute | solution.py:619
  34.3 4.7 %collective-permute-start.9 = (f32[8,128]{1,0:T(8,128)S(1)}, f32[8,128]{1,0:T(8,128)S(1)}, u32[]{:S(2)}, u32[]{:S(2)}) collective-permute-start(f32[8,128]{1,0:T(8,128)S(1)} %get-tuple-element.54.refs_0_), channel_id=1, source_target_pairs={{0,8},{4,12},{8,0},{12,4},{1,9},{5,13},{9,1},{13,5},{2,10},{6,14},... | collective-permute-start | bytes 12296 | tf_op jit(solution)/shard_map/ppermute | solution.py:619
  36.9 5.5 %collective-permute-start.10 = (f32[8,128]{1,0:T(8,128)S(1)}, f32[8,128]{1,0:T(8,128)S(1)}, u32[]{:S(2)}, u32[]{:S(2)}) collective-permute-start(f32[8,128]{1,0:T(8,128)S(1)} %get-tuple-element.54.refs_0_), channel_id=1, source_target_pairs={{0,12},{4,8},{8,4},{12,0},{1,13},{5,9},{9,5},{13,1},{2,14},{6,10},... | collective-permute-start | bytes 12296 | tf_op jit(solution)/shard_map/ppermute | solution.py:619
  38.9 11.5 %collective-permute-start.16 = (bf16[96,1152]{1,0:T(8,128)(2,1)S(1)}, bf16[96,1152]{1,0:T(8,128)(2,1)S(1)}, u32[]{:S(2)}, u32[]{:S(2)}) collective-permute-start(bf16[96,1152]{1,0:T(8,128)(2,1)S(1)} %bundle.1), channel_id=1, source_target_pairs={{0,4},{4,0},{8,12},{12,8},{1,5},{5,1},{9,13},{13,9},{2,6},{6,2},{1... | collective-permute-start | bytes 663560 | tf_op jit(solution)/shard_map/ppermute | solution.py:619
  42.8 5.2 %collective-permute-start.13 = (bf16[416,128]{1,0:T(8,128)(2,1)S(1)}, bf16[416,128]{1,0:T(8,128)(2,1)S(1)}, u32[]{:S(2)}, u32[]{:S(2)}) collective-permute-start(bf16[416,128]{1,0:T(8,128)(2,1)S(1)} %get-tuple-element.67.refs_0_), channel_id=1, source_target_pairs={{0,3},{1,2},{2,1},{3,0},{4,7},{5,6},{6,5},{7,4},{8,11},{9,10},{10,... | collective-permute-start | bytes 319496 | tf_op jit(solution)/shard_map/ppermute | solution.py:619
  42.8 7.5 %collective-permute-start.14 = (bf16[416,128]{1,0:T(8,128)(2,1)S(1)}, bf16[416,128]{1,0:T(8,128)(2,1)S(1)}, u32[]{:S(2)}, u32[]{:S(2)}) collective-permute-start(bf16[416,128]{1,0:T(8,128)(2,1)S(1)} %get-tuple-element.67.refs_0_), channel_id=1, source_target_pairs={{0,2},{1,3},{2,0},{3,1},{4,6},{5,7},{6,4},{7,5},{8,10},{9,11},{10,... | collective-permute-start | bytes 319496 | tf_op jit(solution)/shard_map/ppermute | solution.py:619
  44.4 6.0 %collective-permute-start.15 = (bf16[416,128]{1,0:T(8,128)(2,1)S(1)}, bf16[416,128]{1,0:T(8,128)(2,1)S(1)}, u32[]{:S(2)}, u32[]{:S(2)}) collective-permute-start(bf16[416,128]{1,0:T(8,128)(2,1)S(1)} %get-tuple-element.67.refs_0_), channel_id=1, source_target_pairs={{0,1},{1,0},{2,3},{3,2},{4,5},{5,4},{6,7},{7,6},{8,9},{9,8},{10,11... | collective-permute-start | bytes 319496 | tf_op jit(solution)/shard_map/ppermute | solution.py:619

commit v13 on v12

--- a/solution.py
+++ b/solution.py
@@ -103,15 +103,15 @@
 
 
 def prepare_kernel(
-    shifts_ref, cls_hbm, ctf_hbm, nw_hbm, cos_ref, sin_ref, pow_ref, split_ref, cw_ref, *scratch
+    shifts_ref, cls_ref, ctf_hbm, nw_hbm, cos_ref, sin_ref, pow_ref, cw_ref, *scratch
 ):
-    cls_ref, ctf_ref, nw_ref, angle_ref, sem = scratch
-    rows, _, freq = cls_ref.shape
+    ctf_ref, nw_ref, angle_ref, sem = scratch
+    freq = cls_ref.shape[2]
     poses = cos_ref.shape[0]
     copies = [
         pltpu.make_async_copy(source, target, sem.at[i])
         for i, (source, target) in enumerate(
-            [(cls_hbm, cls_ref), (ctf_hbm, ctf_ref), (nw_hbm, nw_ref)]
+            [(ctf_hbm, ctf_ref), (nw_hbm, nw_ref)]
         )
     ]
     for copy in copies:
@@ -135,10 +135,8 @@
     power = jnp.zeros(pow_ref.shape, f32)
     for q in range(4):
         at = slice(q * cut, (q + 1) * cut)
-        values = cls_ref[:, :, at].astype(f32)
-        re, im = values[:, 0, :], values[:, 1, :]
-        split_ref[0, :, at] = re.astype(bf16)
-        split_ref[1, :, at] = im.astype(bf16)
+        re = cls_ref[0, :, at].astype(f32)
+        im = cls_ref[1, :, at].astype(f32)
         ctf = ctf_ref[:, at]
         weight = ctf * ctf * noise[:, at]
         cw_ref[:, at] = weight
@@ -148,30 +146,29 @@
     pow_ref[...] = power
 
 
-def prepare(shifts, classes, ctf, noise_weight):
-    rows, _, freq = classes.shape
+def prepare(shifts, split, ctf, noise_weight):
+    _, rows, freq = split.shape
     poses, groups = shifts.shape[0], ctf.shape[0]
     return call(
         prepare_kernel,
         "prepare",
-        [SMEM, ANY, ANY, ANY],
+        [SMEM, VMEM, ANY, ANY],
         [
             jax.ShapeDtypeStruct((poses, freq), f32),
             jax.ShapeDtypeStruct((poses, freq), f32),
             jax.ShapeDtypeStruct((rows, groups), f32),
-            jax.ShapeDtypeStruct((2, rows, freq), bf16),
             jax.ShapeDtypeStruct((groups, freq), f32),
         ],
         (
             shifts.T,
-            *[pltpu.with_memory_space_constraint(x, pltpu.HBM) for x in (classes, ctf, noise_weight)],
+            split,
+            *[pltpu.with_memory_space_constraint(x, pltpu.HBM) for x in (ctf, noise_weight)],
         ),
         [
-            pltpu.VMEM(classes.shape, bf16),
             pltpu.VMEM(ctf.shape, f32),
             pltpu.VMEM((freq,), f32),
             pltpu.VMEM((2, poses, BOX), f32),
-            pltpu.SemaphoreType.DMA((3,)),
+            pltpu.SemaphoreType.DMA((2,)),
         ],
         flops=24 * rows * groups * freq,
     )
@@ -223,78 +220,58 @@
     )(split, cos_t, sin_t)
 
 
-def template_kernel(early_hbm, cls_ref, cos_ref, sin_ref, temp_ref, sem):
-    count = early_hbm.shape[0]
-    built = temp_ref.shape[0] - count
-    tile = temp_ref.shape[2] // 2
+def regroup(refs, counts):
+    refs = list(refs)
+    return [[refs.pop(0) for _ in range(count)] for count in counts]
+
+
+def tile_of_particles(shards, chunk, span, t, tile, half):
+    cuts = []
+    for ref, chunked in shards:
+        at = t * tile if chunked else chunk * span + t * tile
+        cuts.append(ref[:, at : at + tile])
+    wide = jnp.concatenate(cuts, axis=0).astype(f32)
+    real = real_index(wide.shape, 0, half)
+    return jnp.concatenate(
+        [jnp.where(real, wide, 0.0).astype(bf16), jnp.where(real, 0.0, wide).astype(bf16)], axis=1
+    )
+
+
+def first_score_kernel(chunked, half, early_hbm, cls_ref, cos_ref, sin_ref, *refs):
+    refs, (acc_ref, late_ref, *buffers, sem) = refs[:-5], refs[-5:]
+    count, _, width = late_ref.shape
+    tile = width // 2
     copies = [
-        pltpu.make_async_copy(early_hbm.at[t], temp_ref.at[built + t], sem.at[t])
-        for t in range(count)
+        pltpu.make_async_copy(early_hbm.at[t], late_ref.at[t], sem.at[t]) for t in range(count)
     ]
     for copy in copies:
         copy.start()
-
-    @pl.loop(0, built)
-    def _(t):
-        write_templates(cls_ref, cos_ref, sin_ref, temp_ref.at[t], t * tile, tile)
-
+    shards = list(zip(refs, chunked))
+    built = cls_ref.shape[2] // tile - count
+    acc_ref[...] = jnp.zeros_like(acc_ref)
+    write_templates(cls_ref, cos_ref, sin_ref, buffers[0], 0, tile)
+    for t in range(built):
+        if t + 1 < built:
+            write_templates(cls_ref, cos_ref, sin_ref, buffers[(t + 1) % 2], (t + 1) * tile, tile)
+        acc_ref[...] += lax.dot_general(
+            buffers[t % 2][...],
+            tile_of_particles(shards, 0, built * tile, t, tile, half),
+            NT,
+            preferred_element_type=f32,
+        )
     for copy in copies:
         copy.wait()
 
 
-def all_templates(early, split, cos_t, sin_t):
-    _, rows, freq = split.shape
-    poses = cos_t.shape[0]
-    count, columns, width = early.shape
-    return call(
-        template_kernel,
-        "templates",
-        [ANY] + [VMEM] * 3,
-        [pltpu.VMEM((freq // (width // 2), columns, width), bf16)],
-        (pltpu.with_memory_space_constraint(early, pltpu.HBM), split, cos_t, sin_t),
-        [pltpu.SemaphoreType.DMA((count,))],
-        flops=20 * poses * rows * freq,
-        moved=2 * poses * rows * freq,
-    )[0]
-
-
-def add_products(acc_ref, temp_ref, chunk, shards, half):
-    count = temp_ref.shape[0] // CHUNKS
-    tile = temp_ref.shape[2] // 2
-    real = real_index((acc_ref.shape[1], tile), 0, half)
-    for t in range(count):
-        cuts = []
-        for refs in shards:
-            ref, at = (refs[0], chunk * count * tile) if len(refs) == 1 else (refs[chunk], 0)
-            cuts.append(ref[:, at + t * tile : at + (t + 1) * tile])
-        wide = jnp.concatenate(cuts, axis=0).astype(f32)
-        split = jnp.concatenate(
-            [jnp.where(real, wide, 0.0).astype(bf16), jnp.where(real, 0.0, wide).astype(bf16)],
-            axis=1,
-        )
-        acc_ref[...] += lax.dot_general(
-            temp_ref[chunk * count + t], split, NT, preferred_element_type=f32
-        )
-
-
-def regroup(refs, counts):
-    refs = list(refs)
-    return [[refs.pop(0) for _ in range(count)] for count in counts]
-
-
-def score_kernel(chunk, counts, half, temp_ref, *refs):
-    *refs, acc_ref = refs
-    acc_ref[...] = jnp.zeros_like(acc_ref) if chunk == 0 else refs.pop(0)[...]
-    add_products(acc_ref, temp_ref, chunk, regroup(refs, counts), half)
-
-
-def last_score_kernel(counts, half, temp_ref, pow_ref, acc_ref, *refs):
+def last_score_kernel(chunked, half, temp_ref, pow_ref, acc_ref, *refs):
     refs, (s_ref, marks_ref, stat_ref) = refs[:-3], refs[-3:]
-    shards = regroup(refs, counts)
+    tail_refs, shards = refs[: len(chunked)], list(zip(refs[len(chunked) :], chunked))
+    count, _, width = temp_ref.shape
+    tile = width // 2
     rows, groups = pow_ref.shape
     lanes = s_ref.shape[1]
     poses = s_ref.shape[0] // rows
-    tails = [refs[0][:, refs[0].shape[1] - LANES :] for refs in shards]
+    tails = [ref[:, ref.shape[1] - LANES :] for ref in tail_refs]
     ids = jnp.concatenate(tails, axis=0).astype(f32)
     group = lax.broadcasted_iota(jnp.int32, (lanes, groups), 1).astype(f32)
     marks = (ids[:, :groups] == group).astype(f32)
@@ -303,7 +280,13 @@
         pow_ref[...], marks, NT, precision=HIGHEST, preferred_element_type=f32
     )
     s_ref[...] = acc_ref[...]
-    add_products(s_ref, temp_ref, CHUNKS - 1, shards, half)
+    for t in range(count):
+        s_ref[...] += lax.dot_general(
+            temp_ref[t],
+            tile_of_particles(shards, 1, count * tile, t, tile, half),
+            NT,
+            preferred_element_type=f32,
+        )
     acc = s_ref[...]
     acc = acc + jnp.where(
         real_index(acc.shape, 1, half), pltpu.roll(acc, lanes - half, 1), pltpu.roll(acc, half, 1)
@@ -317,29 +300,31 @@
     stat_ref[2:8, :] = jnp.zeros((6, lanes), f32)
 
 
-def score(temps, power, shards, half):
-    count, columns, width = temps.shape
+def score(early, split, cos_t, sin_t, power, shards, half):
+    count, columns, width = early.shape
     lanes = sum(refs[0].shape[0] for refs in shards)
-    flops = 2 * columns * 256 * count * width // CHUNKS
+    chunked = [len(refs) > 1 for refs in shards]
+    flops = 2 * columns * 256 * count * width
     acc_shape = jax.ShapeDtypeStruct((columns, lanes), f32)
-    acc = []
-    for c in range(CHUNKS - 1):
-        counts = [1 if len(refs) == 1 else CHUNKS for refs in shards]
-        operands = [temps, *acc]
-        for refs in shards:
-            operands += refs if len(refs) == 1 else [refs[c]] * CHUNKS
-        acc = call(
-            functools.partial(score_kernel, c, counts, half),
-            f"score{c}",
-            [VMEM] * len(operands),
-            [acc_shape],
-            operands,
-            flops=flops,
-        )
-    operands = [temps, power, *acc, *[ref for refs in shards for ref in refs]]
-    return call(
-        functools.partial(last_score_kernel, [len(refs) for refs in shards], half),
-        f"score{CHUNKS - 1}",
+    operands = [pltpu.with_memory_space_constraint(early, pltpu.HBM), split, cos_t, sin_t]
+    operands += [refs[0] for refs in shards]
+    acc, late = call(
+        functools.partial(first_score_kernel, chunked, half),
+        "score0",
+        [ANY] + [VMEM] * (len(operands) - 1),
+        [acc_shape, pltpu.VMEM(early.shape, bf16)],
+        operands,
+        [
+            pltpu.VMEM((columns, width), bf16),
+            pltpu.VMEM((columns, width), bf16),
+            pltpu.SemaphoreType.DMA((count,)),
+        ],
+        flops=4 * flops,
+    )
+    operands = [late, power, acc, *[refs[0] for refs in shards], *[refs[-1] for refs in shards]]
+    return call(
+        functools.partial(last_score_kernel, chunked, half),
+        "score1",
         [VMEM] * len(operands),
         [
             acc_shape,
@@ -491,7 +476,10 @@
                 rows_ref[0, at : at + half, :] = ref[start : start + half, :]
                 rows_ref[1, at : at + half, :] = ref[start + half : start + block, :]
                 at += half
-    cw_ref[...] = weight_ref[:, here]
+    weight = weight_ref[:, here]
+    high = weight.astype(bf16)
+    cw_ref[:, :span] = high
+    cw_ref[:, span:] = (weight - high.astype(f32)).astype(bf16)
     rows = resp_ref.shape[0]
     lanes = s_ref.shape[1]
     scores = s_ref[...].reshape(poses, rows, lanes)
@@ -518,7 +506,7 @@
         [SMEM] + [VMEM] * (3 + len(slices)),
         [
             jax.ShapeDtypeStruct((columns // poses, lanes // 2), f32),
-            jax.ShapeDtypeStruct((weight.shape[0], span), f32),
+            jax.ShapeDtypeStruct((weight.shape[0], 2 * span), bf16),
             jax.ShapeDtypeStruct((2, particles, span), bf16),
         ],
         (me, scores, norm, weight, *slices),
@@ -530,7 +518,7 @@
 
 def finish_kernel(poses, groups, sources, half, me_ref, cw_ref, cos_ref, sin_ref, rows_ref, *refs):
     payloads, refs = refs[:sources], refs[sources:]
-    last, (out_ref, rho_ref, denom_ref, *buffers) = refs[:-5], refs[-5:]
+    last, (out_ref, rho_ref, inverse_ref, *buffers) = refs[:-5], refs[-5:]
     rows, _, span = out_ref.shape
     cut = poses // 2 * rows
     count = payloads[0].shape[1] // 2
@@ -539,10 +527,11 @@
         rho_ref[:cut, i * count : (i + 1) * count] = ref[:cut, :count]
         rho_ref[cut:, i * count : (i + 1) * count] = ref[:cut, count:]
         mass += ref[cut:, :groups].astype(f32) + ref[cut:, groups : 2 * groups].astype(f32)
-    denom_ref[...] = (
-        lax.dot_general(mass, cw_ref[...], NN, precision=HIGHEST, preferred_element_type=f32)
-        + prior_precision
-    )
+    high = mass.astype(bf16)
+    mass = jnp.concatenate([high, (mass - high.astype(f32)).astype(bf16)], axis=0)
+    terms = jnp.dot(mass, cw_ref[...], preferred_element_type=f32)
+    denom = (terms[:rows, :span] + terms[rows:, :span]) + (terms[:rows, span:] + terms[rows:, span:])
+    inverse_ref[...] = 1.0 / (denom + prior_precision)
     tiles = [(a, min(256, span - a)) for a in range(0, span, 256)]
     known = rows_ref.shape[1] // sources
 
@@ -582,9 +571,9 @@
                 numer_re = numer_re + s_re * cos_r + s_im * sin_r
                 numer_im = numer_im + s_im * cos_r - s_re * sin_r
             here = slice(start + a, start + a + LANES)
-            denom = denom_ref[:, here]
-            out_ref[:, 0, here] = numer_re / denom
-            out_ref[:, 1, here] = numer_im / denom
+            inverse = inverse_ref[:, here]
+            out_ref[:, 0, here] = numer_re * inverse
+            out_ref[:, 1, here] = numer_im * inverse
 
     products(0)
     for i in range(1, len(tiles)):
@@ -642,7 +631,8 @@
         mine, *outgoing = cut_slices(me, shards, [(d, 0) for d in (0,) + others], span, freq)
         slices = [[w] for w in [mine] + [swap(w, "img", d) for w, d in zip(outgoing, others)]]
 
-    cos_t, sin_t, power, split, weight = prepare(shifts, classes, ctf, noise_weight)
+    split = jnp.transpose(classes, (1, 0, 2))
+    cos_t, sin_t, power, weight = prepare(shifts, split, ctf, noise_weight)
     early = early_templates(split, cos_t, sin_t)
     if pairwise:
         far, near, slices, split, early = lax.optimization_barrier(
@@ -653,8 +643,7 @@
         mine, *outgoing = cut_slices(me, [[own], [near], far], targets, span, freq)
         arrived = [mine] + [swap(w, "img", d) for w, d in zip(outgoing, others)]
         shards = [[own], [near], far, third]
-    temps = all_templates(early, split, cos_t, sin_t)
-    scores, marks, stat = score(temps, power, shards, half)
+    scores, marks, stat = score(early, split, cos_t, sin_t, power, shards, half)
     if pairwise:
         stat, arrived[-1] = lax.optimization_barrier((stat, arrived[-1]))
         stats = [stat] + [swap(stat, "cls", k) for k in range(1, n_cls)]

time: 53.8 us -> 55.9 us (1.039)
  waiting for transfers between devices: 8.53 us -> 10.6 us
  Pallas kernels: 25.3 us -> 24.1 us
  local copies, waits for them, and re-layouts: 0.68 us -> 1.8 us
    ppermute x17, waiting for transfers between devices: 8.53 us -> 10.6 us  [swap(): return lax.ppermute(values, axis, [(i, i ^ distance) for i in range(size)])]
    pallas_call x12 -> x11, Pallas kernels: 20.8 us -> 19.6 us  [call(): pl.pallas_call(kernel, in_specs=in_specs, out_specs=[VMEM] * len(out_shap...]
    unnamed x2 -> x3, local copies, waits for them, and re-layouts: 0.68 us -> 1.8 us
  transfers between devices with their start and end apart: 17 -> 17, of which waited for: 4 -> 5; matrix products, arithmetic and copies ran while one was open for 0% -> 2% of each run, Pallas kernels for 38% -> 35%
where the time goes in v13:
time: 55.9 us; the launch traced here: 55.6 us
  Pallas kernels  24.1 us (43%)
  starting transfers between devices  18.3 us (33%)
  waiting for transfers between devices  10.6 us (19%)
  local copies, waits for them, and re-layouts  1.8 us (3%)
  between operations  0.78 us (1%)
    pallas_call x11, Pallas kernels, call(): pl.pallas_call(kernel, in_specs=in_specs, out_specs=[VMEM] * len(out_shap...  19.6 us
    ppermute x17, starting transfers between devices, swap(): return lax.ppermute(values, axis, [(i, i ^ distance) for i in range(size)])  18.3 us
    ppermute x17, waiting for transfers between devices, swap(): return lax.ppermute(values, axis, [(i, i ^ distance) for i in range(size)])  10.6 us
    pallas_call x1, Pallas kernels, early_templates(): pl.pallas_call(early_kernel, grid=(count,), in_specs=[pl.BlockSpec((2, ro...  4.53 us
    unnamed x3, local copies, waits for them, and re-layouts  1.8 us
  transfers between devices with their start and end apart: 17, of which 5 were waited for; matrix products, arithmetic and copies ran while one was open for 2% of the time, Pallas kernels for 35%

profile of v13, /device:TPU:0, one launch (start us, length us, event | category | flops | bytes accessed | tf_op | source)
XLA Modules:
  0.0 55.6 jit_solution(5150201178034126657)
XLA Ops:
  0.6 1.7 %weigh.1 = (bf16[32,4736]{1,0:T(8,128)(2,1)S(1)}, bf16[32,2432]{1,0:T(8,128)(2,1)S(1)}, bf16[32,2304]{1,0:T(8,128)(2,1)S(1)}) custom-call(s32[16]{0:T(128)} %ids_hbm.1, bf16[16,2,4608]{2,1,0:T(2,128)(2,1)} %p_hbm.1, f32[64,4608]{1,0:T(8,128)} %ctf_hbm.3, f32[4608]{0:T(1024)} %nw_hbm.3), custom_call_target="tpu_custom_call" | custom-call | flops 294912 | bytes 1179648 | tf_op jit(solution)/shard_map/weigh/pallas_call | solution.py:30
  2.4 3.1 %collective-permute-start.2 = (bf16[32,4736]{1,0:T(8,128)(2,1)S(1)}, bf16[32,4736]{1,0:T(8,128)(2,1)S(1)}, u32[]{:S(2)}, u32[]{:S(2)}) collective-permute-start(bf16[32,4736]{1,0:T(8,128)(2,1)S(1)} %get-tuple-element.38.refs_0_.refs_4_), channel_id=1, source_target_pairs={{0,4},{4,0},{8,12},{12,8},{1,5},{5,1},{9,13},{13,9},{2,6},{6,2},{1... | collective-permute-start | bytes 909320 | tf_op jit(solution)/shard_map/ppermute | solution.py:608
  5.4 2.6 %collective-permute-start = (bf16[32,2432]{1,0:T(8,128)(2,1)S(1)}, bf16[32,2432]{1,0:T(8,128)(2,1)S(1)}, u32[]{:S(2)}, u32[]{:S(2)}) collective-permute-start(bf16[32,2432]{1,0:T(8,128)(2,1)S(1)} %get-tuple-element.36), channel_id=1, source_target_pairs={{0,8},{4,12},{8,0},{12,4},{1,9},{5,13},{9,1},{13,5},{2,10},{6,14},... | collective-permute-start | bytes 466952 | tf_op jit(solution)/shard_map/ppermute | solution.py:608
  8.0 0.3 collective-permute-start.1
  8.4 0.1 pad_add_fusion.me_ref
  8.4 0.6 %cut_slices.3 = (bf16[32,1152]{1,0:T(8,128)(2,1)S(1)}, bf16[32,1152]{1,0:T(8,128)(2,1)S(1)}, bf16[32,1152]{1,0:T(8,128)(2,1)S(1)}) custom-call(s32[2]{0:T(128)S(1)} %pad_add_fusion.me_ref, bf16[32,4736]{1,0:T(8,128)(2,1)S(1)} %get-tuple-element.38.refs_0_.refs_4_), custom_call_target="tpu_custom_call" | custom-call | bytes 442368 | tf_op jit(solution)/shard_map/cut_slices/pallas_call | solution.py:30
  9.0 0.2 collective-permute-start.3
  9.2 1.5 %collective-permute-start.4 = (bf16[32,1152]{1,0:T(8,128)(2,1)S(1)}, bf16[32,1152]{1,0:T(8,128)(2,1)S(1)}, u32[]{:S(2)}, u32[]{:S(2)}) collective-permute-start(bf16[32,1152]{1,0:T(8,128)(2,1)S(1)} %get-tuple-element.41), channel_id=1, source_target_pairs={{0,2},{1,3},{2,0},{3,1},{4,6},{5,7},{6,4},{7,5},{8,10},{9,11},{10,... | collective-permute-start | bytes 221192 | tf_op jit(solution)/shard_map/ppermute | solution.py:608
  10.7 1.1 %copy.10 = bf16[32,2,4608]{2,0,1:T(8,128)(2,1)S(1)} copy(bf16[32,2,4608]{2,1,0:T(2,128)(2,1)} %param.7) | data formatting | bytes 1179648 | tf_op args[1]
  11.8 0.0 copy-start
  11.8 0.7 %copy-done = s32[24,2]{0,1:T(2,128)S(1)} copy-done((s32[24,2]{0,1:T(2,128)S(1)}, s32[24,2]{0,1:T(2,128)}, u32[]{:S(2)}) %copy-start) | copy-done | bytes 216
  12.5 3.1 %prepare.1 = (f32[24,4608]{1,0:T(8,128)S(1)}, f32[24,4608]{1,0:T(8,128)S(1)}, f32[32,64]{1,0:T(8,128)S(1)}, f32[64,4608]{1,0:T(8,128)S(1)}) custom-call(s32[2,24]{1,0:T(2,128)S(1)} %bitcast.10, bf16[2,32,4608]{2,1,0:T(8,128)(2,1)S(1)} %bitcast.7, f32[64,4608]{1,0:T(8,128)} %ctf_hbm.3, f32[4608]{0:T(1024)} %nw_hbm.3), custom_call_target="tpu_custom_call" | custom-call | flops 226492416 | tf_op jit(solution)/shard_map/prepare/pallas_call | solution.py:30
  15.6 4.5 %early_templates.1.early_hbm = bf16[6,768,768]{2,1,0:T(8,128)(2,1)} custom-call(bf16[2,32,4608]{2,1,0:T(8,128)(2,1)S(1)} %bitcast.8, f32[24,4608]{1,0:T(8,128)S(1)} %get-tuple-element.42.cos_ref, f32[24,4608]{1,0:T(8,128)S(1)} %get-tuple-element.43.sin_ref), custom_call_target="tpu_custom_call" | custom-call | flops 70778880 | bytes 7077888 | tf_op jit(solution)/shard_map/early_templates/pallas_call | solution.py:205
  20.1 0.0 collective-permute-done.3.refs_2_
  20.1 0.0 collective-permute-done.4.refs_4_
  20.1 1.4 %collective-permute-done.1.refs_6_.refs_3_ = bf16[32,2304]{1,0:T(8,128)(2,1)S(1)} collective-permute-done((bf16[32,2304]{1,0:T(8,128)(2,1)S(1)}, bf16[32,2304]{1,0:T(8,128)(2,1)S(1)}, u32[]{:S(2)}, u32[]{:S(2)}) %collective-permute-start.1) | collective-permute-done | bytes 147488 | tf_op jit(solution)/shard_map/ppermute | solution.py:608
  21.5 0.0 collective-permute-done.refs_2_
  21.5 0.0 collective-permute-done.2.refs_1_.refs_5_
  21.5 0.5 collective-permute-start.5
  22.0 1.6 %collective-permute-start.6 = (bf16[32,2304]{1,0:T(8,128)(2,1)S(1)}, bf16[32,2304]{1,0:T(8,128)(2,1)S(1)}, u32[]{:S(2)}, u32[]{:S(2)}) collective-permute-start(bf16[32,2304]{1,0:T(8,128)(2,1)S(1)} %collective-permute-done.1.refs_6_.refs_3_), channel_id=1, source_target_pairs={{0,4},{4,0},{8,12},{12,8},{1,5},{5,1},{9,13},{13,9},{2,6},{6,2},{1... | collective-permute-start | bytes 442376 | tf_op jit(solution)/shard_map/ppermute | solution.py:608
  23.6 0.6 %cut_slices.4 = (bf16[64,1152]{1,0:T(8,128)(2,1)S(1)}, bf16[64,1152]{1,0:T(8,128)(2,1)S(1)}, bf16[64,1152]{1,0:T(8,128)(2,1)S(1)}, bf16[96,1152]{1,0:T(8,128)(2,1)S(1)}) custom-call(s32[2]{0:T(128)S(1)} %pad_add_fusion.me_ref, bf16[32,4736]{1,0:T(8,128)(2,1)S(1)} %get-tuple-element.38.refs_0_.refs_4_, ...), custom_call_target="tpu_custom_call" | custom-call | bytes 1327104 | tf_op jit(solution)/shard_map/cut_slices/pallas_call | solution.py:30
  24.2 0.1 collective-permute-start.7
  24.3 1.6 %collective-permute-start.11 = (bf16[64,1152]{1,0:T(8,128)(2,1)S(1)}, bf16[64,1152]{1,0:T(8,128)(2,1)S(1)}, u32[]{:S(2)}, u32[]{:S(2)}) collective-permute-start(bf16[64,1152]{1,0:T(8,128)(2,1)S(1)} %get-tuple-element.62), channel_id=1, source_target_pairs={{0,3},{1,2},{2,1},{3,0},{4,7},{5,6},{6,5},{7,4},{8,11},{9,10},{10,... | collective-permute-start | bytes 442376 | tf_op jit(solution)/shard_map/ppermute | solution.py:608
  25.9 0.5 collective-permute-start.12
  26.4 1.6 %collective-permute-done.5.refs_3_.refs_0_ = bf16[32,2432]{1,0:T(8,128)(2,1)S(1)} collective-permute-done((bf16[32,2432]{1,0:T(8,128)(2,1)S(1)}, bf16[32,2432]{1,0:T(8,128)(2,1)S(1)}, u32[]{:S(2)}, u32[]{:S(2)}) %collective-permute-start.5) | collective-permute-done | bytes 155680 | tf_op jit(solution)/shard_map/ppermute | solution.py:608
  28.0 5.9 %score0.1 = (f32[768,128]{1,0:T(8,128)S(1)}, bf16[6,768,768]{2,1,0:T(8,128)(2,1)S(1)}) custom-call(bf16[6,768,768]{2,1,0:T(8,128)(2,1)} %early_templates.1.early_hbm, bf16[2,32,4608]{2,1,0:T(8,128)(2,1)S(1)} %bitcast.9, f32[24,4608]{1,0:T(8,128)S(1)} %get-tuple-element.42.cos_ref, f32[24,4608]{1,0:T(8,128)S(1)} %get-tuple-element.43.sin_ref, ...), custom_call_target="tpu_custom_call" | custom-call | flops 7247757312 | tf_op jit(solution)/shard_map/score0/pallas_call | solution.py:30
  33.9 0.0 collective-permute-done.6.refs_7_.refs_1_
  33.9 2.3 %score1.1 = (f32[768,128]{1,0:T(8,128)S(1)}, f32[128,64]{1,0:T(8,128)S(1)}, f32[8,128]{1,0:T(8,128)S(1)}) custom-call(bf16[6,768,768]{2,1,0:T(8,128)(2,1)S(1)} %get-tuple-element.48.temp_ref, f32[32,64]{1,0:T(8,128)S(1)} %get-tuple-element.49.pow_ref, f32[768,128]{1,0:T(8,128)S(1)} %get-tuple-element.50.acc_ref, ...), custom_call_target="tpu_custom_call" | custom-call | flops 1811939328 | tf_op jit(solution)/shard_map/score1/pallas_call | solution.py:30
  36.2 0.0 collective-permute-done.7.refs_6_.refs_2_
  36.2 0.5 collective-permute-start.8
  36.6 2.6 %collective-permute-start.9 = (f32[8,128]{1,0:T(8,128)S(1)}, f32[8,128]{1,0:T(8,128)S(1)}, u32[]{:S(2)}, u32[]{:S(2)}) collective-permute-start(f32[8,128]{1,0:T(8,128)S(1)} %get-tuple-element.56.refs_0_), channel_id=1, source_target_pairs={{0,8},{4,12},{8,0},{12,4},{1,9},{5,13},{9,1},{13,5},{2,10},{6,14},... | collective-permute-start | bytes 12296 | tf_op jit(solution)/shard_map/ppermute | solution.py:608
  39.3 1.3 %collective-permute-start.10 = (f32[8,128]{1,0:T(8,128)S(1)}, f32[8,128]{1,0:T(8,128)S(1)}, u32[]{:S(2)}, u32[]{:S(2)}) collective-permute-start(f32[8,128]{1,0:T(8,128)S(1)} %get-tuple-element.56.refs_0_), channel_id=1, source_target_pairs={{0,12},{4,8},{8,4},{12,0},{1,13},{5,9},{9,5},{13,1},{2,14},{6,10},... | collective-permute-start | bytes 12296 | tf_op jit(solution)/shard_map/ppermute | solution.py:608
  40.6 0.6 %cut_slices.5.refs_4_ = bf16[32,1152]{1,0:T(8,128)(2,1)S(1)} custom-call(s32[2]{0:T(128)S(1)} %pad_add_fusion.me_ref, bf16[32,2432]{1,0:T(8,128)(2,1)S(1)} %collective-permute-done.5.refs_3_.refs_0_, bf16[32,2304]{1,0:T(8,128)(2,1)S(1)} %collective-permute-done.6.refs_7_.refs_1_), custom_call_target="tpu_custom_call" | custom-call | bytes 147456 | tf_op jit(solution)/shard_map/cut_slices/pallas_call | solution.py:30
  41.2 0.0 collective-permute-done.11.refs_3_.refs_0_
  41.2 0.0 collective-permute-done.12.refs_5_.refs_1_
  41.2 0.1 collective-permute-start.16
  41.3 0.0 collective-permute-done.8.refs_1_
  41.3 0.0 collective-permute-done.9.refs_2_
  41.3 3.3 %collective-permute-done.10.refs_3_ = f32[8,128]{1,0:T(8,128)S(1)} collective-permute-done((f32[8,128]{1,0:T(8,128)S(1)}, f32[8,128]{1,0:T(8,128)S(1)}, u32[]{:S(2)}, u32[]{:S(2)}) %collective-permute-start.10) | collective-permute-done | bytes 4128 | tf_op jit(solution)/shard_map/ppermute | solution.py:608
  44.7 0.5 responsibilities.1
  45.2 0.0 collective-permute-start.13
  45.2 1.7 %collective-permute-start.14 = (bf16[416,128]{1,0:T(8,128)(2,1)S(1)}, bf16[416,128]{1,0:T(8,128)(2,1)S(1)}, u32[]{:S(2)}, u32[]{:S(2)}) collective-permute-start(bf16[416,128]{1,0:T(8,128)(2,1)S(1)} %get-tuple-element.69.refs_0_), channel_id=1, source_target_pairs={{0,2},{1,3},{2,0},{3,1},{4,6},{5,7},{6,4},{7,5},{8,10},{9,11},{10,... | collective-permute-start | bytes 319496 | tf_op jit(solution)/shard_map/ppermute | solution.py:608
  46.8 0.2 collective-permute-start.15
  47.0 1.5 %gather_rows.1 = (f32[32,64]{1,0:T(8,128)}, bf16[64,2304]{1,0:T(8,128)(2,1)S(1)}, bf16[2,192,1152]{2,1,0:T(8,128)(2,1)S(1)}) custom-call(s32[2]{0:T(128)S(1)} %pad_add_fusion.me_ref, f32[768,128]{1,0:T(8,128)S(1)} %get-tuple-element.52.s_ref, f32[1,128]{1,0:T(1,128)S(1)} %get-tuple-element.57.norm_ref, f32[64,4608]{1,0:T(8,128)S(1)} %get-tuple-element.58.weight_ref, ...), custom_call_target="tpu_custom_call" | custom-call | flops 20000000000 | bytes 1769472 | tf_op jit(solution)/shard_map/gather_rows/pallas_call | solution.py:30
  48.6 1.8 %collective-permute-done.13.refs_1_ = bf16[416,128]{1,0:T(8,128)(2,1)S(1)} collective-permute-done((bf16[416,128]{1,0:T(8,128)(2,1)S(1)}, bf16[416,128]{1,0:T(8,128)(2,1)S(1)}, u32[]{:S(2)}, u32[]{:S(2)}) %collective-permute-start.13) | collective-permute-done | bytes 106528 | tf_op jit(solution)/shard_map/ppermute | solution.py:608
  50.3 2.4 %collective-permute-done.14.refs_2_ = bf16[416,128]{1,0:T(8,128)(2,1)S(1)} collective-permute-done((bf16[416,128]{1,0:T(8,128)(2,1)S(1)}, bf16[416,128]{1,0:T(8,128)(2,1)S(1)}, u32[]{:S(2)}, u32[]{:S(2)}) %collective-permute-start.14) | collective-permute-done | bytes 106528 | tf_op jit(solution)/shard_map/ppermute | solution.py:608
  52.7 0.0 collective-permute-done.15.refs_3_
  52.7 2.9 %finish.1 = f32[32,2,1152]{2,1,0:T(2,128)} custom-call(s32[2]{0:T(128)S(1)} %pad_add_fusion.me_ref, bf16[64,2304]{1,0:T(8,128)(2,1)S(1)} %get-tuple-element.67.cw_ref, f32[24,4608]{1,0:T(8,128)S(1)} %get-tuple-element.42.cos_ref, f32[24,4608]{1,0:T(8,128)S(1)} %get-tuple-element.43.sin_ref, bf16[2,192,1152]{2,1,0:T(8,128)(2,1)S(1)} %get-tuple-element.68.rows_ref, ...), custom_call_target="tpu_custom_call" | custom-call | flops 905969664 | tf_op jit(solution)/shard_map/finish/pallas_call | solution.py:30
  (2 shorter events, 0.0 us)
Async XLA Ops:
  2.4 19.2 %collective-permute-start.2 = (bf16[32,4736]{1,0:T(8,128)(2,1)S(1)}, bf16[32,4736]{1,0:T(8,128)(2,1)S(1)}, u32[]{:S(2)}, u32[]{:S(2)}) collective-permute-start(bf16[32,4736]{1,0:T(8,128)(2,1)S(1)} %get-tuple-element.38.refs_0_.refs_4_), channel_id=1, source_target_pairs={{0,4},{4,0},{8,12},{12,8},{1,5},{5,1},{9,13},{13,9},{2,6},{6,2},{1... | collective-permute-start | bytes 909320 | tf_op jit(solution)/shard_map/ppermute | solution.py:608
  5.4 16.1 %collective-permute-start = (bf16[32,2432]{1,0:T(8,128)(2,1)S(1)}, bf16[32,2432]{1,0:T(8,128)(2,1)S(1)}, u32[]{:S(2)}, u32[]{:S(2)}) collective-permute-start(bf16[32,2432]{1,0:T(8,128)(2,1)S(1)} %get-tuple-element.36), channel_id=1, source_target_pairs={{0,8},{4,12},{8,0},{12,4},{1,9},{5,13},{9,1},{13,5},{2,10},{6,14},... | collective-permute-start | bytes 466952 | tf_op jit(solution)/shard_map/ppermute | solution.py:608
  8.0 13.5 %collective-permute-start.1 = (bf16[32,2304]{1,0:T(8,128)(2,1)S(1)}, bf16[32,2304]{1,0:T(8,128)(2,1)S(1)}, u32[]{:S(2)}, u32[]{:S(2)}) collective-permute-start(bf16[32,2304]{1,0:T(8,128)(2,1)S(1)} %get-tuple-element.37), channel_id=1, source_target_pairs={{0,8},{4,12},{8,0},{12,4},{1,9},{5,13},{9,1},{13,5},{2,10},{6,14},... | collective-permute-start | bytes 442376 | tf_op jit(solution)/shard_map/ppermute | solution.py:608
  9.0 11.1 %collective-permute-start.3 = (bf16[32,1152]{1,0:T(8,128)(2,1)S(1)}, bf16[32,1152]{1,0:T(8,128)(2,1)S(1)}, u32[]{:S(2)}, u32[]{:S(2)}) collective-permute-start(bf16[32,1152]{1,0:T(8,128)(2,1)S(1)} %get-tuple-element.40), channel_id=1, source_target_pairs={{0,3},{1,2},{2,1},{3,0},{4,7},{5,6},{6,5},{7,4},{8,11},{9,10},{10,... | collective-permute-start | bytes 221192 | tf_op jit(solution)/shard_map/ppermute | solution.py:608
  9.2 10.9 %collective-permute-start.4 = (bf16[32,1152]{1,0:T(8,128)(2,1)S(1)}, bf16[32,1152]{1,0:T(8,128)(2,1)S(1)}, u32[]{:S(2)}, u32[]{:S(2)}) collective-permute-start(bf16[32,1152]{1,0:T(8,128)(2,1)S(1)} %get-tuple-element.41), channel_id=1, source_target_pairs={{0,2},{1,3},{2,0},{3,1},{4,6},{5,7},{6,4},{7,5},{8,10},{9,11},{10,... | collective-permute-start | bytes 221192 | tf_op jit(solution)/shard_map/ppermute | solution.py:608
  11.8 0.7 %copy-start = (s32[24,2]{0,1:T(2,128)S(1)}, s32[24,2]{0,1:T(2,128)}, u32[]{:S(2)}) copy-start(s32[24,2]{0,1:T(2,128)} %param.11) | copy-start | bytes 580
  21.5 6.5 %collective-permute-start.5 = (bf16[32,2432]{1,0:T(8,128)(2,1)S(1)}, bf16[32,2432]{1,0:T(8,128)(2,1)S(1)}, u32[]{:S(2)}, u32[]{:S(2)}) collective-permute-start(bf16[32,2432]{1,0:T(8,128)(2,1)S(1)} %collective-permute-done.refs_2_), channel_id=1, source_target_pairs={{0,4},{4,0},{8,12},{12,8},{1,5},{5,1},{9,13},{13,9},{2,6},{6,2},{1... | collective-permute-start | bytes 466952 | tf_op jit(solution)/shard_map/ppermute | solution.py:608
  22.0 11.9 %collective-permute-start.6 = (bf16[32,2304]{1,0:T(8,128)(2,1)S(1)}, bf16[32,2304]{1,0:T(8,128)(2,1)S(1)}, u32[]{:S(2)}, u32[]{:S(2)}) collective-permute-start(bf16[32,2304]{1,0:T(8,128)(2,1)S(1)} %collective-permute-done.1.refs_6_.refs_3_), channel_id=1, source_target_pairs={{0,4},{4,0},{8,12},{12,8},{1,5},{5,1},{9,13},{13,9},{2,6},{6,2},{1... | collective-permute-start | bytes 442376 | tf_op jit(solution)/shard_map/ppermute | solution.py:608
  24.2 12.0 %collective-permute-start.7 = (bf16[96,1152]{1,0:T(8,128)(2,1)S(1)}, bf16[96,1152]{1,0:T(8,128)(2,1)S(1)}, u32[]{:S(2)}, u32[]{:S(2)}) collective-permute-start(bf16[96,1152]{1,0:T(8,128)(2,1)S(1)} %get-tuple-element.55), channel_id=1, source_target_pairs={{0,1},{1,0},{2,3},{3,2},{4,5},{5,4},{6,7},{7,6},{8,9},{9,8},{10,11... | collective-permute-start | bytes 663560 | tf_op jit(solution)/shard_map/ppermute | solution.py:608
  24.3 16.9 %collective-permute-start.11 = (bf16[64,1152]{1,0:T(8,128)(2,1)S(1)}, bf16[64,1152]{1,0:T(8,128)(2,1)S(1)}, u32[]{:S(2)}, u32[]{:S(2)}) collective-permute-start(bf16[64,1152]{1,0:T(8,128)(2,1)S(1)} %get-tuple-element.62), channel_id=1, source_target_pairs={{0,3},{1,2},{2,1},{3,0},{4,7},{5,6},{6,5},{7,4},{8,11},{9,10},{10,... | collective-permute-start | bytes 442376 | tf_op jit(solution)/shard_map/ppermute | solution.py:608
  25.9 15.3 %collective-permute-start.12 = (bf16[64,1152]{1,0:T(8,128)(2,1)S(1)}, bf16[64,1152]{1,0:T(8,128)(2,1)S(1)}, u32[]{:S(2)}, u32[]{:S(2)}) collective-permute-start(bf16[64,1152]{1,0:T(8,128)(2,1)S(1)} %get-tuple-element.64), channel_id=1, source_target_pairs={{0,2},{1,3},{2,0},{3,1},{4,6},{5,7},{6,4},{7,5},{8,10},{9,11},{10,... | collective-permute-start | bytes 442376 | tf_op jit(solution)/shard_map/ppermute | solution.py:608
  36.2 5.2 %collective-permute-start.8 = (f32[8,128]{1,0:T(8,128)S(1)}, f32[8,128]{1,0:T(8,128)S(1)}, u32[]{:S(2)}, u32[]{:S(2)}) collective-permute-start(f32[8,128]{1,0:T(8,128)S(1)} %get-tuple-element.56.refs_0_), channel_id=1, source_target_pairs={{0,4},{4,0},{8,12},{12,8},{1,5},{5,1},{9,13},{13,9},{2,6},{6,2},{1... | collective-permute-start | bytes 12296 | tf_op jit(solution)/shard_map/ppermute | solution.py:608
  36.6 4.7 %collective-permute-start.9 = (f32[8,128]{1,0:T(8,128)S(1)}, f32[8,128]{1,0:T(8,128)S(1)}, u32[]{:S(2)}, u32[]{:S(2)}) collective-permute-start(f32[8,128]{1,0:T(8,128)S(1)} %get-tuple-element.56.refs_0_), channel_id=1, source_target_pairs={{0,8},{4,12},{8,0},{12,4},{1,9},{5,13},{9,1},{13,5},{2,10},{6,14},... | collective-permute-start | bytes 12296 | tf_op jit(solution)/shard_map/ppermute | solution.py:608
  39.3 5.4 %collective-permute-start.10 = (f32[8,128]{1,0:T(8,128)S(1)}, f32[8,128]{1,0:T(8,128)S(1)}, u32[]{:S(2)}, u32[]{:S(2)}) collective-permute-start(f32[8,128]{1,0:T(8,128)S(1)} %get-tuple-element.56.refs_0_), channel_id=1, source_target_pairs={{0,12},{4,8},{8,4},{12,0},{1,13},{5,9},{9,5},{13,1},{2,14},{6,10},... | collective-permute-start | bytes 12296 | tf_op jit(solution)/shard_map/ppermute | solution.py:608
  41.2 11.5 %collective-permute-start.16 = (bf16[96,1152]{1,0:T(8,128)(2,1)S(1)}, bf16[96,1152]{1,0:T(8,128)(2,1)S(1)}, u32[]{:S(2)}, u32[]{:S(2)}) collective-permute-start(bf16[96,1152]{1,0:T(8,128)(2,1)S(1)} %bundle.1), channel_id=1, source_target_pairs={{0,4},{4,0},{8,12},{12,8},{1,5},{5,1},{9,13},{13,9},{2,6},{6,2},{1... | collective-permute-start | bytes 663560 | tf_op jit(solution)/shard_map/ppermute | solution.py:608
  45.2 5.1 %collective-permute-start.13 = (bf16[416,128]{1,0:T(8,128)(2,1)S(1)}, bf16[416,128]{1,0:T(8,128)(2,1)S(1)}, u32[]{:S(2)}, u32[]{:S(2)}) collective-permute-start(bf16[416,128]{1,0:T(8,128)(2,1)S(1)} %get-tuple-element.69.refs_0_), channel_id=1, source_target_pairs={{0,3},{1,2},{2,1},{3,0},{4,7},{5,6},{6,5},{7,4},{8,11},{9,10},{10,... | collective-permute-start | bytes 319496 | tf_op jit(solution)/shard_map/ppermute | solution.py:608
  45.2 7.5 %collective-permute-start.14 = (bf16[416,128]{1,0:T(8,128)(2,1)S(1)}, bf16[416,128]{1,0:T(8,128)(2,1)S(1)}, u32[]{:S(2)}, u32[]{:S(2)}) collective-permute-start(bf16[416,128]{1,0:T(8,128)(2,1)S(1)} %get-tuple-element.69.refs_0_), channel_id=1, source_target_pairs={{0,2},{1,3},{2,0},{3,1},{4,6},{5,7},{6,4},{7,5},{8,10},{9,11},{10,... | collective-permute-start | bytes 319496 | tf_op jit(solution)/shard_map/ppermute | solution.py:608
  46.8 5.9 %collective-permute-start.15 = (bf16[416,128]{1,0:T(8,128)(2,1)S(1)}, bf16[416,128]{1,0:T(8,128)(2,1)S(1)}, u32[]{:S(2)}, u32[]{:S(2)}) collective-permute-start(bf16[416,128]{1,0:T(8,128)(2,1)S(1)} %get-tuple-element.69.refs_0_), channel_id=1, source_target_pairs={{0,1},{1,0},{2,3},{3,2},{4,5},{5,4},{6,7},{7,6},{8,9},{9,8},{10,11... | collective-permute-start | bytes 319496 | tf_op jit(solution)/shard_map/ppermute | solution.py:608

commit v14 on v13

--- a/solution.py
+++ b/solution.py
@@ -200,7 +200,7 @@
     _, rows, freq = split.shape
     poses = cos_t.shape[0]
     tile = template_tile(freq)
-    count = freq // tile // 2
+    count = freq // tile // 2 + 1
     skip = freq // tile - count
     return pl.pallas_call(
         early_kernel,
@@ -237,25 +237,44 @@
     )
 
 
-def first_score_kernel(chunked, half, early_hbm, cls_ref, cos_ref, sin_ref, *refs):
-    refs, (acc_ref, late_ref, *buffers, sem) = refs[:-5], refs[-5:]
-    count, _, width = late_ref.shape
-    tile = width // 2
+def start_copies(early_hbm, moves, sem):
     copies = [
-        pltpu.make_async_copy(early_hbm.at[t], late_ref.at[t], sem.at[t]) for t in range(count)
+        pltpu.make_async_copy(early_hbm.at[source], target, sem.at[i])
+        for i, (source, target) in enumerate(moves)
     ]
     for copy in copies:
         copy.start()
+    return copies
+
+
+def template_kernel(early_hbm, cls_ref, cos_ref, sin_ref, temp_ref, late_ref, sem):
+    built = temp_ref.shape[0] - 1
+    tile = temp_ref.shape[2] // 2
+    moves = [(0, temp_ref.at[built])]
+    moves += [(1 + t, late_ref.at[t]) for t in range(late_ref.shape[0])]
+    copies = start_copies(early_hbm, moves, sem)
+
+    @pl.loop(0, built)
+    def _(t):
+        write_templates(cls_ref, cos_ref, sin_ref, temp_ref.at[t], t * tile, tile)
+
+    for copy in copies:
+        copy.wait()
+
+
+def first_score_kernel(chunked, half, early_hbm, temp_ref, *refs):
+    refs, (acc_ref, late_ref, sem) = refs[:-3], refs[-3:]
+    count, _, width = temp_ref.shape
+    tile = width // 2
+    rest = late_ref.shape[0]
+    skip = early_hbm.shape[0] - rest
+    copies = start_copies(early_hbm, [(skip + t, late_ref.at[t]) for t in range(rest)], sem)
     shards = list(zip(refs, chunked))
-    built = cls_ref.shape[2] // tile - count
     acc_ref[...] = jnp.zeros_like(acc_ref)
-    write_templates(cls_ref, cos_ref, sin_ref, buffers[0], 0, tile)
-    for t in range(built):
-        if t + 1 < built:
-            write_templates(cls_ref, cos_ref, sin_ref, buffers[(t + 1) % 2], (t + 1) * tile, tile)
+    for t in range(count):
         acc_ref[...] += lax.dot_general(
-            buffers[t % 2][...],
-            tile_of_particles(shards, 0, built * tile, t, tile, half),
+            temp_ref[t],
+            tile_of_particles(shards, 0, count * tile, t, tile, half),
             NT,
             preferred_element_type=f32,
         )
@@ -263,11 +282,11 @@
         copy.wait()
 
 
-def last_score_kernel(chunked, half, temp_ref, pow_ref, acc_ref, *refs):
+def last_score_kernel(chunked, half, temp_ref, rest_ref, pow_ref, acc_ref, *refs):
     refs, (s_ref, marks_ref, stat_ref) = refs[:-3], refs[-3:]
     tail_refs, shards = refs[: len(chunked)], list(zip(refs[len(chunked) :], chunked))
-    count, _, width = temp_ref.shape
-    tile = width // 2
+    tile = temp_ref.shape[2] // 2
+    temps = [ref.at[t] for ref in (temp_ref, rest_ref) for t in range(ref.shape[0])]
     rows, groups = pow_ref.shape
     lanes = s_ref.shape[1]
     poses = s_ref.shape[0] // rows
@@ -280,10 +299,10 @@
         pow_ref[...], marks, NT, precision=HIGHEST, preferred_element_type=f32
     )
     s_ref[...] = acc_ref[...]
-    for t in range(count):
+    for t, temp in enumerate(temps):
         s_ref[...] += lax.dot_general(
-            temp_ref[t],
-            tile_of_particles(shards, 1, count * tile, t, tile, half),
+            temp[...],
+            tile_of_particles(shards, 1, len(temps) * tile, t, tile, half),
             NT,
             preferred_element_type=f32,
         )
@@ -302,26 +321,39 @@
 
 def score(early, split, cos_t, sin_t, power, shards, half):
     count, columns, width = early.shape
+    count -= 1
+    some = count // 2
+    freq = split.shape[2]
     lanes = sum(refs[0].shape[0] for refs in shards)
     chunked = [len(refs) > 1 for refs in shards]
     flops = 2 * columns * 256 * count * width
     acc_shape = jax.ShapeDtypeStruct((columns, lanes), f32)
-    operands = [pltpu.with_memory_space_constraint(early, pltpu.HBM), split, cos_t, sin_t]
-    operands += [refs[0] for refs in shards]
-    acc, late = call(
+    early = pltpu.with_memory_space_constraint(early, pltpu.HBM)
+    temps, late = call(
+        template_kernel,
+        "templates",
+        [ANY] + [VMEM] * 3,
+        [
+            pltpu.VMEM((count, columns, width), bf16),
+            pltpu.VMEM((some, columns, width), bf16),
+        ],
+        (early, split, cos_t, sin_t),
+        [pltpu.SemaphoreType.DMA((some + 1,))],
+        flops=20 * columns * freq,
+        moved=2 * columns * freq,
+    )
+    operands = [early, temps, *[refs[0] for refs in shards]]
+    acc, rest = call(
         functools.partial(first_score_kernel, chunked, half),
         "score0",
         [ANY] + [VMEM] * (len(operands) - 1),
-        [acc_shape, pltpu.VMEM(early.shape, bf16)],
+        [acc_shape, pltpu.VMEM((count - some, columns, width), bf16)],
         operands,
-        [
-            pltpu.VMEM((columns, width), bf16),
-            pltpu.VMEM((columns, width), bf16),
-            pltpu.SemaphoreType.DMA((count,)),
-        ],
-        flops=4 * flops,
-    )
-    operands = [late, power, acc, *[refs[0] for refs in shards], *[refs[-1] for refs in shards]]
+        [pltpu.SemaphoreType.DMA((count - some,))],
+        flops=flops,
+    )
+    operands = [late, rest, power, acc]
+    operands += [refs[0] for refs in shards] + [refs[-1] for refs in shards]
     return call(
         functools.partial(last_score_kernel, chunked, half),
         "score1",

time: 55.9 us -> 53.9 us (0.964)
  waiting for transfers between devices: 10.6 us -> 8.02 us
  Pallas kernels: 24.1 us -> 24.7 us
    ppermute x17, waiting for transfers between devices: 10.6 us -> 8.02 us  [swap(): return lax.ppermute(values, axis, [(i, i ^ distance) for i in range(size)])]
    pallas_call x1, Pallas kernels: 4.53 us -> 5.52 us  [early_templates(): pl.pallas_call(early_kernel, grid=(count,), in_specs=[pl.BlockSpec((2, ro...]
    pallas_call x11 -> x12, Pallas kernels: 19.6 us -> 19.2 us  [call(): pl.pallas_call(kernel, in_specs=in_specs, out_specs=[VMEM] * len(out_shap...]
  transfers between devices with their start and end apart: 17 -> 17, of which waited for: 5 -> 4; matrix products, arithmetic and copies ran while one was open for 2% -> 2% of each run, Pallas kernels for 35% -> 38%
where the time goes in v14:
time: 53.9 us; the launch traced here: 53.6 us
  Pallas kernels  24.7 us (46%)
  starting transfers between devices  18.3 us (34%)
  waiting for transfers between devices  8.02 us (15%)
  local copies, waits for them, and re-layouts  1.8 us (3%)
  between operations  0.8 us (1%)
    pallas_call x12, Pallas kernels, call(): pl.pallas_call(kernel, in_specs=in_specs, out_specs=[VMEM] * len(out_shap...  19.2 us
    ppermute x17, starting transfers between devices, swap(): return lax.ppermute(values, axis, [(i, i ^ distance) for i in range(size)])  18.3 us
    ppermute x17, waiting for transfers between devices, swap(): return lax.ppermute(values, axis, [(i, i ^ distance) for i in range(size)])  8.02 us
    pallas_call x1, Pallas kernels, early_templates(): pl.pallas_call(early_kernel, grid=(count,), in_specs=[pl.BlockSpec((2, ro...  5.52 us
    unnamed x3, local copies, waits for them, and re-layouts  1.8 us
  transfers between devices with their start and end apart: 17, of which 4 were waited for; matrix products, arithmetic and copies ran while one was open for 2% of the time, Pallas kernels for 38%

profile of v14, /device:TPU:0, one launch (start us, length us, event | category | flops | bytes accessed | tf_op | source)
XLA Modules:
  0.0 53.6 jit_solution(534307540455151047)
XLA Ops:
  0.6 1.7 %weigh.1 = (bf16[32,4736]{1,0:T(8,128)(2,1)S(1)}, bf16[32,2432]{1,0:T(8,128)(2,1)S(1)}, bf16[32,2304]{1,0:T(8,128)(2,1)S(1)}) custom-call(s32[16]{0:T(128)} %ids_hbm.1, bf16[16,2,4608]{2,1,0:T(2,128)(2,1)} %p_hbm.1, f32[64,4608]{1,0:T(8,128)} %ctf_hbm.3, f32[4608]{0:T(1024)} %nw_hbm.3), custom_call_target="tpu_custom_call" | custom-call | flops 294912 | bytes 1179648 | tf_op jit(solution)/shard_map/weigh/pallas_call | solution.py:30
  2.4 3.1 %collective-permute-start.2 = (bf16[32,4736]{1,0:T(8,128)(2,1)S(1)}, bf16[32,4736]{1,0:T(8,128)(2,1)S(1)}, u32[]{:S(2)}, u32[]{:S(2)}) collective-permute-start(bf16[32,4736]{1,0:T(8,128)(2,1)S(1)} %get-tuple-element.40.refs_0_.refs_4_), channel_id=1, source_target_pairs={{0,4},{4,0},{8,12},{12,8},{1,5},{5,1},{9,13},{13,9},{2,6},{6,2},{1... | collective-permute-start | bytes 909320 | tf_op jit(solution)/shard_map/ppermute | solution.py:640
  5.4 2.6 %collective-permute-start = (bf16[32,2432]{1,0:T(8,128)(2,1)S(1)}, bf16[32,2432]{1,0:T(8,128)(2,1)S(1)}, u32[]{:S(2)}, u32[]{:S(2)}) collective-permute-start(bf16[32,2432]{1,0:T(8,128)(2,1)S(1)} %get-tuple-element.38), channel_id=1, source_target_pairs={{0,8},{4,12},{8,0},{12,4},{1,9},{5,13},{9,1},{13,5},{2,10},{6,14},... | collective-permute-start | bytes 466952 | tf_op jit(solution)/shard_map/ppermute | solution.py:640
  8.0 0.3 collective-permute-start.1
  8.4 0.1 pad_add_fusion.me_ref
  8.4 0.6 %cut_slices.3 = (bf16[32,1152]{1,0:T(8,128)(2,1)S(1)}, bf16[32,1152]{1,0:T(8,128)(2,1)S(1)}, bf16[32,1152]{1,0:T(8,128)(2,1)S(1)}) custom-call(s32[2]{0:T(128)S(1)} %pad_add_fusion.me_ref, bf16[32,4736]{1,0:T(8,128)(2,1)S(1)} %get-tuple-element.40.refs_0_.refs_4_), custom_call_target="tpu_custom_call" | custom-call | bytes 442368 | tf_op jit(solution)/shard_map/cut_slices/pallas_call | solution.py:30
  9.0 0.2 collective-permute-start.3
  9.2 1.5 %collective-permute-start.4 = (bf16[32,1152]{1,0:T(8,128)(2,1)S(1)}, bf16[32,1152]{1,0:T(8,128)(2,1)S(1)}, u32[]{:S(2)}, u32[]{:S(2)}) collective-permute-start(bf16[32,1152]{1,0:T(8,128)(2,1)S(1)} %get-tuple-element.43), channel_id=1, source_target_pairs={{0,2},{1,3},{2,0},{3,1},{4,6},{5,7},{6,4},{7,5},{8,10},{9,11},{10,... | collective-permute-start | bytes 221192 | tf_op jit(solution)/shard_map/ppermute | solution.py:640
  10.7 1.1 %copy.10 = bf16[32,2,4608]{2,0,1:T(8,128)(2,1)S(1)} copy(bf16[32,2,4608]{2,1,0:T(2,128)(2,1)} %param.7) | data formatting | bytes 1179648 | tf_op args[1]
  11.8 0.0 copy-start
  11.8 0.7 %copy-done = s32[24,2]{0,1:T(2,128)S(1)} copy-done((s32[24,2]{0,1:T(2,128)S(1)}, s32[24,2]{0,1:T(2,128)}, u32[]{:S(2)}) %copy-start) | copy-done | bytes 216
  12.5 3.1 %prepare.1 = (f32[24,4608]{1,0:T(8,128)S(1)}, f32[24,4608]{1,0:T(8,128)S(1)}, f32[32,64]{1,0:T(8,128)S(1)}, f32[64,4608]{1,0:T(8,128)S(1)}) custom-call(s32[2,24]{1,0:T(2,128)S(1)} %bitcast.10, bf16[2,32,4608]{2,1,0:T(8,128)(2,1)S(1)} %bitcast.7, f32[64,4608]{1,0:T(8,128)} %ctf_hbm.3, f32[4608]{0:T(1024)} %nw_hbm.3), custom_call_target="tpu_custom_call" | custom-call | flops 226492416 | tf_op jit(solution)/shard_map/prepare/pallas_call | solution.py:30
  15.6 5.5 %early_templates.1.early_hbm = bf16[7,768,768]{2,1,0:T(8,128)(2,1)} custom-call(bf16[2,32,4608]{2,1,0:T(8,128)(2,1)S(1)} %bitcast.8, f32[24,4608]{1,0:T(8,128)S(1)} %get-tuple-element.44.cos_ref, f32[24,4608]{1,0:T(8,128)S(1)} %get-tuple-element.45.sin_ref), custom_call_target="tpu_custom_call" | custom-call | flops 70778880 | bytes 7077888 | tf_op jit(solution)/shard_map/early_templates/pallas_call | solution.py:205
  21.1 0.0 collective-permute-done.4.refs_4_
  21.1 0.4 collective-permute-done.1.refs_6_.refs_3_
  21.5 0.0 collective-permute-done.refs_2_
  21.5 0.0 collective-permute-done.2.refs_1_.refs_5_
  21.5 0.5 collective-permute-start.5
  22.0 1.6 %collective-permute-start.6 = (bf16[32,2304]{1,0:T(8,128)(2,1)S(1)}, bf16[32,2304]{1,0:T(8,128)(2,1)S(1)}, u32[]{:S(2)}, u32[]{:S(2)}) collective-permute-start(bf16[32,2304]{1,0:T(8,128)(2,1)S(1)} %collective-permute-done.1.refs_6_.refs_3_), channel_id=1, source_target_pairs={{0,4},{4,0},{8,12},{12,8},{1,5},{5,1},{9,13},{13,9},{2,6},{6,2},{1... | collective-permute-start | bytes 442376 | tf_op jit(solution)/shard_map/ppermute | solution.py:640
  23.6 0.6 %cut_slices.4 = (bf16[64,1152]{1,0:T(8,128)(2,1)S(1)}, bf16[64,1152]{1,0:T(8,128)(2,1)S(1)}, bf16[64,1152]{1,0:T(8,128)(2,1)S(1)}, bf16[96,1152]{1,0:T(8,128)(2,1)S(1)}) custom-call(s32[2]{0:T(128)S(1)} %pad_add_fusion.me_ref, bf16[32,4736]{1,0:T(8,128)(2,1)S(1)} %get-tuple-element.40.refs_0_.refs_4_, ...), custom_call_target="tpu_custom_call" | custom-call | bytes 1327104 | tf_op jit(solution)/shard_map/cut_slices/pallas_call | solution.py:30
  24.2 0.1 collective-permute-start.7
  24.3 1.6 %collective-permute-start.11 = (bf16[64,1152]{1,0:T(8,128)(2,1)S(1)}, bf16[64,1152]{1,0:T(8,128)(2,1)S(1)}, u32[]{:S(2)}, u32[]{:S(2)}) collective-permute-start(bf16[64,1152]{1,0:T(8,128)(2,1)S(1)} %get-tuple-element.66), channel_id=1, source_target_pairs={{0,3},{1,2},{2,1},{3,0},{4,7},{5,6},{6,5},{7,4},{8,11},{9,10},{10,... | collective-permute-start | bytes 442376 | tf_op jit(solution)/shard_map/ppermute | solution.py:640
  25.9 0.5 collective-permute-start.12
  26.4 2.4 %templates.1 = (bf16[6,768,768]{2,1,0:T(8,128)(2,1)S(1)}, bf16[3,768,768]{2,1,0:T(8,128)(2,1)S(1)}) custom-call(bf16[7,768,768]{2,1,0:T(8,128)(2,1)} %early_templates.1.early_hbm, bf16[2,32,4608]{2,1,0:T(8,128)(2,1)S(1)} %bitcast.9, f32[24,4608]{1,0:T(8,128)S(1)} %get-tuple-element.44.cos_ref, f32[24,4608]{1,0:T(8,128)S(1)} %get-tuple-element.45.sin_ref), custom_call_target="tpu_custom_call" | custom-call | flops 70778880 | bytes 7077888 | tf_op jit(solution)/shard_map/templates/pallas_call | solution.py:30
  28.8 0.0 collective-permute-done.5.refs_3_.refs_0_
  28.8 3.1 %score0.1 = (f32[768,128]{1,0:T(8,128)S(1)}, bf16[3,768,768]{2,1,0:T(8,128)(2,1)S(1)}) custom-call(bf16[7,768,768]{2,1,0:T(8,128)(2,1)} %early_templates.1.early_hbm, bf16[6,768,768]{2,1,0:T(8,128)(2,1)S(1)} %get-tuple-element.49.temp_ref, bf16[32,4736]{1,0:T(8,128)(2,1)S(1)} %get-tuple-element.40.refs_0_.refs_4_, ...), custom_call_target="tpu_custom_call" | custom-call | flops 1811939328 | tf_op jit(solution)/shard_map/score0/pallas_call | solution.py:30
  31.9 0.0 collective-permute-done.6.refs_7_.refs_1_
  31.9 2.2 %score1.1 = (f32[768,128]{1,0:T(8,128)S(1)}, f32[128,64]{1,0:T(8,128)S(1)}, f32[8,128]{1,0:T(8,128)S(1)}) custom-call(bf16[3,768,768]{2,1,0:T(8,128)(2,1)S(1)} %get-tuple-element.48.temp_ref, bf16[3,768,768]{2,1,0:T(8,128)(2,1)S(1)} %get-tuple-element.52.rest_ref, f32[32,64]{1,0:T(8,128)S(1)} %get-tuple-element.53.pow_ref, ...), custom_call_target="tpu_custom_call" | custom-call | flops 1811939328 | tf_op jit(solution)/shard_map/score1/pallas_call | solution.py:30
  34.2 0.0 collective-permute-done.7.refs_6_.refs_2_
  34.2 0.5 collective-permute-start.8
  34.7 2.6 %collective-permute-start.9 = (f32[8,128]{1,0:T(8,128)S(1)}, f32[8,128]{1,0:T(8,128)S(1)}, u32[]{:S(2)}, u32[]{:S(2)}) collective-permute-start(f32[8,128]{1,0:T(8,128)S(1)} %get-tuple-element.60.refs_0_), channel_id=1, source_target_pairs={{0,8},{4,12},{8,0},{12,4},{1,9},{5,13},{9,1},{13,5},{2,10},{6,14},... | collective-permute-start | bytes 12296 | tf_op jit(solution)/shard_map/ppermute | solution.py:640
  37.3 1.4 %collective-permute-start.10 = (f32[8,128]{1,0:T(8,128)S(1)}, f32[8,128]{1,0:T(8,128)S(1)}, u32[]{:S(2)}, u32[]{:S(2)}) collective-permute-start(f32[8,128]{1,0:T(8,128)S(1)} %get-tuple-element.60.refs_0_), channel_id=1, source_target_pairs={{0,12},{4,8},{8,4},{12,0},{1,13},{5,9},{9,5},{13,1},{2,14},{6,10},... | collective-permute-start | bytes 12296 | tf_op jit(solution)/shard_map/ppermute | solution.py:640
  38.6 0.6 %cut_slices.5.refs_4_ = bf16[32,1152]{1,0:T(8,128)(2,1)S(1)} custom-call(s32[2]{0:T(128)S(1)} %pad_add_fusion.me_ref, bf16[32,2432]{1,0:T(8,128)(2,1)S(1)} %collective-permute-done.5.refs_3_.refs_0_, bf16[32,2304]{1,0:T(8,128)(2,1)S(1)} %collective-permute-done.6.refs_7_.refs_1_), custom_call_target="tpu_custom_call" | custom-call | bytes 147456 | tf_op jit(solution)/shard_map/cut_slices/pallas_call | solution.py:30
  39.2 0.0 collective-permute-done.11.refs_3_.refs_0_
  39.2 0.0 collective-permute-done.12.refs_5_.refs_1_
  39.2 0.1 collective-permute-start.16
  39.3 0.0 collective-permute-done.9.refs_2_
  39.3 3.4 %collective-permute-done.10.refs_3_ = f32[8,128]{1,0:T(8,128)S(1)} collective-permute-done((f32[8,128]{1,0:T(8,128)S(1)}, f32[8,128]{1,0:T(8,128)S(1)}, u32[]{:S(2)}, u32[]{:S(2)}) %collective-permute-start.10) | collective-permute-done | bytes 4128 | tf_op jit(solution)/shard_map/ppermute | solution.py:640
  42.7 0.5 responsibilities.1
  43.2 0.0 collective-permute-start.13
  43.2 1.6 %collective-permute-start.14 = (bf16[416,128]{1,0:T(8,128)(2,1)S(1)}, bf16[416,128]{1,0:T(8,128)(2,1)S(1)}, u32[]{:S(2)}, u32[]{:S(2)}) collective-permute-start(bf16[416,128]{1,0:T(8,128)(2,1)S(1)} %get-tuple-element.73.refs_0_), channel_id=1, source_target_pairs={{0,2},{1,3},{2,0},{3,1},{4,6},{5,7},{6,4},{7,5},{8,10},{9,11},{10,... | collective-permute-start | bytes 319496 | tf_op jit(solution)/shard_map/ppermute | solution.py:640
  44.8 0.3 collective-permute-start.15
  45.1 1.5 %gather_rows.1 = (f32[32,64]{1,0:T(8,128)}, bf16[64,2304]{1,0:T(8,128)(2,1)S(1)}, bf16[2,192,1152]{2,1,0:T(8,128)(2,1)S(1)}) custom-call(s32[2]{0:T(128)S(1)} %pad_add_fusion.me_ref, f32[768,128]{1,0:T(8,128)S(1)} %get-tuple-element.56.s_ref, f32[1,128]{1,0:T(1,128)S(1)} %get-tuple-element.61.norm_ref, f32[64,4608]{1,0:T(8,128)S(1)} %get-tuple-element.62.weight_ref, ...), custom_call_target="tpu_custom_call" | custom-call | flops 20000000000 | bytes 1769472 | tf_op jit(solution)/shard_map/gather_rows/pallas_call | solution.py:30
  46.6 1.9 %collective-permute-done.13.refs_1_ = bf16[416,128]{1,0:T(8,128)(2,1)S(1)} collective-permute-done((bf16[416,128]{1,0:T(8,128)(2,1)S(1)}, bf16[416,128]{1,0:T(8,128)(2,1)S(1)}, u32[]{:S(2)}, u32[]{:S(2)}) %collective-permute-start.13) | collective-permute-done | bytes 106528 | tf_op jit(solution)/shard_map/ppermute | solution.py:640
  48.4 2.3 %collective-permute-done.14.refs_2_ = bf16[416,128]{1,0:T(8,128)(2,1)S(1)} collective-permute-done((bf16[416,128]{1,0:T(8,128)(2,1)S(1)}, bf16[416,128]{1,0:T(8,128)(2,1)S(1)}, u32[]{:S(2)}, u32[]{:S(2)}) %collective-permute-start.14) | collective-permute-done | bytes 106528 | tf_op jit(solution)/shard_map/ppermute | solution.py:640
  50.8 0.0 collective-permute-done.15.refs_3_
  50.8 0.0 collective-permute-done.16.refs_5_
  50.8 2.9 %finish.1 = f32[32,2,1152]{2,1,0:T(2,128)} custom-call(s32[2]{0:T(128)S(1)} %pad_add_fusion.me_ref, bf16[64,2304]{1,0:T(8,128)(2,1)S(1)} %get-tuple-element.71.cw_ref, f32[24,4608]{1,0:T(8,128)S(1)} %get-tuple-element.44.cos_ref, f32[24,4608]{1,0:T(8,128)S(1)} %get-tuple-element.45.sin_ref, bf16[2,192,1152]{2,1,0:T(8,128)(2,1)S(1)} %get-tuple-element.72.rows_ref, ...), custom_call_target="tpu_custom_call" | custom-call | flops 905969664 | tf_op jit(solution)/shard_map/finish/pallas_call | solution.py:30
  (3 shorter events, 0.0 us)
Async XLA Ops:
  2.4 19.2 %collective-permute-start.2 = (bf16[32,4736]{1,0:T(8,128)(2,1)S(1)}, bf16[32,4736]{1,0:T(8,128)(2,1)S(1)}, u32[]{:S(2)}, u32[]{:S(2)}) collective-permute-start(bf16[32,4736]{1,0:T(8,128)(2,1)S(1)} %get-tuple-element.40.refs_0_.refs_4_), channel_id=1, source_target_pairs={{0,4},{4,0},{8,12},{12,8},{1,5},{5,1},{9,13},{13,9},{2,6},{6,2},{1... | collective-permute-start | bytes 909320 | tf_op jit(solution)/shard_map/ppermute | solution.py:640
  5.4 16.1 %collective-permute-start = (bf16[32,2432]{1,0:T(8,128)(2,1)S(1)}, bf16[32,2432]{1,0:T(8,128)(2,1)S(1)}, u32[]{:S(2)}, u32[]{:S(2)}) collective-permute-start(bf16[32,2432]{1,0:T(8,128)(2,1)S(1)} %get-tuple-element.38), channel_id=1, source_target_pairs={{0,8},{4,12},{8,0},{12,4},{1,9},{5,13},{9,1},{13,5},{2,10},{6,14},... | collective-permute-start | bytes 466952 | tf_op jit(solution)/shard_map/ppermute | solution.py:640
  8.0 13.5 %collective-permute-start.1 = (bf16[32,2304]{1,0:T(8,128)(2,1)S(1)}, bf16[32,2304]{1,0:T(8,128)(2,1)S(1)}, u32[]{:S(2)}, u32[]{:S(2)}) collective-permute-start(bf16[32,2304]{1,0:T(8,128)(2,1)S(1)} %get-tuple-element.39), channel_id=1, source_target_pairs={{0,8},{4,12},{8,0},{12,4},{1,9},{5,13},{9,1},{13,5},{2,10},{6,14},... | collective-permute-start | bytes 442376 | tf_op jit(solution)/shard_map/ppermute | solution.py:640
  9.0 12.1 %collective-permute-start.3 = (bf16[32,1152]{1,0:T(8,128)(2,1)S(1)}, bf16[32,1152]{1,0:T(8,128)(2,1)S(1)}, u32[]{:S(2)}, u32[]{:S(2)}) collective-permute-start(bf16[32,1152]{1,0:T(8,128)(2,1)S(1)} %get-tuple-element.42), channel_id=1, source_target_pairs={{0,3},{1,2},{2,1},{3,0},{4,7},{5,6},{6,5},{7,4},{8,11},{9,10},{10,... | collective-permute-start | bytes 221192 | tf_op jit(solution)/shard_map/ppermute | solution.py:640
  9.2 11.9 %collective-permute-start.4 = (bf16[32,1152]{1,0:T(8,128)(2,1)S(1)}, bf16[32,1152]{1,0:T(8,128)(2,1)S(1)}, u32[]{:S(2)}, u32[]{:S(2)}) collective-permute-start(bf16[32,1152]{1,0:T(8,128)(2,1)S(1)} %get-tuple-element.43), channel_id=1, source_target_pairs={{0,2},{1,3},{2,0},{3,1},{4,6},{5,7},{6,4},{7,5},{8,10},{9,11},{10,... | collective-permute-start | bytes 221192 | tf_op jit(solution)/shard_map/ppermute | solution.py:640
  11.8 0.7 %copy-start = (s32[24,2]{0,1:T(2,128)S(1)}, s32[24,2]{0,1:T(2,128)}, u32[]{:S(2)}) copy-start(s32[24,2]{0,1:T(2,128)} %param.11) | copy-start | bytes 580
  21.5 7.2 %collective-permute-start.5 = (bf16[32,2432]{1,0:T(8,128)(2,1)S(1)}, bf16[32,2432]{1,0:T(8,128)(2,1)S(1)}, u32[]{:S(2)}, u32[]{:S(2)}) collective-permute-start(bf16[32,2432]{1,0:T(8,128)(2,1)S(1)} %collective-permute-done.refs_2_), channel_id=1, source_target_pairs={{0,4},{4,0},{8,12},{12,8},{1,5},{5,1},{9,13},{13,9},{2,6},{6,2},{1... | collective-permute-start | bytes 466952 | tf_op jit(solution)/shard_map/ppermute | solution.py:640
  22.0 9.9 %collective-permute-start.6 = (bf16[32,2304]{1,0:T(8,128)(2,1)S(1)}, bf16[32,2304]{1,0:T(8,128)(2,1)S(1)}, u32[]{:S(2)}, u32[]{:S(2)}) collective-permute-start(bf16[32,2304]{1,0:T(8,128)(2,1)S(1)} %collective-permute-done.1.refs_6_.refs_3_), channel_id=1, source_target_pairs={{0,4},{4,0},{8,12},{12,8},{1,5},{5,1},{9,13},{13,9},{2,6},{6,2},{1... | collective-permute-start | bytes 442376 | tf_op jit(solution)/shard_map/ppermute | solution.py:640
  24.2 10.0 %collective-permute-start.7 = (bf16[96,1152]{1,0:T(8,128)(2,1)S(1)}, bf16[96,1152]{1,0:T(8,128)(2,1)S(1)}, u32[]{:S(2)}, u32[]{:S(2)}) collective-permute-start(bf16[96,1152]{1,0:T(8,128)(2,1)S(1)} %get-tuple-element.59), channel_id=1, source_target_pairs={{0,1},{1,0},{2,3},{3,2},{4,5},{5,4},{6,7},{7,6},{8,9},{9,8},{10,11... | collective-permute-start | bytes 663560 | tf_op jit(solution)/shard_map/ppermute | solution.py:640
  24.3 14.9 %collective-permute-start.11 = (bf16[64,1152]{1,0:T(8,128)(2,1)S(1)}, bf16[64,1152]{1,0:T(8,128)(2,1)S(1)}, u32[]{:S(2)}, u32[]{:S(2)}) collective-permute-start(bf16[64,1152]{1,0:T(8,128)(2,1)S(1)} %get-tuple-element.66), channel_id=1, source_target_pairs={{0,3},{1,2},{2,1},{3,0},{4,7},{5,6},{6,5},{7,4},{8,11},{9,10},{10,... | collective-permute-start | bytes 442376 | tf_op jit(solution)/shard_map/ppermute | solution.py:640
  25.9 13.3 %collective-permute-start.12 = (bf16[64,1152]{1,0:T(8,128)(2,1)S(1)}, bf16[64,1152]{1,0:T(8,128)(2,1)S(1)}, u32[]{:S(2)}, u32[]{:S(2)}) collective-permute-start(bf16[64,1152]{1,0:T(8,128)(2,1)S(1)} %get-tuple-element.68), channel_id=1, source_target_pairs={{0,2},{1,3},{2,0},{3,1},{4,6},{5,7},{6,4},{7,5},{8,10},{9,11},{10,... | collective-permute-start | bytes 442376 | tf_op jit(solution)/shard_map/ppermute | solution.py:640
  34.2 5.2 %collective-permute-start.8 = (f32[8,128]{1,0:T(8,128)S(1)}, f32[8,128]{1,0:T(8,128)S(1)}, u32[]{:S(2)}, u32[]{:S(2)}) collective-permute-start(f32[8,128]{1,0:T(8,128)S(1)} %get-tuple-element.60.refs_0_), channel_id=1, source_target_pairs={{0,4},{4,0},{8,12},{12,8},{1,5},{5,1},{9,13},{13,9},{2,6},{6,2},{1... | collective-permute-start | bytes 12296 | tf_op jit(solution)/shard_map/ppermute | solution.py:640
  34.7 4.7 %collective-permute-start.9 = (f32[8,128]{1,0:T(8,128)S(1)}, f32[8,128]{1,0:T(8,128)S(1)}, u32[]{:S(2)}, u32[]{:S(2)}) collective-permute-start(f32[8,128]{1,0:T(8,128)S(1)} %get-tuple-element.60.refs_0_), channel_id=1, source_target_pairs={{0,8},{4,12},{8,0},{12,4},{1,9},{5,13},{9,1},{13,5},{2,10},{6,14},... | collective-permute-start | bytes 12296 | tf_op jit(solution)/shard_map/ppermute | solution.py:640
  37.3 5.4 %collective-permute-start.10 = (f32[8,128]{1,0:T(8,128)S(1)}, f32[8,128]{1,0:T(8,128)S(1)}, u32[]{:S(2)}, u32[]{:S(2)}) collective-permute-start(f32[8,128]{1,0:T(8,128)S(1)} %get-tuple-element.60.refs_0_), channel_id=1, source_target_pairs={{0,12},{4,8},{8,4},{12,0},{1,13},{5,9},{9,5},{13,1},{2,14},{6,10},... | collective-permute-start | bytes 12296 | tf_op jit(solution)/shard_map/ppermute | solution.py:640
  39.2 11.5 %collective-permute-start.16 = (bf16[96,1152]{1,0:T(8,128)(2,1)S(1)}, bf16[96,1152]{1,0:T(8,128)(2,1)S(1)}, u32[]{:S(2)}, u32[]{:S(2)}) collective-permute-start(bf16[96,1152]{1,0:T(8,128)(2,1)S(1)} %bundle.1), channel_id=1, source_target_pairs={{0,4},{4,0},{8,12},{12,8},{1,5},{5,1},{9,13},{13,9},{2,6},{6,2},{1... | collective-permute-start | bytes 663560 | tf_op jit(solution)/shard_map/ppermute | solution.py:640
  43.2 5.2 %collective-permute-start.13 = (bf16[416,128]{1,0:T(8,128)(2,1)S(1)}, bf16[416,128]{1,0:T(8,128)(2,1)S(1)}, u32[]{:S(2)}, u32[]{:S(2)}) collective-permute-start(bf16[416,128]{1,0:T(8,128)(2,1)S(1)} %get-tuple-element.73.refs_0_), channel_id=1, source_target_pairs={{0,3},{1,2},{2,1},{3,0},{4,7},{5,6},{6,5},{7,4},{8,11},{9,10},{10,... | collective-permute-start | bytes 319496 | tf_op jit(solution)/shard_map/ppermute | solution.py:640
  43.2 7.5 %collective-permute-start.14 = (bf16[416,128]{1,0:T(8,128)(2,1)S(1)}, bf16[416,128]{1,0:T(8,128)(2,1)S(1)}, u32[]{:S(2)}, u32[]{:S(2)}) collective-permute-start(bf16[416,128]{1,0:T(8,128)(2,1)S(1)} %get-tuple-element.73.refs_0_), channel_id=1, source_target_pairs={{0,2},{1,3},{2,0},{3,1},{4,6},{5,7},{6,4},{7,5},{8,10},{9,11},{10,... | collective-permute-start | bytes 319496 | tf_op jit(solution)/shard_map/ppermute | solution.py:640
  44.8 6.0 %collective-permute-start.15 = (bf16[416,128]{1,0:T(8,128)(2,1)S(1)}, bf16[416,128]{1,0:T(8,128)(2,1)S(1)}, u32[]{:S(2)}, u32[]{:S(2)}) collective-permute-start(bf16[416,128]{1,0:T(8,128)(2,1)S(1)} %get-tuple-element.73.refs_0_), channel_id=1, source_target_pairs={{0,1},{1,0},{2,3},{3,2},{4,5},{5,4},{6,7},{7,6},{8,9},{9,8},{10,11... | collective-permute-start | bytes 319496 | tf_op jit(solution)/shard_map/ppermute | solution.py:640

commit v15 on v13

--- a/solution.py
+++ b/solution.py
@@ -237,30 +237,37 @@
     )
 
 
-def first_score_kernel(chunked, half, early_hbm, cls_ref, cos_ref, sin_ref, *refs):
-    refs, (acc_ref, late_ref, *buffers, sem) = refs[:-5], refs[-5:]
-    count, _, width = late_ref.shape
+def template_kernel(early_hbm, cls_ref, cos_ref, sin_ref, temp_ref, late_ref, sem):
+    count, _, width = temp_ref.shape
     tile = width // 2
     copies = [
-        pltpu.make_async_copy(early_hbm.at[t], late_ref.at[t], sem.at[t]) for t in range(count)
+        pltpu.make_async_copy(early_hbm.at[t], late_ref.at[t], sem.at[t])
+        for t in range(late_ref.shape[0])
     ]
     for copy in copies:
         copy.start()
+
+    @pl.loop(0, count)
+    def _(t):
+        write_templates(cls_ref, cos_ref, sin_ref, temp_ref.at[t], t * tile, tile)
+
+    for copy in copies:
+        copy.wait()
+
+
+def first_score_kernel(chunked, half, temp_ref, *refs):
+    refs, acc_ref = refs[:-1], refs[-1]
+    count, _, width = temp_ref.shape
+    tile = width // 2
     shards = list(zip(refs, chunked))
-    built = cls_ref.shape[2] // tile - count
     acc_ref[...] = jnp.zeros_like(acc_ref)
-    write_templates(cls_ref, cos_ref, sin_ref, buffers[0], 0, tile)
-    for t in range(built):
-        if t + 1 < built:
-            write_templates(cls_ref, cos_ref, sin_ref, buffers[(t + 1) % 2], (t + 1) * tile, tile)
+    for t in range(count):
         acc_ref[...] += lax.dot_general(
-            buffers[t % 2][...],
-            tile_of_particles(shards, 0, built * tile, t, tile, half),
+            temp_ref[t],
+            tile_of_particles(shards, 0, count * tile, t, tile, half),
             NT,
             preferred_element_type=f32,
         )
-    for copy in copies:
-        copy.wait()
 
 
 def last_score_kernel(chunked, half, temp_ref, pow_ref, acc_ref, *refs):
@@ -302,26 +309,32 @@
 
 def score(early, split, cos_t, sin_t, power, shards, half):
     count, columns, width = early.shape
+    freq = split.shape[2]
     lanes = sum(refs[0].shape[0] for refs in shards)
     chunked = [len(refs) > 1 for refs in shards]
     flops = 2 * columns * 256 * count * width
     acc_shape = jax.ShapeDtypeStruct((columns, lanes), f32)
-    operands = [pltpu.with_memory_space_constraint(early, pltpu.HBM), split, cos_t, sin_t]
-    operands += [refs[0] for refs in shards]
-    acc, late = call(
+    temps, late = call(
+        template_kernel,
+        "templates",
+        [ANY] + [VMEM] * 3,
+        [pltpu.VMEM(early.shape, bf16)] * 2,
+        (pltpu.with_memory_space_constraint(early, pltpu.HBM), split, cos_t, sin_t),
+        [pltpu.SemaphoreType.DMA((count,))],
+        flops=20 * columns * freq,
+        moved=2 * columns * freq,
+    )
+    operands = [temps, *[refs[0] for refs in shards]]
+    acc = call(
         functools.partial(first_score_kernel, chunked, half),
         "score0",
-        [ANY] + [VMEM] * (len(operands) - 1),
-        [acc_shape, pltpu.VMEM(early.shape, bf16)],
+        [VMEM] * len(operands),
+        [acc_shape],
         operands,
-        [
-            pltpu.VMEM((columns, width), bf16),
-            pltpu.VMEM((columns, width), bf16),
-            pltpu.SemaphoreType.DMA((count,)),
-        ],
-        flops=4 * flops,
-    )
-    operands = [late, power, acc, *[refs[0] for refs in shards], *[refs[-1] for refs in shards]]
+        flops=flops,
+    )[0]
+    operands = [late, power, acc]
+    operands += [refs[0] for refs in shards] + [refs[-1] for refs in shards]
     return call(
         functools.partial(last_score_kernel, chunked, half),
         "score1",
@@ -646,8 +659,8 @@
     scores, marks, stat = score(early, split, cos_t, sin_t, power, shards, half)
     if pairwise:
         stat, arrived[-1] = lax.optimization_barrier((stat, arrived[-1]))
-        stats = [stat] + [swap(stat, "cls", k) for k in range(1, n_cls)]
-        paired = tuple(range(n_cls))
+        stats = [stat] + [swap(stat, "cls", k) for k in range(n_cls - 1, 0, -1)]
+        paired = (0,) + tuple(range(n_cls - 1, 0, -1))
         last = [*cut_slices(me, [third], [(0, 0)], span, freq)]
         last.append(swap(bundle(arrived[1:], 2 * half), "cls", 1))
         slices = [[a, b] for a, b in zip(slices, arrived)] + [arrived[-1:]]

time: 55.9 us -> 52.1 us (0.932)
  waiting for transfers between devices: 10.6 us -> 7.53 us
  Pallas kernels: 24.1 us -> 23.3 us
    ppermute x17, waiting for transfers between devices: 10.6 us -> 7.53 us  [swap(): return lax.ppermute(values, axis, [(i, i ^ distance) for i in range(size)])]
    pallas_call x11 -> x12, Pallas kernels: 19.6 us -> 18.8 us  [call(): pl.pallas_call(kernel, in_specs=in_specs, out_specs=[VMEM] * len(out_shap...]
  transfers between devices with their start and end apart: 17 -> 17, of which waited for: 5 -> 5; matrix products, arithmetic and copies ran while one was open for 2% -> 2% of each run, Pallas kernels for 35% -> 36%
where the time goes in v15:
time: 52.1 us; the launch traced here: 51.9 us
  Pallas kernels  23.3 us (45%)
  starting transfers between devices  18.4 us (35%)
  waiting for transfers between devices  7.53 us (14%)
  local copies, waits for them, and re-layouts  1.8 us (3%)
  between operations  0.77 us (1%)
    pallas_call x12, Pallas kernels, call(): pl.pallas_call(kernel, in_specs=in_specs, out_specs=[VMEM] * len(out_shap...  18.8 us
    ppermute x17, starting transfers between devices, swap(): return lax.ppermute(values, axis, [(i, i ^ distance) for i in range(size)])  18.4 us
    ppermute x17, waiting for transfers between devices, swap(): return lax.ppermute(values, axis, [(i, i ^ distance) for i in range(size)])  7.53 us
    pallas_call x1, Pallas kernels, early_templates(): pl.pallas_call(early_kernel, grid=(count,), in_specs=[pl.BlockSpec((2, ro...  4.53 us
    unnamed x3, local copies, waits for them, and re-layouts  1.8 us
  transfers between devices with their start and end apart: 17, of which 5 were waited for; matrix products, arithmetic and copies ran while one was open for 2% of the time, Pallas kernels for 36%

profile of v15, /device:TPU:0, one launch (start us, length us, event | category | flops | bytes accessed | tf_op | source)
XLA Modules:
  0.0 51.9 jit_solution(16868210507141544064)
XLA Ops:
  0.6 1.7 %weigh.1 = (bf16[32,4736]{1,0:T(8,128)(2,1)S(1)}, bf16[32,2432]{1,0:T(8,128)(2,1)S(1)}, bf16[32,2304]{1,0:T(8,128)(2,1)S(1)}) custom-call(s32[16]{0:T(128)} %ids_hbm.1, bf16[16,2,4608]{2,1,0:T(2,128)(2,1)} %p_hbm.1, f32[64,4608]{1,0:T(8,128)} %ctf_hbm.3, f32[4608]{0:T(1024)} %nw_hbm.3), custom_call_target="tpu_custom_call" | custom-call | flops 294912 | bytes 1179648 | tf_op jit(solution)/shard_map/weigh/pallas_call | solution.py:30
  2.4 3.1 %collective-permute-start.2 = (bf16[32,4736]{1,0:T(8,128)(2,1)S(1)}, bf16[32,4736]{1,0:T(8,128)(2,1)S(1)}, u32[]{:S(2)}, u32[]{:S(2)}) collective-permute-start(bf16[32,4736]{1,0:T(8,128)(2,1)S(1)} %get-tuple-element.38.refs_0_.refs_4_), channel_id=1, source_target_pairs={{0,4},{4,0},{8,12},{12,8},{1,5},{5,1},{9,13},{13,9},{2,6},{6,2},{1... | collective-permute-start | bytes 909320 | tf_op jit(solution)/shard_map/ppermute | solution.py:621
  5.4 2.6 %collective-permute-start = (bf16[32,2432]{1,0:T(8,128)(2,1)S(1)}, bf16[32,2432]{1,0:T(8,128)(2,1)S(1)}, u32[]{:S(2)}, u32[]{:S(2)}) collective-permute-start(bf16[32,2432]{1,0:T(8,128)(2,1)S(1)} %get-tuple-element.36), channel_id=1, source_target_pairs={{0,8},{4,12},{8,0},{12,4},{1,9},{5,13},{9,1},{13,5},{2,10},{6,14},... | collective-permute-start | bytes 466952 | tf_op jit(solution)/shard_map/ppermute | solution.py:621
  8.0 0.3 collective-permute-start.1
  8.4 0.1 pad_add_fusion.me_ref
  8.4 0.6 %cut_slices.3 = (bf16[32,1152]{1,0:T(8,128)(2,1)S(1)}, bf16[32,1152]{1,0:T(8,128)(2,1)S(1)}, bf16[32,1152]{1,0:T(8,128)(2,1)S(1)}) custom-call(s32[2]{0:T(128)S(1)} %pad_add_fusion.me_ref, bf16[32,4736]{1,0:T(8,128)(2,1)S(1)} %get-tuple-element.38.refs_0_.refs_4_), custom_call_target="tpu_custom_call" | custom-call | bytes 442368 | tf_op jit(solution)/shard_map/cut_slices/pallas_call | solution.py:30
  9.0 0.2 collective-permute-start.3
  9.2 1.5 %collective-permute-start.4 = (bf16[32,1152]{1,0:T(8,128)(2,1)S(1)}, bf16[32,1152]{1,0:T(8,128)(2,1)S(1)}, u32[]{:S(2)}, u32[]{:S(2)}) collective-permute-start(bf16[32,1152]{1,0:T(8,128)(2,1)S(1)} %get-tuple-element.41), channel_id=1, source_target_pairs={{0,2},{1,3},{2,0},{3,1},{4,6},{5,7},{6,4},{7,5},{8,10},{9,11},{10,... | collective-permute-start | bytes 221192 | tf_op jit(solution)/shard_map/ppermute | solution.py:621
  10.7 1.1 %copy.10 = bf16[32,2,4608]{2,0,1:T(8,128)(2,1)S(1)} copy(bf16[32,2,4608]{2,1,0:T(2,128)(2,1)} %param.7) | data formatting | bytes 1179648 | tf_op args[1]
  11.8 0.0 copy-start
  11.8 0.7 %copy-done = s32[24,2]{0,1:T(2,128)S(1)} copy-done((s32[24,2]{0,1:T(2,128)S(1)}, s32[24,2]{0,1:T(2,128)}, u32[]{:S(2)}) %copy-start) | copy-done | bytes 216
  12.5 3.1 %prepare.1 = (f32[24,4608]{1,0:T(8,128)S(1)}, f32[24,4608]{1,0:T(8,128)S(1)}, f32[32,64]{1,0:T(8,128)S(1)}, f32[64,4608]{1,0:T(8,128)S(1)}) custom-call(s32[2,24]{1,0:T(2,128)S(1)} %bitcast.10, bf16[2,32,4608]{2,1,0:T(8,128)(2,1)S(1)} %bitcast.7, f32[64,4608]{1,0:T(8,128)} %ctf_hbm.3, f32[4608]{0:T(1024)} %nw_hbm.3), custom_call_target="tpu_custom_call" | custom-call | flops 226492416 | tf_op jit(solution)/shard_map/prepare/pallas_call | solution.py:30
  15.6 4.5 %early_templates.1.early_hbm = bf16[6,768,768]{2,1,0:T(8,128)(2,1)} custom-call(bf16[2,32,4608]{2,1,0:T(8,128)(2,1)S(1)} %bitcast.8, f32[24,4608]{1,0:T(8,128)S(1)} %get-tuple-element.42.cos_ref, f32[24,4608]{1,0:T(8,128)S(1)} %get-tuple-element.43.sin_ref), custom_call_target="tpu_custom_call" | custom-call | flops 70778880 | bytes 7077888 | tf_op jit(solution)/shard_map/early_templates/pallas_call | solution.py:205
  20.1 0.0 collective-permute-done.3.refs_2_
  20.1 0.0 collective-permute-done.4.refs_4_
  20.1 1.4 %collective-permute-done.1.refs_6_.refs_3_ = bf16[32,2304]{1,0:T(8,128)(2,1)S(1)} collective-permute-done((bf16[32,2304]{1,0:T(8,128)(2,1)S(1)}, bf16[32,2304]{1,0:T(8,128)(2,1)S(1)}, u32[]{:S(2)}, u32[]{:S(2)}) %collective-permute-start.1) | collective-permute-done | bytes 147488 | tf_op jit(solution)/shard_map/ppermute | solution.py:621
  21.5 0.0 collective-permute-done.refs_2_
  21.5 0.0 collective-permute-done.2.refs_1_.refs_5_
  21.5 0.5 collective-permute-start.5
  22.0 1.6 %collective-permute-start.6 = (bf16[32,2304]{1,0:T(8,128)(2,1)S(1)}, bf16[32,2304]{1,0:T(8,128)(2,1)S(1)}, u32[]{:S(2)}, u32[]{:S(2)}) collective-permute-start(bf16[32,2304]{1,0:T(8,128)(2,1)S(1)} %collective-permute-done.1.refs_6_.refs_3_), channel_id=1, source_target_pairs={{0,4},{4,0},{8,12},{12,8},{1,5},{5,1},{9,13},{13,9},{2,6},{6,2},{1... | collective-permute-start | bytes 442376 | tf_op jit(solution)/shard_map/ppermute | solution.py:621
  23.6 0.6 %cut_slices.4 = (bf16[64,1152]{1,0:T(8,128)(2,1)S(1)}, bf16[64,1152]{1,0:T(8,128)(2,1)S(1)}, bf16[64,1152]{1,0:T(8,128)(2,1)S(1)}, bf16[96,1152]{1,0:T(8,128)(2,1)S(1)}) custom-call(s32[2]{0:T(128)S(1)} %pad_add_fusion.me_ref, bf16[32,4736]{1,0:T(8,128)(2,1)S(1)} %get-tuple-element.38.refs_0_.refs_4_, ...), custom_call_target="tpu_custom_call" | custom-call | bytes 1327104 | tf_op jit(solution)/shard_map/cut_slices/pallas_call | solution.py:30
  24.2 0.1 collective-permute-start.7
  24.3 1.6 %collective-permute-start.11 = (bf16[64,1152]{1,0:T(8,128)(2,1)S(1)}, bf16[64,1152]{1,0:T(8,128)(2,1)S(1)}, u32[]{:S(2)}, u32[]{:S(2)}) collective-permute-start(bf16[64,1152]{1,0:T(8,128)(2,1)S(1)} %get-tuple-element.62), channel_id=1, source_target_pairs={{0,3},{1,2},{2,1},{3,0},{4,7},{5,6},{6,5},{7,4},{8,11},{9,10},{10,... | collective-permute-start | bytes 442376 | tf_op jit(solution)/shard_map/ppermute | solution.py:621
  25.9 0.5 %collective-permute-start.12 = (bf16[64,1152]{1,0:T(8,128)(2,1)S(1)}, bf16[64,1152]{1,0:T(8,128)(2,1)S(1)}, u32[]{:S(2)}, u32[]{:S(2)}) collective-permute-start(bf16[64,1152]{1,0:T(8,128)(2,1)S(1)} %get-tuple-element.64), channel_id=1, source_target_pairs={{0,2},{1,3},{2,0},{3,1},{4,6},{5,7},{6,4},{7,5},{8,10},{9,11},{10,... | collective-permute-start | bytes 442376 | tf_op jit(solution)/shard_map/ppermute | solution.py:621
  26.4 3.1 %templates.1 = (bf16[6,768,768]{2,1,0:T(8,128)(2,1)S(1)}, bf16[6,768,768]{2,1,0:T(8,128)(2,1)S(1)}) custom-call(bf16[6,768,768]{2,1,0:T(8,128)(2,1)} %early_templates.1.early_hbm, bf16[2,32,4608]{2,1,0:T(8,128)(2,1)S(1)} %bitcast.9, f32[24,4608]{1,0:T(8,128)S(1)} %get-tuple-element.42.cos_ref, f32[24,4608]{1,0:T(8,128)S(1)} %get-tuple-element.43.sin_ref), custom_call_target="tpu_custom_call" | custom-call | flops 70778880 | bytes 7077888 | tf_op jit(solution)/shard_map/templates/pallas_call | solution.py:30
  29.5 0.0 collective-permute-done.5.refs_3_.refs_0_
  29.5 2.0 %score0.1.acc_ref = f32[768,128]{1,0:T(8,128)S(1)} custom-call(bf16[6,768,768]{2,1,0:T(8,128)(2,1)S(1)} %get-tuple-element.48.temp_ref, bf16[32,4736]{1,0:T(8,128)(2,1)S(1)} %get-tuple-element.38.refs_0_.refs_4_, bf16[32,4736]{1,0:T(8,128)(2,1)S(1)} %collective-permute-done.2.refs_1_.refs_5_, bf16[32,2432]{1,0:T(8,128)(2,1)S(1)} %collective-permute-done.refs_2_, ...), custom_call_target="tpu_custom_call" | custom-call | flops 1811939328 | tf_op jit(solution)/shard_map/score0/pallas_call | solution.py:30
  31.5 0.0 collective-permute-done.6.refs_7_.refs_1_
  31.5 2.2 %score1.1 = (f32[768,128]{1,0:T(8,128)S(1)}, f32[128,64]{1,0:T(8,128)S(1)}, f32[8,128]{1,0:T(8,128)S(1)}) custom-call(bf16[6,768,768]{2,1,0:T(8,128)(2,1)S(1)} %get-tuple-element.46.temp_ref, f32[32,64]{1,0:T(8,128)S(1)} %get-tuple-element.47.pow_ref, f32[768,128]{1,0:T(8,128)S(1)} %score0.1.acc_ref, bf16[32,4736]{1,0:T(8,128)(2,1)S(1)} %get-tuple-element.38.refs_0_.refs_4_, ...), custom_call_target="tpu_custom_call" | custom-call | flops 1811939328 | tf_op jit(solution)/shard_map/score1/pallas_call | solution.py:30
  33.8 0.0 collective-permute-done.7.refs_6_.refs_2_
  33.8 2.5 %collective-permute-start.8 = (f32[8,128]{1,0:T(8,128)S(1)}, f32[8,128]{1,0:T(8,128)S(1)}, u32[]{:S(2)}, u32[]{:S(2)}) collective-permute-start(f32[8,128]{1,0:T(8,128)S(1)} %get-tuple-element.56.refs_0_), channel_id=1, source_target_pairs={{0,12},{4,8},{8,4},{12,0},{1,13},{5,9},{9,5},{13,1},{2,14},{6,10},... | collective-permute-start | bytes 12296 | tf_op jit(solution)/shard_map/ppermute | solution.py:621
  36.3 0.0 collective-permute-start.9
  36.3 1.9 %collective-permute-start.10 = (f32[8,128]{1,0:T(8,128)S(1)}, f32[8,128]{1,0:T(8,128)S(1)}, u32[]{:S(2)}, u32[]{:S(2)}) collective-permute-start(f32[8,128]{1,0:T(8,128)S(1)} %get-tuple-element.56.refs_0_), channel_id=1, source_target_pairs={{0,4},{4,0},{8,12},{12,8},{1,5},{5,1},{9,13},{13,9},{2,6},{6,2},{1... | collective-permute-start | bytes 12296 | tf_op jit(solution)/shard_map/ppermute | solution.py:621
  38.2 0.6 %cut_slices.5.refs_4_ = bf16[32,1152]{1,0:T(8,128)(2,1)S(1)} custom-call(s32[2]{0:T(128)S(1)} %pad_add_fusion.me_ref, bf16[32,2432]{1,0:T(8,128)(2,1)S(1)} %collective-permute-done.5.refs_3_.refs_0_, bf16[32,2304]{1,0:T(8,128)(2,1)S(1)} %collective-permute-done.6.refs_7_.refs_1_), custom_call_target="tpu_custom_call" | custom-call | bytes 147456 | tf_op jit(solution)/shard_map/cut_slices/pallas_call | solution.py:30
  38.8 0.0 collective-permute-done.11.refs_3_.refs_0_
  38.8 0.0 collective-permute-done.12.refs_5_.refs_1_
  38.8 0.2 collective-permute-start.16
  39.0 0.2 collective-permute-done.8.refs_1_
  39.2 1.7 %collective-permute-done.9.refs_2_ = f32[8,128]{1,0:T(8,128)S(1)} collective-permute-done((f32[8,128]{1,0:T(8,128)S(1)}, f32[8,128]{1,0:T(8,128)S(1)}, u32[]{:S(2)}, u32[]{:S(2)}) %collective-permute-start.9) | collective-permute-done | bytes 4128 | tf_op jit(solution)/shard_map/ppermute | solution.py:621
  40.9 0.0 collective-permute-done.10.refs_3_
  40.9 0.5 responsibilities.1
  41.4 0.0 collective-permute-start.13
  41.4 1.6 %collective-permute-start.14 = (bf16[416,128]{1,0:T(8,128)(2,1)S(1)}, bf16[416,128]{1,0:T(8,128)(2,1)S(1)}, u32[]{:S(2)}, u32[]{:S(2)}) collective-permute-start(bf16[416,128]{1,0:T(8,128)(2,1)S(1)} %get-tuple-element.69.refs_0_), channel_id=1, source_target_pairs={{0,2},{1,3},{2,0},{3,1},{4,6},{5,7},{6,4},{7,5},{8,10},{9,11},{10,... | collective-permute-start | bytes 319496 | tf_op jit(solution)/shard_map/ppermute | solution.py:621
  43.0 0.3 collective-permute-start.15
  43.3 1.5 %gather_rows.1 = (f32[32,64]{1,0:T(8,128)}, bf16[64,2304]{1,0:T(8,128)(2,1)S(1)}, bf16[2,192,1152]{2,1,0:T(8,128)(2,1)S(1)}) custom-call(s32[2]{0:T(128)S(1)} %pad_add_fusion.me_ref, f32[768,128]{1,0:T(8,128)S(1)} %get-tuple-element.52.s_ref, f32[1,128]{1,0:T(1,128)S(1)} %get-tuple-element.57.norm_ref, f32[64,4608]{1,0:T(8,128)S(1)} %get-tuple-element.58.weight_ref, ...), custom_call_target="tpu_custom_call" | custom-call | flops 20000000000 | bytes 1769472 | tf_op jit(solution)/shard_map/gather_rows/pallas_call | solution.py:30
  44.8 1.9 %collective-permute-done.13.refs_1_ = bf16[416,128]{1,0:T(8,128)(2,1)S(1)} collective-permute-done((bf16[416,128]{1,0:T(8,128)(2,1)S(1)}, bf16[416,128]{1,0:T(8,128)(2,1)S(1)}, u32[]{:S(2)}, u32[]{:S(2)}) %collective-permute-start.13) | collective-permute-done | bytes 106528 | tf_op jit(solution)/shard_map/ppermute | solution.py:621
  46.7 2.3 %collective-permute-done.14.refs_2_ = bf16[416,128]{1,0:T(8,128)(2,1)S(1)} collective-permute-done((bf16[416,128]{1,0:T(8,128)(2,1)S(1)}, bf16[416,128]{1,0:T(8,128)(2,1)S(1)}, u32[]{:S(2)}, u32[]{:S(2)}) %collective-permute-start.14) | collective-permute-done | bytes 106528 | tf_op jit(solution)/shard_map/ppermute | solution.py:621
  49.0 2.9 %finish.1 = f32[32,2,1152]{2,1,0:T(2,128)} custom-call(s32[2]{0:T(128)S(1)} %pad_add_fusion.me_ref, bf16[64,2304]{1,0:T(8,128)(2,1)S(1)} %get-tuple-element.67.cw_ref, f32[24,4608]{1,0:T(8,128)S(1)} %get-tuple-element.42.cos_ref, f32[24,4608]{1,0:T(8,128)S(1)} %get-tuple-element.43.sin_ref, bf16[2,192,1152]{2,1,0:T(8,128)(2,1)S(1)} %get-tuple-element.68.rows_ref, ...), custom_call_target="tpu_custom_call" | custom-call | flops 905969664 | tf_op jit(solution)/shard_map/finish/pallas_call | solution.py:30
  (3 shorter events, 0.0 us)
Async XLA Ops:
  2.4 19.2 %collective-permute-start.2 = (bf16[32,4736]{1,0:T(8,128)(2,1)S(1)}, bf16[32,4736]{1,0:T(8,128)(2,1)S(1)}, u32[]{:S(2)}, u32[]{:S(2)}) collective-permute-start(bf16[32,4736]{1,0:T(8,128)(2,1)S(1)} %get-tuple-element.38.refs_0_.refs_4_), channel_id=1, source_target_pairs={{0,4},{4,0},{8,12},{12,8},{1,5},{5,1},{9,13},{13,9},{2,6},{6,2},{1... | collective-permute-start | bytes 909320 | tf_op jit(solution)/shard_map/ppermute | solution.py:621
  5.4 16.1 %collective-permute-start = (bf16[32,2432]{1,0:T(8,128)(2,1)S(1)}, bf16[32,2432]{1,0:T(8,128)(2,1)S(1)}, u32[]{:S(2)}, u32[]{:S(2)}) collective-permute-start(bf16[32,2432]{1,0:T(8,128)(2,1)S(1)} %get-tuple-element.36), channel_id=1, source_target_pairs={{0,8},{4,12},{8,0},{12,4},{1,9},{5,13},{9,1},{13,5},{2,10},{6,14},... | collective-permute-start | bytes 466952 | tf_op jit(solution)/shard_map/ppermute | solution.py:621
  8.0 13.5 %collective-permute-start.1 = (bf16[32,2304]{1,0:T(8,128)(2,1)S(1)}, bf16[32,2304]{1,0:T(8,128)(2,1)S(1)}, u32[]{:S(2)}, u32[]{:S(2)}) collective-permute-start(bf16[32,2304]{1,0:T(8,128)(2,1)S(1)} %get-tuple-element.37), channel_id=1, source_target_pairs={{0,8},{4,12},{8,0},{12,4},{1,9},{5,13},{9,1},{13,5},{2,10},{6,14},... | collective-permute-start | bytes 442376 | tf_op jit(solution)/shard_map/ppermute | solution.py:621
  9.0 11.1 %collective-permute-start.3 = (bf16[32,1152]{1,0:T(8,128)(2,1)S(1)}, bf16[32,1152]{1,0:T(8,128)(2,1)S(1)}, u32[]{:S(2)}, u32[]{:S(2)}) collective-permute-start(bf16[32,1152]{1,0:T(8,128)(2,1)S(1)} %get-tuple-element.40), channel_id=1, source_target_pairs={{0,3},{1,2},{2,1},{3,0},{4,7},{5,6},{6,5},{7,4},{8,11},{9,10},{10,... | collective-permute-start | bytes 221192 | tf_op jit(solution)/shard_map/ppermute | solution.py:621
  9.2 10.9 %collective-permute-start.4 = (bf16[32,1152]{1,0:T(8,128)(2,1)S(1)}, bf16[32,1152]{1,0:T(8,128)(2,1)S(1)}, u32[]{:S(2)}, u32[]{:S(2)}) collective-permute-start(bf16[32,1152]{1,0:T(8,128)(2,1)S(1)} %get-tuple-element.41), channel_id=1, source_target_pairs={{0,2},{1,3},{2,0},{3,1},{4,6},{5,7},{6,4},{7,5},{8,10},{9,11},{10,... | collective-permute-start | bytes 221192 | tf_op jit(solution)/shard_map/ppermute | solution.py:621
  11.8 0.7 %copy-start = (s32[24,2]{0,1:T(2,128)S(1)}, s32[24,2]{0,1:T(2,128)}, u32[]{:S(2)}) copy-start(s32[24,2]{0,1:T(2,128)} %param.11) | copy-start | bytes 580
  21.5 8.0 %collective-permute-start.5 = (bf16[32,2432]{1,0:T(8,128)(2,1)S(1)}, bf16[32,2432]{1,0:T(8,128)(2,1)S(1)}, u32[]{:S(2)}, u32[]{:S(2)}) collective-permute-start(bf16[32,2432]{1,0:T(8,128)(2,1)S(1)} %collective-permute-done.refs_2_), channel_id=1, source_target_pairs={{0,4},{4,0},{8,12},{12,8},{1,5},{5,1},{9,13},{13,9},{2,6},{6,2},{1... | collective-permute-start | bytes 466952 | tf_op jit(solution)/shard_map/ppermute | solution.py:621
  22.0 9.5 %collective-permute-start.6 = (bf16[32,2304]{1,0:T(8,128)(2,1)S(1)}, bf16[32,2304]{1,0:T(8,128)(2,1)S(1)}, u32[]{:S(2)}, u32[]{:S(2)}) collective-permute-start(bf16[32,2304]{1,0:T(8,128)(2,1)S(1)} %collective-permute-done.1.refs_6_.refs_3_), channel_id=1, source_target_pairs={{0,4},{4,0},{8,12},{12,8},{1,5},{5,1},{9,13},{13,9},{2,6},{6,2},{1... | collective-permute-start | bytes 442376 | tf_op jit(solution)/shard_map/ppermute | solution.py:621
  24.2 9.6 %collective-permute-start.7 = (bf16[96,1152]{1,0:T(8,128)(2,1)S(1)}, bf16[96,1152]{1,0:T(8,128)(2,1)S(1)}, u32[]{:S(2)}, u32[]{:S(2)}) collective-permute-start(bf16[96,1152]{1,0:T(8,128)(2,1)S(1)} %get-tuple-element.55), channel_id=1, source_target_pairs={{0,1},{1,0},{2,3},{3,2},{4,5},{5,4},{6,7},{7,6},{8,9},{9,8},{10,11... | collective-permute-start | bytes 663560 | tf_op jit(solution)/shard_map/ppermute | solution.py:621
  24.3 14.5 %collective-permute-start.11 = (bf16[64,1152]{1,0:T(8,128)(2,1)S(1)}, bf16[64,1152]{1,0:T(8,128)(2,1)S(1)}, u32[]{:S(2)}, u32[]{:S(2)}) collective-permute-start(bf16[64,1152]{1,0:T(8,128)(2,1)S(1)} %get-tuple-element.62), channel_id=1, source_target_pairs={{0,3},{1,2},{2,1},{3,0},{4,7},{5,6},{6,5},{7,4},{8,11},{9,10},{10,... | collective-permute-start | bytes 442376 | tf_op jit(solution)/shard_map/ppermute | solution.py:621
  25.9 12.9 %collective-permute-start.12 = (bf16[64,1152]{1,0:T(8,128)(2,1)S(1)}, bf16[64,1152]{1,0:T(8,128)(2,1)S(1)}, u32[]{:S(2)}, u32[]{:S(2)}) collective-permute-start(bf16[64,1152]{1,0:T(8,128)(2,1)S(1)} %get-tuple-element.64), channel_id=1, source_target_pairs={{0,2},{1,3},{2,0},{3,1},{4,6},{5,7},{6,4},{7,5},{8,10},{9,11},{10,... | collective-permute-start | bytes 442376 | tf_op jit(solution)/shard_map/ppermute | solution.py:621
  33.8 5.5 %collective-permute-start.8 = (f32[8,128]{1,0:T(8,128)S(1)}, f32[8,128]{1,0:T(8,128)S(1)}, u32[]{:S(2)}, u32[]{:S(2)}) collective-permute-start(f32[8,128]{1,0:T(8,128)S(1)} %get-tuple-element.56.refs_0_), channel_id=1, source_target_pairs={{0,12},{4,8},{8,4},{12,0},{1,13},{5,9},{9,5},{13,1},{2,14},{6,10},... | collective-permute-start | bytes 12296 | tf_op jit(solution)/shard_map/ppermute | solution.py:621
  36.3 4.6 %collective-permute-start.9 = (f32[8,128]{1,0:T(8,128)S(1)}, f32[8,128]{1,0:T(8,128)S(1)}, u32[]{:S(2)}, u32[]{:S(2)}) collective-permute-start(f32[8,128]{1,0:T(8,128)S(1)} %get-tuple-element.56.refs_0_), channel_id=1, source_target_pairs={{0,8},{4,12},{8,0},{12,4},{1,9},{5,13},{9,1},{13,5},{2,10},{6,14},... | collective-permute-start | bytes 12296 | tf_op jit(solution)/shard_map/ppermute | solution.py:621
  36.3 4.6 %collective-permute-start.10 = (f32[8,128]{1,0:T(8,128)S(1)}, f32[8,128]{1,0:T(8,128)S(1)}, u32[]{:S(2)}, u32[]{:S(2)}) collective-permute-start(f32[8,128]{1,0:T(8,128)S(1)} %get-tuple-element.56.refs_0_), channel_id=1, source_target_pairs={{0,4},{4,0},{8,12},{12,8},{1,5},{5,1},{9,13},{13,9},{2,6},{6,2},{1... | collective-permute-start | bytes 12296 | tf_op jit(solution)/shard_map/ppermute | solution.py:621
  38.8 10.1 %collective-permute-start.16 = (bf16[96,1152]{1,0:T(8,128)(2,1)S(1)}, bf16[96,1152]{1,0:T(8,128)(2,1)S(1)}, u32[]{:S(2)}, u32[]{:S(2)}) collective-permute-start(bf16[96,1152]{1,0:T(8,128)(2,1)S(1)} %bundle.1), channel_id=1, source_target_pairs={{0,4},{4,0},{8,12},{12,8},{1,5},{5,1},{9,13},{13,9},{2,6},{6,2},{1... | collective-permute-start | bytes 663560 | tf_op jit(solution)/shard_map/ppermute | solution.py:621
  41.4 5.2 %collective-permute-start.13 = (bf16[416,128]{1,0:T(8,128)(2,1)S(1)}, bf16[416,128]{1,0:T(8,128)(2,1)S(1)}, u32[]{:S(2)}, u32[]{:S(2)}) collective-permute-start(bf16[416,128]{1,0:T(8,128)(2,1)S(1)} %get-tuple-element.69.refs_0_), channel_id=1, source_target_pairs={{0,3},{1,2},{2,1},{3,0},{4,7},{5,6},{6,5},{7,4},{8,11},{9,10},{10,... | collective-permute-start | bytes 319496 | tf_op jit(solution)/shard_map/ppermute | solution.py:621
  41.4 7.5 %collective-permute-start.14 = (bf16[416,128]{1,0:T(8,128)(2,1)S(1)}, bf16[416,128]{1,0:T(8,128)(2,1)S(1)}, u32[]{:S(2)}, u32[]{:S(2)}) collective-permute-start(bf16[416,128]{1,0:T(8,128)(2,1)S(1)} %get-tuple-element.69.refs_0_), channel_id=1, source_target_pairs={{0,2},{1,3},{2,0},{3,1},{4,6},{5,7},{6,4},{7,5},{8,10},{9,11},{10,... | collective-permute-start | bytes 319496 | tf_op jit(solution)/shard_map/ppermute | solution.py:621
  43.0 6.0 %collective-permute-start.15 = (bf16[416,128]{1,0:T(8,128)(2,1)S(1)}, bf16[416,128]{1,0:T(8,128)(2,1)S(1)}, u32[]{:S(2)}, u32[]{:S(2)}) collective-permute-start(bf16[416,128]{1,0:T(8,128)(2,1)S(1)} %get-tuple-element.69.refs_0_), channel_id=1, source_target_pairs={{0,1},{1,0},{2,3},{3,2},{4,5},{5,4},{6,7},{7,6},{8,9},{9,8},{10,11... | collective-permute-start | bytes 319496 | tf_op jit(solution)/shard_map/ppermute | solution.py:621

commit v16 on v15

--- a/solution.py
+++ b/solution.py
@@ -196,12 +196,9 @@
     write_templates(cls_ref, cos_ref, sin_ref, temp_ref, 0, cls_ref.shape[2])
 
 
-def early_templates(split, cos_t, sin_t):
-    _, rows, freq = split.shape
+def early_templates(split, cos_t, sin_t, skip, count, tile):
+    _, rows, _ = split.shape
     poses = cos_t.shape[0]
-    tile = template_tile(freq)
-    count = freq // tile // 2
-    skip = freq // tile - count
     return pl.pallas_call(
         early_kernel,
         grid=(count,),
@@ -211,13 +208,24 @@
             pl.BlockSpec((poses, tile), lambda j: (0, skip + j)),
         ],
         out_specs=pl.BlockSpec((None, poses * rows, 2 * tile), lambda j: (j, 0, 0)),
-        out_shape=pltpu.HBM((count, poses * rows, 2 * tile), bf16),
+        out_shape=jax.ShapeDtypeStruct((count, poses * rows, 2 * tile), bf16),
         compiler_params=pltpu.CompilerParams(vmem_limit_bytes=VMEM_LIMIT),
         cost_estimate=pl.CostEstimate(
-            flops=20 * poses * rows * freq, bytes_accessed=2 * poses * rows * freq, transcendentals=0
+            flops=40 * poses * rows * count * tile,
+            bytes_accessed=4 * poses * rows * count * tile,
+            transcendentals=0,
         ),
-        name="early_templates",
+        name=f"early_templates{skip}",
     )(split, cos_t, sin_t)
+
+
+def template_kernel(cls_ref, cos_ref, sin_ref, temp_ref):
+    count, _, width = temp_ref.shape
+    tile = width // 2
+
+    @pl.loop(0, count)
+    def _(t):
+        write_templates(cls_ref, cos_ref, sin_ref, temp_ref.at[t], t * tile, tile)
 
 
 def regroup(refs, counts):
@@ -237,33 +245,16 @@
     )
 
 
-def template_kernel(early_hbm, cls_ref, cos_ref, sin_ref, temp_ref, late_ref, sem):
-    count, _, width = temp_ref.shape
-    tile = width // 2
-    copies = [
-        pltpu.make_async_copy(early_hbm.at[t], late_ref.at[t], sem.at[t])
-        for t in range(late_ref.shape[0])
-    ]
-    for copy in copies:
-        copy.start()
-
-    @pl.loop(0, count)
-    def _(t):
-        write_templates(cls_ref, cos_ref, sin_ref, temp_ref.at[t], t * tile, tile)
-
-    for copy in copies:
-        copy.wait()
-
-
-def first_score_kernel(chunked, half, temp_ref, *refs):
+def first_score_kernel(chunked, half, built_ref, early_ref, *refs):
     refs, acc_ref = refs[:-1], refs[-1]
-    count, _, width = temp_ref.shape
-    tile = width // 2
+    tile = built_ref.shape[2] // 2
+    temps = [ref.at[t] for ref in (built_ref, early_ref) for t in range(ref.shape[0])]
+    count = len(temps)
     shards = list(zip(refs, chunked))
     acc_ref[...] = jnp.zeros_like(acc_ref)
     for t in range(count):
         acc_ref[...] += lax.dot_general(
-            temp_ref[t],
+            temps[t][...],
             tile_of_particles(shards, 0, count * tile, t, tile, half),
             NT,
             preferred_element_type=f32,
@@ -308,23 +299,23 @@
 
 
 def score(early, split, cos_t, sin_t, power, shards, half):
-    count, columns, width = early.shape
+    first, late = early
+    count, columns, width = late.shape
     freq = split.shape[2]
     lanes = sum(refs[0].shape[0] for refs in shards)
     chunked = [len(refs) > 1 for refs in shards]
     flops = 2 * columns * 256 * count * width
     acc_shape = jax.ShapeDtypeStruct((columns, lanes), f32)
-    temps, late = call(
+    built = count - first.shape[0]
+    temps = call(
         template_kernel,
         "templates",
-        [ANY] + [VMEM] * 3,
-        [pltpu.VMEM(early.shape, bf16)] * 2,
-        (pltpu.with_memory_space_constraint(early, pltpu.HBM), split, cos_t, sin_t),
-        [pltpu.SemaphoreType.DMA((count,))],
-        flops=20 * columns * freq,
-        moved=2 * columns * freq,
-    )
-    operands = [temps, *[refs[0] for refs in shards]]
+        [VMEM] * 3,
+        [pltpu.VMEM((built, columns, width), bf16)],
+        (split, cos_t, sin_t),
+        flops=40 * columns * built * width // 2,
+    )[0]
+    operands = [temps, first, *[refs[0] for refs in shards]]
     acc = call(
         functools.partial(first_score_kernel, chunked, half),
         "score0",
@@ -646,7 +637,13 @@
 
     split = jnp.transpose(classes, (1, 0, 2))
     cos_t, sin_t, power, weight = prepare(shifts, split, ctf, noise_weight)
-    early = early_templates(split, cos_t, sin_t)
+    tile = template_tile(freq)
+    count = freq // CHUNKS // tile
+    built = count - count // 3
+    early = [
+        early_templates(split, cos_t, sin_t, count, count, tile),
+        early_templates(split, cos_t, sin_t, built, count - built, tile),
+    ][::-1]
     if pairwise:
         far, near, slices, split, early = lax.optimization_barrier(
             (far, near, slices, split, early)

time: 52.1 us -> 50.3 us (0.965)
  Pallas kernels: 23.3 us -> 19.8 us
  waiting for transfers between devices: 7.53 us -> 9.88 us
  local copies, waits for them, and re-layouts: 1.8 us -> 1.13 us
    ppermute x17, waiting for transfers between devices: 7.53 us -> 9.88 us  [swap(): return lax.ppermute(values, axis, [(i, i ^ distance) for i in range(size)])]
    pallas_call x12, Pallas kernels: 18.8 us -> 17 us  [call(): pl.pallas_call(kernel, in_specs=in_specs, out_specs=[VMEM] * len(out_shap...]
    pallas_call x1 -> x2, Pallas kernels: 4.53 us -> 2.81 us  [early_templates(): pl.pallas_call(early_kernel, grid=(count,), in_specs=[pl.BlockSpec((2, ro...]
    unnamed x3, local copies, waits for them, and re-layouts: 1.8 us -> 1.13 us
  transfers between devices with their start and end apart: 17 -> 17, of which waited for: 5 -> 5; matrix products, arithmetic and copies ran while one was open for 2% -> 2% of each run, Pallas kernels for 36% -> 30%
where the time goes in v16:
time: 50.3 us; the launch traced here: 50.1 us
  Pallas kernels  19.8 us (39%)
  starting transfers between devices  18.5 us (37%)
  waiting for transfers between devices  9.88 us (20%)
  local copies, waits for them, and re-layouts  1.13 us (2%)
  between operations  0.81 us (2%)
    ppermute x17, starting transfers between devices, swap(): return lax.ppermute(values, axis, [(i, i ^ distance) for i in range(size)])  18.5 us
    pallas_call x12, Pallas kernels, call(): pl.pallas_call(kernel, in_specs=in_specs, out_specs=[VMEM] * len(out_shap...  17 us
    ppermute x17, waiting for transfers between devices, swap(): return lax.ppermute(values, axis, [(i, i ^ distance) for i in range(size)])  9.88 us
    pallas_call x2, Pallas kernels, early_templates(): pl.pallas_call(early_kernel, grid=(count,), in_specs=[pl.BlockSpec((2, ro...  2.81 us
    unnamed x3, local copies, waits for them, and re-layouts  1.13 us
  transfers between devices with their start and end apart: 17, of which 5 were waited for; matrix products, arithmetic and copies ran while one was open for 2% of the time, Pallas kernels for 30%

profile of v16, /device:TPU:0, one launch (start us, length us, event | category | flops | bytes accessed | tf_op | source)
XLA Modules:
  0.0 50.1 jit_solution(2823224649012067632)
XLA Ops:
  0.6 1.7 %weigh.1 = (bf16[32,4736]{1,0:T(8,128)(2,1)S(1)}, bf16[32,2432]{1,0:T(8,128)(2,1)S(1)}, bf16[32,2304]{1,0:T(8,128)(2,1)S(1)}) custom-call(s32[16]{0:T(128)} %ids_hbm.1, bf16[16,2,4608]{2,1,0:T(2,128)(2,1)} %p_hbm.1, f32[64,4608]{1,0:T(8,128)} %ctf_hbm.3, f32[4608]{0:T(1024)} %nw_hbm.3), custom_call_target="tpu_custom_call" | custom-call | flops 294912 | bytes 1179648 | tf_op jit(solution)/shard_map/weigh/pallas_call | solution.py:30
  2.4 3.1 %collective-permute-start.2 = (bf16[32,4736]{1,0:T(8,128)(2,1)S(1)}, bf16[32,4736]{1,0:T(8,128)(2,1)S(1)}, u32[]{:S(2)}, u32[]{:S(2)}) collective-permute-start(bf16[32,4736]{1,0:T(8,128)(2,1)S(1)} %get-tuple-element.37.refs_0_.refs_4_), channel_id=1, source_target_pairs={{0,4},{4,0},{8,12},{12,8},{1,5},{5,1},{9,13},{13,9},{2,6},{6,2},{1... | collective-permute-start | bytes 909320 | tf_op jit(solution)/shard_map/ppermute | solution.py:612
  5.5 2.6 %collective-permute-start = (bf16[32,2432]{1,0:T(8,128)(2,1)S(1)}, bf16[32,2432]{1,0:T(8,128)(2,1)S(1)}, u32[]{:S(2)}, u32[]{:S(2)}) collective-permute-start(bf16[32,2432]{1,0:T(8,128)(2,1)S(1)} %get-tuple-element.35), channel_id=1, source_target_pairs={{0,8},{4,12},{8,0},{12,4},{1,9},{5,13},{9,1},{13,5},{2,10},{6,14},... | collective-permute-start | bytes 466952 | tf_op jit(solution)/shard_map/ppermute | solution.py:612
  8.0 0.3 collective-permute-start.1
  8.4 0.1 pad_add_fusion.me_ref
  8.5 0.6 %cut_slices.3 = (bf16[32,1152]{1,0:T(8,128)(2,1)S(1)}, bf16[32,1152]{1,0:T(8,128)(2,1)S(1)}, bf16[32,1152]{1,0:T(8,128)(2,1)S(1)}) custom-call(s32[2]{0:T(128)S(1)} %pad_add_fusion.me_ref, bf16[32,4736]{1,0:T(8,128)(2,1)S(1)} %get-tuple-element.37.refs_0_.refs_4_), custom_call_target="tpu_custom_call" | custom-call | bytes 442368 | tf_op jit(solution)/shard_map/cut_slices/pallas_call | solution.py:30
  9.0 0.2 collective-permute-start.3
  9.2 1.5 %collective-permute-start.4 = (bf16[32,1152]{1,0:T(8,128)(2,1)S(1)}, bf16[32,1152]{1,0:T(8,128)(2,1)S(1)}, u32[]{:S(2)}, u32[]{:S(2)}) collective-permute-start(bf16[32,1152]{1,0:T(8,128)(2,1)S(1)} %get-tuple-element.40), channel_id=1, source_target_pairs={{0,2},{1,3},{2,0},{3,1},{4,6},{5,7},{6,4},{7,5},{8,10},{9,11},{10,... | collective-permute-start | bytes 221192 | tf_op jit(solution)/shard_map/ppermute | solution.py:612
  10.7 1.1 %copy.10 = bf16[32,2,4608]{2,0,1:T(8,128)(2,1)S(1)} copy(bf16[32,2,4608]{2,1,0:T(2,128)(2,1)} %param.7) | data formatting | bytes 1179648 | tf_op args[1]
  11.8 3.1 %prepare.1 = (f32[24,4608]{1,0:T(8,128)S(1)}, f32[24,4608]{1,0:T(8,128)S(1)}, f32[32,64]{1,0:T(8,128)S(1)}, f32[64,4608]{1,0:T(8,128)S(1)}) custom-call(s32[2,24]{1,0:T(2,128)S(1)} %bitcast.11, bf16[2,32,4608]{2,1,0:T(8,128)(2,1)S(1)} %bitcast.7, f32[64,4608]{1,0:T(8,128)} %ctf_hbm.3, f32[4608]{0:T(1024)} %nw_hbm.3), custom_call_target="tpu_custom_call" | custom-call | flops 226492416 | tf_op jit(solution)/shard_map/prepare/pallas_call | solution.py:30
  14.9 0.7 %early_templates4.1.early_ref = bf16[2,768,768]{2,1,0:T(8,128)(2,1)S(1)} custom-call(bf16[2,32,4608]{2,1,0:T(8,128)(2,1)S(1)} %bitcast.8, f32[24,4608]{1,0:T(8,128)S(1)} %get-tuple-element.41.cos_ref, f32[24,4608]{1,0:T(8,128)S(1)} %get-tuple-element.42.sin_ref), custom_call_target="tpu_custom_call" | custom-call | flops 23592960 | bytes 2359296 | tf_op jit(solution)/shard_map/early_templates4/pallas_call | solution.py:202
  15.6 2.1 %early_templates6.1.temp_ref = bf16[6,768,768]{2,1,0:T(8,128)(2,1)S(1)} custom-call(bf16[2,32,4608]{2,1,0:T(8,128)(2,1)S(1)} %bitcast.9, f32[24,4608]{1,0:T(8,128)S(1)} %get-tuple-element.41.cos_ref, f32[24,4608]{1,0:T(8,128)S(1)} %get-tuple-element.42.sin_ref), custom_call_target="tpu_custom_call" | custom-call | flops 70778880 | bytes 7077888 | tf_op jit(solution)/shard_map/early_templates6/pallas_call | solution.py:202
  17.7 0.0 collective-permute-done.3.refs_2_
  17.8 0.0 collective-permute-done.4.refs_4_
  17.8 3.8 %collective-permute-done.1.refs_6_.refs_3_ = bf16[32,2304]{1,0:T(8,128)(2,1)S(1)} collective-permute-done((bf16[32,2304]{1,0:T(8,128)(2,1)S(1)}, bf16[32,2304]{1,0:T(8,128)(2,1)S(1)}, u32[]{:S(2)}, u32[]{:S(2)}) %collective-permute-start.1) | collective-permute-done | bytes 147488 | tf_op jit(solution)/shard_map/ppermute | solution.py:612
  21.5 0.0 collective-permute-done.refs_2_
  21.5 0.0 collective-permute-done.2.refs_1_.refs_5_
  21.5 0.5 collective-permute-start.5
  22.0 1.6 %collective-permute-start.6 = (bf16[32,2304]{1,0:T(8,128)(2,1)S(1)}, bf16[32,2304]{1,0:T(8,128)(2,1)S(1)}, u32[]{:S(2)}, u32[]{:S(2)}) collective-permute-start(bf16[32,2304]{1,0:T(8,128)(2,1)S(1)} %collective-permute-done.1.refs_6_.refs_3_), channel_id=1, source_target_pairs={{0,4},{4,0},{8,12},{12,8},{1,5},{5,1},{9,13},{13,9},{2,6},{6,2},{1... | collective-permute-start | bytes 442376 | tf_op jit(solution)/shard_map/ppermute | solution.py:612
  23.6 0.6 %cut_slices.4 = (bf16[64,1152]{1,0:T(8,128)(2,1)S(1)}, bf16[64,1152]{1,0:T(8,128)(2,1)S(1)}, bf16[64,1152]{1,0:T(8,128)(2,1)S(1)}, bf16[96,1152]{1,0:T(8,128)(2,1)S(1)}) custom-call(s32[2]{0:T(128)S(1)} %pad_add_fusion.me_ref, bf16[32,4736]{1,0:T(8,128)(2,1)S(1)} %get-tuple-element.37.refs_0_.refs_4_, ...), custom_call_target="tpu_custom_call" | custom-call | bytes 1327104 | tf_op jit(solution)/shard_map/cut_slices/pallas_call | solution.py:30
  24.2 0.1 collective-permute-start.7
  24.3 1.6 %collective-permute-start.11 = (bf16[64,1152]{1,0:T(8,128)(2,1)S(1)}, bf16[64,1152]{1,0:T(8,128)(2,1)S(1)}, u32[]{:S(2)}, u32[]{:S(2)}) collective-permute-start(bf16[64,1152]{1,0:T(8,128)(2,1)S(1)} %get-tuple-element.60), channel_id=1, source_target_pairs={{0,3},{1,2},{2,1},{3,0},{4,7},{5,6},{6,5},{7,4},{8,11},{9,10},{10,... | collective-permute-start | bytes 442376 | tf_op jit(solution)/shard_map/ppermute | solution.py:612
  25.9 0.5 %collective-permute-start.12 = (bf16[64,1152]{1,0:T(8,128)(2,1)S(1)}, bf16[64,1152]{1,0:T(8,128)(2,1)S(1)}, u32[]{:S(2)}, u32[]{:S(2)}) collective-permute-start(bf16[64,1152]{1,0:T(8,128)(2,1)S(1)} %get-tuple-element.62), channel_id=1, source_target_pairs={{0,2},{1,3},{2,0},{3,1},{4,6},{5,7},{6,4},{7,5},{8,10},{9,11},{10,... | collective-permute-start | bytes 442376 | tf_op jit(solution)/shard_map/ppermute | solution.py:612
  26.4 1.3 %templates.1.built_ref = bf16[4,768,768]{2,1,0:T(8,128)(2,1)S(1)} custom-call(bf16[2,32,4608]{2,1,0:T(8,128)(2,1)S(1)} %bitcast.10, f32[24,4608]{1,0:T(8,128)S(1)} %get-tuple-element.41.cos_ref, f32[24,4608]{1,0:T(8,128)S(1)} %get-tuple-element.42.sin_ref), custom_call_target="tpu_custom_call" | custom-call | flops 47185920 | tf_op jit(solution)/shard_map/templates/pallas_call | solution.py:30
  27.7 0.0 collective-permute-done.5.refs_3_.refs_0_
  27.7 2.0 %score0.1.acc_ref = f32[768,128]{1,0:T(8,128)S(1)} custom-call(bf16[4,768,768]{2,1,0:T(8,128)(2,1)S(1)} %templates.1.built_ref, bf16[2,768,768]{2,1,0:T(8,128)(2,1)S(1)} %early_templates4.1.early_ref, bf16[32,4736]{1,0:T(8,128)(2,1)S(1)} %get-tuple-element.37.refs_0_.refs_4_, bf16[32,4736]{1,0:T(8,128)(2,1)S(1)} %collective-permute-done.2.refs_1_.refs_5_, ...), custom_call_target="tpu_custom_call" | custom-call | flops 1811939328 | tf_op jit(solution)/shard_map/score0/pallas_call | solution.py:30
  29.7 0.0 collective-permute-done.6.refs_7_.refs_1_
  29.7 2.2 %score1.1 = (f32[768,128]{1,0:T(8,128)S(1)}, f32[128,64]{1,0:T(8,128)S(1)}, f32[8,128]{1,0:T(8,128)S(1)}) custom-call(bf16[6,768,768]{2,1,0:T(8,128)(2,1)S(1)} %early_templates6.1.temp_ref, f32[32,64]{1,0:T(8,128)S(1)} %get-tuple-element.44.pow_ref, f32[768,128]{1,0:T(8,128)S(1)} %score0.1.acc_ref, bf16[32,4736]{1,0:T(8,128)(2,1)S(1)} %get-tuple-element.37.refs_0_.refs_4_, ...), custom_call_target="tpu_custom_call" | custom-call | flops 1811939328 | tf_op jit(solution)/shard_map/score1/pallas_call | solution.py:30
  31.9 0.0 collective-permute-done.7.refs_6_.refs_2_
  32.0 2.6 %collective-permute-start.8 = (f32[8,128]{1,0:T(8,128)S(1)}, f32[8,128]{1,0:T(8,128)S(1)}, u32[]{:S(2)}, u32[]{:S(2)}) collective-permute-start(f32[8,128]{1,0:T(8,128)S(1)} %get-tuple-element.54.refs_0_), channel_id=1, source_target_pairs={{0,12},{4,8},{8,4},{12,0},{1,13},{5,9},{9,5},{13,1},{2,14},{6,10},... | collective-permute-start | bytes 12296 | tf_op jit(solution)/shard_map/ppermute | solution.py:612
  34.6 0.0 collective-permute-start.9
  34.6 1.8 %collective-permute-start.10 = (f32[8,128]{1,0:T(8,128)S(1)}, f32[8,128]{1,0:T(8,128)S(1)}, u32[]{:S(2)}, u32[]{:S(2)}) collective-permute-start(f32[8,128]{1,0:T(8,128)S(1)} %get-tuple-element.54.refs_0_), channel_id=1, source_target_pairs={{0,4},{4,0},{8,12},{12,8},{1,5},{5,1},{9,13},{13,9},{2,6},{6,2},{1... | collective-permute-start | bytes 12296 | tf_op jit(solution)/shard_map/ppermute | solution.py:612
  36.4 0.6 %cut_slices.5.refs_4_ = bf16[32,1152]{1,0:T(8,128)(2,1)S(1)} custom-call(s32[2]{0:T(128)S(1)} %pad_add_fusion.me_ref, bf16[32,2432]{1,0:T(8,128)(2,1)S(1)} %collective-permute-done.5.refs_3_.refs_0_, bf16[32,2304]{1,0:T(8,128)(2,1)S(1)} %collective-permute-done.6.refs_7_.refs_1_), custom_call_target="tpu_custom_call" | custom-call | bytes 147456 | tf_op jit(solution)/shard_map/cut_slices/pallas_call | solution.py:30
  37.0 0.0 collective-permute-done.12.refs_5_.refs_1_
  37.0 0.3 collective-permute-start.16
  37.3 0.1 collective-permute-done.8.refs_1_
  37.4 1.8 %collective-permute-done.9.refs_2_ = f32[8,128]{1,0:T(8,128)S(1)} collective-permute-done((f32[8,128]{1,0:T(8,128)S(1)}, f32[8,128]{1,0:T(8,128)S(1)}, u32[]{:S(2)}, u32[]{:S(2)}) %collective-permute-start.9) | collective-permute-done | bytes 4128 | tf_op jit(solution)/shard_map/ppermute | solution.py:612
  39.2 0.0 collective-permute-done.10.refs_3_
  39.2 0.5 responsibilities.1
  39.7 0.0 collective-permute-start.13
  39.7 1.6 %collective-permute-start.14 = (bf16[416,128]{1,0:T(8,128)(2,1)S(1)}, bf16[416,128]{1,0:T(8,128)(2,1)S(1)}, u32[]{:S(2)}, u32[]{:S(2)}) collective-permute-start(bf16[416,128]{1,0:T(8,128)(2,1)S(1)} %get-tuple-element.67.refs_0_), channel_id=1, source_target_pairs={{0,2},{1,3},{2,0},{3,1},{4,6},{5,7},{6,4},{7,5},{8,10},{9,11},{10,... | collective-permute-start | bytes 319496 | tf_op jit(solution)/shard_map/ppermute | solution.py:612
  41.2 0.3 collective-permute-start.15
  41.5 1.5 %gather_rows.1 = (f32[32,64]{1,0:T(8,128)}, bf16[64,2304]{1,0:T(8,128)(2,1)S(1)}, bf16[2,192,1152]{2,1,0:T(8,128)(2,1)S(1)}) custom-call(s32[2]{0:T(128)S(1)} %pad_add_fusion.me_ref, f32[768,128]{1,0:T(8,128)S(1)} %get-tuple-element.50.s_ref, f32[1,128]{1,0:T(1,128)S(1)} %get-tuple-element.55.norm_ref, f32[64,4608]{1,0:T(8,128)S(1)} %get-tuple-element.56.weight_ref, ...), custom_call_target="tpu_custom_call" | custom-call | flops 20000000000 | bytes 1769472 | tf_op jit(solution)/shard_map/gather_rows/pallas_call | solution.py:30
  43.1 1.9 %collective-permute-done.13.refs_1_ = bf16[416,128]{1,0:T(8,128)(2,1)S(1)} collective-permute-done((bf16[416,128]{1,0:T(8,128)(2,1)S(1)}, bf16[416,128]{1,0:T(8,128)(2,1)S(1)}, u32[]{:S(2)}, u32[]{:S(2)}) %collective-permute-start.13) | collective-permute-done | bytes 106528 | tf_op jit(solution)/shard_map/ppermute | solution.py:612
  44.9 2.3 %collective-permute-done.14.refs_2_ = bf16[416,128]{1,0:T(8,128)(2,1)S(1)} collective-permute-done((bf16[416,128]{1,0:T(8,128)(2,1)S(1)}, bf16[416,128]{1,0:T(8,128)(2,1)S(1)}, u32[]{:S(2)}, u32[]{:S(2)}) %collective-permute-start.14) | collective-permute-done | bytes 106528 | tf_op jit(solution)/shard_map/ppermute | solution.py:612
  47.2 0.0 collective-permute-done.15.refs_3_
  47.2 0.0 collective-permute-done.16.refs_5_
  47.2 2.9 %finish.1 = f32[32,2,1152]{2,1,0:T(2,128)} custom-call(s32[2]{0:T(128)S(1)} %pad_add_fusion.me_ref, bf16[64,2304]{1,0:T(8,128)(2,1)S(1)} %get-tuple-element.65.cw_ref, f32[24,4608]{1,0:T(8,128)S(1)} %get-tuple-element.41.cos_ref, f32[24,4608]{1,0:T(8,128)S(1)} %get-tuple-element.42.sin_ref, bf16[2,192,1152]{2,1,0:T(8,128)(2,1)S(1)} %get-tuple-element.66.rows_ref, ...), custom_call_target="tpu_custom_call" | custom-call | flops 905969664 | tf_op jit(solution)/shard_map/finish/pallas_call | solution.py:30
  (4 shorter events, 0.0 us)
Async XLA Ops:
  0.6 11.2 %copy-start = (s32[24,2]{0,1:T(2,128)S(1)}, s32[24,2]{0,1:T(2,128)}, u32[]{:S(2)}) copy-start(s32[24,2]{0,1:T(2,128)} %param.11) | copy-start | bytes 580
  2.4 19.2 %collective-permute-start.2 = (bf16[32,4736]{1,0:T(8,128)(2,1)S(1)}, bf16[32,4736]{1,0:T(8,128)(2,1)S(1)}, u32[]{:S(2)}, u32[]{:S(2)}) collective-permute-start(bf16[32,4736]{1,0:T(8,128)(2,1)S(1)} %get-tuple-element.37.refs_0_.refs_4_), channel_id=1, source_target_pairs={{0,4},{4,0},{8,12},{12,8},{1,5},{5,1},{9,13},{13,9},{2,6},{6,2},{1... | collective-permute-start | bytes 909320 | tf_op jit(solution)/shard_map/ppermute | solution.py:612
  5.5 16.1 %collective-permute-start = (bf16[32,2432]{1,0:T(8,128)(2,1)S(1)}, bf16[32,2432]{1,0:T(8,128)(2,1)S(1)}, u32[]{:S(2)}, u32[]{:S(2)}) collective-permute-start(bf16[32,2432]{1,0:T(8,128)(2,1)S(1)} %get-tuple-element.35), channel_id=1, source_target_pairs={{0,8},{4,12},{8,0},{12,4},{1,9},{5,13},{9,1},{13,5},{2,10},{6,14},... | collective-permute-start | bytes 466952 | tf_op jit(solution)/shard_map/ppermute | solution.py:612
  8.0 13.5 %collective-permute-start.1 = (bf16[32,2304]{1,0:T(8,128)(2,1)S(1)}, bf16[32,2304]{1,0:T(8,128)(2,1)S(1)}, u32[]{:S(2)}, u32[]{:S(2)}) collective-permute-start(bf16[32,2304]{1,0:T(8,128)(2,1)S(1)} %get-tuple-element.36), channel_id=1, source_target_pairs={{0,8},{4,12},{8,0},{12,4},{1,9},{5,13},{9,1},{13,5},{2,10},{6,14},... | collective-permute-start | bytes 442376 | tf_op jit(solution)/shard_map/ppermute | solution.py:612
  9.0 8.7 %collective-permute-start.3 = (bf16[32,1152]{1,0:T(8,128)(2,1)S(1)}, bf16[32,1152]{1,0:T(8,128)(2,1)S(1)}, u32[]{:S(2)}, u32[]{:S(2)}) collective-permute-start(bf16[32,1152]{1,0:T(8,128)(2,1)S(1)} %get-tuple-element.39), channel_id=1, source_target_pairs={{0,3},{1,2},{2,1},{3,0},{4,7},{5,6},{6,5},{7,4},{8,11},{9,10},{10,... | collective-permute-start | bytes 221192 | tf_op jit(solution)/shard_map/ppermute | solution.py:612
  9.2 8.6 %collective-permute-start.4 = (bf16[32,1152]{1,0:T(8,128)(2,1)S(1)}, bf16[32,1152]{1,0:T(8,128)(2,1)S(1)}, u32[]{:S(2)}, u32[]{:S(2)}) collective-permute-start(bf16[32,1152]{1,0:T(8,128)(2,1)S(1)} %get-tuple-element.40), channel_id=1, source_target_pairs={{0,2},{1,3},{2,0},{3,1},{4,6},{5,7},{6,4},{7,5},{8,10},{9,11},{10,... | collective-permute-start | bytes 221192 | tf_op jit(solution)/shard_map/ppermute | solution.py:612
  21.5 6.1 %collective-permute-start.5 = (bf16[32,2432]{1,0:T(8,128)(2,1)S(1)}, bf16[32,2432]{1,0:T(8,128)(2,1)S(1)}, u32[]{:S(2)}, u32[]{:S(2)}) collective-permute-start(bf16[32,2432]{1,0:T(8,128)(2,1)S(1)} %collective-permute-done.refs_2_), channel_id=1, source_target_pairs={{0,4},{4,0},{8,12},{12,8},{1,5},{5,1},{9,13},{13,9},{2,6},{6,2},{1... | collective-permute-start | bytes 466952 | tf_op jit(solution)/shard_map/ppermute | solution.py:612
  22.0 7.7 %collective-permute-start.6 = (bf16[32,2304]{1,0:T(8,128)(2,1)S(1)}, bf16[32,2304]{1,0:T(8,128)(2,1)S(1)}, u32[]{:S(2)}, u32[]{:S(2)}) collective-permute-start(bf16[32,2304]{1,0:T(8,128)(2,1)S(1)} %collective-permute-done.1.refs_6_.refs_3_), channel_id=1, source_target_pairs={{0,4},{4,0},{8,12},{12,8},{1,5},{5,1},{9,13},{13,9},{2,6},{6,2},{1... | collective-permute-start | bytes 442376 | tf_op jit(solution)/shard_map/ppermute | solution.py:612
  24.2 7.7 %collective-permute-start.7 = (bf16[96,1152]{1,0:T(8,128)(2,1)S(1)}, bf16[96,1152]{1,0:T(8,128)(2,1)S(1)}, u32[]{:S(2)}, u32[]{:S(2)}) collective-permute-start(bf16[96,1152]{1,0:T(8,128)(2,1)S(1)} %get-tuple-element.53), channel_id=1, source_target_pairs={{0,1},{1,0},{2,3},{3,2},{4,5},{5,4},{6,7},{7,6},{8,9},{9,8},{10,11... | collective-permute-start | bytes 663560 | tf_op jit(solution)/shard_map/ppermute | solution.py:612
  24.3 12.7 %collective-permute-start.11 = (bf16[64,1152]{1,0:T(8,128)(2,1)S(1)}, bf16[64,1152]{1,0:T(8,128)(2,1)S(1)}, u32[]{:S(2)}, u32[]{:S(2)}) collective-permute-start(bf16[64,1152]{1,0:T(8,128)(2,1)S(1)} %get-tuple-element.60), channel_id=1, source_target_pairs={{0,3},{1,2},{2,1},{3,0},{4,7},{5,6},{6,5},{7,4},{8,11},{9,10},{10,... | collective-permute-start | bytes 442376 | tf_op jit(solution)/shard_map/ppermute | solution.py:612
  25.9 11.1 %collective-permute-start.12 = (bf16[64,1152]{1,0:T(8,128)(2,1)S(1)}, bf16[64,1152]{1,0:T(8,128)(2,1)S(1)}, u32[]{:S(2)}, u32[]{:S(2)}) collective-permute-start(bf16[64,1152]{1,0:T(8,128)(2,1)S(1)} %get-tuple-element.62), channel_id=1, source_target_pairs={{0,2},{1,3},{2,0},{3,1},{4,6},{5,7},{6,4},{7,5},{8,10},{9,11},{10,... | collective-permute-start | bytes 442376 | tf_op jit(solution)/shard_map/ppermute | solution.py:612
  32.0 5.5 %collective-permute-start.8 = (f32[8,128]{1,0:T(8,128)S(1)}, f32[8,128]{1,0:T(8,128)S(1)}, u32[]{:S(2)}, u32[]{:S(2)}) collective-permute-start(f32[8,128]{1,0:T(8,128)S(1)} %get-tuple-element.54.refs_0_), channel_id=1, source_target_pairs={{0,12},{4,8},{8,4},{12,0},{1,13},{5,9},{9,5},{13,1},{2,14},{6,10},... | collective-permute-start | bytes 12296 | tf_op jit(solution)/shard_map/ppermute | solution.py:612
  34.6 4.6 %collective-permute-start.9 = (f32[8,128]{1,0:T(8,128)S(1)}, f32[8,128]{1,0:T(8,128)S(1)}, u32[]{:S(2)}, u32[]{:S(2)}) collective-permute-start(f32[8,128]{1,0:T(8,128)S(1)} %get-tuple-element.54.refs_0_), channel_id=1, source_target_pairs={{0,8},{4,12},{8,0},{12,4},{1,9},{5,13},{9,1},{13,5},{2,10},{6,14},... | collective-permute-start | bytes 12296 | tf_op jit(solution)/shard_map/ppermute | solution.py:612
  34.6 4.6 %collective-permute-start.10 = (f32[8,128]{1,0:T(8,128)S(1)}, f32[8,128]{1,0:T(8,128)S(1)}, u32[]{:S(2)}, u32[]{:S(2)}) collective-permute-start(f32[8,128]{1,0:T(8,128)S(1)} %get-tuple-element.54.refs_0_), channel_id=1, source_target_pairs={{0,4},{4,0},{8,12},{12,8},{1,5},{5,1},{9,13},{13,9},{2,6},{6,2},{1... | collective-permute-start | bytes 12296 | tf_op jit(solution)/shard_map/ppermute | solution.py:612
  37.0 10.2 %collective-permute-start.16 = (bf16[96,1152]{1,0:T(8,128)(2,1)S(1)}, bf16[96,1152]{1,0:T(8,128)(2,1)S(1)}, u32[]{:S(2)}, u32[]{:S(2)}) collective-permute-start(bf16[96,1152]{1,0:T(8,128)(2,1)S(1)} %bundle.1), channel_id=1, source_target_pairs={{0,4},{4,0},{8,12},{12,8},{1,5},{5,1},{9,13},{13,9},{2,6},{6,2},{1... | collective-permute-start | bytes 663560 | tf_op jit(solution)/shard_map/ppermute | solution.py:612
  39.7 5.2 %collective-permute-start.13 = (bf16[416,128]{1,0:T(8,128)(2,1)S(1)}, bf16[416,128]{1,0:T(8,128)(2,1)S(1)}, u32[]{:S(2)}, u32[]{:S(2)}) collective-permute-start(bf16[416,128]{1,0:T(8,128)(2,1)S(1)} %get-tuple-element.67.refs_0_), channel_id=1, source_target_pairs={{0,3},{1,2},{2,1},{3,0},{4,7},{5,6},{6,5},{7,4},{8,11},{9,10},{10,... | collective-permute-start | bytes 319496 | tf_op jit(solution)/shard_map/ppermute | solution.py:612
  39.7 7.5 %collective-permute-start.14 = (bf16[416,128]{1,0:T(8,128)(2,1)S(1)}, bf16[416,128]{1,0:T(8,128)(2,1)S(1)}, u32[]{:S(2)}, u32[]{:S(2)}) collective-permute-start(bf16[416,128]{1,0:T(8,128)(2,1)S(1)} %get-tuple-element.67.refs_0_), channel_id=1, source_target_pairs={{0,2},{1,3},{2,0},{3,1},{4,6},{5,7},{6,4},{7,5},{8,10},{9,11},{10,... | collective-permute-start | bytes 319496 | tf_op jit(solution)/shard_map/ppermute | solution.py:612
  41.2 6.0 %collective-permute-start.15 = (bf16[416,128]{1,0:T(8,128)(2,1)S(1)}, bf16[416,128]{1,0:T(8,128)(2,1)S(1)}, u32[]{:S(2)}, u32[]{:S(2)}) collective-permute-start(bf16[416,128]{1,0:T(8,128)(2,1)S(1)} %get-tuple-element.67.refs_0_), channel_id=1, source_target_pairs={{0,1},{1,0},{2,3},{3,2},{4,5},{5,4},{6,7},{7,6},{8,9},{9,8},{10,11... | collective-permute-start | bytes 319496 | tf_op jit(solution)/shard_map/ppermute | solution.py:612

commit v17 on v16

--- a/solution.py
+++ b/solution.py
@@ -192,15 +192,15 @@
     return max(t for t in range(LANES, 385, LANES) if freq // CHUNKS % t == 0)
 
 
-def early_kernel(cls_ref, cos_ref, sin_ref, temp_ref):
+def template_kernel(cls_ref, cos_ref, sin_ref, temp_ref):
     write_templates(cls_ref, cos_ref, sin_ref, temp_ref, 0, cls_ref.shape[2])
 
 
-def early_templates(split, cos_t, sin_t, skip, count, tile):
+def build_templates(split, cos_t, sin_t, skip, count, tile):
     _, rows, _ = split.shape
     poses = cos_t.shape[0]
     return pl.pallas_call(
-        early_kernel,
+        template_kernel,
         grid=(count,),
         in_specs=[
             pl.BlockSpec((2, rows, tile), lambda j: (0, 0, skip + j)),
@@ -215,17 +215,8 @@
             bytes_accessed=4 * poses * rows * count * tile,
             transcendentals=0,
         ),
-        name=f"early_templates{skip}",
+        name=f"templates{skip}",
     )(split, cos_t, sin_t)
-
-
-def template_kernel(cls_ref, cos_ref, sin_ref, temp_ref):
-    count, _, width = temp_ref.shape
-    tile = width // 2
-
-    @pl.loop(0, count)
-    def _(t):
-        write_templates(cls_ref, cos_ref, sin_ref, temp_ref.at[t], t * tile, tile)
 
 
 def regroup(refs, counts):
@@ -245,16 +236,15 @@
     )
 
 
-def first_score_kernel(chunked, half, built_ref, early_ref, *refs):
+def first_score_kernel(chunked, half, temp_ref, *refs):
     refs, acc_ref = refs[:-1], refs[-1]
-    tile = built_ref.shape[2] // 2
-    temps = [ref.at[t] for ref in (built_ref, early_ref) for t in range(ref.shape[0])]
-    count = len(temps)
+    count, _, width = temp_ref.shape
+    tile = width // 2
     shards = list(zip(refs, chunked))
     acc_ref[...] = jnp.zeros_like(acc_ref)
     for t in range(count):
         acc_ref[...] += lax.dot_general(
-            temps[t][...],
+            temp_ref[t],
             tile_of_particles(shards, 0, count * tile, t, tile, half),
             NT,
             preferred_element_type=f32,
@@ -298,24 +288,14 @@
     stat_ref[2:8, :] = jnp.zeros((6, lanes), f32)
 
 
-def score(early, split, cos_t, sin_t, power, shards, half):
-    first, late = early
+def score(temps, power, shards, half):
+    first, late = temps
     count, columns, width = late.shape
-    freq = split.shape[2]
     lanes = sum(refs[0].shape[0] for refs in shards)
     chunked = [len(refs) > 1 for refs in shards]
     flops = 2 * columns * 256 * count * width
     acc_shape = jax.ShapeDtypeStruct((columns, lanes), f32)
-    built = count - first.shape[0]
-    temps = call(
-        template_kernel,
-        "templates",
-        [VMEM] * 3,
-        [pltpu.VMEM((built, columns, width), bf16)],
-        (split, cos_t, sin_t),
-        flops=40 * columns * built * width // 2,
-    )[0]
-    operands = [temps, first, *[refs[0] for refs in shards]]
+    operands = [first, *[refs[0] for refs in shards]]
     acc = call(
         functools.partial(first_score_kernel, chunked, half),
         "score0",
@@ -639,21 +619,19 @@
     cos_t, sin_t, power, weight = prepare(shifts, split, ctf, noise_weight)
     tile = template_tile(freq)
     count = freq // CHUNKS // tile
-    built = count - count // 3
-    early = [
-        early_templates(split, cos_t, sin_t, count, count, tile),
-        early_templates(split, cos_t, sin_t, built, count - built, tile),
-    ][::-1]
+    temps = [
+        build_templates(split, cos_t, sin_t, c * count, count, tile) for c in range(CHUNKS)
+    ]
     if pairwise:
-        far, near, slices, split, early = lax.optimization_barrier(
-            (far, near, slices, split, early)
+        far, near, slices, power, temps = lax.optimization_barrier(
+            (far, near, slices, power, temps)
         )
         third = [swap(w, "cls", 1) for w in far]
         targets = [(d, 1) for d in (0,) + others[:-1]] + [(others[-1], 0)]
         mine, *outgoing = cut_slices(me, [[own], [near], far], targets, span, freq)
         arrived = [mine] + [swap(w, "img", d) for w, d in zip(outgoing, others)]
         shards = [[own], [near], far, third]
-    scores, marks, stat = score(early, split, cos_t, sin_t, power, shards, half)
+    scores, marks, stat = score(temps, power, shards, half)
     if pairwise:
         stat, arrived[-1] = lax.optimization_barrier((stat, arrived[-1]))
         stats = [stat] + [swap(stat, "cls", k) for k in range(n_cls - 1, 0, -1)]

time: 50.3 us -> 50.3 us (level)
  waiting for transfers between devices: 9.88 us -> 9.13 us
  local copies, waits for them, and re-layouts: 1.13 us -> 1.8 us
    pallas_call x2, Pallas kernels: 2.81 us -> 4.18 us  [build_templates(): pl.pallas_call(template_kernel, grid=(count,), in_specs=[pl.BlockSpec((2,...]
    pallas_call x12 -> x11, Pallas kernels: 17 us -> 15.7 us  [call(): pl.pallas_call(kernel, in_specs=in_specs, out_specs=[VMEM] * len(out_shap...]
    ppermute x17, waiting for transfers between devices: 9.88 us -> 9.13 us  [swap(): return lax.ppermute(values, axis, [(i, i ^ distance) for i in range(size)])]
    unnamed x3, local copies, waits for them, and re-layouts: 1.13 us -> 1.8 us
  transfers between devices with their start and end apart: 17 -> 17, of which waited for: 5 -> 6; matrix products, arithmetic and copies ran while one was open for 2% -> 2% of each run, Pallas kernels for 30% -> 31%
where the time goes in v17:
time: 50.3 us; the launch traced here: 50.1 us
  Pallas kernels  19.9 us (40%)
  starting transfers between devices  18.4 us (37%)
  waiting for transfers between devices  9.13 us (18%)
  local copies, waits for them, and re-layouts  1.8 us (4%)
  between operations  0.79 us (2%)
    ppermute x17, starting transfers between devices, swap(): return lax.ppermute(values, axis, [(i, i ^ distance) for i in range(size)])  18.4 us
    pallas_call x11, Pallas kernels, call(): pl.pallas_call(kernel, in_specs=in_specs, out_specs=[VMEM] * len(out_shap...  15.7 us
    ppermute x17, waiting for transfers between devices, swap(): return lax.ppermute(values, axis, [(i, i ^ distance) for i in range(size)])  9.13 us
    pallas_call x2, Pallas kernels, build_templates(): pl.pallas_call(template_kernel, grid=(count,), in_specs=[pl.BlockSpec((2,...  4.18 us
    unnamed x3, local copies, waits for them, and re-layouts  1.8 us
  transfers between devices with their start and end apart: 17, of which 6 were waited for; matrix products, arithmetic and copies ran while one was open for 2% of the time, Pallas kernels for 31%

profile of v17, /device:TPU:0, one launch (start us, length us, event | category | flops | bytes accessed | tf_op | source)
XLA Modules:
  0.0 50.1 jit_solution(8053648133310776275)
XLA Ops:
  0.6 1.7 %weigh.1 = (bf16[32,4736]{1,0:T(8,128)(2,1)S(1)}, bf16[32,2432]{1,0:T(8,128)(2,1)S(1)}, bf16[32,2304]{1,0:T(8,128)(2,1)S(1)}) custom-call(s32[16]{0:T(128)} %ids_hbm.1, bf16[16,2,4608]{2,1,0:T(2,128)(2,1)} %p_hbm.1, f32[64,4608]{1,0:T(8,128)} %ctf_hbm.3, f32[4608]{0:T(1024)} %nw_hbm.3), custom_call_target="tpu_custom_call" | custom-call | flops 294912 | bytes 1179648 | tf_op jit(solution)/shard_map/weigh/pallas_call | solution.py:30
  2.4 3.1 %collective-permute-start.2 = (bf16[32,4736]{1,0:T(8,128)(2,1)S(1)}, bf16[32,4736]{1,0:T(8,128)(2,1)S(1)}, u32[]{:S(2)}, u32[]{:S(2)}) collective-permute-start(bf16[32,4736]{1,0:T(8,128)(2,1)S(1)} %get-tuple-element.37.refs_0_.refs_4_), channel_id=1, source_target_pairs={{0,4},{4,0},{8,12},{12,8},{1,5},{5,1},{9,13},{13,9},{2,6},{6,2},{1... | collective-permute-start | bytes 909320 | tf_op jit(solution)/shard_map/ppermute | solution.py:592
  5.4 2.6 %collective-permute-start = (bf16[32,2432]{1,0:T(8,128)(2,1)S(1)}, bf16[32,2432]{1,0:T(8,128)(2,1)S(1)}, u32[]{:S(2)}, u32[]{:S(2)}) collective-permute-start(bf16[32,2432]{1,0:T(8,128)(2,1)S(1)} %get-tuple-element.35), channel_id=1, source_target_pairs={{0,8},{4,12},{8,0},{12,4},{1,9},{5,13},{9,1},{13,5},{2,10},{6,14},... | collective-permute-start | bytes 466952 | tf_op jit(solution)/shard_map/ppermute | solution.py:592
  8.0 0.3 collective-permute-start.1
  8.4 0.1 pad_add_fusion.me_ref
  8.4 0.6 %cut_slices.3 = (bf16[32,1152]{1,0:T(8,128)(2,1)S(1)}, bf16[32,1152]{1,0:T(8,128)(2,1)S(1)}, bf16[32,1152]{1,0:T(8,128)(2,1)S(1)}) custom-call(s32[2]{0:T(128)S(1)} %pad_add_fusion.me_ref, bf16[32,4736]{1,0:T(8,128)(2,1)S(1)} %get-tuple-element.37.refs_0_.refs_4_), custom_call_target="tpu_custom_call" | custom-call | bytes 442368 | tf_op jit(solution)/shard_map/cut_slices/pallas_call | solution.py:30
  9.0 0.2 collective-permute-start.3
  9.2 1.5 %collective-permute-start.4 = (bf16[32,1152]{1,0:T(8,128)(2,1)S(1)}, bf16[32,1152]{1,0:T(8,128)(2,1)S(1)}, u32[]{:S(2)}, u32[]{:S(2)}) collective-permute-start(bf16[32,1152]{1,0:T(8,128)(2,1)S(1)} %get-tuple-element.40), channel_id=1, source_target_pairs={{0,2},{1,3},{2,0},{3,1},{4,6},{5,7},{6,4},{7,5},{8,10},{9,11},{10,... | collective-permute-start | bytes 221192 | tf_op jit(solution)/shard_map/ppermute | solution.py:592
  10.7 1.1 %copy.10 = bf16[32,2,4608]{2,0,1:T(8,128)(2,1)S(1)} copy(bf16[32,2,4608]{2,1,0:T(2,128)(2,1)} %param.7) | data formatting | bytes 1179648 | tf_op args[1]
  11.8 0.0 copy-start
  11.8 0.7 %copy-done = s32[24,2]{0,1:T(2,128)S(1)} copy-done((s32[24,2]{0,1:T(2,128)S(1)}, s32[24,2]{0,1:T(2,128)}, u32[]{:S(2)}) %copy-start) | copy-done | bytes 216
  12.5 3.1 %prepare.1 = (f32[24,4608]{1,0:T(8,128)S(1)}, f32[24,4608]{1,0:T(8,128)S(1)}, f32[32,64]{1,0:T(8,128)S(1)}, f32[64,4608]{1,0:T(8,128)S(1)}) custom-call(s32[2,24]{1,0:T(2,128)S(1)} %bitcast.10, bf16[2,32,4608]{2,1,0:T(8,128)(2,1)S(1)} %bitcast.7, f32[64,4608]{1,0:T(8,128)} %ctf_hbm.3, f32[4608]{0:T(1024)} %nw_hbm.3), custom_call_target="tpu_custom_call" | custom-call | flops 226492416 | tf_op jit(solution)/shard_map/prepare/pallas_call | solution.py:30
  15.6 2.1 %templates0.1.temp_ref = bf16[6,768,768]{2,1,0:T(8,128)(2,1)S(1)} custom-call(bf16[2,32,4608]{2,1,0:T(8,128)(2,1)S(1)} %bitcast.8, f32[24,4608]{1,0:T(8,128)S(1)} %get-tuple-element.42.cos_ref, f32[24,4608]{1,0:T(8,128)S(1)} %get-tuple-element.43.sin_ref), custom_call_target="tpu_custom_call" | custom-call | flops 70778880 | bytes 7077888 | tf_op jit(solution)/shard_map/templates0/pallas_call | solution.py:202
  17.7 2.1 %templates6.1.temp_ref = bf16[6,768,768]{2,1,0:T(8,128)(2,1)S(1)} custom-call(bf16[2,32,4608]{2,1,0:T(8,128)(2,1)S(1)} %bitcast.9, f32[24,4608]{1,0:T(8,128)S(1)} %get-tuple-element.42.cos_ref, f32[24,4608]{1,0:T(8,128)S(1)} %get-tuple-element.43.sin_ref), custom_call_target="tpu_custom_call" | custom-call | flops 70778880 | bytes 7077888 | tf_op jit(solution)/shard_map/templates6/pallas_call | solution.py:202
  19.8 0.0 collective-permute-done.3.refs_2_
  19.8 0.0 collective-permute-done.4.refs_4_
  19.8 1.7 %collective-permute-done.1.refs_6_.refs_3_ = bf16[32,2304]{1,0:T(8,128)(2,1)S(1)} collective-permute-done((bf16[32,2304]{1,0:T(8,128)(2,1)S(1)}, bf16[32,2304]{1,0:T(8,128)(2,1)S(1)}, u32[]{:S(2)}, u32[]{:S(2)}) %collective-permute-start.1) | collective-permute-done | bytes 147488 | tf_op jit(solution)/shard_map/ppermute | solution.py:592
  21.5 0.0 collective-permute-done.refs_2_
  21.5 0.0 collective-permute-done.2.refs_1_.refs_5_
  21.5 0.5 collective-permute-start.5
  22.0 1.6 %collective-permute-start.6 = (bf16[32,2304]{1,0:T(8,128)(2,1)S(1)}, bf16[32,2304]{1,0:T(8,128)(2,1)S(1)}, u32[]{:S(2)}, u32[]{:S(2)}) collective-permute-start(bf16[32,2304]{1,0:T(8,128)(2,1)S(1)} %collective-permute-done.1.refs_6_.refs_3_), channel_id=1, source_target_pairs={{0,4},{4,0},{8,12},{12,8},{1,5},{5,1},{9,13},{13,9},{2,6},{6,2},{1... | collective-permute-start | bytes 442376 | tf_op jit(solution)/shard_map/ppermute | solution.py:592
  23.6 0.6 %cut_slices.4 = (bf16[64,1152]{1,0:T(8,128)(2,1)S(1)}, bf16[64,1152]{1,0:T(8,128)(2,1)S(1)}, bf16[64,1152]{1,0:T(8,128)(2,1)S(1)}, bf16[96,1152]{1,0:T(8,128)(2,1)S(1)}) custom-call(s32[2]{0:T(128)S(1)} %pad_add_fusion.me_ref, bf16[32,4736]{1,0:T(8,128)(2,1)S(1)} %get-tuple-element.37.refs_0_.refs_4_, ...), custom_call_target="tpu_custom_call" | custom-call | bytes 1327104 | tf_op jit(solution)/shard_map/cut_slices/pallas_call | solution.py:30
  24.2 0.1 collective-permute-start.7
  24.3 1.6 %collective-permute-start.11 = (bf16[64,1152]{1,0:T(8,128)(2,1)S(1)}, bf16[64,1152]{1,0:T(8,128)(2,1)S(1)}, u32[]{:S(2)}, u32[]{:S(2)}) collective-permute-start(bf16[64,1152]{1,0:T(8,128)(2,1)S(1)} %get-tuple-element.60), channel_id=1, source_target_pairs={{0,3},{1,2},{2,1},{3,0},{4,7},{5,6},{6,5},{7,4},{8,11},{9,10},{10,... | collective-permute-start | bytes 442376 | tf_op jit(solution)/shard_map/ppermute | solution.py:592
  25.9 0.5 %collective-permute-start.12 = (bf16[64,1152]{1,0:T(8,128)(2,1)S(1)}, bf16[64,1152]{1,0:T(8,128)(2,1)S(1)}, u32[]{:S(2)}, u32[]{:S(2)}) collective-permute-start(bf16[64,1152]{1,0:T(8,128)(2,1)S(1)} %get-tuple-element.62), channel_id=1, source_target_pairs={{0,2},{1,3},{2,0},{3,1},{4,6},{5,7},{6,4},{7,5},{8,10},{9,11},{10,... | collective-permute-start | bytes 442376 | tf_op jit(solution)/shard_map/ppermute | solution.py:592
  26.4 1.3 %collective-permute-done.5.refs_3_.refs_0_ = bf16[32,2432]{1,0:T(8,128)(2,1)S(1)} collective-permute-done((bf16[32,2432]{1,0:T(8,128)(2,1)S(1)}, bf16[32,2432]{1,0:T(8,128)(2,1)S(1)}, u32[]{:S(2)}, u32[]{:S(2)}) %collective-permute-start.5) | collective-permute-done | bytes 155680 | tf_op jit(solution)/shard_map/ppermute | solution.py:592
  27.7 2.0 %score0.1.acc_ref = f32[768,128]{1,0:T(8,128)S(1)} custom-call(bf16[6,768,768]{2,1,0:T(8,128)(2,1)S(1)} %templates0.1.temp_ref, bf16[32,4736]{1,0:T(8,128)(2,1)S(1)} %get-tuple-element.37.refs_0_.refs_4_, bf16[32,4736]{1,0:T(8,128)(2,1)S(1)} %collective-permute-done.2.refs_1_.refs_5_, bf16[32,2432]{1,0:T(8,128)(2,1)S(1)} %collective-permute-done.refs_2_, ...), custom_call_target="tpu_custom_call" | custom-call | flops 1811939328 | tf_op jit(solution)/shard_map/score0/pallas_call | solution.py:30
  29.7 0.0 collective-permute-done.6.refs_7_.refs_1_
  29.7 2.2 %score1.1 = (f32[768,128]{1,0:T(8,128)S(1)}, f32[128,64]{1,0:T(8,128)S(1)}, f32[8,128]{1,0:T(8,128)S(1)}) custom-call(bf16[6,768,768]{2,1,0:T(8,128)(2,1)S(1)} %templates6.1.temp_ref, f32[32,64]{1,0:T(8,128)S(1)} %get-tuple-element.45.pow_ref, f32[768,128]{1,0:T(8,128)S(1)} %score0.1.acc_ref, bf16[32,4736]{1,0:T(8,128)(2,1)S(1)} %get-tuple-element.37.refs_0_.refs_4_, ...), custom_call_target="tpu_custom_call" | custom-call | flops 1811939328 | tf_op jit(solution)/shard_map/score1/pallas_call | solution.py:30
  32.0 2.5 %collective-permute-start.8 = (f32[8,128]{1,0:T(8,128)S(1)}, f32[8,128]{1,0:T(8,128)S(1)}, u32[]{:S(2)}, u32[]{:S(2)}) collective-permute-start(f32[8,128]{1,0:T(8,128)S(1)} %get-tuple-element.54.refs_0_), channel_id=1, source_target_pairs={{0,12},{4,8},{8,4},{12,0},{1,13},{5,9},{9,5},{13,1},{2,14},{6,10},... | collective-permute-start | bytes 12296 | tf_op jit(solution)/shard_map/ppermute | solution.py:592
  34.5 0.0 collective-permute-start.9
  34.5 1.9 %collective-permute-start.10 = (f32[8,128]{1,0:T(8,128)S(1)}, f32[8,128]{1,0:T(8,128)S(1)}, u32[]{:S(2)}, u32[]{:S(2)}) collective-permute-start(f32[8,128]{1,0:T(8,128)S(1)} %get-tuple-element.54.refs_0_), channel_id=1, source_target_pairs={{0,4},{4,0},{8,12},{12,8},{1,5},{5,1},{9,13},{13,9},{2,6},{6,2},{1... | collective-permute-start | bytes 12296 | tf_op jit(solution)/shard_map/ppermute | solution.py:592
  36.4 0.6 %cut_slices.5.refs_4_ = bf16[32,1152]{1,0:T(8,128)(2,1)S(1)} custom-call(s32[2]{0:T(128)S(1)} %pad_add_fusion.me_ref, bf16[32,2432]{1,0:T(8,128)(2,1)S(1)} %collective-permute-done.5.refs_3_.refs_0_, bf16[32,2304]{1,0:T(8,128)(2,1)S(1)} %collective-permute-done.6.refs_7_.refs_1_), custom_call_target="tpu_custom_call" | custom-call | bytes 147456 | tf_op jit(solution)/shard_map/cut_slices/pallas_call | solution.py:30
  37.0 0.0 collective-permute-done.12.refs_5_.refs_1_
  37.0 0.2 collective-permute-start.16
  37.2 0.3 collective-permute-done.8.refs_1_
  37.5 1.6 %collective-permute-done.9.refs_2_ = f32[8,128]{1,0:T(8,128)S(1)} collective-permute-done((f32[8,128]{1,0:T(8,128)S(1)}, f32[8,128]{1,0:T(8,128)S(1)}, u32[]{:S(2)}, u32[]{:S(2)}) %collective-permute-start.9) | collective-permute-done | bytes 4128 | tf_op jit(solution)/shard_map/ppermute | solution.py:592
  39.1 0.0 collective-permute-done.10.refs_3_
  39.1 0.5 responsibilities.1
  39.6 0.0 collective-permute-start.13
  39.6 1.6 %collective-permute-start.14 = (bf16[416,128]{1,0:T(8,128)(2,1)S(1)}, bf16[416,128]{1,0:T(8,128)(2,1)S(1)}, u32[]{:S(2)}, u32[]{:S(2)}) collective-permute-start(bf16[416,128]{1,0:T(8,128)(2,1)S(1)} %get-tuple-element.67.refs_0_), channel_id=1, source_target_pairs={{0,2},{1,3},{2,0},{3,1},{4,6},{5,7},{6,4},{7,5},{8,10},{9,11},{10,... | collective-permute-start | bytes 319496 | tf_op jit(solution)/shard_map/ppermute | solution.py:592
  41.2 0.3 collective-permute-start.15
  41.5 1.5 %gather_rows.1 = (f32[32,64]{1,0:T(8,128)}, bf16[64,2304]{1,0:T(8,128)(2,1)S(1)}, bf16[2,192,1152]{2,1,0:T(8,128)(2,1)S(1)}) custom-call(s32[2]{0:T(128)S(1)} %pad_add_fusion.me_ref, f32[768,128]{1,0:T(8,128)S(1)} %get-tuple-element.50.s_ref, f32[1,128]{1,0:T(1,128)S(1)} %get-tuple-element.55.norm_ref, f32[64,4608]{1,0:T(8,128)S(1)} %get-tuple-element.56.weight_ref, ...), custom_call_target="tpu_custom_call" | custom-call | flops 20000000000 | bytes 1769472 | tf_op jit(solution)/shard_map/gather_rows/pallas_call | solution.py:30
  43.0 1.8 %collective-permute-done.13.refs_1_ = bf16[416,128]{1,0:T(8,128)(2,1)S(1)} collective-permute-done((bf16[416,128]{1,0:T(8,128)(2,1)S(1)}, bf16[416,128]{1,0:T(8,128)(2,1)S(1)}, u32[]{:S(2)}, u32[]{:S(2)}) %collective-permute-start.13) | collective-permute-done | bytes 106528 | tf_op jit(solution)/shard_map/ppermute | solution.py:592
  44.8 2.3 %collective-permute-done.14.refs_2_ = bf16[416,128]{1,0:T(8,128)(2,1)S(1)} collective-permute-done((bf16[416,128]{1,0:T(8,128)(2,1)S(1)}, bf16[416,128]{1,0:T(8,128)(2,1)S(1)}, u32[]{:S(2)}, u32[]{:S(2)}) %collective-permute-start.14) | collective-permute-done | bytes 106528 | tf_op jit(solution)/shard_map/ppermute | solution.py:592
  47.2 0.0 collective-permute-done.15.refs_3_
  47.2 0.0 collective-permute-done.16.refs_5_
  47.2 2.9 %finish.1 = f32[32,2,1152]{2,1,0:T(2,128)} custom-call(s32[2]{0:T(128)S(1)} %pad_add_fusion.me_ref, bf16[64,2304]{1,0:T(8,128)(2,1)S(1)} %get-tuple-element.65.cw_ref, f32[24,4608]{1,0:T(8,128)S(1)} %get-tuple-element.42.cos_ref, f32[24,4608]{1,0:T(8,128)S(1)} %get-tuple-element.43.sin_ref, bf16[2,192,1152]{2,1,0:T(8,128)(2,1)S(1)} %get-tuple-element.66.rows_ref, ...), custom_call_target="tpu_custom_call" | custom-call | flops 905969664 | tf_op jit(solution)/shard_map/finish/pallas_call | solution.py:30
  (3 shorter events, 0.0 us)
Async XLA Ops:
  2.4 19.2 %collective-permute-start.2 = (bf16[32,4736]{1,0:T(8,128)(2,1)S(1)}, bf16[32,4736]{1,0:T(8,128)(2,1)S(1)}, u32[]{:S(2)}, u32[]{:S(2)}) collective-permute-start(bf16[32,4736]{1,0:T(8,128)(2,1)S(1)} %get-tuple-element.37.refs_0_.refs_4_), channel_id=1, source_target_pairs={{0,4},{4,0},{8,12},{12,8},{1,5},{5,1},{9,13},{13,9},{2,6},{6,2},{1... | collective-permute-start | bytes 909320 | tf_op jit(solution)/shard_map/ppermute | solution.py:592
  5.4 16.1 %collective-permute-start = (bf16[32,2432]{1,0:T(8,128)(2,1)S(1)}, bf16[32,2432]{1,0:T(8,128)(2,1)S(1)}, u32[]{:S(2)}, u32[]{:S(2)}) collective-permute-start(bf16[32,2432]{1,0:T(8,128)(2,1)S(1)} %get-tuple-element.35), channel_id=1, source_target_pairs={{0,8},{4,12},{8,0},{12,4},{1,9},{5,13},{9,1},{13,5},{2,10},{6,14},... | collective-permute-start | bytes 466952 | tf_op jit(solution)/shard_map/ppermute | solution.py:592
  8.0 13.5 %collective-permute-start.1 = (bf16[32,2304]{1,0:T(8,128)(2,1)S(1)}, bf16[32,2304]{1,0:T(8,128)(2,1)S(1)}, u32[]{:S(2)}, u32[]{:S(2)}) collective-permute-start(bf16[32,2304]{1,0:T(8,128)(2,1)S(1)} %get-tuple-element.36), channel_id=1, source_target_pairs={{0,8},{4,12},{8,0},{12,4},{1,9},{5,13},{9,1},{13,5},{2,10},{6,14},... | collective-permute-start | bytes 442376 | tf_op jit(solution)/shard_map/ppermute | solution.py:592
  9.0 10.8 %collective-permute-start.3 = (bf16[32,1152]{1,0:T(8,128)(2,1)S(1)}, bf16[32,1152]{1,0:T(8,128)(2,1)S(1)}, u32[]{:S(2)}, u32[]{:S(2)}) collective-permute-start(bf16[32,1152]{1,0:T(8,128)(2,1)S(1)} %get-tuple-element.39), channel_id=1, source_target_pairs={{0,3},{1,2},{2,1},{3,0},{4,7},{5,6},{6,5},{7,4},{8,11},{9,10},{10,... | collective-permute-start | bytes 221192 | tf_op jit(solution)/shard_map/ppermute | solution.py:592
  9.2 10.6 %collective-permute-start.4 = (bf16[32,1152]{1,0:T(8,128)(2,1)S(1)}, bf16[32,1152]{1,0:T(8,128)(2,1)S(1)}, u32[]{:S(2)}, u32[]{:S(2)}) collective-permute-start(bf16[32,1152]{1,0:T(8,128)(2,1)S(1)} %get-tuple-element.40), channel_id=1, source_target_pairs={{0,2},{1,3},{2,0},{3,1},{4,6},{5,7},{6,4},{7,5},{8,10},{9,11},{10,... | collective-permute-start | bytes 221192 | tf_op jit(solution)/shard_map/ppermute | solution.py:592
  11.8 0.7 %copy-start = (s32[24,2]{0,1:T(2,128)S(1)}, s32[24,2]{0,1:T(2,128)}, u32[]{:S(2)}) copy-start(s32[24,2]{0,1:T(2,128)} %param.11) | copy-start | bytes 580
  21.5 6.2 %collective-permute-start.5 = (bf16[32,2432]{1,0:T(8,128)(2,1)S(1)}, bf16[32,2432]{1,0:T(8,128)(2,1)S(1)}, u32[]{:S(2)}, u32[]{:S(2)}) collective-permute-start(bf16[32,2432]{1,0:T(8,128)(2,1)S(1)} %collective-permute-done.refs_2_), channel_id=1, source_target_pairs={{0,4},{4,0},{8,12},{12,8},{1,5},{5,1},{9,13},{13,9},{2,6},{6,2},{1... | collective-permute-start | bytes 466952 | tf_op jit(solution)/shard_map/ppermute | solution.py:592
  22.0 7.7 %collective-permute-start.6 = (bf16[32,2304]{1,0:T(8,128)(2,1)S(1)}, bf16[32,2304]{1,0:T(8,128)(2,1)S(1)}, u32[]{:S(2)}, u32[]{:S(2)}) collective-permute-start(bf16[32,2304]{1,0:T(8,128)(2,1)S(1)} %collective-permute-done.1.refs_6_.refs_3_), channel_id=1, source_target_pairs={{0,4},{4,0},{8,12},{12,8},{1,5},{5,1},{9,13},{13,9},{2,6},{6,2},{1... | collective-permute-start | bytes 442376 | tf_op jit(solution)/shard_map/ppermute | solution.py:592
  24.2 7.8 %collective-permute-start.7 = (bf16[96,1152]{1,0:T(8,128)(2,1)S(1)}, bf16[96,1152]{1,0:T(8,128)(2,1)S(1)}, u32[]{:S(2)}, u32[]{:S(2)}) collective-permute-start(bf16[96,1152]{1,0:T(8,128)(2,1)S(1)} %get-tuple-element.53), channel_id=1, source_target_pairs={{0,1},{1,0},{2,3},{3,2},{4,5},{5,4},{6,7},{7,6},{8,9},{9,8},{10,11... | collective-permute-start | bytes 663560 | tf_op jit(solution)/shard_map/ppermute | solution.py:592
  24.3 12.7 %collective-permute-start.11 = (bf16[64,1152]{1,0:T(8,128)(2,1)S(1)}, bf16[64,1152]{1,0:T(8,128)(2,1)S(1)}, u32[]{:S(2)}, u32[]{:S(2)}) collective-permute-start(bf16[64,1152]{1,0:T(8,128)(2,1)S(1)} %get-tuple-element.60), channel_id=1, source_target_pairs={{0,3},{1,2},{2,1},{3,0},{4,7},{5,6},{6,5},{7,4},{8,11},{9,10},{10,... | collective-permute-start | bytes 442376 | tf_op jit(solution)/shard_map/ppermute | solution.py:592
  25.9 11.1 %collective-permute-start.12 = (bf16[64,1152]{1,0:T(8,128)(2,1)S(1)}, bf16[64,1152]{1,0:T(8,128)(2,1)S(1)}, u32[]{:S(2)}, u32[]{:S(2)}) collective-permute-start(bf16[64,1152]{1,0:T(8,128)(2,1)S(1)} %get-tuple-element.62), channel_id=1, source_target_pairs={{0,2},{1,3},{2,0},{3,1},{4,6},{5,7},{6,4},{7,5},{8,10},{9,11},{10,... | collective-permute-start | bytes 442376 | tf_op jit(solution)/shard_map/ppermute | solution.py:592
  32.0 5.5 %collective-permute-start.8 = (f32[8,128]{1,0:T(8,128)S(1)}, f32[8,128]{1,0:T(8,128)S(1)}, u32[]{:S(2)}, u32[]{:S(2)}) collective-permute-start(f32[8,128]{1,0:T(8,128)S(1)} %get-tuple-element.54.refs_0_), channel_id=1, source_target_pairs={{0,12},{4,8},{8,4},{12,0},{1,13},{5,9},{9,5},{13,1},{2,14},{6,10},... | collective-permute-start | bytes 12296 | tf_op jit(solution)/shard_map/ppermute | solution.py:592
  34.5 4.6 %collective-permute-start.9 = (f32[8,128]{1,0:T(8,128)S(1)}, f32[8,128]{1,0:T(8,128)S(1)}, u32[]{:S(2)}, u32[]{:S(2)}) collective-permute-start(f32[8,128]{1,0:T(8,128)S(1)} %get-tuple-element.54.refs_0_), channel_id=1, source_target_pairs={{0,8},{4,12},{8,0},{12,4},{1,9},{5,13},{9,1},{13,5},{2,10},{6,14},... | collective-permute-start | bytes 12296 | tf_op jit(solution)/shard_map/ppermute | solution.py:592
  34.5 4.6 %collective-permute-start.10 = (f32[8,128]{1,0:T(8,128)S(1)}, f32[8,128]{1,0:T(8,128)S(1)}, u32[]{:S(2)}, u32[]{:S(2)}) collective-permute-start(f32[8,128]{1,0:T(8,128)S(1)} %get-tuple-element.54.refs_0_), channel_id=1, source_target_pairs={{0,4},{4,0},{8,12},{12,8},{1,5},{5,1},{9,13},{13,9},{2,6},{6,2},{1... | collective-permute-start | bytes 12296 | tf_op jit(solution)/shard_map/ppermute | solution.py:592
  37.0 10.1 %collective-permute-start.16 = (bf16[96,1152]{1,0:T(8,128)(2,1)S(1)}, bf16[96,1152]{1,0:T(8,128)(2,1)S(1)}, u32[]{:S(2)}, u32[]{:S(2)}) collective-permute-start(bf16[96,1152]{1,0:T(8,128)(2,1)S(1)} %bundle.1), channel_id=1, source_target_pairs={{0,4},{4,0},{8,12},{12,8},{1,5},{5,1},{9,13},{13,9},{2,6},{6,2},{1... | collective-permute-start | bytes 663560 | tf_op jit(solution)/shard_map/ppermute | solution.py:592
  39.6 5.2 %collective-permute-start.13 = (bf16[416,128]{1,0:T(8,128)(2,1)S(1)}, bf16[416,128]{1,0:T(8,128)(2,1)S(1)}, u32[]{:S(2)}, u32[]{:S(2)}) collective-permute-start(bf16[416,128]{1,0:T(8,128)(2,1)S(1)} %get-tuple-element.67.refs_0_), channel_id=1, source_target_pairs={{0,3},{1,2},{2,1},{3,0},{4,7},{5,6},{6,5},{7,4},{8,11},{9,10},{10,... | collective-permute-start | bytes 319496 | tf_op jit(solution)/shard_map/ppermute | solution.py:592
  39.6 7.5 %collective-permute-start.14 = (bf16[416,128]{1,0:T(8,128)(2,1)S(1)}, bf16[416,128]{1,0:T(8,128)(2,1)S(1)}, u32[]{:S(2)}, u32[]{:S(2)}) collective-permute-start(bf16[416,128]{1,0:T(8,128)(2,1)S(1)} %get-tuple-element.67.refs_0_), channel_id=1, source_target_pairs={{0,2},{1,3},{2,0},{3,1},{4,6},{5,7},{6,4},{7,5},{8,10},{9,11},{10,... | collective-permute-start | bytes 319496 | tf_op jit(solution)/shard_map/ppermute | solution.py:592
  41.2 6.0 %collective-permute-start.15 = (bf16[416,128]{1,0:T(8,128)(2,1)S(1)}, bf16[416,128]{1,0:T(8,128)(2,1)S(1)}, u32[]{:S(2)}, u32[]{:S(2)}) collective-permute-start(bf16[416,128]{1,0:T(8,128)(2,1)S(1)} %get-tuple-element.67.refs_0_), channel_id=1, source_target_pairs={{0,1},{1,0},{2,3},{3,2},{4,5},{5,4},{6,7},{7,6},{8,9},{9,8},{10,11... | collective-permute-start | bytes 319496 | tf_op jit(solution)/shard_map/ppermute | solution.py:592

commit v18 on v17

--- a/solution.py
+++ b/solution.py
@@ -8,7 +8,6 @@
 from jax.sharding import PartitionSpec as P
 
 BOX = 128
-CHUNKS = 2
 LANES = 128
 VMEM_LIMIT = 24 * 1024 * 1024
 GATHER_FLOPS = 20_000_000_000
@@ -43,8 +42,9 @@
     return lax.rem(lax.broadcasted_iota(jnp.int32, shape, axis) // half, 2) == 0
 
 
-def weigh_kernel(ids_hbm, p_hbm, ctf_hbm, nw_hbm, *refs):
-    out_refs, (ids_ref, p_ref, ctf_ref, nw_ref, scale_ref, sem) = refs[:-6], refs[-6:]
+def weigh_kernel(
+    ids_hbm, p_hbm, ctf_hbm, nw_hbm, out_ref, ids_ref, p_ref, ctf_ref, nw_ref, scale_ref, sem
+):
     count, _, freq = p_ref.shape
     copies = [
         pltpu.make_async_copy(source, target, sem.at[i])
@@ -66,15 +66,10 @@
         scale_ref[n : n + 1, :] = ctf_ref[pl.ds(ids_ref[n], 1), :] * noise
     scale = scale_ref[...]
     values = p_ref[...].astype(f32)
-    chunk = freq // CHUNKS
     for part in range(2):
-        weighted = (values[:, part, :] * scale).astype(bf16)
         here = slice(part * count, (part + 1) * count)
-        out_refs[0][here, :freq] = weighted
-        for c, out_ref in enumerate(out_refs[1:]):
-            out_ref[here, :chunk] = weighted[:, c * chunk : (c + 1) * chunk]
-    for out_ref in out_refs[:2]:
-        out_ref[:, out_ref.shape[1] - LANES :] = ids.astype(bf16)
+        out_ref[here, :freq] = (values[:, part, :] * scale).astype(bf16)
+    out_ref[:, freq:] = ids.astype(bf16)
 
 
 def weigh(particles, ctf, noise_weight, group_ids):
@@ -84,10 +79,7 @@
         weigh_kernel,
         "weigh",
         [ANY] * 4,
-        [
-            jax.ShapeDtypeStruct((2 * rows, width), bf16)
-            for width in [freq + LANES, freq // CHUNKS + LANES] + [freq // CHUNKS] * (CHUNKS - 1)
-        ],
+        [jax.ShapeDtypeStruct((2 * rows, freq + LANES), bf16)],
         [pltpu.with_memory_space_constraint(x, pltpu.HBM) for x in operands],
         [
             pltpu.SMEM((rows,), jnp.int32),
@@ -99,7 +91,7 @@
         ],
         flops=4 * rows * freq,
         moved=16 * rows * freq,
-    )
+    )[0]
 
 
 def prepare_kernel(
@@ -189,7 +181,7 @@
 
 
 def template_tile(freq):
-    return max(t for t in range(LANES, 385, LANES) if freq // CHUNKS % t == 0)
+    return max(t for t in range(LANES, 385, LANES) if freq // 2 % t == 0)
 
 
 def template_kernel(cls_ref, cos_ref, sin_ref, temp_ref):
@@ -224,42 +216,13 @@
     return [[refs.pop(0) for _ in range(count)] for count in counts]
 
 
-def tile_of_particles(shards, chunk, span, t, tile, half):
-    cuts = []
-    for ref, chunked in shards:
-        at = t * tile if chunked else chunk * span + t * tile
-        cuts.append(ref[:, at : at + tile])
-    wide = jnp.concatenate(cuts, axis=0).astype(f32)
-    real = real_index(wide.shape, 0, half)
-    return jnp.concatenate(
-        [jnp.where(real, wide, 0.0).astype(bf16), jnp.where(real, 0.0, wide).astype(bf16)], axis=1
-    )
-
-
-def first_score_kernel(chunked, half, temp_ref, *refs):
-    refs, acc_ref = refs[:-1], refs[-1]
-    count, _, width = temp_ref.shape
-    tile = width // 2
-    shards = list(zip(refs, chunked))
-    acc_ref[...] = jnp.zeros_like(acc_ref)
-    for t in range(count):
-        acc_ref[...] += lax.dot_general(
-            temp_ref[t],
-            tile_of_particles(shards, 0, count * tile, t, tile, half),
-            NT,
-            preferred_element_type=f32,
-        )
-
-
-def last_score_kernel(chunked, half, temp_ref, pow_ref, acc_ref, *refs):
-    refs, (s_ref, marks_ref, stat_ref) = refs[:-3], refs[-3:]
-    tail_refs, shards = refs[: len(chunked)], list(zip(refs[len(chunked) :], chunked))
-    count, _, width = temp_ref.shape
-    tile = width // 2
+def score_kernel(half, parts, pow_ref, *refs):
+    temp_refs, refs = refs[:parts], refs[parts:]
+    shards, (s_ref, marks_ref, stat_ref) = refs[:-3], refs[-3:]
     rows, groups = pow_ref.shape
     lanes = s_ref.shape[1]
     poses = s_ref.shape[0] // rows
-    tails = [ref[:, ref.shape[1] - LANES :] for ref in tail_refs]
+    tails = [ref[:, ref.shape[1] - LANES :] for ref in shards]
     ids = jnp.concatenate(tails, axis=0).astype(f32)
     group = lax.broadcasted_iota(jnp.int32, (lanes, groups), 1).astype(f32)
     marks = (ids[:, :groups] == group).astype(f32)
@@ -267,14 +230,18 @@
     penalty = lax.dot_general(
         pow_ref[...], marks, NT, precision=HIGHEST, preferred_element_type=f32
     )
-    s_ref[...] = acc_ref[...]
-    for t in range(count):
-        s_ref[...] += lax.dot_general(
-            temp_ref[t],
-            tile_of_particles(shards, 1, count * tile, t, tile, half),
-            NT,
-            preferred_element_type=f32,
+    temps = [ref.at[t] for ref in temp_refs for t in range(ref.shape[0])]
+    tile = temp_refs[0].shape[2] // 2
+    real = real_index((lanes, tile), 0, half)
+    s_ref[...] = jnp.zeros_like(s_ref)
+    for t, temp in enumerate(temps):
+        at = slice(t * tile, (t + 1) * tile)
+        wide = jnp.concatenate([ref[:, at] for ref in shards], axis=0).astype(f32)
+        split = jnp.concatenate(
+            [jnp.where(real, wide, 0.0).astype(bf16), jnp.where(real, 0.0, wide).astype(bf16)],
+            axis=1,
         )
+        s_ref[...] += lax.dot_general(temp[...], split, NT, preferred_element_type=f32)
     acc = s_ref[...]
     acc = acc + jnp.where(
         real_index(acc.shape, 1, half), pltpu.roll(acc, lanes - half, 1), pltpu.roll(acc, half, 1)
@@ -289,68 +256,50 @@
 
 
 def score(temps, power, shards, half):
-    first, late = temps
-    count, columns, width = late.shape
-    lanes = sum(refs[0].shape[0] for refs in shards)
-    chunked = [len(refs) > 1 for refs in shards]
-    flops = 2 * columns * 256 * count * width
-    acc_shape = jax.ShapeDtypeStruct((columns, lanes), f32)
-    operands = [first, *[refs[0] for refs in shards]]
-    acc = call(
-        functools.partial(first_score_kernel, chunked, half),
-        "score0",
-        [VMEM] * len(operands),
-        [acc_shape],
-        operands,
-        flops=flops,
-    )[0]
-    operands = [late, power, acc]
-    operands += [refs[0] for refs in shards] + [refs[-1] for refs in shards]
-    return call(
-        functools.partial(last_score_kernel, chunked, half),
-        "score1",
+    count, columns, width = temps[0].shape
+    lanes = sum(ref.shape[0] for ref in shards)
+    operands = [power, *temps, *shards]
+    return call(
+        functools.partial(score_kernel, half, len(temps)),
+        "score",
         [VMEM] * len(operands),
         [
-            acc_shape,
+            jax.ShapeDtypeStruct((columns, lanes), f32),
             jax.ShapeDtypeStruct((lanes, power.shape[1]), f32),
             jax.ShapeDtypeStruct((8, lanes), f32),
         ],
         operands,
-        flops=flops,
-    )
-
-
-def slices_kernel(counts, targets, me_ref, *refs):
-    whole_ref, refs = refs[-1], refs[:-1]
-    shards, out_refs = regroup(refs[: -len(targets)], counts), refs[-len(targets) :]
+        flops=2 * columns * 256 * count * len(temps) * width,
+    )
+
+
+def regroup(refs, counts):
+    refs = list(refs)
+    return [[refs.pop(0) for _ in range(count)] for count in counts]
+
+
+def slices_kernel(targets, me_ref, *refs):
+    shards, out_refs = refs[: -len(targets)], refs[-len(targets) :]
     span = out_refs[0].shape[1]
     filled = [0] * len(targets)
-    for k, refs in enumerate(shards):
-        source = refs[0]
-        height = source.shape[0]
-        if len(refs) > 1:
-            width = refs[-1].shape[1]
-            for c, ref in enumerate(refs):
-                whole_ref[:, c * width : (c + 1) * width] = ref[:, :width]
-            source = whole_ref
+    for k, ref in enumerate(shards):
+        height = ref.shape[0]
         for i, (distance, skip) in enumerate(targets):
             if k >= skip:
                 base = pl.multiple_of((me_ref[0] ^ distance) * span, LANES)
-                out_refs[i][filled[i] : filled[i] + height, :] = source[:, pl.ds(base, span)]
+                out_refs[i][filled[i] : filled[i] + height, :] = ref[:, pl.ds(base, span)]
                 filled[i] += height
 
 
-def cut_slices(me, shards, targets, span, freq):
-    heights = [refs[0].shape[0] for refs in shards]
-    operands = [me, *[ref for refs in shards for ref in refs]]
+def cut_slices(me, shards, targets, span):
+    heights = [ref.shape[0] for ref in shards]
     out_heights = [sum(heights[skip:]) for _, skip in targets]
     return call(
-        functools.partial(slices_kernel, [len(refs) for refs in shards], targets),
+        functools.partial(slices_kernel, targets),
         "cut_slices",
-        [SMEM] + [VMEM] * (len(operands) - 1),
+        [SMEM] + [VMEM] * len(shards),
         [jax.ShapeDtypeStruct((height, span), bf16) for height in out_heights],
-        operands,
-        [pltpu.VMEM((heights[-1], freq), bf16)],
+        (me, *shards),
         moved=4 * span * sum(out_heights),
         limit=VMEM_LIMIT if sum(heights) <= 128 else 2 * VMEM_LIMIT,
     )
@@ -604,39 +553,38 @@
     me = jnp.stack([lax.axis_index("img"), me_cls]).astype(jnp.int32)
     others = tuple(range(n_img - 1, 0, -1))
 
-    own, *own_chunks = weigh(particles, ctf, noise_weight, group_ids)
+    own = weigh(particles, ctf, noise_weight, group_ids)
     if pairwise:
-        far = [swap(w, "cls", 2) for w in own_chunks]
-        near = swap(own, "cls", 1)
-        mine, *outgoing = cut_slices(me, [[own]], [(d, 0) for d in (0,) + others[:-1]], span, freq)
+        far, near = swap(own, "cls", 2), swap(own, "cls", 1)
+        mine, *outgoing = cut_slices(me, [own], [(d, 0) for d in (0,) + others[:-1]], span)
         slices = [mine] + [swap(w, "img", d) for w, d in zip(outgoing, others)]
     else:
-        shards = [[lax.all_gather(own, "cls", axis=0, tiled=True)]]
-        mine, *outgoing = cut_slices(me, shards, [(d, 0) for d in (0,) + others], span, freq)
+        shards = [lax.all_gather(own, "cls", axis=0, tiled=True)]
+        mine, *outgoing = cut_slices(me, shards, [(d, 0) for d in (0,) + others], span)
         slices = [[w] for w in [mine] + [swap(w, "img", d) for w, d in zip(outgoing, others)]]
 
     split = jnp.transpose(classes, (1, 0, 2))
     cos_t, sin_t, power, weight = prepare(shifts, split, ctf, noise_weight)
     tile = template_tile(freq)
-    count = freq // CHUNKS // tile
+    count = freq // tile // 2
     temps = [
-        build_templates(split, cos_t, sin_t, c * count, count, tile) for c in range(CHUNKS)
+        build_templates(split, cos_t, sin_t, part * count, count, tile) for part in range(2)
     ]
     if pairwise:
         far, near, slices, power, temps = lax.optimization_barrier(
             (far, near, slices, power, temps)
         )
-        third = [swap(w, "cls", 1) for w in far]
+        third = swap(far, "cls", 1)
         targets = [(d, 1) for d in (0,) + others[:-1]] + [(others[-1], 0)]
-        mine, *outgoing = cut_slices(me, [[own], [near], far], targets, span, freq)
+        mine, *outgoing = cut_slices(me, [own, near, far], targets, span)
         arrived = [mine] + [swap(w, "img", d) for w, d in zip(outgoing, others)]
-        shards = [[own], [near], far, third]
+        shards = [own, near, far, third]
     scores, marks, stat = score(temps, power, shards, half)
     if pairwise:
         stat, arrived[-1] = lax.optimization_barrier((stat, arrived[-1]))
         stats = [stat] + [swap(stat, "cls", k) for k in range(n_cls - 1, 0, -1)]
         paired = (0,) + tuple(range(n_cls - 1, 0, -1))
-        last = [*cut_slices(me, [third], [(0, 0)], span, freq)]
+        last = [*cut_slices(me, [third], [(0, 0)], span)]
         last.append(swap(bundle(arrived[1:], 2 * half), "cls", 1))
         slices = [[a, b] for a, b in zip(slices, arrived)] + [arrived[-1:]]
     else:

time: 50.3 us -> 51.8 us (1.030)
  waiting for transfers between devices: 9.13 us -> 13.1 us
  starting transfers between devices: 18.4 us -> 16.2 us
    ppermute x17 -> x15, waiting for transfers between devices: 9.13 us -> 13.1 us  [swap(): return lax.ppermute(values, axis, [(i, i ^ distance) for i in range(size)])]
    ppermute x17 -> x15, starting transfers between devices: 18.4 us -> 16.2 us  [swap(): return lax.ppermute(values, axis, [(i, i ^ distance) for i in range(size)])]
    pallas_call x11 -> x10, Pallas kernels: 15.7 us -> 15.5 us  [call(): pl.pallas_call(kernel, in_specs=in_specs, out_specs=[VMEM] * len(out_shap...]
  transfers between devices with their start and end apart: 17 -> 15, of which waited for: 6 -> 6; matrix products, arithmetic and copies ran while one was open for 2% -> 2% of each run, Pallas kernels for 31% -> 29%
where the time goes in v18:
time: 51.8 us; the launch traced here: 51.6 us
  Pallas kernels  19.7 us (38%)
  starting transfers between devices  16.2 us (31%)
  waiting for transfers between devices  13.1 us (25%)
  local copies, waits for them, and re-layouts  1.8 us (3%)
  between operations  0.77 us (1%)
    ppermute x15, starting transfers between devices, swap(): return lax.ppermute(values, axis, [(i, i ^ distance) for i in range(size)])  16.2 us
    pallas_call x10, Pallas kernels, call(): pl.pallas_call(kernel, in_specs=in_specs, out_specs=[VMEM] * len(out_shap...  15.5 us
    ppermute x15, waiting for transfers between devices, swap(): return lax.ppermute(values, axis, [(i, i ^ distance) for i in range(size)])  13.1 us
    pallas_call x2, Pallas kernels, build_templates(): pl.pallas_call(template_kernel, grid=(count,), in_specs=[pl.BlockSpec((2,...  4.18 us
    unnamed x3, local copies, waits for them, and re-layouts  1.8 us
  transfers between devices with their start and end apart: 15, of which 6 were waited for; matrix products, arithmetic and copies ran while one was open for 2% of the time, Pallas kernels for 29%

profile of v18, /device:TPU:0, one launch (start us, length us, event | category | flops | bytes accessed | tf_op | source)
XLA Modules:
  0.0 51.6 jit_solution(13244880197258134914)
XLA Ops:
  0.6 1.7 %weigh.1.refs_0_.refs_2_ = bf16[32,4736]{1,0:T(8,128)(2,1)S(1)} custom-call(s32[16]{0:T(128)} %ids_hbm.1, bf16[16,2,4608]{2,1,0:T(2,128)(2,1)} %p_hbm.1, f32[64,4608]{1,0:T(8,128)} %ctf_hbm.3, f32[4608]{0:T(1024)} %nw_hbm.3), custom_call_target="tpu_custom_call" | custom-call | flops 294912 | bytes 1179648 | tf_op jit(solution)/shard_map/weigh/pallas_call | solution.py:29
  2.3 3.1 %collective-permute-start.1 = (bf16[32,4736]{1,0:T(8,128)(2,1)S(1)}, bf16[32,4736]{1,0:T(8,128)(2,1)S(1)}, u32[]{:S(2)}, u32[]{:S(2)}) collective-permute-start(bf16[32,4736]{1,0:T(8,128)(2,1)S(1)} %weigh.1.refs_0_.refs_2_), channel_id=1, source_target_pairs={{0,4},{4,0},{8,12},{12,8},{1,5},{5,1},{9,13},{13,9},{2,6},{6,2},{1... | collective-permute-start | bytes 909320 | tf_op jit(solution)/shard_map/ppermute | solution.py:541
  5.4 2.6 %collective-permute-start = (bf16[32,4736]{1,0:T(8,128)(2,1)S(1)}, bf16[32,4736]{1,0:T(8,128)(2,1)S(1)}, u32[]{:S(2)}, u32[]{:S(2)}) collective-permute-start(bf16[32,4736]{1,0:T(8,128)(2,1)S(1)} %weigh.1.refs_0_.refs_2_), channel_id=1, source_target_pairs={{0,8},{4,12},{8,0},{12,4},{1,9},{5,13},{9,1},{13,5},{2,10},{6,14},... | collective-permute-start | bytes 909320 | tf_op jit(solution)/shard_map/ppermute | solution.py:541
  8.0 0.1 pad_add_fusion.me_ref
  8.1 0.6 %cut_slices.3 = (bf16[32,1152]{1,0:T(8,128)(2,1)S(1)}, bf16[32,1152]{1,0:T(8,128)(2,1)S(1)}, bf16[32,1152]{1,0:T(8,128)(2,1)S(1)}) custom-call(s32[2]{0:T(128)S(1)} %pad_add_fusion.me_ref, bf16[32,4736]{1,0:T(8,128)(2,1)S(1)} %weigh.1.refs_0_.refs_2_), custom_call_target="tpu_custom_call" | custom-call | bytes 442368 | tf_op jit(solution)/shard_map/cut_slices/pallas_call | solution.py:29
  8.7 0.4 collective-permute-start.2
  9.1 1.2 %collective-permute-start.3 = (bf16[32,1152]{1,0:T(8,128)(2,1)S(1)}, bf16[32,1152]{1,0:T(8,128)(2,1)S(1)}, u32[]{:S(2)}, u32[]{:S(2)}) collective-permute-start(bf16[32,1152]{1,0:T(8,128)(2,1)S(1)} %get-tuple-element.33), channel_id=1, source_target_pairs={{0,2},{1,3},{2,0},{3,1},{4,6},{5,7},{6,4},{7,5},{8,10},{9,11},{10,... | collective-permute-start | bytes 221192 | tf_op jit(solution)/shard_map/ppermute | solution.py:541
  10.3 1.1 %copy.10 = bf16[32,2,4608]{2,0,1:T(8,128)(2,1)S(1)} copy(bf16[32,2,4608]{2,1,0:T(2,128)(2,1)} %param.7) | data formatting | bytes 1179648 | tf_op args[1]
  11.4 0.0 copy-start
  11.4 0.7 %copy-done = s32[24,2]{0,1:T(2,128)S(1)} copy-done((s32[24,2]{0,1:T(2,128)S(1)}, s32[24,2]{0,1:T(2,128)}, u32[]{:S(2)}) %copy-start) | copy-done | bytes 216
  12.1 3.1 %prepare.1 = (f32[24,4608]{1,0:T(8,128)S(1)}, f32[24,4608]{1,0:T(8,128)S(1)}, f32[32,64]{1,0:T(8,128)S(1)}, f32[64,4608]{1,0:T(8,128)S(1)}) custom-call(s32[2,24]{1,0:T(2,128)S(1)} %bitcast.10, bf16[2,32,4608]{2,1,0:T(8,128)(2,1)S(1)} %bitcast.7, f32[64,4608]{1,0:T(8,128)} %ctf_hbm.3, f32[4608]{0:T(1024)} %nw_hbm.3), custom_call_target="tpu_custom_call" | custom-call | flops 226492416 | tf_op jit(solution)/shard_map/prepare/pallas_call | solution.py:29
  15.2 2.1 %templates6.1.refs_1_ = bf16[6,768,768]{2,1,0:T(8,128)(2,1)S(1)} custom-call(bf16[2,32,4608]{2,1,0:T(8,128)(2,1)S(1)} %bitcast.8, f32[24,4608]{1,0:T(8,128)S(1)} %get-tuple-element.35.cos_ref, f32[24,4608]{1,0:T(8,128)S(1)} %get-tuple-element.36.sin_ref), custom_call_target="tpu_custom_call" | custom-call | flops 70778880 | bytes 7077888 | tf_op jit(solution)/shard_map/templates6/pallas_call | solution.py:194
  17.3 2.1 %templates0.1.refs_0_ = bf16[6,768,768]{2,1,0:T(8,128)(2,1)S(1)} custom-call(bf16[2,32,4608]{2,1,0:T(8,128)(2,1)S(1)} %bitcast.9, f32[24,4608]{1,0:T(8,128)S(1)} %get-tuple-element.35.cos_ref, f32[24,4608]{1,0:T(8,128)S(1)} %get-tuple-element.36.sin_ref), custom_call_target="tpu_custom_call" | custom-call | flops 70778880 | bytes 7077888 | tf_op jit(solution)/shard_map/templates0/pallas_call | solution.py:194
  19.4 0.0 collective-permute-done.2.refs_2_
  19.4 0.0 collective-permute-done.3.refs_4_
  19.4 0.0 collective-permute-done.1.refs_3_.refs_1_
  19.5 2.1 %collective-permute-done.refs_4_.refs_2_ = bf16[32,4736]{1,0:T(8,128)(2,1)S(1)} collective-permute-done((bf16[32,4736]{1,0:T(8,128)(2,1)S(1)}, bf16[32,4736]{1,0:T(8,128)(2,1)S(1)}, u32[]{:S(2)}, u32[]{:S(2)}) %collective-permute-start) | collective-permute-done | bytes 303136 | tf_op jit(solution)/shard_map/ppermute | solution.py:541
  21.5 0.4 collective-permute-start.4
  22.0 0.6 %cut_slices.4 = (bf16[64,1152]{1,0:T(8,128)(2,1)S(1)}, bf16[64,1152]{1,0:T(8,128)(2,1)S(1)}, bf16[64,1152]{1,0:T(8,128)(2,1)S(1)}, bf16[96,1152]{1,0:T(8,128)(2,1)S(1)}) custom-call(s32[2]{0:T(128)S(1)} %pad_add_fusion.me_ref, bf16[32,4736]{1,0:T(8,128)(2,1)S(1)} %weigh.1.refs_0_.refs_2_, bf16[32,4736]{1,0:T(8,128)(2,1)S(1)} %collective-permute-done.1.refs_3_.refs_1_, ...), custom_call_target="tpu_custom_call" | custom-call | bytes 1327104 | tf_op jit(solution)/shard_map/cut_slices/pallas_call | solution.py:29
  22.6 0.1 collective-permute-start.9
  22.6 1.6 %collective-permute-start.10 = (bf16[64,1152]{1,0:T(8,128)(2,1)S(1)}, bf16[64,1152]{1,0:T(8,128)(2,1)S(1)}, u32[]{:S(2)}, u32[]{:S(2)}) collective-permute-start(bf16[64,1152]{1,0:T(8,128)(2,1)S(1)} %get-tuple-element.54), channel_id=1, source_target_pairs={{0,2},{1,3},{2,0},{3,1},{4,6},{5,7},{6,4},{7,5},{8,10},{9,11},{10,... | collective-permute-start | bytes 442376 | tf_op jit(solution)/shard_map/ppermute | solution.py:541
  24.2 0.3 collective-permute-start.5
  24.5 4.4 %collective-permute-done.4.refs_5_.refs_0_ = bf16[32,4736]{1,0:T(8,128)(2,1)S(1)} collective-permute-done((bf16[32,4736]{1,0:T(8,128)(2,1)S(1)}, bf16[32,4736]{1,0:T(8,128)(2,1)S(1)}, u32[]{:S(2)}, u32[]{:S(2)}) %collective-permute-start.4) | collective-permute-done | bytes 303136 | tf_op jit(solution)/shard_map/ppermute | solution.py:541
  28.9 4.1 %score.1 = (f32[768,128]{1,0:T(8,128)S(1)}, f32[128,64]{1,0:T(8,128)S(1)}, f32[8,128]{1,0:T(8,128)S(1)}) custom-call(f32[32,64]{1,0:T(8,128)S(1)} %get-tuple-element.37.pow_ref, bf16[6,768,768]{2,1,0:T(8,128)(2,1)S(1)} %templates0.1.refs_0_, bf16[6,768,768]{2,1,0:T(8,128)(2,1)S(1)} %templates6.1.refs_1_, bf16[32,4736]{1,0:T(8,128)(2,1)S(1)} %weigh.1.refs_0_.refs_2_, ...), custom_call_target="tpu_custom_call" | custom-call | flops 3623878656 | tf_op jit(solution)/shard_map/score/pallas_call | solution.py:29
  33.0 0.0 collective-permute-done.5.refs_6_.refs_2_
  33.0 1.1 %collective-permute-start.8 = (f32[8,128]{1,0:T(8,128)S(1)}, f32[8,128]{1,0:T(8,128)S(1)}, u32[]{:S(2)}, u32[]{:S(2)}) collective-permute-start(f32[8,128]{1,0:T(8,128)S(1)} %get-tuple-element.46.refs_0_), channel_id=1, source_target_pairs={{0,4},{4,0},{8,12},{12,8},{1,5},{5,1},{9,13},{13,9},{2,6},{6,2},{1... | collective-permute-start | bytes 12296 | tf_op jit(solution)/shard_map/ppermute | solution.py:541
  34.1 1.5 %collective-permute-start.7 = (f32[8,128]{1,0:T(8,128)S(1)}, f32[8,128]{1,0:T(8,128)S(1)}, u32[]{:S(2)}, u32[]{:S(2)}) collective-permute-start(f32[8,128]{1,0:T(8,128)S(1)} %get-tuple-element.46.refs_0_), channel_id=1, source_target_pairs={{0,8},{4,12},{8,0},{12,4},{1,9},{5,13},{9,1},{13,5},{2,10},{6,14},... | collective-permute-start | bytes 12296 | tf_op jit(solution)/shard_map/ppermute | solution.py:541
  35.6 1.9 %collective-permute-start.6 = (f32[8,128]{1,0:T(8,128)S(1)}, f32[8,128]{1,0:T(8,128)S(1)}, u32[]{:S(2)}, u32[]{:S(2)}) collective-permute-start(f32[8,128]{1,0:T(8,128)S(1)} %get-tuple-element.46.refs_0_), channel_id=1, source_target_pairs={{0,12},{4,8},{8,4},{12,0},{1,13},{5,9},{9,5},{13,1},{2,14},{6,10},... | collective-permute-start | bytes 12296 | tf_op jit(solution)/shard_map/ppermute | solution.py:541
  37.4 0.0 collective-permute-done.9.refs_3_.refs_0_
  37.4 0.0 collective-permute-done.10.refs_5_.refs_1_
  37.5 0.2 collective-permute-start.14
  37.7 0.6 %cut_slices.5.refs_4_ = bf16[32,1152]{1,0:T(8,128)(2,1)S(1)} custom-call(s32[2]{0:T(128)S(1)} %pad_add_fusion.me_ref, bf16[32,4736]{1,0:T(8,128)(2,1)S(1)} %collective-permute-done.4.refs_5_.refs_0_), custom_call_target="tpu_custom_call" | custom-call | bytes 147456 | tf_op jit(solution)/shard_map/cut_slices/pallas_call | solution.py:29
  38.2 0.0 collective-permute-done.8.refs_3_
  38.3 0.5 collective-permute-done.7.refs_2_
  38.7 2.3 %collective-permute-done.6.refs_1_ = f32[8,128]{1,0:T(8,128)S(1)} collective-permute-done((f32[8,128]{1,0:T(8,128)S(1)}, f32[8,128]{1,0:T(8,128)S(1)}, u32[]{:S(2)}, u32[]{:S(2)}) %collective-permute-start.6) | collective-permute-done | bytes 4128 | tf_op jit(solution)/shard_map/ppermute | solution.py:541
  41.0 0.5 responsibilities.1
  41.5 0.0 collective-permute-start.13
  41.5 1.6 %collective-permute-start.12 = (bf16[416,128]{1,0:T(8,128)(2,1)S(1)}, bf16[416,128]{1,0:T(8,128)(2,1)S(1)}, u32[]{:S(2)}, u32[]{:S(2)}) collective-permute-start(bf16[416,128]{1,0:T(8,128)(2,1)S(1)} %get-tuple-element.59.refs_0_), channel_id=1, source_target_pairs={{0,2},{1,3},{2,0},{3,1},{4,6},{5,7},{6,4},{7,5},{8,10},{9,11},{10,... | collective-permute-start | bytes 319496 | tf_op jit(solution)/shard_map/ppermute | solution.py:541
  43.1 0.3 collective-permute-start.11
  43.4 1.5 %gather_rows.1 = (f32[32,64]{1,0:T(8,128)}, bf16[64,2304]{1,0:T(8,128)(2,1)S(1)}, bf16[2,192,1152]{2,1,0:T(8,128)(2,1)S(1)}) custom-call(s32[2]{0:T(128)S(1)} %pad_add_fusion.me_ref, f32[768,128]{1,0:T(8,128)S(1)} %get-tuple-element.42.s_ref, f32[1,128]{1,0:T(1,128)S(1)} %get-tuple-element.47.norm_ref, f32[64,4608]{1,0:T(8,128)S(1)} %get-tuple-element.48.weight_ref, ...), custom_call_target="tpu_custom_call" | custom-call | flops 20000000000 | bytes 1769472 | tf_op jit(solution)/shard_map/gather_rows/pallas_call | solution.py:29
  44.9 0.0 collective-permute-done.13.refs_3_
  44.9 2.5 %collective-permute-done.12.refs_2_ = bf16[416,128]{1,0:T(8,128)(2,1)S(1)} collective-permute-done((bf16[416,128]{1,0:T(8,128)(2,1)S(1)}, bf16[416,128]{1,0:T(8,128)(2,1)S(1)}, u32[]{:S(2)}, u32[]{:S(2)}) %collective-permute-start.12) | collective-permute-done | bytes 106528 | tf_op jit(solution)/shard_map/ppermute | solution.py:541
  47.3 1.4 %collective-permute-done.11.refs_1_ = bf16[416,128]{1,0:T(8,128)(2,1)S(1)} collective-permute-done((bf16[416,128]{1,0:T(8,128)(2,1)S(1)}, bf16[416,128]{1,0:T(8,128)(2,1)S(1)}, u32[]{:S(2)}, u32[]{:S(2)}) %collective-permute-start.11) | collective-permute-done | bytes 106528 | tf_op jit(solution)/shard_map/ppermute | solution.py:541
  48.7 0.0 collective-permute-done.14.refs_5_
  48.7 2.9 %finish.1 = f32[32,2,1152]{2,1,0:T(2,128)} custom-call(s32[2]{0:T(128)S(1)} %pad_add_fusion.me_ref, bf16[64,2304]{1,0:T(8,128)(2,1)S(1)} %get-tuple-element.57.cw_ref, f32[24,4608]{1,0:T(8,128)S(1)} %get-tuple-element.35.cos_ref, f32[24,4608]{1,0:T(8,128)S(1)} %get-tuple-element.36.sin_ref, bf16[2,192,1152]{2,1,0:T(8,128)(2,1)S(1)} %get-tuple-element.58.rows_ref, ...), custom_call_target="tpu_custom_call" | custom-call | flops 905969664 | tf_op jit(solution)/shard_map/finish/pallas_call | solution.py:29
  (1 shorter events, 0.0 us)
Async XLA Ops:
  2.3 17.1 %collective-permute-start.1 = (bf16[32,4736]{1,0:T(8,128)(2,1)S(1)}, bf16[32,4736]{1,0:T(8,128)(2,1)S(1)}, u32[]{:S(2)}, u32[]{:S(2)}) collective-permute-start(bf16[32,4736]{1,0:T(8,128)(2,1)S(1)} %weigh.1.refs_0_.refs_2_), channel_id=1, source_target_pairs={{0,4},{4,0},{8,12},{12,8},{1,5},{5,1},{9,13},{13,9},{2,6},{6,2},{1... | collective-permute-start | bytes 909320 | tf_op jit(solution)/shard_map/ppermute | solution.py:541
  5.4 16.1 %collective-permute-start = (bf16[32,4736]{1,0:T(8,128)(2,1)S(1)}, bf16[32,4736]{1,0:T(8,128)(2,1)S(1)}, u32[]{:S(2)}, u32[]{:S(2)}) collective-permute-start(bf16[32,4736]{1,0:T(8,128)(2,1)S(1)} %weigh.1.refs_0_.refs_2_), channel_id=1, source_target_pairs={{0,8},{4,12},{8,0},{12,4},{1,9},{5,13},{9,1},{13,5},{2,10},{6,14},... | collective-permute-start | bytes 909320 | tf_op jit(solution)/shard_map/ppermute | solution.py:541
  8.7 10.8 %collective-permute-start.2 = (bf16[32,1152]{1,0:T(8,128)(2,1)S(1)}, bf16[32,1152]{1,0:T(8,128)(2,1)S(1)}, u32[]{:S(2)}, u32[]{:S(2)}) collective-permute-start(bf16[32,1152]{1,0:T(8,128)(2,1)S(1)} %get-tuple-element.32), channel_id=1, source_target_pairs={{0,3},{1,2},{2,1},{3,0},{4,7},{5,6},{6,5},{7,4},{8,11},{9,10},{10,... | collective-permute-start | bytes 221192 | tf_op jit(solution)/shard_map/ppermute | solution.py:541
  9.1 10.3 %collective-permute-start.3 = (bf16[32,1152]{1,0:T(8,128)(2,1)S(1)}, bf16[32,1152]{1,0:T(8,128)(2,1)S(1)}, u32[]{:S(2)}, u32[]{:S(2)}) collective-permute-start(bf16[32,1152]{1,0:T(8,128)(2,1)S(1)} %get-tuple-element.33), channel_id=1, source_target_pairs={{0,2},{1,3},{2,0},{3,1},{4,6},{5,7},{6,4},{7,5},{8,10},{9,11},{10,... | collective-permute-start | bytes 221192 | tf_op jit(solution)/shard_map/ppermute | solution.py:541
  11.4 0.7 %copy-start = (s32[24,2]{0,1:T(2,128)S(1)}, s32[24,2]{0,1:T(2,128)}, u32[]{:S(2)}) copy-start(s32[24,2]{0,1:T(2,128)} %param.11) | copy-start | bytes 580
  21.5 7.4 %collective-permute-start.4 = (bf16[32,4736]{1,0:T(8,128)(2,1)S(1)}, bf16[32,4736]{1,0:T(8,128)(2,1)S(1)}, u32[]{:S(2)}, u32[]{:S(2)}) collective-permute-start(bf16[32,4736]{1,0:T(8,128)(2,1)S(1)} %collective-permute-done.refs_4_.refs_2_), channel_id=1, source_target_pairs={{0,4},{4,0},{8,12},{12,8},{1,5},{5,1},{9,13},{13,9},{2,6},{6,2},{1... | collective-permute-start | bytes 909320 | tf_op jit(solution)/shard_map/ppermute | solution.py:541
  22.6 14.9 %collective-permute-start.9 = (bf16[64,1152]{1,0:T(8,128)(2,1)S(1)}, bf16[64,1152]{1,0:T(8,128)(2,1)S(1)}, u32[]{:S(2)}, u32[]{:S(2)}) collective-permute-start(bf16[64,1152]{1,0:T(8,128)(2,1)S(1)} %get-tuple-element.52), channel_id=1, source_target_pairs={{0,3},{1,2},{2,1},{3,0},{4,7},{5,6},{6,5},{7,4},{8,11},{9,10},{10,... | collective-permute-start | bytes 442376 | tf_op jit(solution)/shard_map/ppermute | solution.py:541
  22.6 14.8 %collective-permute-start.10 = (bf16[64,1152]{1,0:T(8,128)(2,1)S(1)}, bf16[64,1152]{1,0:T(8,128)(2,1)S(1)}, u32[]{:S(2)}, u32[]{:S(2)}) collective-permute-start(bf16[64,1152]{1,0:T(8,128)(2,1)S(1)} %get-tuple-element.54), channel_id=1, source_target_pairs={{0,2},{1,3},{2,0},{3,1},{4,6},{5,7},{6,4},{7,5},{8,10},{9,11},{10,... | collective-permute-start | bytes 442376 | tf_op jit(solution)/shard_map/ppermute | solution.py:541
  24.2 8.8 %collective-permute-start.5 = (bf16[96,1152]{1,0:T(8,128)(2,1)S(1)}, bf16[96,1152]{1,0:T(8,128)(2,1)S(1)}, u32[]{:S(2)}, u32[]{:S(2)}) collective-permute-start(bf16[96,1152]{1,0:T(8,128)(2,1)S(1)} %get-tuple-element.45), channel_id=1, source_target_pairs={{0,1},{1,0},{2,3},{3,2},{4,5},{5,4},{6,7},{7,6},{8,9},{9,8},{10,11... | collective-permute-start | bytes 663560 | tf_op jit(solution)/shard_map/ppermute | solution.py:541
  33.0 5.3 %collective-permute-start.8 = (f32[8,128]{1,0:T(8,128)S(1)}, f32[8,128]{1,0:T(8,128)S(1)}, u32[]{:S(2)}, u32[]{:S(2)}) collective-permute-start(f32[8,128]{1,0:T(8,128)S(1)} %get-tuple-element.46.refs_0_), channel_id=1, source_target_pairs={{0,4},{4,0},{8,12},{12,8},{1,5},{5,1},{9,13},{13,9},{2,6},{6,2},{1... | collective-permute-start | bytes 12296 | tf_op jit(solution)/shard_map/ppermute | solution.py:541
  34.1 4.6 %collective-permute-start.7 = (f32[8,128]{1,0:T(8,128)S(1)}, f32[8,128]{1,0:T(8,128)S(1)}, u32[]{:S(2)}, u32[]{:S(2)}) collective-permute-start(f32[8,128]{1,0:T(8,128)S(1)} %get-tuple-element.46.refs_0_), channel_id=1, source_target_pairs={{0,8},{4,12},{8,0},{12,4},{1,9},{5,13},{9,1},{13,5},{2,10},{6,14},... | collective-permute-start | bytes 12296 | tf_op jit(solution)/shard_map/ppermute | solution.py:541
  35.6 5.4 %collective-permute-start.6 = (f32[8,128]{1,0:T(8,128)S(1)}, f32[8,128]{1,0:T(8,128)S(1)}, u32[]{:S(2)}, u32[]{:S(2)}) collective-permute-start(f32[8,128]{1,0:T(8,128)S(1)} %get-tuple-element.46.refs_0_), channel_id=1, source_target_pairs={{0,12},{4,8},{8,4},{12,0},{1,13},{5,9},{9,5},{13,1},{2,14},{6,10},... | collective-permute-start | bytes 12296 | tf_op jit(solution)/shard_map/ppermute | solution.py:541
  37.5 11.2 %collective-permute-start.14 = (bf16[96,1152]{1,0:T(8,128)(2,1)S(1)}, bf16[96,1152]{1,0:T(8,128)(2,1)S(1)}, u32[]{:S(2)}, u32[]{:S(2)}) collective-permute-start(bf16[96,1152]{1,0:T(8,128)(2,1)S(1)} %bundle.1), channel_id=1, source_target_pairs={{0,4},{4,0},{8,12},{12,8},{1,5},{5,1},{9,13},{13,9},{2,6},{6,2},{1... | collective-permute-start | bytes 663560 | tf_op jit(solution)/shard_map/ppermute | solution.py:541
  41.5 3.4 %collective-permute-start.13 = (bf16[416,128]{1,0:T(8,128)(2,1)S(1)}, bf16[416,128]{1,0:T(8,128)(2,1)S(1)}, u32[]{:S(2)}, u32[]{:S(2)}) collective-permute-start(bf16[416,128]{1,0:T(8,128)(2,1)S(1)} %get-tuple-element.59.refs_0_), channel_id=1, source_target_pairs={{0,1},{1,0},{2,3},{3,2},{4,5},{5,4},{6,7},{7,6},{8,9},{9,8},{10,11... | collective-permute-start | bytes 319496 | tf_op jit(solution)/shard_map/ppermute | solution.py:541
  41.5 5.8 %collective-permute-start.12 = (bf16[416,128]{1,0:T(8,128)(2,1)S(1)}, bf16[416,128]{1,0:T(8,128)(2,1)S(1)}, u32[]{:S(2)}, u32[]{:S(2)}) collective-permute-start(bf16[416,128]{1,0:T(8,128)(2,1)S(1)} %get-tuple-element.59.refs_0_), channel_id=1, source_target_pairs={{0,2},{1,3},{2,0},{3,1},{4,6},{5,7},{6,4},{7,5},{8,10},{9,11},{10,... | collective-permute-start | bytes 319496 | tf_op jit(solution)/shard_map/ppermute | solution.py:541
  43.1 5.6 %collective-permute-start.11 = (bf16[416,128]{1,0:T(8,128)(2,1)S(1)}, bf16[416,128]{1,0:T(8,128)(2,1)S(1)}, u32[]{:S(2)}, u32[]{:S(2)}) collective-permute-start(bf16[416,128]{1,0:T(8,128)(2,1)S(1)} %get-tuple-element.59.refs_0_), channel_id=1, source_target_pairs={{0,3},{1,2},{2,1},{3,0},{4,7},{5,6},{6,5},{7,4},{8,11},{9,10},{10,... | collective-permute-start | bytes 319496 | tf_op jit(solution)/shard_map/ppermute | solution.py:541

commit v19 on v18

--- a/solution.py
+++ b/solution.py
@@ -450,7 +450,7 @@
 
 
 def finish_kernel(poses, groups, sources, half, me_ref, cw_ref, cos_ref, sin_ref, rows_ref, *refs):
-    payloads, refs = refs[:sources], refs[sources:]
+    payloads, refs = refs[:1] + refs[sources - 1 : 0 : -1], refs[sources:]
     last, (out_ref, rho_ref, inverse_ref, *buffers) = refs[:-5], refs[-5:]
     rows, _, span = out_ref.shape
     cut = poses // 2 * rows
@@ -582,8 +582,8 @@
     scores, marks, stat = score(temps, power, shards, half)
     if pairwise:
         stat, arrived[-1] = lax.optimization_barrier((stat, arrived[-1]))
-        stats = [stat] + [swap(stat, "cls", k) for k in range(n_cls - 1, 0, -1)]
-        paired = (0,) + tuple(range(n_cls - 1, 0, -1))
+        stats = [stat] + [swap(stat, "cls", k) for k in range(1, n_cls)]
+        paired = tuple(range(n_cls))
         last = [*cut_slices(me, [third], [(0, 0)], span)]
         last.append(swap(bundle(arrived[1:], 2 * half), "cls", 1))
         slices = [[a, b] for a, b in zip(slices, arrived)] + [arrived[-1:]]
@@ -592,7 +592,7 @@
         paired = (0,)
         last = []
     norm, payload = responsibilities(scores, marks, stats, paired, poses, half)
-    payloads = [payload] + [swap(payload, "img", d) for d in others]
+    payloads = [payload] + [swap(payload, "img", d) for d in others[::-1]]
     log_resp, weight_here, rows = gather_rows(
         me, scores, norm, weight, slices, poses, half, span
     )

time: 51.8 us -> 50.7 us (0.979)
  waiting for transfers between devices: 13.1 us -> 12 us
    ppermute x15, waiting for transfers between devices: 13.1 us -> 12 us  [swap(): return lax.ppermute(values, axis, [(i, i ^ distance) for i in range(size)])]
  transfers between devices with their start and end apart: 15 -> 15, of which waited for: 6 -> 6; matrix products, arithmetic and copies ran while one was open for 2% -> 2% of each run, Pallas kernels for 29% -> 30%
where the time goes in v19:
time: 50.7 us; the launch traced here: 50.5 us
  Pallas kernels  19.7 us (39%)
  starting transfers between devices  16.2 us (32%)
  waiting for transfers between devices  12 us (24%)
  local copies, waits for them, and re-layouts  1.8 us (4%)
  between operations  0.77 us (2%)
    ppermute x15, starting transfers between devices, swap(): return lax.ppermute(values, axis, [(i, i ^ distance) for i in range(size)])  16.2 us
    pallas_call x10, Pallas kernels, call(): pl.pallas_call(kernel, in_specs=in_specs, out_specs=[VMEM] * len(out_shap...  15.5 us
    ppermute x15, waiting for transfers between devices, swap(): return lax.ppermute(values, axis, [(i, i ^ distance) for i in range(size)])  12 us
    pallas_call x2, Pallas kernels, build_templates(): pl.pallas_call(template_kernel, grid=(count,), in_specs=[pl.BlockSpec((2,...  4.18 us
    unnamed x3, local copies, waits for them, and re-layouts  1.8 us
  transfers between devices with their start and end apart: 15, of which 6 were waited for; matrix products, arithmetic and copies ran while one was open for 2% of the time, Pallas kernels for 30%

profile of v19, /device:TPU:0, one launch (start us, length us, event | category | flops | bytes accessed | tf_op | source)
XLA Modules:
  0.0 50.5 jit_solution(628909951232056251)
XLA Ops:
  0.6 1.7 %weigh.1.refs_0_.refs_2_ = bf16[32,4736]{1,0:T(8,128)(2,1)S(1)} custom-call(s32[16]{0:T(128)} %ids_hbm.1, bf16[16,2,4608]{2,1,0:T(2,128)(2,1)} %p_hbm.1, f32[64,4608]{1,0:T(8,128)} %ctf_hbm.3, f32[4608]{0:T(1024)} %nw_hbm.3), custom_call_target="tpu_custom_call" | custom-call | flops 294912 | bytes 1179648 | tf_op jit(solution)/shard_map/weigh/pallas_call | solution.py:29
  2.3 3.1 %collective-permute-start.1 = (bf16[32,4736]{1,0:T(8,128)(2,1)S(1)}, bf16[32,4736]{1,0:T(8,128)(2,1)S(1)}, u32[]{:S(2)}, u32[]{:S(2)}) collective-permute-start(bf16[32,4736]{1,0:T(8,128)(2,1)S(1)} %weigh.1.refs_0_.refs_2_), channel_id=1, source_target_pairs={{0,4},{4,0},{8,12},{12,8},{1,5},{5,1},{9,13},{13,9},{2,6},{6,2},{1... | collective-permute-start | bytes 909320 | tf_op jit(solution)/shard_map/ppermute | solution.py:541
  5.4 2.6 %collective-permute-start = (bf16[32,4736]{1,0:T(8,128)(2,1)S(1)}, bf16[32,4736]{1,0:T(8,128)(2,1)S(1)}, u32[]{:S(2)}, u32[]{:S(2)}) collective-permute-start(bf16[32,4736]{1,0:T(8,128)(2,1)S(1)} %weigh.1.refs_0_.refs_2_), channel_id=1, source_target_pairs={{0,8},{4,12},{8,0},{12,4},{1,9},{5,13},{9,1},{13,5},{2,10},{6,14},... | collective-permute-start | bytes 909320 | tf_op jit(solution)/shard_map/ppermute | solution.py:541
  8.0 0.1 pad_add_fusion.me_ref
  8.1 0.6 %cut_slices.3 = (bf16[32,1152]{1,0:T(8,128)(2,1)S(1)}, bf16[32,1152]{1,0:T(8,128)(2,1)S(1)}, bf16[32,1152]{1,0:T(8,128)(2,1)S(1)}) custom-call(s32[2]{0:T(128)S(1)} %pad_add_fusion.me_ref, bf16[32,4736]{1,0:T(8,128)(2,1)S(1)} %weigh.1.refs_0_.refs_2_), custom_call_target="tpu_custom_call" | custom-call | bytes 442368 | tf_op jit(solution)/shard_map/cut_slices/pallas_call | solution.py:29
  8.7 0.4 collective-permute-start.2
  9.1 1.2 %collective-permute-start.3 = (bf16[32,1152]{1,0:T(8,128)(2,1)S(1)}, bf16[32,1152]{1,0:T(8,128)(2,1)S(1)}, u32[]{:S(2)}, u32[]{:S(2)}) collective-permute-start(bf16[32,1152]{1,0:T(8,128)(2,1)S(1)} %get-tuple-element.33), channel_id=1, source_target_pairs={{0,2},{1,3},{2,0},{3,1},{4,6},{5,7},{6,4},{7,5},{8,10},{9,11},{10,... | collective-permute-start | bytes 221192 | tf_op jit(solution)/shard_map/ppermute | solution.py:541
  10.3 1.1 %copy.10 = bf16[32,2,4608]{2,0,1:T(8,128)(2,1)S(1)} copy(bf16[32,2,4608]{2,1,0:T(2,128)(2,1)} %param.7) | data formatting | bytes 1179648 | tf_op args[1]
  11.4 0.0 copy-start
  11.4 0.7 %copy-done = s32[24,2]{0,1:T(2,128)S(1)} copy-done((s32[24,2]{0,1:T(2,128)S(1)}, s32[24,2]{0,1:T(2,128)}, u32[]{:S(2)}) %copy-start) | copy-done | bytes 216
  12.1 3.1 %prepare.1 = (f32[24,4608]{1,0:T(8,128)S(1)}, f32[24,4608]{1,0:T(8,128)S(1)}, f32[32,64]{1,0:T(8,128)S(1)}, f32[64,4608]{1,0:T(8,128)S(1)}) custom-call(s32[2,24]{1,0:T(2,128)S(1)} %bitcast.10, bf16[2,32,4608]{2,1,0:T(8,128)(2,1)S(1)} %bitcast.7, f32[64,4608]{1,0:T(8,128)} %ctf_hbm.3, f32[4608]{0:T(1024)} %nw_hbm.3), custom_call_target="tpu_custom_call" | custom-call | flops 226492416 | tf_op jit(solution)/shard_map/prepare/pallas_call | solution.py:29
  15.2 2.1 %templates6.1.refs_1_ = bf16[6,768,768]{2,1,0:T(8,128)(2,1)S(1)} custom-call(bf16[2,32,4608]{2,1,0:T(8,128)(2,1)S(1)} %bitcast.8, f32[24,4608]{1,0:T(8,128)S(1)} %get-tuple-element.35.cos_ref, f32[24,4608]{1,0:T(8,128)S(1)} %get-tuple-element.36.sin_ref), custom_call_target="tpu_custom_call" | custom-call | flops 70778880 | bytes 7077888 | tf_op jit(solution)/shard_map/templates6/pallas_call | solution.py:194
  17.3 2.1 %templates0.1.refs_0_ = bf16[6,768,768]{2,1,0:T(8,128)(2,1)S(1)} custom-call(bf16[2,32,4608]{2,1,0:T(8,128)(2,1)S(1)} %bitcast.9, f32[24,4608]{1,0:T(8,128)S(1)} %get-tuple-element.35.cos_ref, f32[24,4608]{1,0:T(8,128)S(1)} %get-tuple-element.36.sin_ref), custom_call_target="tpu_custom_call" | custom-call | flops 70778880 | bytes 7077888 | tf_op jit(solution)/shard_map/templates0/pallas_call | solution.py:194
  19.4 0.0 collective-permute-done.2.refs_2_
  19.4 0.0 collective-permute-done.3.refs_4_
  19.4 0.0 collective-permute-done.1.refs_3_.refs_1_
  19.5 2.1 %collective-permute-done.refs_4_.refs_2_ = bf16[32,4736]{1,0:T(8,128)(2,1)S(1)} collective-permute-done((bf16[32,4736]{1,0:T(8,128)(2,1)S(1)}, bf16[32,4736]{1,0:T(8,128)(2,1)S(1)}, u32[]{:S(2)}, u32[]{:S(2)}) %collective-permute-start) | collective-permute-done | bytes 303136 | tf_op jit(solution)/shard_map/ppermute | solution.py:541
  21.5 0.4 collective-permute-start.4
  22.0 0.6 %cut_slices.4 = (bf16[64,1152]{1,0:T(8,128)(2,1)S(1)}, bf16[64,1152]{1,0:T(8,128)(2,1)S(1)}, bf16[64,1152]{1,0:T(8,128)(2,1)S(1)}, bf16[96,1152]{1,0:T(8,128)(2,1)S(1)}) custom-call(s32[2]{0:T(128)S(1)} %pad_add_fusion.me_ref, bf16[32,4736]{1,0:T(8,128)(2,1)S(1)} %weigh.1.refs_0_.refs_2_, bf16[32,4736]{1,0:T(8,128)(2,1)S(1)} %collective-permute-done.1.refs_3_.refs_1_, ...), custom_call_target="tpu_custom_call" | custom-call | bytes 1327104 | tf_op jit(solution)/shard_map/cut_slices/pallas_call | solution.py:29
  22.6 0.1 collective-permute-start.9
  22.6 1.6 %collective-permute-start.10 = (bf16[64,1152]{1,0:T(8,128)(2,1)S(1)}, bf16[64,1152]{1,0:T(8,128)(2,1)S(1)}, u32[]{:S(2)}, u32[]{:S(2)}) collective-permute-start(bf16[64,1152]{1,0:T(8,128)(2,1)S(1)} %get-tuple-element.54), channel_id=1, source_target_pairs={{0,2},{1,3},{2,0},{3,1},{4,6},{5,7},{6,4},{7,5},{8,10},{9,11},{10,... | collective-permute-start | bytes 442376 | tf_op jit(solution)/shard_map/ppermute | solution.py:541
  24.2 0.3 collective-permute-start.5
  24.5 4.4 %collective-permute-done.4.refs_5_.refs_0_ = bf16[32,4736]{1,0:T(8,128)(2,1)S(1)} collective-permute-done((bf16[32,4736]{1,0:T(8,128)(2,1)S(1)}, bf16[32,4736]{1,0:T(8,128)(2,1)S(1)}, u32[]{:S(2)}, u32[]{:S(2)}) %collective-permute-start.4) | collective-permute-done | bytes 303136 | tf_op jit(solution)/shard_map/ppermute | solution.py:541
  28.9 4.1 %score.1 = (f32[768,128]{1,0:T(8,128)S(1)}, f32[128,64]{1,0:T(8,128)S(1)}, f32[8,128]{1,0:T(8,128)S(1)}) custom-call(f32[32,64]{1,0:T(8,128)S(1)} %get-tuple-element.37.pow_ref, bf16[6,768,768]{2,1,0:T(8,128)(2,1)S(1)} %templates0.1.refs_0_, bf16[6,768,768]{2,1,0:T(8,128)(2,1)S(1)} %templates6.1.refs_1_, bf16[32,4736]{1,0:T(8,128)(2,1)S(1)} %weigh.1.refs_0_.refs_2_, ...), custom_call_target="tpu_custom_call" | custom-call | flops 3623878656 | tf_op jit(solution)/shard_map/score/pallas_call | solution.py:29
  33.0 0.0 collective-permute-done.5.refs_6_.refs_2_
  33.0 2.0 %collective-permute-start.8 = (f32[8,128]{1,0:T(8,128)S(1)}, f32[8,128]{1,0:T(8,128)S(1)}, u32[]{:S(2)}, u32[]{:S(2)}) collective-permute-start(f32[8,128]{1,0:T(8,128)S(1)} %get-tuple-element.46.refs_0_), channel_id=1, source_target_pairs={{0,12},{4,8},{8,4},{12,0},{1,13},{5,9},{9,5},{13,1},{2,14},{6,10},... | collective-permute-start | bytes 12296 | tf_op jit(solution)/shard_map/ppermute | solution.py:541
  35.0 0.5 %collective-permute-start.7 = (f32[8,128]{1,0:T(8,128)S(1)}, f32[8,128]{1,0:T(8,128)S(1)}, u32[]{:S(2)}, u32[]{:S(2)}) collective-permute-start(f32[8,128]{1,0:T(8,128)S(1)} %get-tuple-element.46.refs_0_), channel_id=1, source_target_pairs={{0,8},{4,12},{8,0},{12,4},{1,9},{5,13},{9,1},{13,5},{2,10},{6,14},... | collective-permute-start | bytes 12296 | tf_op jit(solution)/shard_map/ppermute | solution.py:541
  35.6 1.9 %collective-permute-start.6 = (f32[8,128]{1,0:T(8,128)S(1)}, f32[8,128]{1,0:T(8,128)S(1)}, u32[]{:S(2)}, u32[]{:S(2)}) collective-permute-start(f32[8,128]{1,0:T(8,128)S(1)} %get-tuple-element.46.refs_0_), channel_id=1, source_target_pairs={{0,4},{4,0},{8,12},{12,8},{1,5},{5,1},{9,13},{13,9},{2,6},{6,2},{1... | collective-permute-start | bytes 12296 | tf_op jit(solution)/shard_map/ppermute | solution.py:541
  37.4 0.0 collective-permute-done.9.refs_3_.refs_0_
  37.4 0.0 collective-permute-done.10.refs_5_.refs_1_
  37.5 0.2 collective-permute-start.14
  37.7 0.6 %cut_slices.5.refs_4_ = bf16[32,1152]{1,0:T(8,128)(2,1)S(1)} custom-call(s32[2]{0:T(128)S(1)} %pad_add_fusion.me_ref, bf16[32,4736]{1,0:T(8,128)(2,1)S(1)} %collective-permute-done.4.refs_5_.refs_0_), custom_call_target="tpu_custom_call" | custom-call | bytes 147456 | tf_op jit(solution)/shard_map/cut_slices/pallas_call | solution.py:29
  38.2 0.3 collective-permute-done.8.refs_3_
  38.6 1.0 %collective-permute-done.7.refs_2_ = f32[8,128]{1,0:T(8,128)S(1)} collective-permute-done((f32[8,128]{1,0:T(8,128)S(1)}, f32[8,128]{1,0:T(8,128)S(1)}, u32[]{:S(2)}, u32[]{:S(2)}) %collective-permute-start.7) | collective-permute-done | bytes 4128 | tf_op jit(solution)/shard_map/ppermute | solution.py:541
  39.5 0.0 collective-permute-done.6.refs_1_
  39.5 0.5 responsibilities.1
  40.0 0.0 collective-permute-start.13
  40.0 1.6 %collective-permute-start.12 = (bf16[416,128]{1,0:T(8,128)(2,1)S(1)}, bf16[416,128]{1,0:T(8,128)(2,1)S(1)}, u32[]{:S(2)}, u32[]{:S(2)}) collective-permute-start(bf16[416,128]{1,0:T(8,128)(2,1)S(1)} %get-tuple-element.59.refs_0_), channel_id=1, source_target_pairs={{0,2},{1,3},{2,0},{3,1},{4,6},{5,7},{6,4},{7,5},{8,10},{9,11},{10,... | collective-permute-start | bytes 319496 | tf_op jit(solution)/shard_map/ppermute | solution.py:541
  41.6 0.3 collective-permute-start.11
  41.9 1.5 %gather_rows.1 = (f32[32,64]{1,0:T(8,128)}, bf16[64,2304]{1,0:T(8,128)(2,1)S(1)}, bf16[2,192,1152]{2,1,0:T(8,128)(2,1)S(1)}) custom-call(s32[2]{0:T(128)S(1)} %pad_add_fusion.me_ref, f32[768,128]{1,0:T(8,128)S(1)} %get-tuple-element.42.s_ref, f32[1,128]{1,0:T(1,128)S(1)} %get-tuple-element.47.norm_ref, f32[64,4608]{1,0:T(8,128)S(1)} %get-tuple-element.48.weight_ref, ...), custom_call_target="tpu_custom_call" | custom-call | flops 20000000000 | bytes 1769472 | tf_op jit(solution)/shard_map/gather_rows/pallas_call | solution.py:29
  43.4 1.9 %collective-permute-done.13.refs_3_ = bf16[416,128]{1,0:T(8,128)(2,1)S(1)} collective-permute-done((bf16[416,128]{1,0:T(8,128)(2,1)S(1)}, bf16[416,128]{1,0:T(8,128)(2,1)S(1)}, u32[]{:S(2)}, u32[]{:S(2)}) %collective-permute-start.13) | collective-permute-done | bytes 106528 | tf_op jit(solution)/shard_map/ppermute | solution.py:541
  45.3 2.3 %collective-permute-done.12.refs_2_ = bf16[416,128]{1,0:T(8,128)(2,1)S(1)} collective-permute-done((bf16[416,128]{1,0:T(8,128)(2,1)S(1)}, bf16[416,128]{1,0:T(8,128)(2,1)S(1)}, u32[]{:S(2)}, u32[]{:S(2)}) %collective-permute-start.12) | collective-permute-done | bytes 106528 | tf_op jit(solution)/shard_map/ppermute | solution.py:541
  47.6 0.0 collective-permute-done.11.refs_1_
  47.6 0.0 collective-permute-done.14.refs_5_
  47.6 2.9 %finish.1 = f32[32,2,1152]{2,1,0:T(2,128)} custom-call(s32[2]{0:T(128)S(1)} %pad_add_fusion.me_ref, bf16[64,2304]{1,0:T(8,128)(2,1)S(1)} %get-tuple-element.57.cw_ref, f32[24,4608]{1,0:T(8,128)S(1)} %get-tuple-element.35.cos_ref, f32[24,4608]{1,0:T(8,128)S(1)} %get-tuple-element.36.sin_ref, bf16[2,192,1152]{2,1,0:T(8,128)(2,1)S(1)} %get-tuple-element.58.rows_ref, ...), custom_call_target="tpu_custom_call" | custom-call | flops 905969664 | tf_op jit(solution)/shard_map/finish/pallas_call | solution.py:29
  (1 shorter events, 0.0 us)
Async XLA Ops:
  2.3 17.1 %collective-permute-start.1 = (bf16[32,4736]{1,0:T(8,128)(2,1)S(1)}, bf16[32,4736]{1,0:T(8,128)(2,1)S(1)}, u32[]{:S(2)}, u32[]{:S(2)}) collective-permute-start(bf16[32,4736]{1,0:T(8,128)(2,1)S(1)} %weigh.1.refs_0_.refs_2_), channel_id=1, source_target_pairs={{0,4},{4,0},{8,12},{12,8},{1,5},{5,1},{9,13},{13,9},{2,6},{6,2},{1... | collective-permute-start | bytes 909320 | tf_op jit(solution)/shard_map/ppermute | solution.py:541
  5.4 16.1 %collective-permute-start = (bf16[32,4736]{1,0:T(8,128)(2,1)S(1)}, bf16[32,4736]{1,0:T(8,128)(2,1)S(1)}, u32[]{:S(2)}, u32[]{:S(2)}) collective-permute-start(bf16[32,4736]{1,0:T(8,128)(2,1)S(1)} %weigh.1.refs_0_.refs_2_), channel_id=1, source_target_pairs={{0,8},{4,12},{8,0},{12,4},{1,9},{5,13},{9,1},{13,5},{2,10},{6,14},... | collective-permute-start | bytes 909320 | tf_op jit(solution)/shard_map/ppermute | solution.py:541
  8.7 10.8 %collective-permute-start.2 = (bf16[32,1152]{1,0:T(8,128)(2,1)S(1)}, bf16[32,1152]{1,0:T(8,128)(2,1)S(1)}, u32[]{:S(2)}, u32[]{:S(2)}) collective-permute-start(bf16[32,1152]{1,0:T(8,128)(2,1)S(1)} %get-tuple-element.32), channel_id=1, source_target_pairs={{0,3},{1,2},{2,1},{3,0},{4,7},{5,6},{6,5},{7,4},{8,11},{9,10},{10,... | collective-permute-start | bytes 221192 | tf_op jit(solution)/shard_map/ppermute | solution.py:541
  9.1 10.3 %collective-permute-start.3 = (bf16[32,1152]{1,0:T(8,128)(2,1)S(1)}, bf16[32,1152]{1,0:T(8,128)(2,1)S(1)}, u32[]{:S(2)}, u32[]{:S(2)}) collective-permute-start(bf16[32,1152]{1,0:T(8,128)(2,1)S(1)} %get-tuple-element.33), channel_id=1, source_target_pairs={{0,2},{1,3},{2,0},{3,1},{4,6},{5,7},{6,4},{7,5},{8,10},{9,11},{10,... | collective-permute-start | bytes 221192 | tf_op jit(solution)/shard_map/ppermute | solution.py:541
  11.4 0.7 %copy-start = (s32[24,2]{0,1:T(2,128)S(1)}, s32[24,2]{0,1:T(2,128)}, u32[]{:S(2)}) copy-start(s32[24,2]{0,1:T(2,128)} %param.11) | copy-start | bytes 580
  21.5 7.4 %collective-permute-start.4 = (bf16[32,4736]{1,0:T(8,128)(2,1)S(1)}, bf16[32,4736]{1,0:T(8,128)(2,1)S(1)}, u32[]{:S(2)}, u32[]{:S(2)}) collective-permute-start(bf16[32,4736]{1,0:T(8,128)(2,1)S(1)} %collective-permute-done.refs_4_.refs_2_), channel_id=1, source_target_pairs={{0,4},{4,0},{8,12},{12,8},{1,5},{5,1},{9,13},{13,9},{2,6},{6,2},{1... | collective-permute-start | bytes 909320 | tf_op jit(solution)/shard_map/ppermute | solution.py:541
  22.6 14.9 %collective-permute-start.9 = (bf16[64,1152]{1,0:T(8,128)(2,1)S(1)}, bf16[64,1152]{1,0:T(8,128)(2,1)S(1)}, u32[]{:S(2)}, u32[]{:S(2)}) collective-permute-start(bf16[64,1152]{1,0:T(8,128)(2,1)S(1)} %get-tuple-element.52), channel_id=1, source_target_pairs={{0,3},{1,2},{2,1},{3,0},{4,7},{5,6},{6,5},{7,4},{8,11},{9,10},{10,... | collective-permute-start | bytes 442376 | tf_op jit(solution)/shard_map/ppermute | solution.py:541
  22.6 14.8 %collective-permute-start.10 = (bf16[64,1152]{1,0:T(8,128)(2,1)S(1)}, bf16[64,1152]{1,0:T(8,128)(2,1)S(1)}, u32[]{:S(2)}, u32[]{:S(2)}) collective-permute-start(bf16[64,1152]{1,0:T(8,128)(2,1)S(1)} %get-tuple-element.54), channel_id=1, source_target_pairs={{0,2},{1,3},{2,0},{3,1},{4,6},{5,7},{6,4},{7,5},{8,10},{9,11},{10,... | collective-permute-start | bytes 442376 | tf_op jit(solution)/shard_map/ppermute | solution.py:541
  24.2 8.8 %collective-permute-start.5 = (bf16[96,1152]{1,0:T(8,128)(2,1)S(1)}, bf16[96,1152]{1,0:T(8,128)(2,1)S(1)}, u32[]{:S(2)}, u32[]{:S(2)}) collective-permute-start(bf16[96,1152]{1,0:T(8,128)(2,1)S(1)} %get-tuple-element.45), channel_id=1, source_target_pairs={{0,1},{1,0},{2,3},{3,2},{4,5},{5,4},{6,7},{7,6},{8,9},{9,8},{10,11... | collective-permute-start | bytes 663560 | tf_op jit(solution)/shard_map/ppermute | solution.py:541
  33.0 5.6 %collective-permute-start.8 = (f32[8,128]{1,0:T(8,128)S(1)}, f32[8,128]{1,0:T(8,128)S(1)}, u32[]{:S(2)}, u32[]{:S(2)}) collective-permute-start(f32[8,128]{1,0:T(8,128)S(1)} %get-tuple-element.46.refs_0_), channel_id=1, source_target_pairs={{0,12},{4,8},{8,4},{12,0},{1,13},{5,9},{9,5},{13,1},{2,14},{6,10},... | collective-permute-start | bytes 12296 | tf_op jit(solution)/shard_map/ppermute | solution.py:541
  35.0 4.5 %collective-permute-start.7 = (f32[8,128]{1,0:T(8,128)S(1)}, f32[8,128]{1,0:T(8,128)S(1)}, u32[]{:S(2)}, u32[]{:S(2)}) collective-permute-start(f32[8,128]{1,0:T(8,128)S(1)} %get-tuple-element.46.refs_0_), channel_id=1, source_target_pairs={{0,8},{4,12},{8,0},{12,4},{1,9},{5,13},{9,1},{13,5},{2,10},{6,14},... | collective-permute-start | bytes 12296 | tf_op jit(solution)/shard_map/ppermute | solution.py:541
  35.6 4.0 %collective-permute-start.6 = (f32[8,128]{1,0:T(8,128)S(1)}, f32[8,128]{1,0:T(8,128)S(1)}, u32[]{:S(2)}, u32[]{:S(2)}) collective-permute-start(f32[8,128]{1,0:T(8,128)S(1)} %get-tuple-element.46.refs_0_), channel_id=1, source_target_pairs={{0,4},{4,0},{8,12},{12,8},{1,5},{5,1},{9,13},{13,9},{2,6},{6,2},{1... | collective-permute-start | bytes 12296 | tf_op jit(solution)/shard_map/ppermute | solution.py:541
  37.5 10.1 %collective-permute-start.14 = (bf16[96,1152]{1,0:T(8,128)(2,1)S(1)}, bf16[96,1152]{1,0:T(8,128)(2,1)S(1)}, u32[]{:S(2)}, u32[]{:S(2)}) collective-permute-start(bf16[96,1152]{1,0:T(8,128)(2,1)S(1)} %bundle.1), channel_id=1, source_target_pairs={{0,4},{4,0},{8,12},{12,8},{1,5},{5,1},{9,13},{13,9},{2,6},{6,2},{1... | collective-permute-start | bytes 663560 | tf_op jit(solution)/shard_map/ppermute | solution.py:541
  40.0 5.2 %collective-permute-start.13 = (bf16[416,128]{1,0:T(8,128)(2,1)S(1)}, bf16[416,128]{1,0:T(8,128)(2,1)S(1)}, u32[]{:S(2)}, u32[]{:S(2)}) collective-permute-start(bf16[416,128]{1,0:T(8,128)(2,1)S(1)} %get-tuple-element.59.refs_0_), channel_id=1, source_target_pairs={{0,3},{1,2},{2,1},{3,0},{4,7},{5,6},{6,5},{7,4},{8,11},{9,10},{10,... | collective-permute-start | bytes 319496 | tf_op jit(solution)/shard_map/ppermute | solution.py:541
  40.0 7.5 %collective-permute-start.12 = (bf16[416,128]{1,0:T(8,128)(2,1)S(1)}, bf16[416,128]{1,0:T(8,128)(2,1)S(1)}, u32[]{:S(2)}, u32[]{:S(2)}) collective-permute-start(bf16[416,128]{1,0:T(8,128)(2,1)S(1)} %get-tuple-element.59.refs_0_), channel_id=1, source_target_pairs={{0,2},{1,3},{2,0},{3,1},{4,6},{5,7},{6,4},{7,5},{8,10},{9,11},{10,... | collective-permute-start | bytes 319496 | tf_op jit(solution)/shard_map/ppermute | solution.py:541
  41.6 6.0 %collective-permute-start.11 = (bf16[416,128]{1,0:T(8,128)(2,1)S(1)}, bf16[416,128]{1,0:T(8,128)(2,1)S(1)}, u32[]{:S(2)}, u32[]{:S(2)}) collective-permute-start(bf16[416,128]{1,0:T(8,128)(2,1)S(1)} %get-tuple-element.59.refs_0_), channel_id=1, source_target_pairs={{0,1},{1,0},{2,3},{3,2},{4,5},{5,4},{6,7},{7,6},{8,9},{9,8},{10,11... | collective-permute-start | bytes 319496 | tf_op jit(solution)/shard_map/ppermute | solution.py:541

commit v20 on v16

--- a/solution.py
+++ b/solution.py
@@ -44,37 +44,40 @@
 
 
 def weigh_kernel(ids_hbm, p_hbm, ctf_hbm, nw_hbm, *refs):
-    out_refs, (ids_ref, p_ref, ctf_ref, nw_ref, scale_ref, sem) = refs[:-6], refs[-6:]
+    out_refs, (ids_ref, p_ref, ctf_ref, nw_ref, raw_ref, scale_ref, sem) = refs[:-7], refs[-7:]
     count, _, freq = p_ref.shape
     copies = [
         pltpu.make_async_copy(source, target, sem.at[i])
         for i, (source, target) in enumerate(
-            [(ids_hbm, ids_ref), (ctf_hbm, ctf_ref), (nw_hbm, nw_ref), (p_hbm, p_ref)]
+            [(p_hbm, p_ref), (ids_hbm, ids_ref), (nw_hbm, nw_ref), (ctf_hbm, ctf_ref)]
         )
     ]
     for copy in copies:
         copy.start()
     copies[0].wait()
+    values = p_ref[...].astype(f32)
+    for part in range(2):
+        raw_ref[part] = values[:, part, :]
+    copies[1].wait()
     row = lax.rem(lax.broadcasted_iota(jnp.int32, (2 * count, LANES), 0), count)
     ids = jnp.zeros((2 * count, LANES), f32)
     for n in range(count):
         ids = jnp.where(row == n, ids_ref[n].astype(f32), ids)
-    for copy in copies[1:]:
-        copy.wait()
+    for out_ref in out_refs[:2]:
+        out_ref[:, out_ref.shape[1] - LANES :] = ids.astype(bf16)
+    copies[2].wait()
     noise = nw_ref[...].reshape(1, freq)
+    copies[3].wait()
     for n in range(count):
         scale_ref[n : n + 1, :] = ctf_ref[pl.ds(ids_ref[n], 1), :] * noise
     scale = scale_ref[...]
-    values = p_ref[...].astype(f32)
     chunk = freq // CHUNKS
     for part in range(2):
-        weighted = (values[:, part, :] * scale).astype(bf16)
+        weighted = (raw_ref[part] * scale).astype(bf16)
         here = slice(part * count, (part + 1) * count)
         out_refs[0][here, :freq] = weighted
         for c, out_ref in enumerate(out_refs[1:]):
             out_ref[here, :chunk] = weighted[:, c * chunk : (c + 1) * chunk]
-    for out_ref in out_refs[:2]:
-        out_ref[:, out_ref.shape[1] - LANES :] = ids.astype(bf16)
 
 
 def weigh(particles, ctf, noise_weight, group_ids):
@@ -94,6 +97,7 @@
             pltpu.VMEM(particles.shape, bf16),
             pltpu.VMEM(ctf.shape, f32),
             pltpu.VMEM((freq,), f32),
+            pltpu.VMEM((2, rows, freq), f32),
             pltpu.VMEM((rows, freq), f32),
             pltpu.SemaphoreType.DMA((4,)),
         ],

time: 50.3 us -> 50.2 us (level)
  no operation moved by 1% of the time
where the time goes in v20:
time: 50.2 us; the launch traced here: 50 us
  Pallas kernels  19.6 us (39%)
  starting transfers between devices  18.5 us (37%)
  waiting for transfers between devices  9.88 us (20%)
  local copies, waits for them, and re-layouts  1.13 us (2%)
  between operations  0.81 us (2%)
    ppermute x17, starting transfers between devices, swap(): return lax.ppermute(values, axis, [(i, i ^ distance) for i in range(size)])  18.5 us
    pallas_call x12, Pallas kernels, call(): pl.pallas_call(kernel, in_specs=in_specs, out_specs=[VMEM] * len(out_shap...  16.8 us
    ppermute x17, waiting for transfers between devices, swap(): return lax.ppermute(values, axis, [(i, i ^ distance) for i in range(size)])  9.88 us
    pallas_call x2, Pallas kernels, early_templates(): pl.pallas_call(early_kernel, grid=(count,), in_specs=[pl.BlockSpec((2, ro...  2.81 us
    unnamed x3, local copies, waits for them, and re-layouts  1.13 us
  transfers between devices with their start and end apart: 17, of which 5 were waited for; matrix products, arithmetic and copies ran while one was open for 2% of the time, Pallas kernels for 30%

profile of v20, /device:TPU:0, one launch (start us, length us, event | category | flops | bytes accessed | tf_op | source)
XLA Modules:
  0.0 50.0 jit_solution(13709405043029409898)
XLA Ops:
  0.6 1.6 %weigh.1 = (bf16[32,4736]{1,0:T(8,128)(2,1)S(1)}, bf16[32,2432]{1,0:T(8,128)(2,1)S(1)}, bf16[32,2304]{1,0:T(8,128)(2,1)S(1)}) custom-call(s32[16]{0:T(128)} %ids_hbm.1, bf16[16,2,4608]{2,1,0:T(2,128)(2,1)} %p_hbm.1, f32[64,4608]{1,0:T(8,128)} %ctf_hbm.3, f32[4608]{0:T(1024)} %nw_hbm.3), custom_call_target="tpu_custom_call" | custom-call | flops 294912 | bytes 1179648 | tf_op jit(solution)/shard_map/weigh/pallas_call | solution.py:30
  2.2 3.1 %collective-permute-start.2 = (bf16[32,4736]{1,0:T(8,128)(2,1)S(1)}, bf16[32,4736]{1,0:T(8,128)(2,1)S(1)}, u32[]{:S(2)}, u32[]{:S(2)}) collective-permute-start(bf16[32,4736]{1,0:T(8,128)(2,1)S(1)} %get-tuple-element.37.refs_0_.refs_4_), channel_id=1, source_target_pairs={{0,4},{4,0},{8,12},{12,8},{1,5},{5,1},{9,13},{13,9},{2,6},{6,2},{1... | collective-permute-start | bytes 909320 | tf_op jit(solution)/shard_map/ppermute | solution.py:616
  5.3 2.6 %collective-permute-start = (bf16[32,2432]{1,0:T(8,128)(2,1)S(1)}, bf16[32,2432]{1,0:T(8,128)(2,1)S(1)}, u32[]{:S(2)}, u32[]{:S(2)}) collective-permute-start(bf16[32,2432]{1,0:T(8,128)(2,1)S(1)} %get-tuple-element.35), channel_id=1, source_target_pairs={{0,8},{4,12},{8,0},{12,4},{1,9},{5,13},{9,1},{13,5},{2,10},{6,14},... | collective-permute-start | bytes 466952 | tf_op jit(solution)/shard_map/ppermute | solution.py:616
  7.9 0.3 collective-permute-start.1
  8.2 0.1 pad_add_fusion.me_ref
  8.3 0.6 %cut_slices.3 = (bf16[32,1152]{1,0:T(8,128)(2,1)S(1)}, bf16[32,1152]{1,0:T(8,128)(2,1)S(1)}, bf16[32,1152]{1,0:T(8,128)(2,1)S(1)}) custom-call(s32[2]{0:T(128)S(1)} %pad_add_fusion.me_ref, bf16[32,4736]{1,0:T(8,128)(2,1)S(1)} %get-tuple-element.37.refs_0_.refs_4_), custom_call_target="tpu_custom_call" | custom-call | bytes 442368 | tf_op jit(solution)/shard_map/cut_slices/pallas_call | solution.py:30
  8.9 0.2 collective-permute-start.3
  9.0 1.5 %collective-permute-start.4 = (bf16[32,1152]{1,0:T(8,128)(2,1)S(1)}, bf16[32,1152]{1,0:T(8,128)(2,1)S(1)}, u32[]{:S(2)}, u32[]{:S(2)}) collective-permute-start(bf16[32,1152]{1,0:T(8,128)(2,1)S(1)} %get-tuple-element.40), channel_id=1, source_target_pairs={{0,2},{1,3},{2,0},{3,1},{4,6},{5,7},{6,4},{7,5},{8,10},{9,11},{10,... | collective-permute-start | bytes 221192 | tf_op jit(solution)/shard_map/ppermute | solution.py:616
  10.5 1.1 %copy.10 = bf16[32,2,4608]{2,0,1:T(8,128)(2,1)S(1)} copy(bf16[32,2,4608]{2,1,0:T(2,128)(2,1)} %param.7) | data formatting | bytes 1179648 | tf_op args[1]
  11.7 3.1 %prepare.1 = (f32[24,4608]{1,0:T(8,128)S(1)}, f32[24,4608]{1,0:T(8,128)S(1)}, f32[32,64]{1,0:T(8,128)S(1)}, f32[64,4608]{1,0:T(8,128)S(1)}) custom-call(s32[2,24]{1,0:T(2,128)S(1)} %bitcast.11, bf16[2,32,4608]{2,1,0:T(8,128)(2,1)S(1)} %bitcast.7, f32[64,4608]{1,0:T(8,128)} %ctf_hbm.3, f32[4608]{0:T(1024)} %nw_hbm.3), custom_call_target="tpu_custom_call" | custom-call | flops 226492416 | tf_op jit(solution)/shard_map/prepare/pallas_call | solution.py:30
  14.8 0.7 %early_templates4.1.early_ref = bf16[2,768,768]{2,1,0:T(8,128)(2,1)S(1)} custom-call(bf16[2,32,4608]{2,1,0:T(8,128)(2,1)S(1)} %bitcast.8, f32[24,4608]{1,0:T(8,128)S(1)} %get-tuple-element.41.cos_ref, f32[24,4608]{1,0:T(8,128)S(1)} %get-tuple-element.42.sin_ref), custom_call_target="tpu_custom_call" | custom-call | flops 23592960 | bytes 2359296 | tf_op jit(solution)/shard_map/early_templates4/pallas_call | solution.py:206
  15.5 2.1 %early_templates6.1.temp_ref = bf16[6,768,768]{2,1,0:T(8,128)(2,1)S(1)} custom-call(bf16[2,32,4608]{2,1,0:T(8,128)(2,1)S(1)} %bitcast.9, f32[24,4608]{1,0:T(8,128)S(1)} %get-tuple-element.41.cos_ref, f32[24,4608]{1,0:T(8,128)S(1)} %get-tuple-element.42.sin_ref), custom_call_target="tpu_custom_call" | custom-call | flops 70778880 | bytes 7077888 | tf_op jit(solution)/shard_map/early_templates6/pallas_call | solution.py:206
  17.6 0.0 collective-permute-done.3.refs_2_
  17.6 0.0 collective-permute-done.4.refs_4_
  17.6 3.8 %collective-permute-done.1.refs_6_.refs_3_ = bf16[32,2304]{1,0:T(8,128)(2,1)S(1)} collective-permute-done((bf16[32,2304]{1,0:T(8,128)(2,1)S(1)}, bf16[32,2304]{1,0:T(8,128)(2,1)S(1)}, u32[]{:S(2)}, u32[]{:S(2)}) %collective-permute-start.1) | collective-permute-done | bytes 147488 | tf_op jit(solution)/shard_map/ppermute | solution.py:616
  21.4 0.0 collective-permute-done.refs_2_
  21.4 0.0 collective-permute-done.2.refs_1_.refs_5_
  21.4 0.5 collective-permute-start.5
  21.9 1.6 %collective-permute-start.6 = (bf16[32,2304]{1,0:T(8,128)(2,1)S(1)}, bf16[32,2304]{1,0:T(8,128)(2,1)S(1)}, u32[]{:S(2)}, u32[]{:S(2)}) collective-permute-start(bf16[32,2304]{1,0:T(8,128)(2,1)S(1)} %collective-permute-done.1.refs_6_.refs_3_), channel_id=1, source_target_pairs={{0,4},{4,0},{8,12},{12,8},{1,5},{5,1},{9,13},{13,9},{2,6},{6,2},{1... | collective-permute-start | bytes 442376 | tf_op jit(solution)/shard_map/ppermute | solution.py:616
  23.4 0.6 %cut_slices.4 = (bf16[64,1152]{1,0:T(8,128)(2,1)S(1)}, bf16[64,1152]{1,0:T(8,128)(2,1)S(1)}, bf16[64,1152]{1,0:T(8,128)(2,1)S(1)}, bf16[96,1152]{1,0:T(8,128)(2,1)S(1)}) custom-call(s32[2]{0:T(128)S(1)} %pad_add_fusion.me_ref, bf16[32,4736]{1,0:T(8,128)(2,1)S(1)} %get-tuple-element.37.refs_0_.refs_4_, ...), custom_call_target="tpu_custom_call" | custom-call | bytes 1327104 | tf_op jit(solution)/shard_map/cut_slices/pallas_call | solution.py:30
  24.1 0.1 collective-permute-start.7
  24.1 1.6 %collective-permute-start.11 = (bf16[64,1152]{1,0:T(8,128)(2,1)S(1)}, bf16[64,1152]{1,0:T(8,128)(2,1)S(1)}, u32[]{:S(2)}, u32[]{:S(2)}) collective-permute-start(bf16[64,1152]{1,0:T(8,128)(2,1)S(1)} %get-tuple-element.60), channel_id=1, source_target_pairs={{0,3},{1,2},{2,1},{3,0},{4,7},{5,6},{6,5},{7,4},{8,11},{9,10},{10,... | collective-permute-start | bytes 442376 | tf_op jit(solution)/shard_map/ppermute | solution.py:616
  25.7 0.5 %collective-permute-start.12 = (bf16[64,1152]{1,0:T(8,128)(2,1)S(1)}, bf16[64,1152]{1,0:T(8,128)(2,1)S(1)}, u32[]{:S(2)}, u32[]{:S(2)}) collective-permute-start(bf16[64,1152]{1,0:T(8,128)(2,1)S(1)} %get-tuple-element.62), channel_id=1, source_target_pairs={{0,2},{1,3},{2,0},{3,1},{4,6},{5,7},{6,4},{7,5},{8,10},{9,11},{10,... | collective-permute-start | bytes 442376 | tf_op jit(solution)/shard_map/ppermute | solution.py:616
  26.3 1.3 %templates.1.built_ref = bf16[4,768,768]{2,1,0:T(8,128)(2,1)S(1)} custom-call(bf16[2,32,4608]{2,1,0:T(8,128)(2,1)S(1)} %bitcast.10, f32[24,4608]{1,0:T(8,128)S(1)} %get-tuple-element.41.cos_ref, f32[24,4608]{1,0:T(8,128)S(1)} %get-tuple-element.42.sin_ref), custom_call_target="tpu_custom_call" | custom-call | flops 47185920 | tf_op jit(solution)/shard_map/templates/pallas_call | solution.py:30
  27.5 0.0 collective-permute-done.5.refs_3_.refs_0_
  27.5 2.0 %score0.1.acc_ref = f32[768,128]{1,0:T(8,128)S(1)} custom-call(bf16[4,768,768]{2,1,0:T(8,128)(2,1)S(1)} %templates.1.built_ref, bf16[2,768,768]{2,1,0:T(8,128)(2,1)S(1)} %early_templates4.1.early_ref, bf16[32,4736]{1,0:T(8,128)(2,1)S(1)} %get-tuple-element.37.refs_0_.refs_4_, bf16[32,4736]{1,0:T(8,128)(2,1)S(1)} %collective-permute-done.2.refs_1_.refs_5_, ...), custom_call_target="tpu_custom_call" | custom-call | flops 1811939328 | tf_op jit(solution)/shard_map/score0/pallas_call | solution.py:30
  29.5 0.0 collective-permute-done.6.refs_7_.refs_1_
  29.5 2.2 %score1.1 = (f32[768,128]{1,0:T(8,128)S(1)}, f32[128,64]{1,0:T(8,128)S(1)}, f32[8,128]{1,0:T(8,128)S(1)}) custom-call(bf16[6,768,768]{2,1,0:T(8,128)(2,1)S(1)} %early_templates6.1.temp_ref, f32[32,64]{1,0:T(8,128)S(1)} %get-tuple-element.44.pow_ref, f32[768,128]{1,0:T(8,128)S(1)} %score0.1.acc_ref, bf16[32,4736]{1,0:T(8,128)(2,1)S(1)} %get-tuple-element.37.refs_0_.refs_4_, ...), custom_call_target="tpu_custom_call" | custom-call | flops 1811939328 | tf_op jit(solution)/shard_map/score1/pallas_call | solution.py:30
  31.8 0.0 collective-permute-done.7.refs_6_.refs_2_
  31.8 2.6 %collective-permute-start.8 = (f32[8,128]{1,0:T(8,128)S(1)}, f32[8,128]{1,0:T(8,128)S(1)}, u32[]{:S(2)}, u32[]{:S(2)}) collective-permute-start(f32[8,128]{1,0:T(8,128)S(1)} %get-tuple-element.54.refs_0_), channel_id=1, source_target_pairs={{0,12},{4,8},{8,4},{12,0},{1,13},{5,9},{9,5},{13,1},{2,14},{6,10},... | collective-permute-start | bytes 12296 | tf_op jit(solution)/shard_map/ppermute | solution.py:616
  34.4 0.0 collective-permute-start.9
  34.4 1.8 %collective-permute-start.10 = (f32[8,128]{1,0:T(8,128)S(1)}, f32[8,128]{1,0:T(8,128)S(1)}, u32[]{:S(2)}, u32[]{:S(2)}) collective-permute-start(f32[8,128]{1,0:T(8,128)S(1)} %get-tuple-element.54.refs_0_), channel_id=1, source_target_pairs={{0,4},{4,0},{8,12},{12,8},{1,5},{5,1},{9,13},{13,9},{2,6},{6,2},{1... | collective-permute-start | bytes 12296 | tf_op jit(solution)/shard_map/ppermute | solution.py:616
  36.3 0.6 %cut_slices.5.refs_4_ = bf16[32,1152]{1,0:T(8,128)(2,1)S(1)} custom-call(s32[2]{0:T(128)S(1)} %pad_add_fusion.me_ref, bf16[32,2432]{1,0:T(8,128)(2,1)S(1)} %collective-permute-done.5.refs_3_.refs_0_, bf16[32,2304]{1,0:T(8,128)(2,1)S(1)} %collective-permute-done.6.refs_7_.refs_1_), custom_call_target="tpu_custom_call" | custom-call | bytes 147456 | tf_op jit(solution)/shard_map/cut_slices/pallas_call | solution.py:30
  36.8 0.0 collective-permute-done.12.refs_5_.refs_1_
  36.9 0.3 collective-permute-start.16
  37.1 0.1 collective-permute-done.8.refs_1_
  37.3 1.8 %collective-permute-done.9.refs_2_ = f32[8,128]{1,0:T(8,128)S(1)} collective-permute-done((f32[8,128]{1,0:T(8,128)S(1)}, f32[8,128]{1,0:T(8,128)S(1)}, u32[]{:S(2)}, u32[]{:S(2)}) %collective-permute-start.9) | collective-permute-done | bytes 4128 | tf_op jit(solution)/shard_map/ppermute | solution.py:616
  39.0 0.0 collective-permute-done.10.refs_3_
  39.0 0.5 responsibilities.1
  39.5 0.0 collective-permute-start.13
  39.6 1.5 %collective-permute-start.14 = (bf16[416,128]{1,0:T(8,128)(2,1)S(1)}, bf16[416,128]{1,0:T(8,128)(2,1)S(1)}, u32[]{:S(2)}, u32[]{:S(2)}) collective-permute-start(bf16[416,128]{1,0:T(8,128)(2,1)S(1)} %get-tuple-element.67.refs_0_), channel_id=1, source_target_pairs={{0,2},{1,3},{2,0},{3,1},{4,6},{5,7},{6,4},{7,5},{8,10},{9,11},{10,... | collective-permute-start | bytes 319496 | tf_op jit(solution)/shard_map/ppermute | solution.py:616
  41.1 0.3 collective-permute-start.15
  41.4 1.5 %gather_rows.1 = (f32[32,64]{1,0:T(8,128)}, bf16[64,2304]{1,0:T(8,128)(2,1)S(1)}, bf16[2,192,1152]{2,1,0:T(8,128)(2,1)S(1)}) custom-call(s32[2]{0:T(128)S(1)} %pad_add_fusion.me_ref, f32[768,128]{1,0:T(8,128)S(1)} %get-tuple-element.50.s_ref, f32[1,128]{1,0:T(1,128)S(1)} %get-tuple-element.55.norm_ref, f32[64,4608]{1,0:T(8,128)S(1)} %get-tuple-element.56.weight_ref, ...), custom_call_target="tpu_custom_call" | custom-call | flops 20000000000 | bytes 1769472 | tf_op jit(solution)/shard_map/gather_rows/pallas_call | solution.py:30
  42.9 1.9 %collective-permute-done.13.refs_1_ = bf16[416,128]{1,0:T(8,128)(2,1)S(1)} collective-permute-done((bf16[416,128]{1,0:T(8,128)(2,1)S(1)}, bf16[416,128]{1,0:T(8,128)(2,1)S(1)}, u32[]{:S(2)}, u32[]{:S(2)}) %collective-permute-start.13) | collective-permute-done | bytes 106528 | tf_op jit(solution)/shard_map/ppermute | solution.py:616
  44.8 2.3 %collective-permute-done.14.refs_2_ = bf16[416,128]{1,0:T(8,128)(2,1)S(1)} collective-permute-done((bf16[416,128]{1,0:T(8,128)(2,1)S(1)}, bf16[416,128]{1,0:T(8,128)(2,1)S(1)}, u32[]{:S(2)}, u32[]{:S(2)}) %collective-permute-start.14) | collective-permute-done | bytes 106528 | tf_op jit(solution)/shard_map/ppermute | solution.py:616
  47.1 0.0 collective-permute-done.15.refs_3_
  47.1 0.0 collective-permute-done.16.refs_5_
  47.1 2.9 %finish.1 = f32[32,2,1152]{2,1,0:T(2,128)} custom-call(s32[2]{0:T(128)S(1)} %pad_add_fusion.me_ref, bf16[64,2304]{1,0:T(8,128)(2,1)S(1)} %get-tuple-element.65.cw_ref, f32[24,4608]{1,0:T(8,128)S(1)} %get-tuple-element.41.cos_ref, f32[24,4608]{1,0:T(8,128)S(1)} %get-tuple-element.42.sin_ref, bf16[2,192,1152]{2,1,0:T(8,128)(2,1)S(1)} %get-tuple-element.66.rows_ref, ...), custom_call_target="tpu_custom_call" | custom-call | flops 905969664 | tf_op jit(solution)/shard_map/finish/pallas_call | solution.py:30
  (4 shorter events, 0.0 us)
Async XLA Ops:
  0.6 11.0 %copy-start = (s32[24,2]{0,1:T(2,128)S(1)}, s32[24,2]{0,1:T(2,128)}, u32[]{:S(2)}) copy-start(s32[24,2]{0,1:T(2,128)} %param.11) | copy-start | bytes 580
  2.2 19.2 %collective-permute-start.2 = (bf16[32,4736]{1,0:T(8,128)(2,1)S(1)}, bf16[32,4736]{1,0:T(8,128)(2,1)S(1)}, u32[]{:S(2)}, u32[]{:S(2)}) collective-permute-start(bf16[32,4736]{1,0:T(8,128)(2,1)S(1)} %get-tuple-element.37.refs_0_.refs_4_), channel_id=1, source_target_pairs={{0,4},{4,0},{8,12},{12,8},{1,5},{5,1},{9,13},{13,9},{2,6},{6,2},{1... | collective-permute-start | bytes 909320 | tf_op jit(solution)/shard_map/ppermute | solution.py:616
  5.3 16.1 %collective-permute-start = (bf16[32,2432]{1,0:T(8,128)(2,1)S(1)}, bf16[32,2432]{1,0:T(8,128)(2,1)S(1)}, u32[]{:S(2)}, u32[]{:S(2)}) collective-permute-start(bf16[32,2432]{1,0:T(8,128)(2,1)S(1)} %get-tuple-element.35), channel_id=1, source_target_pairs={{0,8},{4,12},{8,0},{12,4},{1,9},{5,13},{9,1},{13,5},{2,10},{6,14},... | collective-permute-start | bytes 466952 | tf_op jit(solution)/shard_map/ppermute | solution.py:616
  7.9 13.5 %collective-permute-start.1 = (bf16[32,2304]{1,0:T(8,128)(2,1)S(1)}, bf16[32,2304]{1,0:T(8,128)(2,1)S(1)}, u32[]{:S(2)}, u32[]{:S(2)}) collective-permute-start(bf16[32,2304]{1,0:T(8,128)(2,1)S(1)} %get-tuple-element.36), channel_id=1, source_target_pairs={{0,8},{4,12},{8,0},{12,4},{1,9},{5,13},{9,1},{13,5},{2,10},{6,14},... | collective-permute-start | bytes 442376 | tf_op jit(solution)/shard_map/ppermute | solution.py:616
  8.9 8.7 %collective-permute-start.3 = (bf16[32,1152]{1,0:T(8,128)(2,1)S(1)}, bf16[32,1152]{1,0:T(8,128)(2,1)S(1)}, u32[]{:S(2)}, u32[]{:S(2)}) collective-permute-start(bf16[32,1152]{1,0:T(8,128)(2,1)S(1)} %get-tuple-element.39), channel_id=1, source_target_pairs={{0,3},{1,2},{2,1},{3,0},{4,7},{5,6},{6,5},{7,4},{8,11},{9,10},{10,... | collective-permute-start | bytes 221192 | tf_op jit(solution)/shard_map/ppermute | solution.py:616
  9.0 8.6 %collective-permute-start.4 = (bf16[32,1152]{1,0:T(8,128)(2,1)S(1)}, bf16[32,1152]{1,0:T(8,128)(2,1)S(1)}, u32[]{:S(2)}, u32[]{:S(2)}) collective-permute-start(bf16[32,1152]{1,0:T(8,128)(2,1)S(1)} %get-tuple-element.40), channel_id=1, source_target_pairs={{0,2},{1,3},{2,0},{3,1},{4,6},{5,7},{6,4},{7,5},{8,10},{9,11},{10,... | collective-permute-start | bytes 221192 | tf_op jit(solution)/shard_map/ppermute | solution.py:616
  21.4 6.1 %collective-permute-start.5 = (bf16[32,2432]{1,0:T(8,128)(2,1)S(1)}, bf16[32,2432]{1,0:T(8,128)(2,1)S(1)}, u32[]{:S(2)}, u32[]{:S(2)}) collective-permute-start(bf16[32,2432]{1,0:T(8,128)(2,1)S(1)} %collective-permute-done.refs_2_), channel_id=1, source_target_pairs={{0,4},{4,0},{8,12},{12,8},{1,5},{5,1},{9,13},{13,9},{2,6},{6,2},{1... | collective-permute-start | bytes 466952 | tf_op jit(solution)/shard_map/ppermute | solution.py:616
  21.9 7.7 %collective-permute-start.6 = (bf16[32,2304]{1,0:T(8,128)(2,1)S(1)}, bf16[32,2304]{1,0:T(8,128)(2,1)S(1)}, u32[]{:S(2)}, u32[]{:S(2)}) collective-permute-start(bf16[32,2304]{1,0:T(8,128)(2,1)S(1)} %collective-permute-done.1.refs_6_.refs_3_), channel_id=1, source_target_pairs={{0,4},{4,0},{8,12},{12,8},{1,5},{5,1},{9,13},{13,9},{2,6},{6,2},{1... | collective-permute-start | bytes 442376 | tf_op jit(solution)/shard_map/ppermute | solution.py:616
  24.1 7.7 %collective-permute-start.7 = (bf16[96,1152]{1,0:T(8,128)(2,1)S(1)}, bf16[96,1152]{1,0:T(8,128)(2,1)S(1)}, u32[]{:S(2)}, u32[]{:S(2)}) collective-permute-start(bf16[96,1152]{1,0:T(8,128)(2,1)S(1)} %get-tuple-element.53), channel_id=1, source_target_pairs={{0,1},{1,0},{2,3},{3,2},{4,5},{5,4},{6,7},{7,6},{8,9},{9,8},{10,11... | collective-permute-start | bytes 663560 | tf_op jit(solution)/shard_map/ppermute | solution.py:616
  24.1 12.7 %collective-permute-start.11 = (bf16[64,1152]{1,0:T(8,128)(2,1)S(1)}, bf16[64,1152]{1,0:T(8,128)(2,1)S(1)}, u32[]{:S(2)}, u32[]{:S(2)}) collective-permute-start(bf16[64,1152]{1,0:T(8,128)(2,1)S(1)} %get-tuple-element.60), channel_id=1, source_target_pairs={{0,3},{1,2},{2,1},{3,0},{4,7},{5,6},{6,5},{7,4},{8,11},{9,10},{10,... | collective-permute-start | bytes 442376 | tf_op jit(solution)/shard_map/ppermute | solution.py:616
  25.7 11.1 %collective-permute-start.12 = (bf16[64,1152]{1,0:T(8,128)(2,1)S(1)}, bf16[64,1152]{1,0:T(8,128)(2,1)S(1)}, u32[]{:S(2)}, u32[]{:S(2)}) collective-permute-start(bf16[64,1152]{1,0:T(8,128)(2,1)S(1)} %get-tuple-element.62), channel_id=1, source_target_pairs={{0,2},{1,3},{2,0},{3,1},{4,6},{5,7},{6,4},{7,5},{8,10},{9,11},{10,... | collective-permute-start | bytes 442376 | tf_op jit(solution)/shard_map/ppermute | solution.py:616
  31.8 5.5 %collective-permute-start.8 = (f32[8,128]{1,0:T(8,128)S(1)}, f32[8,128]{1,0:T(8,128)S(1)}, u32[]{:S(2)}, u32[]{:S(2)}) collective-permute-start(f32[8,128]{1,0:T(8,128)S(1)} %get-tuple-element.54.refs_0_), channel_id=1, source_target_pairs={{0,12},{4,8},{8,4},{12,0},{1,13},{5,9},{9,5},{13,1},{2,14},{6,10},... | collective-permute-start | bytes 12296 | tf_op jit(solution)/shard_map/ppermute | solution.py:616
  34.4 4.6 %collective-permute-start.9 = (f32[8,128]{1,0:T(8,128)S(1)}, f32[8,128]{1,0:T(8,128)S(1)}, u32[]{:S(2)}, u32[]{:S(2)}) collective-permute-start(f32[8,128]{1,0:T(8,128)S(1)} %get-tuple-element.54.refs_0_), channel_id=1, source_target_pairs={{0,8},{4,12},{8,0},{12,4},{1,9},{5,13},{9,1},{13,5},{2,10},{6,14},... | collective-permute-start | bytes 12296 | tf_op jit(solution)/shard_map/ppermute | solution.py:616
  34.4 4.6 %collective-permute-start.10 = (f32[8,128]{1,0:T(8,128)S(1)}, f32[8,128]{1,0:T(8,128)S(1)}, u32[]{:S(2)}, u32[]{:S(2)}) collective-permute-start(f32[8,128]{1,0:T(8,128)S(1)} %get-tuple-element.54.refs_0_), channel_id=1, source_target_pairs={{0,4},{4,0},{8,12},{12,8},{1,5},{5,1},{9,13},{13,9},{2,6},{6,2},{1... | collective-permute-start | bytes 12296 | tf_op jit(solution)/shard_map/ppermute | solution.py:616
  36.9 10.2 %collective-permute-start.16 = (bf16[96,1152]{1,0:T(8,128)(2,1)S(1)}, bf16[96,1152]{1,0:T(8,128)(2,1)S(1)}, u32[]{:S(2)}, u32[]{:S(2)}) collective-permute-start(bf16[96,1152]{1,0:T(8,128)(2,1)S(1)} %bundle.1), channel_id=1, source_target_pairs={{0,4},{4,0},{8,12},{12,8},{1,5},{5,1},{9,13},{13,9},{2,6},{6,2},{1... | collective-permute-start | bytes 663560 | tf_op jit(solution)/shard_map/ppermute | solution.py:616
  39.5 5.2 %collective-permute-start.13 = (bf16[416,128]{1,0:T(8,128)(2,1)S(1)}, bf16[416,128]{1,0:T(8,128)(2,1)S(1)}, u32[]{:S(2)}, u32[]{:S(2)}) collective-permute-start(bf16[416,128]{1,0:T(8,128)(2,1)S(1)} %get-tuple-element.67.refs_0_), channel_id=1, source_target_pairs={{0,3},{1,2},{2,1},{3,0},{4,7},{5,6},{6,5},{7,4},{8,11},{9,10},{10,... | collective-permute-start | bytes 319496 | tf_op jit(solution)/shard_map/ppermute | solution.py:616
  39.6 7.5 %collective-permute-start.14 = (bf16[416,128]{1,0:T(8,128)(2,1)S(1)}, bf16[416,128]{1,0:T(8,128)(2,1)S(1)}, u32[]{:S(2)}, u32[]{:S(2)}) collective-permute-start(bf16[416,128]{1,0:T(8,128)(2,1)S(1)} %get-tuple-element.67.refs_0_), channel_id=1, source_target_pairs={{0,2},{1,3},{2,0},{3,1},{4,6},{5,7},{6,4},{7,5},{8,10},{9,11},{10,... | collective-permute-start | bytes 319496 | tf_op jit(solution)/shard_map/ppermute | solution.py:616
  41.1 6.0 %collective-permute-start.15 = (bf16[416,128]{1,0:T(8,128)(2,1)S(1)}, bf16[416,128]{1,0:T(8,128)(2,1)S(1)}, u32[]{:S(2)}, u32[]{:S(2)}) collective-permute-start(bf16[416,128]{1,0:T(8,128)(2,1)S(1)} %get-tuple-element.67.refs_0_), channel_id=1, source_target_pairs={{0,1},{1,0},{2,3},{3,2},{4,5},{5,4},{6,7},{7,6},{8,9},{9,8},{10,11... | collective-permute-start | bytes 319496 | tf_op jit(solution)/shard_map/ppermute | solution.py:616

commit v21 on v20

--- a/solution.py
+++ b/solution.py
@@ -652,9 +652,11 @@
         far, near, slices, split, early = lax.optimization_barrier(
             (far, near, slices, split, early)
         )
-        third = [swap(w, "cls", 1) for w in far]
+        third = [swap(far[0], "cls", 1)]
         targets = [(d, 1) for d in (0,) + others[:-1]] + [(others[-1], 0)]
         mine, *outgoing = cut_slices(me, [[own], [near], far], targets, span, freq)
+        rest, mine = lax.optimization_barrier((far[1], mine))
+        third.append(swap(rest, "cls", 1))
         arrived = [mine] + [swap(w, "img", d) for w, d in zip(outgoing, others)]
         shards = [[own], [near], far, third]
     scores, marks, stat = score(early, split, cos_t, sin_t, power, shards, half)

time: 50.2 us -> 50.2 us (level)
  no operation moved by 1% of the time
where the time goes in v21:
time: 50.2 us; the launch traced here: 50 us
  Pallas kernels  19.6 us (39%)
  starting transfers between devices  18.5 us (37%)
  waiting for transfers between devices  9.88 us (20%)
  local copies, waits for them, and re-layouts  1.13 us (2%)
  between operations  0.8 us (2%)
    ppermute x17, starting transfers between devices, swap(): return lax.ppermute(values, axis, [(i, i ^ distance) for i in range(size)])  18.5 us
    pallas_call x12, Pallas kernels, call(): pl.pallas_call(kernel, in_specs=in_specs, out_specs=[VMEM] * len(out_shap...  16.8 us
    ppermute x17, waiting for transfers between devices, swap(): return lax.ppermute(values, axis, [(i, i ^ distance) for i in range(size)])  9.88 us
    pallas_call x2, Pallas kernels, early_templates(): pl.pallas_call(early_kernel, grid=(count,), in_specs=[pl.BlockSpec((2, ro...  2.81 us
    unnamed x3, local copies, waits for them, and re-layouts  1.13 us
  transfers between devices with their start and end apart: 17, of which 5 were waited for; matrix products, arithmetic and copies ran while one was open for 2% of the time, Pallas kernels for 30%

profile of v21, /device:TPU:0, one launch (start us, length us, event | category | flops | bytes accessed | tf_op | source)
XLA Modules:
  0.0 50.0 jit_solution(10797989828291844615)
XLA Ops:
  0.6 1.6 %weigh.1 = (bf16[32,4736]{1,0:T(8,128)(2,1)S(1)}, bf16[32,2432]{1,0:T(8,128)(2,1)S(1)}, bf16[32,2304]{1,0:T(8,128)(2,1)S(1)}) custom-call(s32[16]{0:T(128)} %ids_hbm.1, bf16[16,2,4608]{2,1,0:T(2,128)(2,1)} %p_hbm.1, f32[64,4608]{1,0:T(8,128)} %ctf_hbm.3, f32[4608]{0:T(1024)} %nw_hbm.3), custom_call_target="tpu_custom_call" | custom-call | flops 294912 | bytes 1179648 | tf_op jit(solution)/shard_map/weigh/pallas_call | solution.py:30
  2.2 3.1 %collective-permute-start.2 = (bf16[32,4736]{1,0:T(8,128)(2,1)S(1)}, bf16[32,4736]{1,0:T(8,128)(2,1)S(1)}, u32[]{:S(2)}, u32[]{:S(2)}) collective-permute-start(bf16[32,4736]{1,0:T(8,128)(2,1)S(1)} %get-tuple-element.39.refs_0_.refs_4_), channel_id=1, source_target_pairs={{0,4},{4,0},{8,12},{12,8},{1,5},{5,1},{9,13},{13,9},{2,6},{6,2},{1... | collective-permute-start | bytes 909320 | tf_op jit(solution)/shard_map/ppermute | solution.py:616
  5.3 2.6 %collective-permute-start = (bf16[32,2432]{1,0:T(8,128)(2,1)S(1)}, bf16[32,2432]{1,0:T(8,128)(2,1)S(1)}, u32[]{:S(2)}, u32[]{:S(2)}) collective-permute-start(bf16[32,2432]{1,0:T(8,128)(2,1)S(1)} %get-tuple-element.37), channel_id=1, source_target_pairs={{0,8},{4,12},{8,0},{12,4},{1,9},{5,13},{9,1},{13,5},{2,10},{6,14},... | collective-permute-start | bytes 466952 | tf_op jit(solution)/shard_map/ppermute | solution.py:616
  7.9 0.3 collective-permute-start.1
  8.2 0.1 pad_add_fusion.me_ref
  8.3 0.6 %cut_slices.3 = (bf16[32,1152]{1,0:T(8,128)(2,1)S(1)}, bf16[32,1152]{1,0:T(8,128)(2,1)S(1)}, bf16[32,1152]{1,0:T(8,128)(2,1)S(1)}) custom-call(s32[2]{0:T(128)S(1)} %pad_add_fusion.me_ref, bf16[32,4736]{1,0:T(8,128)(2,1)S(1)} %get-tuple-element.39.refs_0_.refs_4_), custom_call_target="tpu_custom_call" | custom-call | bytes 442368 | tf_op jit(solution)/shard_map/cut_slices/pallas_call | solution.py:30
  8.9 0.2 collective-permute-start.3
  9.0 1.5 %collective-permute-start.4 = (bf16[32,1152]{1,0:T(8,128)(2,1)S(1)}, bf16[32,1152]{1,0:T(8,128)(2,1)S(1)}, u32[]{:S(2)}, u32[]{:S(2)}) collective-permute-start(bf16[32,1152]{1,0:T(8,128)(2,1)S(1)} %get-tuple-element.42), channel_id=1, source_target_pairs={{0,2},{1,3},{2,0},{3,1},{4,6},{5,7},{6,4},{7,5},{8,10},{9,11},{10,... | collective-permute-start | bytes 221192 | tf_op jit(solution)/shard_map/ppermute | solution.py:616
  10.5 1.1 %copy.10 = bf16[32,2,4608]{2,0,1:T(8,128)(2,1)S(1)} copy(bf16[32,2,4608]{2,1,0:T(2,128)(2,1)} %param.7) | data formatting | bytes 1179648 | tf_op args[1]
  11.7 3.1 %prepare.1 = (f32[24,4608]{1,0:T(8,128)S(1)}, f32[24,4608]{1,0:T(8,128)S(1)}, f32[32,64]{1,0:T(8,128)S(1)}, f32[64,4608]{1,0:T(8,128)S(1)}) custom-call(s32[2,24]{1,0:T(2,128)S(1)} %bitcast.11, bf16[2,32,4608]{2,1,0:T(8,128)(2,1)S(1)} %bitcast.7, f32[64,4608]{1,0:T(8,128)} %ctf_hbm.3, f32[4608]{0:T(1024)} %nw_hbm.3), custom_call_target="tpu_custom_call" | custom-call | flops 226492416 | tf_op jit(solution)/shard_map/prepare/pallas_call | solution.py:30
  14.8 0.7 %early_templates4.1.early_ref = bf16[2,768,768]{2,1,0:T(8,128)(2,1)S(1)} custom-call(bf16[2,32,4608]{2,1,0:T(8,128)(2,1)S(1)} %bitcast.8, f32[24,4608]{1,0:T(8,128)S(1)} %get-tuple-element.43.cos_ref, f32[24,4608]{1,0:T(8,128)S(1)} %get-tuple-element.44.sin_ref), custom_call_target="tpu_custom_call" | custom-call | flops 23592960 | bytes 2359296 | tf_op jit(solution)/shard_map/early_templates4/pallas_call | solution.py:206
  15.5 2.1 %early_templates6.1.temp_ref = bf16[6,768,768]{2,1,0:T(8,128)(2,1)S(1)} custom-call(bf16[2,32,4608]{2,1,0:T(8,128)(2,1)S(1)} %bitcast.9, f32[24,4608]{1,0:T(8,128)S(1)} %get-tuple-element.43.cos_ref, f32[24,4608]{1,0:T(8,128)S(1)} %get-tuple-element.44.sin_ref), custom_call_target="tpu_custom_call" | custom-call | flops 70778880 | bytes 7077888 | tf_op jit(solution)/shard_map/early_templates6/pallas_call | solution.py:206
  17.6 0.0 collective-permute-done.3.refs_2_
  17.6 0.0 collective-permute-done.4.refs_4_
  17.6 3.8 %collective-permute-done.1.refs_3_.refs_6_ = bf16[32,2304]{1,0:T(8,128)(2,1)S(1)} collective-permute-done((bf16[32,2304]{1,0:T(8,128)(2,1)S(1)}, bf16[32,2304]{1,0:T(8,128)(2,1)S(1)}, u32[]{:S(2)}, u32[]{:S(2)}) %collective-permute-start.1) | collective-permute-done | bytes 147488 | tf_op jit(solution)/shard_map/ppermute | solution.py:616
  21.4 0.0 collective-permute-done.refs_2_
  21.4 0.0 collective-permute-done.2.refs_1_.refs_5_
  21.4 0.5 collective-permute-start.5
  21.9 0.6 %cut_slices.4 = (bf16[64,1152]{1,0:T(8,128)(2,1)S(1)}, bf16[64,1152]{1,0:T(8,128)(2,1)S(1)}, bf16[64,1152]{1,0:T(8,128)(2,1)S(1)}, bf16[96,1152]{1,0:T(8,128)(2,1)S(1)}) custom-call(s32[2]{0:T(128)S(1)} %pad_add_fusion.me_ref, bf16[32,4736]{1,0:T(8,128)(2,1)S(1)} %get-tuple-element.39.refs_0_.refs_4_, ...), custom_call_target="tpu_custom_call" | custom-call | bytes 1327104 | tf_op jit(solution)/shard_map/cut_slices/pallas_call | solution.py:30
  22.5 1.6 %collective-permute-start.6 = (bf16[32,2304]{1,0:T(8,128)(2,1)S(1)}, bf16[32,2304]{1,0:T(8,128)(2,1)S(1)}, u32[]{:S(2)}, u32[]{:S(2)}) collective-permute-start(bf16[32,2304]{1,0:T(8,128)(2,1)S(1)} %collective-permute-done.1.refs_3_.refs_6_), channel_id=1, source_target_pairs={{0,4},{4,0},{8,12},{12,8},{1,5},{5,1},{9,13},{13,9},{2,6},{6,2},{1... | collective-permute-start | bytes 442376 | tf_op jit(solution)/shard_map/ppermute | solution.py:616
  24.1 0.0 collective-permute-start.7
  24.1 1.6 %collective-permute-start.11 = (bf16[64,1152]{1,0:T(8,128)(2,1)S(1)}, bf16[64,1152]{1,0:T(8,128)(2,1)S(1)}, u32[]{:S(2)}, u32[]{:S(2)}) collective-permute-start(bf16[64,1152]{1,0:T(8,128)(2,1)S(1)} %get-tuple-element.64), channel_id=1, source_target_pairs={{0,3},{1,2},{2,1},{3,0},{4,7},{5,6},{6,5},{7,4},{8,11},{9,10},{10,... | collective-permute-start | bytes 442376 | tf_op jit(solution)/shard_map/ppermute | solution.py:616
  25.7 0.5 %collective-permute-start.12 = (bf16[64,1152]{1,0:T(8,128)(2,1)S(1)}, bf16[64,1152]{1,0:T(8,128)(2,1)S(1)}, u32[]{:S(2)}, u32[]{:S(2)}) collective-permute-start(bf16[64,1152]{1,0:T(8,128)(2,1)S(1)} %get-tuple-element.66), channel_id=1, source_target_pairs={{0,2},{1,3},{2,0},{3,1},{4,6},{5,7},{6,4},{7,5},{8,10},{9,11},{10,... | collective-permute-start | bytes 442376 | tf_op jit(solution)/shard_map/ppermute | solution.py:616
  26.3 1.3 %templates.1.built_ref = bf16[4,768,768]{2,1,0:T(8,128)(2,1)S(1)} custom-call(bf16[2,32,4608]{2,1,0:T(8,128)(2,1)S(1)} %bitcast.10, f32[24,4608]{1,0:T(8,128)S(1)} %get-tuple-element.43.cos_ref, f32[24,4608]{1,0:T(8,128)S(1)} %get-tuple-element.44.sin_ref), custom_call_target="tpu_custom_call" | custom-call | flops 47185920 | tf_op jit(solution)/shard_map/templates/pallas_call | solution.py:30
  27.5 0.0 collective-permute-done.5.refs_3_.refs_0_
  27.5 2.0 %score0.1.acc_ref = f32[768,128]{1,0:T(8,128)S(1)} custom-call(bf16[4,768,768]{2,1,0:T(8,128)(2,1)S(1)} %templates.1.built_ref, bf16[2,768,768]{2,1,0:T(8,128)(2,1)S(1)} %early_templates4.1.early_ref, bf16[32,4736]{1,0:T(8,128)(2,1)S(1)} %get-tuple-element.39.refs_0_.refs_4_, bf16[32,4736]{1,0:T(8,128)(2,1)S(1)} %collective-permute-done.2.refs_1_.refs_5_, ...), custom_call_target="tpu_custom_call" | custom-call | flops 1811939328 | tf_op jit(solution)/shard_map/score0/pallas_call | solution.py:30
  29.5 0.0 collective-permute-done.6.refs_7_.refs_1_
  29.5 2.2 %score1.1 = (f32[768,128]{1,0:T(8,128)S(1)}, f32[128,64]{1,0:T(8,128)S(1)}, f32[8,128]{1,0:T(8,128)S(1)}) custom-call(bf16[6,768,768]{2,1,0:T(8,128)(2,1)S(1)} %early_templates6.1.temp_ref, f32[32,64]{1,0:T(8,128)S(1)} %get-tuple-element.46.pow_ref, f32[768,128]{1,0:T(8,128)S(1)} %score0.1.acc_ref, bf16[32,4736]{1,0:T(8,128)(2,1)S(1)} %get-tuple-element.39.refs_0_.refs_4_, ...), custom_call_target="tpu_custom_call" | custom-call | flops 1811939328 | tf_op jit(solution)/shard_map/score1/pallas_call | solution.py:30
  31.8 0.0 collective-permute-done.7.refs_6_.refs_2_
  31.8 2.6 %collective-permute-start.8 = (f32[8,128]{1,0:T(8,128)S(1)}, f32[8,128]{1,0:T(8,128)S(1)}, u32[]{:S(2)}, u32[]{:S(2)}) collective-permute-start(f32[8,128]{1,0:T(8,128)S(1)} %get-tuple-element.58.refs_0_), channel_id=1, source_target_pairs={{0,12},{4,8},{8,4},{12,0},{1,13},{5,9},{9,5},{13,1},{2,14},{6,10},... | collective-permute-start | bytes 12296 | tf_op jit(solution)/shard_map/ppermute | solution.py:616
  34.4 0.0 collective-permute-start.9
  34.4 1.8 %collective-permute-start.10 = (f32[8,128]{1,0:T(8,128)S(1)}, f32[8,128]{1,0:T(8,128)S(1)}, u32[]{:S(2)}, u32[]{:S(2)}) collective-permute-start(f32[8,128]{1,0:T(8,128)S(1)} %get-tuple-element.58.refs_0_), channel_id=1, source_target_pairs={{0,4},{4,0},{8,12},{12,8},{1,5},{5,1},{9,13},{13,9},{2,6},{6,2},{1... | collective-permute-start | bytes 12296 | tf_op jit(solution)/shard_map/ppermute | solution.py:616
  36.2 0.6 %cut_slices.5.refs_4_ = bf16[32,1152]{1,0:T(8,128)(2,1)S(1)} custom-call(s32[2]{0:T(128)S(1)} %pad_add_fusion.me_ref, bf16[32,2432]{1,0:T(8,128)(2,1)S(1)} %collective-permute-done.5.refs_3_.refs_0_, bf16[32,2304]{1,0:T(8,128)(2,1)S(1)} %collective-permute-done.6.refs_7_.refs_1_), custom_call_target="tpu_custom_call" | custom-call | bytes 147456 | tf_op jit(solution)/shard_map/cut_slices/pallas_call | solution.py:30
  36.8 0.0 collective-permute-done.11.refs_3_.refs_0_
  36.8 0.0 collective-permute-done.12.refs_5_.refs_1_
  36.9 0.3 collective-permute-start.16
  37.1 0.1 collective-permute-done.8.refs_1_
  37.3 1.8 %collective-permute-done.9.refs_2_ = f32[8,128]{1,0:T(8,128)S(1)} collective-permute-done((f32[8,128]{1,0:T(8,128)S(1)}, f32[8,128]{1,0:T(8,128)S(1)}, u32[]{:S(2)}, u32[]{:S(2)}) %collective-permute-start.9) | collective-permute-done | bytes 4128 | tf_op jit(solution)/shard_map/ppermute | solution.py:616
  39.0 0.0 collective-permute-done.10.refs_3_
  39.0 0.5 responsibilities.1
  39.5 0.0 collective-permute-start.13
  39.5 1.6 %collective-permute-start.14 = (bf16[416,128]{1,0:T(8,128)(2,1)S(1)}, bf16[416,128]{1,0:T(8,128)(2,1)S(1)}, u32[]{:S(2)}, u32[]{:S(2)}) collective-permute-start(bf16[416,128]{1,0:T(8,128)(2,1)S(1)} %get-tuple-element.71.refs_0_), channel_id=1, source_target_pairs={{0,2},{1,3},{2,0},{3,1},{4,6},{5,7},{6,4},{7,5},{8,10},{9,11},{10,... | collective-permute-start | bytes 319496 | tf_op jit(solution)/shard_map/ppermute | solution.py:616
  41.1 0.3 collective-permute-start.15
  41.4 1.5 %gather_rows.1 = (f32[32,64]{1,0:T(8,128)}, bf16[64,2304]{1,0:T(8,128)(2,1)S(1)}, bf16[2,192,1152]{2,1,0:T(8,128)(2,1)S(1)}) custom-call(s32[2]{0:T(128)S(1)} %pad_add_fusion.me_ref, f32[768,128]{1,0:T(8,128)S(1)} %get-tuple-element.54.s_ref, f32[1,128]{1,0:T(1,128)S(1)} %get-tuple-element.59.norm_ref, f32[64,4608]{1,0:T(8,128)S(1)} %get-tuple-element.60.weight_ref, ...), custom_call_target="tpu_custom_call" | custom-call | flops 20000000000 | bytes 1769472 | tf_op jit(solution)/shard_map/gather_rows/pallas_call | solution.py:30
  42.9 1.8 %collective-permute-done.13.refs_1_ = bf16[416,128]{1,0:T(8,128)(2,1)S(1)} collective-permute-done((bf16[416,128]{1,0:T(8,128)(2,1)S(1)}, bf16[416,128]{1,0:T(8,128)(2,1)S(1)}, u32[]{:S(2)}, u32[]{:S(2)}) %collective-permute-start.13) | collective-permute-done | bytes 106528 | tf_op jit(solution)/shard_map/ppermute | solution.py:616
  44.7 2.3 %collective-permute-done.14.refs_2_ = bf16[416,128]{1,0:T(8,128)(2,1)S(1)} collective-permute-done((bf16[416,128]{1,0:T(8,128)(2,1)S(1)}, bf16[416,128]{1,0:T(8,128)(2,1)S(1)}, u32[]{:S(2)}, u32[]{:S(2)}) %collective-permute-start.14) | collective-permute-done | bytes 106528 | tf_op jit(solution)/shard_map/ppermute | solution.py:616
  47.1 0.0 collective-permute-done.15.refs_3_
  47.1 2.9 %finish.1 = f32[32,2,1152]{2,1,0:T(2,128)} custom-call(s32[2]{0:T(128)S(1)} %pad_add_fusion.me_ref, bf16[64,2304]{1,0:T(8,128)(2,1)S(1)} %get-tuple-element.69.cw_ref, f32[24,4608]{1,0:T(8,128)S(1)} %get-tuple-element.43.cos_ref, f32[24,4608]{1,0:T(8,128)S(1)} %get-tuple-element.44.sin_ref, bf16[2,192,1152]{2,1,0:T(8,128)(2,1)S(1)} %get-tuple-element.70.rows_ref, ...), custom_call_target="tpu_custom_call" | custom-call | flops 905969664 | tf_op jit(solution)/shard_map/finish/pallas_call | solution.py:30
  (4 shorter events, 0.0 us)
Async XLA Ops:
  0.6 11.0 %copy-start = (s32[24,2]{0,1:T(2,128)S(1)}, s32[24,2]{0,1:T(2,128)}, u32[]{:S(2)}) copy-start(s32[24,2]{0,1:T(2,128)} %param.11) | copy-start | bytes 580
  2.2 19.2 %collective-permute-start.2 = (bf16[32,4736]{1,0:T(8,128)(2,1)S(1)}, bf16[32,4736]{1,0:T(8,128)(2,1)S(1)}, u32[]{:S(2)}, u32[]{:S(2)}) collective-permute-start(bf16[32,4736]{1,0:T(8,128)(2,1)S(1)} %get-tuple-element.39.refs_0_.refs_4_), channel_id=1, source_target_pairs={{0,4},{4,0},{8,12},{12,8},{1,5},{5,1},{9,13},{13,9},{2,6},{6,2},{1... | collective-permute-start | bytes 909320 | tf_op jit(solution)/shard_map/ppermute | solution.py:616
  5.3 16.1 %collective-permute-start = (bf16[32,2432]{1,0:T(8,128)(2,1)S(1)}, bf16[32,2432]{1,0:T(8,128)(2,1)S(1)}, u32[]{:S(2)}, u32[]{:S(2)}) collective-permute-start(bf16[32,2432]{1,0:T(8,128)(2,1)S(1)} %get-tuple-element.37), channel_id=1, source_target_pairs={{0,8},{4,12},{8,0},{12,4},{1,9},{5,13},{9,1},{13,5},{2,10},{6,14},... | collective-permute-start | bytes 466952 | tf_op jit(solution)/shard_map/ppermute | solution.py:616
  7.9 13.5 %collective-permute-start.1 = (bf16[32,2304]{1,0:T(8,128)(2,1)S(1)}, bf16[32,2304]{1,0:T(8,128)(2,1)S(1)}, u32[]{:S(2)}, u32[]{:S(2)}) collective-permute-start(bf16[32,2304]{1,0:T(8,128)(2,1)S(1)} %get-tuple-element.38), channel_id=1, source_target_pairs={{0,8},{4,12},{8,0},{12,4},{1,9},{5,13},{9,1},{13,5},{2,10},{6,14},... | collective-permute-start | bytes 442376 | tf_op jit(solution)/shard_map/ppermute | solution.py:616
  8.9 8.7 %collective-permute-start.3 = (bf16[32,1152]{1,0:T(8,128)(2,1)S(1)}, bf16[32,1152]{1,0:T(8,128)(2,1)S(1)}, u32[]{:S(2)}, u32[]{:S(2)}) collective-permute-start(bf16[32,1152]{1,0:T(8,128)(2,1)S(1)} %get-tuple-element.41), channel_id=1, source_target_pairs={{0,3},{1,2},{2,1},{3,0},{4,7},{5,6},{6,5},{7,4},{8,11},{9,10},{10,... | collective-permute-start | bytes 221192 | tf_op jit(solution)/shard_map/ppermute | solution.py:616
  9.0 8.6 %collective-permute-start.4 = (bf16[32,1152]{1,0:T(8,128)(2,1)S(1)}, bf16[32,1152]{1,0:T(8,128)(2,1)S(1)}, u32[]{:S(2)}, u32[]{:S(2)}) collective-permute-start(bf16[32,1152]{1,0:T(8,128)(2,1)S(1)} %get-tuple-element.42), channel_id=1, source_target_pairs={{0,2},{1,3},{2,0},{3,1},{4,6},{5,7},{6,4},{7,5},{8,10},{9,11},{10,... | collective-permute-start | bytes 221192 | tf_op jit(solution)/shard_map/ppermute | solution.py:616
  21.4 6.1 %collective-permute-start.5 = (bf16[32,2432]{1,0:T(8,128)(2,1)S(1)}, bf16[32,2432]{1,0:T(8,128)(2,1)S(1)}, u32[]{:S(2)}, u32[]{:S(2)}) collective-permute-start(bf16[32,2432]{1,0:T(8,128)(2,1)S(1)} %collective-permute-done.refs_2_), channel_id=1, source_target_pairs={{0,4},{4,0},{8,12},{12,8},{1,5},{5,1},{9,13},{13,9},{2,6},{6,2},{1... | collective-permute-start | bytes 466952 | tf_op jit(solution)/shard_map/ppermute | solution.py:616
  22.5 7.0 %collective-permute-start.6 = (bf16[32,2304]{1,0:T(8,128)(2,1)S(1)}, bf16[32,2304]{1,0:T(8,128)(2,1)S(1)}, u32[]{:S(2)}, u32[]{:S(2)}) collective-permute-start(bf16[32,2304]{1,0:T(8,128)(2,1)S(1)} %collective-permute-done.1.refs_3_.refs_6_), channel_id=1, source_target_pairs={{0,4},{4,0},{8,12},{12,8},{1,5},{5,1},{9,13},{13,9},{2,6},{6,2},{1... | collective-permute-start | bytes 442376 | tf_op jit(solution)/shard_map/ppermute | solution.py:616
  24.1 7.7 %collective-permute-start.7 = (bf16[96,1152]{1,0:T(8,128)(2,1)S(1)}, bf16[96,1152]{1,0:T(8,128)(2,1)S(1)}, u32[]{:S(2)}, u32[]{:S(2)}) collective-permute-start(bf16[96,1152]{1,0:T(8,128)(2,1)S(1)} %get-tuple-element.57), channel_id=1, source_target_pairs={{0,1},{1,0},{2,3},{3,2},{4,5},{5,4},{6,7},{7,6},{8,9},{9,8},{10,11... | collective-permute-start | bytes 663560 | tf_op jit(solution)/shard_map/ppermute | solution.py:616
  24.1 12.7 %collective-permute-start.11 = (bf16[64,1152]{1,0:T(8,128)(2,1)S(1)}, bf16[64,1152]{1,0:T(8,128)(2,1)S(1)}, u32[]{:S(2)}, u32[]{:S(2)}) collective-permute-start(bf16[64,1152]{1,0:T(8,128)(2,1)S(1)} %get-tuple-element.64), channel_id=1, source_target_pairs={{0,3},{1,2},{2,1},{3,0},{4,7},{5,6},{6,5},{7,4},{8,11},{9,10},{10,... | collective-permute-start | bytes 442376 | tf_op jit(solution)/shard_map/ppermute | solution.py:616
  25.7 11.1 %collective-permute-start.12 = (bf16[64,1152]{1,0:T(8,128)(2,1)S(1)}, bf16[64,1152]{1,0:T(8,128)(2,1)S(1)}, u32[]{:S(2)}, u32[]{:S(2)}) collective-permute-start(bf16[64,1152]{1,0:T(8,128)(2,1)S(1)} %get-tuple-element.66), channel_id=1, source_target_pairs={{0,2},{1,3},{2,0},{3,1},{4,6},{5,7},{6,4},{7,5},{8,10},{9,11},{10,... | collective-permute-start | bytes 442376 | tf_op jit(solution)/shard_map/ppermute | solution.py:616
  31.8 5.5 %collective-permute-start.8 = (f32[8,128]{1,0:T(8,128)S(1)}, f32[8,128]{1,0:T(8,128)S(1)}, u32[]{:S(2)}, u32[]{:S(2)}) collective-permute-start(f32[8,128]{1,0:T(8,128)S(1)} %get-tuple-element.58.refs_0_), channel_id=1, source_target_pairs={{0,12},{4,8},{8,4},{12,0},{1,13},{5,9},{9,5},{13,1},{2,14},{6,10},... | collective-permute-start | bytes 12296 | tf_op jit(solution)/shard_map/ppermute | solution.py:616
  34.4 4.6 %collective-permute-start.9 = (f32[8,128]{1,0:T(8,128)S(1)}, f32[8,128]{1,0:T(8,128)S(1)}, u32[]{:S(2)}, u32[]{:S(2)}) collective-permute-start(f32[8,128]{1,0:T(8,128)S(1)} %get-tuple-element.58.refs_0_), channel_id=1, source_target_pairs={{0,8},{4,12},{8,0},{12,4},{1,9},{5,13},{9,1},{13,5},{2,10},{6,14},... | collective-permute-start | bytes 12296 | tf_op jit(solution)/shard_map/ppermute | solution.py:616
  34.4 4.6 %collective-permute-start.10 = (f32[8,128]{1,0:T(8,128)S(1)}, f32[8,128]{1,0:T(8,128)S(1)}, u32[]{:S(2)}, u32[]{:S(2)}) collective-permute-start(f32[8,128]{1,0:T(8,128)S(1)} %get-tuple-element.58.refs_0_), channel_id=1, source_target_pairs={{0,4},{4,0},{8,12},{12,8},{1,5},{5,1},{9,13},{13,9},{2,6},{6,2},{1... | collective-permute-start | bytes 12296 | tf_op jit(solution)/shard_map/ppermute | solution.py:616
  36.9 10.2 %collective-permute-start.16 = (bf16[96,1152]{1,0:T(8,128)(2,1)S(1)}, bf16[96,1152]{1,0:T(8,128)(2,1)S(1)}, u32[]{:S(2)}, u32[]{:S(2)}) collective-permute-start(bf16[96,1152]{1,0:T(8,128)(2,1)S(1)} %bundle.1), channel_id=1, source_target_pairs={{0,4},{4,0},{8,12},{12,8},{1,5},{5,1},{9,13},{13,9},{2,6},{6,2},{1... | collective-permute-start | bytes 663560 | tf_op jit(solution)/shard_map/ppermute | solution.py:616
  39.5 5.2 %collective-permute-start.13 = (bf16[416,128]{1,0:T(8,128)(2,1)S(1)}, bf16[416,128]{1,0:T(8,128)(2,1)S(1)}, u32[]{:S(2)}, u32[]{:S(2)}) collective-permute-start(bf16[416,128]{1,0:T(8,128)(2,1)S(1)} %get-tuple-element.71.refs_0_), channel_id=1, source_target_pairs={{0,3},{1,2},{2,1},{3,0},{4,7},{5,6},{6,5},{7,4},{8,11},{9,10},{10,... | collective-permute-start | bytes 319496 | tf_op jit(solution)/shard_map/ppermute | solution.py:616
  39.5 7.5 %collective-permute-start.14 = (bf16[416,128]{1,0:T(8,128)(2,1)S(1)}, bf16[416,128]{1,0:T(8,128)(2,1)S(1)}, u32[]{:S(2)}, u32[]{:S(2)}) collective-permute-start(bf16[416,128]{1,0:T(8,128)(2,1)S(1)} %get-tuple-element.71.refs_0_), channel_id=1, source_target_pairs={{0,2},{1,3},{2,0},{3,1},{4,6},{5,7},{6,4},{7,5},{8,10},{9,11},{10,... | collective-permute-start | bytes 319496 | tf_op jit(solution)/shard_map/ppermute | solution.py:616
  41.1 6.0 %collective-permute-start.15 = (bf16[416,128]{1,0:T(8,128)(2,1)S(1)}, bf16[416,128]{1,0:T(8,128)(2,1)S(1)}, u32[]{:S(2)}, u32[]{:S(2)}) collective-permute-start(bf16[416,128]{1,0:T(8,128)(2,1)S(1)} %get-tuple-element.71.refs_0_), channel_id=1, source_target_pairs={{0,1},{1,0},{2,3},{3,2},{4,5},{5,4},{6,7},{7,6},{8,9},{9,8},{10,11... | collective-permute-start | bytes 319496 | tf_op jit(solution)/shard_map/ppermute | solution.py:616

commit v22 on v20

--- a/solution.py
+++ b/solution.py
@@ -559,6 +559,12 @@
 
     def products(i):
         start, width = tiles[i]
+        if 2 * width <= 256:
+            both = jnp.concatenate([rows_of(0, start, width), rows_of(1, start, width)], axis=1)
+            buffers[i % 2][0, :, : 2 * width] = jnp.dot(
+                rho_ref[...], both, preferred_element_type=f32
+            )
+            return
         for part in range(2):
             buffers[i % 2][part, :, :width] = jnp.dot(
                 rho_ref[...], rows_of(part, start, width), preferred_element_type=f32
@@ -575,7 +581,11 @@
                 cos_r = cos_ref[r : r + 1, at]
                 sin_r = sin_ref[r : r + 1, at]
                 s_re = buffer[0, r * rows : (r + 1) * rows, a : a + LANES]
-                s_im = buffer[1, r * rows : (r + 1) * rows, a : a + LANES]
+                row = slice(r * rows, (r + 1) * rows)
+                if 2 * width <= 256:
+                    s_im = buffer[0, row, width + a : width + a + LANES]
+                else:
+                    s_im = buffer[1, row, a : a + LANES]
                 numer_re = numer_re + s_re * cos_r + s_im * sin_r
                 numer_im = numer_im + s_im * cos_r - s_re * sin_r
             here = slice(start + a, start + a + LANES)

time: 50.2 us -> 50.4 us (level)
  no operation moved by 1% of the time
where the time goes in v22:
time: 50.4 us; the launch traced here: 50.2 us
  Pallas kernels  19.9 us (39%)
  starting transfers between devices  18.5 us (37%)
  waiting for transfers between devices  9.88 us (20%)
  local copies, waits for them, and re-layouts  1.13 us (2%)
  between operations  0.81 us (2%)
    ppermute x17, starting transfers between devices, swap(): return lax.ppermute(values, axis, [(i, i ^ distance) for i in range(size)])  18.5 us
    pallas_call x12, Pallas kernels, call(): pl.pallas_call(kernel, in_specs=in_specs, out_specs=[VMEM] * len(out_shap...  17.1 us
    ppermute x17, waiting for transfers between devices, swap(): return lax.ppermute(values, axis, [(i, i ^ distance) for i in range(size)])  9.88 us
    pallas_call x2, Pallas kernels, early_templates(): pl.pallas_call(early_kernel, grid=(count,), in_specs=[pl.BlockSpec((2, ro...  2.81 us
    unnamed x3, local copies, waits for them, and re-layouts  1.13 us
  transfers between devices with their start and end apart: 17, of which 5 were waited for; matrix products, arithmetic and copies ran while one was open for 2% of the time, Pallas kernels for 30%

profile of v22, /device:TPU:0, one launch (start us, length us, event | category | flops | bytes accessed | tf_op | source)
XLA Modules:
  0.0 50.2 jit_solution(9934816498317996382)
XLA Ops:
  0.6 1.6 %weigh.1 = (bf16[32,4736]{1,0:T(8,128)(2,1)S(1)}, bf16[32,2432]{1,0:T(8,128)(2,1)S(1)}, bf16[32,2304]{1,0:T(8,128)(2,1)S(1)}) custom-call(s32[16]{0:T(128)} %ids_hbm.1, bf16[16,2,4608]{2,1,0:T(2,128)(2,1)} %p_hbm.1, f32[64,4608]{1,0:T(8,128)} %ctf_hbm.3, f32[4608]{0:T(1024)} %nw_hbm.3), custom_call_target="tpu_custom_call" | custom-call | flops 294912 | bytes 1179648 | tf_op jit(solution)/shard_map/weigh/pallas_call | solution.py:30
  2.2 3.1 %collective-permute-start.2 = (bf16[32,4736]{1,0:T(8,128)(2,1)S(1)}, bf16[32,4736]{1,0:T(8,128)(2,1)S(1)}, u32[]{:S(2)}, u32[]{:S(2)}) collective-permute-start(bf16[32,4736]{1,0:T(8,128)(2,1)S(1)} %get-tuple-element.37.refs_0_.refs_4_), channel_id=1, source_target_pairs={{0,4},{4,0},{8,12},{12,8},{1,5},{5,1},{9,13},{13,9},{2,6},{6,2},{1... | collective-permute-start | bytes 909320 | tf_op jit(solution)/shard_map/ppermute | solution.py:626
  5.3 2.6 %collective-permute-start = (bf16[32,2432]{1,0:T(8,128)(2,1)S(1)}, bf16[32,2432]{1,0:T(8,128)(2,1)S(1)}, u32[]{:S(2)}, u32[]{:S(2)}) collective-permute-start(bf16[32,2432]{1,0:T(8,128)(2,1)S(1)} %get-tuple-element.35), channel_id=1, source_target_pairs={{0,8},{4,12},{8,0},{12,4},{1,9},{5,13},{9,1},{13,5},{2,10},{6,14},... | collective-permute-start | bytes 466952 | tf_op jit(solution)/shard_map/ppermute | solution.py:626
  7.9 0.3 collective-permute-start.1
  8.2 0.1 pad_add_fusion.me_ref
  8.3 0.6 %cut_slices.3 = (bf16[32,1152]{1,0:T(8,128)(2,1)S(1)}, bf16[32,1152]{1,0:T(8,128)(2,1)S(1)}, bf16[32,1152]{1,0:T(8,128)(2,1)S(1)}) custom-call(s32[2]{0:T(128)S(1)} %pad_add_fusion.me_ref, bf16[32,4736]{1,0:T(8,128)(2,1)S(1)} %get-tuple-element.37.refs_0_.refs_4_), custom_call_target="tpu_custom_call" | custom-call | bytes 442368 | tf_op jit(solution)/shard_map/cut_slices/pallas_call | solution.py:30
  8.9 0.2 collective-permute-start.3
  9.0 1.5 %collective-permute-start.4 = (bf16[32,1152]{1,0:T(8,128)(2,1)S(1)}, bf16[32,1152]{1,0:T(8,128)(2,1)S(1)}, u32[]{:S(2)}, u32[]{:S(2)}) collective-permute-start(bf16[32,1152]{1,0:T(8,128)(2,1)S(1)} %get-tuple-element.40), channel_id=1, source_target_pairs={{0,2},{1,3},{2,0},{3,1},{4,6},{5,7},{6,4},{7,5},{8,10},{9,11},{10,... | collective-permute-start | bytes 221192 | tf_op jit(solution)/shard_map/ppermute | solution.py:626
  10.5 1.1 %copy.10 = bf16[32,2,4608]{2,0,1:T(8,128)(2,1)S(1)} copy(bf16[32,2,4608]{2,1,0:T(2,128)(2,1)} %param.7) | data formatting | bytes 1179648 | tf_op args[1]
  11.7 3.1 %prepare.1 = (f32[24,4608]{1,0:T(8,128)S(1)}, f32[24,4608]{1,0:T(8,128)S(1)}, f32[32,64]{1,0:T(8,128)S(1)}, f32[64,4608]{1,0:T(8,128)S(1)}) custom-call(s32[2,24]{1,0:T(2,128)S(1)} %bitcast.11, bf16[2,32,4608]{2,1,0:T(8,128)(2,1)S(1)} %bitcast.7, f32[64,4608]{1,0:T(8,128)} %ctf_hbm.3, f32[4608]{0:T(1024)} %nw_hbm.3), custom_call_target="tpu_custom_call" | custom-call | flops 226492416 | tf_op jit(solution)/shard_map/prepare/pallas_call | solution.py:30
  14.8 0.7 %early_templates4.1.early_ref = bf16[2,768,768]{2,1,0:T(8,128)(2,1)S(1)} custom-call(bf16[2,32,4608]{2,1,0:T(8,128)(2,1)S(1)} %bitcast.8, f32[24,4608]{1,0:T(8,128)S(1)} %get-tuple-element.41.cos_ref, f32[24,4608]{1,0:T(8,128)S(1)} %get-tuple-element.42.sin_ref), custom_call_target="tpu_custom_call" | custom-call | flops 23592960 | bytes 2359296 | tf_op jit(solution)/shard_map/early_templates4/pallas_call | solution.py:206
  15.5 2.1 %early_templates6.1.temp_ref = bf16[6,768,768]{2,1,0:T(8,128)(2,1)S(1)} custom-call(bf16[2,32,4608]{2,1,0:T(8,128)(2,1)S(1)} %bitcast.9, f32[24,4608]{1,0:T(8,128)S(1)} %get-tuple-element.41.cos_ref, f32[24,4608]{1,0:T(8,128)S(1)} %get-tuple-element.42.sin_ref), custom_call_target="tpu_custom_call" | custom-call | flops 70778880 | bytes 7077888 | tf_op jit(solution)/shard_map/early_templates6/pallas_call | solution.py:206
  17.6 0.0 collective-permute-done.3.refs_2_
  17.6 0.0 collective-permute-done.4.refs_4_
  17.6 3.8 %collective-permute-done.1.refs_6_.refs_3_ = bf16[32,2304]{1,0:T(8,128)(2,1)S(1)} collective-permute-done((bf16[32,2304]{1,0:T(8,128)(2,1)S(1)}, bf16[32,2304]{1,0:T(8,128)(2,1)S(1)}, u32[]{:S(2)}, u32[]{:S(2)}) %collective-permute-start.1) | collective-permute-done | bytes 147488 | tf_op jit(solution)/shard_map/ppermute | solution.py:626
  21.4 0.0 collective-permute-done.refs_2_
  21.4 0.0 collective-permute-done.2.refs_1_.refs_5_
  21.4 0.5 collective-permute-start.5
  21.9 1.6 %collective-permute-start.6 = (bf16[32,2304]{1,0:T(8,128)(2,1)S(1)}, bf16[32,2304]{1,0:T(8,128)(2,1)S(1)}, u32[]{:S(2)}, u32[]{:S(2)}) collective-permute-start(bf16[32,2304]{1,0:T(8,128)(2,1)S(1)} %collective-permute-done.1.refs_6_.refs_3_), channel_id=1, source_target_pairs={{0,4},{4,0},{8,12},{12,8},{1,5},{5,1},{9,13},{13,9},{2,6},{6,2},{1... | collective-permute-start | bytes 442376 | tf_op jit(solution)/shard_map/ppermute | solution.py:626
  23.4 0.6 %cut_slices.4 = (bf16[64,1152]{1,0:T(8,128)(2,1)S(1)}, bf16[64,1152]{1,0:T(8,128)(2,1)S(1)}, bf16[64,1152]{1,0:T(8,128)(2,1)S(1)}, bf16[96,1152]{1,0:T(8,128)(2,1)S(1)}) custom-call(s32[2]{0:T(128)S(1)} %pad_add_fusion.me_ref, bf16[32,4736]{1,0:T(8,128)(2,1)S(1)} %get-tuple-element.37.refs_0_.refs_4_, ...), custom_call_target="tpu_custom_call" | custom-call | bytes 1327104 | tf_op jit(solution)/shard_map/cut_slices/pallas_call | solution.py:30
  24.1 0.1 collective-permute-start.7
  24.1 1.6 %collective-permute-start.11 = (bf16[64,1152]{1,0:T(8,128)(2,1)S(1)}, bf16[64,1152]{1,0:T(8,128)(2,1)S(1)}, u32[]{:S(2)}, u32[]{:S(2)}) collective-permute-start(bf16[64,1152]{1,0:T(8,128)(2,1)S(1)} %get-tuple-element.60), channel_id=1, source_target_pairs={{0,3},{1,2},{2,1},{3,0},{4,7},{5,6},{6,5},{7,4},{8,11},{9,10},{10,... | collective-permute-start | bytes 442376 | tf_op jit(solution)/shard_map/ppermute | solution.py:626
  25.7 0.5 %collective-permute-start.12 = (bf16[64,1152]{1,0:T(8,128)(2,1)S(1)}, bf16[64,1152]{1,0:T(8,128)(2,1)S(1)}, u32[]{:S(2)}, u32[]{:S(2)}) collective-permute-start(bf16[64,1152]{1,0:T(8,128)(2,1)S(1)} %get-tuple-element.62), channel_id=1, source_target_pairs={{0,2},{1,3},{2,0},{3,1},{4,6},{5,7},{6,4},{7,5},{8,10},{9,11},{10,... | collective-permute-start | bytes 442376 | tf_op jit(solution)/shard_map/ppermute | solution.py:626
  26.3 1.3 %templates.1.built_ref = bf16[4,768,768]{2,1,0:T(8,128)(2,1)S(1)} custom-call(bf16[2,32,4608]{2,1,0:T(8,128)(2,1)S(1)} %bitcast.10, f32[24,4608]{1,0:T(8,128)S(1)} %get-tuple-element.41.cos_ref, f32[24,4608]{1,0:T(8,128)S(1)} %get-tuple-element.42.sin_ref), custom_call_target="tpu_custom_call" | custom-call | flops 47185920 | tf_op jit(solution)/shard_map/templates/pallas_call | solution.py:30
  27.5 0.0 collective-permute-done.5.refs_3_.refs_0_
  27.5 2.0 %score0.1.acc_ref = f32[768,128]{1,0:T(8,128)S(1)} custom-call(bf16[4,768,768]{2,1,0:T(8,128)(2,1)S(1)} %templates.1.built_ref, bf16[2,768,768]{2,1,0:T(8,128)(2,1)S(1)} %early_templates4.1.early_ref, bf16[32,4736]{1,0:T(8,128)(2,1)S(1)} %get-tuple-element.37.refs_0_.refs_4_, bf16[32,4736]{1,0:T(8,128)(2,1)S(1)} %collective-permute-done.2.refs_1_.refs_5_, ...), custom_call_target="tpu_custom_call" | custom-call | flops 1811939328 | tf_op jit(solution)/shard_map/score0/pallas_call | solution.py:30
  29.5 0.0 collective-permute-done.6.refs_7_.refs_1_
  29.5 2.2 %score1.1 = (f32[768,128]{1,0:T(8,128)S(1)}, f32[128,64]{1,0:T(8,128)S(1)}, f32[8,128]{1,0:T(8,128)S(1)}) custom-call(bf16[6,768,768]{2,1,0:T(8,128)(2,1)S(1)} %early_templates6.1.temp_ref, f32[32,64]{1,0:T(8,128)S(1)} %get-tuple-element.44.pow_ref, f32[768,128]{1,0:T(8,128)S(1)} %score0.1.acc_ref, bf16[32,4736]{1,0:T(8,128)(2,1)S(1)} %get-tuple-element.37.refs_0_.refs_4_, ...), custom_call_target="tpu_custom_call" | custom-call | flops 1811939328 | tf_op jit(solution)/shard_map/score1/pallas_call | solution.py:30
  31.8 0.0 collective-permute-done.7.refs_6_.refs_2_
  31.8 2.6 %collective-permute-start.8 = (f32[8,128]{1,0:T(8,128)S(1)}, f32[8,128]{1,0:T(8,128)S(1)}, u32[]{:S(2)}, u32[]{:S(2)}) collective-permute-start(f32[8,128]{1,0:T(8,128)S(1)} %get-tuple-element.54.refs_0_), channel_id=1, source_target_pairs={{0,12},{4,8},{8,4},{12,0},{1,13},{5,9},{9,5},{13,1},{2,14},{6,10},... | collective-permute-start | bytes 12296 | tf_op jit(solution)/shard_map/ppermute | solution.py:626
  34.4 0.0 collective-permute-start.9
  34.4 1.8 %collective-permute-start.10 = (f32[8,128]{1,0:T(8,128)S(1)}, f32[8,128]{1,0:T(8,128)S(1)}, u32[]{:S(2)}, u32[]{:S(2)}) collective-permute-start(f32[8,128]{1,0:T(8,128)S(1)} %get-tuple-element.54.refs_0_), channel_id=1, source_target_pairs={{0,4},{4,0},{8,12},{12,8},{1,5},{5,1},{9,13},{13,9},{2,6},{6,2},{1... | collective-permute-start | bytes 12296 | tf_op jit(solution)/shard_map/ppermute | solution.py:626
  36.3 0.6 %cut_slices.5.refs_4_ = bf16[32,1152]{1,0:T(8,128)(2,1)S(1)} custom-call(s32[2]{0:T(128)S(1)} %pad_add_fusion.me_ref, bf16[32,2432]{1,0:T(8,128)(2,1)S(1)} %collective-permute-done.5.refs_3_.refs_0_, bf16[32,2304]{1,0:T(8,128)(2,1)S(1)} %collective-permute-done.6.refs_7_.refs_1_), custom_call_target="tpu_custom_call" | custom-call | bytes 147456 | tf_op jit(solution)/shard_map/cut_slices/pallas_call | solution.py:30
  36.8 0.0 collective-permute-done.11.refs_3_.refs_0_
  36.8 0.0 collective-permute-done.12.refs_5_.refs_1_
  36.9 0.3 collective-permute-start.16
  37.1 0.1 collective-permute-done.8.refs_1_
  37.3 1.8 %collective-permute-done.9.refs_2_ = f32[8,128]{1,0:T(8,128)S(1)} collective-permute-done((f32[8,128]{1,0:T(8,128)S(1)}, f32[8,128]{1,0:T(8,128)S(1)}, u32[]{:S(2)}, u32[]{:S(2)}) %collective-permute-start.9) | collective-permute-done | bytes 4128 | tf_op jit(solution)/shard_map/ppermute | solution.py:626
  39.0 0.0 collective-permute-done.10.refs_3_
  39.0 0.5 responsibilities.1
  39.5 0.0 collective-permute-start.13
  39.6 1.5 %collective-permute-start.14 = (bf16[416,128]{1,0:T(8,128)(2,1)S(1)}, bf16[416,128]{1,0:T(8,128)(2,1)S(1)}, u32[]{:S(2)}, u32[]{:S(2)}) collective-permute-start(bf16[416,128]{1,0:T(8,128)(2,1)S(1)} %get-tuple-element.67.refs_0_), channel_id=1, source_target_pairs={{0,2},{1,3},{2,0},{3,1},{4,6},{5,7},{6,4},{7,5},{8,10},{9,11},{10,... | collective-permute-start | bytes 319496 | tf_op jit(solution)/shard_map/ppermute | solution.py:626
  41.1 0.3 collective-permute-start.15
  41.4 1.5 %gather_rows.1 = (f32[32,64]{1,0:T(8,128)}, bf16[64,2304]{1,0:T(8,128)(2,1)S(1)}, bf16[2,192,1152]{2,1,0:T(8,128)(2,1)S(1)}) custom-call(s32[2]{0:T(128)S(1)} %pad_add_fusion.me_ref, f32[768,128]{1,0:T(8,128)S(1)} %get-tuple-element.50.s_ref, f32[1,128]{1,0:T(1,128)S(1)} %get-tuple-element.55.norm_ref, f32[64,4608]{1,0:T(8,128)S(1)} %get-tuple-element.56.weight_ref, ...), custom_call_target="tpu_custom_call" | custom-call | flops 20000000000 | bytes 1769472 | tf_op jit(solution)/shard_map/gather_rows/pallas_call | solution.py:30
  42.9 1.9 %collective-permute-done.13.refs_1_ = bf16[416,128]{1,0:T(8,128)(2,1)S(1)} collective-permute-done((bf16[416,128]{1,0:T(8,128)(2,1)S(1)}, bf16[416,128]{1,0:T(8,128)(2,1)S(1)}, u32[]{:S(2)}, u32[]{:S(2)}) %collective-permute-start.13) | collective-permute-done | bytes 106528 | tf_op jit(solution)/shard_map/ppermute | solution.py:626
  44.8 2.3 %collective-permute-done.14.refs_2_ = bf16[416,128]{1,0:T(8,128)(2,1)S(1)} collective-permute-done((bf16[416,128]{1,0:T(8,128)(2,1)S(1)}, bf16[416,128]{1,0:T(8,128)(2,1)S(1)}, u32[]{:S(2)}, u32[]{:S(2)}) %collective-permute-start.14) | collective-permute-done | bytes 106528 | tf_op jit(solution)/shard_map/ppermute | solution.py:626
  47.1 0.0 collective-permute-done.15.refs_3_
  47.1 3.1 %finish.1 = f32[32,2,1152]{2,1,0:T(2,128)} custom-call(s32[2]{0:T(128)S(1)} %pad_add_fusion.me_ref, bf16[64,2304]{1,0:T(8,128)(2,1)S(1)} %get-tuple-element.65.cw_ref, f32[24,4608]{1,0:T(8,128)S(1)} %get-tuple-element.41.cos_ref, f32[24,4608]{1,0:T(8,128)S(1)} %get-tuple-element.42.sin_ref, bf16[2,192,1152]{2,1,0:T(8,128)(2,1)S(1)} %get-tuple-element.66.rows_ref, ...), custom_call_target="tpu_custom_call" | custom-call | flops 905969664 | tf_op jit(solution)/shard_map/finish/pallas_call | solution.py:30
  (4 shorter events, 0.0 us)
Async XLA Ops:
  0.6 11.0 %copy-start = (s32[24,2]{0,1:T(2,128)S(1)}, s32[24,2]{0,1:T(2,128)}, u32[]{:S(2)}) copy-start(s32[24,2]{0,1:T(2,128)} %param.11) | copy-start | bytes 580
  2.2 19.2 %collective-permute-start.2 = (bf16[32,4736]{1,0:T(8,128)(2,1)S(1)}, bf16[32,4736]{1,0:T(8,128)(2,1)S(1)}, u32[]{:S(2)}, u32[]{:S(2)}) collective-permute-start(bf16[32,4736]{1,0:T(8,128)(2,1)S(1)} %get-tuple-element.37.refs_0_.refs_4_), channel_id=1, source_target_pairs={{0,4},{4,0},{8,12},{12,8},{1,5},{5,1},{9,13},{13,9},{2,6},{6,2},{1... | collective-permute-start | bytes 909320 | tf_op jit(solution)/shard_map/ppermute | solution.py:626
  5.3 16.1 %collective-permute-start = (bf16[32,2432]{1,0:T(8,128)(2,1)S(1)}, bf16[32,2432]{1,0:T(8,128)(2,1)S(1)}, u32[]{:S(2)}, u32[]{:S(2)}) collective-permute-start(bf16[32,2432]{1,0:T(8,128)(2,1)S(1)} %get-tuple-element.35), channel_id=1, source_target_pairs={{0,8},{4,12},{8,0},{12,4},{1,9},{5,13},{9,1},{13,5},{2,10},{6,14},... | collective-permute-start | bytes 466952 | tf_op jit(solution)/shard_map/ppermute | solution.py:626
  7.9 13.5 %collective-permute-start.1 = (bf16[32,2304]{1,0:T(8,128)(2,1)S(1)}, bf16[32,2304]{1,0:T(8,128)(2,1)S(1)}, u32[]{:S(2)}, u32[]{:S(2)}) collective-permute-start(bf16[32,2304]{1,0:T(8,128)(2,1)S(1)} %get-tuple-element.36), channel_id=1, source_target_pairs={{0,8},{4,12},{8,0},{12,4},{1,9},{5,13},{9,1},{13,5},{2,10},{6,14},... | collective-permute-start | bytes 442376 | tf_op jit(solution)/shard_map/ppermute | solution.py:626
  8.9 8.7 %collective-permute-start.3 = (bf16[32,1152]{1,0:T(8,128)(2,1)S(1)}, bf16[32,1152]{1,0:T(8,128)(2,1)S(1)}, u32[]{:S(2)}, u32[]{:S(2)}) collective-permute-start(bf16[32,1152]{1,0:T(8,128)(2,1)S(1)} %get-tuple-element.39), channel_id=1, source_target_pairs={{0,3},{1,2},{2,1},{3,0},{4,7},{5,6},{6,5},{7,4},{8,11},{9,10},{10,... | collective-permute-start | bytes 221192 | tf_op jit(solution)/shard_map/ppermute | solution.py:626
  9.0 8.6 %collective-permute-start.4 = (bf16[32,1152]{1,0:T(8,128)(2,1)S(1)}, bf16[32,1152]{1,0:T(8,128)(2,1)S(1)}, u32[]{:S(2)}, u32[]{:S(2)}) collective-permute-start(bf16[32,1152]{1,0:T(8,128)(2,1)S(1)} %get-tuple-element.40), channel_id=1, source_target_pairs={{0,2},{1,3},{2,0},{3,1},{4,6},{5,7},{6,4},{7,5},{8,10},{9,11},{10,... | collective-permute-start | bytes 221192 | tf_op jit(solution)/shard_map/ppermute | solution.py:626
  21.4 6.1 %collective-permute-start.5 = (bf16[32,2432]{1,0:T(8,128)(2,1)S(1)}, bf16[32,2432]{1,0:T(8,128)(2,1)S(1)}, u32[]{:S(2)}, u32[]{:S(2)}) collective-permute-start(bf16[32,2432]{1,0:T(8,128)(2,1)S(1)} %collective-permute-done.refs_2_), channel_id=1, source_target_pairs={{0,4},{4,0},{8,12},{12,8},{1,5},{5,1},{9,13},{13,9},{2,6},{6,2},{1... | collective-permute-start | bytes 466952 | tf_op jit(solution)/shard_map/ppermute | solution.py:626
  21.9 7.7 %collective-permute-start.6 = (bf16[32,2304]{1,0:T(8,128)(2,1)S(1)}, bf16[32,2304]{1,0:T(8,128)(2,1)S(1)}, u32[]{:S(2)}, u32[]{:S(2)}) collective-permute-start(bf16[32,2304]{1,0:T(8,128)(2,1)S(1)} %collective-permute-done.1.refs_6_.refs_3_), channel_id=1, source_target_pairs={{0,4},{4,0},{8,12},{12,8},{1,5},{5,1},{9,13},{13,9},{2,6},{6,2},{1... | collective-permute-start | bytes 442376 | tf_op jit(solution)/shard_map/ppermute | solution.py:626
  24.1 7.7 %collective-permute-start.7 = (bf16[96,1152]{1,0:T(8,128)(2,1)S(1)}, bf16[96,1152]{1,0:T(8,128)(2,1)S(1)}, u32[]{:S(2)}, u32[]{:S(2)}) collective-permute-start(bf16[96,1152]{1,0:T(8,128)(2,1)S(1)} %get-tuple-element.53), channel_id=1, source_target_pairs={{0,1},{1,0},{2,3},{3,2},{4,5},{5,4},{6,7},{7,6},{8,9},{9,8},{10,11... | collective-permute-start | bytes 663560 | tf_op jit(solution)/shard_map/ppermute | solution.py:626
  24.1 12.7 %collective-permute-start.11 = (bf16[64,1152]{1,0:T(8,128)(2,1)S(1)}, bf16[64,1152]{1,0:T(8,128)(2,1)S(1)}, u32[]{:S(2)}, u32[]{:S(2)}) collective-permute-start(bf16[64,1152]{1,0:T(8,128)(2,1)S(1)} %get-tuple-element.60), channel_id=1, source_target_pairs={{0,3},{1,2},{2,1},{3,0},{4,7},{5,6},{6,5},{7,4},{8,11},{9,10},{10,... | collective-permute-start | bytes 442376 | tf_op jit(solution)/shard_map/ppermute | solution.py:626
  25.7 11.1 %collective-permute-start.12 = (bf16[64,1152]{1,0:T(8,128)(2,1)S(1)}, bf16[64,1152]{1,0:T(8,128)(2,1)S(1)}, u32[]{:S(2)}, u32[]{:S(2)}) collective-permute-start(bf16[64,1152]{1,0:T(8,128)(2,1)S(1)} %get-tuple-element.62), channel_id=1, source_target_pairs={{0,2},{1,3},{2,0},{3,1},{4,6},{5,7},{6,4},{7,5},{8,10},{9,11},{10,... | collective-permute-start | bytes 442376 | tf_op jit(solution)/shard_map/ppermute | solution.py:626
  31.8 5.5 %collective-permute-start.8 = (f32[8,128]{1,0:T(8,128)S(1)}, f32[8,128]{1,0:T(8,128)S(1)}, u32[]{:S(2)}, u32[]{:S(2)}) collective-permute-start(f32[8,128]{1,0:T(8,128)S(1)} %get-tuple-element.54.refs_0_), channel_id=1, source_target_pairs={{0,12},{4,8},{8,4},{12,0},{1,13},{5,9},{9,5},{13,1},{2,14},{6,10},... | collective-permute-start | bytes 12296 | tf_op jit(solution)/shard_map/ppermute | solution.py:626
  34.4 4.6 %collective-permute-start.9 = (f32[8,128]{1,0:T(8,128)S(1)}, f32[8,128]{1,0:T(8,128)S(1)}, u32[]{:S(2)}, u32[]{:S(2)}) collective-permute-start(f32[8,128]{1,0:T(8,128)S(1)} %get-tuple-element.54.refs_0_), channel_id=1, source_target_pairs={{0,8},{4,12},{8,0},{12,4},{1,9},{5,13},{9,1},{13,5},{2,10},{6,14},... | collective-permute-start | bytes 12296 | tf_op jit(solution)/shard_map/ppermute | solution.py:626
  34.4 4.6 %collective-permute-start.10 = (f32[8,128]{1,0:T(8,128)S(1)}, f32[8,128]{1,0:T(8,128)S(1)}, u32[]{:S(2)}, u32[]{:S(2)}) collective-permute-start(f32[8,128]{1,0:T(8,128)S(1)} %get-tuple-element.54.refs_0_), channel_id=1, source_target_pairs={{0,4},{4,0},{8,12},{12,8},{1,5},{5,1},{9,13},{13,9},{2,6},{6,2},{1... | collective-permute-start | bytes 12296 | tf_op jit(solution)/shard_map/ppermute | solution.py:626
  36.9 10.2 %collective-permute-start.16 = (bf16[96,1152]{1,0:T(8,128)(2,1)S(1)}, bf16[96,1152]{1,0:T(8,128)(2,1)S(1)}, u32[]{:S(2)}, u32[]{:S(2)}) collective-permute-start(bf16[96,1152]{1,0:T(8,128)(2,1)S(1)} %bundle.1), channel_id=1, source_target_pairs={{0,4},{4,0},{8,12},{12,8},{1,5},{5,1},{9,13},{13,9},{2,6},{6,2},{1... | collective-permute-start | bytes 663560 | tf_op jit(solution)/shard_map/ppermute | solution.py:626
  39.5 5.2 %collective-permute-start.13 = (bf16[416,128]{1,0:T(8,128)(2,1)S(1)}, bf16[416,128]{1,0:T(8,128)(2,1)S(1)}, u32[]{:S(2)}, u32[]{:S(2)}) collective-permute-start(bf16[416,128]{1,0:T(8,128)(2,1)S(1)} %get-tuple-element.67.refs_0_), channel_id=1, source_target_pairs={{0,3},{1,2},{2,1},{3,0},{4,7},{5,6},{6,5},{7,4},{8,11},{9,10},{10,... | collective-permute-start | bytes 319496 | tf_op jit(solution)/shard_map/ppermute | solution.py:626
  39.6 7.5 %collective-permute-start.14 = (bf16[416,128]{1,0:T(8,128)(2,1)S(1)}, bf16[416,128]{1,0:T(8,128)(2,1)S(1)}, u32[]{:S(2)}, u32[]{:S(2)}) collective-permute-start(bf16[416,128]{1,0:T(8,128)(2,1)S(1)} %get-tuple-element.67.refs_0_), channel_id=1, source_target_pairs={{0,2},{1,3},{2,0},{3,1},{4,6},{5,7},{6,4},{7,5},{8,10},{9,11},{10,... | collective-permute-start | bytes 319496 | tf_op jit(solution)/shard_map/ppermute | solution.py:626
  41.1 6.0 %collective-permute-start.15 = (bf16[416,128]{1,0:T(8,128)(2,1)S(1)}, bf16[416,128]{1,0:T(8,128)(2,1)S(1)}, u32[]{:S(2)}, u32[]{:S(2)}) collective-permute-start(bf16[416,128]{1,0:T(8,128)(2,1)S(1)} %get-tuple-element.67.refs_0_), channel_id=1, source_target_pairs={{0,1},{1,0},{2,3},{3,2},{4,5},{5,4},{6,7},{7,6},{8,9},{9,8},{10,11... | collective-permute-start | bytes 319496 | tf_op jit(solution)/shard_map/ppermute | solution.py:626
